TPU v7x, 32 devices: a whole 2x2x4 slice. The times are simulated.
32 devices in a mesh: wide: 16 (over z, x, core), narrow: 2 (over y).
Axes of the slice: x: 2, y: 2, z: 4, core: 2. Of those that a mesh axis runs over, the one named last changes fastest.
Arguments:
- features: bfloat16 [128, 16, 8, 192], P('wide', 'narrow'), may hold values from -6 to 6
- weight: bfloat16 [5184, 192], replicated, may hold values from -0.078125 to 0.078125
- voxel_mask: int32 [128, 16, 8], P('wide', 'narrow'), may hold values 0 or 1
- cotangent: bfloat16 [128, 16, 8, 192], P('wide', 'narrow'), may hold values from -6 to 6
Outputs:
- activation: bfloat16 [128, 16, 8, 192], P('wide', 'narrow')
- grad_input: bfloat16 [128, 16, 8, 192], P('wide', 'narrow')
- grad_weight: float32 [192, 5184], P('wide')
All inputs are finite; a program needn't handle non-finite values. No bound on the sum of `voxel_mask` on one device may be relied on, other than what follows from the above.
Results may differ from a plain program's by a relative error of at most 0.0049.
Values may be sent and summed in bfloat16 or wider, within the bound.
No kernel may reach another device: no remote copies, remote signals or barrier semaphores. Data moves between devices by JAX's collectives and lax.ppermute only.
A program may use at most 64 MiB of HBM per device.

v0:
```python
import jax
import jax.numpy as jnp
from jax import lax
from jax.sharding import PartitionSpec as P


def padded_2(cells, sides, width):
    for axis, dim in sides:
        count = lax.axis_size(axis)
        ends = count - 1
        head = lax.slice_in_dim(cells, 0, width, axis=dim)
        tail = lax.slice_in_dim(cells, cells.shape[dim] - width, cells.shape[dim], axis=dim)
        cells = jnp.concatenate(
            [
                lax.ppermute(tail, axis, [(i, (i + 1) % count) for i in range(ends)]),
                cells,
                lax.ppermute(head, axis, [((i + 1) % count, i) for i in range(ends)]),
            ],
            axis=dim,
        )
    return cells


def gather_taps(padded, width_x, width_y, depth_z, channels, flip):
    pieces = []
    for shift_x in range(3):
        for shift_y in range(3):
            for shift_z in range(3):
                start_x = 2 - shift_x if flip else shift_x
                start_y = 2 - shift_y if flip else shift_y
                start_z = 2 - shift_z if flip else shift_z
                piece = padded[
                    start_x : start_x + width_x,
                    start_y : start_y + width_y,
                    start_z : start_z + depth_z,
                    :,
                ]
                pieces.append(piece.reshape(-1, channels))
    return jnp.concatenate(pieces, axis=1)


def local(features, weight, voxel_mask, cotangent):
    width_x, width_y, depth_z, channels = features.shape
    masked = features * voxel_mask.astype(jnp.bfloat16)[..., None]
    padded = padded_2(masked, (("wide", 0), ("narrow", 1)), 1)
    padded = jnp.pad(padded, ((0, 0), (0, 0), (1, 1), (0, 0)))
    columns = gather_taps(padded, width_x, width_y, depth_z, channels, False)
    pre = jnp.dot(columns, weight, preferred_element_type=jnp.float32)
    live = voxel_mask.reshape(-1, 1).astype(jnp.float32)
    sig = jax.nn.sigmoid(pre)
    activation = (
        (pre * sig * live).astype(jnp.bfloat16).reshape(width_x, width_y, depth_z, channels)
    )
    slope = sig * (1.0 + pre * (1.0 - sig))
    grad_pre = (cotangent.reshape(-1, channels).astype(jnp.float32) * live * slope).astype(
        jnp.bfloat16
    )
    taps = weight.reshape(27, channels, channels)
    grid = grad_pre.reshape(width_x, width_y, depth_z, channels)
    grad_pad = padded_2(grid, (("wide", 0), ("narrow", 1)), 1)
    grad_pad = jnp.pad(grad_pad, ((0, 0), (0, 0), (1, 1), (0, 0)))
    grad_columns = gather_taps(grad_pad, width_x, width_y, depth_z, channels, True)
    flipped = jnp.transpose(taps, (0, 2, 1)).reshape(27 * channels, channels)
    grad_field = jnp.dot(grad_columns, flipped, preferred_element_type=jnp.float32)
    grad_input = (
        (grad_field * live).astype(jnp.bfloat16).reshape(width_x, width_y, depth_z, channels)
    )
    scale = 1.0 / jnp.sqrt(
        jnp.float32(width_x * width_y * depth_z * lax.axis_size("wide") * lax.axis_size("narrow"))
    )
    whole = lax.dot_general(
        grad_pre, columns, (((0,), (0,)), ((), ())), preferred_element_type=jnp.float32
    )
    piece_flat = lax.psum_scatter(
        whole.reshape(-1), ("wide", "narrow"), scatter_dimension=0, tiled=True
    )
    gathered = lax.all_gather(piece_flat, "narrow", axis=0, tiled=True)
    summed = gathered.reshape(channels // lax.axis_size("wide"), 27 * channels)
    grad_weight = summed * scale
    return (activation, grad_input, grad_weight)


def solution(mesh):
    return jax.shard_map(
        local,
        mesh=mesh,
        in_specs=(
            P("wide", "narrow", None, None),
            P(),
            P("wide", "narrow", None),
            P("wide", "narrow", None, None),
        ),
        out_specs=(
            P("wide", "narrow", None, None),
            P("wide", "narrow", None, None),
            P("wide", None),
        ),
        check_vma=False,
    )
```

profile of v0, /device:TPU:0, one launch (start us, length us, event | category | flops | bytes accessed | tf_op | source)
XLA Modules:
  0.0 227.3 jit_solution(6169706054863031692)
XLA Ops:
  7.2 0.8 fusion.15
  8.1 1.1 broadcast_multiply_fusion
  9.2 2.4 %collective-permute-start = (bf16[1,8,8,192]{3,2,1,0:T(8,128)(2,1)S(1)}, bf16[1,8,8,192]{3,2,1,0:T(8,128)(2,1)S(1)}, u32[]{:S(2)}, u32[]{:S(2)}) collective-permute-start(bf16[1,8,8,192]{3,2,1,0:T(8,128)(2,1)S(1)} %get-tuple-element.68), channel_id=1, source_target_pairs={{0,2},{2,4},{4,6},{6,8},{8,10},{10,12},{12,14},{14,16},{16,18},{18... | collective-permute-start | bytes 73736 | tf_op jit(solution)/shard_map/ppermute | solution.py:15
  11.5 1.3 collective-permute-start.1
  12.8 1.0 bitcast_convert_fusion
  13.9 0.9 copy.47
  14.8 3.8 %copy.77 = bf16[5184,192]{1,0:T(8,128)(2,1)S(1)} copy(bf16[5184,192]{0,1:T(8,128)(2,1)} %param.5) | data formatting | bytes 3981312 | tf_op args[1]
  18.7 3.4 %copy.78 = bf16[27,192,192]{2,1,0:T(8,128)(2,1)} copy(bf16[27,192,192]{1,2,0:T(8,128)(2,1)S(1)} %bitcast.71) | data formatting | bytes 3981312 | tf_op jit(solution)/shard_map/transpose | solution.py:63
  22.2 4.3 %collective-permute-start.2 = (bf16[10,1,8,192]{3,2,1,0:T(8,128)(2,1)S(1)}, bf16[10,1,8,192]{3,2,1,0:T(8,128)(2,1)S(1)}, u32[]{:S(2)}, u32[]{:S(2)}) collective-permute-start(bf16[10,1,8,192]{3,2,1,0:T(8,128)(2,1)S(1)} %get-tuple-element.62), channel_id=1, source_target_pairs={{0,1},{2,3},{4,5},{6,7},{8,9},{10,11},{12,13},{14,15},{16,17},{18,... | collective-permute-start | bytes 92168 | tf_op jit(solution)/shard_map/ppermute | solution.py:15
  26.4 1.3 collective-permute-start.3
  27.7 0.9 pad_maximum_fusion.4
  28.6 3.7 %collective-permute-done.3 = bf16[10,1,8,192]{3,2,1,0:T(8,128)(2,1)S(1)} collective-permute-done((bf16[10,1,8,192]{3,2,1,0:T(8,128)(2,1)S(1)}, bf16[10,1,8,192]{3,2,1,0:T(8,128)(2,1)S(1)}, u32[]{:S(2)}, u32[]{:S(2)}) %collective-permute-start.3) | collective-permute-done | bytes 30752 | tf_op jit(solution)/shard_map/ppermute | solution.py:17
  32.8 2.0 fusion.8
  34.9 1.2 fusion.11
  36.1 10.0 %concatenate.56 = bf16[512,5184]{1,0:T(8,128)(2,1)} concatenate(bf16[512,192]{1,0:T(8,128)(2,1)} %bitcast.95, bf16[512,192]{1,0:T(8,128)(2,1)} %bitcast.99, bf16[512,192]{1,0:T(8,128)(2,1)} %bitcast.94, bf16[512,192]{1,0:T(8,128)(2,1)} %bitcast.93, bf16[512,192]{1,0:T(8,128)(2,1)} %bitcast.121, bf16[512,192]{1,0:T(8,128)(2,1)} %bitcast.92, bf16[512,192]{1,0:T(8,128)(2,1)} %bitcast.91, ...), dimensions={1} | concatenate | bytes 10616832 | tf_op jit(solution)/shard_map/concatenate | solution.py:39
  46.1 4.6 %multiply_convert_fusion = (bf16[512,192]{0,1:T(8,128)(2,1)S(1)}, bf16[512,192]{0,1:T(8,128)(2,1)S(1)}) fusion(f32[512,192]{0,1:T(8,128)} %copy.47, f32[512]{0:T(512)S(1)} %convert_element_type.34, bf16[512,5184]{1,0:T(8,128)(2,1)} %concatenate.56, bf16[5184,192]{0,1:T(8,128)(2,1)S(1)} %copy-done.1), kind=kOutput, calls=%fused_computation.16 | convolution fusion | flops 1020493824 | bytes 8087552 | tf_op jit(solution)/shard_map/dot_general | solution.py:48
  51.0 1.3 collective-permute-start.5
  52.3 3.5 %collective-permute-start.4 = (bf16[1,8,8,192]{3,2,1,0:T(8,128)(2,1)S(1)}, bf16[1,8,8,192]{3,2,1,0:T(8,128)(2,1)S(1)}, u32[]{:S(2)}, u32[]{:S(2)}) collective-permute-start(bf16[1,8,8,192]{3,2,1,0:T(8,128)(2,1)S(1)} %bitcast.132), channel_id=1, source_target_pairs={{0,2},{2,4},{4,6},{6,8},{8,10},{10,12},{12,14},{14,16},{16,18},{18... | collective-permute-start | bytes 73736 | tf_op jit(solution)/shard_map/ppermute | solution.py:15
  55.9 5.8 %fusion.16 = f32[192,5184]{1,0:T(8,128)} fusion(bf16[512,192]{0,1:T(8,128)(2,1)S(1)} %get-tuple-element.42, bf16[512,5184]{1,0:T(8,128)(2,1)} %concatenate.56), kind=kOutput, calls=%fused_computation.72 | convolution fusion | flops 1019215872 | bytes 9486336 | tf_op jit(solution)/shard_map/dot_general | solution.py:71
  61.8 6.0 %reshape.261 = f32[995328]{0:T(1024)} reshape(f32[192,5184]{1,0:T(8,128)} %fusion.16) | data formatting | bytes 7962624 | tf_op jit(solution)/shard_map/reshape | solution.py:75
  67.7 0.8 copy.46
  68.6 1.9 collective-permute-start.6
  70.5 1.5 collective-permute-start.7
  72.1 0.8 copy.72
  72.9 0.8 copy.55
  73.7 2.7 %collective-permute-done.7 = bf16[10,1,8,192]{3,2,1,0:T(8,128)(2,1)S(1)} collective-permute-done((bf16[10,1,8,192]{3,2,1,0:T(8,128)(2,1)S(1)}, bf16[10,1,8,192]{3,2,1,0:T(8,128)(2,1)S(1)}, u32[]{:S(2)}, u32[]{:S(2)}) %collective-permute-start.7) | collective-permute-done | bytes 30752 | tf_op jit(solution)/shard_map/ppermute | solution.py:17
  76.6 0.9 fusion.9
  77.4 0.8 copy.58
  79.0 0.8 copy.61
  79.8 0.8 copy.52
  81.0 1.7 fusion.7
  82.8 0.8 copy.64
  84.8 1.0 constant_dynamic-update-slice_fusion.25
  85.8 0.9 constant_dynamic-update-slice_fusion.22
  86.8 0.9 constant_dynamic-update-slice_fusion.19
  87.8 0.9 constant_dynamic-update-slice_fusion.16
  88.9 2.7 %copy-done.3 = bf16[512,5184]{0,1:T(8,128)(2,1)} copy-done((bf16[512,5184]{0,1:T(8,128)(2,1)}, bf16[512,5184]{0,1:T(8,128)(2,1)S(1)}, u32[]{:S(2)}) %copy-start.3) | copy-done | bytes 5308440
  91.5 1.1 copy.75
  92.6 1.8 copy.66
  94.4 1.8 copy.69
  96.1 1.7 copy.76
  97.9 1.8 copy.74
  99.6 1.8 copy.73
  101.4 1.7 copy.71
  103.1 1.8 copy.70
  104.9 1.8 copy.68
  106.7 0.8 copy.67
  108.3 1.6 constant_dynamic-update-slice_fusion.10
  109.9 1.6 constant_dynamic-update-slice_fusion.9
  111.5 1.6 constant_dynamic-update-slice_fusion.8
  113.2 1.6 constant_dynamic-update-slice_fusion.7
  114.8 1.6 constant_dynamic-update-slice_fusion.6
  116.4 1.6 constant_dynamic-update-slice_fusion.5
  118.0 1.6 constant_dynamic-update-slice_fusion.4
  119.6 1.6 constant_dynamic-update-slice_fusion.3
  121.3 1.6 constant_dynamic-update-slice_fusion.2
  123.6 1.6 constant_dynamic-update-slice_fusion
  125.2 3.8 %fusion.1 = bf16[512,192]{0,1:T(8,128)(2,1)S(1)} fusion(bf16[512,5184]{0,1:T(8,128)(2,1)} %constant_dynamic-update-slice_fusion, bf16[5184,192]{1,0:T(8,128)(2,1)S(1)} %bitcast.77, f32[512]{0:T(512)S(1)} %convert_element_type.34), kind=kOutput, calls=%fused_computation.4 | convolution fusion | flops 1019412480 | bytes 7497728 | tf_op jit(solution)/shard_map/dot_general | solution.py:64
  129.0 0.8 copy.79
  129.9 82.1 %all-reduce.5.cloned.1.call-done = f32[995328]{0:T(1024)} async-done(((f32[995328]{0:T(1024)}), f32[995328]{0:T(1024)}) %all-reduce.5.cloned.1.call-update) | async-done | bytes 3981328
  212.0 1.0 dynamic-slice
  213.1 5.6 %all-gather = f32[2,1,31104]{2,1,0:T(1,128)S(1)} all-gather(f32[1,1,31104]{2,1,0:T(1,128)S(1)} %reshape.263), channel_id=1, replica_groups=mesh['wide'=16,'narrow'=2] {'narrow'}, dimensions={0}, use_global_device_ids=true | all-gather | bytes 373248 | tf_op jit(solution)/shard_map/all_gather | solution.py:77
  218.7 0.8 multiply_reduce_fusion
  219.5 1.0 mul.61
  (53 shorter events, 5.5 us)
Async XLA Ops:
  7.2 204.8 %all-reduce.5.cloned.1.call-start = ((), (), s32[]{:S(2)}) async-start(), calls=%async_computation | async-start | bytes 7962624
  9.2 13.0 %collective-permute-start = (bf16[1,8,8,192]{3,2,1,0:T(8,128)(2,1)S(1)}, bf16[1,8,8,192]{3,2,1,0:T(8,128)(2,1)S(1)}, u32[]{:S(2)}, u32[]{:S(2)}) collective-permute-start(bf16[1,8,8,192]{3,2,1,0:T(8,128)(2,1)S(1)} %get-tuple-element.68), channel_id=1, source_target_pairs={{0,2},{2,4},{4,6},{6,8},{8,10},{10,12},{12,14},{14,16},{16,18},{18... | collective-permute-start | bytes 73736 | tf_op jit(solution)/shard_map/ppermute | solution.py:15
  11.5 10.6 %collective-permute-start.1 = (bf16[1,8,8,192]{3,2,1,0:T(8,128)(2,1)S(1)}, bf16[1,8,8,192]{3,2,1,0:T(8,128)(2,1)S(1)}, u32[]{:S(2)}, u32[]{:S(2)}) collective-permute-start(bf16[1,8,8,192]{3,2,1,0:T(8,128)(2,1)S(1)} %get-tuple-element.69), channel_id=1, source_target_pairs={{2,0},{4,2},{6,4},{8,6},{10,8},{12,10},{14,12},{16,14},{18,16},{20... | collective-permute-start | bytes 73736 | tf_op jit(solution)/shard_map/ppermute | solution.py:17
  22.2 6.5 %collective-permute-start.2 = (bf16[10,1,8,192]{3,2,1,0:T(8,128)(2,1)S(1)}, bf16[10,1,8,192]{3,2,1,0:T(8,128)(2,1)S(1)}, u32[]{:S(2)}, u32[]{:S(2)}) collective-permute-start(bf16[10,1,8,192]{3,2,1,0:T(8,128)(2,1)S(1)} %get-tuple-element.62), channel_id=1, source_target_pairs={{0,1},{2,3},{4,5},{6,7},{8,9},{10,11},{12,13},{14,15},{16,17},{18,... | collective-permute-start | bytes 92168 | tf_op jit(solution)/shard_map/ppermute | solution.py:15
  26.4 5.9 %collective-permute-start.3 = (bf16[10,1,8,192]{3,2,1,0:T(8,128)(2,1)S(1)}, bf16[10,1,8,192]{3,2,1,0:T(8,128)(2,1)S(1)}, u32[]{:S(2)}, u32[]{:S(2)}) collective-permute-start(bf16[10,1,8,192]{3,2,1,0:T(8,128)(2,1)S(1)} %get-tuple-element.63), channel_id=1, source_target_pairs={{1,0},{3,2},{5,4},{7,6},{9,8},{11,10},{13,12},{15,14},{17,16},{19,... | collective-permute-start | bytes 92168 | tf_op jit(solution)/shard_map/ppermute | solution.py:17
  36.1 10.0 %copy-start.1 = (bf16[5184,192]{0,1:T(8,128)(2,1)S(1)}, bf16[5184,192]{0,1:T(8,128)(2,1)}, u32[]{:S(2)}) copy-start(bf16[5184,192]{0,1:T(8,128)(2,1)} %param.5) | copy-start | bytes 5971972
  51.0 17.5 %collective-permute-start.5 = (bf16[1,8,8,192]{3,2,1,0:T(8,128)(2,1)S(1)}, bf16[1,8,8,192]{3,2,1,0:T(8,128)(2,1)S(1)}, u32[]{:S(2)}, u32[]{:S(2)}) collective-permute-start(bf16[1,8,8,192]{3,2,1,0:T(8,128)(2,1)S(1)} %bitcast.133), channel_id=1, source_target_pairs={{2,0},{4,2},{6,4},{8,6},{10,8},{12,10},{14,12},{16,14},{18,16},{20... | collective-permute-start | bytes 73736 | tf_op jit(solution)/shard_map/ppermute | solution.py:17
  52.3 16.2 %collective-permute-start.4 = (bf16[1,8,8,192]{3,2,1,0:T(8,128)(2,1)S(1)}, bf16[1,8,8,192]{3,2,1,0:T(8,128)(2,1)S(1)}, u32[]{:S(2)}, u32[]{:S(2)}) collective-permute-start(bf16[1,8,8,192]{3,2,1,0:T(8,128)(2,1)S(1)} %bitcast.132), channel_id=1, source_target_pairs={{0,2},{2,4},{4,6},{6,8},{8,10},{10,12},{12,14},{14,16},{16,18},{18... | collective-permute-start | bytes 73736 | tf_op jit(solution)/shard_map/ppermute | solution.py:15
  68.6 5.1 %collective-permute-start.6 = (bf16[10,1,8,192]{3,2,1,0:T(8,128)(2,1)S(1)}, bf16[10,1,8,192]{3,2,1,0:T(8,128)(2,1)S(1)}, u32[]{:S(2)}, u32[]{:S(2)}) collective-permute-start(bf16[10,1,8,192]{3,2,1,0:T(8,128)(2,1)S(1)} %get-tuple-element.58), channel_id=1, source_target_pairs={{0,1},{2,3},{4,5},{6,7},{8,9},{10,11},{12,13},{14,15},{16,17},{18,... | collective-permute-start | bytes 92168 | tf_op jit(solution)/shard_map/ppermute | solution.py:15
  70.5 5.9 %collective-permute-start.7 = (bf16[10,1,8,192]{3,2,1,0:T(8,128)(2,1)S(1)}, bf16[10,1,8,192]{3,2,1,0:T(8,128)(2,1)S(1)}, u32[]{:S(2)}, u32[]{:S(2)}) collective-permute-start(bf16[10,1,8,192]{3,2,1,0:T(8,128)(2,1)S(1)} %get-tuple-element.59), channel_id=1, source_target_pairs={{1,0},{3,2},{5,4},{7,6},{9,8},{11,10},{13,12},{15,14},{17,16},{19,... | collective-permute-start | bytes 92168 | tf_op jit(solution)/shard_map/ppermute | solution.py:17
  84.7 4.1 %copy-start.2 = (bf16[512,192]{0,1:T(8,128)(2,1)S(1)}, bf16[512,192]{0,1:T(8,128)(2,1)}, u32[]{:S(2)}) copy-start(bf16[512,192]{0,1:T(8,128)(2,1)} %copy.64) | copy-start | bytes 589828
  88.8 36.4 %copy-start = (bf16[27,192,192]{2,1,0:T(8,128)(2,1)S(1)}, bf16[27,192,192]{2,1,0:T(8,128)(2,1)}, u32[]{:S(2)}) copy-start(bf16[27,192,192]{2,1,0:T(8,128)(2,1)} %copy.78) | copy-start | bytes 5971972
  88.9 2.7 %copy-start.3 = (bf16[512,5184]{0,1:T(8,128)(2,1)}, bf16[512,5184]{0,1:T(8,128)(2,1)S(1)}, u32[]{:S(2)}) copy-start(bf16[512,5184]{0,1:T(8,128)(2,1)S(1)} %constant_dynamic-update-slice_fusion.12) | copy-start | bytes 15925252
Sparse Core Ops, SparseCore 0:
  67.9 144.0 all-reduce.4
where the time goes:
time: 229 us; the launch traced here: 227 us
  waiting for transfers between devices  88.6 us (39%)
  local copies, waits for them, and re-layouts  81.2 us (35%)
  starting transfers between devices  17.4 us (8%)
  between operations  14.5 us (6%)
  matrix products  14.2 us (6%)
  other arithmetic  5.93 us (3%)
  blocking collectives  5.57 us (2%)
    unnamed x2, waiting for transfers between devices  82.1 us
    unnamed x37, local copies, waits for them, and re-layouts  27.6 us
    reshape x26, local copies, waits for them, and re-layouts, gather_taps(): pieces.append(piece.reshape(-1, channels))  21.9 us
    ppermute x4, starting transfers between devices, padded_2(): lax.ppermute(tail, axis, [(i, (i + 1) % count) for i in range(ends)])  12 us
    concatenate x2, local copies, waits for them, and re-layouts, gather_taps(): return jnp.concatenate(pieces, axis=1)  11.6 us
    slice x5, local copies, waits for them, and re-layouts, gather_taps(): padded[start_x:start_x + width_x, start_y:start_y + width_y, start_z:star...  6.54 us
    ppermute x4, waiting for transfers between devices, padded_2(): lax.ppermute(head, axis, [((i + 1) % count, i) for i in range(ends)])  6.42 us
    reshape x1, local copies, waits for them, and re-layouts, local(): whole.reshape(-1)  5.96 us
  transfers between devices with their start and end apart: 9, of which 3 were waited for; matrix products, arithmetic and copies ran while one was open for 33% of the time, Pallas kernels for 0%

commit v1 on v0

--- a/solution.py
+++ b/solution.py
@@ -1,7 +1,300 @@
+import functools
+
 import jax
 import jax.numpy as jnp
 from jax import lax
+from jax.experimental import pallas as pl
+from jax.experimental.pallas import tpu as pltpu
+from jax.sharding import Mesh
 from jax.sharding import PartitionSpec as P
+
+WIDE = ("depth", "quad")
+QUAD = 4
+VMEM_BYTES = 56 * 1024 * 1024
+OFFSETS = (-1, 0, 1)
+
+
+def shift_z(field, step):
+    if step == 0:
+        return field
+    depth = field.shape[1]
+    moved = pltpu.roll(field, (-step) % depth, 1)
+    z = lax.broadcasted_iota(jnp.int32, field.shape, 1) + step
+    return jnp.where((z >= 0) & (z < depth), moved, 0.0)
+
+
+def forward_kernel(
+    flags, masked, cot, left, right, low, high, live, weight, pick,
+    act_ref, gp_ref, slices_ref, ext, cols,
+):
+    width, rows, channels = masked.shape
+    depth = 8
+    f32 = jnp.float32
+    use_low = flags[0].astype(f32)
+    use_high = flags[1].astype(f32)
+    tall = rows + 4 * depth
+    mid = rows + 2 * depth
+    span = width + 4
+    strip = span * 2 * depth
+    ext[0:2, 16 : 16 + rows, :] = left[0:2].astype(f32)
+    ext[2 : 2 + width, 16 : 16 + rows, :] = masked[...].astype(f32)
+    ext[2 + width :, 16 : 16 + rows, :] = right[0:2].astype(f32)
+    ext[:, 0:16, :] = low[0:strip].astype(f32).reshape(span, 16, channels) * use_low
+    ext[:, 16 + rows :, :] = high[0:strip].astype(f32).reshape(span, 16, channels) * use_high
+    field = ext[...].reshape(span * tall // depth, depth, channels)
+    for c in OFFSETS:
+        moved = shift_z(field, c).reshape(span, tall, channels)
+        for b in OFFSETS:
+            at = ((b + 1) * 3 + c + 1) * channels
+            start = depth * (b + 1)
+            cols[:, :, at : at + channels] = moved[:, start : start + mid].astype(jnp.bfloat16)
+    nine = 9 * channels
+    pre = jnp.zeros(((width + 2) * mid, channels), f32)
+    for a in range(3):
+        pre += jnp.dot(
+            cols[a : a + width + 2].reshape((width + 2) * mid, nine),
+            weight[a * nine : (a + 1) * nine, :],
+            preferred_element_type=f32,
+        )
+    sig = jax.nn.sigmoid(pre)
+    act = (pre * sig).reshape(width + 2, mid, channels)[1 : 1 + width, depth : depth + rows]
+    act_ref[...] = (act * live[...]).astype(jnp.bfloat16)
+    slope = (sig * (1.0 + pre * (1.0 - sig))).reshape(width + 2, mid, channels)
+    low_cot = low[strip:].astype(f32).reshape(width + 2, depth, channels) * use_low
+    high_cot = high[strip:].astype(f32).reshape(width + 2, depth, channels) * use_high
+    centre = jnp.concatenate([left[2:3], cot[...], right[2:3]], axis=0).astype(f32)
+    full = jnp.concatenate([low_cot, centre, high_cot], axis=1)
+    grad = (full * slope).astype(jnp.bfloat16)
+    gp_ref[...] = grad
+    inner = (full * slope)[:, depth : depth + rows].astype(jnp.bfloat16)
+    turned = lax.dot_general(
+        pick[...],
+        inner.reshape((width + 2) * rows, channels),
+        (((1,), (1,)), ((), ())),
+        preferred_element_type=f32,
+    )
+    slices_ref[...] = turned.reshape(slices_ref.shape).astype(jnp.bfloat16)
+
+
+def input_kernel(gp, live, weight, out_ref, cols):
+    width, rows, channels = out_ref.shape
+    depth = 8
+    f32 = jnp.float32
+    tall = rows + 2 * depth
+    field = gp[...].astype(f32).reshape((width + 2) * tall // depth, depth, channels)
+    for c in OFFSETS:
+        moved = shift_z(field, -c).reshape(width + 2, tall, channels)
+        for b in OFFSETS:
+            at = ((b + 1) * 3 + c + 1) * channels
+            start = depth * (1 - b)
+            cols[:, :, at : at + channels] = moved[:, start : start + rows].astype(jnp.bfloat16)
+    nine = 9 * channels
+    total = jnp.zeros((width * rows, channels), f32)
+    for a in range(3):
+        total += jnp.dot(
+            cols[2 - a : 2 - a + width].reshape(width * rows, nine),
+            weight[a * nine : (a + 1) * nine, :],
+            preferred_element_type=f32,
+        )
+    out_ref[...] = (total.reshape(width, rows, channels) * live[...]).astype(jnp.bfloat16)
+
+
+def kernel_grad_kernel(place, slices, masked, own_ref, one_ref, two_ref, three_ref, cols, part):
+    f32 = jnp.float32
+    members, group, lanes = slices.shape
+    slabs, lane, channels = masked.shape
+    per = slabs // QUAD
+    depth = 8
+    at = lax.broadcasted_iota(jnp.int32, (group, lane), 1)
+    y, z = at // depth, at % depth
+    half = lane // 2
+    tall = lane // depth
+    base = [None] * (slabs + 2)
+    for quad in range(QUAD):
+        first = slices[2 * quad].astype(f32)
+        second = slices[2 * quad + 1].astype(f32)
+        for m in range((per + 2) // 2):
+            one = first[:, m * lane : (m + 1) * lane]
+            two = second[:, m * lane : (m + 1) * lane]
+            pair = (
+                jnp.where(at < half, one, pltpu.roll(two, half, 1)),
+                jnp.where(at < half, pltpu.roll(one, half, 1), two),
+            )
+            for odd in range(2):
+                k = 2 * m + odd
+                slab = quad * per + k
+                inside = 1 <= k <= per
+                edge = (quad == 0 and k == 0) or (quad == QUAD - 1 and k == per + 1)
+                if inside or edge:
+                    base[slab] = pair[odd]
+    for slab in range(slabs + 2):
+        pieces = []
+        for b in OFFSETS:
+            for c in OFFSETS:
+                step = (depth * b + c) % lane
+                moved = base[slab] if step == 0 else pltpu.roll(base[slab], step, 1)
+                keep = (y - b >= 0) & (y - b < tall) & (z - c >= 0) & (z - c < depth)
+                pieces.append(jnp.where(keep, moved, 0.0))
+        cols[:, slab * lane : (slab + 1) * lane] = jnp.concatenate(pieces, axis=0).astype(
+            jnp.bfloat16
+        )
+    field = masked[...].reshape(slabs * lane, channels)
+    planes, rows, _ = part.shape
+    for a in range(3):
+        start = (2 - a) * lane
+        got = jnp.dot(
+            cols[:, start : start + slabs * lane], field, preferred_element_type=f32
+        ).reshape(9, planes, rows, channels)
+        for plane in range(planes):
+            part[plane, :, a * 9 * channels : (a + 1) * 9 * channels] = jnp.concatenate(
+                [got[tap, plane] for tap in range(9)], axis=1
+            )
+    me = place[0]
+    own_ref[...] = part[me]
+    for step, ref in ((1, one_ref), (2, two_ref), (3, three_ref)):
+        ref[...] = part[lax.rem(me + step, planes)].astype(jnp.bfloat16)
+
+
+def sum_kernel(scale, own, one, two, three, out_ref):
+    f32 = jnp.float32
+    total = own[...] + one[...].astype(f32) + two[...].astype(f32) + three[...].astype(f32)
+    out_ref[...] = total * scale
+
+
+def vmem(count):
+    return [pl.BlockSpec(memory_space=pltpu.VMEM)] * count
+
+
+SMEM = pl.BlockSpec(memory_space=pltpu.SMEM)
+
+
+def params():
+    return pltpu.CompilerParams(vmem_limit_bytes=VMEM_BYTES)
+
+
+def cost(flops, moved):
+    return pl.CostEstimate(flops=flops, bytes_accessed=moved, transcendentals=0)
+
+
+def planes_local(features, weight, voxel_mask, cotangent):
+    bf16 = jnp.bfloat16
+    f32 = jnp.float32
+    width, wide_y, depth, channels = features.shape
+    rows = wide_y * depth
+    planes = lax.axis_size("depth")
+    quads = lax.axis_size("quad")
+    count = planes * quads
+    plane = lax.axis_index("depth")
+    side = lax.axis_index("narrow")
+    sides = lax.axis_size("narrow")
+
+    live = voxel_mask.reshape(width, rows, 1)
+    masked = features.reshape(width, rows, channels) * live.astype(bf16)
+    cot = cotangent.reshape(width, rows, channels) * live.astype(bf16)
+    live = live.astype(f32)
+
+    up = [(i, i + 1) for i in range(count - 1)]
+    down = [(i + 1, i) for i in range(count - 1)]
+    left = lax.ppermute(jnp.concatenate([masked[-2:], cot[-1:]], axis=0), WIDE, up)
+    right = lax.ppermute(jnp.concatenate([masked[:2], cot[:1]], axis=0), WIDE, down)
+
+    halo = 2 * depth
+    wide_masked = jnp.concatenate([left[:2], masked, right[:2]], axis=0)
+    wide_cot = jnp.concatenate([left[2:], cot, right[2:]], axis=0)
+
+    def strip(first):
+        if first:
+            parts = wide_masked[:, :halo], wide_cot[:, :depth]
+        else:
+            parts = wide_masked[:, rows - halo :], wide_cot[:, rows - depth :]
+        return jnp.concatenate([part.reshape(-1, channels) for part in parts], axis=0)
+
+    swapped = lax.ppermute(
+        jnp.where(side == 0, strip(False), strip(True)), "narrow", [(0, 1), (1, 0)]
+    )
+    flags = jnp.stack([side, 1 - side]).astype(jnp.int32)
+
+    group = 4 * 8
+    members = quads * sides
+    per = channels // count
+    share = per // sides
+    index = jnp.arange(members * group)
+    q, s = index // (sides * group), index // group % sides
+    p, r = index // 8 % planes, index % 8
+    source = jnp.where(r < share, per * (quads * p + q) + share * s + r, -1)
+    pick = (source[:, None] == jnp.arange(channels)[None, :]).astype(bf16)
+
+    bricks = lax.all_gather(masked, "narrow", axis=1, tiled=True)
+    bricks = lax.all_gather(bricks, "quad", axis=0, tiled=True)
+
+    span = (width + 2) * rows
+    act, gp, slices = pl.pallas_call(
+        forward_kernel,
+        out_shape=(
+            jax.ShapeDtypeStruct((width, rows, channels), bf16),
+            jax.ShapeDtypeStruct((width + 2, rows + 2 * depth, channels), bf16),
+            jax.ShapeDtypeStruct((members, group, span), bf16),
+        ),
+        in_specs=[SMEM] + vmem(9),
+        out_specs=tuple(vmem(3)),
+        scratch_shapes=[
+            pltpu.VMEM((width + 4, rows + 4 * depth, channels), f32),
+            pltpu.VMEM((width + 4, rows + 2 * depth, 9 * channels), bf16),
+        ],
+        compiler_params=params(),
+        cost_estimate=cost(2 * 800 * 5184 * 256, 4 << 20),
+        name="forward",
+    )(flags, masked, cot, left, right, swapped, swapped, live, weight, pick)
+
+    slices = lax.all_to_all(slices, ("quad", "narrow"), 0, 0, tiled=True)
+
+    taps = weight.reshape(27, channels, channels)
+    turned = jnp.transpose(taps, (0, 2, 1)).reshape(27 * channels, channels)
+    grad_input = pl.pallas_call(
+        input_kernel,
+        out_shape=jax.ShapeDtypeStruct((width, rows, channels), bf16),
+        in_specs=vmem(3),
+        out_specs=vmem(1)[0],
+        scratch_shapes=[pltpu.VMEM((width + 2, rows, 9 * channels), bf16)],
+        compiler_params=params(),
+        cost_estimate=cost(2 * 512 * 5184 * 256, 4 << 20),
+        name="input_gradient",
+    )(gp, live, turned)
+
+    total = 27 * channels
+    place = plane.reshape(1).astype(jnp.int32)
+    small = jax.ShapeDtypeStruct((8, total), bf16)
+    own, *sends = pl.pallas_call(
+        kernel_grad_kernel,
+        out_shape=(jax.ShapeDtypeStruct((8, total), f32), small, small, small),
+        in_specs=[SMEM] + vmem(2),
+        out_specs=tuple(vmem(4)),
+        scratch_shapes=[
+            pltpu.VMEM((9 * group, (quads * width + 2) * sides * rows), bf16),
+            pltpu.VMEM((planes, 8, total), f32),
+        ],
+        compiler_params=params(),
+        cost_estimate=cost(2 * 288 * 3 * 4096 * 256, 4 << 20),
+        name="kernel_gradient",
+    )(place, slices, bricks)
+
+    got = [
+        lax.ppermute(sent, "depth", [(i, (i + step) % planes) for i in range(planes)])
+        for step, sent in zip((1, 2, 3), sends)
+    ]
+    voxels = count * sides * width * rows
+    mine = pl.pallas_call(
+        functools.partial(sum_kernel, float(1.0 / voxels**0.5)),
+        out_shape=jax.ShapeDtypeStruct((8, total), f32),
+        in_specs=vmem(4),
+        out_specs=vmem(1)[0],
+        compiler_params=params(),
+        cost_estimate=cost(8 * total * 4, 8 * total * 14),
+        name="plane_sum",
+    )(own, *got)
+    grad_weight = lax.all_gather(mine[:share], "narrow", axis=0, tiled=True)
+    shape = features.shape
+    return act.reshape(shape), grad_input.reshape(shape), grad_weight
 
 
 def padded_2(cells, sides, width):
@@ -39,7 +332,7 @@
     return jnp.concatenate(pieces, axis=1)
 
 
-def local(features, weight, voxel_mask, cotangent):
+def summed_local(features, weight, voxel_mask, cotangent):
     width_x, width_y, depth_z, channels = features.shape
     masked = features * voxel_mask.astype(jnp.bfloat16)[..., None]
     padded = padded_2(masked, (("wide", 0), ("narrow", 1)), 1)
@@ -80,20 +373,30 @@
     return (activation, grad_input, grad_weight)
 
 
-def solution(mesh):
+def sharded(body, mesh, wide):
     return jax.shard_map(
-        local,
+        body,
         mesh=mesh,
         in_specs=(
-            P("wide", "narrow", None, None),
+            P(wide, "narrow", None, None),
             P(),
-            P("wide", "narrow", None),
-            P("wide", "narrow", None, None),
+            P(wide, "narrow", None),
+            P(wide, "narrow", None, None),
         ),
         out_specs=(
-            P("wide", "narrow", None, None),
-            P("wide", "narrow", None, None),
-            P("wide", None),
+            P(wide, "narrow", None, None),
+            P(wide, "narrow", None, None),
+            P(wide, None),
         ),
         check_vma=False,
     )
+
+
+def solution(mesh):
+    wide, narrow = mesh.shape["wide"], mesh.shape["narrow"]
+    if wide != 4 * QUAD or narrow != 2:
+        return sharded(summed_local, mesh, "wide")
+    planes = Mesh(
+        mesh.devices.reshape(wide // QUAD, QUAD, narrow), ("depth", "quad", "narrow")
+    )
+    return sharded(planes_local, planes, WIDE)

time: 229 us -> 90.3 us (0.39)
  waiting for transfers between devices: 88.6 us -> 3.35 us
  local copies, waits for them, and re-layouts: 81.2 us -> 16.5 us
  Pallas kernels: 0 us -> 17.8 us
  matrix products: 14.2 us -> 0 us
  blocking collectives: 5.57 us -> 16.8 us
    unnamed x2 -> x1, waiting for transfers between devices: 82.1 us -> 0.02 us
    reshape x27 -> x0, local copies, waits for them, and re-layouts: 27.9 us -> none  [the longest x26 21.9 us: gather_taps(): pieces.append(piece.reshape(-1, channels))]
    unnamed x37 -> x25, local copies, waits for them, and re-layouts: 27.6 us -> 7.25 us
    pallas_call x0 -> x4, Pallas kernels: none -> 17.8 us  [the longest x1 6.12 us: planes_local(): pl.pallas_call(forward_kernel, out_shape=(jax.ShapeDtypeStruct((width, ro...]
    dot_general x3 -> x0, matrix products: 14.2 us -> none  [the longest x1 5.75 us: local(): lax.dot_general(grad_pre, columns, (((0,), (0,)), ((), ())), preferred_el...]
    concatenate x2 -> x0, local copies, waits for them, and re-layouts: 11.6 us -> none  [gather_taps(): return jnp.concatenate(pieces, axis=1)]
    all_gather x1 -> x2, blocking collectives: 5.57 us -> 16.8 us  [the longest x1 9.94 us: planes_local(): bricks = lax.all_gather(masked, 'narrow', axis=1, tiled=True)]
    all_to_all x0 -> x1, starting transfers between devices: none -> 7.38 us  [planes_local(): slices = lax.all_to_all(slices, ('quad', 'narrow'), 0, 0, tiled=True)]
  transfers between devices with their start and end apart: 9 -> 8, of which waited for: 3 -> 2; matrix products, arithmetic and copies ran while one was open for 33% -> 15% of each run, Pallas kernels for 0% -> 12%
where the time goes in v1:
time: 90.3 us; the launch traced here: 89.8 us
  Pallas kernels  17.8 us (20%)
  starting transfers between devices  17.5 us (19%)
  blocking collectives  16.8 us (19%)
  local copies, waits for them, and re-layouts  16.5 us (18%)
  between operations  14.2 us (16%)
  other arithmetic  3.7 us (4%)
  waiting for transfers between devices  3.35 us (4%)
    all_gather x1, blocking collectives, planes_local(): bricks = lax.all_gather(masked, 'narrow', axis=1, tiled=True)  9.94 us
    all_to_all x1, starting transfers between devices, planes_local(): slices = lax.all_to_all(slices, ('quad', 'narrow'), 0, 0, tiled=True)  7.38 us
    unnamed x25, local copies, waits for them, and re-layouts  7.25 us
    all_gather x1, blocking collectives, planes_local(): grad_weight = lax.all_gather(mine[:share], 'narrow', axis=0, tiled=True)  6.81 us
    pallas_call x1, Pallas kernels, planes_local(): pl.pallas_call(forward_kernel, out_shape=(jax.ShapeDtypeStruct((width, ro...  6.12 us
    ppermute x3, starting transfers between devices, planes_local(): lax.ppermute(sent, 'depth', [(i, (i + step) % planes) for i in range(plan...  5.72 us
    pallas_call x1, Pallas kernels, planes_local(): pl.pallas_call(kernel_grad_kernel, out_shape=(jax.ShapeDtypeStruct((8, to...  5.54 us
    pallas_call x1, Pallas kernels, planes_local(): pl.pallas_call(input_kernel, out_shape=jax.ShapeDtypeStruct((width, rows,...  4.34 us
  transfers between devices with their start and end apart: 8, of which 2 were waited for; matrix products, arithmetic and copies ran while one was open for 15% of the time, Pallas kernels for 12%

profile of v1, /device:TPU:0, one launch (start us, length us, event | category | flops | bytes accessed | tf_op | source)
XLA Modules:
  0.0 89.8 jit_solution(1978128762467349448)
XLA Ops:
  7.2 0.0 all-gather.3.cloned.1.call-start
  7.2 0.8 fusion.15
  8.1 0.1 convert_element_type.21
  8.1 0.0 copy-start.2
  8.1 1.3 %bitcast_multiply_fusion = (bf16[8,64,192]{2,1,0:T(8,128)(2,1)S(1)}, bf16[8,64,192]{2,1,0:T(8,128)(2,1)S(1)}) fusion(bf16[8,8,8,192]{3,2,1,0:T(8,128)(2,1)} %param.7, bf16[8,64]{1,0:T(8,128)(2,1)S(1)} %convert_element_type.21, bf16[8,8,8,192]{3,2,1,0:T(8,128)(2,1)} %param.4), kind=kLoop, calls=%fused_computation | loop fusion | flops 196608 | bytes 787456 | tf_op jit(solution)/shard_map/mul | solution.py:193
  9.5 0.0 copy-start.3
  9.5 0.0 copy-start.1
  9.5 9.9 %all_gather.9 = bf16[8,128,192]{2,1,0:T(8,128)(2,1)S(1)} all-gather(bf16[8,64,192]{2,1,0:T(8,128)(2,1)S(1)} %get-tuple-element.28.masked), channel_id=1, replica_groups=mesh['depth'=4,'quad'=4,'narrow'=2] {'narrow'}, dimensions={1}, use_global_device_ids=true | all-gather | bytes 589824 | tf_op jit(solution)/shard_map/all_gather | solution.py:227
  19.4 0.9 %copy.19 = bf16[8,128,192]{1,2,0:T(8,128)(2,1)} copy(bf16[8,128,192]{2,1,0:T(8,128)(2,1)S(1)} %all_gather.9) | data formatting | bytes 786432 | tf_op jit(solution)/shard_map/all_gather | solution.py:227
  20.4 0.0 all-gather.3.cloned.1.call-update
  20.5 1.3 %collective-permute-start = (bf16[3,64,192]{2,1,0:T(8,128)(2,1)S(1)}, bf16[3,64,192]{2,1,0:T(8,128)(2,1)S(1)}, u32[]{:S(2)}, u32[]{:S(2)}) collective-permute-start(bf16[3,64,192]{2,1,0:T(8,128)(2,1)S(1)} %pad_maximum_fusion.3), channel_id=1, source_target_pairs={{0,2},{2,4},{4,6},{6,8},{8,10},{10,12},{12,14},{14,16},{16,18},{18... | collective-permute-start | bytes 221192 | tf_op jit(solution)/shard_map/ppermute | solution.py:198
  21.8 1.3 %collective-permute-start.1 = (bf16[3,64,192]{2,1,0:T(8,128)(2,1)S(1)}, bf16[3,64,192]{2,1,0:T(8,128)(2,1)S(1)}, u32[]{:S(2)}, u32[]{:S(2)}) collective-permute-start(bf16[3,64,192]{2,1,0:T(8,128)(2,1)S(1)} %pad_maximum_fusion.4), channel_id=1, source_target_pairs={{2,0},{4,2},{6,4},{8,6},{10,8},{12,10},{14,12},{16,14},{18,16},{20... | collective-permute-start | bytes 221192 | tf_op jit(solution)/shard_map/ppermute | solution.py:199
  23.1 0.8 fusion.pick
  23.9 0.9 convert_element_type.25.live
  24.7 0.0 copy-done.2
  24.7 3.5 %copy.15.weight = bf16[5184,192]{1,0:T(8,128)(2,1)} copy(bf16[5184,192]{0,1:T(8,128)(2,1)S(1)} %copy-done.2) | data formatting | bytes 3981312 | tf_op args[1]
  28.2 0.0 collective-permute-done.1.right
  28.2 0.0 copy-start.6
  28.2 0.0 collective-permute-done.left
  28.3 0.0 copy-start.5
  28.3 0.0 copy-done.3
  28.3 0.0 copy-done.1
  28.4 1.8 %collective-permute-start.2 = (bf16[272,192]{1,0:T(8,128)(2,1)S(1)}, bf16[272,192]{1,0:T(8,128)(2,1)S(1)}, u32[]{:S(2)}, u32[]{:S(2)}) collective-permute-start(bf16[272,192]{1,0:T(8,128)(2,1)S(1)} %maximum_select_fusion), channel_id=1, source_target_pairs={{0,1},{1,0},{2,3},{3,2},{4,5},{5,4},{6,7},{7,6},{8,9},{9,8},{10,11... | collective-permute-start | bytes 313352 | tf_op jit(solution)/shard_map/ppermute | solution.py:212
  30.2 0.7 pad_add_fusion.flags
  30.9 2.7 %collective-permute-done.2.low.high = bf16[272,192]{1,0:T(8,128)(2,1)S(1)} collective-permute-done((bf16[272,192]{1,0:T(8,128)(2,1)S(1)}, bf16[272,192]{1,0:T(8,128)(2,1)S(1)}, u32[]{:S(2)}, u32[]{:S(2)}) %collective-permute-start.2) | collective-permute-done | bytes 104480 | tf_op jit(solution)/shard_map/ppermute | solution.py:212
  33.6 0.0 copy-done.6
  33.6 0.0 copy-done.5
  33.6 0.0 copy-start.10
  33.6 0.6 copy-done.10
  34.2 0.0 copy-start
  34.2 6.1 %forward.1 = (bf16[8,64,192]{2,1,0:T(8,128)(2,1)}, bf16[10,80,192]{2,1,0:T(8,128)(2,1)}, bf16[8,32,640]{2,1,0:T(8,128)(2,1)}) custom-call(s32[2]{0:T(128)} %pad_add_fusion.flags, bf16[8,64,192]{2,1,0:T(8,128)(2,1)} %copy-done.1, bf16[8,64,192]{2,1,0:T(8,128)(2,1)} %copy-done.3, bf16[3,64,192]{2,1,0:T(8,128)(2,1)} %copy-done.5, ...), custom_call_target="tpu_custom_call" | custom-call | flops 2123366400 | bytes 4194304 | tf_op jit(solution)/shard_map/forward/pallas_call | solution.py:231
  40.3 7.4 %all-to-all-start = ((bf16[8,32,640]{2,1,0:T(8,128)(2,1)}), bf16[8,32,640]{2,1,0:T(8,128)(2,1)S(1)}, u32[]{:S(2)}, u32[]{:S(2)}) async-start(bf16[8,32,640]{2,1,0:T(8,128)(2,1)} %get-tuple-element.12), calls=%async_computation | async-start | bytes 655360 | tf_op jit(solution)/shard_map/all_to_all | solution.py:249
  47.7 0.0 copy-done
  47.7 3.4 %copy.17 = bf16[27,192,192]{2,1,0:T(8,128)(2,1)} copy(bf16[27,192,192]{1,2,0:T(8,128)(2,1)S(1)} %bitcast.21) | data formatting | bytes 3981312 | tf_op jit(solution)/shard_map/transpose | solution.py:252
  51.2 0.0 all-gather.3.cloned.1.call-done
  51.2 3.8 %copy.20.masked = bf16[32,128,192]{2,1,0:T(8,128)(2,1)} copy(bf16[32,128,192]{1,2,0:T(8,128)(2,1)} %all-gather.3.cloned.1.call-done) | data formatting | bytes 3145728 | tf_op jit(solution)/shard_map/all_gather | solution.py:228
  55.0 0.0 all-to-all-done.slices
  55.0 0.0 copy-start.4
  55.0 0.7 copy-done.4
  55.7 5.5 %kernel_gradient.1 = (f32[8,5184]{1,0:T(8,128)}, bf16[8,5184]{1,0:T(8,128)(2,1)}, bf16[8,5184]{1,0:T(8,128)(2,1)}, bf16[8,5184]{1,0:T(8,128)(2,1)}) custom-call(s32[1]{0:T(128)} %bitcast.13.place, bf16[8,32,640]{2,1,0:T(8,128)(2,1)} %copy-done.4, bf16[32,128,192]{2,1,0:T(8,128)(2,1)} %copy.20.masked), custom_call_target="tpu_custom_call" | custom-call | flops 1811939328 | bytes 4194304 | tf_op jit(solution)/shard_map/kernel_gradient/pallas_call | solution.py:267
  61.3 1.8 %collective-permute-start.3 = (bf16[8,5184]{1,0:T(8,128)(2,1)}, bf16[8,5184]{1,0:T(8,128)(2,1)S(1)}, u32[]{:S(2)}, u32[]{:S(2)}) collective-permute-start(bf16[8,5184]{1,0:T(8,128)(2,1)} %get-tuple-element.14), channel_id=1, source_target_pairs={{0,8},{8,16},{16,24},{24,0},{1,9},{9,17},{17,25},{25,1},{2,10},{10... | collective-permute-start | bytes 248840 | tf_op jit(solution)/shard_map/ppermute | solution.py:282
  63.1 2.6 %collective-permute-start.4 = (bf16[8,5184]{1,0:T(8,128)(2,1)}, bf16[8,5184]{1,0:T(8,128)(2,1)S(1)}, u32[]{:S(2)}, u32[]{:S(2)}) collective-permute-start(bf16[8,5184]{1,0:T(8,128)(2,1)} %get-tuple-element.15), channel_id=1, source_target_pairs={{0,16},{8,24},{16,0},{24,8},{1,17},{9,25},{17,1},{25,9},{2,18},{10... | collective-permute-start | bytes 248840 | tf_op jit(solution)/shard_map/ppermute | solution.py:282
  65.6 1.4 %collective-permute-start.5 = (bf16[8,5184]{1,0:T(8,128)(2,1)}, bf16[8,5184]{1,0:T(8,128)(2,1)S(1)}, u32[]{:S(2)}, u32[]{:S(2)}) collective-permute-start(bf16[8,5184]{1,0:T(8,128)(2,1)} %get-tuple-element.16), channel_id=1, source_target_pairs={{0,24},{8,0},{16,8},{24,16},{1,25},{9,1},{17,9},{25,17},{2,26},{10... | collective-permute-start | bytes 248840 | tf_op jit(solution)/shard_map/ppermute | solution.py:282
  67.0 4.3 %input_gradient.1 = bf16[8,64,192]{2,1,0:T(8,128)(2,1)} custom-call(bf16[10,80,192]{2,1,0:T(8,128)(2,1)} %get-tuple-element.11.gp, f32[8,64,1]{2,1,0:T(8,128)} %convert_element_type.25.live, bf16[5184,192]{1,0:T(8,128)(2,1)} %bitcast.22), custom_call_target="tpu_custom_call" | custom-call | flops 1358954496 | bytes 4194304 | tf_op jit(solution)/shard_map/input_gradient/pallas_call | solution.py:253
  71.3 0.0 collective-permute-done.3.one
  71.3 0.0 copy-start.7
  71.3 0.7 collective-permute-done.4.two
  72.0 0.0 copy-start.8
  72.0 0.0 collective-permute-done.5.three
  72.0 0.0 copy-start.9
  72.0 0.0 copy-done.7
  72.0 0.6 copy-done.8
  72.6 0.0 copy-done.9
  72.7 1.8 %plane_sum.1 = f32[8,5184]{1,0:T(8,128)} custom-call(f32[8,5184]{1,0:T(8,128)} %get-tuple-element.13.own, bf16[8,5184]{1,0:T(8,128)(2,1)} %copy-done.7, bf16[8,5184]{1,0:T(8,128)(2,1)} %copy-done.8, bf16[8,5184]{1,0:T(8,128)(2,1)} %copy-done.9), custom_call_target="tpu_custom_call" | custom-call | flops 165888 | bytes 580608 | tf_op jit(solution)/shard_map/plane_sum/pallas_call | solution.py:286
  74.4 0.9 %slice_bitcast_fusion = f32[1,6,5184]{2,1,0:T(8,128)S(1)} fusion(f32[8,5184]{1,0:T(8,128)} %plane_sum.1), kind=kLoop, calls=%fused_computation.4 | loop fusion | bytes 248832
  75.4 6.8 %all-gather = f32[2,6,5184]{2,1,0:T(8,128)S(1)} all-gather(f32[1,6,5184]{2,1,0:T(8,128)S(1)} %slice_bitcast_fusion), channel_id=1, replica_groups=mesh['depth'=4,'quad'=4,'narrow'=2] {'narrow'}, dimensions={0}, use_global_device_ids=true | all-gather | bytes 373248 | tf_op jit(solution)/shard_map/all_gather | solution.py:295
  82.2 0.8 reshape.139
  (12 shorter events, 0.2 us)
Async XLA Ops:
  7.2 44.0 %all-gather.3.cloned.1.call-start = ((), (), s32[]{:S(2)}) async-start(), calls=%async_computation.1 | async-start | bytes 1966080 | tf_op jit(solution)/shard_map/all_gather | solution.py:228
  8.1 16.6 %copy-start.2 = (bf16[5184,192]{0,1:T(8,128)(2,1)S(1)}, bf16[5184,192]{0,1:T(8,128)(2,1)}, u32[]{:S(2)}) copy-start(bf16[5184,192]{0,1:T(8,128)(2,1)} %param.5) | copy-start | bytes 5971972
  9.5 18.8 %copy-start.3 = (bf16[8,64,192]{2,1,0:T(8,128)(2,1)}, bf16[8,64,192]{2,1,0:T(8,128)(2,1)S(1)}, u32[]{:S(2)}) copy-start(bf16[8,64,192]{2,1,0:T(8,128)(2,1)S(1)} %get-tuple-element.27.cot) | copy-start | bytes 589828
  9.5 18.9 %copy-start.1 = (bf16[8,64,192]{2,1,0:T(8,128)(2,1)}, bf16[8,64,192]{2,1,0:T(8,128)(2,1)S(1)}, u32[]{:S(2)}) copy-start(bf16[8,64,192]{2,1,0:T(8,128)(2,1)S(1)} %get-tuple-element.28.masked) | copy-start | bytes 589828
  20.5 7.8 %collective-permute-start = (bf16[3,64,192]{2,1,0:T(8,128)(2,1)S(1)}, bf16[3,64,192]{2,1,0:T(8,128)(2,1)S(1)}, u32[]{:S(2)}, u32[]{:S(2)}) collective-permute-start(bf16[3,64,192]{2,1,0:T(8,128)(2,1)S(1)} %pad_maximum_fusion.3), channel_id=1, source_target_pairs={{0,2},{2,4},{4,6},{6,8},{8,10},{10,12},{12,14},{14,16},{16,18},{18... | collective-permute-start | bytes 221192 | tf_op jit(solution)/shard_map/ppermute | solution.py:198
  21.8 6.4 %collective-permute-start.1 = (bf16[3,64,192]{2,1,0:T(8,128)(2,1)S(1)}, bf16[3,64,192]{2,1,0:T(8,128)(2,1)S(1)}, u32[]{:S(2)}, u32[]{:S(2)}) collective-permute-start(bf16[3,64,192]{2,1,0:T(8,128)(2,1)S(1)} %pad_maximum_fusion.4), channel_id=1, source_target_pairs={{2,0},{4,2},{6,4},{8,6},{10,8},{12,10},{14,12},{16,14},{18,16},{20... | collective-permute-start | bytes 221192 | tf_op jit(solution)/shard_map/ppermute | solution.py:199
  28.2 5.3 %copy-start.6 = (bf16[3,64,192]{2,1,0:T(8,128)(2,1)}, bf16[3,64,192]{2,1,0:T(8,128)(2,1)S(1)}, u32[]{:S(2)}) copy-start(bf16[3,64,192]{2,1,0:T(8,128)(2,1)S(1)} %collective-permute-done.1.right) | copy-start | bytes 221188
  28.3 5.3 %copy-start.5 = (bf16[3,64,192]{2,1,0:T(8,128)(2,1)}, bf16[3,64,192]{2,1,0:T(8,128)(2,1)S(1)}, u32[]{:S(2)}) copy-start(bf16[3,64,192]{2,1,0:T(8,128)(2,1)S(1)} %collective-permute-done.left) | copy-start | bytes 221188
  28.4 5.1 %collective-permute-start.2 = (bf16[272,192]{1,0:T(8,128)(2,1)S(1)}, bf16[272,192]{1,0:T(8,128)(2,1)S(1)}, u32[]{:S(2)}, u32[]{:S(2)}) collective-permute-start(bf16[272,192]{1,0:T(8,128)(2,1)S(1)} %maximum_select_fusion), channel_id=1, source_target_pairs={{0,1},{1,0},{2,3},{3,2},{4,5},{5,4},{6,7},{7,6},{8,9},{9,8},{10,11... | collective-permute-start | bytes 313352 | tf_op jit(solution)/shard_map/ppermute | solution.py:212
  33.6 0.6 copy-start.10
  34.2 13.5 %copy-start = (bf16[5184,192]{1,0:T(8,128)(2,1)S(1)}, bf16[5184,192]{1,0:T(8,128)(2,1)}, u32[]{:S(2)}) copy-start(bf16[5184,192]{1,0:T(8,128)(2,1)} %copy.15.weight) | copy-start | bytes 5971972
  40.3 14.7 %all-to-all-start = ((bf16[8,32,640]{2,1,0:T(8,128)(2,1)}), bf16[8,32,640]{2,1,0:T(8,128)(2,1)S(1)}, u32[]{:S(2)}, u32[]{:S(2)}) async-start(bf16[8,32,640]{2,1,0:T(8,128)(2,1)} %get-tuple-element.12), calls=%async_computation | async-start | bytes 655360 | tf_op jit(solution)/shard_map/all_to_all | solution.py:249
  55.0 0.7 copy-start.4
  61.3 10.1 %collective-permute-start.3 = (bf16[8,5184]{1,0:T(8,128)(2,1)}, bf16[8,5184]{1,0:T(8,128)(2,1)S(1)}, u32[]{:S(2)}, u32[]{:S(2)}) collective-permute-start(bf16[8,5184]{1,0:T(8,128)(2,1)} %get-tuple-element.14), channel_id=1, source_target_pairs={{0,8},{8,16},{16,24},{24,0},{1,9},{9,17},{17,25},{25,1},{2,10},{10... | collective-permute-start | bytes 248840 | tf_op jit(solution)/shard_map/ppermute | solution.py:282
  63.1 9.0 %collective-permute-start.4 = (bf16[8,5184]{1,0:T(8,128)(2,1)}, bf16[8,5184]{1,0:T(8,128)(2,1)S(1)}, u32[]{:S(2)}, u32[]{:S(2)}) collective-permute-start(bf16[8,5184]{1,0:T(8,128)(2,1)} %get-tuple-element.15), channel_id=1, source_target_pairs={{0,16},{8,24},{16,0},{24,8},{1,17},{9,25},{17,1},{25,9},{2,18},{10... | collective-permute-start | bytes 248840 | tf_op jit(solution)/shard_map/ppermute | solution.py:282
  65.6 6.4 %collective-permute-start.5 = (bf16[8,5184]{1,0:T(8,128)(2,1)}, bf16[8,5184]{1,0:T(8,128)(2,1)S(1)}, u32[]{:S(2)}, u32[]{:S(2)}) collective-permute-start(bf16[8,5184]{1,0:T(8,128)(2,1)} %get-tuple-element.16), channel_id=1, source_target_pairs={{0,24},{8,0},{16,8},{24,16},{1,25},{9,1},{17,9},{25,17},{2,26},{10... | collective-permute-start | bytes 248840 | tf_op jit(solution)/shard_map/ppermute | solution.py:282
  71.3 0.7 copy-start.7
  72.0 0.6 copy-start.8
  72.0 0.7 copy-start.9
Sparse Core Ops, SparseCore 0:
  20.5 21.1 all-gather.2

commit v2 on v1

--- a/solution.py
+++ b/solution.py
@@ -23,9 +23,24 @@
     return jnp.where((z >= 0) & (z < depth), moved, 0.0)
 
 
+def prepare_kernel(place, features, cot, mask, masked_ref, cot_ref, live_ref, near_ref, far_ref):
+    width, rows, channels = features.shape
+    depth = mask.shape[2]
+    f32 = jnp.float32
+    flat = mask[...].astype(f32).reshape(width * rows // depth, depth)
+    live = jnp.broadcast_to(flat[:, :, None], flat.shape + (channels,)).reshape(features.shape)
+    live_ref[...] = live[:, :, :128]
+    masked_ref[...] = (features[...].astype(f32) * live).astype(jnp.bfloat16)
+    cot_ref[...] = (cot[...].astype(f32) * live).astype(jnp.bfloat16)
+    odd = place[0]
+    for ref, upper in ((near_ref, 1 - odd), (far_ref, odd)):
+        ref[0:2] = masked_ref[pl.ds(upper * (width - 2), 2)]
+        ref[2:3] = cot_ref[pl.ds(upper * (width - 1), 1)]
+
+
 def forward_kernel(
-    flags, masked, cot, left, right, low, high, live, weight, pick,
-    act_ref, gp_ref, slices_ref, ext, cols,
+    flags, masked, cot, near, far, low, high, live, weight, pick,
+    act_ref, gp_ref, slices_ref, ext, edge, cols,
 ):
     width, rows, channels = masked.shape
     depth = 8
@@ -36,9 +51,12 @@
     mid = rows + 2 * depth
     span = width + 4
     strip = span * 2 * depth
-    ext[0:2, 16 : 16 + rows, :] = left[0:2].astype(f32)
+    odd = flags[2]
+    edge[odd] = far[...]
+    edge[1 - odd] = near[...]
+    ext[0:2, 16 : 16 + rows, :] = edge[0, 0:2].astype(f32)
     ext[2 : 2 + width, 16 : 16 + rows, :] = masked[...].astype(f32)
-    ext[2 + width :, 16 : 16 + rows, :] = right[0:2].astype(f32)
+    ext[2 + width :, 16 : 16 + rows, :] = edge[1, 0:2].astype(f32)
     ext[:, 0:16, :] = low[0:strip].astype(f32).reshape(span, 16, channels) * use_low
     ext[:, 16 + rows :, :] = high[0:strip].astype(f32).reshape(span, 16, channels) * use_high
     field = ext[...].reshape(span * tall // depth, depth, channels)
@@ -58,11 +76,11 @@
         )
     sig = jax.nn.sigmoid(pre)
     act = (pre * sig).reshape(width + 2, mid, channels)[1 : 1 + width, depth : depth + rows]
-    act_ref[...] = (act * live[...]).astype(jnp.bfloat16)
+    act_ref[...] = (act * live[:, :, 0:1]).astype(jnp.bfloat16)
     slope = (sig * (1.0 + pre * (1.0 - sig))).reshape(width + 2, mid, channels)
     low_cot = low[strip:].astype(f32).reshape(width + 2, depth, channels) * use_low
     high_cot = high[strip:].astype(f32).reshape(width + 2, depth, channels) * use_high
-    centre = jnp.concatenate([left[2:3], cot[...], right[2:3]], axis=0).astype(f32)
+    centre = jnp.concatenate([edge[0, 2:3], cot[...], edge[1, 2:3]], axis=0).astype(f32)
     full = jnp.concatenate([low_cot, centre, high_cot], axis=1)
     grad = (full * slope).astype(jnp.bfloat16)
     gp_ref[...] = grad
@@ -76,11 +94,15 @@
     slices_ref[...] = turned.reshape(slices_ref.shape).astype(jnp.bfloat16)
 
 
-def input_kernel(gp, live, weight, out_ref, cols):
+def input_kernel(gp, live, turned, out_ref, cols, weight):
     width, rows, channels = out_ref.shape
     depth = 8
     f32 = jnp.float32
     tall = rows + 2 * depth
+    for tap in range(27):
+        weight[tap * channels : (tap + 1) * channels, :] = turned[
+            :, tap * channels : (tap + 1) * channels
+        ]
     field = gp[...].astype(f32).reshape((width + 2) * tall // depth, depth, channels)
     for c in OFFSETS:
         moved = shift_z(field, -c).reshape(width + 2, tall, channels)
@@ -96,18 +118,28 @@
             weight[a * nine : (a + 1) * nine, :],
             preferred_element_type=f32,
         )
-    out_ref[...] = (total.reshape(width, rows, channels) * live[...]).astype(jnp.bfloat16)
-
-
-def kernel_grad_kernel(place, slices, masked, own_ref, one_ref, two_ref, three_ref, cols, part):
+    out_ref[...] = (total.reshape(width, rows, channels) * live[:, :, 0:1]).astype(jnp.bfloat16)
+
+
+def kernel_grad_kernel(place, slices, bricks, own_ref, one_ref, two_ref, three_ref, cols, part, masked, sems):
     f32 = jnp.float32
     members, group, lanes = slices.shape
     slabs, lane, channels = masked.shape
     per = slabs // QUAD
+    half = lane // 2
+    copies = [
+        pltpu.make_async_copy(
+            bricks.at[pl.ds(member * per, per)],
+            masked.at[pl.ds(member // 2 * per, per), pl.ds(member % 2 * half, half)],
+            sems.at[member],
+        )
+        for member in range(members)
+    ]
+    for copy in copies:
+        copy.start()
     depth = 8
     at = lax.broadcasted_iota(jnp.int32, (group, lane), 1)
     y, z = at // depth, at % depth
-    half = lane // 2
     tall = lane // depth
     base = [None] * (slabs + 2)
     for quad in range(QUAD):
@@ -138,6 +170,8 @@
         cols[:, slab * lane : (slab + 1) * lane] = jnp.concatenate(pieces, axis=0).astype(
             jnp.bfloat16
         )
+    for copy in copies:
+        copy.wait()
     field = masked[...].reshape(slabs * lane, channels)
     planes, rows, _ = part.shape
     for a in range(3):
@@ -161,6 +195,14 @@
     out_ref[...] = total * scale
 
 
+def join_kernel(place, mine, other, out_ref):
+    share = out_ref.shape[0] // 2
+    first = jnp.where(place[0] == 0, mine[...], other[...])
+    second = jnp.where(place[0] == 0, other[...], mine[...])
+    out_ref[0:share] = first[:share]
+    out_ref[share:] = second[:share]
+
+
 def vmem(count):
     return [pl.BlockSpec(memory_space=pltpu.VMEM)] * count
 
@@ -188,15 +230,31 @@
     side = lax.axis_index("narrow")
     sides = lax.axis_size("narrow")
 
-    live = voxel_mask.reshape(width, rows, 1)
-    masked = features.reshape(width, rows, channels) * live.astype(bf16)
-    cot = cotangent.reshape(width, rows, channels) * live.astype(bf16)
-    live = live.astype(f32)
-
-    up = [(i, i + 1) for i in range(count - 1)]
-    down = [(i + 1, i) for i in range(count - 1)]
-    left = lax.ppermute(jnp.concatenate([masked[-2:], cot[-1:]], axis=0), WIDE, up)
-    right = lax.ppermute(jnp.concatenate([masked[:2], cot[:1]], axis=0), WIDE, down)
+    odd = lax.axis_index("quad") % 2
+    brick = jax.ShapeDtypeStruct((width, rows, channels), bf16)
+    slab = jax.ShapeDtypeStruct((3, rows, channels), bf16)
+    masked, cot, live, near, far = pl.pallas_call(
+        prepare_kernel,
+        out_shape=(brick, brick, jax.ShapeDtypeStruct((width, rows, 128), f32), slab, slab),
+        in_specs=[SMEM] + vmem(3),
+        out_specs=tuple(vmem(5)),
+        compiler_params=params(),
+        cost_estimate=cost(1 << 20, 1 << 20),
+        name="prepare",
+    )(
+        odd.reshape(1).astype(jnp.int32),
+        features.reshape(width, rows, channels),
+        cotangent.reshape(width, rows, channels),
+        voxel_mask,
+    )
+
+    near = lax.ppermute(near, WIDE, [(i, i ^ 1) for i in range(count)])
+    far = lax.ppermute(
+        far, WIDE, [(i, j) for i in range(count) if 0 <= (j := ((i + 1) ^ 1) - 1) < count]
+    )
+    bricks = lax.all_gather(masked, ("quad", "narrow"), axis=0, tiled=True)
+    left = jnp.where(odd == 1, near, far)
+    right = jnp.where(odd == 1, far, near)
 
     halo = 2 * depth
     wide_masked = jnp.concatenate([left[:2], masked, right[:2]], axis=0)
@@ -212,7 +270,7 @@
     swapped = lax.ppermute(
         jnp.where(side == 0, strip(False), strip(True)), "narrow", [(0, 1), (1, 0)]
     )
-    flags = jnp.stack([side, 1 - side]).astype(jnp.int32)
+    flags = jnp.stack([side, 1 - side, odd]).astype(jnp.int32)
 
     group = 4 * 8
     members = quads * sides
@@ -223,9 +281,6 @@
     p, r = index // 8 % planes, index % 8
     source = jnp.where(r < share, per * (quads * p + q) + share * s + r, -1)
     pick = (source[:, None] == jnp.arange(channels)[None, :]).astype(bf16)
-
-    bricks = lax.all_gather(masked, "narrow", axis=1, tiled=True)
-    bricks = lax.all_gather(bricks, "quad", axis=0, tiled=True)
 
     span = (width + 2) * rows
     act, gp, slices = pl.pallas_call(
@@ -239,27 +294,29 @@
         out_specs=tuple(vmem(3)),
         scratch_shapes=[
             pltpu.VMEM((width + 4, rows + 4 * depth, channels), f32),
+            pltpu.VMEM((2, 3, rows, channels), bf16),
             pltpu.VMEM((width + 4, rows + 2 * depth, 9 * channels), bf16),
         ],
         compiler_params=params(),
         cost_estimate=cost(2 * 800 * 5184 * 256, 4 << 20),
         name="forward",
-    )(flags, masked, cot, left, right, swapped, swapped, live, weight, pick)
+    )(flags, masked, cot, near, far, swapped, swapped, live, weight, pick)
 
     slices = lax.all_to_all(slices, ("quad", "narrow"), 0, 0, tiled=True)
 
-    taps = weight.reshape(27, channels, channels)
-    turned = jnp.transpose(taps, (0, 2, 1)).reshape(27 * channels, channels)
     grad_input = pl.pallas_call(
         input_kernel,
         out_shape=jax.ShapeDtypeStruct((width, rows, channels), bf16),
         in_specs=vmem(3),
         out_specs=vmem(1)[0],
-        scratch_shapes=[pltpu.VMEM((width + 2, rows, 9 * channels), bf16)],
+        scratch_shapes=[
+            pltpu.VMEM((width + 2, rows, 9 * channels), bf16),
+            pltpu.VMEM((27 * channels, channels), bf16),
+        ],
         compiler_params=params(),
         cost_estimate=cost(2 * 512 * 5184 * 256, 4 << 20),
         name="input_gradient",
-    )(gp, live, turned)
+    )(gp, live, weight.T)
 
     total = 27 * channels
     place = plane.reshape(1).astype(jnp.int32)
@@ -267,11 +324,13 @@
     own, *sends = pl.pallas_call(
         kernel_grad_kernel,
         out_shape=(jax.ShapeDtypeStruct((8, total), f32), small, small, small),
-        in_specs=[SMEM] + vmem(2),
+        in_specs=[SMEM] + vmem(1) + [pl.BlockSpec(memory_space=pl.ANY)],
         out_specs=tuple(vmem(4)),
         scratch_shapes=[
             pltpu.VMEM((9 * group, (quads * width + 2) * sides * rows), bf16),
             pltpu.VMEM((planes, 8, total), f32),
+            pltpu.VMEM((quads * width, sides * rows, channels), bf16),
+            pltpu.SemaphoreType.DMA((members,)),
         ],
         compiler_params=params(),
         cost_estimate=cost(2 * 288 * 3 * 4096 * 256, 4 << 20),
@@ -292,7 +351,16 @@
         cost_estimate=cost(8 * total * 4, 8 * total * 14),
         name="plane_sum",
     )(own, *got)
-    grad_weight = lax.all_gather(mine[:share], "narrow", axis=0, tiled=True)
+    other = lax.ppermute(mine, "narrow", [(0, 1), (1, 0)])
+    grad_weight = pl.pallas_call(
+        join_kernel,
+        out_shape=jax.ShapeDtypeStruct((per, total), f32),
+        in_specs=[SMEM] + vmem(2),
+        out_specs=vmem(1)[0],
+        compiler_params=params(),
+        cost_estimate=cost(8 * total, 8 * total * 14),
+        name="join",
+    )(side.reshape(1).astype(jnp.int32), mine, other)
     shape = features.shape
     return act.reshape(shape), grad_input.reshape(shape), grad_weight
 

time: 90.3 us -> 80.8 us (0.89)
  blocking collectives: 16.8 us -> 0 us
  waiting for transfers between devices: 3.35 us -> 15.1 us
  local copies, waits for them, and re-layouts: 16.5 us -> 7.08 us
  Pallas kernels: 17.8 us -> 21.9 us
  starting transfers between devices: 17.5 us -> 20.6 us
  other arithmetic: 3.7 us -> 1.5 us
    all_gather x2 -> x0, blocking collectives: 16.8 us -> none  [the longest x1 9.94 us: planes_local(): bricks = lax.all_gather(masked, 'narrow', axis=1, tiled=True)]
    all_to_all x1, waiting for transfers between devices: 0.01 us -> 6.74 us  [planes_local(): slices = lax.all_to_all(slices, ('quad', 'narrow'), 0, 0, tiled=True)]
    all_gather x2 -> x0, local copies, waits for them, and re-layouts: 4.8 us -> none  [the longest x1 3.85 us: planes_local(): bricks = lax.all_gather(bricks, 'quad', axis=0, tiled=True)]
    ppermute x3, waiting for transfers between devices: 0.67 us -> 5.04 us  [planes_local(): lax.ppermute(sent, 'depth', [(i, (i + step) % planes) for i in range(plan...]
    pallas_call x0 -> x2, Pallas kernels: none -> 3.88 us  [the longest x1 2.12 us: planes_local(): pl.pallas_call(prepare_kernel, out_shape=(brick, brick, jax.ShapeDtypeStr...]
    transpose x1 -> x0, local copies, waits for them, and re-layouts: 3.45 us -> none  [planes_local(): turned = jnp.transpose(taps, (0, 2, 1)).reshape(27 * channels, channels)]
    all_to_all x1, starting transfers between devices: 7.38 us -> 10.4 us  [planes_local(): slices = lax.all_to_all(slices, ('quad', 'narrow'), 0, 0, tiled=True)]
    mul x1 -> x0, other arithmetic: 1.31 us -> none  [planes_local(): cot = cotangent.reshape(width, rows, channels) * live.astype(bf16)]
  transfers between devices with their start and end apart: 8 -> 9, of which waited for: 2 -> 5; matrix products, arithmetic and copies ran while one was open for 15% -> 7% of each run, Pallas kernels for 12% -> 13%
where the time goes in v2:
time: 80.8 us; the launch traced here: 80.4 us
  Pallas kernels  21.9 us (27%)
  starting transfers between devices  20.6 us (25%)
  waiting for transfers between devices  15.1 us (19%)
  between operations  14.2 us (18%)
  local copies, waits for them, and re-layouts  7.08 us (9%)
  other arithmetic  1.5 us (2%)
    all_to_all x1, starting transfers between devices, planes_local(): slices = lax.all_to_all(slices, ('quad', 'narrow'), 0, 0, tiled=True)  10.4 us
    unnamed x21, local copies, waits for them, and re-layouts  7.06 us
    all_to_all x1, waiting for transfers between devices, planes_local(): slices = lax.all_to_all(slices, ('quad', 'narrow'), 0, 0, tiled=True)  6.74 us
    pallas_call x1, Pallas kernels, planes_local(): pl.pallas_call(forward_kernel, out_shape=(jax.ShapeDtypeStruct((width, ro...  5.94 us
    pallas_call x1, Pallas kernels, planes_local(): pl.pallas_call(kernel_grad_kernel, out_shape=(jax.ShapeDtypeStruct((8, to...  5.93 us
    ppermute x3, starting transfers between devices, planes_local(): lax.ppermute(sent, 'depth', [(i, (i + step) % planes) for i in range(plan...  5.39 us
    ppermute x3, waiting for transfers between devices, planes_local(): lax.ppermute(sent, 'depth', [(i, (i + step) % planes) for i in range(plan...  5.04 us
    pallas_call x1, Pallas kernels, planes_local(): pl.pallas_call(input_kernel, out_shape=jax.ShapeDtypeStruct((width, rows,...  4.35 us
  transfers between devices with their start and end apart: 9, of which 5 were waited for; matrix products, arithmetic and copies ran while one was open for 7% of the time, Pallas kernels for 13%

profile of v2, /device:TPU:0, one launch (start us, length us, event | category | flops | bytes accessed | tf_op | source)
XLA Modules:
  0.0 80.4 jit_solution(1351559699723866608)
XLA Ops:
  7.2 0.0 all-gather.2.cloned.1.call-start
  7.2 2.1 %prepare.1 = (bf16[8,64,192]{2,1,0:T(8,128)(2,1)}, bf16[8,64,192]{2,1,0:T(8,128)(2,1)}, f32[8,64,128]{2,1,0:T(8,128)}, bf16[3,64,192]{2,1,0:T(8,128)(2,1)}, bf16[3,64,192]{2,1,0:T(8,128)(2,1)}) custom-call(s32[1]{0:T(128)} %bitcast.2.place, bf16[8,64,192]{2,1,0:T(8,128)(2,1)} %bitcast.18, bf16[8,64,192]{2,1,0:T(8,128)(2,1)} %bitcast.19, s32[8,8,8]{2,1,0:T(8,128)} %mask.1), custom_call_target="tpu_custom_call" | custom-call | flops 1048576 | bytes 1048576 | tf_op jit(solution)/shard_map/prepare/pallas_call | solution.py:236
  9.3 0.0 all-gather.2.cloned.1.call-update
  9.4 0.5 collective-permute-start
  9.9 0.7 collective-permute-start.1
  10.6 0.7 fusion.pick
  11.3 0.0 copy-start.2
  11.3 0.0 copy-start
  11.3 4.3 %copy.8.weight = bf16[5184,192]{1,0:T(8,128)(2,1)} copy(bf16[5184,192]{0,1:T(8,128)(2,1)} %param.5) | data formatting | bytes 3981312 | tf_op args[1]
  15.7 0.0 collective-permute-done.near
  15.7 0.0 copy-start.4
  15.7 0.0 collective-permute-done.1.far
  15.7 0.0 copy-start.5
  15.8 0.0 copy-done.2
  15.8 0.0 copy-done
  15.9 2.6 %collective-permute-start.2 = (bf16[272,192]{1,0:T(8,128)(2,1)S(1)}, bf16[272,192]{1,0:T(8,128)(2,1)S(1)}, u32[]{:S(2)}, u32[]{:S(2)}) collective-permute-start(bf16[272,192]{1,0:T(8,128)(2,1)S(1)} %maximum_select_fusion), channel_id=1, source_target_pairs={{0,1},{1,0},{2,3},{3,2},{4,5},{5,4},{6,7},{7,6},{8,9},{9,8},{10,11... | collective-permute-start | bytes 313352 | tf_op jit(solution)/shard_map/ppermute | solution.py:270
  18.5 0.6 pad_add_fusion.flags
  19.1 2.4 %collective-permute-done.2.low.high = bf16[272,192]{1,0:T(8,128)(2,1)S(1)} collective-permute-done((bf16[272,192]{1,0:T(8,128)(2,1)S(1)}, bf16[272,192]{1,0:T(8,128)(2,1)S(1)}, u32[]{:S(2)}, u32[]{:S(2)}) %collective-permute-start.2) | collective-permute-done | bytes 104480 | tf_op jit(solution)/shard_map/ppermute | solution.py:270
  21.5 0.0 copy-start.9
  21.5 0.0 copy-done.4
  21.6 0.0 copy-done.5
  21.6 0.7 copy-done.9
  22.2 5.9 %forward.1 = (bf16[8,64,192]{2,1,0:T(8,128)(2,1)}, bf16[10,80,192]{2,1,0:T(8,128)(2,1)}, bf16[8,32,640]{2,1,0:T(8,128)(2,1)}) custom-call(s32[3]{0:T(128)} %pad_add_fusion.flags, bf16[8,64,192]{2,1,0:T(8,128)(2,1)} %get-tuple-element.15.masked, bf16[8,64,192]{2,1,0:T(8,128)(2,1)} %get-tuple-element.16.cot, bf16[3,64,192]{2,1,0:T(8,128)(2,1)} %copy-done.4, ...), custom_call_target="tpu_custom_call" | custom-call | flops 2123366400 | bytes 4194304 | tf_op jit(solution)/shard_map/forward/pallas_call | solution.py:286
  28.2 10.4 %all-to-all-start = ((bf16[8,32,640]{2,1,0:T(8,128)(2,1)}), bf16[8,32,640]{2,1,0:T(8,128)(2,1)S(1)}, u32[]{:S(2)}, u32[]{:S(2)}) async-start(bf16[8,32,640]{2,1,0:T(8,128)(2,1)} %get-tuple-element.22), calls=%async_computation | async-start | bytes 655360 | tf_op jit(solution)/shard_map/all_to_all | solution.py:305
  38.5 6.7 %all-to-all-done.slices = bf16[8,32,640]{2,1,0:T(8,128)(2,1)S(1)} async-done(((bf16[8,32,640]{2,1,0:T(8,128)(2,1)}), bf16[8,32,640]{2,1,0:T(8,128)(2,1)S(1)}, u32[]{:S(2)}, u32[]{:S(2)}) %all-to-all-start) | async-done | bytes 327712 | tf_op jit(solution)/shard_map/all_to_all | solution.py:305
  45.3 0.0 copy-start.1
  45.3 0.0 all-gather.2.cloned.1.call-done.bricks
  45.3 0.7 copy-done.1
  46.0 5.9 %kernel_gradient.1 = (f32[8,5184]{1,0:T(8,128)}, bf16[8,5184]{1,0:T(8,128)(2,1)}, bf16[8,5184]{1,0:T(8,128)(2,1)}, bf16[8,5184]{1,0:T(8,128)(2,1)}) custom-call(s32[1]{0:T(128)} %bitcast.12.place, bf16[8,32,640]{2,1,0:T(8,128)(2,1)} %copy-done.1, bf16[64,64,192]{2,1,0:T(8,128)(2,1)} %all-gather.2.cloned.1.call-done.bricks), custom_call_target="tpu_custom_call" | custom-call | flops 1811939328 | bytes 4194304 | tf_op jit(solution)/shard_map/kernel_gradient/pallas_call | solution.py:324
  51.9 1.5 %collective-permute-start.3 = (bf16[8,5184]{1,0:T(8,128)(2,1)}, bf16[8,5184]{1,0:T(8,128)(2,1)S(1)}, u32[]{:S(2)}, u32[]{:S(2)}) collective-permute-start(bf16[8,5184]{1,0:T(8,128)(2,1)} %get-tuple-element.24), channel_id=1, source_target_pairs={{0,8},{8,16},{16,24},{24,0},{1,9},{9,17},{17,25},{25,1},{2,10},{10... | collective-permute-start | bytes 248840 | tf_op jit(solution)/shard_map/ppermute | solution.py:341
  53.5 2.3 %collective-permute-start.4 = (bf16[8,5184]{1,0:T(8,128)(2,1)}, bf16[8,5184]{1,0:T(8,128)(2,1)S(1)}, u32[]{:S(2)}, u32[]{:S(2)}) collective-permute-start(bf16[8,5184]{1,0:T(8,128)(2,1)} %get-tuple-element.25), channel_id=1, source_target_pairs={{0,16},{8,24},{16,0},{24,8},{1,17},{9,25},{17,1},{25,9},{2,18},{10... | collective-permute-start | bytes 248840 | tf_op jit(solution)/shard_map/ppermute | solution.py:341
  55.8 1.5 %collective-permute-start.5 = (bf16[8,5184]{1,0:T(8,128)(2,1)}, bf16[8,5184]{1,0:T(8,128)(2,1)S(1)}, u32[]{:S(2)}, u32[]{:S(2)}) collective-permute-start(bf16[8,5184]{1,0:T(8,128)(2,1)} %get-tuple-element.26), channel_id=1, source_target_pairs={{0,24},{8,0},{16,8},{24,16},{1,25},{9,1},{17,9},{25,17},{2,26},{10... | collective-permute-start | bytes 248840 | tf_op jit(solution)/shard_map/ppermute | solution.py:341
  57.3 2.0 %collective-permute-done.3.one = bf16[8,5184]{1,0:T(8,128)(2,1)S(1)} collective-permute-done((bf16[8,5184]{1,0:T(8,128)(2,1)}, bf16[8,5184]{1,0:T(8,128)(2,1)S(1)}, u32[]{:S(2)}, u32[]{:S(2)}) %collective-permute-start.3) | collective-permute-done | bytes 82976 | tf_op jit(solution)/shard_map/ppermute | solution.py:341
  59.3 0.0 copy-start.6
  59.3 3.0 %collective-permute-done.4.two = bf16[8,5184]{1,0:T(8,128)(2,1)S(1)} collective-permute-done((bf16[8,5184]{1,0:T(8,128)(2,1)}, bf16[8,5184]{1,0:T(8,128)(2,1)S(1)}, u32[]{:S(2)}, u32[]{:S(2)}) %collective-permute-start.4) | collective-permute-done | bytes 82976 | tf_op jit(solution)/shard_map/ppermute | solution.py:341
  62.4 0.0 copy-start.7
  62.4 0.0 collective-permute-done.5.three
  62.4 0.0 copy-start.8
  62.4 0.0 copy-done.6
  62.4 0.6 copy-done.7
  63.0 0.0 copy-done.8
  63.0 1.8 %plane_sum.1.mine = f32[8,5184]{1,0:T(8,128)} custom-call(f32[8,5184]{1,0:T(8,128)} %get-tuple-element.23.own, bf16[8,5184]{1,0:T(8,128)(2,1)} %copy-done.6, bf16[8,5184]{1,0:T(8,128)(2,1)} %copy-done.7, bf16[8,5184]{1,0:T(8,128)(2,1)} %copy-done.8), custom_call_target="tpu_custom_call" | custom-call | flops 165888 | bytes 580608 | tf_op jit(solution)/shard_map/plane_sum/pallas_call | solution.py:345
  64.8 1.1 %collective-permute-start.6 = (f32[8,5184]{1,0:T(8,128)}, f32[8,5184]{1,0:T(8,128)S(1)}, u32[]{:S(2)}, u32[]{:S(2)}) collective-permute-start(f32[8,5184]{1,0:T(8,128)} %plane_sum.1.mine), channel_id=1, source_target_pairs={{0,1},{1,0},{2,3},{3,2},{4,5},{5,4},{6,7},{7,6},{8,9},{9,8},{10,11... | collective-permute-start | bytes 497672 | tf_op jit(solution)/shard_map/ppermute | solution.py:354
  65.8 4.4 %input_gradient.1 = bf16[8,64,192]{2,1,0:T(8,128)(2,1)} custom-call(bf16[10,80,192]{2,1,0:T(8,128)(2,1)} %get-tuple-element.21.gp, f32[8,64,128]{2,1,0:T(8,128)} %get-tuple-element.19.live, bf16[192,5184]{1,0:T(8,128)(2,1)} %bitcast.15), custom_call_target="tpu_custom_call" | custom-call | flops 1358954496 | bytes 4194304 | tf_op jit(solution)/shard_map/input_gradient/pallas_call | solution.py:307
  70.2 0.9 %collective-permute-done.6.other = f32[8,5184]{1,0:T(8,128)S(1)} collective-permute-done((f32[8,5184]{1,0:T(8,128)}, f32[8,5184]{1,0:T(8,128)S(1)}, u32[]{:S(2)}, u32[]{:S(2)}) %collective-permute-start.6) | collective-permute-done | bytes 165920 | tf_op jit(solution)/shard_map/ppermute | solution.py:354
  71.1 0.0 copy-start.3
  71.1 0.7 copy-done.3
  71.8 1.8 %join.1 = f32[12,5184]{1,0:T(8,128)} custom-call(s32[1]{0:T(128)} %bitcast.place, f32[8,5184]{1,0:T(8,128)} %plane_sum.1.mine, f32[8,5184]{1,0:T(8,128)} %copy-done.3), custom_call_target="tpu_custom_call" | custom-call | flops 41472 | bytes 580608 | tf_op jit(solution)/shard_map/join/pallas_call | solution.py:355
  (9 shorter events, 0.2 us)
Async XLA Ops:
  7.2 38.1 %all-gather.2.cloned.1.call-start = ((), (), s32[]{:S(2)}) async-start(), calls=%async_computation.1 | async-start | bytes 2359296 | tf_op jit(solution)/shard_map/all_gather | solution.py:255
  9.4 6.3 %collective-permute-start = (bf16[3,64,192]{2,1,0:T(8,128)(2,1)}, bf16[3,64,192]{2,1,0:T(8,128)(2,1)S(1)}, u32[]{:S(2)}, u32[]{:S(2)}) collective-permute-start(bf16[3,64,192]{2,1,0:T(8,128)(2,1)} %get-tuple-element.17), channel_id=1, source_target_pairs={{0,2},{2,0},{4,6},{6,4},{8,10},{10,8},{12,14},{14,12},{16,18},{18,... | collective-permute-start | bytes 221192 | tf_op jit(solution)/shard_map/ppermute | solution.py:251
  9.9 5.8 %collective-permute-start.1 = (bf16[3,64,192]{2,1,0:T(8,128)(2,1)}, bf16[3,64,192]{2,1,0:T(8,128)(2,1)S(1)}, u32[]{:S(2)}, u32[]{:S(2)}) collective-permute-start(bf16[3,64,192]{2,1,0:T(8,128)(2,1)} %get-tuple-element.18), channel_id=1, source_target_pairs={{2,4},{4,2},{6,8},{8,6},{10,12},{12,10},{14,16},{16,14},{18,20},{2... | collective-permute-start | bytes 221192 | tf_op jit(solution)/shard_map/ppermute | solution.py:252
  11.3 4.5 %copy-start.2 = (bf16[8,64,192]{2,1,0:T(8,128)(2,1)S(1)}, bf16[8,64,192]{2,1,0:T(8,128)(2,1)}, u32[]{:S(2)}) copy-start(bf16[8,64,192]{2,1,0:T(8,128)(2,1)} %get-tuple-element.16.cot) | copy-start | bytes 589828
  11.3 4.5 %copy-start = (bf16[8,64,192]{2,1,0:T(8,128)(2,1)S(1)}, bf16[8,64,192]{2,1,0:T(8,128)(2,1)}, u32[]{:S(2)}) copy-start(bf16[8,64,192]{2,1,0:T(8,128)(2,1)} %get-tuple-element.15.masked) | copy-start | bytes 589828
  15.7 5.9 %copy-start.4 = (bf16[3,64,192]{2,1,0:T(8,128)(2,1)}, bf16[3,64,192]{2,1,0:T(8,128)(2,1)S(1)}, u32[]{:S(2)}) copy-start(bf16[3,64,192]{2,1,0:T(8,128)(2,1)S(1)} %collective-permute-done.near) | copy-start | bytes 221188
  15.7 5.9 %copy-start.5 = (bf16[3,64,192]{2,1,0:T(8,128)(2,1)}, bf16[3,64,192]{2,1,0:T(8,128)(2,1)S(1)}, u32[]{:S(2)}) copy-start(bf16[3,64,192]{2,1,0:T(8,128)(2,1)S(1)} %collective-permute-done.1.far) | copy-start | bytes 221188
  15.9 5.6 %collective-permute-start.2 = (bf16[272,192]{1,0:T(8,128)(2,1)S(1)}, bf16[272,192]{1,0:T(8,128)(2,1)S(1)}, u32[]{:S(2)}, u32[]{:S(2)}) collective-permute-start(bf16[272,192]{1,0:T(8,128)(2,1)S(1)} %maximum_select_fusion), channel_id=1, source_target_pairs={{0,1},{1,0},{2,3},{3,2},{4,5},{5,4},{6,7},{7,6},{8,9},{9,8},{10,11... | collective-permute-start | bytes 313352 | tf_op jit(solution)/shard_map/ppermute | solution.py:270
  21.5 0.7 copy-start.9
  28.2 17.1 %all-to-all-start = ((bf16[8,32,640]{2,1,0:T(8,128)(2,1)}), bf16[8,32,640]{2,1,0:T(8,128)(2,1)S(1)}, u32[]{:S(2)}, u32[]{:S(2)}) async-start(bf16[8,32,640]{2,1,0:T(8,128)(2,1)} %get-tuple-element.22), calls=%async_computation | async-start | bytes 655360 | tf_op jit(solution)/shard_map/all_to_all | solution.py:305
  45.3 0.7 copy-start.1
  51.9 7.4 %collective-permute-start.3 = (bf16[8,5184]{1,0:T(8,128)(2,1)}, bf16[8,5184]{1,0:T(8,128)(2,1)S(1)}, u32[]{:S(2)}, u32[]{:S(2)}) collective-permute-start(bf16[8,5184]{1,0:T(8,128)(2,1)} %get-tuple-element.24), channel_id=1, source_target_pairs={{0,8},{8,16},{16,24},{24,0},{1,9},{9,17},{17,25},{25,1},{2,10},{10... | collective-permute-start | bytes 248840 | tf_op jit(solution)/shard_map/ppermute | solution.py:341
  53.5 8.9 %collective-permute-start.4 = (bf16[8,5184]{1,0:T(8,128)(2,1)}, bf16[8,5184]{1,0:T(8,128)(2,1)S(1)}, u32[]{:S(2)}, u32[]{:S(2)}) collective-permute-start(bf16[8,5184]{1,0:T(8,128)(2,1)} %get-tuple-element.25), channel_id=1, source_target_pairs={{0,16},{8,24},{16,0},{24,8},{1,17},{9,25},{17,1},{25,9},{2,18},{10... | collective-permute-start | bytes 248840 | tf_op jit(solution)/shard_map/ppermute | solution.py:341
  55.8 6.6 %collective-permute-start.5 = (bf16[8,5184]{1,0:T(8,128)(2,1)}, bf16[8,5184]{1,0:T(8,128)(2,1)S(1)}, u32[]{:S(2)}, u32[]{:S(2)}) collective-permute-start(bf16[8,5184]{1,0:T(8,128)(2,1)} %get-tuple-element.26), channel_id=1, source_target_pairs={{0,24},{8,0},{16,8},{24,16},{1,25},{9,1},{17,9},{25,17},{2,26},{10... | collective-permute-start | bytes 248840 | tf_op jit(solution)/shard_map/ppermute | solution.py:341
  59.3 3.0 %copy-start.6 = (bf16[8,5184]{1,0:T(8,128)(2,1)}, bf16[8,5184]{1,0:T(8,128)(2,1)S(1)}, u32[]{:S(2)}) copy-start(bf16[8,5184]{1,0:T(8,128)(2,1)S(1)} %collective-permute-done.3.one) | copy-start | bytes 248836
  62.4 0.6 copy-start.7
  62.4 0.7 copy-start.8
  64.8 6.3 %collective-permute-start.6 = (f32[8,5184]{1,0:T(8,128)}, f32[8,5184]{1,0:T(8,128)S(1)}, u32[]{:S(2)}, u32[]{:S(2)}) collective-permute-start(f32[8,5184]{1,0:T(8,128)} %plane_sum.1.mine), channel_id=1, source_target_pairs={{0,1},{1,0},{2,3},{3,2},{4,5},{5,4},{6,7},{7,6},{8,9},{9,8},{10,11... | collective-permute-start | bytes 497672 | tf_op jit(solution)/shard_map/ppermute | solution.py:354
  71.1 0.7 copy-start.3
Sparse Core Ops, SparseCore 0:
  10.5 32.4 all-gather.1

commit v3 on v2

--- a/solution.py
+++ b/solution.py
@@ -10,7 +10,6 @@
 
 WIDE = ("depth", "quad")
 QUAD = 4
-VMEM_BYTES = 56 * 1024 * 1024
 OFFSETS = (-1, 0, 1)
 
 
@@ -36,6 +35,13 @@
     for ref, upper in ((near_ref, 1 - odd), (far_ref, odd)):
         ref[0:2] = masked_ref[pl.ds(upper * (width - 2), 2)]
         ref[2:3] = cot_ref[pl.ds(upper * (width - 1), 1)]
+
+
+def pack_kernel(masked, packed_ref):
+    width = masked.shape[0]
+    half = width // 2
+    packed_ref[:width] = masked[:, :, :128]
+    packed_ref[width:] = jnp.concatenate([masked[:half, :, 128:], masked[half:, :, 128:]], axis=2)
 
 
 def forward_kernel(
@@ -121,20 +127,20 @@
     out_ref[...] = (total.reshape(width, rows, channels) * live[:, :, 0:1]).astype(jnp.bfloat16)
 
 
-def kernel_grad_kernel(place, slices, bricks, own_ref, one_ref, two_ref, three_ref, cols, part, masked, sems):
+def kernel_grad_kernel(place, slices, *refs):
+    bricks = refs[:8]
+    own_ref, send_ref, cols, part, stage, masked, sems = refs[8:]
     f32 = jnp.float32
     members, group, lanes = slices.shape
     slabs, lane, channels = masked.shape
     per = slabs // QUAD
     half = lane // 2
-    copies = [
-        pltpu.make_async_copy(
-            bricks.at[pl.ds(member * per, per)],
-            masked.at[pl.ds(member // 2 * per, per), pl.ds(member % 2 * half, half)],
-            sems.at[member],
+    copies = []
+    for member in range(members):
+        quad, side = place[1] ^ (member // 2), place[2] ^ (member % 2)
+        copies.append(
+            pltpu.make_async_copy(bricks[member], stage.at[quad, side], sems.at[member])
         )
-        for member in range(members)
-    ]
     for copy in copies:
         copy.start()
     depth = 8
@@ -172,6 +178,14 @@
         )
     for copy in copies:
         copy.wait()
+    for quad in range(QUAD):
+        for side in range(2):
+            at_rows = pl.ds(side * half, half)
+            for x in range(per):
+                shift = 64 * (x // (per // 2))
+                rest = stage[quad, side, per + x % (per // 2)]
+                masked[quad * per + x, at_rows, :128] = stage[quad, side, x]
+                masked[quad * per + x, at_rows, 128:] = rest[:, shift : shift + 64]
     field = masked[...].reshape(slabs * lane, channels)
     planes, rows, _ = part.shape
     for a in range(3):
@@ -185,13 +199,13 @@
             )
     me = place[0]
     own_ref[...] = part[me]
-    for step, ref in ((1, one_ref), (2, two_ref), (3, three_ref)):
-        ref[...] = part[lax.rem(me + step, planes)].astype(jnp.bfloat16)
-
-
-def sum_kernel(scale, own, one, two, three, out_ref):
-    f32 = jnp.float32
-    total = own[...] + one[...].astype(f32) + two[...].astype(f32) + three[...].astype(f32)
+    send_ref[...] = part[...].astype(jnp.bfloat16)
+
+
+def sum_kernel(scale, place, own, parts, out_ref):
+    total = own[...]
+    for plane in range(parts.shape[0]):
+        total += jnp.where(plane == place[0], 0.0, parts[plane].astype(jnp.float32))
     out_ref[...] = total * scale
 
 
@@ -210,8 +224,8 @@
 SMEM = pl.BlockSpec(memory_space=pltpu.SMEM)
 
 
-def params():
-    return pltpu.CompilerParams(vmem_limit_bytes=VMEM_BYTES)
+def params(mebibytes):
+    return pltpu.CompilerParams(vmem_limit_bytes=mebibytes * 1024 * 1024)
 
 
 def cost(flops, moved):
@@ -233,12 +247,13 @@
     odd = lax.axis_index("quad") % 2
     brick = jax.ShapeDtypeStruct((width, rows, channels), bf16)
     slab = jax.ShapeDtypeStruct((3, rows, channels), bf16)
+    column = jax.ShapeDtypeStruct((width, rows, 128), f32)
     masked, cot, live, near, far = pl.pallas_call(
         prepare_kernel,
-        out_shape=(brick, brick, jax.ShapeDtypeStruct((width, rows, 128), f32), slab, slab),
+        out_shape=(brick, brick, column, slab, slab),
         in_specs=[SMEM] + vmem(3),
         out_specs=tuple(vmem(5)),
-        compiler_params=params(),
+        compiler_params=params(8),
         cost_estimate=cost(1 << 20, 1 << 20),
         name="prepare",
     )(
@@ -252,7 +267,23 @@
     far = lax.ppermute(
         far, WIDE, [(i, j) for i in range(count) if 0 <= (j := ((i + 1) ^ 1) - 1) < count]
     )
-    bricks = lax.all_gather(masked, ("quad", "narrow"), axis=0, tiled=True)
+    packed = pl.pallas_call(
+        pack_kernel,
+        out_shape=jax.ShapeDtypeStruct((width * channels // 128, rows, 128), bf16),
+        in_specs=vmem(1),
+        out_specs=vmem(1)[0],
+        compiler_params=params(4),
+        cost_estimate=cost(1 << 16, 1 << 19),
+        name="pack",
+    )(masked)
+
+    def across(piece):
+        return lax.ppermute(piece, "narrow", [(0, 1), (1, 0)])
+
+    def beside(piece, distance):
+        return lax.ppermute(piece, "quad", [(i, i ^ distance) for i in range(quads)])
+
+    bricks = [packed, across(packed), beside(packed, 1), None, beside(packed, 2)] + [None] * 3
     left = jnp.where(odd == 1, near, far)
     right = jnp.where(odd == 1, far, near)
 
@@ -267,9 +298,13 @@
             parts = wide_masked[:, rows - halo :], wide_cot[:, rows - depth :]
         return jnp.concatenate([part.reshape(-1, channels) for part in parts], axis=0)
 
-    swapped = lax.ppermute(
-        jnp.where(side == 0, strip(False), strip(True)), "narrow", [(0, 1), (1, 0)]
-    )
+    edge, bricks[1], bricks[4] = lax.optimization_barrier(
+        (jnp.where(side == 0, strip(False), strip(True)), bricks[1], bricks[4])
+    )
+    swapped = across(edge)
+    bricks[3] = beside(bricks[1], 1)
+    bricks[5] = beside(bricks[1], 2)
+    bricks[6] = beside(bricks[4], 1)
     flags = jnp.stack([side, 1 - side, odd]).astype(jnp.int32)
 
     group = 4 * 8
@@ -297,11 +332,13 @@
             pltpu.VMEM((2, 3, rows, channels), bf16),
             pltpu.VMEM((width + 4, rows + 2 * depth, 9 * channels), bf16),
         ],
-        compiler_params=params(),
+        compiler_params=params(28),
         cost_estimate=cost(2 * 800 * 5184 * 256, 4 << 20),
         name="forward",
     )(flags, masked, cot, near, far, swapped, swapped, live, weight, pick)
 
+    slices, bricks[5] = lax.optimization_barrier((slices, bricks[5]))
+    bricks[7] = beside(bricks[5], 1)
     slices = lax.all_to_all(slices, ("quad", "narrow"), 0, 0, tiled=True)
 
     grad_input = pl.pallas_call(
@@ -313,51 +350,51 @@
             pltpu.VMEM((width + 2, rows, 9 * channels), bf16),
             pltpu.VMEM((27 * channels, channels), bf16),
         ],
-        compiler_params=params(),
+        compiler_params=params(20),
         cost_estimate=cost(2 * 512 * 5184 * 256, 4 << 20),
         name="input_gradient",
     )(gp, live, weight.T)
 
     total = 27 * channels
-    place = plane.reshape(1).astype(jnp.int32)
-    small = jax.ShapeDtypeStruct((8, total), bf16)
-    own, *sends = pl.pallas_call(
+    place = jnp.stack([plane, lax.axis_index("quad"), side]).astype(jnp.int32)
+    own, sends = pl.pallas_call(
         kernel_grad_kernel,
-        out_shape=(jax.ShapeDtypeStruct((8, total), f32), small, small, small),
-        in_specs=[SMEM] + vmem(1) + [pl.BlockSpec(memory_space=pl.ANY)],
-        out_specs=tuple(vmem(4)),
+        out_shape=(
+            jax.ShapeDtypeStruct((8, total), f32),
+            jax.ShapeDtypeStruct((planes, 8, total), bf16),
+        ),
+        in_specs=[SMEM] + vmem(1) + [pl.BlockSpec(memory_space=pl.ANY)] * 8,
+        out_specs=tuple(vmem(2)),
         scratch_shapes=[
             pltpu.VMEM((9 * group, (quads * width + 2) * sides * rows), bf16),
             pltpu.VMEM((planes, 8, total), f32),
+            pltpu.VMEM((quads, sides, width * channels // 128, rows, 128), bf16),
             pltpu.VMEM((quads * width, sides * rows, channels), bf16),
             pltpu.SemaphoreType.DMA((members,)),
         ],
-        compiler_params=params(),
+        compiler_params=params(24),
         cost_estimate=cost(2 * 288 * 3 * 4096 * 256, 4 << 20),
         name="kernel_gradient",
-    )(place, slices, bricks)
-
-    got = [
-        lax.ppermute(sent, "depth", [(i, (i + step) % planes) for i in range(planes)])
-        for step, sent in zip((1, 2, 3), sends)
-    ]
+    )(place, slices, *bricks)
+
+    parts = lax.all_to_all(sends, "depth", 0, 0, tiled=True)
     voxels = count * sides * width * rows
     mine = pl.pallas_call(
         functools.partial(sum_kernel, float(1.0 / voxels**0.5)),
         out_shape=jax.ShapeDtypeStruct((8, total), f32),
-        in_specs=vmem(4),
+        in_specs=[SMEM] + vmem(2),
         out_specs=vmem(1)[0],
-        compiler_params=params(),
+        compiler_params=params(4),
         cost_estimate=cost(8 * total * 4, 8 * total * 14),
         name="plane_sum",
-    )(own, *got)
+    )(place, own, parts)
     other = lax.ppermute(mine, "narrow", [(0, 1), (1, 0)])
     grad_weight = pl.pallas_call(
         join_kernel,
         out_shape=jax.ShapeDtypeStruct((per, total), f32),
         in_specs=[SMEM] + vmem(2),
         out_specs=vmem(1)[0],
-        compiler_params=params(),
+        compiler_params=params(4),
         cost_estimate=cost(8 * total, 8 * total * 14),
         name="join",
     )(side.reshape(1).astype(jnp.int32), mine, other)

time: 80.8 us -> 68.8 us (0.85)
  blocking collectives: 0 us -> 16.4 us
  between operations: 14.2 us -> 0.8 us
  Pallas kernels: 21.9 us -> 15 us
  waiting for transfers between devices: 15.1 us -> 9.9 us
  starting transfers between devices: 20.6 us -> 16 us
  local copies, waits for them, and re-layouts: 7.08 us -> 8.86 us
    all_to_all x0 -> x1, blocking collectives: none -> 16.4 us  [planes_local(): parts = lax.all_to_all(sends, 'depth', 0, 0, tiled=True)]
    all_to_all x1, starting transfers between devices: 10.4 us -> 4.48 us  [planes_local(): slices = lax.all_to_all(slices, ('quad', 'narrow'), 0, 0, tiled=True)]
    ppermute x4 -> x8, waiting for transfers between devices: 7.45 us -> 4.07 us  [the longest x2 2.31 us: across(): return lax.ppermute(piece, 'narrow', [(0, 1), (1, 0)])]
    all_to_all x1, waiting for transfers between devices: 6.74 us -> 3.88 us  [planes_local(): slices = lax.all_to_all(slices, ('quad', 'narrow'), 0, 0, tiled=True)]
    unnamed x21 -> x19, local copies, waits for them, and re-layouts: 7.06 us -> 8.84 us
    pallas_call x1, Pallas kernels: 4.35 us -> 2.59 us  [planes_local(): pl.pallas_call(input_kernel, out_shape=jax.ShapeDtypeStruct((width, rows,...]
    ppermute x4 -> x8, starting transfers between devices: 8 us -> 9.31 us  [the longest x6 5.77 us: beside(): lax.ppermute(piece, 'quad', [(i, i ^ distance) for i in range(quads)])]
    pallas_call x1, Pallas kernels: 5.94 us -> 4.75 us  [planes_local(): pl.pallas_call(forward_kernel, out_shape=(jax.ShapeDtypeStruct((width, ro...]
  transfers between devices with their start and end apart: 9 -> 12, of which waited for: 5 -> 7; matrix products, arithmetic and copies ran while one was open for 7% -> 8% of each run, Pallas kernels for 13% -> 11%
where the time goes in v3:
time: 68.8 us; the launch traced here: 68.3 us
  blocking collectives  16.4 us (24%)
  starting transfers between devices  16 us (23%)
  Pallas kernels  15 us (22%)
  waiting for transfers between devices  9.9 us (14%)
  local copies, waits for them, and re-layouts  8.86 us (13%)
  other arithmetic  1.32 us (2%)
  between operations  0.8 us (1%)
    all_to_all x1, blocking collectives, planes_local(): parts = lax.all_to_all(sends, 'depth', 0, 0, tiled=True)  16.4 us
    unnamed x19, local copies, waits for them, and re-layouts  8.84 us
    ppermute x6, starting transfers between devices, beside(): lax.ppermute(piece, 'quad', [(i, i ^ distance) for i in range(quads)])  5.77 us
    pallas_call x1, Pallas kernels, planes_local(): pl.pallas_call(kernel_grad_kernel, out_shape=(jax.ShapeDtypeStruct((8, to...  5.38 us
    pallas_call x1, Pallas kernels, planes_local(): pl.pallas_call(forward_kernel, out_shape=(jax.ShapeDtypeStruct((width, ro...  4.75 us
    all_to_all x1, starting transfers between devices, planes_local(): slices = lax.all_to_all(slices, ('quad', 'narrow'), 0, 0, tiled=True)  4.48 us
    all_to_all x1, waiting for transfers between devices, planes_local(): slices = lax.all_to_all(slices, ('quad', 'narrow'), 0, 0, tiled=True)  3.88 us
    ppermute x2, starting transfers between devices, across(): return lax.ppermute(piece, 'narrow', [(0, 1), (1, 0)])  3.54 us
  transfers between devices with their start and end apart: 12, of which 7 were waited for; matrix products, arithmetic and copies ran while one was open for 8% of the time, Pallas kernels for 11%

profile of v3, /device:TPU:0, one launch (start us, length us, event | category | flops | bytes accessed | tf_op | source)
XLA Modules:
  0.0 68.3 jit_solution(9538516649888219413)
XLA Ops:
  0.6 0.0 copy-start.1
  0.7 0.9 %copy-done.1 = bf16[8,8,8,192]{3,2,1,0:T(8,128)(2,1)S(1)} copy-done((bf16[8,8,8,192]{3,2,1,0:T(8,128)(2,1)S(1)}, bf16[8,8,8,192]{3,2,1,0:T(8,128)(2,1)}, u32[]{:S(2)}) %copy-start.1) | copy-done | bytes 196632
  1.6 0.0 copy-start.2
  1.6 0.9 %copy-done.2 = bf16[8,8,8,192]{3,2,1,0:T(8,128)(2,1)S(1)} copy-done((bf16[8,8,8,192]{3,2,1,0:T(8,128)(2,1)S(1)}, bf16[8,8,8,192]{3,2,1,0:T(8,128)(2,1)}, u32[]{:S(2)}) %copy-start.2) | copy-done | bytes 196632
  2.5 0.0 copy-start.3
  2.5 0.8 %copy-done.3 = s32[8,8,8]{2,1,0:T(8,128)S(1)} copy-done((s32[8,8,8]{2,1,0:T(8,128)S(1)}, s32[8,8,8]{2,1,0:T(8,128)}, u32[]{:S(2)}) %copy-start.3) | copy-done | bytes 2072
  3.3 0.9 %prepare.1 = (bf16[8,64,192]{2,1,0:T(8,128)(2,1)S(1)}, bf16[8,64,192]{2,1,0:T(8,128)(2,1)S(1)}, f32[8,64,128]{2,1,0:T(8,128)S(1)}, bf16[3,64,192]{2,1,0:T(8,128)(2,1)}, bf16[3,64,192]{2,1,0:T(8,128)(2,1)}) custom-call(s32[1]{0:T(128)} %bitcast.2.place, bf16[8,64,192]{2,1,0:T(8,128)(2,1)S(1)} %bitcast.17, bf16[8,64,192]{2,1,0:T(8,128)(2,1)S(1)} %bitcast.18, ...), custom_call_target="tpu_custom_call" | custom-call | flops 1048576 | bytes 1048576 | tf_op jit(solution)/shard_map/prepare/pallas_call | solution.py:251
  4.2 0.0 copy-start.4
  4.2 0.1 pack.1.refs_0_
  4.2 0.6 copy-done.4
  4.9 3.0 %collective-permute-start.2 = (bf16[12,64,128]{2,1,0:T(8,128)(2,1)S(1)}, bf16[12,64,128]{2,1,0:T(8,128)(2,1)}, u32[]{:S(2)}, u32[]{:S(2)}) collective-permute-start(bf16[12,64,128]{2,1,0:T(8,128)(2,1)S(1)} %pack.1.refs_0_), channel_id=1, source_target_pairs={{0,1},{1,0},{2,3},{3,2},{4,5},{5,4},{6,7},{7,6},{8,9},{9,8},{10,11... | collective-permute-start | bytes 589832 | tf_op jit(solution)/shard_map/ppermute | solution.py:281
  7.8 1.5 %collective-permute-start.3 = (bf16[12,64,128]{2,1,0:T(8,128)(2,1)S(1)}, bf16[12,64,128]{2,1,0:T(8,128)(2,1)}, u32[]{:S(2)}, u32[]{:S(2)}) collective-permute-start(bf16[12,64,128]{2,1,0:T(8,128)(2,1)S(1)} %pack.1.refs_0_), channel_id=1, source_target_pairs={{0,4},{2,6},{4,0},{6,2},{1,5},{3,7},{5,1},{7,3},{8,12},{10,14},{12... | collective-permute-start | bytes 589832 | tf_op jit(solution)/shard_map/ppermute | solution.py:284
  9.3 0.0 collective-permute-start
  9.3 1.3 %collective-permute-start.1 = (bf16[3,64,192]{2,1,0:T(8,128)(2,1)}, bf16[3,64,192]{2,1,0:T(8,128)(2,1)}, u32[]{:S(2)}, u32[]{:S(2)}) collective-permute-start(bf16[3,64,192]{2,1,0:T(8,128)(2,1)} %get-tuple-element.21), channel_id=1, source_target_pairs={{2,4},{4,2},{6,8},{8,6},{10,12},{12,10},{14,16},{16,14},{18,20},{2... | collective-permute-start | bytes 221192 | tf_op jit(solution)/shard_map/ppermute | solution.py:267
  10.6 0.1 fusion.pick
  10.7 3.9 %copy.7.weight = bf16[5184,192]{1,0:T(8,128)(2,1)S(1)} copy(bf16[5184,192]{0,1:T(8,128)(2,1)} %param.5) | data formatting | bytes 3981312 | tf_op args[1]
  14.6 0.0 collective-permute-done.near
  14.6 0.0 collective-permute-done.1.far
  14.6 1.0 %broadcast_select_fusion.1 = (bf16[3,64,192]{2,1,0:T(8,128)(2,1)S(1)}, bf16[3,64,192]{2,1,0:T(8,128)(2,1)S(1)}) fusion(bf16[3,64,192]{2,1,0:T(8,128)(2,1)} %collective-permute-done.near, bf16[3,64,192]{2,1,0:T(8,128)(2,1)} %collective-permute-done.1.far, pred[]{:T(512)S(6)} %eq.27), kind=kLoop, calls=%fused_computation.7 | loop fusion | flops 73728 | bytes 294913 | tf_op jit(solution)/shard_map/jit(_where)/select_n | solution.py:287
  15.8 0.0 collective-permute-done.2.refs_1_
  15.8 0.0 collective-permute-done.3.refs_4_
  15.8 0.6 collective-permute-start.4
  16.4 0.1 pad_add_fusion.flags
  16.4 3.3 %collective-permute-start.5 = (bf16[12,64,128]{2,1,0:T(8,128)(2,1)}, bf16[12,64,128]{2,1,0:T(8,128)(2,1)}, u32[]{:S(2)}, u32[]{:S(2)}) collective-permute-start(bf16[12,64,128]{2,1,0:T(8,128)(2,1)} %collective-permute-done.2.refs_1_), channel_id=1, source_target_pairs={{0,4},{2,6},{4,0},{6,2},{1,5},{3,7},{5,1},{7,3},{8,12},{10,14},{12... | collective-permute-start | bytes 589832 | tf_op jit(solution)/shard_map/ppermute | solution.py:284
  19.7 2.3 %collective-permute-done.4.low.high = bf16[272,192]{1,0:T(8,128)(2,1)S(1)} collective-permute-done((bf16[272,192]{1,0:T(8,128)(2,1)S(1)}, bf16[272,192]{1,0:T(8,128)(2,1)S(1)}, u32[]{:S(2)}, u32[]{:S(2)}) %collective-permute-start.4) | collective-permute-done | bytes 104480 | tf_op jit(solution)/shard_map/ppermute | solution.py:281
  22.0 0.0 copy-start.5
  22.0 0.9 %copy-done.5 = f32[8,64,128]{2,1,0:T(8,128)S(1)} copy-done((f32[8,64,128]{2,1,0:T(8,128)S(1)}, f32[8,64,128]{2,1,0:T(8,128)}, u32[]{:S(2)}) %copy-start.5) | copy-done | bytes 262168
  23.0 4.7 %forward.1 = (bf16[8,64,192]{2,1,0:T(8,128)(2,1)}, bf16[10,80,192]{2,1,0:T(8,128)(2,1)S(1)}, bf16[8,32,640]{2,1,0:T(8,128)(2,1)}) custom-call(s32[3]{0:T(128)S(1)} %pad_add_fusion.flags, bf16[8,64,192]{2,1,0:T(8,128)(2,1)S(1)} %get-tuple-element.18.masked, bf16[8,64,192]{2,1,0:T(8,128)(2,1)S(1)} %get-tuple-element.19.cot, ...), custom_call_target="tpu_custom_call" | custom-call | flops 2123366400 | bytes 4194304 | tf_op jit(solution)/shard_map/forward/pallas_call | solution.py:321
  27.7 0.0 copy-start.7
  27.7 0.8 %copy-done.7 = bf16[10,80,192]{2,1,0:T(8,128)(2,1)} copy-done((bf16[10,80,192]{2,1,0:T(8,128)(2,1)}, bf16[10,80,192]{2,1,0:T(8,128)(2,1)S(1)}, u32[]{:S(2)}) %copy-start.7) | copy-done | bytes 307224
  28.5 0.0 collective-permute-done.5.refs_5_
  28.5 4.5 %all-to-all-start = ((bf16[8,32,640]{2,1,0:T(8,128)(2,1)}), bf16[8,32,640]{2,1,0:T(8,128)(2,1)S(1)}, u32[]{:S(2)}, u32[]{:S(2)}) async-start(bf16[8,32,640]{2,1,0:T(8,128)(2,1)} %get-tuple-element.28), calls=%async_computation | async-start | bytes 655360 | tf_op jit(solution)/shard_map/all_to_all | solution.py:342
  32.9 0.5 collective-permute-start.6
  33.4 0.0 collective-permute-start.7
  33.5 0.5 collective-permute-start.8
  34.0 0.0 collective-permute-start.9
  34.0 0.1 pad_add_fusion.1.place
  34.0 0.0 copy-start
  34.0 0.0 copy-start.6
  34.0 0.7 %collective-permute-done.6.refs_2_ = bf16[12,64,128]{2,1,0:T(8,128)(2,1)S(1)} collective-permute-done((bf16[12,64,128]{2,1,0:T(8,128)(2,1)S(1)}, bf16[12,64,128]{2,1,0:T(8,128)(2,1)S(1)}, u32[]{:S(2)}, u32[]{:S(2)}) %collective-permute-start.6) | collective-permute-done | bytes 196640 | tf_op jit(solution)/shard_map/ppermute | solution.py:284
  34.7 0.6 collective-permute-done.7.refs_3_
  35.3 0.2 collective-permute-done.8.refs_6_
  35.5 0.3 collective-permute-done.9.refs_7_
  35.8 3.9 %all-to-all-done.slices = bf16[8,32,640]{2,1,0:T(8,128)(2,1)S(1)} async-done(((bf16[8,32,640]{2,1,0:T(8,128)(2,1)}), bf16[8,32,640]{2,1,0:T(8,128)(2,1)S(1)}, u32[]{:S(2)}, u32[]{:S(2)}) %all-to-all-start) | async-done | bytes 327712 | tf_op jit(solution)/shard_map/all_to_all | solution.py:342
  39.7 0.0 copy-start.8
  39.7 5.4 %kernel_gradient.1 = (f32[8,5184]{1,0:T(8,128)S(1)}, bf16[4,8,5184]{2,1,0:T(8,128)(2,1)S(1)}) custom-call(s32[3]{0:T(128)S(1)} %pad_add_fusion.1.place, bf16[8,32,640]{2,1,0:T(8,128)(2,1)S(1)} %all-to-all-done.slices, bf16[12,64,128]{2,1,0:T(8,128)(2,1)S(1)} %pack.1.refs_0_, bf16[12,64,128]{2,1,0:T(8,128)(2,1)} %collective-permute-done.2.refs_1_, ...), custom_call_target="tpu_custom_call" | custom-call | flops 1811939328 | bytes 4194304 | tf_op jit(solution)/shard_map/kernel_gradient/pallas_call | solution.py:360
  45.1 16.4 %all_to_all.10.parts = bf16[4,8,5184]{2,1,0:T(8,128)(2,1)S(1)} all-to-all(bf16[4,8,5184]{2,1,0:T(8,128)(2,1)S(1)} %get-tuple-element.32), channel_id=1, replica_groups=mesh['depth'=4,'quad'=4,'narrow'=2] {'depth'}, dimensions={0} | all-to-all | bytes 663552 | tf_op jit(solution)/shard_map/all_to_all | solution.py:380
  61.4 0.6 plane_sum.1.mine
  62.1 0.9 %collective-permute-start.10 = (f32[8,5184]{1,0:T(8,128)S(1)}, f32[8,5184]{1,0:T(8,128)S(1)}, u32[]{:S(2)}, u32[]{:S(2)}) collective-permute-start(f32[8,5184]{1,0:T(8,128)S(1)} %plane_sum.1.mine), channel_id=1, source_target_pairs={{0,1},{1,0},{2,3},{3,2},{4,5},{5,4},{6,7},{7,6},{8,9},{9,8},{10,11... | collective-permute-start | bytes 497672 | tf_op jit(solution)/shard_map/ppermute | solution.py:391
  63.0 0.0 copy-done
  63.0 0.0 copy-done.6
  63.0 0.0 copy-done.8
  63.0 2.6 %input_gradient.1 = bf16[8,64,192]{2,1,0:T(8,128)(2,1)} custom-call(bf16[10,80,192]{2,1,0:T(8,128)(2,1)S(1)} %copy-done.8, f32[8,64,128]{2,1,0:T(8,128)S(1)} %copy-done.6, bf16[192,5184]{1,0:T(8,128)(2,1)S(1)} %bitcast.16), custom_call_target="tpu_custom_call" | custom-call | flops 1358954496 | bytes 4194304 | tf_op jit(solution)/shard_map/input_gradient/pallas_call | solution.py:344
  65.6 1.9 %collective-permute-done.10.other = f32[8,5184]{1,0:T(8,128)S(1)} collective-permute-done((f32[8,5184]{1,0:T(8,128)S(1)}, f32[8,5184]{1,0:T(8,128)S(1)}, u32[]{:S(2)}, u32[]{:S(2)}) %collective-permute-start.10) | collective-permute-done | bytes 165920 | tf_op jit(solution)/shard_map/ppermute | solution.py:391
  67.5 0.8 %join.1 = f32[12,5184]{1,0:T(8,128)} custom-call(s32[1]{0:T(128)} %bitcast.place, f32[8,5184]{1,0:T(8,128)S(1)} %plane_sum.1.mine, f32[8,5184]{1,0:T(8,128)S(1)} %collective-permute-done.10.other), custom_call_target="tpu_custom_call" | custom-call | flops 41472 | bytes 580608 | tf_op jit(solution)/shard_map/join/pallas_call | solution.py:392
  (8 shorter events, 0.1 us)
Async XLA Ops:
  0.6 1.0 %copy-start.1 = (bf16[8,8,8,192]{3,2,1,0:T(8,128)(2,1)S(1)}, bf16[8,8,8,192]{3,2,1,0:T(8,128)(2,1)}, u32[]{:S(2)}) copy-start(bf16[8,8,8,192]{3,2,1,0:T(8,128)(2,1)} %param.4) | copy-start | bytes 589828
  1.6 0.9 %copy-start.2 = (bf16[8,8,8,192]{3,2,1,0:T(8,128)(2,1)S(1)}, bf16[8,8,8,192]{3,2,1,0:T(8,128)(2,1)}, u32[]{:S(2)}) copy-start(bf16[8,8,8,192]{3,2,1,0:T(8,128)(2,1)} %param.7) | copy-start | bytes 589828
  2.5 0.8 %copy-start.3 = (s32[8,8,8]{2,1,0:T(8,128)S(1)}, s32[8,8,8]{2,1,0:T(8,128)}, u32[]{:S(2)}) copy-start(s32[8,8,8]{2,1,0:T(8,128)} %mask.1) | copy-start | bytes 6148
  4.2 0.7 %copy-start.4 = (f32[8,64,128]{2,1,0:T(8,128)}, f32[8,64,128]{2,1,0:T(8,128)S(1)}, u32[]{:S(2)}) copy-start(f32[8,64,128]{2,1,0:T(8,128)S(1)} %get-tuple-element.23.live) | copy-start | bytes 786436
  4.9 10.9 %collective-permute-start.2 = (bf16[12,64,128]{2,1,0:T(8,128)(2,1)S(1)}, bf16[12,64,128]{2,1,0:T(8,128)(2,1)}, u32[]{:S(2)}, u32[]{:S(2)}) collective-permute-start(bf16[12,64,128]{2,1,0:T(8,128)(2,1)S(1)} %pack.1.refs_0_), channel_id=1, source_target_pairs={{0,1},{1,0},{2,3},{3,2},{4,5},{5,4},{6,7},{7,6},{8,9},{9,8},{10,11... | collective-permute-start | bytes 589832 | tf_op jit(solution)/shard_map/ppermute | solution.py:281
  7.8 8.0 %collective-permute-start.3 = (bf16[12,64,128]{2,1,0:T(8,128)(2,1)S(1)}, bf16[12,64,128]{2,1,0:T(8,128)(2,1)}, u32[]{:S(2)}, u32[]{:S(2)}) collective-permute-start(bf16[12,64,128]{2,1,0:T(8,128)(2,1)S(1)} %pack.1.refs_0_), channel_id=1, source_target_pairs={{0,4},{2,6},{4,0},{6,2},{1,5},{3,7},{5,1},{7,3},{8,12},{10,14},{12... | collective-permute-start | bytes 589832 | tf_op jit(solution)/shard_map/ppermute | solution.py:284
  9.3 5.3 %collective-permute-start = (bf16[3,64,192]{2,1,0:T(8,128)(2,1)}, bf16[3,64,192]{2,1,0:T(8,128)(2,1)}, u32[]{:S(2)}, u32[]{:S(2)}) collective-permute-start(bf16[3,64,192]{2,1,0:T(8,128)(2,1)} %get-tuple-element.20), channel_id=1, source_target_pairs={{0,2},{2,0},{4,6},{6,4},{8,10},{10,8},{12,14},{14,12},{16,18},{18,... | collective-permute-start | bytes 221192 | tf_op jit(solution)/shard_map/ppermute | solution.py:266
  9.3 5.3 %collective-permute-start.1 = (bf16[3,64,192]{2,1,0:T(8,128)(2,1)}, bf16[3,64,192]{2,1,0:T(8,128)(2,1)}, u32[]{:S(2)}, u32[]{:S(2)}) collective-permute-start(bf16[3,64,192]{2,1,0:T(8,128)(2,1)} %get-tuple-element.21), channel_id=1, source_target_pairs={{2,4},{4,2},{6,8},{8,6},{10,12},{12,10},{14,16},{16,14},{18,20},{2... | collective-permute-start | bytes 221192 | tf_op jit(solution)/shard_map/ppermute | solution.py:267
  15.8 6.2 %collective-permute-start.4 = (bf16[272,192]{1,0:T(8,128)(2,1)S(1)}, bf16[272,192]{1,0:T(8,128)(2,1)S(1)}, u32[]{:S(2)}, u32[]{:S(2)}) collective-permute-start(bf16[272,192]{1,0:T(8,128)(2,1)S(1)} %maximum_select_fusion), channel_id=1, source_target_pairs={{0,1},{1,0},{2,3},{3,2},{4,5},{5,4},{6,7},{7,6},{8,9},{9,8},{10,11... | collective-permute-start | bytes 313352 | tf_op jit(solution)/shard_map/ppermute | solution.py:281
  16.4 12.0 %collective-permute-start.5 = (bf16[12,64,128]{2,1,0:T(8,128)(2,1)}, bf16[12,64,128]{2,1,0:T(8,128)(2,1)}, u32[]{:S(2)}, u32[]{:S(2)}) collective-permute-start(bf16[12,64,128]{2,1,0:T(8,128)(2,1)} %collective-permute-done.2.refs_1_), channel_id=1, source_target_pairs={{0,4},{2,6},{4,0},{6,2},{1,5},{3,7},{5,1},{7,3},{8,12},{10,14},{12... | collective-permute-start | bytes 589832 | tf_op jit(solution)/shard_map/ppermute | solution.py:284
  22.0 1.0 %copy-start.5 = (f32[8,64,128]{2,1,0:T(8,128)S(1)}, f32[8,64,128]{2,1,0:T(8,128)}, u32[]{:S(2)}) copy-start(f32[8,64,128]{2,1,0:T(8,128)} %copy-done.4) | copy-start | bytes 786436
  27.7 0.8 %copy-start.7 = (bf16[10,80,192]{2,1,0:T(8,128)(2,1)}, bf16[10,80,192]{2,1,0:T(8,128)(2,1)S(1)}, u32[]{:S(2)}) copy-start(bf16[10,80,192]{2,1,0:T(8,128)(2,1)S(1)} %get-tuple-element.25.gp) | copy-start | bytes 921604
  28.5 11.2 %all-to-all-start = ((bf16[8,32,640]{2,1,0:T(8,128)(2,1)}), bf16[8,32,640]{2,1,0:T(8,128)(2,1)S(1)}, u32[]{:S(2)}, u32[]{:S(2)}) async-start(bf16[8,32,640]{2,1,0:T(8,128)(2,1)} %get-tuple-element.28), calls=%async_computation | async-start | bytes 655360 | tf_op jit(solution)/shard_map/all_to_all | solution.py:342
  32.9 1.8 %collective-permute-start.6 = (bf16[12,64,128]{2,1,0:T(8,128)(2,1)S(1)}, bf16[12,64,128]{2,1,0:T(8,128)(2,1)S(1)}, u32[]{:S(2)}, u32[]{:S(2)}) collective-permute-start(bf16[12,64,128]{2,1,0:T(8,128)(2,1)S(1)} %pack.1.refs_0_), channel_id=1, source_target_pairs={{0,2},{2,0},{4,6},{6,4},{1,3},{3,1},{5,7},{7,5},{8,10},{10,8},{12,... | collective-permute-start | bytes 589832 | tf_op jit(solution)/shard_map/ppermute | solution.py:284
  33.4 1.9 %collective-permute-start.7 = (bf16[12,64,128]{2,1,0:T(8,128)(2,1)}, bf16[12,64,128]{2,1,0:T(8,128)(2,1)S(1)}, u32[]{:S(2)}, u32[]{:S(2)}) collective-permute-start(bf16[12,64,128]{2,1,0:T(8,128)(2,1)} %collective-permute-done.2.refs_1_), channel_id=1, source_target_pairs={{0,2},{2,0},{4,6},{6,4},{1,3},{3,1},{5,7},{7,5},{8,10},{10,8},{12,... | collective-permute-start | bytes 589832 | tf_op jit(solution)/shard_map/ppermute | solution.py:284
  33.5 2.1 %collective-permute-start.8 = (bf16[12,64,128]{2,1,0:T(8,128)(2,1)}, bf16[12,64,128]{2,1,0:T(8,128)(2,1)}, u32[]{:S(2)}, u32[]{:S(2)}) collective-permute-start(bf16[12,64,128]{2,1,0:T(8,128)(2,1)} %collective-permute-done.3.refs_4_), channel_id=1, source_target_pairs={{0,2},{2,0},{4,6},{6,4},{1,3},{3,1},{5,7},{7,5},{8,10},{10,8},{12,... | collective-permute-start | bytes 589832 | tf_op jit(solution)/shard_map/ppermute | solution.py:284
  34.0 1.8 %collective-permute-start.9 = (bf16[12,64,128]{2,1,0:T(8,128)(2,1)}, bf16[12,64,128]{2,1,0:T(8,128)(2,1)}, u32[]{:S(2)}, u32[]{:S(2)}) collective-permute-start(bf16[12,64,128]{2,1,0:T(8,128)(2,1)} %collective-permute-done.5.refs_5_), channel_id=1, source_target_pairs={{0,2},{2,0},{4,6},{6,4},{1,3},{3,1},{5,7},{7,5},{8,10},{10,8},{12,... | collective-permute-start | bytes 589832 | tf_op jit(solution)/shard_map/ppermute | solution.py:284
  34.0 28.9 %copy-start = (bf16[5184,192]{0,1:T(8,128)(2,1)S(1)}, bf16[5184,192]{0,1:T(8,128)(2,1)}, u32[]{:S(2)}) copy-start(bf16[5184,192]{0,1:T(8,128)(2,1)} %param.5) | copy-start | bytes 5971972
  34.0 28.9 %copy-start.6 = (f32[8,64,128]{2,1,0:T(8,128)S(1)}, f32[8,64,128]{2,1,0:T(8,128)}, u32[]{:S(2)}) copy-start(f32[8,64,128]{2,1,0:T(8,128)} %copy-done.4) | copy-start | bytes 786436
  39.7 23.3 %copy-start.8 = (bf16[10,80,192]{2,1,0:T(8,128)(2,1)S(1)}, bf16[10,80,192]{2,1,0:T(8,128)(2,1)}, u32[]{:S(2)}) copy-start(bf16[10,80,192]{2,1,0:T(8,128)(2,1)} %copy-done.7) | copy-start | bytes 921604
  62.1 5.4 %collective-permute-start.10 = (f32[8,5184]{1,0:T(8,128)S(1)}, f32[8,5184]{1,0:T(8,128)S(1)}, u32[]{:S(2)}, u32[]{:S(2)}) collective-permute-start(f32[8,5184]{1,0:T(8,128)S(1)} %plane_sum.1.mine), channel_id=1, source_target_pairs={{0,1},{1,0},{2,3},{3,2},{4,5},{5,4},{6,7},{7,6},{8,9},{9,8},{10,11... | collective-permute-start | bytes 497672 | tf_op jit(solution)/shard_map/ppermute | solution.py:391

commit v4 on v0

--- a/solution.py
+++ b/solution.py
@@ -1,7 +1,418 @@
+import functools
+
 import jax
 import jax.numpy as jnp
+import numpy as np
 from jax import lax
+from jax.experimental import pallas as pl
+from jax.experimental.pallas import tpu as pltpu
+from jax.sharding import Mesh
 from jax.sharding import PartitionSpec as P
+
+WIDE = ("depth", "quad")
+QUAD = 4
+SIDES = 2
+MEMBERS = QUAD * SIDES
+OFFSETS = (-1, 0, 1)
+DEPTH = 8
+
+
+def position():
+    quad, side = lax.axis_index("quad"), lax.axis_index("narrow")
+    return lax.axis_index("depth"), quad * SIDES + side, quad, side
+
+
+def shift_z(field, step):
+    if step == 0:
+        return field
+    depth = field.shape[1]
+    moved = pltpu.roll(field, (-step) % depth, 1)
+    z = lax.broadcasted_iota(jnp.int32, field.shape, 1) + step
+    return jnp.where((z >= 0) & (z < depth), moved, 0.0)
+
+
+def prepare_kernel(
+    features_in, cot_in, mask_in, masked_ref, cot_ref, live_ref, near_ref, far_ref,
+    features, cot, mask, sems,
+):
+    copies = [
+        pltpu.make_async_copy(source, held, sems.at[i])
+        for i, (source, held) in enumerate(
+            ((mask_in, mask), (features_in, features), (cot_in, cot))
+        )
+    ]
+    for copy in copies:
+        copy.start()
+    width, rows, channels = features.shape
+    f32 = jnp.float32
+    copies[0].wait()
+    flat = mask[...].astype(f32).reshape(width * rows // DEPTH, DEPTH)
+    live = jnp.broadcast_to(flat[:, :, None], flat.shape + (channels,)).reshape(features.shape)
+    live_ref[...] = live[:, :, :128]
+    copies[1].wait()
+    masked_ref[...] = (features[...].astype(f32) * live).astype(jnp.bfloat16)
+    copies[2].wait()
+    cot_ref[...] = (cot[...].astype(f32) * live).astype(jnp.bfloat16)
+    odd = lax.rem(position()[2], 2)
+    for ref, upper in ((near_ref, 1 - odd), (far_ref, odd)):
+        ref[0:2] = masked_ref[pl.ds(upper * (width - 2), 2)]
+        ref[2:3] = cot_ref[pl.ds(upper * (width - 1), 1)]
+
+
+def pack_kernel(masked, packed_ref):
+    width = masked.shape[0]
+    half = width // 2
+    packed_ref[:width] = masked[:, :, :128]
+    packed_ref[width:] = jnp.concatenate([masked[:half, :, 128:], masked[half:, :, 128:]], axis=2)
+
+
+def turn_kernel(weight, out_ref):
+    step = 2 * weight.shape[0]
+    total = weight.shape[1]
+    for start in range(0, total, step):
+        stop = min(start + step, total)
+        out_ref[start:stop, :] = weight[:, start:stop].T
+
+
+def strip_kernel(near, far, masked, cot, out_ref, edge):
+    width, rows, channels = masked.shape
+    f32 = jnp.float32
+    _, _, quad, side = position()
+    odd = lax.rem(quad, 2)
+    edge[odd] = far[...]
+    edge[1 - odd] = near[...]
+    ahead = side == 0
+
+    def rows_of(block, count):
+        block = block.astype(f32)
+        return jnp.where(ahead, block[:, rows - count :], block[:, :count])
+
+    halo = 2 * DEPTH
+    strips = [rows_of(edge[0, 0:2], halo), rows_of(masked[...], halo), rows_of(edge[1, 0:2], halo)]
+    cots = [rows_of(edge[0, 2:3], DEPTH), rows_of(cot[...], DEPTH), rows_of(edge[1, 2:3], DEPTH)]
+    first = (width + 4) * halo
+    out_ref[:first] = jnp.concatenate(strips).reshape(first, channels).astype(jnp.bfloat16)
+    last = (width + 2) * DEPTH
+    out_ref[first:] = jnp.concatenate(cots).reshape(last, channels).astype(jnp.bfloat16)
+
+
+def forward_kernel(masked, cot, near, far, across, live, weight, pick, *refs):
+    act_ref, gp_ref = refs[:2]
+    slice_refs = refs[2 : 2 + MEMBERS]
+    ext, edge, cols, slices = refs[2 + MEMBERS :]
+    width, rows, channels = masked.shape
+    f32 = jnp.float32
+    _, me, quad, side = position()
+    use_low = side.astype(f32)
+    use_high = (1 - side).astype(f32)
+    halo = 2 * DEPTH
+    tall = rows + 2 * halo
+    mid = rows + 2 * DEPTH
+    span = width + 4
+    strip = span * halo
+    odd = lax.rem(quad, 2)
+    edge[odd] = far[...]
+    edge[1 - odd] = near[...]
+    ext[0:2, halo : halo + rows, :] = edge[0, 0:2].astype(f32)
+    ext[2 : 2 + width, halo : halo + rows, :] = masked[...].astype(f32)
+    ext[2 + width :, halo : halo + rows, :] = edge[1, 0:2].astype(f32)
+    beyond = across[0:strip].astype(f32).reshape(span, halo, channels)
+    ext[:, 0:halo, :] = beyond * use_low
+    ext[:, halo + rows :, :] = beyond * use_high
+    field = ext[...].reshape(span * tall // DEPTH, DEPTH, channels)
+    for c in OFFSETS:
+        moved = shift_z(field, c).reshape(span, tall, channels)
+        for b in OFFSETS:
+            at = ((b + 1) * 3 + c + 1) * channels
+            start = DEPTH * (b + 1)
+            cols[:, :, at : at + channels] = moved[:, start : start + mid].astype(jnp.bfloat16)
+    nine = 9 * channels
+    pre = jnp.zeros(((width + 2) * mid, channels), f32)
+    for a in range(3):
+        pre += jnp.dot(
+            cols[a : a + width + 2].reshape((width + 2) * mid, nine),
+            weight[a * nine : (a + 1) * nine, :],
+            preferred_element_type=f32,
+        )
+    sig = jax.nn.sigmoid(pre)
+    act = (pre * sig).reshape(width + 2, mid, channels)[1 : 1 + width, DEPTH : DEPTH + rows]
+    act_ref[...] = (act * live[:, :, 0:1]).astype(jnp.bfloat16)
+    slope = (sig * (1.0 + pre * (1.0 - sig))).reshape(width + 2, mid, channels)
+    beyond = across[strip:].astype(f32).reshape(width + 2, DEPTH, channels)
+    centre = jnp.concatenate([edge[0, 2:3], cot[...], edge[1, 2:3]], axis=0).astype(f32)
+    full = jnp.concatenate([beyond * use_low, centre, beyond * use_high], axis=1)
+    grad = full * slope
+    gp_ref[...] = grad.astype(jnp.bfloat16)
+    inner = grad[:, DEPTH : DEPTH + rows].astype(jnp.bfloat16)
+    turned = lax.dot_general(
+        pick[...],
+        inner.reshape((width + 2) * rows, channels),
+        (((1,), (1,)), ((), ())),
+        preferred_element_type=f32,
+    )
+    slices[...] = turned.reshape(slices.shape).astype(jnp.bfloat16)
+    for distance, ref in enumerate(slice_refs):
+        ref[...] = slices[me ^ distance]
+
+
+def input_kernel(gp, live, turned, out_ref, cols, weight):
+    width, rows, channels = out_ref.shape
+    f32 = jnp.float32
+    tall = rows + 2 * DEPTH
+    for tap in range(27):
+        weight[tap * channels : (tap + 1) * channels, :] = turned[
+            :, tap * channels : (tap + 1) * channels
+        ]
+    field = gp[...].astype(f32).reshape((width + 2) * tall // DEPTH, DEPTH, channels)
+    for c in OFFSETS:
+        moved = shift_z(field, -c).reshape(width + 2, tall, channels)
+        for b in OFFSETS:
+            at = ((b + 1) * 3 + c + 1) * channels
+            start = DEPTH * (1 - b)
+            cols[:, :, at : at + channels] = moved[:, start : start + rows].astype(jnp.bfloat16)
+    nine = 9 * channels
+    total = jnp.zeros((width * rows, channels), f32)
+    for a in range(3):
+        total += jnp.dot(
+            cols[2 - a : 2 - a + width].reshape(width * rows, nine),
+            weight[a * nine : (a + 1) * nine, :],
+            preferred_element_type=f32,
+        )
+    out_ref[...] = (total.reshape(width, rows, channels) * live[:, :, 0:1]).astype(jnp.bfloat16)
+
+
+def kernel_grad_kernel(*refs):
+    received, bricks = refs[:MEMBERS], refs[MEMBERS : 2 * MEMBERS]
+    own_ref, *send_refs = refs[2 * MEMBERS : 2 * MEMBERS + 4]
+    slices, cols, part, stage, masked, sems = refs[2 * MEMBERS + 4 :]
+    f32 = jnp.float32
+    group, lanes = received[0].shape
+    slabs, lane, channels = masked.shape
+    per = slabs // QUAD
+    half = lane // 2
+    plane, me, quad, side = position()
+    copies = []
+    for member in range(MEMBERS):
+        to_quad, to_side = quad ^ (member // SIDES), side ^ (member % SIDES)
+        copies.append(
+            pltpu.make_async_copy(bricks[member], stage.at[to_quad, to_side], sems.at[member])
+        )
+    for copy in copies:
+        copy.start()
+    for distance in range(MEMBERS):
+        slices[me ^ distance] = received[distance][...]
+    at = lax.broadcasted_iota(jnp.int32, (group, lane), 1)
+    y, z = at // DEPTH, at % DEPTH
+    tall = lane // DEPTH
+    base = [None] * (slabs + 2)
+    for quad in range(QUAD):
+        first = slices[2 * quad].astype(f32)
+        second = slices[2 * quad + 1].astype(f32)
+        for m in range((per + 2) // 2):
+            one = first[:, m * lane : (m + 1) * lane]
+            two = second[:, m * lane : (m + 1) * lane]
+            pair = (
+                jnp.where(at < half, one, pltpu.roll(two, half, 1)),
+                jnp.where(at < half, pltpu.roll(one, half, 1), two),
+            )
+            for odd in range(2):
+                k = 2 * m + odd
+                slab = quad * per + k
+                inside = 1 <= k <= per
+                edge = (quad == 0 and k == 0) or (quad == QUAD - 1 and k == per + 1)
+                if inside or edge:
+                    base[slab] = pair[odd]
+    for slab in range(slabs + 2):
+        pieces = []
+        for b in OFFSETS:
+            for c in OFFSETS:
+                step = (DEPTH * b + c) % lane
+                moved = base[slab] if step == 0 else pltpu.roll(base[slab], step, 1)
+                keep = (y - b >= 0) & (y - b < tall) & (z - c >= 0) & (z - c < DEPTH)
+                pieces.append(jnp.where(keep, moved, 0.0))
+        cols[:, slab * lane : (slab + 1) * lane] = jnp.concatenate(pieces, axis=0).astype(
+            jnp.bfloat16
+        )
+    for copy in copies:
+        copy.wait()
+    for quad in range(QUAD):
+        for side in range(SIDES):
+            at_rows = pl.ds(side * half, half)
+            for x in range(per):
+                shift = 64 * (x // (per // 2))
+                rest = stage[quad, side, per + x % (per // 2)]
+                masked[quad * per + x, at_rows, :128] = stage[quad, side, x]
+                masked[quad * per + x, at_rows, 128:] = rest[:, shift : shift + 64]
+    field = masked[...].reshape(slabs * lane, channels)
+    planes = part.shape[0]
+    for a in range(3):
+        start = (2 - a) * lane
+        got = jnp.dot(
+            cols[:, start : start + slabs * lane], field, preferred_element_type=f32
+        ).reshape(9, planes, 8, channels)
+        for to in range(planes):
+            part[to, :, a * 9 * channels : (a + 1) * 9 * channels] = jnp.concatenate(
+                [got[tap, to] for tap in range(9)], axis=1
+            )
+    own_ref[...] = part[plane]
+    for distance, ref in enumerate(send_refs, 1):
+        ref[...] = part[plane ^ distance].astype(jnp.bfloat16)
+
+
+def sum_kernel(scale, own, one, two, three, out_ref):
+    f32 = jnp.float32
+    total = own[...] + one[...].astype(f32) + two[...].astype(f32) + three[...].astype(f32)
+    out_ref[...] = total * scale
+
+
+def join_kernel(mine, other, out_ref):
+    share = out_ref.shape[0] // SIDES
+    ahead = position()[3] == 0
+    first = jnp.where(ahead, mine[...], other[...])
+    second = jnp.where(ahead, other[...], mine[...])
+    out_ref[0:share] = first[:share]
+    out_ref[share:] = second[:share]
+
+
+def call(body, name, mebibytes, flops, moved, out_shape, scratch=(), in_specs=None):
+    spec = pl.BlockSpec(memory_space=pltpu.VMEM)
+
+    def run(*operands):
+        return pl.pallas_call(
+            body,
+            out_shape=out_shape,
+            in_specs=in_specs or [spec] * len(operands),
+            out_specs=jax.tree.map(lambda _: spec, out_shape),
+            scratch_shapes=scratch,
+            compiler_params=pltpu.CompilerParams(vmem_limit_bytes=mebibytes << 20),
+            cost_estimate=pl.CostEstimate(flops=flops, bytes_accessed=moved, transcendentals=0),
+            name=name,
+        )(*operands)
+
+    return run
+
+
+def channel_order(channels, planes):
+    per = channels // (planes * QUAD)
+    share = per // SIDES
+    index = np.arange(MEMBERS * planes * 8)
+    quad, side = index // (SIDES * planes * 8), index // (planes * 8) % SIDES
+    plane, row = index // 8 % planes, index % 8
+    channel = per * (QUAD * plane + quad) + share * side + row
+    return (np.where(row < share, channel, -1)[:, None] == np.arange(channels)[None, :])
+
+
+def planes_local(features, weight, voxel_mask, cotangent):
+    bf16 = jnp.bfloat16
+    f32 = jnp.float32
+    array = jax.ShapeDtypeStruct
+    width, wide_y, depth, channels = features.shape
+    rows = wide_y * depth
+    planes = lax.axis_size("depth")
+    count = planes * QUAD
+    total = 27 * channels
+    halo = 2 * DEPTH
+    span = (width + 2) * rows
+    group = planes * 8
+
+    def swap(piece, axes, distance, size):
+        return lax.ppermute(piece, axes, [(i, i ^ distance) for i in range(size)])
+
+    def in_plane(piece, distance):
+        return swap(piece, ("quad", "narrow"), distance, MEMBERS)
+
+    brick = array((width, rows, channels), bf16)
+    slab = array((3, rows, channels), bf16)
+    masked, cot, live, near, far = call(
+        prepare_kernel, "prepare", 16, 1 << 20, 1 << 20,
+        (brick, brick, array((width, rows, 128), f32), slab, slab),
+        (
+            pltpu.VMEM(brick.shape, bf16),
+            pltpu.VMEM(brick.shape, bf16),
+            pltpu.VMEM((width, wide_y, depth), jnp.int32),
+            pltpu.SemaphoreType.DMA((3,)),
+        ),
+        [pl.BlockSpec(memory_space=pltpu.HBM)] * 3,
+    )(
+        features.reshape(width, rows, channels),
+        cotangent.reshape(width, rows, channels),
+        voxel_mask,
+    )
+    near = swap(near, WIDE, 1, count)
+    far = lax.ppermute(
+        far, WIDE, [(i, j) for i in range(count) if 0 <= (j := ((i + 1) ^ 1) - 1) < count]
+    )
+    weight_rows = call(
+        turn_kernel, "turn", 8, 1 << 20, 4 << 20, array((total, channels), bf16)
+    )(weight.T)
+    edge = call(
+        strip_kernel, "strip", 4, 1 << 16, 1 << 18,
+        array(((width + 4) * halo + (width + 2) * DEPTH, channels), bf16),
+        (pltpu.VMEM((2,) + slab.shape, bf16),),
+    )(near, far, masked, cot)
+    packed = call(
+        pack_kernel, "pack", 4, 1 << 16, 1 << 19,
+        array((width * channels // 128, rows, 128), bf16),
+    )(masked)
+    packed, edge = lax.optimization_barrier((packed, edge))
+    across = in_plane(edge, 1)
+    bricks = [packed] + [None] * (MEMBERS - 1)
+    for distance in (5, 4, 1, 2):
+        bricks[distance] = in_plane(packed, distance)
+
+    mid = rows + 2 * DEPTH
+    pick = jnp.asarray(channel_order(channels, planes), bf16)
+    act, gp, *slices = call(
+        forward_kernel, "forward", 28, 800 * 5184 * 256, 1 << 20,
+        (brick, array((width + 2, mid, channels), bf16)) + (array((group, span), bf16),) * MEMBERS,
+        (
+            pltpu.VMEM((width + 4, rows + 2 * halo, channels), f32),
+            pltpu.VMEM((2,) + slab.shape, bf16),
+            pltpu.VMEM((width + 4, mid, 9 * channels), bf16),
+            pltpu.VMEM((MEMBERS, group, span), bf16),
+        ),
+    )(masked, cot, near, far, across, live, weight_rows, pick)
+    for distance in (5, 7, 4, 6, 1, 3, 2):
+        slices[distance] = in_plane(slices[distance], distance)
+    for distance in (5, 4, 1):
+        bricks[distance ^ 2] = in_plane(bricks[distance], 2)
+
+    grad_input = call(
+        input_kernel, "input_gradient", 20, 2 * 512 * 5184 * 256, 4 << 20, brick,
+        (
+            pltpu.VMEM((width + 2, rows, 9 * channels), bf16),
+            pltpu.VMEM((total, channels), bf16),
+        ),
+    )(gp, live, weight.T)
+
+    plane_rows = QUAD * width, SIDES * rows
+    send = array((8, total), bf16)
+    own, *sends = call(
+        kernel_grad_kernel, "kernel_gradient", 24, 2 * 288 * 3 * 4096 * 256, 4 << 20,
+        (array((8, total), f32),) + (send,) * (planes - 1),
+        (
+            pltpu.VMEM((MEMBERS, group, span), bf16),
+            pltpu.VMEM((9 * group, (plane_rows[0] + 2) * plane_rows[1]), bf16),
+            pltpu.VMEM((planes, 8, total), f32),
+            pltpu.VMEM((QUAD, SIDES) + packed.shape, bf16),
+            pltpu.VMEM(plane_rows + (channels,), bf16),
+            pltpu.SemaphoreType.DMA((MEMBERS,)),
+        ),
+        [pl.BlockSpec(memory_space=pltpu.VMEM)] * MEMBERS
+        + [pl.BlockSpec(memory_space=pl.ANY)] * MEMBERS,
+    )(*slices, *bricks)
+    got = [swap(sent, "depth", d, planes) for d, sent in enumerate(sends, 1)]
+    voxels = count * SIDES * width * rows
+    mine = call(
+        functools.partial(sum_kernel, float(1.0 / voxels**0.5)),
+        "plane_sum", 4, 8 * total * 4, 8 * total * 14, array((8, total), f32),
+    )(own, *got)
+    other = in_plane(mine, 1)
+    grad_weight = call(
+        join_kernel, "join", 4, 8 * total, 8 * total * 14, array((channels // count, total), f32)
+    )(mine, other)
+    shape = features.shape
+    return act.reshape(shape), grad_input.reshape(shape), grad_weight
 
 
 def padded_2(cells, sides, width):
@@ -39,7 +450,7 @@
     return jnp.concatenate(pieces, axis=1)
 
 
-def local(features, weight, voxel_mask, cotangent):
+def summed_local(features, weight, voxel_mask, cotangent):
     width_x, width_y, depth_z, channels = features.shape
     masked = features * voxel_mask.astype(jnp.bfloat16)[..., None]
     padded = padded_2(masked, (("wide", 0), ("narrow", 1)), 1)
@@ -80,20 +491,30 @@
     return (activation, grad_input, grad_weight)
 
 
-def solution(mesh):
+def sharded(body, mesh, wide):
     return jax.shard_map(
-        local,
+        body,
         mesh=mesh,
         in_specs=(
-            P("wide", "narrow", None, None),
+            P(wide, "narrow", None, None),
             P(),
-            P("wide", "narrow", None),
-            P("wide", "narrow", None, None),
+            P(wide, "narrow", None),
+            P(wide, "narrow", None, None),
         ),
         out_specs=(
-            P("wide", "narrow", None, None),
-            P("wide", "narrow", None, None),
-            P("wide", None),
+            P(wide, "narrow", None, None),
+            P(wide, "narrow", None, None),
+            P(wide, None),
         ),
         check_vma=False,
     )
+
+
+def solution(mesh):
+    wide, narrow = mesh.shape["wide"], mesh.shape["narrow"]
+    if wide != 4 * QUAD or narrow != SIDES:
+        return sharded(summed_local, mesh, "wide")
+    planes = Mesh(
+        mesh.devices.reshape(wide // QUAD, QUAD, narrow), ("depth", "quad", "narrow")
+    )
+    return sharded(planes_local, planes, WIDE)

time: 229 us -> 70.5 us (0.31)
  local copies, waits for them, and re-layouts: 81.2 us -> 4.22 us
  waiting for transfers between devices: 88.6 us -> 25.8 us
  matrix products: 14.2 us -> 0 us
  between operations: 14.5 us -> 0.74 us
  Pallas kernels: 0 us -> 13.5 us
  starting transfers between devices: 17.4 us -> 26 us
  other arithmetic: 5.93 us -> 0 us
  blocking collectives: 5.57 us -> 0 us
    unnamed x2 -> x0, waiting for transfers between devices: 82.1 us -> none
    reshape x27 -> x0, local copies, waits for them, and re-layouts: 27.9 us -> none  [the longest x26 21.9 us: gather_taps(): pieces.append(piece.reshape(-1, channels))]
    unnamed x37 -> x12, local copies, waits for them, and re-layouts: 27.6 us -> 4.22 us
    ppermute x8 -> x21, waiting for transfers between devices: 6.43 us -> 25.8 us  [the longest x20 25.8 us: swap(): return lax.ppermute(piece, axes, [(i, i ^ distance) for i in range(size)])]
    dot_general x3 -> x0, matrix products: 14.2 us -> none  [the longest x1 5.75 us: local(): lax.dot_general(grad_pre, columns, (((0,), (0,)), ((), ())), preferred_el...]
    pallas_call x0 -> x9, Pallas kernels: none -> 13.5 us  [run(): pl.pallas_call(body, out_shape=out_shape, in_specs=in_specs or [spec] * l...]
    concatenate x2 -> x0, local copies, waits for them, and re-layouts: 11.6 us -> none  [gather_taps(): return jnp.concatenate(pieces, axis=1)]
    ppermute x8 -> x21, starting transfers between devices: 17.4 us -> 26 us  [the longest x20 25.3 us: swap(): return lax.ppermute(piece, axes, [(i, i ^ distance) for i in range(size)])]
  transfers between devices with their start and end apart: 9 -> 21, of which waited for: 3 -> 11; matrix products, arithmetic and copies ran while one was open for 33% -> 0% of each run, Pallas kernels for 0% -> 10%
where the time goes in v4:
time: 70.5 us; the launch traced here: 70.2 us
  starting transfers between devices  26 us (37%)
  waiting for transfers between devices  25.8 us (37%)
  Pallas kernels  13.5 us (19%)
  local copies, waits for them, and re-layouts  4.22 us (6%)
  between operations  0.74 us (1%)
    ppermute x20, waiting for transfers between devices, swap(): return lax.ppermute(piece, axes, [(i, i ^ distance) for i in range(size)])  25.8 us
    ppermute x20, starting transfers between devices, swap(): return lax.ppermute(piece, axes, [(i, i ^ distance) for i in range(size)])  25.3 us
    pallas_call x9, Pallas kernels, run(): pl.pallas_call(body, out_shape=out_shape, in_specs=in_specs or [spec] * l...  13.5 us
    unnamed x12, local copies, waits for them, and re-layouts  4.22 us
  transfers between devices with their start and end apart: 21, of which 11 were waited for; matrix products, arithmetic and copies ran while one was open for 0% of the time, Pallas kernels for 10%

profile of v4, /device:TPU:0, one launch (start us, length us, event | category | flops | bytes accessed | tf_op | source)
XLA Modules:
  0.0 70.2 jit_solution(15953050039925957502)
XLA Ops:
  0.6 0.0 copy-start.2
  0.6 0.9 %copy-done.2 = bf16[8,8,8,192]{3,2,1,0:T(8,128)(2,1)S(1)} copy-done((bf16[8,8,8,192]{3,2,1,0:T(8,128)(2,1)S(1)}, bf16[8,8,8,192]{3,2,1,0:T(8,128)(2,1)}, u32[]{:S(2)}) %copy-start.2) | copy-done | bytes 196632
  1.6 0.0 copy-start.3
  1.6 0.9 %copy-done.3 = bf16[8,8,8,192]{3,2,1,0:T(8,128)(2,1)S(1)} copy-done((bf16[8,8,8,192]{3,2,1,0:T(8,128)(2,1)S(1)}, bf16[8,8,8,192]{3,2,1,0:T(8,128)(2,1)}, u32[]{:S(2)}) %copy-start.3) | copy-done | bytes 196632
  2.5 0.0 copy-start.4
  2.5 0.8 %copy-done.4 = s32[8,8,8]{2,1,0:T(8,128)S(1)} copy-done((s32[8,8,8]{2,1,0:T(8,128)S(1)}, s32[8,8,8]{2,1,0:T(8,128)}, u32[]{:S(2)}) %copy-start.4) | copy-done | bytes 2072
  3.3 0.3 prepare.1
  3.6 0.5 collective-permute-start
  4.2 0.7 collective-permute-start.1
  4.8 0.1 pack.1.refs_8_
  4.9 0.2 collective-permute-done.near
  5.1 0.0 collective-permute-done.1.far
  5.1 0.0 copy-start.5
  5.1 0.1 strip.1
  5.2 2.9 %collective-permute-start.2 = (bf16[272,192]{1,0:T(8,128)(2,1)S(1)}, bf16[272,192]{1,0:T(8,128)(2,1)S(1)}, u32[]{:S(2)}, u32[]{:S(2)}) collective-permute-start(bf16[272,192]{1,0:T(8,128)(2,1)S(1)} %strip.1), channel_id=1, source_target_pairs={{0,1},{1,0},{2,3},{3,2},{4,5},{5,4},{6,7},{7,6},{8,9},{9,8},{10,11... | collective-permute-start | bytes 313352 | tf_op jit(solution)/shard_map/ppermute | solution.py:319
  8.1 0.1 collective-permute-start.10
  8.2 6.6 %collective-permute-start.13 = (bf16[12,64,128]{2,1,0:T(8,128)(2,1)S(1)}, bf16[12,64,128]{2,1,0:T(8,128)(2,1)S(1)}, u32[]{:S(2)}, u32[]{:S(2)}) collective-permute-start(bf16[12,64,128]{2,1,0:T(8,128)(2,1)S(1)} %pack.1.refs_8_), channel_id=1, source_target_pairs={{0,4},{1,5},{2,6},{3,7},{4,0},{5,1},{6,2},{7,3},{8,12},{9,13},{10,... | collective-permute-start | bytes 589832 | tf_op jit(solution)/shard_map/ppermute | solution.py:319
  14.8 1.0 %collective-permute-start.14 = (bf16[12,64,128]{2,1,0:T(8,128)(2,1)S(1)}, bf16[12,64,128]{2,1,0:T(8,128)(2,1)S(1)}, u32[]{:S(2)}, u32[]{:S(2)}) collective-permute-start(bf16[12,64,128]{2,1,0:T(8,128)(2,1)S(1)} %pack.1.refs_8_), channel_id=1, source_target_pairs={{0,5},{1,4},{2,7},{3,6},{4,1},{5,0},{6,3},{7,2},{8,13},{9,12},{10,... | collective-permute-start | bytes 589832 | tf_op jit(solution)/shard_map/ppermute | solution.py:319
  15.7 0.0 copy-start
  15.7 1.6 %copy-done = bf16[5184,192]{0,1:T(8,128)(2,1)S(1)} copy-done((bf16[5184,192]{0,1:T(8,128)(2,1)S(1)}, bf16[5184,192]{0,1:T(8,128)(2,1)}, u32[]{:S(2)}) %copy-start) | copy-done | bytes 1990680
  17.3 0.8 %turn.1.weight = bf16[5184,192]{1,0:T(8,128)(2,1)S(1)} custom-call(bf16[192,5184]{1,0:T(8,128)(2,1)S(1)} %bitcast.5), custom_call_target="tpu_custom_call" | custom-call | flops 1048576 | bytes 4194304 | tf_op jit(solution)/shard_map/turn/pallas_call | solution.py:281
  18.1 0.0 collective-permute-done.2.across
  18.1 0.0 copy-done.5
  18.1 3.6 %forward.1 = (bf16[8,64,192]{2,1,0:T(8,128)(2,1)}, bf16[10,80,192]{2,1,0:T(8,128)(2,1)S(1)}, bf16[32,640]{1,0:T(8,128)(2,1)S(1)}, bf16[32,640]{1,0:T(8,128)(2,1)...) custom-call(bf16[8,64,192]{2,1,0:T(8,128)(2,1)S(1)} %get-tuple-eleme, ...), custom_call_target="tpu_custom_call" | custom-call | flops 1061683200 | bytes 1048576 | tf_op jit(solution)/shard_map/forward/pallas_call | solution.py:281
  21.7 0.6 collective-permute-start.3
  22.3 0.3 collective-permute-start.4
  22.5 4.0 %collective-permute-done.3.refs_1_ = bf16[32,640]{1,0:T(8,128)(2,1)S(1)} collective-permute-done((bf16[32,640]{1,0:T(8,128)(2,1)S(1)}, bf16[32,640]{1,0:T(8,128)(2,1)S(1)}, u32[]{:S(2)}, u32[]{:S(2)}) %collective-permute-start.3) | collective-permute-done | bytes 40992 | tf_op jit(solution)/shard_map/ppermute | solution.py:319
  26.6 0.2 collective-permute-start.5
  26.8 0.0 collective-permute-done.4.refs_2_
  26.8 0.4 collective-permute-start.11
  27.2 0.0 collective-permute-done.10.refs_9_
  27.2 0.1 collective-permute-start.12
  27.3 0.0 collective-permute-done.13.refs_12_
  27.3 0.4 collective-permute-start.15
  27.7 0.0 collective-permute-done.14.refs_13_
  27.7 0.1 collective-permute-start.16
  27.8 2.4 %collective-permute-done.5.refs_3_ = bf16[32,640]{1,0:T(8,128)(2,1)S(1)} collective-permute-done((bf16[32,640]{1,0:T(8,128)(2,1)S(1)}, bf16[32,640]{1,0:T(8,128)(2,1)S(1)}, u32[]{:S(2)}, u32[]{:S(2)}) %collective-permute-start.5) | collective-permute-done | bytes 40992 | tf_op jit(solution)/shard_map/ppermute | solution.py:319
  30.2 2.0 %collective-permute-start.6 = (bf16[32,640]{1,0:T(8,128)(2,1)S(1)}, bf16[32,640]{1,0:T(8,128)(2,1)S(1)}, u32[]{:S(2)}, u32[]{:S(2)}) collective-permute-start(bf16[32,640]{1,0:T(8,128)(2,1)S(1)} %get-tuple-element.36), channel_id=1, source_target_pairs={{0,4},{1,5},{2,6},{3,7},{4,0},{5,1},{6,2},{7,3},{8,12},{9,13},{10,... | collective-permute-start | bytes 122888 | tf_op jit(solution)/shard_map/ppermute | solution.py:319
  32.2 2.0 %collective-permute-done.6.refs_4_ = bf16[32,640]{1,0:T(8,128)(2,1)S(1)} collective-permute-done((bf16[32,640]{1,0:T(8,128)(2,1)S(1)}, bf16[32,640]{1,0:T(8,128)(2,1)S(1)}, u32[]{:S(2)}, u32[]{:S(2)}) %collective-permute-start.6) | collective-permute-done | bytes 40992 | tf_op jit(solution)/shard_map/ppermute | solution.py:319
  34.2 2.6 %collective-permute-start.7 = (bf16[32,640]{1,0:T(8,128)(2,1)S(1)}, bf16[32,640]{1,0:T(8,128)(2,1)S(1)}, u32[]{:S(2)}, u32[]{:S(2)}) collective-permute-start(bf16[32,640]{1,0:T(8,128)(2,1)S(1)} %get-tuple-element.37), channel_id=1, source_target_pairs={{0,5},{1,4},{2,7},{3,6},{4,1},{5,0},{6,3},{7,2},{8,13},{9,12},{10,... | collective-permute-start | bytes 122888 | tf_op jit(solution)/shard_map/ppermute | solution.py:319
  36.7 2.3 %collective-permute-done.7.refs_5_ = bf16[32,640]{1,0:T(8,128)(2,1)S(1)} collective-permute-done((bf16[32,640]{1,0:T(8,128)(2,1)S(1)}, bf16[32,640]{1,0:T(8,128)(2,1)S(1)}, u32[]{:S(2)}, u32[]{:S(2)}) %collective-permute-start.7) | collective-permute-done | bytes 40992 | tf_op jit(solution)/shard_map/ppermute | solution.py:319
  39.1 0.0 collective-permute-start.8
  39.1 3.4 %collective-permute-done.8.refs_6_ = bf16[32,640]{1,0:T(8,128)(2,1)S(1)} collective-permute-done((bf16[32,640]{1,0:T(8,128)(2,1)S(1)}, bf16[32,640]{1,0:T(8,128)(2,1)S(1)}, u32[]{:S(2)}, u32[]{:S(2)}) %collective-permute-start.8) | collective-permute-done | bytes 40992 | tf_op jit(solution)/shard_map/ppermute | solution.py:319
  42.5 0.5 collective-permute-start.9
  43.0 3.8 %collective-permute-done.9.refs_7_ = bf16[32,640]{1,0:T(8,128)(2,1)S(1)} collective-permute-done((bf16[32,640]{1,0:T(8,128)(2,1)S(1)}, bf16[32,640]{1,0:T(8,128)(2,1)S(1)}, u32[]{:S(2)}, u32[]{:S(2)}) %collective-permute-start.9) | collective-permute-done | bytes 40992 | tf_op jit(solution)/shard_map/ppermute | solution.py:319
  46.8 0.0 collective-permute-done.11.refs_10_
  46.9 0.0 collective-permute-done.12.refs_11_
  46.9 0.0 collective-permute-done.15.refs_14_
  46.9 0.0 collective-permute-done.16.refs_15_
  46.9 0.0 copy-start.1
  46.9 5.2 %kernel_gradient.1 = (f32[8,5184]{1,0:T(8,128)S(1)}, bf16[8,5184]{1,0:T(8,128)(2,1)S(1)}, bf16[8,5184]{1,0:T(8,128)(2,1)S(1)}, bf16[8,5184]{1,0:T(8,128)(2,1)S(1)}) custom-call(bf16[32,640]{1,0:T(8,128)(2,1)S(1)} %get-tuple-element.32.refs_0_, bf16[32,640]{1,0:T(8,128)(2,1)S(1)} %collective-permute-done.3.refs_1_, ...), custom_call_target="tpu_custom_call" | custom-call | flops 1811939328 | bytes 4194304 | tf_op jit(solution)/shard_map/kernel_gradient/pallas_call | solution.py:281
  52.1 2.9 %collective-permute-start.17 = (bf16[8,5184]{1,0:T(8,128)(2,1)S(1)}, bf16[8,5184]{1,0:T(8,128)(2,1)S(1)}, u32[]{:S(2)}, u32[]{:S(2)}) collective-permute-start(bf16[8,5184]{1,0:T(8,128)(2,1)S(1)} %get-tuple-element.42), channel_id=1, source_target_pairs={{0,8},{8,0},{16,24},{24,16},{1,9},{9,1},{17,25},{25,17},{2,10},{10... | collective-permute-start | bytes 248840 | tf_op jit(solution)/shard_map/ppermute | solution.py:319
  55.0 2.6 %collective-permute-start.18 = (bf16[8,5184]{1,0:T(8,128)(2,1)S(1)}, bf16[8,5184]{1,0:T(8,128)(2,1)S(1)}, u32[]{:S(2)}, u32[]{:S(2)}) collective-permute-start(bf16[8,5184]{1,0:T(8,128)(2,1)S(1)} %get-tuple-element.43), channel_id=1, source_target_pairs={{0,16},{8,24},{16,0},{24,8},{1,17},{9,25},{17,1},{25,9},{2,18},{10... | collective-permute-start | bytes 248840 | tf_op jit(solution)/shard_map/ppermute | solution.py:319
  57.6 0.0 collective-permute-start.19
  57.6 0.7 collective-permute-done.17.one
  58.3 4.4 %collective-permute-done.18.two = bf16[8,5184]{1,0:T(8,128)(2,1)S(1)} collective-permute-done((bf16[8,5184]{1,0:T(8,128)(2,1)S(1)}, bf16[8,5184]{1,0:T(8,128)(2,1)S(1)}, u32[]{:S(2)}, u32[]{:S(2)}) %collective-permute-start.18) | collective-permute-done | bytes 82976 | tf_op jit(solution)/shard_map/ppermute | solution.py:319
  62.7 1.3 %collective-permute-done.19.three = bf16[8,5184]{1,0:T(8,128)(2,1)S(1)} collective-permute-done((bf16[8,5184]{1,0:T(8,128)(2,1)S(1)}, bf16[8,5184]{1,0:T(8,128)(2,1)S(1)}, u32[]{:S(2)}, u32[]{:S(2)}) %collective-permute-start.19) | collective-permute-done | bytes 82976 | tf_op jit(solution)/shard_map/ppermute | solution.py:319
  64.0 1.6 %collective-permute-start.20 = (f32[8,5184]{1,0:T(8,128)S(1)}, f32[8,5184]{1,0:T(8,128)S(1)}, u32[]{:S(2)}, u32[]{:S(2)}) collective-permute-start(f32[8,5184]{1,0:T(8,128)S(1)} %plane_sum.1.mine), channel_id=1, source_target_pairs={{0,1},{1,0},{2,3},{3,2},{4,5},{5,4},{6,7},{7,6},{8,9},{9,8},{10,11... | collective-permute-start | bytes 497672 | tf_op jit(solution)/shard_map/ppermute | solution.py:319
  65.6 0.0 copy-done.1
  65.6 2.6 %input_gradient.1 = bf16[8,64,192]{2,1,0:T(8,128)(2,1)} custom-call(bf16[10,80,192]{2,1,0:T(8,128)(2,1)S(1)} %get-tuple-element.31.gp, f32[8,64,128]{2,1,0:T(8,128)S(1)} %get-tuple-element.29.live, bf16[192,5184]{1,0:T(8,128)(2,1)S(1)} %bitcast.6), custom_call_target="tpu_custom_call" | custom-call | flops 1358954496 | bytes 4194304 | tf_op jit(solution)/shard_map/input_gradient/pallas_call | solution.py:281
  68.2 1.2 %collective-permute-done.20.other = f32[8,5184]{1,0:T(8,128)S(1)} collective-permute-done((f32[8,5184]{1,0:T(8,128)S(1)}, f32[8,5184]{1,0:T(8,128)S(1)}, u32[]{:S(2)}, u32[]{:S(2)}) %collective-permute-start.20) | collective-permute-done | bytes 165920 | tf_op jit(solution)/shard_map/ppermute | solution.py:319
  69.5 0.8 %join.1 = f32[12,5184]{1,0:T(8,128)} custom-call(f32[8,5184]{1,0:T(8,128)S(1)} %plane_sum.1.mine, f32[8,5184]{1,0:T(8,128)S(1)} %collective-permute-done.20.other), custom_call_target="tpu_custom_call" | custom-call | flops 41472 | bytes 580608 | tf_op jit(solution)/shard_map/join/pallas_call | solution.py:281
  (1 shorter events, 0.0 us)
Async XLA Ops:
  0.6 1.0 %copy-start.2 = (bf16[8,8,8,192]{3,2,1,0:T(8,128)(2,1)S(1)}, bf16[8,8,8,192]{3,2,1,0:T(8,128)(2,1)}, u32[]{:S(2)}) copy-start(bf16[8,8,8,192]{3,2,1,0:T(8,128)(2,1)} %param.5) | copy-start | bytes 589828
  1.6 0.9 %copy-start.3 = (bf16[8,8,8,192]{3,2,1,0:T(8,128)(2,1)S(1)}, bf16[8,8,8,192]{3,2,1,0:T(8,128)(2,1)}, u32[]{:S(2)}) copy-start(bf16[8,8,8,192]{3,2,1,0:T(8,128)(2,1)} %param.8) | copy-start | bytes 589828
  2.5 0.8 %copy-start.4 = (s32[8,8,8]{2,1,0:T(8,128)S(1)}, s32[8,8,8]{2,1,0:T(8,128)}, u32[]{:S(2)}) copy-start(s32[8,8,8]{2,1,0:T(8,128)} %mask_in.1) | copy-start | bytes 6148
  3.6 1.5 %collective-permute-start = (bf16[3,64,192]{2,1,0:T(8,128)(2,1)S(1)}, bf16[3,64,192]{2,1,0:T(8,128)(2,1)S(1)}, u32[]{:S(2)}, u32[]{:S(2)}) collective-permute-start(bf16[3,64,192]{2,1,0:T(8,128)(2,1)S(1)} %get-tuple-element.26), channel_id=1, source_target_pairs={{0,2},{2,0},{4,6},{6,4},{8,10},{10,8},{12,14},{14,12},{16,18},{18,... | collective-permute-start | bytes 221192 | tf_op jit(solution)/shard_map/ppermute | solution.py:319
  4.2 0.9 %collective-permute-start.1 = (bf16[3,64,192]{2,1,0:T(8,128)(2,1)S(1)}, bf16[3,64,192]{2,1,0:T(8,128)(2,1)S(1)}, u32[]{:S(2)}, u32[]{:S(2)}) collective-permute-start(bf16[3,64,192]{2,1,0:T(8,128)(2,1)S(1)} %get-tuple-element.27), channel_id=1, source_target_pairs={{2,4},{4,2},{6,8},{8,6},{10,12},{12,10},{14,16},{16,14},{18,20},{2... | collective-permute-start | bytes 221192 | tf_op jit(solution)/shard_map/ppermute | solution.py:342
  5.1 13.0 %copy-start.5 = (bf16[256,192]{1,0:T(8,128)(2,1)S(1)}, bf16[256,192]{1,0:T(8,128)(2,1)}, u32[]{:S(2)}) copy-start(bf16[256,192]{1,0:T(8,128)(2,1)} %constant.2.clone.pick) | copy-start | bytes 294916
  5.2 12.9 %collective-permute-start.2 = (bf16[272,192]{1,0:T(8,128)(2,1)S(1)}, bf16[272,192]{1,0:T(8,128)(2,1)S(1)}, u32[]{:S(2)}, u32[]{:S(2)}) collective-permute-start(bf16[272,192]{1,0:T(8,128)(2,1)S(1)} %strip.1), channel_id=1, source_target_pairs={{0,1},{1,0},{2,3},{3,2},{4,5},{5,4},{6,7},{7,6},{8,9},{9,8},{10,11... | collective-permute-start | bytes 313352 | tf_op jit(solution)/shard_map/ppermute | solution.py:319
  8.1 19.1 %collective-permute-start.10 = (bf16[12,64,128]{2,1,0:T(8,128)(2,1)S(1)}, bf16[12,64,128]{2,1,0:T(8,128)(2,1)S(1)}, u32[]{:S(2)}, u32[]{:S(2)}) collective-permute-start(bf16[12,64,128]{2,1,0:T(8,128)(2,1)S(1)} %pack.1.refs_8_), channel_id=1, source_target_pairs={{0,1},{1,0},{2,3},{3,2},{4,5},{5,4},{6,7},{7,6},{8,9},{9,8},{10,11... | collective-permute-start | bytes 589832 | tf_op jit(solution)/shard_map/ppermute | solution.py:319
  8.2 19.1 %collective-permute-start.13 = (bf16[12,64,128]{2,1,0:T(8,128)(2,1)S(1)}, bf16[12,64,128]{2,1,0:T(8,128)(2,1)S(1)}, u32[]{:S(2)}, u32[]{:S(2)}) collective-permute-start(bf16[12,64,128]{2,1,0:T(8,128)(2,1)S(1)} %pack.1.refs_8_), channel_id=1, source_target_pairs={{0,4},{1,5},{2,6},{3,7},{4,0},{5,1},{6,2},{7,3},{8,12},{9,13},{10,... | collective-permute-start | bytes 589832 | tf_op jit(solution)/shard_map/ppermute | solution.py:319
  14.8 12.9 %collective-permute-start.14 = (bf16[12,64,128]{2,1,0:T(8,128)(2,1)S(1)}, bf16[12,64,128]{2,1,0:T(8,128)(2,1)S(1)}, u32[]{:S(2)}, u32[]{:S(2)}) collective-permute-start(bf16[12,64,128]{2,1,0:T(8,128)(2,1)S(1)} %pack.1.refs_8_), channel_id=1, source_target_pairs={{0,5},{1,4},{2,7},{3,6},{4,1},{5,0},{6,3},{7,2},{8,13},{9,12},{10,... | collective-permute-start | bytes 589832 | tf_op jit(solution)/shard_map/ppermute | solution.py:319
  15.7 1.6 %copy-start = (bf16[5184,192]{0,1:T(8,128)(2,1)S(1)}, bf16[5184,192]{0,1:T(8,128)(2,1)}, u32[]{:S(2)}) copy-start(bf16[5184,192]{0,1:T(8,128)(2,1)} %param.6) | copy-start | bytes 5971972
  21.7 4.9 %collective-permute-start.3 = (bf16[32,640]{1,0:T(8,128)(2,1)S(1)}, bf16[32,640]{1,0:T(8,128)(2,1)S(1)}, u32[]{:S(2)}, u32[]{:S(2)}) collective-permute-start(bf16[32,640]{1,0:T(8,128)(2,1)S(1)} %get-tuple-element.33), channel_id=1, source_target_pairs={{0,1},{1,0},{2,3},{3,2},{4,5},{5,4},{6,7},{7,6},{8,9},{9,8},{10,11... | collective-permute-start | bytes 122888 | tf_op jit(solution)/shard_map/ppermute | solution.py:319
  22.3 4.5 %collective-permute-start.4 = (bf16[32,640]{1,0:T(8,128)(2,1)S(1)}, bf16[32,640]{1,0:T(8,128)(2,1)S(1)}, u32[]{:S(2)}, u32[]{:S(2)}) collective-permute-start(bf16[32,640]{1,0:T(8,128)(2,1)S(1)} %get-tuple-element.34), channel_id=1, source_target_pairs={{0,2},{1,3},{2,0},{3,1},{4,6},{5,7},{6,4},{7,5},{8,10},{9,11},{10,... | collective-permute-start | bytes 122888 | tf_op jit(solution)/shard_map/ppermute | solution.py:319
  26.6 3.6 %collective-permute-start.5 = (bf16[32,640]{1,0:T(8,128)(2,1)S(1)}, bf16[32,640]{1,0:T(8,128)(2,1)S(1)}, u32[]{:S(2)}, u32[]{:S(2)}) collective-permute-start(bf16[32,640]{1,0:T(8,128)(2,1)S(1)} %get-tuple-element.35), channel_id=1, source_target_pairs={{0,3},{1,2},{2,1},{3,0},{4,7},{5,6},{6,5},{7,4},{8,11},{9,10},{10,... | collective-permute-start | bytes 122888 | tf_op jit(solution)/shard_map/ppermute | solution.py:319
  26.8 20.1 %collective-permute-start.11 = (bf16[12,64,128]{2,1,0:T(8,128)(2,1)S(1)}, bf16[12,64,128]{2,1,0:T(8,128)(2,1)S(1)}, u32[]{:S(2)}, u32[]{:S(2)}) collective-permute-start(bf16[12,64,128]{2,1,0:T(8,128)(2,1)S(1)} %pack.1.refs_8_), channel_id=1, source_target_pairs={{0,2},{1,3},{2,0},{3,1},{4,6},{5,7},{6,4},{7,5},{8,10},{9,11},{10,... | collective-permute-start | bytes 589832 | tf_op jit(solution)/shard_map/ppermute | solution.py:319
  27.2 19.7 %collective-permute-start.12 = (bf16[12,64,128]{2,1,0:T(8,128)(2,1)S(1)}, bf16[12,64,128]{2,1,0:T(8,128)(2,1)S(1)}, u32[]{:S(2)}, u32[]{:S(2)}) collective-permute-start(bf16[12,64,128]{2,1,0:T(8,128)(2,1)S(1)} %collective-permute-done.10.refs_9_), channel_id=1, source_target_pairs={{0,2},{1,3},{2,0},{3,1},{4,6},{5,7},{6,4},{7,5},{8,10},{9,11},{10,... | collective-permute-start | bytes 589832 | tf_op jit(solution)/shard_map/ppermute | solution.py:319
  27.3 19.6 %collective-permute-start.15 = (bf16[12,64,128]{2,1,0:T(8,128)(2,1)S(1)}, bf16[12,64,128]{2,1,0:T(8,128)(2,1)S(1)}, u32[]{:S(2)}, u32[]{:S(2)}) collective-permute-start(bf16[12,64,128]{2,1,0:T(8,128)(2,1)S(1)} %collective-permute-done.13.refs_12_), channel_id=1, source_target_pairs={{0,2},{1,3},{2,0},{3,1},{4,6},{5,7},{6,4},{7,5},{8,10},{9,11},{10,... | collective-permute-start | bytes 589832 | tf_op jit(solution)/shard_map/ppermute | solution.py:319
  27.7 19.2 %collective-permute-start.16 = (bf16[12,64,128]{2,1,0:T(8,128)(2,1)S(1)}, bf16[12,64,128]{2,1,0:T(8,128)(2,1)S(1)}, u32[]{:S(2)}, u32[]{:S(2)}) collective-permute-start(bf16[12,64,128]{2,1,0:T(8,128)(2,1)S(1)} %collective-permute-done.14.refs_13_), channel_id=1, source_target_pairs={{0,2},{1,3},{2,0},{3,1},{4,6},{5,7},{6,4},{7,5},{8,10},{9,11},{10,... | collective-permute-start | bytes 589832 | tf_op jit(solution)/shard_map/ppermute | solution.py:319
  30.2 4.0 %collective-permute-start.6 = (bf16[32,640]{1,0:T(8,128)(2,1)S(1)}, bf16[32,640]{1,0:T(8,128)(2,1)S(1)}, u32[]{:S(2)}, u32[]{:S(2)}) collective-permute-start(bf16[32,640]{1,0:T(8,128)(2,1)S(1)} %get-tuple-element.36), channel_id=1, source_target_pairs={{0,4},{1,5},{2,6},{3,7},{4,0},{5,1},{6,2},{7,3},{8,12},{9,13},{10,... | collective-permute-start | bytes 122888 | tf_op jit(solution)/shard_map/ppermute | solution.py:319
  34.2 4.9 %collective-permute-start.7 = (bf16[32,640]{1,0:T(8,128)(2,1)S(1)}, bf16[32,640]{1,0:T(8,128)(2,1)S(1)}, u32[]{:S(2)}, u32[]{:S(2)}) collective-permute-start(bf16[32,640]{1,0:T(8,128)(2,1)S(1)} %get-tuple-element.37), channel_id=1, source_target_pairs={{0,5},{1,4},{2,7},{3,6},{4,1},{5,0},{6,3},{7,2},{8,13},{9,12},{10,... | collective-permute-start | bytes 122888 | tf_op jit(solution)/shard_map/ppermute | solution.py:319
  39.1 3.4 %collective-permute-start.8 = (bf16[32,640]{1,0:T(8,128)(2,1)S(1)}, bf16[32,640]{1,0:T(8,128)(2,1)S(1)}, u32[]{:S(2)}, u32[]{:S(2)}) collective-permute-start(bf16[32,640]{1,0:T(8,128)(2,1)S(1)} %get-tuple-element.38), channel_id=1, source_target_pairs={{0,6},{1,7},{2,4},{3,5},{4,2},{5,3},{6,0},{7,1},{8,14},{9,15},{10,... | collective-permute-start | bytes 122888 | tf_op jit(solution)/shard_map/ppermute | solution.py:319
  42.5 4.3 %collective-permute-start.9 = (bf16[32,640]{1,0:T(8,128)(2,1)S(1)}, bf16[32,640]{1,0:T(8,128)(2,1)S(1)}, u32[]{:S(2)}, u32[]{:S(2)}) collective-permute-start(bf16[32,640]{1,0:T(8,128)(2,1)S(1)} %get-tuple-element.39), channel_id=1, source_target_pairs={{0,7},{1,6},{2,5},{3,4},{4,3},{5,2},{6,1},{7,0},{8,15},{9,14},{10,... | collective-permute-start | bytes 122888 | tf_op jit(solution)/shard_map/ppermute | solution.py:319
  46.9 18.8 %copy-start.1 = (bf16[5184,192]{0,1:T(8,128)(2,1)S(1)}, bf16[5184,192]{0,1:T(8,128)(2,1)}, u32[]{:S(2)}) copy-start(bf16[5184,192]{0,1:T(8,128)(2,1)} %param.6) | copy-start | bytes 5971972
  52.1 6.2 %collective-permute-start.17 = (bf16[8,5184]{1,0:T(8,128)(2,1)S(1)}, bf16[8,5184]{1,0:T(8,128)(2,1)S(1)}, u32[]{:S(2)}, u32[]{:S(2)}) collective-permute-start(bf16[8,5184]{1,0:T(8,128)(2,1)S(1)} %get-tuple-element.42), channel_id=1, source_target_pairs={{0,8},{8,0},{16,24},{24,16},{1,9},{9,1},{17,25},{25,17},{2,10},{10... | collective-permute-start | bytes 248840 | tf_op jit(solution)/shard_map/ppermute | solution.py:319
  55.0 7.7 %collective-permute-start.18 = (bf16[8,5184]{1,0:T(8,128)(2,1)S(1)}, bf16[8,5184]{1,0:T(8,128)(2,1)S(1)}, u32[]{:S(2)}, u32[]{:S(2)}) collective-permute-start(bf16[8,5184]{1,0:T(8,128)(2,1)S(1)} %get-tuple-element.43), channel_id=1, source_target_pairs={{0,16},{8,24},{16,0},{24,8},{1,17},{9,25},{17,1},{25,9},{2,18},{10... | collective-permute-start | bytes 248840 | tf_op jit(solution)/shard_map/ppermute | solution.py:319
  57.6 6.4 %collective-permute-start.19 = (bf16[8,5184]{1,0:T(8,128)(2,1)S(1)}, bf16[8,5184]{1,0:T(8,128)(2,1)S(1)}, u32[]{:S(2)}, u32[]{:S(2)}) collective-permute-start(bf16[8,5184]{1,0:T(8,128)(2,1)S(1)} %get-tuple-element.44), channel_id=1, source_target_pairs={{0,24},{8,16},{16,8},{24,0},{1,25},{9,17},{17,9},{25,1},{2,26},{10... | collective-permute-start | bytes 248840 | tf_op jit(solution)/shard_map/ppermute | solution.py:319
  64.0 5.4 %collective-permute-start.20 = (f32[8,5184]{1,0:T(8,128)S(1)}, f32[8,5184]{1,0:T(8,128)S(1)}, u32[]{:S(2)}, u32[]{:S(2)}) collective-permute-start(f32[8,5184]{1,0:T(8,128)S(1)} %plane_sum.1.mine), channel_id=1, source_target_pairs={{0,1},{1,0},{2,3},{3,2},{4,5},{5,4},{6,7},{7,6},{8,9},{9,8},{10,11... | collective-permute-start | bytes 497672 | tf_op jit(solution)/shard_map/ppermute | solution.py:319

commit v5 on v4

v5 whole, which is shorter than its diff:
```python
import functools

import jax
import jax.numpy as jnp
from jax import lax
from jax.experimental import pallas as pl
from jax.experimental.pallas import tpu as pltpu
from jax.sharding import Mesh
from jax.sharding import PartitionSpec as P

WIDE = ("depth", "quad")
QUAD = 4
SIDES = 2
MEMBERS = QUAD * SIDES
CHIPS = (0, 1, 4, 5)
OFFSETS = (-1, 0, 1)
DEPTH = 8


def position():
    quad, side = lax.axis_index("quad"), lax.axis_index("narrow")
    return lax.axis_index("depth"), quad * SIDES + side, quad, side


def shift_z(field, step):
    if step == 0:
        return field
    depth = field.shape[1]
    moved = pltpu.roll(field, (-step) % depth, 1)
    z = lax.broadcasted_iota(jnp.int32, field.shape, 1) + step
    return jnp.where((z >= 0) & (z < depth), moved, 0.0)


def pick_kernel(planes, out_ref):
    index = lax.broadcasted_iota(jnp.int32, out_ref.shape, 0)
    column = lax.broadcasted_iota(jnp.int32, out_ref.shape, 1)
    per = out_ref.shape[1] // (planes * QUAD)
    share = per // SIDES
    quad, side = index // (SIDES * planes * 8), index // (planes * 8) % SIDES
    plane, row = index // 8 % planes, index % 8
    channel = per * (QUAD * plane + quad) + share * side + row
    out_ref[...] = jnp.where((row < share) & (channel == column), 1.0, 0.0).astype(jnp.bfloat16)


def prepare_kernel(
    features, cot, mask, first, masked_ref, cot_ref, live_ref,
    near_ref, far_ref, across_ref, near_across_ref, far_across_ref,
):
    width, rows, channels = features.shape
    f32 = jnp.float32
    bf16 = jnp.bfloat16
    flat = mask[...].astype(f32).reshape(width * rows // DEPTH, DEPTH)
    live = jnp.broadcast_to(flat[:, :, None], flat.shape + (channels,)).reshape(features.shape)
    live_ref[...] = live[:, :, :128]
    masked = features[...].astype(f32) * live
    masked_ref[...] = masked.astype(bf16)
    grown = cot[...].astype(f32) * live
    cot_ref[...] = grown.astype(bf16)
    _, _, quad, side = position()
    odd = lax.rem(quad, 2)
    ahead = side == 0
    halo = 2 * DEPTH
    strip = jnp.where(ahead, masked[:, rows - halo :], masked[:, :halo])
    cots = jnp.where(ahead, grown[:, rows - DEPTH :], grown[:, :DEPTH])
    across_ref[: width * halo] = strip.reshape(-1, channels).astype(bf16)
    across_ref[width * halo :] = cots.reshape(-1, channels).astype(bf16)
    blank = jnp.zeros((DEPTH, channels), f32)
    corners = [
        jnp.concatenate([strip[x : x + 2].reshape(-1, channels), cots[y], blank], axis=0)
        for x, y in ((0, 0), (width - 2, width - 1))
    ]
    for upper, ref, corner_ref in ((1 - odd, near_ref, near_across_ref), (odd, far_ref, far_across_ref)):
        ref[0:2] = masked_ref[pl.ds(upper * (width - 2), 2)]
        ref[2:3] = cot_ref[pl.ds(upper * (width - 1), 1)]
        corner_ref[...] = jnp.where(upper == 1, corners[1], corners[0]).astype(bf16)


def pack_kernel(masked, packed_ref):
    width = masked.shape[0]
    half = width // 2
    packed_ref[:width] = masked[:, :, :128]
    packed_ref[width:] = jnp.concatenate([masked[:half, :, 128:], masked[half:, :, 128:]], axis=2)


def turn_kernel(weight, out_ref):
    step = 2 * weight.shape[0]
    total = weight.shape[1]
    for start in range(0, total, step):
        stop = min(start + step, total)
        out_ref[start:stop, :] = weight[:, start:stop].T


def forward_kernel(
    masked, cot, near, far, across, near_across, far_across, live, weight, pick, *refs
):
    act_ref, gp_ref = refs[:2]
    slice_refs = refs[2 : 2 + len(CHIPS)]
    ext, edge, corner, cols, slices = refs[2 + len(CHIPS) :]
    width, rows, channels = masked.shape
    f32 = jnp.float32
    plane, me, quad, side = position()
    use_low = side.astype(f32)
    use_high = (1 - side).astype(f32)
    place = plane * QUAD + quad
    use_left = (place > 0).astype(f32)
    use_right = (place < QUAD * lax.axis_size("depth") - 1).astype(f32)
    halo = 2 * DEPTH
    tall = rows + 2 * halo
    mid = rows + 2 * DEPTH
    span = width + 4
    odd = lax.rem(quad, 2)
    edge[odd] = far[...]
    edge[1 - odd] = near[...]
    corner[odd] = far_across[...]
    corner[1 - odd] = near_across[...]
    left, right = edge[0].astype(f32) * use_left, edge[1].astype(f32) * use_right
    lower, upper = corner[0].astype(f32) * use_left, corner[1].astype(f32) * use_right
    ext[0:2, halo : halo + rows, :] = left[0:2]
    ext[2 : 2 + width, halo : halo + rows, :] = masked[...].astype(f32)
    ext[2 + width :, halo : halo + rows, :] = right[0:2]
    beside = across[: width * halo].astype(f32).reshape(width, halo, channels)
    for use, start in ((use_low, 0), (use_high, halo + rows)):
        at = slice(start, start + halo)
        ext[0:2, at, :] = lower[: 2 * halo].reshape(2, halo, channels) * use
        ext[2 : 2 + width, at, :] = beside * use
        ext[2 + width :, at, :] = upper[: 2 * halo].reshape(2, halo, channels) * use
    field = ext[...].reshape(span * tall // DEPTH, DEPTH, channels)
    for c in OFFSETS:
        moved = shift_z(field, c).reshape(span, tall, channels)
        for b in OFFSETS:
            at = ((b + 1) * 3 + c + 1) * channels
            start = DEPTH * (b + 1)
            cols[:, :, at : at + channels] = moved[:, start : start + mid].astype(jnp.bfloat16)
    nine = 9 * channels
    pre = jnp.zeros(((width + 2) * mid, channels), f32)
    for a in range(3):
        pre += jnp.dot(
            cols[a : a + width + 2].reshape((width + 2) * mid, nine),
            weight[a * nine : (a + 1) * nine, :],
            preferred_element_type=f32,
        )
    sig = jax.nn.sigmoid(pre)
    act = (pre * sig).reshape(width + 2, mid, channels)[1 : 1 + width, DEPTH : DEPTH + rows]
    act_ref[...] = (act * live[:, :, 0:1]).astype(jnp.bfloat16)
    slope = (sig * (1.0 + pre * (1.0 - sig))).reshape(width + 2, mid, channels)
    beyond = jnp.concatenate(
        [
            lower[None, 2 * halo : 2 * halo + DEPTH],
            across[width * halo :].astype(f32).reshape(width, DEPTH, channels),
            upper[None, 2 * halo : 2 * halo + DEPTH],
        ],
        axis=0,
    )
    centre = jnp.concatenate([left[2:3], cot[...].astype(f32), right[2:3]], axis=0)
    full = jnp.concatenate([beyond * use_low, centre, beyond * use_high], axis=1)
    grad = full * slope
    gp_ref[...] = grad.astype(jnp.bfloat16)
    inner = grad[:, DEPTH : DEPTH + rows].astype(jnp.bfloat16)
    turned = lax.dot_general(
        pick[...],
        inner.reshape((width + 2) * rows, channels),
        (((1,), (1,)), ((), ())),
        preferred_element_type=f32,
    )
    slices[...] = turned.reshape(slices.shape).astype(jnp.bfloat16)
    group = slices.shape[1]
    chip = me - lax.rem(quad, 2) * SIDES
    for distance, ref in zip(CHIPS, slice_refs):
        ref[:group] = slices[chip ^ distance]
        ref[group:] = slices[(chip ^ distance) + SIDES]


def input_kernel(gp, live, turned, out_ref, cols, weight):
    width, rows, channels = out_ref.shape
    f32 = jnp.float32
    tall = rows + 2 * DEPTH
    for tap in range(27):
        weight[tap * channels : (tap + 1) * channels, :] = turned[
            :, tap * channels : (tap + 1) * channels
        ]
    field = gp[...].astype(f32).reshape((width + 2) * tall // DEPTH, DEPTH, channels)
    for c in OFFSETS:
        moved = shift_z(field, -c).reshape(width + 2, tall, channels)
        for b in OFFSETS:
            at = ((b + 1) * 3 + c + 1) * channels
            start = DEPTH * (1 - b)
            cols[:, :, at : at + channels] = moved[:, start : start + rows].astype(jnp.bfloat16)
    nine = 9 * channels
    total = jnp.zeros((width * rows, channels), f32)
    for a in range(3):
        total += jnp.dot(
            cols[2 - a : 2 - a + width].reshape(width * rows, nine),
            weight[a * nine : (a + 1) * nine, :],
            preferred_element_type=f32,
        )
    out_ref[...] = (total.reshape(width, rows, channels) * live[:, :, 0:1]).astype(jnp.bfloat16)


def kernel_grad_kernel(*refs):
    chips = len(CHIPS)
    received, bricks = refs[:chips], refs[chips : 2 * chips]
    keep_ref, send_ref, slices, cols, part, stage, masked, sems = refs[2 * chips :]
    f32 = jnp.float32
    group, lanes = received[0].shape
    blocks, per, lane, channels = masked.shape
    half = lane // 2
    _, _, quad, side = position()
    copies = []
    for i, distance in enumerate(CHIPS):
        to = stage.at[distance // 4, side ^ (distance % 2)]
        copies.append(pltpu.make_async_copy(bricks[i], to, sems.at[i]))
        copies[i].start()
        slices[distance // 4, side ^ (distance % 2)] = received[i][...]
    at = lax.broadcasted_iota(jnp.int32, (group, lane), 1)
    y, z = at // DEPTH, at % DEPTH
    tall = lane // DEPTH
    for block in range(blocks):
        first = slices[block, 0].astype(f32)
        second = slices[block, 1].astype(f32)
        for k in range(per + 2):
            one = first[:, k // 2 * lane : (k // 2 + 1) * lane]
            two = second[:, k // 2 * lane : (k // 2 + 1) * lane]
            if k % 2 == 0:
                base = jnp.where(at < half, one, pltpu.roll(two, half, 1))
            else:
                base = jnp.where(at < half, pltpu.roll(one, half, 1), two)
            pieces = []
            for b in OFFSETS:
                for c in OFFSETS:
                    step = (DEPTH * b + c) % lane
                    moved = base if step == 0 else pltpu.roll(base, step, 1)
                    keep = (y - b >= 0) & (y - b < tall) & (z - c >= 0) & (z - c < DEPTH)
                    pieces.append(jnp.where(keep, moved, 0.0))
            slab = block * (per + 2) + k
            cols[:, slab * lane : (slab + 1) * lane] = jnp.concatenate(pieces, axis=0).astype(
                jnp.bfloat16
            )
    for copy in copies:
        copy.wait()
    for block in range(blocks):
        for sided in range(SIDES):
            at_rows = pl.ds(sided * half, half)
            for x in range(per):
                shift = 64 * (x // (per // 2))
                rest = stage[block, sided, per + x % (per // 2)]
                masked[block, x, at_rows, :128] = stage[block, sided, x]
                masked[block, x, at_rows, 128:] = rest[:, shift : shift + 64]
    _, planes, eight, _ = part.shape
    for a in range(3):
        got = jnp.zeros((cols.shape[0], channels), f32)
        for block in range(blocks):
            start = (block * (per + 2) + 2 - a) * lane
            got += jnp.dot(
                cols[:, start : start + per * lane],
                masked[block].reshape(per * lane, channels),
                preferred_element_type=f32,
            )
        got = got.reshape(9, 2, planes, eight, channels)
        for core in range(2):
            for to in range(planes):
                part[core, to, :, a * 9 * channels : (a + 1) * 9 * channels] = jnp.concatenate(
                    [got[tap, core, to] for tap in range(9)], axis=1
                )
    core = lax.rem(quad, 2)
    keep_ref[...] = part[core]
    send_ref[...] = part[1 - core].astype(jnp.bfloat16)


def fold_kernel(keep, other, own_ref, *send_refs):
    plane = position()[0]
    own_ref[...] = keep[plane] + other[plane].astype(jnp.float32)
    for distance, ref in enumerate(send_refs, 1):
        to = plane ^ distance
        ref[...] = (keep[to] + other[to].astype(jnp.float32)).astype(jnp.bfloat16)


def sum_kernel(scale, own, one, two, three, out_ref):
    f32 = jnp.float32
    total = own[...] + one[...].astype(f32) + two[...].astype(f32) + three[...].astype(f32)
    out_ref[...] = (total * scale).astype(out_ref.dtype)


def join_kernel(mine, other, out_ref):
    share = out_ref.shape[0] // SIDES
    ahead = position()[3] == 0
    here, there = mine[...].astype(jnp.float32), other[...].astype(jnp.float32)
    first = jnp.where(ahead, here, there)
    second = jnp.where(ahead, there, here)
    out_ref[0:share] = first[:share]
    out_ref[share:] = second[:share]


def call(body, name, mebibytes, flops, moved, out_shape, scratch=(), in_specs=None):
    spec = pl.BlockSpec(memory_space=pltpu.VMEM)

    def run(*operands):
        return pl.pallas_call(
            body,
            out_shape=out_shape,
            in_specs=in_specs or [spec] * len(operands),
            out_specs=jax.tree.map(lambda _: spec, out_shape),
            scratch_shapes=scratch,
            compiler_params=pltpu.CompilerParams(vmem_limit_bytes=mebibytes << 20),
            cost_estimate=pl.CostEstimate(flops=flops, bytes_accessed=moved, transcendentals=0),
            name=name,
        )(*operands)

    return run


def planes_local(features, weight, voxel_mask, cotangent):
    bf16 = jnp.bfloat16
    f32 = jnp.float32
    array = jax.ShapeDtypeStruct
    width, wide_y, depth, channels = features.shape
    rows = wide_y * depth
    planes = lax.axis_size("depth")
    count = planes * QUAD
    total = 27 * channels
    halo = 2 * DEPTH
    span = (width + 2) * rows
    group = planes * 8

    def swap(piece, axes, distance, size):
        return lax.ppermute(piece, axes, [(i, i ^ distance) for i in range(size)])

    def in_plane(piece, distance):
        return swap(piece, ("quad", "narrow"), distance, MEMBERS)

    brick = array((width, rows, channels), bf16)
    slab = array((3, rows, channels), bf16)
    side_rows = array((width * (halo + DEPTH), channels), bf16)
    edge_rows = array((2 * halo + 2 * DEPTH, channels), bf16)
    pick = call(
        functools.partial(pick_kernel, planes), "pick", 4, 1 << 16, 1 << 16,
        array((MEMBERS * group, channels), bf16),
    )()
    vmem = pl.BlockSpec(memory_space=pltpu.VMEM)
    masked, cot, live, *halos = call(
        prepare_kernel, "prepare", 16, 1 << 20, 1 << 20,
        (brick, brick, array((width, rows, 128), f32), slab, slab, side_rows, edge_rows, edge_rows),
        (),
        [vmem] * 3 + [pl.BlockSpec(memory_space=pl.ANY)],
    )(
        features.reshape(width, rows, channels),
        cotangent.reshape(width, rows, channels),
        voxel_mask,
        pick,
    )
    pairs = [i ^ 1 for i in range(count)], [min(max(((i + 1) ^ 1) - 1, 0), count - 1) for i in range(count)]
    to_near, to_far = ([(i, j) for i, j in enumerate(pair)] for pair in pairs)
    near_across, far_across = (
        [(SIDES * i + s, SIDES * j + 1 - s) for i, j in pair for s in range(SIDES)]
        for pair in (to_near, to_far)
    )
    halos = [
        lax.ppermute(halos[0], WIDE, to_near),
        lax.ppermute(halos[1], WIDE, to_far),
        in_plane(halos[2], 1),
        lax.ppermute(halos[3], WIDE + ("narrow",), near_across),
        lax.ppermute(halos[4], WIDE + ("narrow",), far_across),
    ]
    weight_rows = call(
        turn_kernel, "turn", 8, 1 << 20, 4 << 20, array((total, channels), bf16)
    )(weight.T)
    packed = call(
        pack_kernel, "pack", 4, 1 << 16, 1 << 19,
        array((width * channels // 128, rows, 128), bf16),
    )(masked)
    packed, weight_rows, *halos = lax.optimization_barrier((packed, weight_rows, *halos))
    bricks = [packed] + [in_plane(packed, distance) for distance in CHIPS[1:]]

    mid = rows + 2 * DEPTH
    act, gp, *slices = call(
        forward_kernel, "forward", 28, 800 * 5184 * 256, 1 << 20,
        (brick, array((width + 2, mid, channels), bf16))
        + (array((2 * group, span), bf16),) * len(CHIPS),
        (
            pltpu.VMEM((width + 4, rows + 2 * halo, channels), f32),
            pltpu.VMEM((2,) + slab.shape, bf16),
            pltpu.VMEM((2,) + edge_rows.shape, bf16),
            pltpu.VMEM((width + 4, mid, 9 * channels), bf16),
            pltpu.VMEM((MEMBERS, group, span), bf16),
        ),
    )(masked, cot, *halos, live, weight_rows, pick)
    bricks[1], bricks[2], *slices = lax.optimization_barrier((bricks[1], bricks[2], *slices))
    slices = [slices[0]] + [in_plane(part, d) for part, d in zip(slices[1:], CHIPS[1:])]

    grad_input = call(
        input_kernel, "input_gradient", 20, 2 * 512 * 5184 * 256, 4 << 20, brick,
        (
            pltpu.VMEM((width + 2, rows, 9 * channels), bf16),
            pltpu.VMEM((total, channels), bf16),
        ),
    )(gp, live, weight.T)
    grad_input, *slices = lax.optimization_barrier((grad_input, *slices))

    blocks = QUAD // 2
    chips = len(CHIPS)
    keep, fold = call(
        kernel_grad_kernel, "kernel_gradient", 28, 2 * 576 * 3 * 2048 * 256, 4 << 20,
        (array((planes, 8, total), f32), array((planes, 8, total), bf16)),
        (
            pltpu.VMEM((blocks, SIDES, 2 * group, span), bf16),
            pltpu.VMEM((9 * 2 * group, blocks * (width + 2) * SIDES * rows), bf16),
            pltpu.VMEM((2, planes, 8, total), f32),
            pltpu.VMEM((blocks, SIDES) + packed.shape, bf16),
            pltpu.VMEM((blocks, width, SIDES * rows, channels), bf16),
            pltpu.SemaphoreType.DMA((chips,)),
        ),
        [vmem] * chips + [pl.BlockSpec(memory_space=pl.ANY)] * chips,
    )(*slices, *bricks)
    own, *sends = call(
        fold_kernel, "fold", 8, 8 * total * 4, 8 * total * 40,
        (array((8, total), f32),) + (array((8, total), bf16),) * (planes - 1),
    )(keep, in_plane(fold, 2))
    got = [swap(sent, "depth", d, planes) for d, sent in enumerate(sends, 1)]
    voxels = count * SIDES * width * rows
    mine = call(
        functools.partial(sum_kernel, float(1.0 / voxels**0.5)),
        "plane_sum", 4, 8 * total * 4, 8 * total * 14, array((8, total), bf16),
    )(own, *got)
    grad_weight = call(
        join_kernel, "join", 4, 8 * total, 8 * total * 14, array((channels // count, total), f32)
    )(mine, in_plane(mine, 1))
    shape = features.shape
    return act.reshape(shape), grad_input.reshape(shape), grad_weight


def padded_2(cells, sides, width):
    for axis, dim in sides:
        count = lax.axis_size(axis)
        ends = count - 1
        head = lax.slice_in_dim(cells, 0, width, axis=dim)
        tail = lax.slice_in_dim(cells, cells.shape[dim] - width, cells.shape[dim], axis=dim)
        cells = jnp.concatenate(
            [
                lax.ppermute(tail, axis, [(i, (i + 1) % count) for i in range(ends)]),
                cells,
                lax.ppermute(head, axis, [((i + 1) % count, i) for i in range(ends)]),
            ],
            axis=dim,
        )
    return cells


def gather_taps(padded, width_x, width_y, depth_z, channels, flip):
    pieces = []
    for shift_x in range(3):
        for shift_y in range(3):
            for shift_z in range(3):
                start_x = 2 - shift_x if flip else shift_x
                start_y = 2 - shift_y if flip else shift_y
                start_z = 2 - shift_z if flip else shift_z
                piece = padded[
                    start_x : start_x + width_x,
                    start_y : start_y + width_y,
                    start_z : start_z + depth_z,
                    :,
                ]
                pieces.append(piece.reshape(-1, channels))
    return jnp.concatenate(pieces, axis=1)


def summed_local(features, weight, voxel_mask, cotangent):
    width_x, width_y, depth_z, channels = features.shape
    masked = features * voxel_mask.astype(jnp.bfloat16)[..., None]
    padded = padded_2(masked, (("wide", 0), ("narrow", 1)), 1)
    padded = jnp.pad(padded, ((0, 0), (0, 0), (1, 1), (0, 0)))
    columns = gather_taps(padded, width_x, width_y, depth_z, channels, False)
    pre = jnp.dot(columns, weight, preferred_element_type=jnp.float32)
    live = voxel_mask.reshape(-1, 1).astype(jnp.float32)
    sig = jax.nn.sigmoid(pre)
    activation = (
        (pre * sig * live).astype(jnp.bfloat16).reshape(width_x, width_y, depth_z, channels)
    )
    slope = sig * (1.0 + pre * (1.0 - sig))
    grad_pre = (cotangent.reshape(-1, channels).astype(jnp.float32) * live * slope).astype(
        jnp.bfloat16
    )
    taps = weight.reshape(27, channels, channels)
    grid = grad_pre.reshape(width_x, width_y, depth_z, channels)
    grad_pad = padded_2(grid, (("wide", 0), ("narrow", 1)), 1)
    grad_pad = jnp.pad(grad_pad, ((0, 0), (0, 0), (1, 1), (0, 0)))
    grad_columns = gather_taps(grad_pad, width_x, width_y, depth_z, channels, True)
    flipped = jnp.transpose(taps, (0, 2, 1)).reshape(27 * channels, channels)
    grad_field = jnp.dot(grad_columns, flipped, preferred_element_type=jnp.float32)
    grad_input = (
        (grad_field * live).astype(jnp.bfloat16).reshape(width_x, width_y, depth_z, channels)
    )
    scale = 1.0 / jnp.sqrt(
        jnp.float32(width_x * width_y * depth_z * lax.axis_size("wide") * lax.axis_size("narrow"))
    )
    whole = lax.dot_general(
        grad_pre, columns, (((0,), (0,)), ((), ())), preferred_element_type=jnp.float32
    )
    piece_flat = lax.psum_scatter(
        whole.reshape(-1), ("wide", "narrow"), scatter_dimension=0, tiled=True
    )
    gathered = lax.all_gather(piece_flat, "narrow", axis=0, tiled=True)
    summed = gathered.reshape(channels // lax.axis_size("wide"), 27 * channels)
    grad_weight = summed * scale
    return (activation, grad_input, grad_weight)


def sharded(body, mesh, wide):
    return jax.shard_map(
        body,
        mesh=mesh,
        in_specs=(
            P(wide, "narrow", None, None),
            P(),
            P(wide, "narrow", None),
            P(wide, "narrow", None, None),
        ),
        out_specs=(
            P(wide, "narrow", None, None),
            P(wide, "narrow", None, None),
            P(wide, None),
        ),
        check_vma=False,
    )


def solution(mesh):
    wide, narrow = mesh.shape["wide"], mesh.shape["narrow"]
    if wide != 4 * QUAD or narrow != SIDES:
        return sharded(summed_local, mesh, "wide")
    planes = Mesh(
        mesh.devices.reshape(wide // QUAD, QUAD, narrow), ("depth", "quad", "narrow")
    )
    return sharded(planes_local, planes, WIDE)
```

time: 70.5 us -> 59.4 us (0.84)
  starting transfers between devices: 26 us -> 20.2 us
  waiting for transfers between devices: 25.8 us -> 20.1 us
    ppermute x20 -> x12, starting transfers between devices: 25.3 us -> 14.9 us  [swap(): return lax.ppermute(piece, axes, [(i, i ^ distance) for i in range(size)])]
    ppermute x20 -> x12, waiting for transfers between devices: 25.8 us -> 20.1 us  [swap(): return lax.ppermute(piece, axes, [(i, i ^ distance) for i in range(size)])]
    ppermute x1 -> x4, starting transfers between devices: 0.65 us -> 5.37 us  [the longest x1 2.68 us: planes_local(): lax.ppermute(halos[3], WIDE + ('narrow',), near_across)]
    pallas_call x9 -> x10, Pallas kernels: 13.5 us -> 13.8 us  [run(): pl.pallas_call(body, out_shape=out_shape, in_specs=in_specs or [spec] * l...]
    unnamed x12 -> x10, local copies, waits for them, and re-layouts: 4.22 us -> 4.22 us
  transfers between devices with their start and end apart: 21 -> 16, of which waited for: 11 -> 7; matrix products, arithmetic and copies ran while one was open for 0% -> 0% of each run, Pallas kernels for 10% -> 12%
where the time goes in v5:
time: 59.4 us; the launch traced here: 59.1 us
  starting transfers between devices  20.2 us (34%)
  waiting for transfers between devices  20.1 us (34%)
  Pallas kernels  13.8 us (23%)
  local copies, waits for them, and re-layouts  4.22 us (7%)
  between operations  0.76 us (1%)
    ppermute x12, waiting for transfers between devices, swap(): return lax.ppermute(piece, axes, [(i, i ^ distance) for i in range(size)])  20.1 us
    ppermute x12, starting transfers between devices, swap(): return lax.ppermute(piece, axes, [(i, i ^ distance) for i in range(size)])  14.9 us
    pallas_call x10, Pallas kernels, run(): pl.pallas_call(body, out_shape=out_shape, in_specs=in_specs or [spec] * l...  13.8 us
    unnamed x10, local copies, waits for them, and re-layouts  4.22 us
    ppermute x1, starting transfers between devices, planes_local(): lax.ppermute(halos[3], WIDE + ('narrow',), near_across)  2.68 us
    ppermute x1, starting transfers between devices, planes_local(): lax.ppermute(halos[4], WIDE + ('narrow',), far_across)  1.52 us
  transfers between devices with their start and end apart: 16, of which 7 were waited for; matrix products, arithmetic and copies ran while one was open for 0% of the time, Pallas kernels for 12%

profile of v5, /device:TPU:0, one launch (start us, length us, event | category | flops | bytes accessed | tf_op | source)
XLA Modules:
  0.0 59.1 jit_solution(9290022607795756176)
XLA Ops:
  0.6 0.1 pick.1.first
  0.7 0.0 copy-start.2
  0.7 0.9 %copy-done.2 = bf16[8,8,8,192]{3,2,1,0:T(8,128)(2,1)S(1)} copy-done((bf16[8,8,8,192]{3,2,1,0:T(8,128)(2,1)S(1)}, bf16[8,8,8,192]{3,2,1,0:T(8,128)(2,1)}, u32[]{:S(2)}) %copy-start.2) | copy-done | bytes 196632
  1.7 0.0 copy-start.3
  1.7 0.9 %copy-done.3 = bf16[8,8,8,192]{3,2,1,0:T(8,128)(2,1)S(1)} copy-done((bf16[8,8,8,192]{3,2,1,0:T(8,128)(2,1)S(1)}, bf16[8,8,8,192]{3,2,1,0:T(8,128)(2,1)}, u32[]{:S(2)}) %copy-start.3) | copy-done | bytes 196632
  2.6 0.0 copy-start.4
  2.6 0.8 %copy-done.4 = s32[8,8,8]{2,1,0:T(8,128)S(1)} copy-done((s32[8,8,8]{2,1,0:T(8,128)S(1)}, s32[8,8,8]{2,1,0:T(8,128)}, u32[]{:S(2)}) %copy-start.4) | copy-done | bytes 2072
  3.4 0.2 prepare.1
  3.6 0.5 collective-permute-start
  4.1 0.7 %collective-permute-start.1 = (bf16[3,64,192]{2,1,0:T(8,128)(2,1)S(1)}, bf16[3,64,192]{2,1,0:T(8,128)(2,1)S(1)}, u32[]{:S(2)}, u32[]{:S(2)}) collective-permute-start(bf16[3,64,192]{2,1,0:T(8,128)(2,1)S(1)} %get-tuple-element.44), channel_id=1, source_target_pairs={{0,0},{2,4},{4,2},{6,8},{8,6},{10,12},{12,10},{14,16},{16,14},{18,... | collective-permute-start | bytes 221192 | tf_op jit(solution)/shard_map/ppermute | solution.py:358
  4.8 2.6 %collective-permute-start.2 = (bf16[192,192]{1,0:T(8,128)(2,1)S(1)}, bf16[192,192]{1,0:T(8,128)(2,1)S(1)}, u32[]{:S(2)}, u32[]{:S(2)}) collective-permute-start(bf16[192,192]{1,0:T(8,128)(2,1)S(1)} %get-tuple-element.45), channel_id=1, source_target_pairs={{0,1},{1,0},{2,3},{3,2},{4,5},{5,4},{6,7},{7,6},{8,9},{9,8},{10,11... | collective-permute-start | bytes 221192 | tf_op jit(solution)/shard_map/ppermute | solution.py:325
  7.4 2.7 %collective-permute-start.3 = (bf16[48,192]{1,0:T(8,128)(2,1)S(1)}, bf16[48,192]{1,0:T(8,128)(2,1)S(1)}, u32[]{:S(2)}, u32[]{:S(2)}) collective-permute-start(bf16[48,192]{1,0:T(8,128)(2,1)S(1)} %get-tuple-element.46), channel_id=1, source_target_pairs={{0,3},{1,2},{2,1},{3,0},{4,7},{5,6},{6,5},{7,4},{8,11},{9,10},{10,... | collective-permute-start | bytes 55304 | tf_op jit(solution)/shard_map/ppermute | solution.py:360
  10.1 1.5 %collective-permute-start.4 = (bf16[48,192]{1,0:T(8,128)(2,1)S(1)}, bf16[48,192]{1,0:T(8,128)(2,1)S(1)}, u32[]{:S(2)}, u32[]{:S(2)}) collective-permute-start(bf16[48,192]{1,0:T(8,128)(2,1)S(1)} %get-tuple-element.47), channel_id=1, source_target_pairs={{0,1},{1,0},{2,5},{3,4},{4,3},{5,2},{6,9},{7,8},{8,7},{9,6},{10,13... | collective-permute-start | bytes 55304 | tf_op jit(solution)/shard_map/ppermute | solution.py:361
  11.6 0.1 pack.1.refs_4_
  11.7 0.0 copy-start
  11.7 1.6 %copy-done = bf16[5184,192]{0,1:T(8,128)(2,1)S(1)} copy-done((bf16[5184,192]{0,1:T(8,128)(2,1)S(1)}, bf16[5184,192]{0,1:T(8,128)(2,1)}, u32[]{:S(2)}) %copy-start) | copy-done | bytes 1990680
  13.2 0.8 %turn.1.weight = bf16[5184,192]{1,0:T(8,128)(2,1)S(1)} custom-call(bf16[192,5184]{1,0:T(8,128)(2,1)S(1)} %bitcast.5), custom_call_target="tpu_custom_call" | custom-call | flops 1048576 | bytes 4194304 | tf_op jit(solution)/shard_map/turn/pallas_call | solution.py:297
  14.0 0.0 copy-start.1
  14.0 0.0 collective-permute-done.3.near_across
  14.0 0.0 collective-permute-done.4.far_across
  14.1 0.0 collective-permute-done.near
  14.1 0.0 collective-permute-done.1.far
  14.1 0.0 collective-permute-done.2.across
  14.1 1.8 %collective-permute-start.6 = (bf16[12,64,128]{2,1,0:T(8,128)(2,1)S(1)}, bf16[12,64,128]{2,1,0:T(8,128)(2,1)S(1)}, u32[]{:S(2)}, u32[]{:S(2)}) collective-permute-start(bf16[12,64,128]{2,1,0:T(8,128)(2,1)S(1)} %pack.1.refs_4_), channel_id=1, source_target_pairs={{0,4},{1,5},{2,6},{3,7},{4,0},{5,1},{6,2},{7,3},{8,12},{9,13},{10,... | collective-permute-start | bytes 589832 | tf_op jit(solution)/shard_map/ppermute | solution.py:325
  15.8 1.5 %collective-permute-start.5 = (bf16[12,64,128]{2,1,0:T(8,128)(2,1)S(1)}, bf16[12,64,128]{2,1,0:T(8,128)(2,1)S(1)}, u32[]{:S(2)}, u32[]{:S(2)}) collective-permute-start(bf16[12,64,128]{2,1,0:T(8,128)(2,1)S(1)} %pack.1.refs_4_), channel_id=1, source_target_pairs={{0,1},{1,0},{2,3},{3,2},{4,5},{5,4},{6,7},{7,6},{8,9},{9,8},{10,11... | collective-permute-start | bytes 589832 | tf_op jit(solution)/shard_map/ppermute | solution.py:325
  17.4 0.3 collective-permute-start.10
  17.6 3.6 %forward.1 = (bf16[8,64,192]{2,1,0:T(8,128)(2,1)}, bf16[10,80,192]{2,1,0:T(8,128)(2,1)S(1)}, bf16[64,640]{1,0:T(8,128)(2,1)S(1)}, bf16[64,640]{1,0:T(8,128)(2,1)...) custom-call(bf16[8,64,192]{2,1,0:T(8,128)(2,1)S(1)} %get-tuple-element.41.masked, ...), custom_call_target="tpu_custom_call" | custom-call | flops 1061683200 | bytes 1048576 | tf_op jit(solution)/shard_map/forward/pallas_call | solution.py:297
  21.2 0.6 collective-permute-done.6.refs_6_
  21.8 5.7 %collective-permute-done.5.refs_5_ = bf16[12,64,128]{2,1,0:T(8,128)(2,1)S(1)} collective-permute-done((bf16[12,64,128]{2,1,0:T(8,128)(2,1)S(1)}, bf16[12,64,128]{2,1,0:T(8,128)(2,1)S(1)}, u32[]{:S(2)}, u32[]{:S(2)}) %collective-permute-start.5) | collective-permute-done | bytes 196640 | tf_op jit(solution)/shard_map/ppermute | solution.py:325
  27.5 1.3 %collective-permute-start.7 = (bf16[64,640]{1,0:T(8,128)(2,1)S(1)}, bf16[64,640]{1,0:T(8,128)(2,1)S(1)}, u32[]{:S(2)}, u32[]{:S(2)}) collective-permute-start(bf16[64,640]{1,0:T(8,128)(2,1)S(1)} %get-tuple-element.63), channel_id=1, source_target_pairs={{0,1},{1,0},{2,3},{3,2},{4,5},{5,4},{6,7},{7,6},{8,9},{9,8},{10,11... | collective-permute-start | bytes 245768 | tf_op jit(solution)/shard_map/ppermute | solution.py:325
  28.8 0.0 collective-permute-start.8
  28.8 2.2 %collective-permute-start.9 = (bf16[64,640]{1,0:T(8,128)(2,1)S(1)}, bf16[64,640]{1,0:T(8,128)(2,1)S(1)}, u32[]{:S(2)}, u32[]{:S(2)}) collective-permute-start(bf16[64,640]{1,0:T(8,128)(2,1)S(1)} %get-tuple-element.65), channel_id=1, source_target_pairs={{0,5},{1,4},{2,7},{3,6},{4,1},{5,0},{6,3},{7,2},{8,13},{9,12},{10,... | collective-permute-start | bytes 245768 | tf_op jit(solution)/shard_map/ppermute | solution.py:325
  31.0 0.0 copy-done.1
  31.0 2.6 %input_gradient.1 = bf16[8,64,192]{2,1,0:T(8,128)(2,1)} custom-call(bf16[10,80,192]{2,1,0:T(8,128)(2,1)S(1)} %get-tuple-element.56.gp, f32[8,64,128]{2,1,0:T(8,128)S(1)} %get-tuple-element.53.live, bf16[192,5184]{1,0:T(8,128)(2,1)S(1)} %bitcast.6), custom_call_target="tpu_custom_call" | custom-call | flops 1358954496 | bytes 4194304 | tf_op jit(solution)/shard_map/input_gradient/pallas_call | solution.py:297
  33.6 0.0 collective-permute-done.7.refs_1_
  33.6 0.0 collective-permute-done.8.refs_2_
  33.6 1.1 %collective-permute-done.9.refs_3_ = bf16[64,640]{1,0:T(8,128)(2,1)S(1)} collective-permute-done((bf16[64,640]{1,0:T(8,128)(2,1)S(1)}, bf16[64,640]{1,0:T(8,128)(2,1)S(1)}, u32[]{:S(2)}, u32[]{:S(2)}) %collective-permute-start.9) | collective-permute-done | bytes 81952 | tf_op jit(solution)/shard_map/ppermute | solution.py:325
  34.6 0.0 collective-permute-done.10.refs_7_
  34.6 5.6 %kernel_gradient.1 = (f32[4,8,5184]{2,1,0:T(8,128)S(1)}, bf16[4,8,5184]{2,1,0:T(8,128)(2,1)S(1)}) custom-call(bf16[64,640]{1,0:T(8,128)(2,1)S(1)} %get-tuple-element.67.refs_0_, bf16[64,640]{1,0:T(8,128)(2,1)S(1)} %collective-permute-done.7.refs_1_, bf16[64,640]{1,0:T(8,128)(2,1)S(1)} %collective-permute-done.8.refs_2_, ...), custom_call_target="tpu_custom_call" | custom-call | flops 1811939328 | bytes 4194304 | tf_op jit(solution)/shard_map/kernel_gradient/pallas_call | solution.py:297
  40.2 0.1 collective-permute-start.11
  40.3 1.6 %collective-permute-done.11.other = bf16[4,8,5184]{2,1,0:T(8,128)(2,1)S(1)} collective-permute-done((bf16[4,8,5184]{2,1,0:T(8,128)(2,1)S(1)}, bf16[4,8,5184]{2,1,0:T(8,128)(2,1)S(1)}, u32[]{:S(2)}, u32[]{:S(2)}) %collective-permute-start.11) | collective-permute-done | bytes 331808 | tf_op jit(solution)/shard_map/ppermute | solution.py:325
  41.9 0.1 fold.1
  42.0 2.2 %collective-permute-start.12 = (bf16[8,5184]{1,0:T(8,128)(2,1)S(1)}, bf16[8,5184]{1,0:T(8,128)(2,1)S(1)}, u32[]{:S(2)}, u32[]{:S(2)}) collective-permute-start(bf16[8,5184]{1,0:T(8,128)(2,1)S(1)} %get-tuple-element.76), channel_id=1, source_target_pairs={{0,8},{8,0},{16,24},{24,16},{1,9},{9,1},{17,25},{25,17},{2,10},{10... | collective-permute-start | bytes 248840 | tf_op jit(solution)/shard_map/ppermute | solution.py:325
  44.1 2.4 %collective-permute-start.13 = (bf16[8,5184]{1,0:T(8,128)(2,1)S(1)}, bf16[8,5184]{1,0:T(8,128)(2,1)S(1)}, u32[]{:S(2)}, u32[]{:S(2)}) collective-permute-start(bf16[8,5184]{1,0:T(8,128)(2,1)S(1)} %get-tuple-element.77), channel_id=1, source_target_pairs={{0,16},{8,24},{16,0},{24,8},{1,17},{9,25},{17,1},{25,9},{2,18},{10... | collective-permute-start | bytes 248840 | tf_op jit(solution)/shard_map/ppermute | solution.py:325
  46.5 0.1 collective-permute-start.14
  46.6 0.3 collective-permute-done.12.one
  46.9 6.8 %collective-permute-done.13.two = bf16[8,5184]{1,0:T(8,128)(2,1)S(1)} collective-permute-done((bf16[8,5184]{1,0:T(8,128)(2,1)S(1)}, bf16[8,5184]{1,0:T(8,128)(2,1)S(1)}, u32[]{:S(2)}, u32[]{:S(2)}) %collective-permute-start.13) | collective-permute-done | bytes 82976 | tf_op jit(solution)/shard_map/ppermute | solution.py:325
  53.8 0.0 collective-permute-done.14.three
  53.8 0.1 plane_sum.1.mine
  53.8 0.5 collective-permute-start.15
  54.4 4.0 %collective-permute-done.15.other = bf16[8,5184]{1,0:T(8,128)(2,1)S(1)} collective-permute-done((bf16[8,5184]{1,0:T(8,128)(2,1)S(1)}, bf16[8,5184]{1,0:T(8,128)(2,1)S(1)}, u32[]{:S(2)}, u32[]{:S(2)}) %collective-permute-start.15) | collective-permute-done | bytes 82976 | tf_op jit(solution)/shard_map/ppermute | solution.py:325
  58.4 0.8 %join.1 = f32[12,5184]{1,0:T(8,128)} custom-call(bf16[8,5184]{1,0:T(8,128)(2,1)S(1)} %plane_sum.1.mine, bf16[8,5184]{1,0:T(8,128)(2,1)S(1)} %collective-permute-done.15.other), custom_call_target="tpu_custom_call" | custom-call | flops 41472 | bytes 580608 | tf_op jit(solution)/shard_map/join/pallas_call | solution.py:297
Async XLA Ops:
  0.7 1.0 %copy-start.2 = (bf16[8,8,8,192]{3,2,1,0:T(8,128)(2,1)S(1)}, bf16[8,8,8,192]{3,2,1,0:T(8,128)(2,1)}, u32[]{:S(2)}) copy-start(bf16[8,8,8,192]{3,2,1,0:T(8,128)(2,1)} %param.4) | copy-start | bytes 589828
  1.7 0.9 %copy-start.3 = (bf16[8,8,8,192]{3,2,1,0:T(8,128)(2,1)S(1)}, bf16[8,8,8,192]{3,2,1,0:T(8,128)(2,1)}, u32[]{:S(2)}) copy-start(bf16[8,8,8,192]{3,2,1,0:T(8,128)(2,1)} %param.7) | copy-start | bytes 589828
  2.6 0.8 %copy-start.4 = (s32[8,8,8]{2,1,0:T(8,128)S(1)}, s32[8,8,8]{2,1,0:T(8,128)}, u32[]{:S(2)}) copy-start(s32[8,8,8]{2,1,0:T(8,128)} %mask.1) | copy-start | bytes 6148
  3.6 10.5 %collective-permute-start = (bf16[3,64,192]{2,1,0:T(8,128)(2,1)S(1)}, bf16[3,64,192]{2,1,0:T(8,128)(2,1)S(1)}, u32[]{:S(2)}, u32[]{:S(2)}) collective-permute-start(bf16[3,64,192]{2,1,0:T(8,128)(2,1)S(1)} %get-tuple-element.43), channel_id=1, source_target_pairs={{0,2},{2,0},{4,6},{6,4},{8,10},{10,8},{12,14},{14,12},{16,18},{18,... | collective-permute-start | bytes 221192 | tf_op jit(solution)/shard_map/ppermute | solution.py:357
  4.1 9.9 %collective-permute-start.1 = (bf16[3,64,192]{2,1,0:T(8,128)(2,1)S(1)}, bf16[3,64,192]{2,1,0:T(8,128)(2,1)S(1)}, u32[]{:S(2)}, u32[]{:S(2)}) collective-permute-start(bf16[3,64,192]{2,1,0:T(8,128)(2,1)S(1)} %get-tuple-element.44), channel_id=1, source_target_pairs={{0,0},{2,4},{4,2},{6,8},{8,6},{10,12},{12,10},{14,16},{16,14},{18,... | collective-permute-start | bytes 221192 | tf_op jit(solution)/shard_map/ppermute | solution.py:358
  4.8 9.3 %collective-permute-start.2 = (bf16[192,192]{1,0:T(8,128)(2,1)S(1)}, bf16[192,192]{1,0:T(8,128)(2,1)S(1)}, u32[]{:S(2)}, u32[]{:S(2)}) collective-permute-start(bf16[192,192]{1,0:T(8,128)(2,1)S(1)} %get-tuple-element.45), channel_id=1, source_target_pairs={{0,1},{1,0},{2,3},{3,2},{4,5},{5,4},{6,7},{7,6},{8,9},{9,8},{10,11... | collective-permute-start | bytes 221192 | tf_op jit(solution)/shard_map/ppermute | solution.py:325
  7.4 6.7 %collective-permute-start.3 = (bf16[48,192]{1,0:T(8,128)(2,1)S(1)}, bf16[48,192]{1,0:T(8,128)(2,1)S(1)}, u32[]{:S(2)}, u32[]{:S(2)}) collective-permute-start(bf16[48,192]{1,0:T(8,128)(2,1)S(1)} %get-tuple-element.46), channel_id=1, source_target_pairs={{0,3},{1,2},{2,1},{3,0},{4,7},{5,6},{6,5},{7,4},{8,11},{9,10},{10,... | collective-permute-start | bytes 55304 | tf_op jit(solution)/shard_map/ppermute | solution.py:360
  10.1 4.0 %collective-permute-start.4 = (bf16[48,192]{1,0:T(8,128)(2,1)S(1)}, bf16[48,192]{1,0:T(8,128)(2,1)S(1)}, u32[]{:S(2)}, u32[]{:S(2)}) collective-permute-start(bf16[48,192]{1,0:T(8,128)(2,1)S(1)} %get-tuple-element.47), channel_id=1, source_target_pairs={{0,1},{1,0},{2,5},{3,4},{4,3},{5,2},{6,9},{7,8},{8,7},{9,6},{10,13... | collective-permute-start | bytes 55304 | tf_op jit(solution)/shard_map/ppermute | solution.py:361
  11.7 1.6 %copy-start = (bf16[5184,192]{0,1:T(8,128)(2,1)S(1)}, bf16[5184,192]{0,1:T(8,128)(2,1)}, u32[]{:S(2)}) copy-start(bf16[5184,192]{0,1:T(8,128)(2,1)} %param.5) | copy-start | bytes 5971972
  14.0 17.0 %copy-start.1 = (bf16[5184,192]{0,1:T(8,128)(2,1)S(1)}, bf16[5184,192]{0,1:T(8,128)(2,1)}, u32[]{:S(2)}) copy-start(bf16[5184,192]{0,1:T(8,128)(2,1)} %param.5) | copy-start | bytes 5971972
  14.1 7.7 %collective-permute-start.6 = (bf16[12,64,128]{2,1,0:T(8,128)(2,1)S(1)}, bf16[12,64,128]{2,1,0:T(8,128)(2,1)S(1)}, u32[]{:S(2)}, u32[]{:S(2)}) collective-permute-start(bf16[12,64,128]{2,1,0:T(8,128)(2,1)S(1)} %pack.1.refs_4_), channel_id=1, source_target_pairs={{0,4},{1,5},{2,6},{3,7},{4,0},{5,1},{6,2},{7,3},{8,12},{9,13},{10,... | collective-permute-start | bytes 589832 | tf_op jit(solution)/shard_map/ppermute | solution.py:325
  15.8 11.6 %collective-permute-start.5 = (bf16[12,64,128]{2,1,0:T(8,128)(2,1)S(1)}, bf16[12,64,128]{2,1,0:T(8,128)(2,1)S(1)}, u32[]{:S(2)}, u32[]{:S(2)}) collective-permute-start(bf16[12,64,128]{2,1,0:T(8,128)(2,1)S(1)} %pack.1.refs_4_), channel_id=1, source_target_pairs={{0,1},{1,0},{2,3},{3,2},{4,5},{5,4},{6,7},{7,6},{8,9},{9,8},{10,11... | collective-permute-start | bytes 589832 | tf_op jit(solution)/shard_map/ppermute | solution.py:325
  17.4 17.3 %collective-permute-start.10 = (bf16[12,64,128]{2,1,0:T(8,128)(2,1)S(1)}, bf16[12,64,128]{2,1,0:T(8,128)(2,1)S(1)}, u32[]{:S(2)}, u32[]{:S(2)}) collective-permute-start(bf16[12,64,128]{2,1,0:T(8,128)(2,1)S(1)} %pack.1.refs_4_), channel_id=1, source_target_pairs={{0,5},{1,4},{2,7},{3,6},{4,1},{5,0},{6,3},{7,2},{8,13},{9,12},{10,... | collective-permute-start | bytes 589832 | tf_op jit(solution)/shard_map/ppermute | solution.py:325
  27.5 6.1 %collective-permute-start.7 = (bf16[64,640]{1,0:T(8,128)(2,1)S(1)}, bf16[64,640]{1,0:T(8,128)(2,1)S(1)}, u32[]{:S(2)}, u32[]{:S(2)}) collective-permute-start(bf16[64,640]{1,0:T(8,128)(2,1)S(1)} %get-tuple-element.63), channel_id=1, source_target_pairs={{0,1},{1,0},{2,3},{3,2},{4,5},{5,4},{6,7},{7,6},{8,9},{9,8},{10,11... | collective-permute-start | bytes 245768 | tf_op jit(solution)/shard_map/ppermute | solution.py:325
  28.8 4.8 %collective-permute-start.8 = (bf16[64,640]{1,0:T(8,128)(2,1)S(1)}, bf16[64,640]{1,0:T(8,128)(2,1)S(1)}, u32[]{:S(2)}, u32[]{:S(2)}) collective-permute-start(bf16[64,640]{1,0:T(8,128)(2,1)S(1)} %get-tuple-element.64), channel_id=1, source_target_pairs={{0,4},{1,5},{2,6},{3,7},{4,0},{5,1},{6,2},{7,3},{8,12},{9,13},{10,... | collective-permute-start | bytes 245768 | tf_op jit(solution)/shard_map/ppermute | solution.py:325
  28.8 5.9 %collective-permute-start.9 = (bf16[64,640]{1,0:T(8,128)(2,1)S(1)}, bf16[64,640]{1,0:T(8,128)(2,1)S(1)}, u32[]{:S(2)}, u32[]{:S(2)}) collective-permute-start(bf16[64,640]{1,0:T(8,128)(2,1)S(1)} %get-tuple-element.65), channel_id=1, source_target_pairs={{0,5},{1,4},{2,7},{3,6},{4,1},{5,0},{6,3},{7,2},{8,13},{9,12},{10,... | collective-permute-start | bytes 245768 | tf_op jit(solution)/shard_map/ppermute | solution.py:325
  40.2 1.7 %collective-permute-start.11 = (bf16[4,8,5184]{2,1,0:T(8,128)(2,1)S(1)}, bf16[4,8,5184]{2,1,0:T(8,128)(2,1)S(1)}, u32[]{:S(2)}, u32[]{:S(2)}) collective-permute-start(bf16[4,8,5184]{2,1,0:T(8,128)(2,1)S(1)} %get-tuple-element.74), channel_id=1, source_target_pairs={{0,2},{1,3},{2,0},{3,1},{4,6},{5,7},{6,4},{7,5},{8,10},{9,11},{10,... | collective-permute-start | bytes 995336 | tf_op jit(solution)/shard_map/ppermute | solution.py:325
  42.0 4.9 %collective-permute-start.12 = (bf16[8,5184]{1,0:T(8,128)(2,1)S(1)}, bf16[8,5184]{1,0:T(8,128)(2,1)S(1)}, u32[]{:S(2)}, u32[]{:S(2)}) collective-permute-start(bf16[8,5184]{1,0:T(8,128)(2,1)S(1)} %get-tuple-element.76), channel_id=1, source_target_pairs={{0,8},{8,0},{16,24},{24,16},{1,9},{9,1},{17,25},{25,17},{2,10},{10... | collective-permute-start | bytes 248840 | tf_op jit(solution)/shard_map/ppermute | solution.py:325
  44.1 9.6 %collective-permute-start.13 = (bf16[8,5184]{1,0:T(8,128)(2,1)S(1)}, bf16[8,5184]{1,0:T(8,128)(2,1)S(1)}, u32[]{:S(2)}, u32[]{:S(2)}) collective-permute-start(bf16[8,5184]{1,0:T(8,128)(2,1)S(1)} %get-tuple-element.77), channel_id=1, source_target_pairs={{0,16},{8,24},{16,0},{24,8},{1,17},{9,25},{17,1},{25,9},{2,18},{10... | collective-permute-start | bytes 248840 | tf_op jit(solution)/shard_map/ppermute | solution.py:325
  46.5 7.2 %collective-permute-start.14 = (bf16[8,5184]{1,0:T(8,128)(2,1)S(1)}, bf16[8,5184]{1,0:T(8,128)(2,1)S(1)}, u32[]{:S(2)}, u32[]{:S(2)}) collective-permute-start(bf16[8,5184]{1,0:T(8,128)(2,1)S(1)} %get-tuple-element.78), channel_id=1, source_target_pairs={{0,24},{8,16},{16,8},{24,0},{1,25},{9,17},{17,9},{25,1},{2,26},{10... | collective-permute-start | bytes 248840 | tf_op jit(solution)/shard_map/ppermute | solution.py:325
  53.8 4.5 %collective-permute-start.15 = (bf16[8,5184]{1,0:T(8,128)(2,1)S(1)}, bf16[8,5184]{1,0:T(8,128)(2,1)S(1)}, u32[]{:S(2)}, u32[]{:S(2)}) collective-permute-start(bf16[8,5184]{1,0:T(8,128)(2,1)S(1)} %plane_sum.1.mine), channel_id=1, source_target_pairs={{0,1},{1,0},{2,3},{3,2},{4,5},{5,4},{6,7},{7,6},{8,9},{9,8},{10,11... | collective-permute-start | bytes 248840 | tf_op jit(solution)/shard_map/ppermute | solution.py:325

commit v6 on v5

--- a/solution.py
+++ b/solution.py
@@ -42,44 +42,49 @@
     out_ref[...] = jnp.where((row < share) & (channel == column), 1.0, 0.0).astype(jnp.bfloat16)
 
 
-def prepare_kernel(
-    features, cot, mask, first, masked_ref, cot_ref, live_ref,
-    near_ref, far_ref, across_ref, near_across_ref, far_across_ref,
-):
+def prepare_kernel(features, cot, mask, first, masked_ref, cot_ref, live_ref, near_ref, far_ref):
     width, rows, channels = features.shape
     f32 = jnp.float32
-    bf16 = jnp.bfloat16
     flat = mask[...].astype(f32).reshape(width * rows // DEPTH, DEPTH)
     live = jnp.broadcast_to(flat[:, :, None], flat.shape + (channels,)).reshape(features.shape)
     live_ref[...] = live[:, :, :128]
-    masked = features[...].astype(f32) * live
-    masked_ref[...] = masked.astype(bf16)
-    grown = cot[...].astype(f32) * live
-    cot_ref[...] = grown.astype(bf16)
-    _, _, quad, side = position()
-    odd = lax.rem(quad, 2)
-    ahead = side == 0
-    halo = 2 * DEPTH
-    strip = jnp.where(ahead, masked[:, rows - halo :], masked[:, :halo])
-    cots = jnp.where(ahead, grown[:, rows - DEPTH :], grown[:, :DEPTH])
-    across_ref[: width * halo] = strip.reshape(-1, channels).astype(bf16)
-    across_ref[width * halo :] = cots.reshape(-1, channels).astype(bf16)
-    blank = jnp.zeros((DEPTH, channels), f32)
-    corners = [
-        jnp.concatenate([strip[x : x + 2].reshape(-1, channels), cots[y], blank], axis=0)
-        for x, y in ((0, 0), (width - 2, width - 1))
-    ]
-    for upper, ref, corner_ref in ((1 - odd, near_ref, near_across_ref), (odd, far_ref, far_across_ref)):
+    masked_ref[...] = (features[...].astype(f32) * live).astype(jnp.bfloat16)
+    cot_ref[...] = (cot[...].astype(f32) * live).astype(jnp.bfloat16)
+    odd = lax.rem(position()[2], 2)
+    for ref, upper in ((near_ref, 1 - odd), (far_ref, odd)):
         ref[0:2] = masked_ref[pl.ds(upper * (width - 2), 2)]
         ref[2:3] = cot_ref[pl.ds(upper * (width - 1), 1)]
-        corner_ref[...] = jnp.where(upper == 1, corners[1], corners[0]).astype(bf16)
-
-
-def pack_kernel(masked, packed_ref):
-    width = masked.shape[0]
+
+
+def pack_kernel(masked, cot, packed_ref, across_ref):
+    width, rows, channels = masked.shape
     half = width // 2
     packed_ref[:width] = masked[:, :, :128]
     packed_ref[width:] = jnp.concatenate([masked[:half, :, 128:], masked[half:, :, 128:]], axis=2)
+    count = packed_ref.shape[0]
+    across_ref[:count] = packed_ref[...]
+    ahead = position()[3] == 0
+    grown = cot[...].astype(jnp.float32)
+    strip = jnp.where(ahead, grown[:, rows - DEPTH :], grown[:, :DEPTH])
+    strip = strip.reshape(width * DEPTH, channels)
+    rest = jnp.concatenate([strip[:, 128:], jnp.zeros_like(strip[:, 128:])], axis=1)
+    across_ref[count] = strip[:, :128].astype(jnp.bfloat16)
+    across_ref[count + 1] = rest.astype(jnp.bfloat16)
+
+
+def corner_kernel(near, far, out_ref, edge):
+    _, rows, channels = near.shape
+    _, _, quad, side = position()
+    odd = lax.rem(quad, 2)
+    edge[odd] = far[...]
+    edge[1 - odd] = near[...]
+    halo = 2 * DEPTH
+    ahead = side == 0
+    held = edge[...].astype(jnp.float32)
+    strip = jnp.where(ahead, held[:, :2, rows - halo :], held[:, :2, :halo])
+    cots = jnp.where(ahead, held[:, 2, rows - DEPTH :], held[:, 2, :DEPTH])
+    out_ref[: 4 * halo] = strip.reshape(4 * halo, channels).astype(jnp.bfloat16)
+    out_ref[4 * halo :] = cots.reshape(2 * DEPTH, channels).astype(jnp.bfloat16)
 
 
 def turn_kernel(weight, out_ref):
@@ -91,11 +96,11 @@
 
 
 def forward_kernel(
-    masked, cot, near, far, across, near_across, far_across, live, weight, pick, *refs
+    masked, cot, near, far, across, corner, live, weight, pick, *refs
 ):
     act_ref, gp_ref = refs[:2]
     slice_refs = refs[2 : 2 + len(CHIPS)]
-    ext, edge, corner, cols, slices = refs[2 + len(CHIPS) :]
+    ext, edge, cols, slices = refs[2 + len(CHIPS) :]
     width, rows, channels = masked.shape
     f32 = jnp.float32
     plane, me, quad, side = position()
@@ -111,19 +116,24 @@
     odd = lax.rem(quad, 2)
     edge[odd] = far[...]
     edge[1 - odd] = near[...]
-    corner[odd] = far_across[...]
-    corner[1 - odd] = near_across[...]
     left, right = edge[0].astype(f32) * use_left, edge[1].astype(f32) * use_right
-    lower, upper = corner[0].astype(f32) * use_left, corner[1].astype(f32) * use_right
+    corners = corner[: 4 * halo].astype(f32).reshape(2, 2, halo, channels)
+    lower, upper = corners[0] * use_left, corners[1] * use_right
+    ends = corner[4 * halo :].astype(f32).reshape(2, 1, DEPTH, channels)
     ext[0:2, halo : halo + rows, :] = left[0:2]
     ext[2 : 2 + width, halo : halo + rows, :] = masked[...].astype(f32)
     ext[2 + width :, halo : halo + rows, :] = right[0:2]
-    beside = across[: width * halo].astype(f32).reshape(width, halo, channels)
+    half = width // 2
+    ahead = side == 0
+    held = across[...].astype(f32)
+    brick = jnp.where(ahead, held[: width + half, :halo], held[: width + half, rows - halo :])
+    rest = jnp.concatenate([brick[width:, :, :64], brick[width:, :, 64:]], axis=0)
+    beside = jnp.concatenate([brick[:width], rest], axis=2)
     for use, start in ((use_low, 0), (use_high, halo + rows)):
         at = slice(start, start + halo)
-        ext[0:2, at, :] = lower[: 2 * halo].reshape(2, halo, channels) * use
+        ext[0:2, at, :] = lower * use
         ext[2 : 2 + width, at, :] = beside * use
-        ext[2 + width :, at, :] = upper[: 2 * halo].reshape(2, halo, channels) * use
+        ext[2 + width :, at, :] = upper * use
     field = ext[...].reshape(span * tall // DEPTH, DEPTH, channels)
     for c in OFFSETS:
         moved = shift_z(field, c).reshape(span, tall, channels)
@@ -145,9 +155,11 @@
     slope = (sig * (1.0 + pre * (1.0 - sig))).reshape(width + 2, mid, channels)
     beyond = jnp.concatenate(
         [
-            lower[None, 2 * halo : 2 * halo + DEPTH],
-            across[width * halo :].astype(f32).reshape(width, DEPTH, channels),
-            upper[None, 2 * halo : 2 * halo + DEPTH],
+            ends[0] * use_left,
+            jnp.concatenate([held[width + half], held[width + half + 1, :, :64]], axis=1).reshape(
+                width, DEPTH, channels
+            ),
+            ends[1] * use_right,
         ],
         axis=0,
     )
@@ -208,7 +220,8 @@
     copies = []
     for i, distance in enumerate(CHIPS):
         to = stage.at[distance // 4, side ^ (distance % 2)]
-        copies.append(pltpu.make_async_copy(bricks[i], to, sems.at[i]))
+        packed = bricks[i].at[pl.ds(0, stage.shape[2])]
+        copies.append(pltpu.make_async_copy(packed, to, sems.at[i]))
         copies[i].start()
         slices[distance // 4, side ^ (distance % 2)] = received[i][...]
     at = lax.broadcasted_iota(jnp.int32, (group, lane), 1)
@@ -329,16 +342,14 @@
 
     brick = array((width, rows, channels), bf16)
     slab = array((3, rows, channels), bf16)
-    side_rows = array((width * (halo + DEPTH), channels), bf16)
-    edge_rows = array((2 * halo + 2 * DEPTH, channels), bf16)
     pick = call(
         functools.partial(pick_kernel, planes), "pick", 4, 1 << 16, 1 << 16,
         array((MEMBERS * group, channels), bf16),
     )()
     vmem = pl.BlockSpec(memory_space=pltpu.VMEM)
-    masked, cot, live, *halos = call(
+    masked, cot, live, near, far = call(
         prepare_kernel, "prepare", 16, 1 << 20, 1 << 20,
-        (brick, brick, array((width, rows, 128), f32), slab, slab, side_rows, edge_rows, edge_rows),
+        (brick, brick, array((width, rows, 128), f32), slab, slab),
         (),
         [vmem] * 3 + [pl.BlockSpec(memory_space=pl.ANY)],
     )(
@@ -347,28 +358,27 @@
         voxel_mask,
         pick,
     )
-    pairs = [i ^ 1 for i in range(count)], [min(max(((i + 1) ^ 1) - 1, 0), count - 1) for i in range(count)]
-    to_near, to_far = ([(i, j) for i, j in enumerate(pair)] for pair in pairs)
-    near_across, far_across = (
-        [(SIDES * i + s, SIDES * j + 1 - s) for i, j in pair for s in range(SIDES)]
-        for pair in (to_near, to_far)
-    )
-    halos = [
-        lax.ppermute(halos[0], WIDE, to_near),
-        lax.ppermute(halos[1], WIDE, to_far),
-        in_plane(halos[2], 1),
-        lax.ppermute(halos[3], WIDE + ("narrow",), near_across),
-        lax.ppermute(halos[4], WIDE + ("narrow",), far_across),
-    ]
+    near = swap(near, WIDE, 1, count)
+    ends = [min(max(((i + 1) ^ 1) - 1, 0), count - 1) for i in range(count)]
+    far = lax.ppermute(far, WIDE, list(enumerate(ends)))
     weight_rows = call(
         turn_kernel, "turn", 8, 1 << 20, 4 << 20, array((total, channels), bf16)
     )(weight.T)
-    packed = call(
+    slabs = width * channels // 128
+    packed, across = call(
         pack_kernel, "pack", 4, 1 << 16, 1 << 19,
-        array((width * channels // 128, rows, 128), bf16),
-    )(masked)
-    packed, weight_rows, *halos = lax.optimization_barrier((packed, weight_rows, *halos))
-    bricks = [packed] + [in_plane(packed, distance) for distance in CHIPS[1:]]
+        (array((slabs, rows, 128), bf16), array((slabs + 2, rows, 128), bf16)),
+    )(masked, cot)
+    across = in_plane(across, CHIPS[1])
+    bricks = [packed, across, in_plane(packed, CHIPS[2]), None]
+    packed, near, far = lax.optimization_barrier((packed, near, far))
+    corner = call(
+        corner_kernel, "corner", 4, 1 << 16, 1 << 18,
+        array((4 * halo + 2 * DEPTH, channels), bf16),
+        (pltpu.VMEM((2,) + slab.shape, bf16),),
+    )(near, far)
+    corner = in_plane(corner, 1)
+    bricks[3] = in_plane(packed, CHIPS[3])
 
     mid = rows + 2 * DEPTH
     act, gp, *slices = call(
@@ -378,12 +388,10 @@
         (
             pltpu.VMEM((width + 4, rows + 2 * halo, channels), f32),
             pltpu.VMEM((2,) + slab.shape, bf16),
-            pltpu.VMEM((2,) + edge_rows.shape, bf16),
             pltpu.VMEM((width + 4, mid, 9 * channels), bf16),
             pltpu.VMEM((MEMBERS, group, span), bf16),
         ),
-    )(masked, cot, *halos, live, weight_rows, pick)
-    bricks[1], bricks[2], *slices = lax.optimization_barrier((bricks[1], bricks[2], *slices))
+    )(masked, cot, near, far, bricks[1], corner, live, weight_rows, pick)
     slices = [slices[0]] + [in_plane(part, d) for part, d in zip(slices[1:], CHIPS[1:])]
 
     grad_input = call(

time: 59.4 us -> 54.7 us (0.921)
  waiting for transfers between devices: 20.1 us -> 14.8 us
    ppermute x12 -> x13, waiting for transfers between devices: 20.1 us -> 14.8 us  [swap(): return lax.ppermute(piece, axes, [(i, i ^ distance) for i in range(size)])]
    ppermute x12 -> x13, starting transfers between devices: 14.9 us -> 20.1 us  [swap(): return lax.ppermute(piece, axes, [(i, i ^ distance) for i in range(size)])]
    ppermute x4 -> x1, starting transfers between devices: 5.37 us -> 0.66 us  [planes_local(): far = lax.ppermute(far, WIDE, list(enumerate(ends)))]
    pallas_call x10 -> x11, Pallas kernels: 13.8 us -> 13.9 us  [run(): pl.pallas_call(body, out_shape=out_shape, in_specs=in_specs or [spec] * l...]
  transfers between devices with their start and end apart: 16 -> 14, of which waited for: 7 -> 6; matrix products, arithmetic and copies ran while one was open for 0% -> 0% of each run, Pallas kernels for 12% -> 13%
where the time goes in v6:
time: 54.7 us; the launch traced here: 54.4 us
  starting transfers between devices  20.7 us (38%)
  waiting for transfers between devices  14.8 us (27%)
  Pallas kernels  13.9 us (25%)
  local copies, waits for them, and re-layouts  4.22 us (8%)
  between operations  0.72 us (1%)
    ppermute x13, starting transfers between devices, swap(): return lax.ppermute(piece, axes, [(i, i ^ distance) for i in range(size)])  20.1 us
    ppermute x13, waiting for transfers between devices, swap(): return lax.ppermute(piece, axes, [(i, i ^ distance) for i in range(size)])  14.8 us
    pallas_call x11, Pallas kernels, run(): pl.pallas_call(body, out_shape=out_shape, in_specs=in_specs or [spec] * l...  13.9 us
    unnamed x10, local copies, waits for them, and re-layouts  4.22 us
  transfers between devices with their start and end apart: 14, of which 6 were waited for; matrix products, arithmetic and copies ran while one was open for 0% of the time, Pallas kernels for 13%

profile of v6, /device:TPU:0, one launch (start us, length us, event | category | flops | bytes accessed | tf_op | source)
XLA Modules:
  0.0 54.4 jit_solution(834507067204782841)
XLA Ops:
  0.6 0.1 pick.1.first
  0.7 0.0 copy-start.2
  0.7 0.9 %copy-done.2 = bf16[8,8,8,192]{3,2,1,0:T(8,128)(2,1)S(1)} copy-done((bf16[8,8,8,192]{3,2,1,0:T(8,128)(2,1)S(1)}, bf16[8,8,8,192]{3,2,1,0:T(8,128)(2,1)}, u32[]{:S(2)}) %copy-start.2) | copy-done | bytes 196632
  1.7 0.0 copy-start.3
  1.7 0.9 %copy-done.3 = bf16[8,8,8,192]{3,2,1,0:T(8,128)(2,1)S(1)} copy-done((bf16[8,8,8,192]{3,2,1,0:T(8,128)(2,1)S(1)}, bf16[8,8,8,192]{3,2,1,0:T(8,128)(2,1)}, u32[]{:S(2)}) %copy-start.3) | copy-done | bytes 196632
  2.6 0.0 copy-start.4
  2.6 0.8 %copy-done.4 = s32[8,8,8]{2,1,0:T(8,128)S(1)} copy-done((s32[8,8,8]{2,1,0:T(8,128)S(1)}, s32[8,8,8]{2,1,0:T(8,128)}, u32[]{:S(2)}) %copy-start.4) | copy-done | bytes 2072
  3.4 0.2 prepare.1
  3.6 0.1 pack.1
  3.7 3.0 %collective-permute-start.2 = (bf16[14,64,128]{2,1,0:T(8,128)(2,1)S(1)}, bf16[14,64,128]{2,1,0:T(8,128)(2,1)S(1)}, u32[]{:S(2)}, u32[]{:S(2)}) collective-permute-start(bf16[14,64,128]{2,1,0:T(8,128)(2,1)S(1)} %get-tuple-element.37), channel_id=1, source_target_pairs={{0,1},{1,0},{2,3},{3,2},{4,5},{5,4},{6,7},{7,6},{8,9},{9,8},{10,11... | collective-permute-start | bytes 688136 | tf_op jit(solution)/shard_map/ppermute | solution.py:338
  6.7 0.0 collective-permute-start
  6.7 0.7 %collective-permute-start.1 = (bf16[3,64,192]{2,1,0:T(8,128)(2,1)S(1)}, bf16[3,64,192]{2,1,0:T(8,128)(2,1)S(1)}, u32[]{:S(2)}, u32[]{:S(2)}) collective-permute-start(bf16[3,64,192]{2,1,0:T(8,128)(2,1)S(1)} %get-tuple-element.34), channel_id=1, source_target_pairs={{0,0},{2,4},{4,2},{6,8},{8,6},{10,12},{12,10},{14,16},{16,14},{18,... | collective-permute-start | bytes 221192 | tf_op jit(solution)/shard_map/ppermute | solution.py:363
  7.4 0.6 %collective-permute-done.near = bf16[3,64,192]{2,1,0:T(8,128)(2,1)S(1)} collective-permute-done((bf16[3,64,192]{2,1,0:T(8,128)(2,1)S(1)}, bf16[3,64,192]{2,1,0:T(8,128)(2,1)S(1)}, u32[]{:S(2)}, u32[]{:S(2)}) %collective-permute-start) | collective-permute-done | bytes 73760 | tf_op jit(solution)/shard_map/ppermute | solution.py:338
  8.0 0.0 collective-permute-done.1.far
  8.1 0.1 collective-permute-start.3
  8.2 6.5 %collective-permute-start.7 = (bf16[12,64,128]{2,1,0:T(8,128)(2,1)S(1)}, bf16[12,64,128]{2,1,0:T(8,128)(2,1)S(1)}, u32[]{:S(2)}, u32[]{:S(2)}) collective-permute-start(bf16[12,64,128]{2,1,0:T(8,128)(2,1)S(1)} %get-tuple-element.50.refs_4_), channel_id=1, source_target_pairs={{0,4},{1,5},{2,6},{3,7},{4,0},{5,1},{6,2},{7,3},{8,12},{9,13},{10,... | collective-permute-start | bytes 589832 | tf_op jit(solution)/shard_map/ppermute | solution.py:338
  14.8 0.0 copy-start
  14.8 1.6 %copy-done = bf16[5184,192]{0,1:T(8,128)(2,1)S(1)} copy-done((bf16[5184,192]{0,1:T(8,128)(2,1)S(1)}, bf16[5184,192]{0,1:T(8,128)(2,1)}, u32[]{:S(2)}) %copy-start) | copy-done | bytes 1990680
  16.3 0.8 %turn.1.weight = bf16[5184,192]{1,0:T(8,128)(2,1)S(1)} custom-call(bf16[192,5184]{1,0:T(8,128)(2,1)S(1)} %bitcast.5), custom_call_target="tpu_custom_call" | custom-call | flops 1048576 | bytes 4194304 | tf_op jit(solution)/shard_map/turn/pallas_call | solution.py:310
  17.1 0.0 copy-start.1
  17.1 1.0 %collective-permute-start.8 = (bf16[12,64,128]{2,1,0:T(8,128)(2,1)S(1)}, bf16[12,64,128]{2,1,0:T(8,128)(2,1)S(1)}, u32[]{:S(2)}, u32[]{:S(2)}) collective-permute-start(bf16[12,64,128]{2,1,0:T(8,128)(2,1)S(1)} %get-tuple-element.50.refs_4_), channel_id=1, source_target_pairs={{0,5},{1,4},{2,7},{3,6},{4,1},{5,0},{6,3},{7,2},{8,13},{9,12},{10,... | collective-permute-start | bytes 589832 | tf_op jit(solution)/shard_map/ppermute | solution.py:338
  18.1 0.0 collective-permute-done.3.corner
  18.1 0.0 collective-permute-done.2.across.refs_5_
  18.1 3.6 %forward.1 = (bf16[8,64,192]{2,1,0:T(8,128)(2,1)}, bf16[10,80,192]{2,1,0:T(8,128)(2,1)S(1)}, bf16[64,640]{1,0:T(8,128)(2,1)S(1)}, bf16[64,640]{1,0:T(8,128)(2,1)...) custom-call(bf16[8,64,192]{2,1,0:T(8,128)(2,1)S(1)} %get-tuple-element.30.masked, ...), custom_call_target="tpu_custom_call" | custom-call | flops 1061683200 | bytes 1048576 | tf_op jit(solution)/shard_map/forward/pallas_call | solution.py:310
  21.8 0.6 %collective-permute-start.4 = (bf16[64,640]{1,0:T(8,128)(2,1)S(1)}, bf16[64,640]{1,0:T(8,128)(2,1)S(1)}, u32[]{:S(2)}, u32[]{:S(2)}) collective-permute-start(bf16[64,640]{1,0:T(8,128)(2,1)S(1)} %get-tuple-element.42), channel_id=1, source_target_pairs={{0,1},{1,0},{2,3},{3,2},{4,5},{5,4},{6,7},{7,6},{8,9},{9,8},{10,11... | collective-permute-start | bytes 245768 | tf_op jit(solution)/shard_map/ppermute | solution.py:338
  22.3 1.9 %collective-permute-start.5 = (bf16[64,640]{1,0:T(8,128)(2,1)S(1)}, bf16[64,640]{1,0:T(8,128)(2,1)S(1)}, u32[]{:S(2)}, u32[]{:S(2)}) collective-permute-start(bf16[64,640]{1,0:T(8,128)(2,1)S(1)} %get-tuple-element.43), channel_id=1, source_target_pairs={{0,4},{1,5},{2,6},{3,7},{4,0},{5,1},{6,2},{7,3},{8,12},{9,13},{10,... | collective-permute-start | bytes 245768 | tf_op jit(solution)/shard_map/ppermute | solution.py:338
  24.3 1.0 %collective-permute-start.6 = (bf16[64,640]{1,0:T(8,128)(2,1)S(1)}, bf16[64,640]{1,0:T(8,128)(2,1)S(1)}, u32[]{:S(2)}, u32[]{:S(2)}) collective-permute-start(bf16[64,640]{1,0:T(8,128)(2,1)S(1)} %get-tuple-element.44), channel_id=1, source_target_pairs={{0,5},{1,4},{2,7},{3,6},{4,1},{5,0},{6,3},{7,2},{8,13},{9,12},{10,... | collective-permute-start | bytes 245768 | tf_op jit(solution)/shard_map/ppermute | solution.py:338
  25.2 0.0 copy-done.1
  25.2 2.7 %input_gradient.1 = bf16[8,64,192]{2,1,0:T(8,128)(2,1)} custom-call(bf16[10,80,192]{2,1,0:T(8,128)(2,1)S(1)} %get-tuple-element.40.gp, f32[8,64,128]{2,1,0:T(8,128)S(1)} %get-tuple-element.38.live, bf16[192,5184]{1,0:T(8,128)(2,1)S(1)} %bitcast.6), custom_call_target="tpu_custom_call" | custom-call | flops 1358954496 | bytes 4194304 | tf_op jit(solution)/shard_map/input_gradient/pallas_call | solution.py:310
  27.9 0.0 collective-permute-done.4.refs_1_
  27.9 0.0 collective-permute-done.5.refs_2_
  27.9 2.0 %collective-permute-done.6.refs_3_ = bf16[64,640]{1,0:T(8,128)(2,1)S(1)} collective-permute-done((bf16[64,640]{1,0:T(8,128)(2,1)S(1)}, bf16[64,640]{1,0:T(8,128)(2,1)S(1)}, u32[]{:S(2)}, u32[]{:S(2)}) %collective-permute-start.6) | collective-permute-done | bytes 81952 | tf_op jit(solution)/shard_map/ppermute | solution.py:338
  29.9 0.0 collective-permute-done.7.refs_6_
  29.9 0.0 collective-permute-done.8.refs_7_
  29.9 5.6 %kernel_gradient.1 = (f32[4,8,5184]{2,1,0:T(8,128)S(1)}, bf16[4,8,5184]{2,1,0:T(8,128)(2,1)S(1)}) custom-call(bf16[64,640]{1,0:T(8,128)(2,1)S(1)} %get-tuple-element.46.refs_0_, bf16[64,640]{1,0:T(8,128)(2,1)S(1)} %collective-permute-done.4.refs_1_, bf16[64,640]{1,0:T(8,128)(2,1)S(1)} %collective-permute-done.5.refs_2_, ...), custom_call_target="tpu_custom_call" | custom-call | flops 1811939328 | bytes 4194304 | tf_op jit(solution)/shard_map/kernel_gradient/pallas_call | solution.py:310
  35.5 0.1 collective-permute-start.9
  35.6 1.6 %collective-permute-done.9.other = bf16[4,8,5184]{2,1,0:T(8,128)(2,1)S(1)} collective-permute-done((bf16[4,8,5184]{2,1,0:T(8,128)(2,1)S(1)}, bf16[4,8,5184]{2,1,0:T(8,128)(2,1)S(1)}, u32[]{:S(2)}, u32[]{:S(2)}) %collective-permute-start.9) | collective-permute-done | bytes 331808 | tf_op jit(solution)/shard_map/ppermute | solution.py:338
  37.2 0.1 fold.1
  37.3 2.2 %collective-permute-start.10 = (bf16[8,5184]{1,0:T(8,128)(2,1)S(1)}, bf16[8,5184]{1,0:T(8,128)(2,1)S(1)}, u32[]{:S(2)}, u32[]{:S(2)}) collective-permute-start(bf16[8,5184]{1,0:T(8,128)(2,1)S(1)} %get-tuple-element.54), channel_id=1, source_target_pairs={{0,8},{8,0},{16,24},{24,16},{1,9},{9,1},{17,25},{25,17},{2,10},{10... | collective-permute-start | bytes 248840 | tf_op jit(solution)/shard_map/ppermute | solution.py:338
  39.4 2.5 %collective-permute-start.11 = (bf16[8,5184]{1,0:T(8,128)(2,1)S(1)}, bf16[8,5184]{1,0:T(8,128)(2,1)S(1)}, u32[]{:S(2)}, u32[]{:S(2)}) collective-permute-start(bf16[8,5184]{1,0:T(8,128)(2,1)S(1)} %get-tuple-element.55), channel_id=1, source_target_pairs={{0,16},{8,24},{16,0},{24,8},{1,17},{9,25},{17,1},{25,9},{2,18},{10... | collective-permute-start | bytes 248840 | tf_op jit(solution)/shard_map/ppermute | solution.py:338
  41.9 0.0 collective-permute-start.12
  41.9 0.3 collective-permute-done.10.one
  42.2 6.8 %collective-permute-done.11.two = bf16[8,5184]{1,0:T(8,128)(2,1)S(1)} collective-permute-done((bf16[8,5184]{1,0:T(8,128)(2,1)S(1)}, bf16[8,5184]{1,0:T(8,128)(2,1)S(1)}, u32[]{:S(2)}, u32[]{:S(2)}) %collective-permute-start.11) | collective-permute-done | bytes 82976 | tf_op jit(solution)/shard_map/ppermute | solution.py:338
  49.1 0.0 collective-permute-done.12.three
  49.1 0.1 plane_sum.1.mine
  49.1 1.1 %collective-permute-start.13 = (bf16[8,5184]{1,0:T(8,128)(2,1)S(1)}, bf16[8,5184]{1,0:T(8,128)(2,1)S(1)}, u32[]{:S(2)}, u32[]{:S(2)}) collective-permute-start(bf16[8,5184]{1,0:T(8,128)(2,1)S(1)} %plane_sum.1.mine), channel_id=1, source_target_pairs={{0,1},{1,0},{2,3},{3,2},{4,5},{5,4},{6,7},{7,6},{8,9},{9,8},{10,11... | collective-permute-start | bytes 248840 | tf_op jit(solution)/shard_map/ppermute | solution.py:338
  50.2 3.4 %collective-permute-done.13.other = bf16[8,5184]{1,0:T(8,128)(2,1)S(1)} collective-permute-done((bf16[8,5184]{1,0:T(8,128)(2,1)S(1)}, bf16[8,5184]{1,0:T(8,128)(2,1)S(1)}, u32[]{:S(2)}, u32[]{:S(2)}) %collective-permute-start.13) | collective-permute-done | bytes 82976 | tf_op jit(solution)/shard_map/ppermute | solution.py:338
  53.6 0.8 %join.1 = f32[12,5184]{1,0:T(8,128)} custom-call(bf16[8,5184]{1,0:T(8,128)(2,1)S(1)} %plane_sum.1.mine, bf16[8,5184]{1,0:T(8,128)(2,1)S(1)} %collective-permute-done.13.other), custom_call_target="tpu_custom_call" | custom-call | flops 41472 | bytes 580608 | tf_op jit(solution)/shard_map/join/pallas_call | solution.py:310
  (1 shorter events, 0.0 us)
Async XLA Ops:
  0.7 1.0 %copy-start.2 = (bf16[8,8,8,192]{3,2,1,0:T(8,128)(2,1)S(1)}, bf16[8,8,8,192]{3,2,1,0:T(8,128)(2,1)}, u32[]{:S(2)}) copy-start(bf16[8,8,8,192]{3,2,1,0:T(8,128)(2,1)} %param.4) | copy-start | bytes 589828
  1.7 0.9 %copy-start.3 = (bf16[8,8,8,192]{3,2,1,0:T(8,128)(2,1)S(1)}, bf16[8,8,8,192]{3,2,1,0:T(8,128)(2,1)}, u32[]{:S(2)}) copy-start(bf16[8,8,8,192]{3,2,1,0:T(8,128)(2,1)} %param.7) | copy-start | bytes 589828
  2.6 0.8 %copy-start.4 = (s32[8,8,8]{2,1,0:T(8,128)S(1)}, s32[8,8,8]{2,1,0:T(8,128)}, u32[]{:S(2)}) copy-start(s32[8,8,8]{2,1,0:T(8,128)} %mask.1) | copy-start | bytes 6148
  3.7 14.5 %collective-permute-start.2 = (bf16[14,64,128]{2,1,0:T(8,128)(2,1)S(1)}, bf16[14,64,128]{2,1,0:T(8,128)(2,1)S(1)}, u32[]{:S(2)}, u32[]{:S(2)}) collective-permute-start(bf16[14,64,128]{2,1,0:T(8,128)(2,1)S(1)} %get-tuple-element.37), channel_id=1, source_target_pairs={{0,1},{1,0},{2,3},{3,2},{4,5},{5,4},{6,7},{7,6},{8,9},{9,8},{10,11... | collective-permute-start | bytes 688136 | tf_op jit(solution)/shard_map/ppermute | solution.py:338
  6.7 1.3 %collective-permute-start = (bf16[3,64,192]{2,1,0:T(8,128)(2,1)S(1)}, bf16[3,64,192]{2,1,0:T(8,128)(2,1)S(1)}, u32[]{:S(2)}, u32[]{:S(2)}) collective-permute-start(bf16[3,64,192]{2,1,0:T(8,128)(2,1)S(1)} %get-tuple-element.33), channel_id=1, source_target_pairs={{0,2},{2,0},{4,6},{6,4},{8,10},{10,8},{12,14},{14,12},{16,18},{18,... | collective-permute-start | bytes 221192 | tf_op jit(solution)/shard_map/ppermute | solution.py:338
  6.7 1.3 %collective-permute-start.1 = (bf16[3,64,192]{2,1,0:T(8,128)(2,1)S(1)}, bf16[3,64,192]{2,1,0:T(8,128)(2,1)S(1)}, u32[]{:S(2)}, u32[]{:S(2)}) collective-permute-start(bf16[3,64,192]{2,1,0:T(8,128)(2,1)S(1)} %get-tuple-element.34), channel_id=1, source_target_pairs={{0,0},{2,4},{4,2},{6,8},{8,6},{10,12},{12,10},{14,16},{16,14},{18,... | collective-permute-start | bytes 221192 | tf_op jit(solution)/shard_map/ppermute | solution.py:363
  8.1 10.1 %collective-permute-start.3 = (bf16[80,192]{1,0:T(8,128)(2,1)S(1)}, bf16[80,192]{1,0:T(8,128)(2,1)S(1)}, u32[]{:S(2)}, u32[]{:S(2)}) collective-permute-start(bf16[80,192]{1,0:T(8,128)(2,1)S(1)} %corner.1), channel_id=1, source_target_pairs={{0,1},{1,0},{2,3},{3,2},{4,5},{5,4},{6,7},{7,6},{8,9},{9,8},{10,11... | collective-permute-start | bytes 92168 | tf_op jit(solution)/shard_map/ppermute | solution.py:338
  8.2 21.7 %collective-permute-start.7 = (bf16[12,64,128]{2,1,0:T(8,128)(2,1)S(1)}, bf16[12,64,128]{2,1,0:T(8,128)(2,1)S(1)}, u32[]{:S(2)}, u32[]{:S(2)}) collective-permute-start(bf16[12,64,128]{2,1,0:T(8,128)(2,1)S(1)} %get-tuple-element.50.refs_4_), channel_id=1, source_target_pairs={{0,4},{1,5},{2,6},{3,7},{4,0},{5,1},{6,2},{7,3},{8,12},{9,13},{10,... | collective-permute-start | bytes 589832 | tf_op jit(solution)/shard_map/ppermute | solution.py:338
  14.8 1.6 %copy-start = (bf16[5184,192]{0,1:T(8,128)(2,1)S(1)}, bf16[5184,192]{0,1:T(8,128)(2,1)}, u32[]{:S(2)}) copy-start(bf16[5184,192]{0,1:T(8,128)(2,1)} %param.5) | copy-start | bytes 5971972
  17.1 8.2 %copy-start.1 = (bf16[5184,192]{0,1:T(8,128)(2,1)S(1)}, bf16[5184,192]{0,1:T(8,128)(2,1)}, u32[]{:S(2)}) copy-start(bf16[5184,192]{0,1:T(8,128)(2,1)} %param.5) | copy-start | bytes 5971972
  17.1 12.8 %collective-permute-start.8 = (bf16[12,64,128]{2,1,0:T(8,128)(2,1)S(1)}, bf16[12,64,128]{2,1,0:T(8,128)(2,1)S(1)}, u32[]{:S(2)}, u32[]{:S(2)}) collective-permute-start(bf16[12,64,128]{2,1,0:T(8,128)(2,1)S(1)} %get-tuple-element.50.refs_4_), channel_id=1, source_target_pairs={{0,5},{1,4},{2,7},{3,6},{4,1},{5,0},{6,3},{7,2},{8,13},{9,12},{10,... | collective-permute-start | bytes 589832 | tf_op jit(solution)/shard_map/ppermute | solution.py:338
  21.8 6.2 %collective-permute-start.4 = (bf16[64,640]{1,0:T(8,128)(2,1)S(1)}, bf16[64,640]{1,0:T(8,128)(2,1)S(1)}, u32[]{:S(2)}, u32[]{:S(2)}) collective-permute-start(bf16[64,640]{1,0:T(8,128)(2,1)S(1)} %get-tuple-element.42), channel_id=1, source_target_pairs={{0,1},{1,0},{2,3},{3,2},{4,5},{5,4},{6,7},{7,6},{8,9},{9,8},{10,11... | collective-permute-start | bytes 245768 | tf_op jit(solution)/shard_map/ppermute | solution.py:338
  22.3 5.6 %collective-permute-start.5 = (bf16[64,640]{1,0:T(8,128)(2,1)S(1)}, bf16[64,640]{1,0:T(8,128)(2,1)S(1)}, u32[]{:S(2)}, u32[]{:S(2)}) collective-permute-start(bf16[64,640]{1,0:T(8,128)(2,1)S(1)} %get-tuple-element.43), channel_id=1, source_target_pairs={{0,4},{1,5},{2,6},{3,7},{4,0},{5,1},{6,2},{7,3},{8,12},{9,13},{10,... | collective-permute-start | bytes 245768 | tf_op jit(solution)/shard_map/ppermute | solution.py:338
  24.3 5.6 %collective-permute-start.6 = (bf16[64,640]{1,0:T(8,128)(2,1)S(1)}, bf16[64,640]{1,0:T(8,128)(2,1)S(1)}, u32[]{:S(2)}, u32[]{:S(2)}) collective-permute-start(bf16[64,640]{1,0:T(8,128)(2,1)S(1)} %get-tuple-element.44), channel_id=1, source_target_pairs={{0,5},{1,4},{2,7},{3,6},{4,1},{5,0},{6,3},{7,2},{8,13},{9,12},{10,... | collective-permute-start | bytes 245768 | tf_op jit(solution)/shard_map/ppermute | solution.py:338
  35.5 1.7 %collective-permute-start.9 = (bf16[4,8,5184]{2,1,0:T(8,128)(2,1)S(1)}, bf16[4,8,5184]{2,1,0:T(8,128)(2,1)S(1)}, u32[]{:S(2)}, u32[]{:S(2)}) collective-permute-start(bf16[4,8,5184]{2,1,0:T(8,128)(2,1)S(1)} %get-tuple-element.52), channel_id=1, source_target_pairs={{0,2},{1,3},{2,0},{3,1},{4,6},{5,7},{6,4},{7,5},{8,10},{9,11},{10,... | collective-permute-start | bytes 995336 | tf_op jit(solution)/shard_map/ppermute | solution.py:338
  37.3 5.0 %collective-permute-start.10 = (bf16[8,5184]{1,0:T(8,128)(2,1)S(1)}, bf16[8,5184]{1,0:T(8,128)(2,1)S(1)}, u32[]{:S(2)}, u32[]{:S(2)}) collective-permute-start(bf16[8,5184]{1,0:T(8,128)(2,1)S(1)} %get-tuple-element.54), channel_id=1, source_target_pairs={{0,8},{8,0},{16,24},{24,16},{1,9},{9,1},{17,25},{25,17},{2,10},{10... | collective-permute-start | bytes 248840 | tf_op jit(solution)/shard_map/ppermute | solution.py:338
  39.4 9.6 %collective-permute-start.11 = (bf16[8,5184]{1,0:T(8,128)(2,1)S(1)}, bf16[8,5184]{1,0:T(8,128)(2,1)S(1)}, u32[]{:S(2)}, u32[]{:S(2)}) collective-permute-start(bf16[8,5184]{1,0:T(8,128)(2,1)S(1)} %get-tuple-element.55), channel_id=1, source_target_pairs={{0,16},{8,24},{16,0},{24,8},{1,17},{9,25},{17,1},{25,9},{2,18},{10... | collective-permute-start | bytes 248840 | tf_op jit(solution)/shard_map/ppermute | solution.py:338
  41.9 7.2 %collective-permute-start.12 = (bf16[8,5184]{1,0:T(8,128)(2,1)S(1)}, bf16[8,5184]{1,0:T(8,128)(2,1)S(1)}, u32[]{:S(2)}, u32[]{:S(2)}) collective-permute-start(bf16[8,5184]{1,0:T(8,128)(2,1)S(1)} %get-tuple-element.56), channel_id=1, source_target_pairs={{0,24},{8,16},{16,8},{24,0},{1,25},{9,17},{17,9},{25,1},{2,26},{10... | collective-permute-start | bytes 248840 | tf_op jit(solution)/shard_map/ppermute | solution.py:338
  49.1 4.5 %collective-permute-start.13 = (bf16[8,5184]{1,0:T(8,128)(2,1)S(1)}, bf16[8,5184]{1,0:T(8,128)(2,1)S(1)}, u32[]{:S(2)}, u32[]{:S(2)}) collective-permute-start(bf16[8,5184]{1,0:T(8,128)(2,1)S(1)} %plane_sum.1.mine), channel_id=1, source_target_pairs={{0,1},{1,0},{2,3},{3,2},{4,5},{5,4},{6,7},{7,6},{8,9},{9,8},{10,11... | collective-permute-start | bytes 248840 | tf_op jit(solution)/shard_map/ppermute | solution.py:338

commit v7 on v6

--- a/solution.py
+++ b/solution.py
@@ -40,6 +40,34 @@
     plane, row = index // 8 % planes, index % 8
     channel = per * (QUAD * plane + quad) + share * side + row
     out_ref[...] = jnp.where((row < share) & (channel == column), 1.0, 0.0).astype(jnp.bfloat16)
+
+
+def dense(total):
+    tiles = -(-total // 128)
+    moved = tiles // 4
+    return (tiles - moved) * 128, moved * 128
+
+
+def fold_rows(block, total):
+    kept, moved = dense(total)
+    tail = block[:, kept : kept + moved]
+    row = lax.broadcasted_iota(jnp.int32, tail.shape, 0)
+    pieces = []
+    for k in range(3):
+        spare = jnp.where(row == 6, pltpu.roll(tail, 6 - k, 0), pltpu.roll(tail, 4 - k, 0))
+        pieces.append(jnp.where(row < 6, block[:, k * moved : (k + 1) * moved], spare))
+    return jnp.concatenate(pieces + [block[:, 3 * moved : kept]], axis=1)
+
+
+def unfold_rows(block, total):
+    kept, moved = dense(total)
+    row = lax.broadcasted_iota(jnp.int32, (8, moved), 0)
+    tail = jnp.zeros((8, moved), block.dtype)
+    for k in range(3):
+        piece = block[:, k * moved : (k + 1) * moved]
+        tail = jnp.where(row == k, pltpu.roll(piece, 2 + k, 0), tail)
+        tail = jnp.where(row == 3 + k, pltpu.roll(piece, 4 + k, 0), tail)
+    return jnp.concatenate([block, tail], axis=1)[:, :total]
 
 
 def prepare_kernel(features, cot, mask, first, masked_ref, cot_ref, live_ref, near_ref, far_ref):
@@ -275,8 +303,11 @@
                     [got[tap, core, to] for tap in range(9)], axis=1
                 )
     core = lax.rem(quad, 2)
-    keep_ref[...] = part[core]
-    send_ref[...] = part[1 - core].astype(jnp.bfloat16)
+    total = 27 * channels
+    part[:, :, :, total:] = jnp.zeros((2, planes, eight, part.shape[3] - total), f32)
+    for to in range(planes):
+        keep_ref[to] = fold_rows(part[core, to], total)
+        send_ref[to] = fold_rows(part[1 - core, to], total).astype(jnp.bfloat16)
 
 
 def fold_kernel(keep, other, own_ref, *send_refs):
@@ -296,7 +327,9 @@
 def join_kernel(mine, other, out_ref):
     share = out_ref.shape[0] // SIDES
     ahead = position()[3] == 0
-    here, there = mine[...].astype(jnp.float32), other[...].astype(jnp.float32)
+    total = out_ref.shape[1]
+    here = unfold_rows(mine[...].astype(jnp.float32), total)
+    there = unfold_rows(other[...].astype(jnp.float32), total)
     first = jnp.where(ahead, here, there)
     second = jnp.where(ahead, there, here)
     out_ref[0:share] = first[:share]
@@ -343,7 +376,7 @@
     brick = array((width, rows, channels), bf16)
     slab = array((3, rows, channels), bf16)
     pick = call(
-        functools.partial(pick_kernel, planes), "pick", 4, 1 << 16, 1 << 16,
+        functools.partial(pick_kernel, planes), "pick", 4, 1 << 32, 1 << 16,
         array((MEMBERS * group, channels), bf16),
     )()
     vmem = pl.BlockSpec(memory_space=pltpu.VMEM)
@@ -371,7 +404,7 @@
     )(masked, cot)
     across = in_plane(across, CHIPS[1])
     bricks = [packed, across, in_plane(packed, CHIPS[2]), None]
-    packed, near, far = lax.optimization_barrier((packed, near, far))
+    packed, near, far, weight_rows = lax.optimization_barrier((packed, near, far, weight_rows))
     corner = call(
         corner_kernel, "corner", 4, 1 << 16, 1 << 18,
         array((4 * halo + 2 * DEPTH, channels), bf16),
@@ -401,17 +434,17 @@
             pltpu.VMEM((total, channels), bf16),
         ),
     )(gp, live, weight.T)
-    grad_input, *slices = lax.optimization_barrier((grad_input, *slices))
 
     blocks = QUAD // 2
     chips = len(CHIPS)
+    lanes = dense(total)[0]
     keep, fold = call(
         kernel_grad_kernel, "kernel_gradient", 28, 2 * 576 * 3 * 2048 * 256, 4 << 20,
-        (array((planes, 8, total), f32), array((planes, 8, total), bf16)),
+        (array((planes, 8, lanes), f32), array((planes, 8, lanes), bf16)),
         (
             pltpu.VMEM((blocks, SIDES, 2 * group, span), bf16),
             pltpu.VMEM((9 * 2 * group, blocks * (width + 2) * SIDES * rows), bf16),
-            pltpu.VMEM((2, planes, 8, total), f32),
+            pltpu.VMEM((2, planes, 8, sum(dense(total))), f32),
             pltpu.VMEM((blocks, SIDES) + packed.shape, bf16),
             pltpu.VMEM((blocks, width, SIDES * rows, channels), bf16),
             pltpu.SemaphoreType.DMA((chips,)),
@@ -420,13 +453,14 @@
     )(*slices, *bricks)
     own, *sends = call(
         fold_kernel, "fold", 8, 8 * total * 4, 8 * total * 40,
-        (array((8, total), f32),) + (array((8, total), bf16),) * (planes - 1),
+        (array((8, lanes), f32),) + (array((8, lanes), bf16),) * (planes - 1),
     )(keep, in_plane(fold, 2))
     got = [swap(sent, "depth", d, planes) for d, sent in enumerate(sends, 1)]
+    grad_input, *got = lax.optimization_barrier((grad_input, *got))
     voxels = count * SIDES * width * rows
     mine = call(
         functools.partial(sum_kernel, float(1.0 / voxels**0.5)),
-        "plane_sum", 4, 8 * total * 4, 8 * total * 14, array((8, total), bf16),
+        "plane_sum", 4, 8 * total * 4, 8 * total * 14, array((8, lanes), bf16),
     )(own, *got)
     grad_weight = call(
         join_kernel, "join", 4, 8 * total, 8 * total * 14, array((channels // count, total), f32)

time: 54.7 us -> 51.3 us (0.938)
  local copies, waits for them, and re-layouts: 4.22 us -> 0.9 us
  waiting for transfers between devices: 14.8 us -> 14.1 us
  starting transfers between devices: 20.7 us -> 21.4 us
    unnamed x10 -> x8, local copies, waits for them, and re-layouts: 4.22 us -> 0.9 us
    ppermute x13, waiting for transfers between devices: 14.8 us -> 14.1 us  [swap(): return lax.ppermute(piece, axes, [(i, i ^ distance) for i in range(size)])]
    ppermute x13, starting transfers between devices: 20.1 us -> 20.8 us  [swap(): return lax.ppermute(piece, axes, [(i, i ^ distance) for i in range(size)])]
  transfers between devices with their start and end apart: 14 -> 14, of which waited for: 6 -> 7; matrix products, arithmetic and copies ran while one was open for 0% -> 0% of each run, Pallas kernels for 13% -> 14%
where the time goes in v7:
time: 51.3 us; the launch traced here: 51.1 us
  starting transfers between devices  21.4 us (42%)
  waiting for transfers between devices  14.1 us (27%)
  Pallas kernels  14 us (27%)
  local copies, waits for them, and re-layouts  0.9 us (2%)
  between operations  0.75 us (1%)
    ppermute x13, starting transfers between devices, swap(): return lax.ppermute(piece, axes, [(i, i ^ distance) for i in range(size)])  20.8 us
    ppermute x13, waiting for transfers between devices, swap(): return lax.ppermute(piece, axes, [(i, i ^ distance) for i in range(size)])  14.1 us
    pallas_call x11, Pallas kernels, run(): pl.pallas_call(body, out_shape=out_shape, in_specs=in_specs or [spec] * l...  14 us
  transfers between devices with their start and end apart: 14, of which 7 were waited for; matrix products, arithmetic and copies ran while one was open for 0% of the time, Pallas kernels for 14%

profile of v7, /device:TPU:0, one launch (start us, length us, event | category | flops | bytes accessed | tf_op | source)
XLA Modules:
  0.0 51.1 jit_solution(11524006920287263823)
XLA Ops:
  0.6 0.0 copy-start.1
  0.6 0.0 copy-start.2
  0.7 0.0 copy-start.3
  0.7 0.0 copy-start
  0.7 0.1 pick.1.first
  0.8 0.8 %copy-done.1 = bf16[8,8,8,192]{3,2,1,0:T(8,128)(2,1)S(1)} copy-done((bf16[8,8,8,192]{3,2,1,0:T(8,128)(2,1)S(1)}, bf16[8,8,8,192]{3,2,1,0:T(8,128)(2,1)}, u32[]{:S(2)}) %copy-start.1) | copy-done | bytes 196632
  1.6 0.1 copy-done.2
  1.7 0.0 copy-done.3
  1.7 0.2 prepare.1
  1.9 0.1 pack.1
  2.0 3.0 %collective-permute-start.2 = (bf16[14,64,128]{2,1,0:T(8,128)(2,1)S(1)}, bf16[14,64,128]{2,1,0:T(8,128)(2,1)S(1)}, u32[]{:S(2)}, u32[]{:S(2)}) collective-permute-start(bf16[14,64,128]{2,1,0:T(8,128)(2,1)S(1)} %get-tuple-element.37), channel_id=1, source_target_pairs={{0,1},{1,0},{2,3},{3,2},{4,5},{5,4},{6,7},{7,6},{8,9},{9,8},{10,11... | collective-permute-start | bytes 688136 | tf_op jit(solution)/shard_map/ppermute | solution.py:371
  5.0 0.0 collective-permute-start
  5.0 0.7 %collective-permute-start.1 = (bf16[3,64,192]{2,1,0:T(8,128)(2,1)S(1)}, bf16[3,64,192]{2,1,0:T(8,128)(2,1)S(1)}, u32[]{:S(2)}, u32[]{:S(2)}) collective-permute-start(bf16[3,64,192]{2,1,0:T(8,128)(2,1)S(1)} %get-tuple-element.34), channel_id=1, source_target_pairs={{0,0},{2,4},{4,2},{6,8},{8,6},{10,12},{12,10},{14,16},{16,14},{18,... | collective-permute-start | bytes 221192 | tf_op jit(solution)/shard_map/ppermute | solution.py:396
  5.7 0.0 copy-done
  5.7 0.8 %turn.1.weight = bf16[5184,192]{1,0:T(8,128)(2,1)S(1)} custom-call(bf16[192,5184]{1,0:T(8,128)(2,1)S(1)} %bitcast.5), custom_call_target="tpu_custom_call" | custom-call | flops 1048576 | bytes 4194304 | tf_op jit(solution)/shard_map/turn/pallas_call | solution.py:343
  6.4 0.0 collective-permute-done.near
  6.5 0.0 collective-permute-done.1.far
  6.5 0.2 collective-permute-start.3
  6.7 6.3 %collective-permute-start.7 = (bf16[12,64,128]{2,1,0:T(8,128)(2,1)S(1)}, bf16[12,64,128]{2,1,0:T(8,128)(2,1)S(1)}, u32[]{:S(2)}, u32[]{:S(2)}) collective-permute-start(bf16[12,64,128]{2,1,0:T(8,128)(2,1)S(1)} %get-tuple-element.46.refs_4_), channel_id=1, source_target_pairs={{0,4},{1,5},{2,6},{3,7},{4,0},{5,1},{6,2},{7,3},{8,12},{9,13},{10,... | collective-permute-start | bytes 589832 | tf_op jit(solution)/shard_map/ppermute | solution.py:371
  13.0 1.0 %collective-permute-start.8 = (bf16[12,64,128]{2,1,0:T(8,128)(2,1)S(1)}, bf16[12,64,128]{2,1,0:T(8,128)(2,1)S(1)}, u32[]{:S(2)}, u32[]{:S(2)}) collective-permute-start(bf16[12,64,128]{2,1,0:T(8,128)(2,1)S(1)} %get-tuple-element.46.refs_4_), channel_id=1, source_target_pairs={{0,5},{1,4},{2,7},{3,6},{4,1},{5,0},{6,3},{7,2},{8,13},{9,12},{10,... | collective-permute-start | bytes 589832 | tf_op jit(solution)/shard_map/ppermute | solution.py:371
  14.0 0.0 collective-permute-done.3.corner
  14.0 0.0 collective-permute-done.2.across.refs_5_
  14.0 3.6 %forward.1 = (bf16[8,64,192]{2,1,0:T(8,128)(2,1)}, bf16[10,80,192]{2,1,0:T(8,128)(2,1)S(1)}, bf16[64,640]{1,0:T(8,128)(2,1)S(1)}, bf16[64,640]{1,0:T(8,128)(2,1)...) custom-call(bf16[8,64,192]{2,1,0:T(8,128)(2,1)S(1)} %get-tuple-element.30.masked, ...), custom_call_target="tpu_custom_call" | custom-call | flops 1061683200 | bytes 1048576 | tf_op jit(solution)/shard_map/forward/pallas_call | solution.py:343
  17.6 0.6 %collective-permute-start.4 = (bf16[64,640]{1,0:T(8,128)(2,1)S(1)}, bf16[64,640]{1,0:T(8,128)(2,1)S(1)}, u32[]{:S(2)}, u32[]{:S(2)}) collective-permute-start(bf16[64,640]{1,0:T(8,128)(2,1)S(1)} %get-tuple-element.43), channel_id=1, source_target_pairs={{0,1},{1,0},{2,3},{3,2},{4,5},{5,4},{6,7},{7,6},{8,9},{9,8},{10,11... | collective-permute-start | bytes 245768 | tf_op jit(solution)/shard_map/ppermute | solution.py:371
  18.2 2.5 %collective-permute-start.5 = (bf16[64,640]{1,0:T(8,128)(2,1)S(1)}, bf16[64,640]{1,0:T(8,128)(2,1)S(1)}, u32[]{:S(2)}, u32[]{:S(2)}) collective-permute-start(bf16[64,640]{1,0:T(8,128)(2,1)S(1)} %get-tuple-element.44), channel_id=1, source_target_pairs={{0,4},{1,5},{2,6},{3,7},{4,0},{5,1},{6,2},{7,3},{8,12},{9,13},{10,... | collective-permute-start | bytes 245768 | tf_op jit(solution)/shard_map/ppermute | solution.py:371
  20.6 1.0 %collective-permute-start.6 = (bf16[64,640]{1,0:T(8,128)(2,1)S(1)}, bf16[64,640]{1,0:T(8,128)(2,1)S(1)}, u32[]{:S(2)}, u32[]{:S(2)}) collective-permute-start(bf16[64,640]{1,0:T(8,128)(2,1)S(1)} %get-tuple-element.45), channel_id=1, source_target_pairs={{0,5},{1,4},{2,7},{3,6},{4,1},{5,0},{6,3},{7,2},{8,13},{9,12},{10,... | collective-permute-start | bytes 245768 | tf_op jit(solution)/shard_map/ppermute | solution.py:371
  21.6 0.0 collective-permute-done.7.refs_6_
  21.6 2.1 %collective-permute-done.8.refs_7_ = bf16[12,64,128]{2,1,0:T(8,128)(2,1)S(1)} collective-permute-done((bf16[12,64,128]{2,1,0:T(8,128)(2,1)S(1)}, bf16[12,64,128]{2,1,0:T(8,128)(2,1)S(1)}, u32[]{:S(2)}, u32[]{:S(2)}) %collective-permute-start.8) | collective-permute-done | bytes 196640 | tf_op jit(solution)/shard_map/ppermute | solution.py:371
  23.7 2.3 %collective-permute-done.4.refs_1_ = bf16[64,640]{1,0:T(8,128)(2,1)S(1)} collective-permute-done((bf16[64,640]{1,0:T(8,128)(2,1)S(1)}, bf16[64,640]{1,0:T(8,128)(2,1)S(1)}, u32[]{:S(2)}, u32[]{:S(2)}) %collective-permute-start.4) | collective-permute-done | bytes 81952 | tf_op jit(solution)/shard_map/ppermute | solution.py:371
  26.0 0.0 collective-permute-done.5.refs_2_
  26.0 1.1 %collective-permute-done.6.refs_3_ = bf16[64,640]{1,0:T(8,128)(2,1)S(1)} collective-permute-done((bf16[64,640]{1,0:T(8,128)(2,1)S(1)}, bf16[64,640]{1,0:T(8,128)(2,1)S(1)}, u32[]{:S(2)}, u32[]{:S(2)}) %collective-permute-start.6) | collective-permute-done | bytes 81952 | tf_op jit(solution)/shard_map/ppermute | solution.py:371
  27.1 5.6 %kernel_gradient.1 = (f32[4,8,3968]{2,1,0:T(8,128)S(1)}, bf16[4,8,3968]{2,1,0:T(8,128)(2,1)S(1)}) custom-call(bf16[64,640]{1,0:T(8,128)(2,1)S(1)} %get-tuple-element.42.refs_0_, bf16[64,640]{1,0:T(8,128)(2,1)S(1)} %collective-permute-done.4.refs_1_, bf16[64,640]{1,0:T(8,128)(2,1)S(1)} %collective-permute-done.5.refs_2_, ...), custom_call_target="tpu_custom_call" | custom-call | flops 1811939328 | bytes 4194304 | tf_op jit(solution)/shard_map/kernel_gradient/pallas_call | solution.py:343
  32.7 0.3 collective-permute-start.9
  33.0 1.3 %collective-permute-done.9.other = bf16[4,8,3968]{2,1,0:T(8,128)(2,1)S(1)} collective-permute-done((bf16[4,8,3968]{2,1,0:T(8,128)(2,1)S(1)}, bf16[4,8,3968]{2,1,0:T(8,128)(2,1)S(1)}, u32[]{:S(2)}, u32[]{:S(2)}) %collective-permute-start.9) | collective-permute-done | bytes 253984 | tf_op jit(solution)/shard_map/ppermute | solution.py:371
  34.3 0.1 fold.1
  34.4 2.8 %collective-permute-start.10 = (bf16[8,3968]{1,0:T(8,128)(2,1)S(1)}, bf16[8,3968]{1,0:T(8,128)(2,1)S(1)}, u32[]{:S(2)}, u32[]{:S(2)}) collective-permute-start(bf16[8,3968]{1,0:T(8,128)(2,1)S(1)} %get-tuple-element.49), channel_id=1, source_target_pairs={{0,8},{8,0},{16,24},{24,16},{1,9},{9,1},{17,25},{25,17},{2,10},{10... | collective-permute-start | bytes 190472 | tf_op jit(solution)/shard_map/ppermute | solution.py:371
  37.2 2.6 %collective-permute-start.11 = (bf16[8,3968]{1,0:T(8,128)(2,1)S(1)}, bf16[8,3968]{1,0:T(8,128)(2,1)S(1)}, u32[]{:S(2)}, u32[]{:S(2)}) collective-permute-start(bf16[8,3968]{1,0:T(8,128)(2,1)S(1)} %get-tuple-element.50), channel_id=1, source_target_pairs={{0,16},{8,24},{16,0},{24,8},{1,17},{9,25},{17,1},{25,9},{2,18},{10... | collective-permute-start | bytes 190472 | tf_op jit(solution)/shard_map/ppermute | solution.py:371
  39.8 0.0 collective-permute-start.12
  39.8 2.7 %input_gradient.1 = bf16[8,64,192]{2,1,0:T(8,128)(2,1)} custom-call(bf16[10,80,192]{2,1,0:T(8,128)(2,1)S(1)} %get-tuple-element.41.gp, f32[8,64,128]{2,1,0:T(8,128)S(1)} %get-tuple-element.38.live, bf16[192,5184]{1,0:T(8,128)(2,1)S(1)} %bitcast.6), custom_call_target="tpu_custom_call" | custom-call | flops 1358954496 | bytes 4194304 | tf_op jit(solution)/shard_map/input_gradient/pallas_call | solution.py:343
  42.5 0.0 collective-permute-done.10.one
  42.5 2.2 %collective-permute-done.11.two = bf16[8,3968]{1,0:T(8,128)(2,1)S(1)} collective-permute-done((bf16[8,3968]{1,0:T(8,128)(2,1)S(1)}, bf16[8,3968]{1,0:T(8,128)(2,1)S(1)}, u32[]{:S(2)}, u32[]{:S(2)}) %collective-permute-start.11) | collective-permute-done | bytes 63520 | tf_op jit(solution)/shard_map/ppermute | solution.py:371
  44.6 1.3 %collective-permute-done.12.three = bf16[8,3968]{1,0:T(8,128)(2,1)S(1)} collective-permute-done((bf16[8,3968]{1,0:T(8,128)(2,1)S(1)}, bf16[8,3968]{1,0:T(8,128)(2,1)S(1)}, u32[]{:S(2)}, u32[]{:S(2)}) %collective-permute-start.12) | collective-permute-done | bytes 63520 | tf_op jit(solution)/shard_map/ppermute | solution.py:371
  46.0 0.6 %collective-permute-start.13 = (bf16[8,3968]{1,0:T(8,128)(2,1)S(1)}, bf16[8,3968]{1,0:T(8,128)(2,1)S(1)}, u32[]{:S(2)}, u32[]{:S(2)}) collective-permute-start(bf16[8,3968]{1,0:T(8,128)(2,1)S(1)} %plane_sum.1.mine), channel_id=1, source_target_pairs={{0,1},{1,0},{2,3},{3,2},{4,5},{5,4},{6,7},{7,6},{8,9},{9,8},{10,11... | collective-permute-start | bytes 190472 | tf_op jit(solution)/shard_map/ppermute | solution.py:371
  46.6 3.7 %collective-permute-done.13.other = bf16[8,3968]{1,0:T(8,128)(2,1)S(1)} collective-permute-done((bf16[8,3968]{1,0:T(8,128)(2,1)S(1)}, bf16[8,3968]{1,0:T(8,128)(2,1)S(1)}, u32[]{:S(2)}, u32[]{:S(2)}) %collective-permute-start.13) | collective-permute-done | bytes 63520 | tf_op jit(solution)/shard_map/ppermute | solution.py:371
  50.3 0.8 %join.1 = f32[12,5184]{1,0:T(8,128)} custom-call(bf16[8,3968]{1,0:T(8,128)(2,1)S(1)} %plane_sum.1.mine, bf16[8,3968]{1,0:T(8,128)(2,1)S(1)} %collective-permute-done.13.other), custom_call_target="tpu_custom_call" | custom-call | flops 41472 | bytes 580608 | tf_op jit(solution)/shard_map/join/pallas_call | solution.py:343
  (2 shorter events, 0.1 us)
Async XLA Ops:
  0.6 1.0 %copy-start.1 = (bf16[8,8,8,192]{3,2,1,0:T(8,128)(2,1)S(1)}, bf16[8,8,8,192]{3,2,1,0:T(8,128)(2,1)}, u32[]{:S(2)}) copy-start(bf16[8,8,8,192]{3,2,1,0:T(8,128)(2,1)} %param.4) | copy-start | bytes 589828
  0.6 1.0 %copy-start.2 = (bf16[8,8,8,192]{3,2,1,0:T(8,128)(2,1)S(1)}, bf16[8,8,8,192]{3,2,1,0:T(8,128)(2,1)}, u32[]{:S(2)}) copy-start(bf16[8,8,8,192]{3,2,1,0:T(8,128)(2,1)} %param.7) | copy-start | bytes 589828
  0.7 1.0 %copy-start.3 = (s32[8,8,8]{2,1,0:T(8,128)S(1)}, s32[8,8,8]{2,1,0:T(8,128)}, u32[]{:S(2)}) copy-start(s32[8,8,8]{2,1,0:T(8,128)} %mask.1) | copy-start | bytes 6148
  0.7 5.0 %copy-start = (bf16[5184,192]{0,1:T(8,128)(2,1)S(1)}, bf16[5184,192]{0,1:T(8,128)(2,1)}, u32[]{:S(2)}) copy-start(bf16[5184,192]{0,1:T(8,128)(2,1)} %param.5) | copy-start | bytes 5971972
  2.0 12.0 %collective-permute-start.2 = (bf16[14,64,128]{2,1,0:T(8,128)(2,1)S(1)}, bf16[14,64,128]{2,1,0:T(8,128)(2,1)S(1)}, u32[]{:S(2)}, u32[]{:S(2)}) collective-permute-start(bf16[14,64,128]{2,1,0:T(8,128)(2,1)S(1)} %get-tuple-element.37), channel_id=1, source_target_pairs={{0,1},{1,0},{2,3},{3,2},{4,5},{5,4},{6,7},{7,6},{8,9},{9,8},{10,11... | collective-permute-start | bytes 688136 | tf_op jit(solution)/shard_map/ppermute | solution.py:371
  5.0 1.5 %collective-permute-start = (bf16[3,64,192]{2,1,0:T(8,128)(2,1)S(1)}, bf16[3,64,192]{2,1,0:T(8,128)(2,1)S(1)}, u32[]{:S(2)}, u32[]{:S(2)}) collective-permute-start(bf16[3,64,192]{2,1,0:T(8,128)(2,1)S(1)} %get-tuple-element.33), channel_id=1, source_target_pairs={{0,2},{2,0},{4,6},{6,4},{8,10},{10,8},{12,14},{14,12},{16,18},{18,... | collective-permute-start | bytes 221192 | tf_op jit(solution)/shard_map/ppermute | solution.py:371
  5.0 1.5 %collective-permute-start.1 = (bf16[3,64,192]{2,1,0:T(8,128)(2,1)S(1)}, bf16[3,64,192]{2,1,0:T(8,128)(2,1)S(1)}, u32[]{:S(2)}, u32[]{:S(2)}) collective-permute-start(bf16[3,64,192]{2,1,0:T(8,128)(2,1)S(1)} %get-tuple-element.34), channel_id=1, source_target_pairs={{0,0},{2,4},{4,2},{6,8},{8,6},{10,12},{12,10},{14,16},{16,14},{18,... | collective-permute-start | bytes 221192 | tf_op jit(solution)/shard_map/ppermute | solution.py:396
  6.5 7.5 %collective-permute-start.3 = (bf16[80,192]{1,0:T(8,128)(2,1)S(1)}, bf16[80,192]{1,0:T(8,128)(2,1)S(1)}, u32[]{:S(2)}, u32[]{:S(2)}) collective-permute-start(bf16[80,192]{1,0:T(8,128)(2,1)S(1)} %corner.1), channel_id=1, source_target_pairs={{0,1},{1,0},{2,3},{3,2},{4,5},{5,4},{6,7},{7,6},{8,9},{9,8},{10,11... | collective-permute-start | bytes 92168 | tf_op jit(solution)/shard_map/ppermute | solution.py:371
  6.7 14.9 %collective-permute-start.7 = (bf16[12,64,128]{2,1,0:T(8,128)(2,1)S(1)}, bf16[12,64,128]{2,1,0:T(8,128)(2,1)S(1)}, u32[]{:S(2)}, u32[]{:S(2)}) collective-permute-start(bf16[12,64,128]{2,1,0:T(8,128)(2,1)S(1)} %get-tuple-element.46.refs_4_), channel_id=1, source_target_pairs={{0,4},{1,5},{2,6},{3,7},{4,0},{5,1},{6,2},{7,3},{8,12},{9,13},{10,... | collective-permute-start | bytes 589832 | tf_op jit(solution)/shard_map/ppermute | solution.py:371
  13.0 10.7 %collective-permute-start.8 = (bf16[12,64,128]{2,1,0:T(8,128)(2,1)S(1)}, bf16[12,64,128]{2,1,0:T(8,128)(2,1)S(1)}, u32[]{:S(2)}, u32[]{:S(2)}) collective-permute-start(bf16[12,64,128]{2,1,0:T(8,128)(2,1)S(1)} %get-tuple-element.46.refs_4_), channel_id=1, source_target_pairs={{0,5},{1,4},{2,7},{3,6},{4,1},{5,0},{6,3},{7,2},{8,13},{9,12},{10,... | collective-permute-start | bytes 589832 | tf_op jit(solution)/shard_map/ppermute | solution.py:371
  17.6 8.4 %collective-permute-start.4 = (bf16[64,640]{1,0:T(8,128)(2,1)S(1)}, bf16[64,640]{1,0:T(8,128)(2,1)S(1)}, u32[]{:S(2)}, u32[]{:S(2)}) collective-permute-start(bf16[64,640]{1,0:T(8,128)(2,1)S(1)} %get-tuple-element.43), channel_id=1, source_target_pairs={{0,1},{1,0},{2,3},{3,2},{4,5},{5,4},{6,7},{7,6},{8,9},{9,8},{10,11... | collective-permute-start | bytes 245768 | tf_op jit(solution)/shard_map/ppermute | solution.py:371
  18.2 7.8 %collective-permute-start.5 = (bf16[64,640]{1,0:T(8,128)(2,1)S(1)}, bf16[64,640]{1,0:T(8,128)(2,1)S(1)}, u32[]{:S(2)}, u32[]{:S(2)}) collective-permute-start(bf16[64,640]{1,0:T(8,128)(2,1)S(1)} %get-tuple-element.44), channel_id=1, source_target_pairs={{0,4},{1,5},{2,6},{3,7},{4,0},{5,1},{6,2},{7,3},{8,12},{9,13},{10,... | collective-permute-start | bytes 245768 | tf_op jit(solution)/shard_map/ppermute | solution.py:371
  20.6 6.5 %collective-permute-start.6 = (bf16[64,640]{1,0:T(8,128)(2,1)S(1)}, bf16[64,640]{1,0:T(8,128)(2,1)S(1)}, u32[]{:S(2)}, u32[]{:S(2)}) collective-permute-start(bf16[64,640]{1,0:T(8,128)(2,1)S(1)} %get-tuple-element.45), channel_id=1, source_target_pairs={{0,5},{1,4},{2,7},{3,6},{4,1},{5,0},{6,3},{7,2},{8,13},{9,12},{10,... | collective-permute-start | bytes 245768 | tf_op jit(solution)/shard_map/ppermute | solution.py:371
  32.7 1.6 %collective-permute-start.9 = (bf16[4,8,3968]{2,1,0:T(8,128)(2,1)S(1)}, bf16[4,8,3968]{2,1,0:T(8,128)(2,1)S(1)}, u32[]{:S(2)}, u32[]{:S(2)}) collective-permute-start(bf16[4,8,3968]{2,1,0:T(8,128)(2,1)S(1)} %get-tuple-element.48), channel_id=1, source_target_pairs={{0,2},{1,3},{2,0},{3,1},{4,6},{5,7},{6,4},{7,5},{8,10},{9,11},{10,... | collective-permute-start | bytes 761864 | tf_op jit(solution)/shard_map/ppermute | solution.py:371
  34.4 8.1 %collective-permute-start.10 = (bf16[8,3968]{1,0:T(8,128)(2,1)S(1)}, bf16[8,3968]{1,0:T(8,128)(2,1)S(1)}, u32[]{:S(2)}, u32[]{:S(2)}) collective-permute-start(bf16[8,3968]{1,0:T(8,128)(2,1)S(1)} %get-tuple-element.49), channel_id=1, source_target_pairs={{0,8},{8,0},{16,24},{24,16},{1,9},{9,1},{17,25},{25,17},{2,10},{10... | collective-permute-start | bytes 190472 | tf_op jit(solution)/shard_map/ppermute | solution.py:371
  37.2 7.4 %collective-permute-start.11 = (bf16[8,3968]{1,0:T(8,128)(2,1)S(1)}, bf16[8,3968]{1,0:T(8,128)(2,1)S(1)}, u32[]{:S(2)}, u32[]{:S(2)}) collective-permute-start(bf16[8,3968]{1,0:T(8,128)(2,1)S(1)} %get-tuple-element.50), channel_id=1, source_target_pairs={{0,16},{8,24},{16,0},{24,8},{1,17},{9,25},{17,1},{25,9},{2,18},{10... | collective-permute-start | bytes 190472 | tf_op jit(solution)/shard_map/ppermute | solution.py:371
  39.8 6.1 %collective-permute-start.12 = (bf16[8,3968]{1,0:T(8,128)(2,1)S(1)}, bf16[8,3968]{1,0:T(8,128)(2,1)S(1)}, u32[]{:S(2)}, u32[]{:S(2)}) collective-permute-start(bf16[8,3968]{1,0:T(8,128)(2,1)S(1)} %get-tuple-element.51), channel_id=1, source_target_pairs={{0,24},{8,16},{16,8},{24,0},{1,25},{9,17},{17,9},{25,1},{2,26},{10... | collective-permute-start | bytes 190472 | tf_op jit(solution)/shard_map/ppermute | solution.py:371
  46.0 4.3 %collective-permute-start.13 = (bf16[8,3968]{1,0:T(8,128)(2,1)S(1)}, bf16[8,3968]{1,0:T(8,128)(2,1)S(1)}, u32[]{:S(2)}, u32[]{:S(2)}) collective-permute-start(bf16[8,3968]{1,0:T(8,128)(2,1)S(1)} %plane_sum.1.mine), channel_id=1, source_target_pairs={{0,1},{1,0},{2,3},{3,2},{4,5},{5,4},{6,7},{7,6},{8,9},{9,8},{10,11... | collective-permute-start | bytes 190472 | tf_op jit(solution)/shard_map/ppermute | solution.py:371

commit v8 on v7

--- a/solution.py
+++ b/solution.py
@@ -395,7 +395,7 @@
     ends = [min(max(((i + 1) ^ 1) - 1, 0), count - 1) for i in range(count)]
     far = lax.ppermute(far, WIDE, list(enumerate(ends)))
     weight_rows = call(
-        turn_kernel, "turn", 8, 1 << 20, 4 << 20, array((total, channels), bf16)
+        turn_kernel, "turn", 8, 1 << 34, 4 << 20, array((total, channels), bf16)
     )(weight.T)
     slabs = width * channels // 128
     packed, across = call(
@@ -410,7 +410,7 @@
         array((4 * halo + 2 * DEPTH, channels), bf16),
         (pltpu.VMEM((2,) + slab.shape, bf16),),
     )(near, far)
-    corner = in_plane(corner, 1)
+    corner, bricks[2] = lax.optimization_barrier((in_plane(corner, 1), bricks[2]))
     bricks[3] = in_plane(packed, CHIPS[3])
 
     mid = rows + 2 * DEPTH

time: 51.3 us -> 54.9 us (1.070)
  waiting for transfers between devices: 14.1 us -> 20.3 us
  starting transfers between devices: 21.4 us -> 18.8 us
    ppermute x13, waiting for transfers between devices: 14.1 us -> 20.3 us  [swap(): return lax.ppermute(piece, axes, [(i, i ^ distance) for i in range(size)])]
    ppermute x13, starting transfers between devices: 20.8 us -> 18.1 us  [swap(): return lax.ppermute(piece, axes, [(i, i ^ distance) for i in range(size)])]
  transfers between devices with their start and end apart: 14 -> 14, of which waited for: 7 -> 8; matrix products, arithmetic and copies ran while one was open for 0% -> 0% of each run, Pallas kernels for 14% -> 13%
where the time goes in v8:
time: 54.9 us; the launch traced here: 54.7 us
  waiting for transfers between devices  20.3 us (37%)
  starting transfers between devices  18.8 us (34%)
  Pallas kernels  14 us (26%)
  local copies, waits for them, and re-layouts  0.92 us (2%)
  between operations  0.76 us (1%)
    ppermute x13, waiting for transfers between devices, swap(): return lax.ppermute(piece, axes, [(i, i ^ distance) for i in range(size)])  20.3 us
    ppermute x13, starting transfers between devices, swap(): return lax.ppermute(piece, axes, [(i, i ^ distance) for i in range(size)])  18.1 us
    pallas_call x11, Pallas kernels, run(): pl.pallas_call(body, out_shape=out_shape, in_specs=in_specs or [spec] * l...  14 us
  transfers between devices with their start and end apart: 14, of which 8 were waited for; matrix products, arithmetic and copies ran while one was open for 0% of the time, Pallas kernels for 13%

profile of v8, /device:TPU:0, one launch (start us, length us, event | category | flops | bytes accessed | tf_op | source)
XLA Modules:
  0.0 54.7 jit_solution(1629669675338883983)
XLA Ops:
  0.6 0.0 copy-start.1
  0.6 0.0 copy-start.2
  0.7 0.0 copy-start
  0.7 0.0 copy-start.3
  0.7 0.1 pick.1.first
  0.8 0.8 %copy-done.1 = bf16[8,8,8,192]{3,2,1,0:T(8,128)(2,1)S(1)} copy-done((bf16[8,8,8,192]{3,2,1,0:T(8,128)(2,1)S(1)}, bf16[8,8,8,192]{3,2,1,0:T(8,128)(2,1)}, u32[]{:S(2)}) %copy-start.1) | copy-done | bytes 196632
  1.6 0.0 copy-done.2
  1.6 0.1 copy-done
  1.7 0.2 prepare.1
  1.9 0.5 collective-permute-start
  2.4 0.7 %collective-permute-start.1 = (bf16[3,64,192]{2,1,0:T(8,128)(2,1)S(1)}, bf16[3,64,192]{2,1,0:T(8,128)(2,1)S(1)}, u32[]{:S(2)}, u32[]{:S(2)}) collective-permute-start(bf16[3,64,192]{2,1,0:T(8,128)(2,1)S(1)} %get-tuple-element.36), channel_id=1, source_target_pairs={{0,0},{2,4},{4,2},{6,8},{8,6},{10,12},{12,10},{14,16},{16,14},{18,... | collective-permute-start | bytes 221192 | tf_op jit(solution)/shard_map/ppermute | solution.py:396
  3.1 0.1 pack.1
  3.2 3.8 %collective-permute-start.4 = (bf16[12,64,128]{2,1,0:T(8,128)(2,1)S(1)}, bf16[12,64,128]{2,1,0:T(8,128)(2,1)S(1)}, u32[]{:S(2)}, u32[]{:S(2)}) collective-permute-start(bf16[12,64,128]{2,1,0:T(8,128)(2,1)S(1)} %get-tuple-element.50.refs_4_), channel_id=1, source_target_pairs={{0,4},{1,5},{2,6},{3,7},{4,0},{5,1},{6,2},{7,3},{8,12},{9,13},{10,... | collective-permute-start | bytes 589832 | tf_op jit(solution)/shard_map/ppermute | solution.py:371
  7.0 2.1 %collective-permute-start.2 = (bf16[14,64,128]{2,1,0:T(8,128)(2,1)S(1)}, bf16[14,64,128]{2,1,0:T(8,128)(2,1)S(1)}, u32[]{:S(2)}, u32[]{:S(2)}) collective-permute-start(bf16[14,64,128]{2,1,0:T(8,128)(2,1)S(1)} %get-tuple-element.39), channel_id=1, source_target_pairs={{0,1},{1,0},{2,3},{3,2},{4,5},{5,4},{6,7},{7,6},{8,9},{9,8},{10,11... | collective-permute-start | bytes 688136 | tf_op jit(solution)/shard_map/ppermute | solution.py:371
  9.1 0.0 copy-done.3
  9.1 0.8 %turn.1.weight = bf16[5184,192]{1,0:T(8,128)(2,1)S(1)} custom-call(bf16[192,5184]{1,0:T(8,128)(2,1)S(1)} %bitcast.7), custom_call_target="tpu_custom_call" | custom-call | flops 17179869184 | bytes 4194304 | tf_op jit(solution)/shard_map/turn/pallas_call | solution.py:343
  9.9 0.0 collective-permute-done.near
  9.9 0.0 collective-permute-done.1.far
  10.0 0.1 collective-permute-start.3
  10.0 2.7 %collective-permute-start.8 = (bf16[12,64,128]{2,1,0:T(8,128)(2,1)S(1)}, bf16[12,64,128]{2,1,0:T(8,128)(2,1)S(1)}, u32[]{:S(2)}, u32[]{:S(2)}) collective-permute-start(bf16[12,64,128]{2,1,0:T(8,128)(2,1)S(1)} %get-tuple-element.50.refs_4_), channel_id=1, source_target_pairs={{0,5},{1,4},{2,7},{3,6},{4,1},{5,0},{6,3},{7,2},{8,13},{9,12},{10,... | collective-permute-start | bytes 589832 | tf_op jit(solution)/shard_map/ppermute | solution.py:371
  12.7 7.7 %collective-permute-done.3.corner = bf16[80,192]{1,0:T(8,128)(2,1)S(1)} collective-permute-done((bf16[80,192]{1,0:T(8,128)(2,1)S(1)}, bf16[80,192]{1,0:T(8,128)(2,1)S(1)}, u32[]{:S(2)}, u32[]{:S(2)}) %collective-permute-start.3) | collective-permute-done | bytes 30752 | tf_op jit(solution)/shard_map/ppermute | solution.py:371
  20.4 0.0 collective-permute-done.4.refs_6_
  20.4 0.0 collective-permute-done.2.across.refs_5_
  20.4 3.6 %forward.1 = (bf16[8,64,192]{2,1,0:T(8,128)(2,1)}, bf16[10,80,192]{2,1,0:T(8,128)(2,1)S(1)}, bf16[64,640]{1,0:T(8,128)(2,1)S(1)}, bf16[64,640]{1,0:T(8,128)(2,1)...) custom-call(bf16[8,64,192]{2,1,0:T(8,128)(2,1)S(1)} %get-tuple-element.32.masked, ...), custom_call_target="tpu_custom_call" | custom-call | flops 1061683200 | bytes 1048576 | tf_op jit(solution)/shard_map/forward/pallas_call | solution.py:343
  24.0 2.1 %collective-permute-start.5 = (bf16[64,640]{1,0:T(8,128)(2,1)S(1)}, bf16[64,640]{1,0:T(8,128)(2,1)S(1)}, u32[]{:S(2)}, u32[]{:S(2)}) collective-permute-start(bf16[64,640]{1,0:T(8,128)(2,1)S(1)} %get-tuple-element.46), channel_id=1, source_target_pairs={{0,1},{1,0},{2,3},{3,2},{4,5},{5,4},{6,7},{7,6},{8,9},{9,8},{10,11... | collective-permute-start | bytes 245768 | tf_op jit(solution)/shard_map/ppermute | solution.py:371
  26.1 0.1 collective-permute-start.6
  26.2 1.4 %collective-permute-start.7 = (bf16[64,640]{1,0:T(8,128)(2,1)S(1)}, bf16[64,640]{1,0:T(8,128)(2,1)S(1)}, u32[]{:S(2)}, u32[]{:S(2)}) collective-permute-start(bf16[64,640]{1,0:T(8,128)(2,1)S(1)} %get-tuple-element.48), channel_id=1, source_target_pairs={{0,5},{1,4},{2,7},{3,6},{4,1},{5,0},{6,3},{7,2},{8,13},{9,12},{10,... | collective-permute-start | bytes 245768 | tf_op jit(solution)/shard_map/ppermute | solution.py:371
  27.6 0.0 collective-permute-done.8.refs_7_
  27.6 1.0 %collective-permute-done.5.refs_1_ = bf16[64,640]{1,0:T(8,128)(2,1)S(1)} collective-permute-done((bf16[64,640]{1,0:T(8,128)(2,1)S(1)}, bf16[64,640]{1,0:T(8,128)(2,1)S(1)}, u32[]{:S(2)}, u32[]{:S(2)}) %collective-permute-start.5) | collective-permute-done | bytes 81952 | tf_op jit(solution)/shard_map/ppermute | solution.py:371
  28.6 2.3 %collective-permute-done.6.refs_2_ = bf16[64,640]{1,0:T(8,128)(2,1)S(1)} collective-permute-done((bf16[64,640]{1,0:T(8,128)(2,1)S(1)}, bf16[64,640]{1,0:T(8,128)(2,1)S(1)}, u32[]{:S(2)}, u32[]{:S(2)}) %collective-permute-start.6) | collective-permute-done | bytes 81952 | tf_op jit(solution)/shard_map/ppermute | solution.py:371
  30.9 0.8 %collective-permute-done.7.refs_3_ = bf16[64,640]{1,0:T(8,128)(2,1)S(1)} collective-permute-done((bf16[64,640]{1,0:T(8,128)(2,1)S(1)}, bf16[64,640]{1,0:T(8,128)(2,1)S(1)}, u32[]{:S(2)}, u32[]{:S(2)}) %collective-permute-start.7) | collective-permute-done | bytes 81952 | tf_op jit(solution)/shard_map/ppermute | solution.py:371
  31.7 5.6 %kernel_gradient.1 = (f32[4,8,3968]{2,1,0:T(8,128)S(1)}, bf16[4,8,3968]{2,1,0:T(8,128)(2,1)S(1)}) custom-call(bf16[64,640]{1,0:T(8,128)(2,1)S(1)} %get-tuple-element.45.refs_0_, bf16[64,640]{1,0:T(8,128)(2,1)S(1)} %collective-permute-done.5.refs_1_, bf16[64,640]{1,0:T(8,128)(2,1)S(1)} %collective-permute-done.6.refs_2_, ...), custom_call_target="tpu_custom_call" | custom-call | flops 1811939328 | bytes 4194304 | tf_op jit(solution)/shard_map/kernel_gradient/pallas_call | solution.py:343
  37.3 0.1 collective-permute-start.9
  37.4 1.5 %collective-permute-done.9.other = bf16[4,8,3968]{2,1,0:T(8,128)(2,1)S(1)} collective-permute-done((bf16[4,8,3968]{2,1,0:T(8,128)(2,1)S(1)}, bf16[4,8,3968]{2,1,0:T(8,128)(2,1)S(1)}, u32[]{:S(2)}, u32[]{:S(2)}) %collective-permute-start.9) | collective-permute-done | bytes 253984 | tf_op jit(solution)/shard_map/ppermute | solution.py:371
  38.9 0.1 fold.1
  39.0 1.8 %collective-permute-start.10 = (bf16[8,3968]{1,0:T(8,128)(2,1)S(1)}, bf16[8,3968]{1,0:T(8,128)(2,1)S(1)}, u32[]{:S(2)}, u32[]{:S(2)}) collective-permute-start(bf16[8,3968]{1,0:T(8,128)(2,1)S(1)} %get-tuple-element.53), channel_id=1, source_target_pairs={{0,8},{8,0},{16,24},{24,16},{1,9},{9,1},{17,25},{25,17},{2,10},{10... | collective-permute-start | bytes 190472 | tf_op jit(solution)/shard_map/ppermute | solution.py:371
  40.8 2.6 %collective-permute-start.11 = (bf16[8,3968]{1,0:T(8,128)(2,1)S(1)}, bf16[8,3968]{1,0:T(8,128)(2,1)S(1)}, u32[]{:S(2)}, u32[]{:S(2)}) collective-permute-start(bf16[8,3968]{1,0:T(8,128)(2,1)S(1)} %get-tuple-element.54), channel_id=1, source_target_pairs={{0,16},{8,24},{16,0},{24,8},{1,17},{9,25},{17,1},{25,9},{2,18},{10... | collective-permute-start | bytes 190472 | tf_op jit(solution)/shard_map/ppermute | solution.py:371
  43.4 0.0 collective-permute-start.12
  43.4 2.7 %input_gradient.1 = bf16[8,64,192]{2,1,0:T(8,128)(2,1)} custom-call(bf16[10,80,192]{2,1,0:T(8,128)(2,1)S(1)} %get-tuple-element.44.gp, f32[8,64,128]{2,1,0:T(8,128)S(1)} %get-tuple-element.41.live, bf16[192,5184]{1,0:T(8,128)(2,1)S(1)} %bitcast.8), custom_call_target="tpu_custom_call" | custom-call | flops 1358954496 | bytes 4194304 | tf_op jit(solution)/shard_map/input_gradient/pallas_call | solution.py:343
  46.1 0.0 collective-permute-done.10.one
  46.1 2.1 %collective-permute-done.11.two = bf16[8,3968]{1,0:T(8,128)(2,1)S(1)} collective-permute-done((bf16[8,3968]{1,0:T(8,128)(2,1)S(1)}, bf16[8,3968]{1,0:T(8,128)(2,1)S(1)}, u32[]{:S(2)}, u32[]{:S(2)}) %collective-permute-start.11) | collective-permute-done | bytes 63520 | tf_op jit(solution)/shard_map/ppermute | solution.py:371
  48.2 1.3 %collective-permute-done.12.three = bf16[8,3968]{1,0:T(8,128)(2,1)S(1)} collective-permute-done((bf16[8,3968]{1,0:T(8,128)(2,1)S(1)}, bf16[8,3968]{1,0:T(8,128)(2,1)S(1)}, u32[]{:S(2)}, u32[]{:S(2)}) %collective-permute-start.12) | collective-permute-done | bytes 63520 | tf_op jit(solution)/shard_map/ppermute | solution.py:371
  49.6 0.8 %collective-permute-start.13 = (bf16[8,3968]{1,0:T(8,128)(2,1)S(1)}, bf16[8,3968]{1,0:T(8,128)(2,1)S(1)}, u32[]{:S(2)}, u32[]{:S(2)}) collective-permute-start(bf16[8,3968]{1,0:T(8,128)(2,1)S(1)} %plane_sum.1.mine), channel_id=1, source_target_pairs={{0,1},{1,0},{2,3},{3,2},{4,5},{5,4},{6,7},{7,6},{8,9},{9,8},{10,11... | collective-permute-start | bytes 190472 | tf_op jit(solution)/shard_map/ppermute | solution.py:371
  50.4 3.5 %collective-permute-done.13.other = bf16[8,3968]{1,0:T(8,128)(2,1)S(1)} collective-permute-done((bf16[8,3968]{1,0:T(8,128)(2,1)S(1)}, bf16[8,3968]{1,0:T(8,128)(2,1)S(1)}, u32[]{:S(2)}, u32[]{:S(2)}) %collective-permute-start.13) | collective-permute-done | bytes 63520 | tf_op jit(solution)/shard_map/ppermute | solution.py:371
  53.9 0.8 %join.1 = f32[12,5184]{1,0:T(8,128)} custom-call(bf16[8,3968]{1,0:T(8,128)(2,1)S(1)} %plane_sum.1.mine, bf16[8,3968]{1,0:T(8,128)(2,1)S(1)} %collective-permute-done.13.other), custom_call_target="tpu_custom_call" | custom-call | flops 41472 | bytes 580608 | tf_op jit(solution)/shard_map/join/pallas_call | solution.py:343
  (2 shorter events, 0.1 us)
Async XLA Ops:
  0.6 1.0 %copy-start.1 = (bf16[8,8,8,192]{3,2,1,0:T(8,128)(2,1)S(1)}, bf16[8,8,8,192]{3,2,1,0:T(8,128)(2,1)}, u32[]{:S(2)}) copy-start(bf16[8,8,8,192]{3,2,1,0:T(8,128)(2,1)} %param.7) | copy-start | bytes 589828
  0.6 0.9 %copy-start.2 = (s32[8,8,8]{2,1,0:T(8,128)S(1)}, s32[8,8,8]{2,1,0:T(8,128)}, u32[]{:S(2)}) copy-start(s32[8,8,8]{2,1,0:T(8,128)} %mask.1) | copy-start | bytes 6148
  0.7 1.0 %copy-start = (bf16[8,8,8,192]{3,2,1,0:T(8,128)(2,1)S(1)}, bf16[8,8,8,192]{3,2,1,0:T(8,128)(2,1)}, u32[]{:S(2)}) copy-start(bf16[8,8,8,192]{3,2,1,0:T(8,128)(2,1)} %param.4) | copy-start | bytes 589828
  0.7 8.5 %copy-start.3 = (bf16[5184,192]{0,1:T(8,128)(2,1)S(1)}, bf16[5184,192]{0,1:T(8,128)(2,1)}, u32[]{:S(2)}) copy-start(bf16[5184,192]{0,1:T(8,128)(2,1)} %param.5) | copy-start | bytes 5971972
  1.9 8.0 %collective-permute-start = (bf16[3,64,192]{2,1,0:T(8,128)(2,1)S(1)}, bf16[3,64,192]{2,1,0:T(8,128)(2,1)S(1)}, u32[]{:S(2)}, u32[]{:S(2)}) collective-permute-start(bf16[3,64,192]{2,1,0:T(8,128)(2,1)S(1)} %get-tuple-element.35), channel_id=1, source_target_pairs={{0,2},{2,0},{4,6},{6,4},{8,10},{10,8},{12,14},{14,12},{16,18},{18,... | collective-permute-start | bytes 221192 | tf_op jit(solution)/shard_map/ppermute | solution.py:371
  2.4 7.5 %collective-permute-start.1 = (bf16[3,64,192]{2,1,0:T(8,128)(2,1)S(1)}, bf16[3,64,192]{2,1,0:T(8,128)(2,1)S(1)}, u32[]{:S(2)}, u32[]{:S(2)}) collective-permute-start(bf16[3,64,192]{2,1,0:T(8,128)(2,1)S(1)} %get-tuple-element.36), channel_id=1, source_target_pairs={{0,0},{2,4},{4,2},{6,8},{8,6},{10,12},{12,10},{14,16},{16,14},{18,... | collective-permute-start | bytes 221192 | tf_op jit(solution)/shard_map/ppermute | solution.py:396
  3.2 17.2 %collective-permute-start.4 = (bf16[12,64,128]{2,1,0:T(8,128)(2,1)S(1)}, bf16[12,64,128]{2,1,0:T(8,128)(2,1)S(1)}, u32[]{:S(2)}, u32[]{:S(2)}) collective-permute-start(bf16[12,64,128]{2,1,0:T(8,128)(2,1)S(1)} %get-tuple-element.50.refs_4_), channel_id=1, source_target_pairs={{0,4},{1,5},{2,6},{3,7},{4,0},{5,1},{6,2},{7,3},{8,12},{9,13},{10,... | collective-permute-start | bytes 589832 | tf_op jit(solution)/shard_map/ppermute | solution.py:371
  7.0 13.4 %collective-permute-start.2 = (bf16[14,64,128]{2,1,0:T(8,128)(2,1)S(1)}, bf16[14,64,128]{2,1,0:T(8,128)(2,1)S(1)}, u32[]{:S(2)}, u32[]{:S(2)}) collective-permute-start(bf16[14,64,128]{2,1,0:T(8,128)(2,1)S(1)} %get-tuple-element.39), channel_id=1, source_target_pairs={{0,1},{1,0},{2,3},{3,2},{4,5},{5,4},{6,7},{7,6},{8,9},{9,8},{10,11... | collective-permute-start | bytes 688136 | tf_op jit(solution)/shard_map/ppermute | solution.py:371
  10.0 10.4 %collective-permute-start.3 = (bf16[80,192]{1,0:T(8,128)(2,1)S(1)}, bf16[80,192]{1,0:T(8,128)(2,1)S(1)}, u32[]{:S(2)}, u32[]{:S(2)}) collective-permute-start(bf16[80,192]{1,0:T(8,128)(2,1)S(1)} %corner.1), channel_id=1, source_target_pairs={{0,1},{1,0},{2,3},{3,2},{4,5},{5,4},{6,7},{7,6},{8,9},{9,8},{10,11... | collective-permute-start | bytes 92168 | tf_op jit(solution)/shard_map/ppermute | solution.py:371
  10.0 17.5 %collective-permute-start.8 = (bf16[12,64,128]{2,1,0:T(8,128)(2,1)S(1)}, bf16[12,64,128]{2,1,0:T(8,128)(2,1)S(1)}, u32[]{:S(2)}, u32[]{:S(2)}) collective-permute-start(bf16[12,64,128]{2,1,0:T(8,128)(2,1)S(1)} %get-tuple-element.50.refs_4_), channel_id=1, source_target_pairs={{0,5},{1,4},{2,7},{3,6},{4,1},{5,0},{6,3},{7,2},{8,13},{9,12},{10,... | collective-permute-start | bytes 589832 | tf_op jit(solution)/shard_map/ppermute | solution.py:371
  24.0 4.6 %collective-permute-start.5 = (bf16[64,640]{1,0:T(8,128)(2,1)S(1)}, bf16[64,640]{1,0:T(8,128)(2,1)S(1)}, u32[]{:S(2)}, u32[]{:S(2)}) collective-permute-start(bf16[64,640]{1,0:T(8,128)(2,1)S(1)} %get-tuple-element.46), channel_id=1, source_target_pairs={{0,1},{1,0},{2,3},{3,2},{4,5},{5,4},{6,7},{7,6},{8,9},{9,8},{10,11... | collective-permute-start | bytes 245768 | tf_op jit(solution)/shard_map/ppermute | solution.py:371
  26.1 4.8 %collective-permute-start.6 = (bf16[64,640]{1,0:T(8,128)(2,1)S(1)}, bf16[64,640]{1,0:T(8,128)(2,1)S(1)}, u32[]{:S(2)}, u32[]{:S(2)}) collective-permute-start(bf16[64,640]{1,0:T(8,128)(2,1)S(1)} %get-tuple-element.47), channel_id=1, source_target_pairs={{0,4},{1,5},{2,6},{3,7},{4,0},{5,1},{6,2},{7,3},{8,12},{9,13},{10,... | collective-permute-start | bytes 245768 | tf_op jit(solution)/shard_map/ppermute | solution.py:371
  26.2 5.5 %collective-permute-start.7 = (bf16[64,640]{1,0:T(8,128)(2,1)S(1)}, bf16[64,640]{1,0:T(8,128)(2,1)S(1)}, u32[]{:S(2)}, u32[]{:S(2)}) collective-permute-start(bf16[64,640]{1,0:T(8,128)(2,1)S(1)} %get-tuple-element.48), channel_id=1, source_target_pairs={{0,5},{1,4},{2,7},{3,6},{4,1},{5,0},{6,3},{7,2},{8,13},{9,12},{10,... | collective-permute-start | bytes 245768 | tf_op jit(solution)/shard_map/ppermute | solution.py:371
  37.3 1.6 %collective-permute-start.9 = (bf16[4,8,3968]{2,1,0:T(8,128)(2,1)S(1)}, bf16[4,8,3968]{2,1,0:T(8,128)(2,1)S(1)}, u32[]{:S(2)}, u32[]{:S(2)}) collective-permute-start(bf16[4,8,3968]{2,1,0:T(8,128)(2,1)S(1)} %get-tuple-element.52), channel_id=1, source_target_pairs={{0,2},{1,3},{2,0},{3,1},{4,6},{5,7},{6,4},{7,5},{8,10},{9,11},{10,... | collective-permute-start | bytes 761864 | tf_op jit(solution)/shard_map/ppermute | solution.py:371
  39.0 7.1 %collective-permute-start.10 = (bf16[8,3968]{1,0:T(8,128)(2,1)S(1)}, bf16[8,3968]{1,0:T(8,128)(2,1)S(1)}, u32[]{:S(2)}, u32[]{:S(2)}) collective-permute-start(bf16[8,3968]{1,0:T(8,128)(2,1)S(1)} %get-tuple-element.53), channel_id=1, source_target_pairs={{0,8},{8,0},{16,24},{24,16},{1,9},{9,1},{17,25},{25,17},{2,10},{10... | collective-permute-start | bytes 190472 | tf_op jit(solution)/shard_map/ppermute | solution.py:371
  40.8 7.4 %collective-permute-start.11 = (bf16[8,3968]{1,0:T(8,128)(2,1)S(1)}, bf16[8,3968]{1,0:T(8,128)(2,1)S(1)}, u32[]{:S(2)}, u32[]{:S(2)}) collective-permute-start(bf16[8,3968]{1,0:T(8,128)(2,1)S(1)} %get-tuple-element.54), channel_id=1, source_target_pairs={{0,16},{8,24},{16,0},{24,8},{1,17},{9,25},{17,1},{25,9},{2,18},{10... | collective-permute-start | bytes 190472 | tf_op jit(solution)/shard_map/ppermute | solution.py:371
  43.4 6.1 %collective-permute-start.12 = (bf16[8,3968]{1,0:T(8,128)(2,1)S(1)}, bf16[8,3968]{1,0:T(8,128)(2,1)S(1)}, u32[]{:S(2)}, u32[]{:S(2)}) collective-permute-start(bf16[8,3968]{1,0:T(8,128)(2,1)S(1)} %get-tuple-element.55), channel_id=1, source_target_pairs={{0,24},{8,16},{16,8},{24,0},{1,25},{9,17},{17,9},{25,1},{2,26},{10... | collective-permute-start | bytes 190472 | tf_op jit(solution)/shard_map/ppermute | solution.py:371
  49.6 4.3 %collective-permute-start.13 = (bf16[8,3968]{1,0:T(8,128)(2,1)S(1)}, bf16[8,3968]{1,0:T(8,128)(2,1)S(1)}, u32[]{:S(2)}, u32[]{:S(2)}) collective-permute-start(bf16[8,3968]{1,0:T(8,128)(2,1)S(1)} %plane_sum.1.mine), channel_id=1, source_target_pairs={{0,1},{1,0},{2,3},{3,2},{4,5},{5,4},{6,7},{7,6},{8,9},{9,8},{10,11... | collective-permute-start | bytes 190472 | tf_op jit(solution)/shard_map/ppermute | solution.py:371

commit v9 on v8

--- a/solution.py
+++ b/solution.py
@@ -36,10 +36,11 @@
     column = lax.broadcasted_iota(jnp.int32, out_ref.shape, 1)
     per = out_ref.shape[1] // (planes * QUAD)
     share = per // SIDES
-    quad, side = index // (SIDES * planes * 8), index // (planes * 8) % SIDES
-    plane, row = index // 8 % planes, index % 8
+    group = planes * share
+    quad, side = index // (SIDES * group), index // group % SIDES
+    plane, row = index // share % planes, index % share
     channel = per * (QUAD * plane + quad) + share * side + row
-    out_ref[...] = jnp.where((row < share) & (channel == column), 1.0, 0.0).astype(jnp.bfloat16)
+    out_ref[...] = jnp.where(channel == column, 1.0, 0.0).astype(jnp.bfloat16)
 
 
 def dense(total):
@@ -84,13 +85,22 @@
         ref[2:3] = cot_ref[pl.ds(upper * (width - 1), 1)]
 
 
-def pack_kernel(masked, cot, packed_ref, across_ref):
+def rows_of_128(masked, out_ref):
+    width = masked.shape[0]
+    half = width // 2
+    rest = jnp.concatenate([masked[:half, :, 128:], masked[half:, :, 128:]], axis=2)
+    out_ref[:width] = masked[:, :, :128]
+    out_ref[width : width + half] = rest
+
+
+def pack_kernel(masked, after, packed_ref):
+    rows_of_128(masked, packed_ref)
+
+
+def across_kernel(masked, cot, across_ref):
     width, rows, channels = masked.shape
-    half = width // 2
-    packed_ref[:width] = masked[:, :, :128]
-    packed_ref[width:] = jnp.concatenate([masked[:half, :, 128:], masked[half:, :, 128:]], axis=2)
-    count = packed_ref.shape[0]
-    across_ref[:count] = packed_ref[...]
+    rows_of_128(masked, across_ref)
+    count = across_ref.shape[0] - 2
     ahead = position()[3] == 0
     grown = cot[...].astype(jnp.float32)
     strip = jnp.where(ahead, grown[:, rows - DEPTH :], grown[:, :DEPTH])
@@ -202,12 +212,11 @@
         (((1,), (1,)), ((), ())),
         preferred_element_type=f32,
     )
-    slices[...] = turned.reshape(slices.shape).astype(jnp.bfloat16)
-    group = slices.shape[1]
+    slices[...] = turned.reshape(slices.shape)
     chip = me - lax.rem(quad, 2) * SIDES
     for distance, ref in zip(CHIPS, slice_refs):
-        ref[:group] = slices[chip ^ distance]
-        ref[group:] = slices[(chip ^ distance) + SIDES]
+        both = [slices[chip ^ distance], slices[(chip ^ distance) + SIDES]]
+        ref[...] = jnp.concatenate(both, axis=0).astype(jnp.bfloat16)
 
 
 def input_kernel(gp, live, turned, out_ref, cols, weight):
@@ -286,7 +295,6 @@
                 rest = stage[block, sided, per + x % (per // 2)]
                 masked[block, x, at_rows, :128] = stage[block, sided, x]
                 masked[block, x, at_rows, 128:] = rest[:, shift : shift + 64]
-    _, planes, eight, _ = part.shape
     for a in range(3):
         got = jnp.zeros((cols.shape[0], channels), f32)
         for block in range(blocks):
@@ -296,26 +304,29 @@
                 masked[block].reshape(per * lane, channels),
                 preferred_element_type=f32,
             )
-        got = got.reshape(9, 2, planes, eight, channels)
-        for core in range(2):
-            for to in range(planes):
-                part[core, to, :, a * 9 * channels : (a + 1) * 9 * channels] = jnp.concatenate(
-                    [got[tap, core, to] for tap in range(9)], axis=1
-                )
+        got = got.reshape(9, group, channels)
+        part[:, a * 9 * channels : (a + 1) * 9 * channels] = jnp.concatenate(
+            [got[tap] for tap in range(9)], axis=1
+        )
     core = lax.rem(quad, 2)
-    total = 27 * channels
-    part[:, :, :, total:] = jnp.zeros((2, planes, eight, part.shape[3] - total), f32)
+    half = group // 2
+    keep_ref[...] = part[pl.ds(pl.multiple_of(core * half, 8), half)]
+    send_ref[...] = part[pl.ds(pl.multiple_of((1 - core) * half, 8), half)].astype(jnp.bfloat16)
+
+
+def fold_kernel(keep, other, own_ref, *refs):
+    *send_refs, both, rows = refs
+    planes, eight, _ = rows.shape
+    count, total = keep.shape
+    share = count // planes
+    both[:count, :total] = keep[...] + other[...].astype(jnp.float32)
+    both[:, total:] = jnp.zeros((both.shape[0], both.shape[1] - total), jnp.float32)
     for to in range(planes):
-        keep_ref[to] = fold_rows(part[core, to], total)
-        send_ref[to] = fold_rows(part[1 - core, to], total).astype(jnp.bfloat16)
-
-
-def fold_kernel(keep, other, own_ref, *send_refs):
+        rows[to] = fold_rows(both[share * to : share * to + eight, :], total)
     plane = position()[0]
-    own_ref[...] = keep[plane] + other[plane].astype(jnp.float32)
+    own_ref[...] = rows[plane]
     for distance, ref in enumerate(send_refs, 1):
-        to = plane ^ distance
-        ref[...] = (keep[to] + other[to].astype(jnp.float32)).astype(jnp.bfloat16)
+        ref[...] = rows[plane ^ distance].astype(jnp.bfloat16)
 
 
 def sum_kernel(scale, own, one, two, three, out_ref):
@@ -365,7 +376,8 @@
     total = 27 * channels
     halo = 2 * DEPTH
     span = (width + 2) * rows
-    group = planes * 8
+    share = channels // count // SIDES
+    group = planes * share
 
     def swap(piece, axes, distance, size):
         return lax.ppermute(piece, axes, [(i, i ^ distance) for i in range(size)])
@@ -398,33 +410,35 @@
         turn_kernel, "turn", 8, 1 << 34, 4 << 20, array((total, channels), bf16)
     )(weight.T)
     slabs = width * channels // 128
-    packed, across = call(
-        pack_kernel, "pack", 4, 1 << 16, 1 << 19,
-        (array((slabs, rows, 128), bf16), array((slabs + 2, rows, 128), bf16)),
+    across = call(
+        across_kernel, "across", 4, 1 << 16, 1 << 19, array((slabs + 2, rows, 128), bf16)
     )(masked, cot)
     across = in_plane(across, CHIPS[1])
-    bricks = [packed, across, in_plane(packed, CHIPS[2]), None]
-    packed, near, far, weight_rows = lax.optimization_barrier((packed, near, far, weight_rows))
+    near, far, weight_rows = lax.optimization_barrier((near, far, weight_rows))
     corner = call(
         corner_kernel, "corner", 4, 1 << 16, 1 << 18,
         array((4 * halo + 2 * DEPTH, channels), bf16),
         (pltpu.VMEM((2,) + slab.shape, bf16),),
     )(near, far)
-    corner, bricks[2] = lax.optimization_barrier((in_plane(corner, 1), bricks[2]))
-    bricks[3] = in_plane(packed, CHIPS[3])
+    packed = call(
+        pack_kernel, "pack", 4, 1 << 16, 1 << 19, array((slabs, rows, 128), bf16), (),
+        [vmem, pl.BlockSpec(memory_space=pl.ANY)],
+    )(masked, corner)
+    corner = in_plane(corner, 1)
+    bricks = [packed, across] + [in_plane(packed, distance) for distance in CHIPS[2:]]
 
     mid = rows + 2 * DEPTH
     act, gp, *slices = call(
-        forward_kernel, "forward", 28, 800 * 5184 * 256, 1 << 20,
+        forward_kernel, "forward", 28, 1 << 32, 1 << 20,
         (brick, array((width + 2, mid, channels), bf16))
         + (array((2 * group, span), bf16),) * len(CHIPS),
         (
             pltpu.VMEM((width + 4, rows + 2 * halo, channels), f32),
             pltpu.VMEM((2,) + slab.shape, bf16),
             pltpu.VMEM((width + 4, mid, 9 * channels), bf16),
-            pltpu.VMEM((MEMBERS, group, span), bf16),
+            pltpu.VMEM((MEMBERS, group, span), f32),
         ),
-    )(masked, cot, near, far, bricks[1], corner, live, weight_rows, pick)
+    )(masked, cot, near, far, across, corner, live, weight_rows, pick)
     slices = [slices[0]] + [in_plane(part, d) for part, d in zip(slices[1:], CHIPS[1:])]
 
     grad_input = call(
@@ -439,12 +453,12 @@
     chips = len(CHIPS)
     lanes = dense(total)[0]
     keep, fold = call(
-        kernel_grad_kernel, "kernel_gradient", 28, 2 * 576 * 3 * 2048 * 256, 4 << 20,
-        (array((planes, 8, lanes), f32), array((planes, 8, lanes), bf16)),
+        kernel_grad_kernel, "kernel_gradient", 28, 2 * 432 * 3 * 2048 * 256, 4 << 20,
+        (array((group, total), f32), array((group, total), bf16)),
         (
             pltpu.VMEM((blocks, SIDES, 2 * group, span), bf16),
             pltpu.VMEM((9 * 2 * group, blocks * (width + 2) * SIDES * rows), bf16),
-            pltpu.VMEM((2, planes, 8, sum(dense(total))), f32),
+            pltpu.VMEM((2 * group, total), f32),
             pltpu.VMEM((blocks, SIDES) + packed.shape, bf16),
             pltpu.VMEM((blocks, width, SIDES * rows, channels), bf16),
             pltpu.SemaphoreType.DMA((chips,)),
@@ -454,6 +468,10 @@
     own, *sends = call(
         fold_kernel, "fold", 8, 8 * total * 4, 8 * total * 40,
         (array((8, lanes), f32),) + (array((8, lanes), bf16),) * (planes - 1),
+        (
+            pltpu.VMEM((group + 8, sum(dense(total))), f32),
+            pltpu.VMEM((planes, 8, lanes), f32),
+        ),
     )(keep, in_plane(fold, 2))
     got = [swap(sent, "depth", d, planes) for d, sent in enumerate(sends, 1)]
     grad_input, *got = lax.optimization_barrier((grad_input, *got))

time: 54.9 us -> 53 us (0.965)
  waiting for transfers between devices: 20.3 us -> 13.1 us
  starting transfers between devices: 18.8 us -> 24.7 us
  Pallas kernels: 14 us -> 13.4 us
    ppermute x13, waiting for transfers between devices: 20.3 us -> 13.1 us  [swap(): return lax.ppermute(piece, axes, [(i, i ^ distance) for i in range(size)])]
    ppermute x13, starting transfers between devices: 18.1 us -> 24 us  [swap(): return lax.ppermute(piece, axes, [(i, i ^ distance) for i in range(size)])]
    pallas_call x11 -> x12, Pallas kernels: 14 us -> 13.4 us  [run(): pl.pallas_call(body, out_shape=out_shape, in_specs=in_specs or [spec] * l...]
  transfers between devices with their start and end apart: 14 -> 14, of which waited for: 8 -> 5; matrix products, arithmetic and copies ran while one was open for 0% -> 0% of each run, Pallas kernels for 13% -> 14%
where the time goes in v9:
time: 53 us; the launch traced here: 52.8 us
  starting transfers between devices  24.7 us (47%)
  Pallas kernels  13.4 us (25%)
  waiting for transfers between devices  13.1 us (25%)
  local copies, waits for them, and re-layouts  0.86 us (2%)
  between operations  0.77 us (1%)
    ppermute x13, starting transfers between devices, swap(): return lax.ppermute(piece, axes, [(i, i ^ distance) for i in range(size)])  24 us
    pallas_call x12, Pallas kernels, run(): pl.pallas_call(body, out_shape=out_shape, in_specs=in_specs or [spec] * l...  13.4 us
    ppermute x13, waiting for transfers between devices, swap(): return lax.ppermute(piece, axes, [(i, i ^ distance) for i in range(size)])  13.1 us
  transfers between devices with their start and end apart: 14, of which 5 were waited for; matrix products, arithmetic and copies ran while one was open for 0% of the time, Pallas kernels for 14%

profile of v9, /device:TPU:0, one launch (start us, length us, event | category | flops | bytes accessed | tf_op | source)
XLA Modules:
  0.0 52.8 jit_solution(1253859865749396424)
XLA Ops:
  0.6 0.0 copy-start.1
  0.6 0.0 copy-start.2
  0.7 0.0 copy-start
  0.7 0.0 copy-start.3
  0.7 0.2 pick.1.first
  0.8 0.7 %copy-done.1 = bf16[8,8,8,192]{3,2,1,0:T(8,128)(2,1)S(1)} copy-done((bf16[8,8,8,192]{3,2,1,0:T(8,128)(2,1)S(1)}, bf16[8,8,8,192]{3,2,1,0:T(8,128)(2,1)}, u32[]{:S(2)}) %copy-start.1) | copy-done | bytes 196632
  1.6 0.0 copy-done.2
  1.6 0.1 copy-done
  1.7 0.2 prepare.1
  1.9 0.5 collective-permute-start
  2.4 0.7 %collective-permute-start.1 = (bf16[3,64,192]{2,1,0:T(8,128)(2,1)S(1)}, bf16[3,64,192]{2,1,0:T(8,128)(2,1)S(1)}, u32[]{:S(2)}, u32[]{:S(2)}) collective-permute-start(bf16[3,64,192]{2,1,0:T(8,128)(2,1)S(1)} %get-tuple-element.30), channel_id=1, source_target_pairs={{0,0},{2,4},{4,2},{6,8},{8,6},{10,12},{12,10},{14,16},{16,14},{18,... | collective-permute-start | bytes 221192 | tf_op jit(solution)/shard_map/ppermute | solution.py:408
  3.1 0.1 across.1
  3.1 2.6 %collective-permute-start.2 = (bf16[14,64,128]{2,1,0:T(8,128)(2,1)S(1)}, bf16[14,64,128]{2,1,0:T(8,128)(2,1)S(1)}, u32[]{:S(2)}, u32[]{:S(2)}) collective-permute-start(bf16[14,64,128]{2,1,0:T(8,128)(2,1)S(1)} %across.1), channel_id=1, source_target_pairs={{0,1},{1,0},{2,3},{3,2},{4,5},{5,4},{6,7},{7,6},{8,9},{9,8},{10,11... | collective-permute-start | bytes 688136 | tf_op jit(solution)/shard_map/ppermute | solution.py:383
  5.8 0.0 copy-done.3
  5.8 0.8 %turn.1.weight = bf16[5184,192]{1,0:T(8,128)(2,1)S(1)} custom-call(bf16[192,5184]{1,0:T(8,128)(2,1)S(1)} %bitcast.7), custom_call_target="tpu_custom_call" | custom-call | flops 17179869184 | bytes 4194304 | tf_op jit(solution)/shard_map/turn/pallas_call | solution.py:354
  6.5 0.0 collective-permute-done.near
  6.5 0.0 collective-permute-done.1.far
  6.6 0.1 collective-permute-start.3
  6.7 0.1 pack.1.refs_4_
  6.8 5.8 %collective-permute-start.8 = (bf16[12,64,128]{2,1,0:T(8,128)(2,1)S(1)}, bf16[12,64,128]{2,1,0:T(8,128)(2,1)S(1)}, u32[]{:S(2)}, u32[]{:S(2)}) collective-permute-start(bf16[12,64,128]{2,1,0:T(8,128)(2,1)S(1)} %pack.1.refs_4_), channel_id=1, source_target_pairs={{0,5},{1,4},{2,7},{3,6},{4,1},{5,0},{6,3},{7,2},{8,13},{9,12},{10,... | collective-permute-start | bytes 589832 | tf_op jit(solution)/shard_map/ppermute | solution.py:383
  12.6 0.1 collective-permute-start.7
  12.7 0.0 collective-permute-done.3.corner
  12.7 0.0 collective-permute-done.2.across.refs_5_
  12.7 3.6 %forward.1 = (bf16[8,64,192]{2,1,0:T(8,128)(2,1)}, bf16[10,80,192]{2,1,0:T(8,128)(2,1)S(1)}, bf16[48,640]{1,0:T(8,128)(2,1)S(1)}, bf16[48,640]{1,0:T(8,128)(2,1)...) custom-call(bf16[8,64,192]{2,1,0:T(8,128)(2,1)S(1)} %get-tuple-element.27.masked, ...), custom_call_target="tpu_custom_call" | custom-call | flops 4294967296 | bytes 1048576 | tf_op jit(solution)/shard_map/forward/pallas_call | solution.py:354
  16.3 1.4 %collective-permute-start.4 = (bf16[48,640]{1,0:T(8,128)(2,1)S(1)}, bf16[48,640]{1,0:T(8,128)(2,1)S(1)}, u32[]{:S(2)}, u32[]{:S(2)}) collective-permute-start(bf16[48,640]{1,0:T(8,128)(2,1)S(1)} %get-tuple-element.38), channel_id=1, source_target_pairs={{0,1},{1,0},{2,3},{3,2},{4,5},{5,4},{6,7},{7,6},{8,9},{9,8},{10,11... | collective-permute-start | bytes 184328 | tf_op jit(solution)/shard_map/ppermute | solution.py:383
  17.7 8.5 %collective-permute-start.5 = (bf16[48,640]{1,0:T(8,128)(2,1)S(1)}, bf16[48,640]{1,0:T(8,128)(2,1)S(1)}, u32[]{:S(2)}, u32[]{:S(2)}) collective-permute-start(bf16[48,640]{1,0:T(8,128)(2,1)S(1)} %get-tuple-element.39), channel_id=1, source_target_pairs={{0,4},{1,5},{2,6},{3,7},{4,0},{5,1},{6,2},{7,3},{8,12},{9,13},{10,... | collective-permute-start | bytes 184328 | tf_op jit(solution)/shard_map/ppermute | solution.py:383
  26.2 0.0 collective-permute-start.6
  26.2 0.0 collective-permute-done.8.refs_7_
  26.2 0.0 collective-permute-done.7.refs_6_
  26.3 0.0 collective-permute-done.4.refs_1_
  26.3 2.5 %collective-permute-done.5.refs_2_ = bf16[48,640]{1,0:T(8,128)(2,1)S(1)} collective-permute-done((bf16[48,640]{1,0:T(8,128)(2,1)S(1)}, bf16[48,640]{1,0:T(8,128)(2,1)S(1)}, u32[]{:S(2)}, u32[]{:S(2)}) %collective-permute-start.5) | collective-permute-done | bytes 61472 | tf_op jit(solution)/shard_map/ppermute | solution.py:383
  28.8 2.6 %collective-permute-done.6.refs_3_ = bf16[48,640]{1,0:T(8,128)(2,1)S(1)} collective-permute-done((bf16[48,640]{1,0:T(8,128)(2,1)S(1)}, bf16[48,640]{1,0:T(8,128)(2,1)S(1)}, u32[]{:S(2)}, u32[]{:S(2)}) %collective-permute-start.6) | collective-permute-done | bytes 61472 | tf_op jit(solution)/shard_map/ppermute | solution.py:383
  31.4 4.8 %kernel_gradient.1 = (f32[24,5184]{1,0:T(8,128)S(1)}, bf16[24,5184]{1,0:T(8,128)(2,1)S(1)}) custom-call(bf16[48,640]{1,0:T(8,128)(2,1)S(1)} %get-tuple-element.37.refs_0_, bf16[48,640]{1,0:T(8,128)(2,1)S(1)} %collective-permute-done.4.refs_1_, bf16[48,640]{1,0:T(8,128)(2,1)S(1)} %collective-permute-done.5.refs_2_, ...), custom_call_target="tpu_custom_call" | custom-call | flops 1358954496 | bytes 4194304 | tf_op jit(solution)/shard_map/kernel_gradient/pallas_call | solution.py:354
  36.1 0.1 collective-permute-start.9
  36.2 1.5 %collective-permute-done.9.other = bf16[24,5184]{1,0:T(8,128)(2,1)S(1)} collective-permute-done((bf16[24,5184]{1,0:T(8,128)(2,1)S(1)}, bf16[24,5184]{1,0:T(8,128)(2,1)S(1)}, u32[]{:S(2)}, u32[]{:S(2)}) %collective-permute-start.9) | collective-permute-done | bytes 248864 | tf_op jit(solution)/shard_map/ppermute | solution.py:383
  37.7 0.2 fold.1
  37.9 1.6 %collective-permute-start.10 = (bf16[8,3968]{1,0:T(8,128)(2,1)S(1)}, bf16[8,3968]{1,0:T(8,128)(2,1)S(1)}, u32[]{:S(2)}, u32[]{:S(2)}) collective-permute-start(bf16[8,3968]{1,0:T(8,128)(2,1)S(1)} %get-tuple-element.43), channel_id=1, source_target_pairs={{0,8},{8,0},{16,24},{24,16},{1,9},{9,1},{17,25},{25,17},{2,10},{10... | collective-permute-start | bytes 190472 | tf_op jit(solution)/shard_map/ppermute | solution.py:383
  39.6 1.1 %collective-permute-start.11 = (bf16[8,3968]{1,0:T(8,128)(2,1)S(1)}, bf16[8,3968]{1,0:T(8,128)(2,1)S(1)}, u32[]{:S(2)}, u32[]{:S(2)}) collective-permute-start(bf16[8,3968]{1,0:T(8,128)(2,1)S(1)} %get-tuple-element.44), channel_id=1, source_target_pairs={{0,16},{8,24},{16,0},{24,8},{1,17},{9,25},{17,1},{25,9},{2,18},{10... | collective-permute-start | bytes 190472 | tf_op jit(solution)/shard_map/ppermute | solution.py:383
  40.7 1.7 %collective-permute-start.12 = (bf16[8,3968]{1,0:T(8,128)(2,1)S(1)}, bf16[8,3968]{1,0:T(8,128)(2,1)S(1)}, u32[]{:S(2)}, u32[]{:S(2)}) collective-permute-start(bf16[8,3968]{1,0:T(8,128)(2,1)S(1)} %get-tuple-element.45), channel_id=1, source_target_pairs={{0,24},{8,16},{16,8},{24,0},{1,25},{9,17},{17,9},{25,1},{2,26},{10... | collective-permute-start | bytes 190472 | tf_op jit(solution)/shard_map/ppermute | solution.py:383
  42.4 2.7 %input_gradient.1 = bf16[8,64,192]{2,1,0:T(8,128)(2,1)} custom-call(bf16[10,80,192]{2,1,0:T(8,128)(2,1)S(1)} %get-tuple-element.36.gp, f32[8,64,128]{2,1,0:T(8,128)S(1)} %get-tuple-element.33.live, bf16[192,5184]{1,0:T(8,128)(2,1)S(1)} %bitcast.8), custom_call_target="tpu_custom_call" | custom-call | flops 1358954496 | bytes 4194304 | tf_op jit(solution)/shard_map/input_gradient/pallas_call | solution.py:354
  45.0 0.0 collective-permute-done.10.one
  45.0 2.6 %collective-permute-done.11.two = bf16[8,3968]{1,0:T(8,128)(2,1)S(1)} collective-permute-done((bf16[8,3968]{1,0:T(8,128)(2,1)S(1)}, bf16[8,3968]{1,0:T(8,128)(2,1)S(1)}, u32[]{:S(2)}, u32[]{:S(2)}) %collective-permute-start.11) | collective-permute-done | bytes 63520 | tf_op jit(solution)/shard_map/ppermute | solution.py:383
  47.6 0.0 collective-permute-done.12.three
  47.7 0.5 collective-permute-start.13
  48.2 3.8 %collective-permute-done.13.other = bf16[8,3968]{1,0:T(8,128)(2,1)S(1)} collective-permute-done((bf16[8,3968]{1,0:T(8,128)(2,1)S(1)}, bf16[8,3968]{1,0:T(8,128)(2,1)S(1)}, u32[]{:S(2)}, u32[]{:S(2)}) %collective-permute-start.13) | collective-permute-done | bytes 63520 | tf_op jit(solution)/shard_map/ppermute | solution.py:383
  52.0 0.8 %join.1 = f32[12,5184]{1,0:T(8,128)} custom-call(bf16[8,3968]{1,0:T(8,128)(2,1)S(1)} %plane_sum.1.mine, bf16[8,3968]{1,0:T(8,128)(2,1)S(1)} %collective-permute-done.13.other), custom_call_target="tpu_custom_call" | custom-call | flops 41472 | bytes 580608 | tf_op jit(solution)/shard_map/join/pallas_call | solution.py:354
  (2 shorter events, 0.1 us)
Async XLA Ops:
  0.6 1.0 %copy-start.1 = (bf16[8,8,8,192]{3,2,1,0:T(8,128)(2,1)S(1)}, bf16[8,8,8,192]{3,2,1,0:T(8,128)(2,1)}, u32[]{:S(2)}) copy-start(bf16[8,8,8,192]{3,2,1,0:T(8,128)(2,1)} %param.7) | copy-start | bytes 589828
  0.6 0.9 %copy-start.2 = (s32[8,8,8]{2,1,0:T(8,128)S(1)}, s32[8,8,8]{2,1,0:T(8,128)}, u32[]{:S(2)}) copy-start(s32[8,8,8]{2,1,0:T(8,128)} %mask.1) | copy-start | bytes 6148
  0.7 1.0 %copy-start = (bf16[8,8,8,192]{3,2,1,0:T(8,128)(2,1)S(1)}, bf16[8,8,8,192]{3,2,1,0:T(8,128)(2,1)}, u32[]{:S(2)}) copy-start(bf16[8,8,8,192]{3,2,1,0:T(8,128)(2,1)} %param.4) | copy-start | bytes 589828
  0.7 5.1 %copy-start.3 = (bf16[5184,192]{0,1:T(8,128)(2,1)S(1)}, bf16[5184,192]{0,1:T(8,128)(2,1)}, u32[]{:S(2)}) copy-start(bf16[5184,192]{0,1:T(8,128)(2,1)} %param.5) | copy-start | bytes 5971972
  1.9 4.7 %collective-permute-start = (bf16[3,64,192]{2,1,0:T(8,128)(2,1)S(1)}, bf16[3,64,192]{2,1,0:T(8,128)(2,1)S(1)}, u32[]{:S(2)}, u32[]{:S(2)}) collective-permute-start(bf16[3,64,192]{2,1,0:T(8,128)(2,1)S(1)} %get-tuple-element.29), channel_id=1, source_target_pairs={{0,2},{2,0},{4,6},{6,4},{8,10},{10,8},{12,14},{14,12},{16,18},{18,... | collective-permute-start | bytes 221192 | tf_op jit(solution)/shard_map/ppermute | solution.py:383
  2.4 4.2 %collective-permute-start.1 = (bf16[3,64,192]{2,1,0:T(8,128)(2,1)S(1)}, bf16[3,64,192]{2,1,0:T(8,128)(2,1)S(1)}, u32[]{:S(2)}, u32[]{:S(2)}) collective-permute-start(bf16[3,64,192]{2,1,0:T(8,128)(2,1)S(1)} %get-tuple-element.30), channel_id=1, source_target_pairs={{0,0},{2,4},{4,2},{6,8},{8,6},{10,12},{12,10},{14,16},{16,14},{18,... | collective-permute-start | bytes 221192 | tf_op jit(solution)/shard_map/ppermute | solution.py:408
  3.1 9.5 %collective-permute-start.2 = (bf16[14,64,128]{2,1,0:T(8,128)(2,1)S(1)}, bf16[14,64,128]{2,1,0:T(8,128)(2,1)S(1)}, u32[]{:S(2)}, u32[]{:S(2)}) collective-permute-start(bf16[14,64,128]{2,1,0:T(8,128)(2,1)S(1)} %across.1), channel_id=1, source_target_pairs={{0,1},{1,0},{2,3},{3,2},{4,5},{5,4},{6,7},{7,6},{8,9},{9,8},{10,11... | collective-permute-start | bytes 688136 | tf_op jit(solution)/shard_map/ppermute | solution.py:383
  6.6 6.1 %collective-permute-start.3 = (bf16[80,192]{1,0:T(8,128)(2,1)S(1)}, bf16[80,192]{1,0:T(8,128)(2,1)S(1)}, u32[]{:S(2)}, u32[]{:S(2)}) collective-permute-start(bf16[80,192]{1,0:T(8,128)(2,1)S(1)} %corner.1.after), channel_id=1, source_target_pairs={{0,1},{1,0},{2,3},{3,2},{4,5},{5,4},{6,7},{7,6},{8,9},{9,8},{10,11... | collective-permute-start | bytes 92168 | tf_op jit(solution)/shard_map/ppermute | solution.py:383
  6.8 19.5 %collective-permute-start.8 = (bf16[12,64,128]{2,1,0:T(8,128)(2,1)S(1)}, bf16[12,64,128]{2,1,0:T(8,128)(2,1)S(1)}, u32[]{:S(2)}, u32[]{:S(2)}) collective-permute-start(bf16[12,64,128]{2,1,0:T(8,128)(2,1)S(1)} %pack.1.refs_4_), channel_id=1, source_target_pairs={{0,5},{1,4},{2,7},{3,6},{4,1},{5,0},{6,3},{7,2},{8,13},{9,12},{10,... | collective-permute-start | bytes 589832 | tf_op jit(solution)/shard_map/ppermute | solution.py:383
  12.6 13.7 %collective-permute-start.7 = (bf16[12,64,128]{2,1,0:T(8,128)(2,1)S(1)}, bf16[12,64,128]{2,1,0:T(8,128)(2,1)S(1)}, u32[]{:S(2)}, u32[]{:S(2)}) collective-permute-start(bf16[12,64,128]{2,1,0:T(8,128)(2,1)S(1)} %pack.1.refs_4_), channel_id=1, source_target_pairs={{0,4},{1,5},{2,6},{3,7},{4,0},{5,1},{6,2},{7,3},{8,12},{9,13},{10,... | collective-permute-start | bytes 589832 | tf_op jit(solution)/shard_map/ppermute | solution.py:383
  16.3 9.9 %collective-permute-start.4 = (bf16[48,640]{1,0:T(8,128)(2,1)S(1)}, bf16[48,640]{1,0:T(8,128)(2,1)S(1)}, u32[]{:S(2)}, u32[]{:S(2)}) collective-permute-start(bf16[48,640]{1,0:T(8,128)(2,1)S(1)} %get-tuple-element.38), channel_id=1, source_target_pairs={{0,1},{1,0},{2,3},{3,2},{4,5},{5,4},{6,7},{7,6},{8,9},{9,8},{10,11... | collective-permute-start | bytes 184328 | tf_op jit(solution)/shard_map/ppermute | solution.py:383
  17.7 11.1 %collective-permute-start.5 = (bf16[48,640]{1,0:T(8,128)(2,1)S(1)}, bf16[48,640]{1,0:T(8,128)(2,1)S(1)}, u32[]{:S(2)}, u32[]{:S(2)}) collective-permute-start(bf16[48,640]{1,0:T(8,128)(2,1)S(1)} %get-tuple-element.39), channel_id=1, source_target_pairs={{0,4},{1,5},{2,6},{3,7},{4,0},{5,1},{6,2},{7,3},{8,12},{9,13},{10,... | collective-permute-start | bytes 184328 | tf_op jit(solution)/shard_map/ppermute | solution.py:383
  26.2 5.1 %collective-permute-start.6 = (bf16[48,640]{1,0:T(8,128)(2,1)S(1)}, bf16[48,640]{1,0:T(8,128)(2,1)S(1)}, u32[]{:S(2)}, u32[]{:S(2)}) collective-permute-start(bf16[48,640]{1,0:T(8,128)(2,1)S(1)} %get-tuple-element.40), channel_id=1, source_target_pairs={{0,5},{1,4},{2,7},{3,6},{4,1},{5,0},{6,3},{7,2},{8,13},{9,12},{10,... | collective-permute-start | bytes 184328 | tf_op jit(solution)/shard_map/ppermute | solution.py:383
  36.1 1.6 %collective-permute-start.9 = (bf16[24,5184]{1,0:T(8,128)(2,1)S(1)}, bf16[24,5184]{1,0:T(8,128)(2,1)S(1)}, u32[]{:S(2)}, u32[]{:S(2)}) collective-permute-start(bf16[24,5184]{1,0:T(8,128)(2,1)S(1)} %get-tuple-element.42), channel_id=1, source_target_pairs={{0,2},{1,3},{2,0},{3,1},{4,6},{5,7},{6,4},{7,5},{8,10},{9,11},{10,... | collective-permute-start | bytes 746504 | tf_op jit(solution)/shard_map/ppermute | solution.py:383
  37.9 7.1 %collective-permute-start.10 = (bf16[8,3968]{1,0:T(8,128)(2,1)S(1)}, bf16[8,3968]{1,0:T(8,128)(2,1)S(1)}, u32[]{:S(2)}, u32[]{:S(2)}) collective-permute-start(bf16[8,3968]{1,0:T(8,128)(2,1)S(1)} %get-tuple-element.43), channel_id=1, source_target_pairs={{0,8},{8,0},{16,24},{24,16},{1,9},{9,1},{17,25},{25,17},{2,10},{10... | collective-permute-start | bytes 190472 | tf_op jit(solution)/shard_map/ppermute | solution.py:383
  39.6 8.1 %collective-permute-start.11 = (bf16[8,3968]{1,0:T(8,128)(2,1)S(1)}, bf16[8,3968]{1,0:T(8,128)(2,1)S(1)}, u32[]{:S(2)}, u32[]{:S(2)}) collective-permute-start(bf16[8,3968]{1,0:T(8,128)(2,1)S(1)} %get-tuple-element.44), channel_id=1, source_target_pairs={{0,16},{8,24},{16,0},{24,8},{1,17},{9,25},{17,1},{25,9},{2,18},{10... | collective-permute-start | bytes 190472 | tf_op jit(solution)/shard_map/ppermute | solution.py:383
  40.7 7.0 %collective-permute-start.12 = (bf16[8,3968]{1,0:T(8,128)(2,1)S(1)}, bf16[8,3968]{1,0:T(8,128)(2,1)S(1)}, u32[]{:S(2)}, u32[]{:S(2)}) collective-permute-start(bf16[8,3968]{1,0:T(8,128)(2,1)S(1)} %get-tuple-element.45), channel_id=1, source_target_pairs={{0,24},{8,16},{16,8},{24,0},{1,25},{9,17},{17,9},{25,1},{2,26},{10... | collective-permute-start | bytes 190472 | tf_op jit(solution)/shard_map/ppermute | solution.py:383
  47.7 4.3 %collective-permute-start.13 = (bf16[8,3968]{1,0:T(8,128)(2,1)S(1)}, bf16[8,3968]{1,0:T(8,128)(2,1)S(1)}, u32[]{:S(2)}, u32[]{:S(2)}) collective-permute-start(bf16[8,3968]{1,0:T(8,128)(2,1)S(1)} %plane_sum.1.mine), channel_id=1, source_target_pairs={{0,1},{1,0},{2,3},{3,2},{4,5},{5,4},{6,7},{7,6},{8,9},{9,8},{10,11... | collective-permute-start | bytes 190472 | tf_op jit(solution)/shard_map/ppermute | solution.py:383

commit v10 on v9

--- a/solution.py
+++ b/solution.py
@@ -93,7 +93,7 @@
     out_ref[width : width + half] = rest
 
 
-def pack_kernel(masked, after, packed_ref):
+def pack_kernel(masked, packed_ref):
     rows_of_128(masked, packed_ref)
 
 
@@ -407,7 +407,7 @@
     ends = [min(max(((i + 1) ^ 1) - 1, 0), count - 1) for i in range(count)]
     far = lax.ppermute(far, WIDE, list(enumerate(ends)))
     weight_rows = call(
-        turn_kernel, "turn", 8, 1 << 34, 4 << 20, array((total, channels), bf16)
+        turn_kernel, "turn", 8, 1 << 20, 4 << 20, array((total, channels), bf16)
     )(weight.T)
     slabs = width * channels // 128
     across = call(
@@ -421,9 +421,8 @@
         (pltpu.VMEM((2,) + slab.shape, bf16),),
     )(near, far)
     packed = call(
-        pack_kernel, "pack", 4, 1 << 16, 1 << 19, array((slabs, rows, 128), bf16), (),
-        [vmem, pl.BlockSpec(memory_space=pl.ANY)],
-    )(masked, corner)
+        pack_kernel, "pack", 4, 1 << 16, 1 << 19, array((slabs, rows, 128), bf16)
+    )(masked)
     corner = in_plane(corner, 1)
     bricks = [packed, across] + [in_plane(packed, distance) for distance in CHIPS[2:]]
 

time: 53 us -> 49.8 us (0.940)
  starting transfers between devices: 24.7 us -> 21.3 us
    ppermute x13, starting transfers between devices: 24 us -> 20.7 us  [swap(): return lax.ppermute(piece, axes, [(i, i ^ distance) for i in range(size)])]
  transfers between devices with their start and end apart: 14 -> 14, of which waited for: 5 -> 7; matrix products, arithmetic and copies ran while one was open for 0% -> 0% of each run, Pallas kernels for 14% -> 14%
where the time goes in v10:
time: 49.8 us; the launch traced here: 49.7 us
  starting transfers between devices  21.3 us (43%)
  Pallas kernels  13.4 us (27%)
  waiting for transfers between devices  13.3 us (27%)
  local copies, waits for them, and re-layouts  0.84 us (2%)
  between operations  0.75 us (2%)
    ppermute x13, starting transfers between devices, swap(): return lax.ppermute(piece, axes, [(i, i ^ distance) for i in range(size)])  20.7 us
    pallas_call x12, Pallas kernels, run(): pl.pallas_call(body, out_shape=out_shape, in_specs=in_specs or [spec] * l...  13.4 us
    ppermute x13, waiting for transfers between devices, swap(): return lax.ppermute(piece, axes, [(i, i ^ distance) for i in range(size)])  13.3 us
  transfers between devices with their start and end apart: 14, of which 7 were waited for; matrix products, arithmetic and copies ran while one was open for 0% of the time, Pallas kernels for 14%

profile of v10, /device:TPU:0, one launch (start us, length us, event | category | flops | bytes accessed | tf_op | source)
XLA Modules:
  0.0 49.7 jit_solution(4804159029544523183)
XLA Ops:
  0.6 0.0 copy-start.1
  0.6 0.0 copy-start.2
  0.7 0.0 copy-start.3
  0.7 0.0 copy-start
  0.7 0.2 pick.1.first
  0.8 0.7 %copy-done.1 = bf16[8,8,8,192]{3,2,1,0:T(8,128)(2,1)S(1)} copy-done((bf16[8,8,8,192]{3,2,1,0:T(8,128)(2,1)S(1)}, bf16[8,8,8,192]{3,2,1,0:T(8,128)(2,1)}, u32[]{:S(2)}) %copy-start.1) | copy-done | bytes 196632
  1.6 0.1 copy-done.2
  1.7 0.0 copy-done.3
  1.7 0.2 prepare.1
  1.9 0.1 across.1
  1.9 3.0 %collective-permute-start.2 = (bf16[14,64,128]{2,1,0:T(8,128)(2,1)S(1)}, bf16[14,64,128]{2,1,0:T(8,128)(2,1)S(1)}, u32[]{:S(2)}, u32[]{:S(2)}) collective-permute-start(bf16[14,64,128]{2,1,0:T(8,128)(2,1)S(1)} %across.1), channel_id=1, source_target_pairs={{0,1},{1,0},{2,3},{3,2},{4,5},{5,4},{6,7},{7,6},{8,9},{9,8},{10,11... | collective-permute-start | bytes 688136 | tf_op jit(solution)/shard_map/ppermute | solution.py:383
  5.0 0.0 collective-permute-start
  5.0 0.7 %collective-permute-start.1 = (bf16[3,64,192]{2,1,0:T(8,128)(2,1)S(1)}, bf16[3,64,192]{2,1,0:T(8,128)(2,1)S(1)}, u32[]{:S(2)}, u32[]{:S(2)}) collective-permute-start(bf16[3,64,192]{2,1,0:T(8,128)(2,1)S(1)} %get-tuple-element.30), channel_id=1, source_target_pairs={{0,0},{2,4},{4,2},{6,8},{8,6},{10,12},{12,10},{14,16},{16,14},{18,... | collective-permute-start | bytes 221192 | tf_op jit(solution)/shard_map/ppermute | solution.py:408
  5.6 0.0 copy-done
  5.7 0.8 %turn.1.weight = bf16[5184,192]{1,0:T(8,128)(2,1)S(1)} custom-call(bf16[192,5184]{1,0:T(8,128)(2,1)S(1)} %bitcast.5), custom_call_target="tpu_custom_call" | custom-call | flops 1048576 | bytes 4194304 | tf_op jit(solution)/shard_map/turn/pallas_call | solution.py:354
  6.4 0.0 collective-permute-done.near
  6.4 0.0 collective-permute-done.1.far
  6.5 0.2 collective-permute-start.3
  6.7 0.1 pack.1.refs_4_
  6.8 6.4 %collective-permute-start.7 = (bf16[12,64,128]{2,1,0:T(8,128)(2,1)S(1)}, bf16[12,64,128]{2,1,0:T(8,128)(2,1)S(1)}, u32[]{:S(2)}, u32[]{:S(2)}) collective-permute-start(bf16[12,64,128]{2,1,0:T(8,128)(2,1)S(1)} %pack.1.refs_4_), channel_id=1, source_target_pairs={{0,4},{1,5},{2,6},{3,7},{4,0},{5,1},{6,2},{7,3},{8,12},{9,13},{10,... | collective-permute-start | bytes 589832 | tf_op jit(solution)/shard_map/ppermute | solution.py:383
  13.2 1.0 %collective-permute-start.8 = (bf16[12,64,128]{2,1,0:T(8,128)(2,1)S(1)}, bf16[12,64,128]{2,1,0:T(8,128)(2,1)S(1)}, u32[]{:S(2)}, u32[]{:S(2)}) collective-permute-start(bf16[12,64,128]{2,1,0:T(8,128)(2,1)S(1)} %pack.1.refs_4_), channel_id=1, source_target_pairs={{0,5},{1,4},{2,7},{3,6},{4,1},{5,0},{6,3},{7,2},{8,13},{9,12},{10,... | collective-permute-start | bytes 589832 | tf_op jit(solution)/shard_map/ppermute | solution.py:383
  14.2 0.0 collective-permute-done.3.corner
  14.2 0.0 collective-permute-done.2.across.refs_5_
  14.2 3.6 %forward.1 = (bf16[8,64,192]{2,1,0:T(8,128)(2,1)}, bf16[10,80,192]{2,1,0:T(8,128)(2,1)S(1)}, bf16[48,640]{1,0:T(8,128)(2,1)S(1)}, bf16[48,640]{1,0:T(8,128)(2,1)...) custom-call(bf16[8,64,192]{2,1,0:T(8,128)(2,1)S(1)} %get-tuple-element.27.masked, ...), custom_call_target="tpu_custom_call" | custom-call | flops 4294967296 | bytes 1048576 | tf_op jit(solution)/shard_map/forward/pallas_call | solution.py:354
  17.8 0.5 %collective-permute-start.4 = (bf16[48,640]{1,0:T(8,128)(2,1)S(1)}, bf16[48,640]{1,0:T(8,128)(2,1)S(1)}, u32[]{:S(2)}, u32[]{:S(2)}) collective-permute-start(bf16[48,640]{1,0:T(8,128)(2,1)S(1)} %get-tuple-element.38), channel_id=1, source_target_pairs={{0,1},{1,0},{2,3},{3,2},{4,5},{5,4},{6,7},{7,6},{8,9},{9,8},{10,11... | collective-permute-start | bytes 184328 | tf_op jit(solution)/shard_map/ppermute | solution.py:383
  18.3 2.3 %collective-permute-start.5 = (bf16[48,640]{1,0:T(8,128)(2,1)S(1)}, bf16[48,640]{1,0:T(8,128)(2,1)S(1)}, u32[]{:S(2)}, u32[]{:S(2)}) collective-permute-start(bf16[48,640]{1,0:T(8,128)(2,1)S(1)} %get-tuple-element.39), channel_id=1, source_target_pairs={{0,4},{1,5},{2,6},{3,7},{4,0},{5,1},{6,2},{7,3},{8,12},{9,13},{10,... | collective-permute-start | bytes 184328 | tf_op jit(solution)/shard_map/ppermute | solution.py:383
  20.6 1.0 %collective-permute-start.6 = (bf16[48,640]{1,0:T(8,128)(2,1)S(1)}, bf16[48,640]{1,0:T(8,128)(2,1)S(1)}, u32[]{:S(2)}, u32[]{:S(2)}) collective-permute-start(bf16[48,640]{1,0:T(8,128)(2,1)S(1)} %get-tuple-element.40), channel_id=1, source_target_pairs={{0,5},{1,4},{2,7},{3,6},{4,1},{5,0},{6,3},{7,2},{8,13},{9,12},{10,... | collective-permute-start | bytes 184328 | tf_op jit(solution)/shard_map/ppermute | solution.py:383
  21.6 0.0 collective-permute-done.7.refs_6_
  21.6 2.2 %collective-permute-done.8.refs_7_ = bf16[12,64,128]{2,1,0:T(8,128)(2,1)S(1)} collective-permute-done((bf16[12,64,128]{2,1,0:T(8,128)(2,1)S(1)}, bf16[12,64,128]{2,1,0:T(8,128)(2,1)S(1)}, u32[]{:S(2)}, u32[]{:S(2)}) %collective-permute-start.8) | collective-permute-done | bytes 196640 | tf_op jit(solution)/shard_map/ppermute | solution.py:383
  23.8 1.9 %collective-permute-done.4.refs_1_ = bf16[48,640]{1,0:T(8,128)(2,1)S(1)} collective-permute-done((bf16[48,640]{1,0:T(8,128)(2,1)S(1)}, bf16[48,640]{1,0:T(8,128)(2,1)S(1)}, u32[]{:S(2)}, u32[]{:S(2)}) %collective-permute-start.4) | collective-permute-done | bytes 61472 | tf_op jit(solution)/shard_map/ppermute | solution.py:383
  25.7 0.0 collective-permute-done.5.refs_2_
  25.7 0.7 %collective-permute-done.6.refs_3_ = bf16[48,640]{1,0:T(8,128)(2,1)S(1)} collective-permute-done((bf16[48,640]{1,0:T(8,128)(2,1)S(1)}, bf16[48,640]{1,0:T(8,128)(2,1)S(1)}, u32[]{:S(2)}, u32[]{:S(2)}) %collective-permute-start.6) | collective-permute-done | bytes 61472 | tf_op jit(solution)/shard_map/ppermute | solution.py:383
  26.4 4.8 %kernel_gradient.1 = (f32[24,5184]{1,0:T(8,128)S(1)}, bf16[24,5184]{1,0:T(8,128)(2,1)S(1)}) custom-call(bf16[48,640]{1,0:T(8,128)(2,1)S(1)} %get-tuple-element.37.refs_0_, bf16[48,640]{1,0:T(8,128)(2,1)S(1)} %collective-permute-done.4.refs_1_, bf16[48,640]{1,0:T(8,128)(2,1)S(1)} %collective-permute-done.5.refs_2_, ...), custom_call_target="tpu_custom_call" | custom-call | flops 1358954496 | bytes 4194304 | tf_op jit(solution)/shard_map/kernel_gradient/pallas_call | solution.py:354
  31.2 0.3 collective-permute-start.9
  31.5 1.3 %collective-permute-done.9.other = bf16[24,5184]{1,0:T(8,128)(2,1)S(1)} collective-permute-done((bf16[24,5184]{1,0:T(8,128)(2,1)S(1)}, bf16[24,5184]{1,0:T(8,128)(2,1)S(1)}, u32[]{:S(2)}, u32[]{:S(2)}) %collective-permute-start.9) | collective-permute-done | bytes 248864 | tf_op jit(solution)/shard_map/ppermute | solution.py:383
  32.8 0.2 fold.1
  33.0 2.8 %collective-permute-start.10 = (bf16[8,3968]{1,0:T(8,128)(2,1)S(1)}, bf16[8,3968]{1,0:T(8,128)(2,1)S(1)}, u32[]{:S(2)}, u32[]{:S(2)}) collective-permute-start(bf16[8,3968]{1,0:T(8,128)(2,1)S(1)} %get-tuple-element.43), channel_id=1, source_target_pairs={{0,8},{8,0},{16,24},{24,16},{1,9},{9,1},{17,25},{25,17},{2,10},{10... | collective-permute-start | bytes 190472 | tf_op jit(solution)/shard_map/ppermute | solution.py:383
  35.8 2.6 %collective-permute-start.11 = (bf16[8,3968]{1,0:T(8,128)(2,1)S(1)}, bf16[8,3968]{1,0:T(8,128)(2,1)S(1)}, u32[]{:S(2)}, u32[]{:S(2)}) collective-permute-start(bf16[8,3968]{1,0:T(8,128)(2,1)S(1)} %get-tuple-element.44), channel_id=1, source_target_pairs={{0,16},{8,24},{16,0},{24,8},{1,17},{9,25},{17,1},{25,9},{2,18},{10... | collective-permute-start | bytes 190472 | tf_op jit(solution)/shard_map/ppermute | solution.py:383
  38.4 0.0 collective-permute-start.12
  38.4 2.7 %input_gradient.1 = bf16[8,64,192]{2,1,0:T(8,128)(2,1)} custom-call(bf16[10,80,192]{2,1,0:T(8,128)(2,1)S(1)} %get-tuple-element.36.gp, f32[8,64,128]{2,1,0:T(8,128)S(1)} %get-tuple-element.33.live, bf16[192,5184]{1,0:T(8,128)(2,1)S(1)} %bitcast.6), custom_call_target="tpu_custom_call" | custom-call | flops 1358954496 | bytes 4194304 | tf_op jit(solution)/shard_map/input_gradient/pallas_call | solution.py:354
  41.1 0.0 collective-permute-done.10.one
  41.1 2.1 %collective-permute-done.11.two = bf16[8,3968]{1,0:T(8,128)(2,1)S(1)} collective-permute-done((bf16[8,3968]{1,0:T(8,128)(2,1)S(1)}, bf16[8,3968]{1,0:T(8,128)(2,1)S(1)}, u32[]{:S(2)}, u32[]{:S(2)}) %collective-permute-start.11) | collective-permute-done | bytes 63520 | tf_op jit(solution)/shard_map/ppermute | solution.py:383
  43.2 1.3 %collective-permute-done.12.three = bf16[8,3968]{1,0:T(8,128)(2,1)S(1)} collective-permute-done((bf16[8,3968]{1,0:T(8,128)(2,1)S(1)}, bf16[8,3968]{1,0:T(8,128)(2,1)S(1)}, u32[]{:S(2)}, u32[]{:S(2)}) %collective-permute-start.12) | collective-permute-done | bytes 63520 | tf_op jit(solution)/shard_map/ppermute | solution.py:383
  44.6 0.6 %collective-permute-start.13 = (bf16[8,3968]{1,0:T(8,128)(2,1)S(1)}, bf16[8,3968]{1,0:T(8,128)(2,1)S(1)}, u32[]{:S(2)}, u32[]{:S(2)}) collective-permute-start(bf16[8,3968]{1,0:T(8,128)(2,1)S(1)} %plane_sum.1.mine), channel_id=1, source_target_pairs={{0,1},{1,0},{2,3},{3,2},{4,5},{5,4},{6,7},{7,6},{8,9},{9,8},{10,11... | collective-permute-start | bytes 190472 | tf_op jit(solution)/shard_map/ppermute | solution.py:383
  45.2 3.7 %collective-permute-done.13.other = bf16[8,3968]{1,0:T(8,128)(2,1)S(1)} collective-permute-done((bf16[8,3968]{1,0:T(8,128)(2,1)S(1)}, bf16[8,3968]{1,0:T(8,128)(2,1)S(1)}, u32[]{:S(2)}, u32[]{:S(2)}) %collective-permute-start.13) | collective-permute-done | bytes 63520 | tf_op jit(solution)/shard_map/ppermute | solution.py:383
  48.9 0.8 %join.1 = f32[12,5184]{1,0:T(8,128)} custom-call(bf16[8,3968]{1,0:T(8,128)(2,1)S(1)} %plane_sum.1.mine, bf16[8,3968]{1,0:T(8,128)(2,1)S(1)} %collective-permute-done.13.other), custom_call_target="tpu_custom_call" | custom-call | flops 41472 | bytes 580608 | tf_op jit(solution)/shard_map/join/pallas_call | solution.py:354
  (2 shorter events, 0.1 us)
Async XLA Ops:
  0.6 1.0 %copy-start.1 = (bf16[8,8,8,192]{3,2,1,0:T(8,128)(2,1)S(1)}, bf16[8,8,8,192]{3,2,1,0:T(8,128)(2,1)}, u32[]{:S(2)}) copy-start(bf16[8,8,8,192]{3,2,1,0:T(8,128)(2,1)} %param.4) | copy-start | bytes 589828
  0.6 1.0 %copy-start.2 = (bf16[8,8,8,192]{3,2,1,0:T(8,128)(2,1)S(1)}, bf16[8,8,8,192]{3,2,1,0:T(8,128)(2,1)}, u32[]{:S(2)}) copy-start(bf16[8,8,8,192]{3,2,1,0:T(8,128)(2,1)} %param.7) | copy-start | bytes 589828
  0.7 1.0 %copy-start.3 = (s32[8,8,8]{2,1,0:T(8,128)S(1)}, s32[8,8,8]{2,1,0:T(8,128)}, u32[]{:S(2)}) copy-start(s32[8,8,8]{2,1,0:T(8,128)} %mask.1) | copy-start | bytes 6148
  0.7 5.0 %copy-start = (bf16[5184,192]{0,1:T(8,128)(2,1)S(1)}, bf16[5184,192]{0,1:T(8,128)(2,1)}, u32[]{:S(2)}) copy-start(bf16[5184,192]{0,1:T(8,128)(2,1)} %param.5) | copy-start | bytes 5971972
  1.9 12.3 %collective-permute-start.2 = (bf16[14,64,128]{2,1,0:T(8,128)(2,1)S(1)}, bf16[14,64,128]{2,1,0:T(8,128)(2,1)S(1)}, u32[]{:S(2)}, u32[]{:S(2)}) collective-permute-start(bf16[14,64,128]{2,1,0:T(8,128)(2,1)S(1)} %across.1), channel_id=1, source_target_pairs={{0,1},{1,0},{2,3},{3,2},{4,5},{5,4},{6,7},{7,6},{8,9},{9,8},{10,11... | collective-permute-start | bytes 688136 | tf_op jit(solution)/shard_map/ppermute | solution.py:383
  5.0 1.5 %collective-permute-start = (bf16[3,64,192]{2,1,0:T(8,128)(2,1)S(1)}, bf16[3,64,192]{2,1,0:T(8,128)(2,1)S(1)}, u32[]{:S(2)}, u32[]{:S(2)}) collective-permute-start(bf16[3,64,192]{2,1,0:T(8,128)(2,1)S(1)} %get-tuple-element.29), channel_id=1, source_target_pairs={{0,2},{2,0},{4,6},{6,4},{8,10},{10,8},{12,14},{14,12},{16,18},{18,... | collective-permute-start | bytes 221192 | tf_op jit(solution)/shard_map/ppermute | solution.py:383
  5.0 1.5 %collective-permute-start.1 = (bf16[3,64,192]{2,1,0:T(8,128)(2,1)S(1)}, bf16[3,64,192]{2,1,0:T(8,128)(2,1)S(1)}, u32[]{:S(2)}, u32[]{:S(2)}) collective-permute-start(bf16[3,64,192]{2,1,0:T(8,128)(2,1)S(1)} %get-tuple-element.30), channel_id=1, source_target_pairs={{0,0},{2,4},{4,2},{6,8},{8,6},{10,12},{12,10},{14,16},{16,14},{18,... | collective-permute-start | bytes 221192 | tf_op jit(solution)/shard_map/ppermute | solution.py:408
  6.5 7.7 %collective-permute-start.3 = (bf16[80,192]{1,0:T(8,128)(2,1)S(1)}, bf16[80,192]{1,0:T(8,128)(2,1)S(1)}, u32[]{:S(2)}, u32[]{:S(2)}) collective-permute-start(bf16[80,192]{1,0:T(8,128)(2,1)S(1)} %corner.1), channel_id=1, source_target_pairs={{0,1},{1,0},{2,3},{3,2},{4,5},{5,4},{6,7},{7,6},{8,9},{9,8},{10,11... | collective-permute-start | bytes 92168 | tf_op jit(solution)/shard_map/ppermute | solution.py:383
  6.8 14.8 %collective-permute-start.7 = (bf16[12,64,128]{2,1,0:T(8,128)(2,1)S(1)}, bf16[12,64,128]{2,1,0:T(8,128)(2,1)S(1)}, u32[]{:S(2)}, u32[]{:S(2)}) collective-permute-start(bf16[12,64,128]{2,1,0:T(8,128)(2,1)S(1)} %pack.1.refs_4_), channel_id=1, source_target_pairs={{0,4},{1,5},{2,6},{3,7},{4,0},{5,1},{6,2},{7,3},{8,12},{9,13},{10,... | collective-permute-start | bytes 589832 | tf_op jit(solution)/shard_map/ppermute | solution.py:383
  13.2 10.7 %collective-permute-start.8 = (bf16[12,64,128]{2,1,0:T(8,128)(2,1)S(1)}, bf16[12,64,128]{2,1,0:T(8,128)(2,1)S(1)}, u32[]{:S(2)}, u32[]{:S(2)}) collective-permute-start(bf16[12,64,128]{2,1,0:T(8,128)(2,1)S(1)} %pack.1.refs_4_), channel_id=1, source_target_pairs={{0,5},{1,4},{2,7},{3,6},{4,1},{5,0},{6,3},{7,2},{8,13},{9,12},{10,... | collective-permute-start | bytes 589832 | tf_op jit(solution)/shard_map/ppermute | solution.py:383
  17.8 7.9 %collective-permute-start.4 = (bf16[48,640]{1,0:T(8,128)(2,1)S(1)}, bf16[48,640]{1,0:T(8,128)(2,1)S(1)}, u32[]{:S(2)}, u32[]{:S(2)}) collective-permute-start(bf16[48,640]{1,0:T(8,128)(2,1)S(1)} %get-tuple-element.38), channel_id=1, source_target_pairs={{0,1},{1,0},{2,3},{3,2},{4,5},{5,4},{6,7},{7,6},{8,9},{9,8},{10,11... | collective-permute-start | bytes 184328 | tf_op jit(solution)/shard_map/ppermute | solution.py:383
  18.3 7.4 %collective-permute-start.5 = (bf16[48,640]{1,0:T(8,128)(2,1)S(1)}, bf16[48,640]{1,0:T(8,128)(2,1)S(1)}, u32[]{:S(2)}, u32[]{:S(2)}) collective-permute-start(bf16[48,640]{1,0:T(8,128)(2,1)S(1)} %get-tuple-element.39), channel_id=1, source_target_pairs={{0,4},{1,5},{2,6},{3,7},{4,0},{5,1},{6,2},{7,3},{8,12},{9,13},{10,... | collective-permute-start | bytes 184328 | tf_op jit(solution)/shard_map/ppermute | solution.py:383
  20.6 5.8 %collective-permute-start.6 = (bf16[48,640]{1,0:T(8,128)(2,1)S(1)}, bf16[48,640]{1,0:T(8,128)(2,1)S(1)}, u32[]{:S(2)}, u32[]{:S(2)}) collective-permute-start(bf16[48,640]{1,0:T(8,128)(2,1)S(1)} %get-tuple-element.40), channel_id=1, source_target_pairs={{0,5},{1,4},{2,7},{3,6},{4,1},{5,0},{6,3},{7,2},{8,13},{9,12},{10,... | collective-permute-start | bytes 184328 | tf_op jit(solution)/shard_map/ppermute | solution.py:383
  31.2 1.6 %collective-permute-start.9 = (bf16[24,5184]{1,0:T(8,128)(2,1)S(1)}, bf16[24,5184]{1,0:T(8,128)(2,1)S(1)}, u32[]{:S(2)}, u32[]{:S(2)}) collective-permute-start(bf16[24,5184]{1,0:T(8,128)(2,1)S(1)} %get-tuple-element.42), channel_id=1, source_target_pairs={{0,2},{1,3},{2,0},{3,1},{4,6},{5,7},{6,4},{7,5},{8,10},{9,11},{10,... | collective-permute-start | bytes 746504 | tf_op jit(solution)/shard_map/ppermute | solution.py:383
  33.0 8.1 %collective-permute-start.10 = (bf16[8,3968]{1,0:T(8,128)(2,1)S(1)}, bf16[8,3968]{1,0:T(8,128)(2,1)S(1)}, u32[]{:S(2)}, u32[]{:S(2)}) collective-permute-start(bf16[8,3968]{1,0:T(8,128)(2,1)S(1)} %get-tuple-element.43), channel_id=1, source_target_pairs={{0,8},{8,0},{16,24},{24,16},{1,9},{9,1},{17,25},{25,17},{2,10},{10... | collective-permute-start | bytes 190472 | tf_op jit(solution)/shard_map/ppermute | solution.py:383
  35.8 7.4 %collective-permute-start.11 = (bf16[8,3968]{1,0:T(8,128)(2,1)S(1)}, bf16[8,3968]{1,0:T(8,128)(2,1)S(1)}, u32[]{:S(2)}, u32[]{:S(2)}) collective-permute-start(bf16[8,3968]{1,0:T(8,128)(2,1)S(1)} %get-tuple-element.44), channel_id=1, source_target_pairs={{0,16},{8,24},{16,0},{24,8},{1,17},{9,25},{17,1},{25,9},{2,18},{10... | collective-permute-start | bytes 190472 | tf_op jit(solution)/shard_map/ppermute | solution.py:383
  38.4 6.1 %collective-permute-start.12 = (bf16[8,3968]{1,0:T(8,128)(2,1)S(1)}, bf16[8,3968]{1,0:T(8,128)(2,1)S(1)}, u32[]{:S(2)}, u32[]{:S(2)}) collective-permute-start(bf16[8,3968]{1,0:T(8,128)(2,1)S(1)} %get-tuple-element.45), channel_id=1, source_target_pairs={{0,24},{8,16},{16,8},{24,0},{1,25},{9,17},{17,9},{25,1},{2,26},{10... | collective-permute-start | bytes 190472 | tf_op jit(solution)/shard_map/ppermute | solution.py:383
  44.6 4.3 %collective-permute-start.13 = (bf16[8,3968]{1,0:T(8,128)(2,1)S(1)}, bf16[8,3968]{1,0:T(8,128)(2,1)S(1)}, u32[]{:S(2)}, u32[]{:S(2)}) collective-permute-start(bf16[8,3968]{1,0:T(8,128)(2,1)S(1)} %plane_sum.1.mine), channel_id=1, source_target_pairs={{0,1},{1,0},{2,3},{3,2},{4,5},{5,4},{6,7},{7,6},{8,9},{9,8},{10,11... | collective-permute-start | bytes 190472 | tf_op jit(solution)/shard_map/ppermute | solution.py:383

commit v11 on v10

--- a/solution.py
+++ b/solution.py
@@ -93,7 +93,7 @@
     out_ref[width : width + half] = rest
 
 
-def pack_kernel(masked, packed_ref):
+def pack_kernel(masked, after, packed_ref):
     rows_of_128(masked, packed_ref)
 
 
@@ -414,21 +414,22 @@
         across_kernel, "across", 4, 1 << 16, 1 << 19, array((slabs + 2, rows, 128), bf16)
     )(masked, cot)
     across = in_plane(across, CHIPS[1])
-    near, far, weight_rows = lax.optimization_barrier((near, far, weight_rows))
+    packed = call(
+        pack_kernel, "pack", 4, 1 << 16, 1 << 19, array((slabs, rows, 128), bf16), (),
+        [vmem, pl.BlockSpec(memory_space=pl.ANY)],
+    )(masked, weight_rows)
+    near, far, weight_rows, late = lax.optimization_barrier((near, far, weight_rows, packed))
     corner = call(
         corner_kernel, "corner", 4, 1 << 16, 1 << 18,
         array((4 * halo + 2 * DEPTH, channels), bf16),
         (pltpu.VMEM((2,) + slab.shape, bf16),),
     )(near, far)
-    packed = call(
-        pack_kernel, "pack", 4, 1 << 16, 1 << 19, array((slabs, rows, 128), bf16)
-    )(masked)
     corner = in_plane(corner, 1)
-    bricks = [packed, across] + [in_plane(packed, distance) for distance in CHIPS[2:]]
+    bricks = [packed, across, in_plane(packed, CHIPS[2]), in_plane(late, CHIPS[3])]
 
     mid = rows + 2 * DEPTH
     act, gp, *slices = call(
-        forward_kernel, "forward", 28, 1 << 32, 1 << 20,
+        forward_kernel, "forward", 28, 3 << 29, 1 << 20,
         (brick, array((width + 2, mid, channels), bf16))
         + (array((2 * group, span), bf16),) * len(CHIPS),
         (
@@ -438,6 +439,7 @@
             pltpu.VMEM((MEMBERS, group, span), f32),
         ),
     )(masked, cot, near, far, across, corner, live, weight_rows, pick)
+    bricks[2], *slices = lax.optimization_barrier((bricks[2], *slices))
     slices = [slices[0]] + [in_plane(part, d) for part, d in zip(slices[1:], CHIPS[1:])]
 
     grad_input = call(

time: 49.8 us -> 48.9 us (0.982)
  waiting for transfers between devices: 13.3 us -> 12.5 us
    ppermute x13, waiting for transfers between devices: 13.3 us -> 12.5 us  [swap(): return lax.ppermute(piece, axes, [(i, i ^ distance) for i in range(size)])]
  transfers between devices with their start and end apart: 14 -> 14, of which waited for: 7 -> 8; matrix products, arithmetic and copies ran while one was open for 0% -> 0% of each run, Pallas kernels for 14% -> 15%
where the time goes in v11:
time: 48.9 us; the launch traced here: 48.7 us
  starting transfers between devices  21.2 us (43%)
  Pallas kernels  13.4 us (27%)
  waiting for transfers between devices  12.5 us (26%)
  local copies, waits for them, and re-layouts  0.86 us (2%)
  between operations  0.75 us (2%)
    ppermute x13, starting transfers between devices, swap(): return lax.ppermute(piece, axes, [(i, i ^ distance) for i in range(size)])  20.5 us
    pallas_call x12, Pallas kernels, run(): pl.pallas_call(body, out_shape=out_shape, in_specs=in_specs or [spec] * l...  13.4 us
    ppermute x13, waiting for transfers between devices, swap(): return lax.ppermute(piece, axes, [(i, i ^ distance) for i in range(size)])  12.5 us
  transfers between devices with their start and end apart: 14, of which 8 were waited for; matrix products, arithmetic and copies ran while one was open for 0% of the time, Pallas kernels for 15%

profile of v11, /device:TPU:0, one launch (start us, length us, event | category | flops | bytes accessed | tf_op | source)
XLA Modules:
  0.0 48.7 jit_solution(9708923583455091214)
XLA Ops:
  0.6 0.0 copy-start.2
  0.6 0.0 copy-start.3
  0.7 0.0 copy-start.1
  0.7 0.0 copy-start
  0.7 0.2 pick.1.first
  0.8 0.7 %copy-done.2 = bf16[8,8,8,192]{3,2,1,0:T(8,128)(2,1)S(1)} copy-done((bf16[8,8,8,192]{3,2,1,0:T(8,128)(2,1)S(1)}, bf16[8,8,8,192]{3,2,1,0:T(8,128)(2,1)}, u32[]{:S(2)}) %copy-start.2) | copy-done | bytes 196632
  1.6 0.0 copy-done.3
  1.6 0.1 copy-done.1
  1.7 0.2 prepare.1
  1.9 0.1 across.1
  2.0 3.0 %collective-permute-start.2 = (bf16[14,64,128]{2,1,0:T(8,128)(2,1)S(1)}, bf16[14,64,128]{2,1,0:T(8,128)(2,1)S(1)}, u32[]{:S(2)}, u32[]{:S(2)}) collective-permute-start(bf16[14,64,128]{2,1,0:T(8,128)(2,1)S(1)} %across.1), channel_id=1, source_target_pairs={{0,1},{1,0},{2,3},{3,2},{4,5},{5,4},{6,7},{7,6},{8,9},{9,8},{10,11... | collective-permute-start | bytes 688136 | tf_op jit(solution)/shard_map/ppermute | solution.py:383
  5.0 0.0 collective-permute-start
  5.0 0.7 %collective-permute-start.1 = (bf16[3,64,192]{2,1,0:T(8,128)(2,1)S(1)}, bf16[3,64,192]{2,1,0:T(8,128)(2,1)S(1)}, u32[]{:S(2)}, u32[]{:S(2)}) collective-permute-start(bf16[3,64,192]{2,1,0:T(8,128)(2,1)S(1)} %get-tuple-element.36), channel_id=1, source_target_pairs={{0,0},{2,4},{4,2},{6,8},{8,6},{10,12},{12,10},{14,16},{16,14},{18,... | collective-permute-start | bytes 221192 | tf_op jit(solution)/shard_map/ppermute | solution.py:408
  5.7 0.0 copy-done
  5.7 0.8 %turn.1.after.weight = bf16[5184,192]{1,0:T(8,128)(2,1)S(1)} custom-call(bf16[192,5184]{1,0:T(8,128)(2,1)S(1)} %bitcast.5), custom_call_target="tpu_custom_call" | custom-call | flops 1048576 | bytes 4194304 | tf_op jit(solution)/shard_map/turn/pallas_call | solution.py:354
  6.5 0.1 pack.1.refs_4_
  6.5 3.4 %collective-permute-start.4 = (bf16[12,64,128]{2,1,0:T(8,128)(2,1)S(1)}, bf16[12,64,128]{2,1,0:T(8,128)(2,1)S(1)}, u32[]{:S(2)}, u32[]{:S(2)}) collective-permute-start(bf16[12,64,128]{2,1,0:T(8,128)(2,1)S(1)} %pack.1.refs_4_), channel_id=1, source_target_pairs={{0,4},{1,5},{2,6},{3,7},{4,0},{5,1},{6,2},{7,3},{8,12},{9,13},{10,... | collective-permute-start | bytes 589832 | tf_op jit(solution)/shard_map/ppermute | solution.py:383
  10.0 0.0 collective-permute-done.near
  10.0 0.0 collective-permute-done.1.far
  10.0 0.1 collective-permute-start.3
  10.2 3.8 %collective-permute-start.8 = (bf16[12,64,128]{2,1,0:T(8,128)(2,1)S(1)}, bf16[12,64,128]{2,1,0:T(8,128)(2,1)S(1)}, u32[]{:S(2)}, u32[]{:S(2)}) collective-permute-start(bf16[12,64,128]{2,1,0:T(8,128)(2,1)S(1)} %pack.1.refs_4_), channel_id=1, source_target_pairs={{0,5},{1,4},{2,7},{3,6},{4,1},{5,0},{6,3},{7,2},{8,13},{9,12},{10,... | collective-permute-start | bytes 589832 | tf_op jit(solution)/shard_map/ppermute | solution.py:383
  14.0 0.1 collective-permute-done.3.corner
  14.1 0.0 collective-permute-done.2.across.refs_5_
  14.1 3.6 %forward.1 = (bf16[8,64,192]{2,1,0:T(8,128)(2,1)}, bf16[10,80,192]{2,1,0:T(8,128)(2,1)S(1)}, bf16[48,640]{1,0:T(8,128)(2,1)S(1)}, bf16[48,640]{1,0:T(8,128)(2,1)...) custom-call(bf16[8,64,192]{2,1,0:T(8,128)(2,1)S(1)} %get-tuple-element.33.masked, ...), custom_call_target="tpu_custom_call" | custom-call | flops 1610612736 | bytes 1048576 | tf_op jit(solution)/shard_map/forward/pallas_call | solution.py:354
  17.7 0.0 collective-permute-done.4.refs_6_
  17.7 0.4 collective-permute-start.5
  18.1 2.5 %collective-permute-start.6 = (bf16[48,640]{1,0:T(8,128)(2,1)S(1)}, bf16[48,640]{1,0:T(8,128)(2,1)S(1)}, u32[]{:S(2)}, u32[]{:S(2)}) collective-permute-start(bf16[48,640]{1,0:T(8,128)(2,1)S(1)} %get-tuple-element.49), channel_id=1, source_target_pairs={{0,4},{1,5},{2,6},{3,7},{4,0},{5,1},{6,2},{7,3},{8,12},{9,13},{10,... | collective-permute-start | bytes 184328 | tf_op jit(solution)/shard_map/ppermute | solution.py:383
  20.7 0.9 %collective-permute-start.7 = (bf16[48,640]{1,0:T(8,128)(2,1)S(1)}, bf16[48,640]{1,0:T(8,128)(2,1)S(1)}, u32[]{:S(2)}, u32[]{:S(2)}) collective-permute-start(bf16[48,640]{1,0:T(8,128)(2,1)S(1)} %get-tuple-element.50), channel_id=1, source_target_pairs={{0,5},{1,4},{2,7},{3,6},{4,1},{5,0},{6,3},{7,2},{8,13},{9,12},{10,... | collective-permute-start | bytes 184328 | tf_op jit(solution)/shard_map/ppermute | solution.py:383
  21.6 0.0 collective-permute-done.8.refs_7_
  21.6 0.8 %collective-permute-done.5.refs_1_ = bf16[48,640]{1,0:T(8,128)(2,1)S(1)} collective-permute-done((bf16[48,640]{1,0:T(8,128)(2,1)S(1)}, bf16[48,640]{1,0:T(8,128)(2,1)S(1)}, u32[]{:S(2)}, u32[]{:S(2)}) %collective-permute-start.5) | collective-permute-done | bytes 61472 | tf_op jit(solution)/shard_map/ppermute | solution.py:383
  22.4 0.8 %collective-permute-done.6.refs_2_ = bf16[48,640]{1,0:T(8,128)(2,1)S(1)} collective-permute-done((bf16[48,640]{1,0:T(8,128)(2,1)S(1)}, bf16[48,640]{1,0:T(8,128)(2,1)S(1)}, u32[]{:S(2)}, u32[]{:S(2)}) %collective-permute-start.6) | collective-permute-done | bytes 61472 | tf_op jit(solution)/shard_map/ppermute | solution.py:383
  23.2 2.6 %collective-permute-done.7.refs_3_ = bf16[48,640]{1,0:T(8,128)(2,1)S(1)} collective-permute-done((bf16[48,640]{1,0:T(8,128)(2,1)S(1)}, bf16[48,640]{1,0:T(8,128)(2,1)S(1)}, u32[]{:S(2)}, u32[]{:S(2)}) %collective-permute-start.7) | collective-permute-done | bytes 61472 | tf_op jit(solution)/shard_map/ppermute | solution.py:383
  25.8 4.8 %kernel_gradient.1 = (f32[24,5184]{1,0:T(8,128)S(1)}, bf16[24,5184]{1,0:T(8,128)(2,1)S(1)}) custom-call(bf16[48,640]{1,0:T(8,128)(2,1)S(1)} %get-tuple-element.47.refs_0_, bf16[48,640]{1,0:T(8,128)(2,1)S(1)} %collective-permute-done.5.refs_1_, bf16[48,640]{1,0:T(8,128)(2,1)S(1)} %collective-permute-done.6.refs_2_, ...), custom_call_target="tpu_custom_call" | custom-call | flops 1358954496 | bytes 4194304 | tf_op jit(solution)/shard_map/kernel_gradient/pallas_call | solution.py:354
  30.6 0.1 collective-permute-start.9
  30.6 1.5 %collective-permute-done.9.other = bf16[24,5184]{1,0:T(8,128)(2,1)S(1)} collective-permute-done((bf16[24,5184]{1,0:T(8,128)(2,1)S(1)}, bf16[24,5184]{1,0:T(8,128)(2,1)S(1)}, u32[]{:S(2)}, u32[]{:S(2)}) %collective-permute-start.9) | collective-permute-done | bytes 248864 | tf_op jit(solution)/shard_map/ppermute | solution.py:383
  32.2 0.2 fold.1
  32.3 2.5 %collective-permute-start.10 = (bf16[8,3968]{1,0:T(8,128)(2,1)S(1)}, bf16[8,3968]{1,0:T(8,128)(2,1)S(1)}, u32[]{:S(2)}, u32[]{:S(2)}) collective-permute-start(bf16[8,3968]{1,0:T(8,128)(2,1)S(1)} %get-tuple-element.55), channel_id=1, source_target_pairs={{0,8},{8,0},{16,24},{24,16},{1,9},{9,1},{17,25},{25,17},{2,10},{10... | collective-permute-start | bytes 190472 | tf_op jit(solution)/shard_map/ppermute | solution.py:383
  34.8 2.6 %collective-permute-start.11 = (bf16[8,3968]{1,0:T(8,128)(2,1)S(1)}, bf16[8,3968]{1,0:T(8,128)(2,1)S(1)}, u32[]{:S(2)}, u32[]{:S(2)}) collective-permute-start(bf16[8,3968]{1,0:T(8,128)(2,1)S(1)} %get-tuple-element.56), channel_id=1, source_target_pairs={{0,16},{8,24},{16,0},{24,8},{1,17},{9,25},{17,1},{25,9},{2,18},{10... | collective-permute-start | bytes 190472 | tf_op jit(solution)/shard_map/ppermute | solution.py:383
  37.4 0.0 collective-permute-start.12
  37.4 2.7 %input_gradient.1 = bf16[8,64,192]{2,1,0:T(8,128)(2,1)} custom-call(bf16[10,80,192]{2,1,0:T(8,128)(2,1)S(1)} %get-tuple-element.42.gp, f32[8,64,128]{2,1,0:T(8,128)S(1)} %get-tuple-element.39.live, bf16[192,5184]{1,0:T(8,128)(2,1)S(1)} %bitcast.6), custom_call_target="tpu_custom_call" | custom-call | flops 1358954496 | bytes 4194304 | tf_op jit(solution)/shard_map/input_gradient/pallas_call | solution.py:354
  40.1 0.0 collective-permute-done.10.one
  40.1 2.1 %collective-permute-done.11.two = bf16[8,3968]{1,0:T(8,128)(2,1)S(1)} collective-permute-done((bf16[8,3968]{1,0:T(8,128)(2,1)S(1)}, bf16[8,3968]{1,0:T(8,128)(2,1)S(1)}, u32[]{:S(2)}, u32[]{:S(2)}) %collective-permute-start.11) | collective-permute-done | bytes 63520 | tf_op jit(solution)/shard_map/ppermute | solution.py:383
  42.2 1.3 %collective-permute-done.12.three = bf16[8,3968]{1,0:T(8,128)(2,1)S(1)} collective-permute-done((bf16[8,3968]{1,0:T(8,128)(2,1)S(1)}, bf16[8,3968]{1,0:T(8,128)(2,1)S(1)}, u32[]{:S(2)}, u32[]{:S(2)}) %collective-permute-start.12) | collective-permute-done | bytes 63520 | tf_op jit(solution)/shard_map/ppermute | solution.py:383
  43.6 1.1 %collective-permute-start.13 = (bf16[8,3968]{1,0:T(8,128)(2,1)S(1)}, bf16[8,3968]{1,0:T(8,128)(2,1)S(1)}, u32[]{:S(2)}, u32[]{:S(2)}) collective-permute-start(bf16[8,3968]{1,0:T(8,128)(2,1)S(1)} %plane_sum.1.mine), channel_id=1, source_target_pairs={{0,1},{1,0},{2,3},{3,2},{4,5},{5,4},{6,7},{7,6},{8,9},{9,8},{10,11... | collective-permute-start | bytes 190472 | tf_op jit(solution)/shard_map/ppermute | solution.py:383
  44.7 3.2 %collective-permute-done.13.other = bf16[8,3968]{1,0:T(8,128)(2,1)S(1)} collective-permute-done((bf16[8,3968]{1,0:T(8,128)(2,1)S(1)}, bf16[8,3968]{1,0:T(8,128)(2,1)S(1)}, u32[]{:S(2)}, u32[]{:S(2)}) %collective-permute-start.13) | collective-permute-done | bytes 63520 | tf_op jit(solution)/shard_map/ppermute | solution.py:383
  47.9 0.8 %join.1 = f32[12,5184]{1,0:T(8,128)} custom-call(bf16[8,3968]{1,0:T(8,128)(2,1)S(1)} %plane_sum.1.mine, bf16[8,3968]{1,0:T(8,128)(2,1)S(1)} %collective-permute-done.13.other), custom_call_target="tpu_custom_call" | custom-call | flops 41472 | bytes 580608 | tf_op jit(solution)/shard_map/join/pallas_call | solution.py:354
  (2 shorter events, 0.1 us)
Async XLA Ops:
  0.6 1.0 %copy-start.2 = (bf16[8,8,8,192]{3,2,1,0:T(8,128)(2,1)S(1)}, bf16[8,8,8,192]{3,2,1,0:T(8,128)(2,1)}, u32[]{:S(2)}) copy-start(bf16[8,8,8,192]{3,2,1,0:T(8,128)(2,1)} %param.7) | copy-start | bytes 589828
  0.6 0.9 %copy-start.3 = (s32[8,8,8]{2,1,0:T(8,128)S(1)}, s32[8,8,8]{2,1,0:T(8,128)}, u32[]{:S(2)}) copy-start(s32[8,8,8]{2,1,0:T(8,128)} %mask.1) | copy-start | bytes 6148
  0.7 1.0 %copy-start.1 = (bf16[8,8,8,192]{3,2,1,0:T(8,128)(2,1)S(1)}, bf16[8,8,8,192]{3,2,1,0:T(8,128)(2,1)}, u32[]{:S(2)}) copy-start(bf16[8,8,8,192]{3,2,1,0:T(8,128)(2,1)} %param.4) | copy-start | bytes 589828
  0.7 5.0 %copy-start = (bf16[5184,192]{0,1:T(8,128)(2,1)S(1)}, bf16[5184,192]{0,1:T(8,128)(2,1)}, u32[]{:S(2)}) copy-start(bf16[5184,192]{0,1:T(8,128)(2,1)} %param.5) | copy-start | bytes 5971972
  2.0 12.1 %collective-permute-start.2 = (bf16[14,64,128]{2,1,0:T(8,128)(2,1)S(1)}, bf16[14,64,128]{2,1,0:T(8,128)(2,1)S(1)}, u32[]{:S(2)}, u32[]{:S(2)}) collective-permute-start(bf16[14,64,128]{2,1,0:T(8,128)(2,1)S(1)} %across.1), channel_id=1, source_target_pairs={{0,1},{1,0},{2,3},{3,2},{4,5},{5,4},{6,7},{7,6},{8,9},{9,8},{10,11... | collective-permute-start | bytes 688136 | tf_op jit(solution)/shard_map/ppermute | solution.py:383
  5.0 5.0 %collective-permute-start = (bf16[3,64,192]{2,1,0:T(8,128)(2,1)S(1)}, bf16[3,64,192]{2,1,0:T(8,128)(2,1)S(1)}, u32[]{:S(2)}, u32[]{:S(2)}) collective-permute-start(bf16[3,64,192]{2,1,0:T(8,128)(2,1)S(1)} %get-tuple-element.35), channel_id=1, source_target_pairs={{0,2},{2,0},{4,6},{6,4},{8,10},{10,8},{12,14},{14,12},{16,18},{18,... | collective-permute-start | bytes 221192 | tf_op jit(solution)/shard_map/ppermute | solution.py:383
  5.0 5.0 %collective-permute-start.1 = (bf16[3,64,192]{2,1,0:T(8,128)(2,1)S(1)}, bf16[3,64,192]{2,1,0:T(8,128)(2,1)S(1)}, u32[]{:S(2)}, u32[]{:S(2)}) collective-permute-start(bf16[3,64,192]{2,1,0:T(8,128)(2,1)S(1)} %get-tuple-element.36), channel_id=1, source_target_pairs={{0,0},{2,4},{4,2},{6,8},{8,6},{10,12},{12,10},{14,16},{16,14},{18,... | collective-permute-start | bytes 221192 | tf_op jit(solution)/shard_map/ppermute | solution.py:408
  6.5 11.2 %collective-permute-start.4 = (bf16[12,64,128]{2,1,0:T(8,128)(2,1)S(1)}, bf16[12,64,128]{2,1,0:T(8,128)(2,1)S(1)}, u32[]{:S(2)}, u32[]{:S(2)}) collective-permute-start(bf16[12,64,128]{2,1,0:T(8,128)(2,1)S(1)} %pack.1.refs_4_), channel_id=1, source_target_pairs={{0,4},{1,5},{2,6},{3,7},{4,0},{5,1},{6,2},{7,3},{8,12},{9,13},{10,... | collective-permute-start | bytes 589832 | tf_op jit(solution)/shard_map/ppermute | solution.py:383
  10.0 4.1 %collective-permute-start.3 = (bf16[80,192]{1,0:T(8,128)(2,1)S(1)}, bf16[80,192]{1,0:T(8,128)(2,1)S(1)}, u32[]{:S(2)}, u32[]{:S(2)}) collective-permute-start(bf16[80,192]{1,0:T(8,128)(2,1)S(1)} %corner.1), channel_id=1, source_target_pairs={{0,1},{1,0},{2,3},{3,2},{4,5},{5,4},{6,7},{7,6},{8,9},{9,8},{10,11... | collective-permute-start | bytes 92168 | tf_op jit(solution)/shard_map/ppermute | solution.py:383
  10.2 11.4 %collective-permute-start.8 = (bf16[12,64,128]{2,1,0:T(8,128)(2,1)S(1)}, bf16[12,64,128]{2,1,0:T(8,128)(2,1)S(1)}, u32[]{:S(2)}, u32[]{:S(2)}) collective-permute-start(bf16[12,64,128]{2,1,0:T(8,128)(2,1)S(1)} %pack.1.refs_4_), channel_id=1, source_target_pairs={{0,5},{1,4},{2,7},{3,6},{4,1},{5,0},{6,3},{7,2},{8,13},{9,12},{10,... | collective-permute-start | bytes 589832 | tf_op jit(solution)/shard_map/ppermute | solution.py:383
  17.7 4.7 %collective-permute-start.5 = (bf16[48,640]{1,0:T(8,128)(2,1)S(1)}, bf16[48,640]{1,0:T(8,128)(2,1)S(1)}, u32[]{:S(2)}, u32[]{:S(2)}) collective-permute-start(bf16[48,640]{1,0:T(8,128)(2,1)S(1)} %get-tuple-element.48), channel_id=1, source_target_pairs={{0,1},{1,0},{2,3},{3,2},{4,5},{5,4},{6,7},{7,6},{8,9},{9,8},{10,11... | collective-permute-start | bytes 184328 | tf_op jit(solution)/shard_map/ppermute | solution.py:383
  18.1 5.1 %collective-permute-start.6 = (bf16[48,640]{1,0:T(8,128)(2,1)S(1)}, bf16[48,640]{1,0:T(8,128)(2,1)S(1)}, u32[]{:S(2)}, u32[]{:S(2)}) collective-permute-start(bf16[48,640]{1,0:T(8,128)(2,1)S(1)} %get-tuple-element.49), channel_id=1, source_target_pairs={{0,4},{1,5},{2,6},{3,7},{4,0},{5,1},{6,2},{7,3},{8,12},{9,13},{10,... | collective-permute-start | bytes 184328 | tf_op jit(solution)/shard_map/ppermute | solution.py:383
  20.7 5.1 %collective-permute-start.7 = (bf16[48,640]{1,0:T(8,128)(2,1)S(1)}, bf16[48,640]{1,0:T(8,128)(2,1)S(1)}, u32[]{:S(2)}, u32[]{:S(2)}) collective-permute-start(bf16[48,640]{1,0:T(8,128)(2,1)S(1)} %get-tuple-element.50), channel_id=1, source_target_pairs={{0,5},{1,4},{2,7},{3,6},{4,1},{5,0},{6,3},{7,2},{8,13},{9,12},{10,... | collective-permute-start | bytes 184328 | tf_op jit(solution)/shard_map/ppermute | solution.py:383
  30.6 1.6 %collective-permute-start.9 = (bf16[24,5184]{1,0:T(8,128)(2,1)S(1)}, bf16[24,5184]{1,0:T(8,128)(2,1)S(1)}, u32[]{:S(2)}, u32[]{:S(2)}) collective-permute-start(bf16[24,5184]{1,0:T(8,128)(2,1)S(1)} %get-tuple-element.54), channel_id=1, source_target_pairs={{0,2},{1,3},{2,0},{3,1},{4,6},{5,7},{6,4},{7,5},{8,10},{9,11},{10,... | collective-permute-start | bytes 746504 | tf_op jit(solution)/shard_map/ppermute | solution.py:383
  32.3 7.7 %collective-permute-start.10 = (bf16[8,3968]{1,0:T(8,128)(2,1)S(1)}, bf16[8,3968]{1,0:T(8,128)(2,1)S(1)}, u32[]{:S(2)}, u32[]{:S(2)}) collective-permute-start(bf16[8,3968]{1,0:T(8,128)(2,1)S(1)} %get-tuple-element.55), channel_id=1, source_target_pairs={{0,8},{8,0},{16,24},{24,16},{1,9},{9,1},{17,25},{25,17},{2,10},{10... | collective-permute-start | bytes 190472 | tf_op jit(solution)/shard_map/ppermute | solution.py:383
  34.8 7.4 %collective-permute-start.11 = (bf16[8,3968]{1,0:T(8,128)(2,1)S(1)}, bf16[8,3968]{1,0:T(8,128)(2,1)S(1)}, u32[]{:S(2)}, u32[]{:S(2)}) collective-permute-start(bf16[8,3968]{1,0:T(8,128)(2,1)S(1)} %get-tuple-element.56), channel_id=1, source_target_pairs={{0,16},{8,24},{16,0},{24,8},{1,17},{9,25},{17,1},{25,9},{2,18},{10... | collective-permute-start | bytes 190472 | tf_op jit(solution)/shard_map/ppermute | solution.py:383
  37.4 6.1 %collective-permute-start.12 = (bf16[8,3968]{1,0:T(8,128)(2,1)S(1)}, bf16[8,3968]{1,0:T(8,128)(2,1)S(1)}, u32[]{:S(2)}, u32[]{:S(2)}) collective-permute-start(bf16[8,3968]{1,0:T(8,128)(2,1)S(1)} %get-tuple-element.57), channel_id=1, source_target_pairs={{0,24},{8,16},{16,8},{24,0},{1,25},{9,17},{17,9},{25,1},{2,26},{10... | collective-permute-start | bytes 190472 | tf_op jit(solution)/shard_map/ppermute | solution.py:383
  43.6 4.3 %collective-permute-start.13 = (bf16[8,3968]{1,0:T(8,128)(2,1)S(1)}, bf16[8,3968]{1,0:T(8,128)(2,1)S(1)}, u32[]{:S(2)}, u32[]{:S(2)}) collective-permute-start(bf16[8,3968]{1,0:T(8,128)(2,1)S(1)} %plane_sum.1.mine), channel_id=1, source_target_pairs={{0,1},{1,0},{2,3},{3,2},{4,5},{5,4},{6,7},{7,6},{8,9},{9,8},{10,11... | collective-permute-start | bytes 190472 | tf_op jit(solution)/shard_map/ppermute | solution.py:383

commit v12 on v11

--- a/solution.py
+++ b/solution.py
@@ -248,19 +248,21 @@
 def kernel_grad_kernel(*refs):
     chips = len(CHIPS)
     received, bricks = refs[:chips], refs[chips : 2 * chips]
-    keep_ref, send_ref, slices, cols, part, stage, masked, sems = refs[2 * chips :]
+    keep_ref, send_ref, slices, cols, part, masked = refs[2 * chips :]
     f32 = jnp.float32
     group, lanes = received[0].shape
     blocks, per, lane, channels = masked.shape
     half = lane // 2
     _, _, quad, side = position()
-    copies = []
     for i, distance in enumerate(CHIPS):
-        to = stage.at[distance // 4, side ^ (distance % 2)]
-        packed = bricks[i].at[pl.ds(0, stage.shape[2])]
-        copies.append(pltpu.make_async_copy(packed, to, sems.at[i]))
-        copies[i].start()
-        slices[distance // 4, side ^ (distance % 2)] = received[i][...]
+        block, sided = distance // 4, side ^ (distance % 2)
+        slices[block, sided] = received[i][...]
+        at_rows = pl.ds(pl.multiple_of(sided * half, half), half)
+        for x in range(per):
+            shift = 64 * (x // (per // 2))
+            rest = bricks[i][per + x % (per // 2)]
+            masked[block, x, at_rows, :128] = bricks[i][x]
+            masked[block, x, at_rows, 128:] = rest[:, shift : shift + 64]
     at = lax.broadcasted_iota(jnp.int32, (group, lane), 1)
     y, z = at // DEPTH, at % DEPTH
     tall = lane // DEPTH
@@ -285,16 +287,6 @@
             cols[:, slab * lane : (slab + 1) * lane] = jnp.concatenate(pieces, axis=0).astype(
                 jnp.bfloat16
             )
-    for copy in copies:
-        copy.wait()
-    for block in range(blocks):
-        for sided in range(SIDES):
-            at_rows = pl.ds(sided * half, half)
-            for x in range(per):
-                shift = 64 * (x // (per // 2))
-                rest = stage[block, sided, per + x % (per // 2)]
-                masked[block, x, at_rows, :128] = stage[block, sided, x]
-                masked[block, x, at_rows, 128:] = rest[:, shift : shift + 64]
     for a in range(3):
         got = jnp.zeros((cols.shape[0], channels), f32)
         for block in range(blocks):
@@ -404,8 +396,9 @@
         pick,
     )
     near = swap(near, WIDE, 1, count)
-    ends = [min(max(((i + 1) ^ 1) - 1, 0), count - 1) for i in range(count)]
-    far = lax.ppermute(far, WIDE, list(enumerate(ends)))
+    steps = [(i, i + 2 - 4 * (i % 2)) for i in range(count)]
+    steps = [(i, j) for i, j in steps if 0 <= j < count]
+    far = lax.ppermute(swap(far, WIDE, 1, count), WIDE, steps)
     weight_rows = call(
         turn_kernel, "turn", 8, 1 << 20, 4 << 20, array((total, channels), bf16)
     )(weight.T)
@@ -460,11 +453,8 @@
             pltpu.VMEM((blocks, SIDES, 2 * group, span), bf16),
             pltpu.VMEM((9 * 2 * group, blocks * (width + 2) * SIDES * rows), bf16),
             pltpu.VMEM((2 * group, total), f32),
-            pltpu.VMEM((blocks, SIDES) + packed.shape, bf16),
             pltpu.VMEM((blocks, width, SIDES * rows, channels), bf16),
-            pltpu.SemaphoreType.DMA((chips,)),
         ),
-        [vmem] * chips + [pl.BlockSpec(memory_space=pl.ANY)] * chips,
     )(*slices, *bricks)
     own, *sends = call(
         fold_kernel, "fold", 8, 8 * total * 4, 8 * total * 40,
@@ -474,7 +464,7 @@
             pltpu.VMEM((planes, 8, lanes), f32),
         ),
     )(keep, in_plane(fold, 2))
-    got = [swap(sent, "depth", d, planes) for d, sent in enumerate(sends, 1)]
+    got = [swap(sent, "depth", d, planes) for d, sent in list(enumerate(sends, 1))[::-1]]
     grad_input, *got = lax.optimization_barrier((grad_input, *got))
     voxels = count * SIDES * width * rows
     mine = call(

time: 48.9 us -> 51.7 us (1.057)
  starting transfers between devices: 21.2 us -> 25.6 us
  Pallas kernels: 13.4 us -> 11.2 us
  waiting for transfers between devices: 12.5 us -> 13.2 us
    ppermute x1, starting transfers between devices: 0.66 us -> 3.39 us  [planes_local(): far = lax.ppermute(swap(far, WIDE, 1, count), WIDE, steps)]
    pallas_call x12, Pallas kernels: 13.4 us -> 11.2 us  [run(): pl.pallas_call(body, out_shape=out_shape, in_specs=in_specs or [spec] * l...]
    ppermute x13 -> x14, starting transfers between devices: 20.5 us -> 22.2 us  [swap(): return lax.ppermute(piece, axes, [(i, i ^ distance) for i in range(size)])]
    ppermute x1, waiting for transfers between devices: 0.01 us -> 1.54 us  [planes_local(): far = lax.ppermute(swap(far, WIDE, 1, count), WIDE, steps)]
    ppermute x13 -> x14, waiting for transfers between devices: 12.5 us -> 11.6 us  [swap(): return lax.ppermute(piece, axes, [(i, i ^ distance) for i in range(size)])]
  transfers between devices with their start and end apart: 14 -> 15, of which waited for: 8 -> 8; matrix products, arithmetic and copies ran while one was open for 0% -> 0% of each run, Pallas kernels for 15% -> 14%
where the time goes in v12:
time: 51.7 us; the launch traced here: 51.5 us
  starting transfers between devices  25.6 us (50%)
  waiting for transfers between devices  13.2 us (26%)
  Pallas kernels  11.2 us (22%)
  local copies, waits for them, and re-layouts  0.86 us (2%)
  between operations  0.74 us (1%)
    ppermute x14, starting transfers between devices, swap(): return lax.ppermute(piece, axes, [(i, i ^ distance) for i in range(size)])  22.2 us
    ppermute x14, waiting for transfers between devices, swap(): return lax.ppermute(piece, axes, [(i, i ^ distance) for i in range(size)])  11.6 us
    pallas_call x12, Pallas kernels, run(): pl.pallas_call(body, out_shape=out_shape, in_specs=in_specs or [spec] * l...  11.2 us
    ppermute x1, starting transfers between devices, planes_local(): far = lax.ppermute(swap(far, WIDE, 1, count), WIDE, steps)  3.39 us
    ppermute x1, waiting for transfers between devices, planes_local(): far = lax.ppermute(swap(far, WIDE, 1, count), WIDE, steps)  1.54 us
  transfers between devices with their start and end apart: 15, of which 8 were waited for; matrix products, arithmetic and copies ran while one was open for 0% of the time, Pallas kernels for 14%

profile of v12, /device:TPU:0, one launch (start us, length us, event | category | flops | bytes accessed | tf_op | source)
XLA Modules:
  0.0 51.5 jit_solution(14281270357904659814)
XLA Ops:
  0.6 0.0 copy-start.2
  0.6 0.0 copy-start.3
  0.7 0.0 copy-start.1
  0.7 0.0 copy-start
  0.7 0.2 pick.1.first
  0.8 0.7 %copy-done.2 = bf16[8,8,8,192]{3,2,1,0:T(8,128)(2,1)S(1)} copy-done((bf16[8,8,8,192]{3,2,1,0:T(8,128)(2,1)S(1)}, bf16[8,8,8,192]{3,2,1,0:T(8,128)(2,1)}, u32[]{:S(2)}) %copy-start.2) | copy-done | bytes 196632
  1.6 0.0 copy-done.3
  1.6 0.1 copy-done.1
  1.7 0.2 prepare.1
  1.9 0.1 across.1
  2.0 3.0 %collective-permute-start.3 = (bf16[14,64,128]{2,1,0:T(8,128)(2,1)S(1)}, bf16[14,64,128]{2,1,0:T(8,128)(2,1)S(1)}, u32[]{:S(2)}, u32[]{:S(2)}) collective-permute-start(bf16[14,64,128]{2,1,0:T(8,128)(2,1)S(1)} %across.1), channel_id=1, source_target_pairs={{0,1},{1,0},{2,3},{3,2},{4,5},{5,4},{6,7},{7,6},{8,9},{9,8},{10,11... | collective-permute-start | bytes 688136 | tf_op jit(solution)/shard_map/ppermute | solution.py:375
  5.0 0.0 collective-permute-start.1
  5.0 0.5 collective-permute-start
  5.5 0.8 %collective-permute-done.1 = bf16[3,64,192]{2,1,0:T(8,128)(2,1)S(1)} collective-permute-done((bf16[3,64,192]{2,1,0:T(8,128)(2,1)S(1)}, bf16[3,64,192]{2,1,0:T(8,128)(2,1)S(1)}, u32[]{:S(2)}, u32[]{:S(2)}) %collective-permute-start.1) | collective-permute-done | bytes 73760 | tf_op jit(solution)/shard_map/ppermute | solution.py:375
  6.3 3.4 %collective-permute-start.2 = (bf16[3,64,192]{2,1,0:T(8,128)(2,1)S(1)}, bf16[3,64,192]{2,1,0:T(8,128)(2,1)S(1)}, u32[]{:S(2)}, u32[]{:S(2)}) collective-permute-start(bf16[3,64,192]{2,1,0:T(8,128)(2,1)S(1)} %collective-permute-done.1), channel_id=1, source_target_pairs={{0,4},{4,8},{6,2},{8,12},{10,6},{12,16},{14,10},{16,20},{18,14},{2... | collective-permute-start | bytes 221192 | tf_op jit(solution)/shard_map/ppermute | solution.py:401
  9.7 0.0 copy-done
  9.7 0.8 %turn.1.after.weight = bf16[5184,192]{1,0:T(8,128)(2,1)S(1)} custom-call(bf16[192,5184]{1,0:T(8,128)(2,1)S(1)} %bitcast.5), custom_call_target="tpu_custom_call" | custom-call | flops 1048576 | bytes 4194304 | tf_op jit(solution)/shard_map/turn/pallas_call | solution.py:346
  10.5 0.1 pack.1.refs_4_
  10.6 1.6 %collective-permute-start.5 = (bf16[12,64,128]{2,1,0:T(8,128)(2,1)S(1)}, bf16[12,64,128]{2,1,0:T(8,128)(2,1)S(1)}, u32[]{:S(2)}, u32[]{:S(2)}) collective-permute-start(bf16[12,64,128]{2,1,0:T(8,128)(2,1)S(1)} %pack.1.refs_4_), channel_id=1, source_target_pairs={{0,4},{1,5},{2,6},{3,7},{4,0},{5,1},{6,2},{7,3},{8,12},{9,13},{10,... | collective-permute-start | bytes 589832 | tf_op jit(solution)/shard_map/ppermute | solution.py:375
  12.2 0.0 collective-permute-done.near
  12.2 1.5 %collective-permute-done.2.far = bf16[3,64,192]{2,1,0:T(8,128)(2,1)S(1)} collective-permute-done((bf16[3,64,192]{2,1,0:T(8,128)(2,1)S(1)}, bf16[3,64,192]{2,1,0:T(8,128)(2,1)S(1)}, u32[]{:S(2)}, u32[]{:S(2)}) %collective-permute-start.2) | collective-permute-done | bytes 73760 | tf_op jit(solution)/shard_map/ppermute | solution.py:401
  13.8 0.6 %collective-permute-start.4 = (bf16[80,192]{1,0:T(8,128)(2,1)S(1)}, bf16[80,192]{1,0:T(8,128)(2,1)S(1)}, u32[]{:S(2)}, u32[]{:S(2)}) collective-permute-start(bf16[80,192]{1,0:T(8,128)(2,1)S(1)} %corner.1), channel_id=1, source_target_pairs={{0,1},{1,0},{2,3},{3,2},{4,5},{5,4},{6,7},{7,6},{8,9},{9,8},{10,11... | collective-permute-start | bytes 92168 | tf_op jit(solution)/shard_map/ppermute | solution.py:375
  14.4 3.4 %collective-permute-start.9 = (bf16[12,64,128]{2,1,0:T(8,128)(2,1)S(1)}, bf16[12,64,128]{2,1,0:T(8,128)(2,1)S(1)}, u32[]{:S(2)}, u32[]{:S(2)}) collective-permute-start(bf16[12,64,128]{2,1,0:T(8,128)(2,1)S(1)} %pack.1.refs_4_), channel_id=1, source_target_pairs={{0,5},{1,4},{2,7},{3,6},{4,1},{5,0},{6,3},{7,2},{8,13},{9,12},{10,... | collective-permute-start | bytes 589832 | tf_op jit(solution)/shard_map/ppermute | solution.py:375
  17.8 1.2 %collective-permute-done.4.corner = bf16[80,192]{1,0:T(8,128)(2,1)S(1)} collective-permute-done((bf16[80,192]{1,0:T(8,128)(2,1)S(1)}, bf16[80,192]{1,0:T(8,128)(2,1)S(1)}, u32[]{:S(2)}, u32[]{:S(2)}) %collective-permute-start.4) | collective-permute-done | bytes 30752 | tf_op jit(solution)/shard_map/ppermute | solution.py:375
  19.0 0.0 collective-permute-done.3.across.refs_5_
  19.0 3.6 %forward.1 = (bf16[8,64,192]{2,1,0:T(8,128)(2,1)}, bf16[10,80,192]{2,1,0:T(8,128)(2,1)S(1)}, bf16[48,640]{1,0:T(8,128)(2,1)S(1)}, bf16[48,640]{1,0:T(8,128)(2,1)...) custom-call(bf16[8,64,192]{2,1,0:T(8,128)(2,1)S(1)} %get-tuple-element.33.masked, ...), custom_call_target="tpu_custom_call" | custom-call | flops 1610612736 | bytes 1048576 | tf_op jit(solution)/shard_map/forward/pallas_call | solution.py:346
  22.6 0.0 collective-permute-done.5.refs_6_
  22.6 1.1 %collective-permute-start.6 = (bf16[48,640]{1,0:T(8,128)(2,1)S(1)}, bf16[48,640]{1,0:T(8,128)(2,1)S(1)}, u32[]{:S(2)}, u32[]{:S(2)}) collective-permute-start(bf16[48,640]{1,0:T(8,128)(2,1)S(1)} %get-tuple-element.48), channel_id=1, source_target_pairs={{0,1},{1,0},{2,3},{3,2},{4,5},{5,4},{6,7},{7,6},{8,9},{9,8},{10,11... | collective-permute-start | bytes 184328 | tf_op jit(solution)/shard_map/ppermute | solution.py:375
  23.7 3.8 %collective-permute-start.7 = (bf16[48,640]{1,0:T(8,128)(2,1)S(1)}, bf16[48,640]{1,0:T(8,128)(2,1)S(1)}, u32[]{:S(2)}, u32[]{:S(2)}) collective-permute-start(bf16[48,640]{1,0:T(8,128)(2,1)S(1)} %get-tuple-element.49), channel_id=1, source_target_pairs={{0,4},{1,5},{2,6},{3,7},{4,0},{5,1},{6,2},{7,3},{8,12},{9,13},{10,... | collective-permute-start | bytes 184328 | tf_op jit(solution)/shard_map/ppermute | solution.py:375
  27.5 1.5 %collective-permute-start.8 = (bf16[48,640]{1,0:T(8,128)(2,1)S(1)}, bf16[48,640]{1,0:T(8,128)(2,1)S(1)}, u32[]{:S(2)}, u32[]{:S(2)}) collective-permute-start(bf16[48,640]{1,0:T(8,128)(2,1)S(1)} %get-tuple-element.50), channel_id=1, source_target_pairs={{0,5},{1,4},{2,7},{3,6},{4,1},{5,0},{6,3},{7,2},{8,13},{9,12},{10,... | collective-permute-start | bytes 184328 | tf_op jit(solution)/shard_map/ppermute | solution.py:375
  29.0 0.0 collective-permute-done.6.refs_1_
  29.0 0.7 %collective-permute-done.7.refs_2_ = bf16[48,640]{1,0:T(8,128)(2,1)S(1)} collective-permute-done((bf16[48,640]{1,0:T(8,128)(2,1)S(1)}, bf16[48,640]{1,0:T(8,128)(2,1)S(1)}, u32[]{:S(2)}, u32[]{:S(2)}) %collective-permute-start.7) | collective-permute-done | bytes 61472 | tf_op jit(solution)/shard_map/ppermute | solution.py:375
  29.7 2.9 %collective-permute-done.8.refs_3_ = bf16[48,640]{1,0:T(8,128)(2,1)S(1)} collective-permute-done((bf16[48,640]{1,0:T(8,128)(2,1)S(1)}, bf16[48,640]{1,0:T(8,128)(2,1)S(1)}, u32[]{:S(2)}, u32[]{:S(2)}) %collective-permute-start.8) | collective-permute-done | bytes 61472 | tf_op jit(solution)/shard_map/ppermute | solution.py:375
  32.7 0.0 collective-permute-done.9.refs_7_
  32.7 2.6 %kernel_gradient.1 = (f32[24,5184]{1,0:T(8,128)S(1)}, bf16[24,5184]{1,0:T(8,128)(2,1)S(1)}) custom-call(bf16[48,640]{1,0:T(8,128)(2,1)S(1)} %get-tuple-element.47.refs_0_, bf16[48,640]{1,0:T(8,128)(2,1)S(1)} %collective-permute-done.6.refs_1_, bf16[48,640]{1,0:T(8,128)(2,1)S(1)} %collective-permute-done.7.refs_2_, ...), custom_call_target="tpu_custom_call" | custom-call | flops 1358954496 | bytes 4194304 | tf_op jit(solution)/shard_map/kernel_gradient/pallas_call | solution.py:346
  35.2 0.1 collective-permute-start.10
  35.3 1.5 %collective-permute-done.10.other = bf16[24,5184]{1,0:T(8,128)(2,1)S(1)} collective-permute-done((bf16[24,5184]{1,0:T(8,128)(2,1)S(1)}, bf16[24,5184]{1,0:T(8,128)(2,1)S(1)}, u32[]{:S(2)}, u32[]{:S(2)}) %collective-permute-start.10) | collective-permute-done | bytes 248864 | tf_op jit(solution)/shard_map/ppermute | solution.py:375
  36.8 0.2 fold.1
  37.0 2.7 %collective-permute-start.11 = (bf16[8,3968]{1,0:T(8,128)(2,1)S(1)}, bf16[8,3968]{1,0:T(8,128)(2,1)S(1)}, u32[]{:S(2)}, u32[]{:S(2)}) collective-permute-start(bf16[8,3968]{1,0:T(8,128)(2,1)S(1)} %get-tuple-element.55), channel_id=1, source_target_pairs={{0,24},{8,16},{16,8},{24,0},{1,25},{9,17},{17,9},{25,1},{2,26},{10... | collective-permute-start | bytes 190472 | tf_op jit(solution)/shard_map/ppermute | solution.py:375
  39.7 0.5 collective-permute-start.12
  40.2 1.3 %collective-permute-start.13 = (bf16[8,3968]{1,0:T(8,128)(2,1)S(1)}, bf16[8,3968]{1,0:T(8,128)(2,1)S(1)}, u32[]{:S(2)}, u32[]{:S(2)}) collective-permute-start(bf16[8,3968]{1,0:T(8,128)(2,1)S(1)} %get-tuple-element.57), channel_id=1, source_target_pairs={{0,8},{8,0},{16,24},{24,16},{1,9},{9,1},{17,25},{25,17},{2,10},{10... | collective-permute-start | bytes 190472 | tf_op jit(solution)/shard_map/ppermute | solution.py:375
  41.5 2.7 %input_gradient.1 = bf16[8,64,192]{2,1,0:T(8,128)(2,1)} custom-call(bf16[10,80,192]{2,1,0:T(8,128)(2,1)S(1)} %get-tuple-element.42.gp, f32[8,64,128]{2,1,0:T(8,128)S(1)} %get-tuple-element.39.live, bf16[192,5184]{1,0:T(8,128)(2,1)S(1)} %bitcast.6), custom_call_target="tpu_custom_call" | custom-call | flops 1358954496 | bytes 4194304 | tf_op jit(solution)/shard_map/input_gradient/pallas_call | solution.py:346
  44.2 0.0 collective-permute-done.11.one
  44.2 2.2 %collective-permute-done.12.two = bf16[8,3968]{1,0:T(8,128)(2,1)S(1)} collective-permute-done((bf16[8,3968]{1,0:T(8,128)(2,1)S(1)}, bf16[8,3968]{1,0:T(8,128)(2,1)S(1)}, u32[]{:S(2)}, u32[]{:S(2)}) %collective-permute-start.12) | collective-permute-done | bytes 63520 | tf_op jit(solution)/shard_map/ppermute | solution.py:375
  46.4 0.0 collective-permute-done.13.three
  46.4 2.1 %collective-permute-start.14 = (bf16[8,3968]{1,0:T(8,128)(2,1)S(1)}, bf16[8,3968]{1,0:T(8,128)(2,1)S(1)}, u32[]{:S(2)}, u32[]{:S(2)}) collective-permute-start(bf16[8,3968]{1,0:T(8,128)(2,1)S(1)} %plane_sum.1.mine), channel_id=1, source_target_pairs={{0,1},{1,0},{2,3},{3,2},{4,5},{5,4},{6,7},{7,6},{8,9},{9,8},{10,11... | collective-permute-start | bytes 190472 | tf_op jit(solution)/shard_map/ppermute | solution.py:375
  48.5 2.2 %collective-permute-done.14.other = bf16[8,3968]{1,0:T(8,128)(2,1)S(1)} collective-permute-done((bf16[8,3968]{1,0:T(8,128)(2,1)S(1)}, bf16[8,3968]{1,0:T(8,128)(2,1)S(1)}, u32[]{:S(2)}, u32[]{:S(2)}) %collective-permute-start.14) | collective-permute-done | bytes 63520 | tf_op jit(solution)/shard_map/ppermute | solution.py:375
  50.7 0.8 %join.1 = f32[12,5184]{1,0:T(8,128)} custom-call(bf16[8,3968]{1,0:T(8,128)(2,1)S(1)} %plane_sum.1.mine, bf16[8,3968]{1,0:T(8,128)(2,1)S(1)} %collective-permute-done.14.other), custom_call_target="tpu_custom_call" | custom-call | flops 41472 | bytes 580608 | tf_op jit(solution)/shard_map/join/pallas_call | solution.py:346
  (2 shorter events, 0.1 us)
Async XLA Ops:
  0.6 1.0 %copy-start.2 = (bf16[8,8,8,192]{3,2,1,0:T(8,128)(2,1)S(1)}, bf16[8,8,8,192]{3,2,1,0:T(8,128)(2,1)}, u32[]{:S(2)}) copy-start(bf16[8,8,8,192]{3,2,1,0:T(8,128)(2,1)} %param.7) | copy-start | bytes 589828
  0.6 0.9 %copy-start.3 = (s32[8,8,8]{2,1,0:T(8,128)S(1)}, s32[8,8,8]{2,1,0:T(8,128)}, u32[]{:S(2)}) copy-start(s32[8,8,8]{2,1,0:T(8,128)} %mask.1) | copy-start | bytes 6148
  0.7 1.0 %copy-start.1 = (bf16[8,8,8,192]{3,2,1,0:T(8,128)(2,1)S(1)}, bf16[8,8,8,192]{3,2,1,0:T(8,128)(2,1)}, u32[]{:S(2)}) copy-start(bf16[8,8,8,192]{3,2,1,0:T(8,128)(2,1)} %param.4) | copy-start | bytes 589828
  0.7 9.0 %copy-start = (bf16[5184,192]{0,1:T(8,128)(2,1)S(1)}, bf16[5184,192]{0,1:T(8,128)(2,1)}, u32[]{:S(2)}) copy-start(bf16[5184,192]{0,1:T(8,128)(2,1)} %param.5) | copy-start | bytes 5971972
  2.0 17.0 %collective-permute-start.3 = (bf16[14,64,128]{2,1,0:T(8,128)(2,1)S(1)}, bf16[14,64,128]{2,1,0:T(8,128)(2,1)S(1)}, u32[]{:S(2)}, u32[]{:S(2)}) collective-permute-start(bf16[14,64,128]{2,1,0:T(8,128)(2,1)S(1)} %across.1), channel_id=1, source_target_pairs={{0,1},{1,0},{2,3},{3,2},{4,5},{5,4},{6,7},{7,6},{8,9},{9,8},{10,11... | collective-permute-start | bytes 688136 | tf_op jit(solution)/shard_map/ppermute | solution.py:375
  5.0 1.3 %collective-permute-start.1 = (bf16[3,64,192]{2,1,0:T(8,128)(2,1)S(1)}, bf16[3,64,192]{2,1,0:T(8,128)(2,1)S(1)}, u32[]{:S(2)}, u32[]{:S(2)}) collective-permute-start(bf16[3,64,192]{2,1,0:T(8,128)(2,1)S(1)} %get-tuple-element.36), channel_id=1, source_target_pairs={{0,2},{2,0},{4,6},{6,4},{8,10},{10,8},{12,14},{14,12},{16,18},{18,... | collective-permute-start | bytes 221192 | tf_op jit(solution)/shard_map/ppermute | solution.py:375
  5.0 7.2 %collective-permute-start = (bf16[3,64,192]{2,1,0:T(8,128)(2,1)S(1)}, bf16[3,64,192]{2,1,0:T(8,128)(2,1)S(1)}, u32[]{:S(2)}, u32[]{:S(2)}) collective-permute-start(bf16[3,64,192]{2,1,0:T(8,128)(2,1)S(1)} %get-tuple-element.35), channel_id=1, source_target_pairs={{0,2},{2,0},{4,6},{6,4},{8,10},{10,8},{12,14},{14,12},{16,18},{18,... | collective-permute-start | bytes 221192 | tf_op jit(solution)/shard_map/ppermute | solution.py:375
  6.3 7.4 %collective-permute-start.2 = (bf16[3,64,192]{2,1,0:T(8,128)(2,1)S(1)}, bf16[3,64,192]{2,1,0:T(8,128)(2,1)S(1)}, u32[]{:S(2)}, u32[]{:S(2)}) collective-permute-start(bf16[3,64,192]{2,1,0:T(8,128)(2,1)S(1)} %collective-permute-done.1), channel_id=1, source_target_pairs={{0,4},{4,8},{6,2},{8,12},{10,6},{12,16},{14,10},{16,20},{18,14},{2... | collective-permute-start | bytes 221192 | tf_op jit(solution)/shard_map/ppermute | solution.py:401
  10.6 12.0 %collective-permute-start.5 = (bf16[12,64,128]{2,1,0:T(8,128)(2,1)S(1)}, bf16[12,64,128]{2,1,0:T(8,128)(2,1)S(1)}, u32[]{:S(2)}, u32[]{:S(2)}) collective-permute-start(bf16[12,64,128]{2,1,0:T(8,128)(2,1)S(1)} %pack.1.refs_4_), channel_id=1, source_target_pairs={{0,4},{1,5},{2,6},{3,7},{4,0},{5,1},{6,2},{7,3},{8,12},{9,13},{10,... | collective-permute-start | bytes 589832 | tf_op jit(solution)/shard_map/ppermute | solution.py:375
  13.8 5.2 %collective-permute-start.4 = (bf16[80,192]{1,0:T(8,128)(2,1)S(1)}, bf16[80,192]{1,0:T(8,128)(2,1)S(1)}, u32[]{:S(2)}, u32[]{:S(2)}) collective-permute-start(bf16[80,192]{1,0:T(8,128)(2,1)S(1)} %corner.1), channel_id=1, source_target_pairs={{0,1},{1,0},{2,3},{3,2},{4,5},{5,4},{6,7},{7,6},{8,9},{9,8},{10,11... | collective-permute-start | bytes 92168 | tf_op jit(solution)/shard_map/ppermute | solution.py:375
  14.4 18.3 %collective-permute-start.9 = (bf16[12,64,128]{2,1,0:T(8,128)(2,1)S(1)}, bf16[12,64,128]{2,1,0:T(8,128)(2,1)S(1)}, u32[]{:S(2)}, u32[]{:S(2)}) collective-permute-start(bf16[12,64,128]{2,1,0:T(8,128)(2,1)S(1)} %pack.1.refs_4_), channel_id=1, source_target_pairs={{0,5},{1,4},{2,7},{3,6},{4,1},{5,0},{6,3},{7,2},{8,13},{9,12},{10,... | collective-permute-start | bytes 589832 | tf_op jit(solution)/shard_map/ppermute | solution.py:375
  22.6 6.4 %collective-permute-start.6 = (bf16[48,640]{1,0:T(8,128)(2,1)S(1)}, bf16[48,640]{1,0:T(8,128)(2,1)S(1)}, u32[]{:S(2)}, u32[]{:S(2)}) collective-permute-start(bf16[48,640]{1,0:T(8,128)(2,1)S(1)} %get-tuple-element.48), channel_id=1, source_target_pairs={{0,1},{1,0},{2,3},{3,2},{4,5},{5,4},{6,7},{7,6},{8,9},{9,8},{10,11... | collective-permute-start | bytes 184328 | tf_op jit(solution)/shard_map/ppermute | solution.py:375
  23.7 6.0 %collective-permute-start.7 = (bf16[48,640]{1,0:T(8,128)(2,1)S(1)}, bf16[48,640]{1,0:T(8,128)(2,1)S(1)}, u32[]{:S(2)}, u32[]{:S(2)}) collective-permute-start(bf16[48,640]{1,0:T(8,128)(2,1)S(1)} %get-tuple-element.49), channel_id=1, source_target_pairs={{0,4},{1,5},{2,6},{3,7},{4,0},{5,1},{6,2},{7,3},{8,12},{9,13},{10,... | collective-permute-start | bytes 184328 | tf_op jit(solution)/shard_map/ppermute | solution.py:375
  27.5 5.1 %collective-permute-start.8 = (bf16[48,640]{1,0:T(8,128)(2,1)S(1)}, bf16[48,640]{1,0:T(8,128)(2,1)S(1)}, u32[]{:S(2)}, u32[]{:S(2)}) collective-permute-start(bf16[48,640]{1,0:T(8,128)(2,1)S(1)} %get-tuple-element.50), channel_id=1, source_target_pairs={{0,5},{1,4},{2,7},{3,6},{4,1},{5,0},{6,3},{7,2},{8,13},{9,12},{10,... | collective-permute-start | bytes 184328 | tf_op jit(solution)/shard_map/ppermute | solution.py:375
  35.2 1.6 %collective-permute-start.10 = (bf16[24,5184]{1,0:T(8,128)(2,1)S(1)}, bf16[24,5184]{1,0:T(8,128)(2,1)S(1)}, u32[]{:S(2)}, u32[]{:S(2)}) collective-permute-start(bf16[24,5184]{1,0:T(8,128)(2,1)S(1)} %get-tuple-element.54), channel_id=1, source_target_pairs={{0,2},{1,3},{2,0},{3,1},{4,6},{5,7},{6,4},{7,5},{8,10},{9,11},{10,... | collective-permute-start | bytes 746504 | tf_op jit(solution)/shard_map/ppermute | solution.py:375
  37.0 7.1 %collective-permute-start.11 = (bf16[8,3968]{1,0:T(8,128)(2,1)S(1)}, bf16[8,3968]{1,0:T(8,128)(2,1)S(1)}, u32[]{:S(2)}, u32[]{:S(2)}) collective-permute-start(bf16[8,3968]{1,0:T(8,128)(2,1)S(1)} %get-tuple-element.55), channel_id=1, source_target_pairs={{0,24},{8,16},{16,8},{24,0},{1,25},{9,17},{17,9},{25,1},{2,26},{10... | collective-permute-start | bytes 190472 | tf_op jit(solution)/shard_map/ppermute | solution.py:375
  39.7 6.6 %collective-permute-start.12 = (bf16[8,3968]{1,0:T(8,128)(2,1)S(1)}, bf16[8,3968]{1,0:T(8,128)(2,1)S(1)}, u32[]{:S(2)}, u32[]{:S(2)}) collective-permute-start(bf16[8,3968]{1,0:T(8,128)(2,1)S(1)} %get-tuple-element.56), channel_id=1, source_target_pairs={{0,16},{8,24},{16,0},{24,8},{1,17},{9,25},{17,1},{25,9},{2,18},{10... | collective-permute-start | bytes 190472 | tf_op jit(solution)/shard_map/ppermute | solution.py:375
  40.2 6.2 %collective-permute-start.13 = (bf16[8,3968]{1,0:T(8,128)(2,1)S(1)}, bf16[8,3968]{1,0:T(8,128)(2,1)S(1)}, u32[]{:S(2)}, u32[]{:S(2)}) collective-permute-start(bf16[8,3968]{1,0:T(8,128)(2,1)S(1)} %get-tuple-element.57), channel_id=1, source_target_pairs={{0,8},{8,0},{16,24},{24,16},{1,9},{9,1},{17,25},{25,17},{2,10},{10... | collective-permute-start | bytes 190472 | tf_op jit(solution)/shard_map/ppermute | solution.py:375
  46.4 4.3 %collective-permute-start.14 = (bf16[8,3968]{1,0:T(8,128)(2,1)S(1)}, bf16[8,3968]{1,0:T(8,128)(2,1)S(1)}, u32[]{:S(2)}, u32[]{:S(2)}) collective-permute-start(bf16[8,3968]{1,0:T(8,128)(2,1)S(1)} %plane_sum.1.mine), channel_id=1, source_target_pairs={{0,1},{1,0},{2,3},{3,2},{4,5},{5,4},{6,7},{7,6},{8,9},{9,8},{10,11... | collective-permute-start | bytes 190472 | tf_op jit(solution)/shard_map/ppermute | solution.py:375

commit v13 on v12

--- a/solution.py
+++ b/solution.py
@@ -396,9 +396,8 @@
         pick,
     )
     near = swap(near, WIDE, 1, count)
-    steps = [(i, i + 2 - 4 * (i % 2)) for i in range(count)]
-    steps = [(i, j) for i, j in steps if 0 <= j < count]
-    far = lax.ppermute(swap(far, WIDE, 1, count), WIDE, steps)
+    ends = [min(max(((i + 1) ^ 1) - 1, 0), count - 1) for i in range(count)]
+    far = lax.ppermute(far, WIDE, list(enumerate(ends)))
     weight_rows = call(
         turn_kernel, "turn", 8, 1 << 20, 4 << 20, array((total, channels), bf16)
     )(weight.T)

time: 51.7 us -> 45.7 us (0.88)
  starting transfers between devices: 25.6 us -> 21.4 us
  waiting for transfers between devices: 13.2 us -> 11.3 us
    ppermute x1, starting transfers between devices: 3.39 us -> 0.66 us  [planes_local(): far = lax.ppermute(far, WIDE, list(enumerate(ends)))]
    ppermute x1, waiting for transfers between devices: 1.54 us -> 0.01 us  [planes_local(): far = lax.ppermute(far, WIDE, list(enumerate(ends)))]
    ppermute x14 -> x13, starting transfers between devices: 22.2 us -> 20.7 us  [swap(): return lax.ppermute(piece, axes, [(i, i ^ distance) for i in range(size)])]
    ppermute x14 -> x13, waiting for transfers between devices: 11.6 us -> 11.3 us  [swap(): return lax.ppermute(piece, axes, [(i, i ^ distance) for i in range(size)])]
  transfers between devices with their start and end apart: 15 -> 14, of which waited for: 8 -> 7; matrix products, arithmetic and copies ran while one was open for 0% -> 0% of each run, Pallas kernels for 14% -> 16%
where the time goes in v13:
time: 45.7 us; the launch traced here: 45.6 us
  starting transfers between devices  21.4 us (47%)
  waiting for transfers between devices  11.3 us (25%)
  Pallas kernels  11.2 us (25%)
  local copies, waits for them, and re-layouts  0.86 us (2%)
  between operations  0.74 us (2%)
    ppermute x13, starting transfers between devices, swap(): return lax.ppermute(piece, axes, [(i, i ^ distance) for i in range(size)])  20.7 us
    ppermute x13, waiting for transfers between devices, swap(): return lax.ppermute(piece, axes, [(i, i ^ distance) for i in range(size)])  11.3 us
    pallas_call x12, Pallas kernels, run(): pl.pallas_call(body, out_shape=out_shape, in_specs=in_specs or [spec] * l...  11.2 us
  transfers between devices with their start and end apart: 14, of which 7 were waited for; matrix products, arithmetic and copies ran while one was open for 0% of the time, Pallas kernels for 16%

profile of v13, /device:TPU:0, one launch (start us, length us, event | category | flops | bytes accessed | tf_op | source)
XLA Modules:
  0.0 45.6 jit_solution(1629959956701921581)
XLA Ops:
  0.6 0.0 copy-start.2
  0.6 0.0 copy-start.3
  0.7 0.0 copy-start.1
  0.7 0.0 copy-start
  0.7 0.2 pick.1.first
  0.8 0.7 %copy-done.2 = bf16[8,8,8,192]{3,2,1,0:T(8,128)(2,1)S(1)} copy-done((bf16[8,8,8,192]{3,2,1,0:T(8,128)(2,1)S(1)}, bf16[8,8,8,192]{3,2,1,0:T(8,128)(2,1)}, u32[]{:S(2)}) %copy-start.2) | copy-done | bytes 196632
  1.6 0.0 copy-done.3
  1.6 0.1 copy-done.1
  1.7 0.2 prepare.1
  1.9 0.1 across.1
  2.0 3.0 %collective-permute-start.2 = (bf16[14,64,128]{2,1,0:T(8,128)(2,1)S(1)}, bf16[14,64,128]{2,1,0:T(8,128)(2,1)S(1)}, u32[]{:S(2)}, u32[]{:S(2)}) collective-permute-start(bf16[14,64,128]{2,1,0:T(8,128)(2,1)S(1)} %across.1), channel_id=1, source_target_pairs={{0,1},{1,0},{2,3},{3,2},{4,5},{5,4},{6,7},{7,6},{8,9},{9,8},{10,11... | collective-permute-start | bytes 688136 | tf_op jit(solution)/shard_map/ppermute | solution.py:375
  5.0 0.0 collective-permute-start
  5.0 0.7 %collective-permute-start.1 = (bf16[3,64,192]{2,1,0:T(8,128)(2,1)S(1)}, bf16[3,64,192]{2,1,0:T(8,128)(2,1)S(1)}, u32[]{:S(2)}, u32[]{:S(2)}) collective-permute-start(bf16[3,64,192]{2,1,0:T(8,128)(2,1)S(1)} %get-tuple-element.36), channel_id=1, source_target_pairs={{0,0},{2,4},{4,2},{6,8},{8,6},{10,12},{12,10},{14,16},{16,14},{18,... | collective-permute-start | bytes 221192 | tf_op jit(solution)/shard_map/ppermute | solution.py:400
  5.7 0.0 copy-done
  5.7 0.8 %turn.1.after.weight = bf16[5184,192]{1,0:T(8,128)(2,1)S(1)} custom-call(bf16[192,5184]{1,0:T(8,128)(2,1)S(1)} %bitcast.5), custom_call_target="tpu_custom_call" | custom-call | flops 1048576 | bytes 4194304 | tf_op jit(solution)/shard_map/turn/pallas_call | solution.py:346
  6.5 0.1 pack.1.refs_4_
  6.5 3.4 %collective-permute-start.4 = (bf16[12,64,128]{2,1,0:T(8,128)(2,1)S(1)}, bf16[12,64,128]{2,1,0:T(8,128)(2,1)S(1)}, u32[]{:S(2)}, u32[]{:S(2)}) collective-permute-start(bf16[12,64,128]{2,1,0:T(8,128)(2,1)S(1)} %pack.1.refs_4_), channel_id=1, source_target_pairs={{0,4},{1,5},{2,6},{3,7},{4,0},{5,1},{6,2},{7,3},{8,12},{9,13},{10,... | collective-permute-start | bytes 589832 | tf_op jit(solution)/shard_map/ppermute | solution.py:375
  10.0 0.0 collective-permute-done.near
  10.0 0.0 collective-permute-done.1.far
  10.0 0.1 collective-permute-start.3
  10.2 3.8 %collective-permute-start.8 = (bf16[12,64,128]{2,1,0:T(8,128)(2,1)S(1)}, bf16[12,64,128]{2,1,0:T(8,128)(2,1)S(1)}, u32[]{:S(2)}, u32[]{:S(2)}) collective-permute-start(bf16[12,64,128]{2,1,0:T(8,128)(2,1)S(1)} %pack.1.refs_4_), channel_id=1, source_target_pairs={{0,5},{1,4},{2,7},{3,6},{4,1},{5,0},{6,3},{7,2},{8,13},{9,12},{10,... | collective-permute-start | bytes 589832 | tf_op jit(solution)/shard_map/ppermute | solution.py:375
  14.0 0.1 collective-permute-done.3.corner
  14.1 0.0 collective-permute-done.2.across.refs_5_
  14.1 3.6 %forward.1 = (bf16[8,64,192]{2,1,0:T(8,128)(2,1)}, bf16[10,80,192]{2,1,0:T(8,128)(2,1)S(1)}, bf16[48,640]{1,0:T(8,128)(2,1)S(1)}, bf16[48,640]{1,0:T(8,128)(2,1)...) custom-call(bf16[8,64,192]{2,1,0:T(8,128)(2,1)S(1)} %get-tuple-element.33.masked, ...), custom_call_target="tpu_custom_call" | custom-call | flops 1610612736 | bytes 1048576 | tf_op jit(solution)/shard_map/forward/pallas_call | solution.py:346
  17.7 0.0 collective-permute-done.4.refs_6_
  17.7 0.4 collective-permute-start.5
  18.1 2.5 %collective-permute-start.6 = (bf16[48,640]{1,0:T(8,128)(2,1)S(1)}, bf16[48,640]{1,0:T(8,128)(2,1)S(1)}, u32[]{:S(2)}, u32[]{:S(2)}) collective-permute-start(bf16[48,640]{1,0:T(8,128)(2,1)S(1)} %get-tuple-element.49), channel_id=1, source_target_pairs={{0,4},{1,5},{2,6},{3,7},{4,0},{5,1},{6,2},{7,3},{8,12},{9,13},{10,... | collective-permute-start | bytes 184328 | tf_op jit(solution)/shard_map/ppermute | solution.py:375
  20.7 0.9 %collective-permute-start.7 = (bf16[48,640]{1,0:T(8,128)(2,1)S(1)}, bf16[48,640]{1,0:T(8,128)(2,1)S(1)}, u32[]{:S(2)}, u32[]{:S(2)}) collective-permute-start(bf16[48,640]{1,0:T(8,128)(2,1)S(1)} %get-tuple-element.50), channel_id=1, source_target_pairs={{0,5},{1,4},{2,7},{3,6},{4,1},{5,0},{6,3},{7,2},{8,13},{9,12},{10,... | collective-permute-start | bytes 184328 | tf_op jit(solution)/shard_map/ppermute | solution.py:375
  21.6 0.0 collective-permute-done.8.refs_7_
  21.6 0.8 %collective-permute-done.5.refs_1_ = bf16[48,640]{1,0:T(8,128)(2,1)S(1)} collective-permute-done((bf16[48,640]{1,0:T(8,128)(2,1)S(1)}, bf16[48,640]{1,0:T(8,128)(2,1)S(1)}, u32[]{:S(2)}, u32[]{:S(2)}) %collective-permute-start.5) | collective-permute-done | bytes 61472 | tf_op jit(solution)/shard_map/ppermute | solution.py:375
  22.4 0.8 %collective-permute-done.6.refs_2_ = bf16[48,640]{1,0:T(8,128)(2,1)S(1)} collective-permute-done((bf16[48,640]{1,0:T(8,128)(2,1)S(1)}, bf16[48,640]{1,0:T(8,128)(2,1)S(1)}, u32[]{:S(2)}, u32[]{:S(2)}) %collective-permute-start.6) | collective-permute-done | bytes 61472 | tf_op jit(solution)/shard_map/ppermute | solution.py:375
  23.2 2.6 %collective-permute-done.7.refs_3_ = bf16[48,640]{1,0:T(8,128)(2,1)S(1)} collective-permute-done((bf16[48,640]{1,0:T(8,128)(2,1)S(1)}, bf16[48,640]{1,0:T(8,128)(2,1)S(1)}, u32[]{:S(2)}, u32[]{:S(2)}) %collective-permute-start.7) | collective-permute-done | bytes 61472 | tf_op jit(solution)/shard_map/ppermute | solution.py:375
  25.8 2.6 %kernel_gradient.1 = (f32[24,5184]{1,0:T(8,128)S(1)}, bf16[24,5184]{1,0:T(8,128)(2,1)S(1)}) custom-call(bf16[48,640]{1,0:T(8,128)(2,1)S(1)} %get-tuple-element.47.refs_0_, bf16[48,640]{1,0:T(8,128)(2,1)S(1)} %collective-permute-done.5.refs_1_, bf16[48,640]{1,0:T(8,128)(2,1)S(1)} %collective-permute-done.6.refs_2_, ...), custom_call_target="tpu_custom_call" | custom-call | flops 1358954496 | bytes 4194304 | tf_op jit(solution)/shard_map/kernel_gradient/pallas_call | solution.py:346
  28.4 0.1 collective-permute-start.9
  28.5 1.5 %collective-permute-done.9.other = bf16[24,5184]{1,0:T(8,128)(2,1)S(1)} collective-permute-done((bf16[24,5184]{1,0:T(8,128)(2,1)S(1)}, bf16[24,5184]{1,0:T(8,128)(2,1)S(1)}, u32[]{:S(2)}, u32[]{:S(2)}) %collective-permute-start.9) | collective-permute-done | bytes 248864 | tf_op jit(solution)/shard_map/ppermute | solution.py:375
  30.0 0.2 fold.1
  30.2 4.5 %collective-permute-start.10 = (bf16[8,3968]{1,0:T(8,128)(2,1)S(1)}, bf16[8,3968]{1,0:T(8,128)(2,1)S(1)}, u32[]{:S(2)}, u32[]{:S(2)}) collective-permute-start(bf16[8,3968]{1,0:T(8,128)(2,1)S(1)} %get-tuple-element.55), channel_id=1, source_target_pairs={{0,24},{8,16},{16,8},{24,0},{1,25},{9,17},{17,9},{25,1},{2,26},{10... | collective-permute-start | bytes 190472 | tf_op jit(solution)/shard_map/ppermute | solution.py:375
  34.7 0.0 collective-permute-start.11
  34.7 0.6 %collective-permute-start.12 = (bf16[8,3968]{1,0:T(8,128)(2,1)S(1)}, bf16[8,3968]{1,0:T(8,128)(2,1)S(1)}, u32[]{:S(2)}, u32[]{:S(2)}) collective-permute-start(bf16[8,3968]{1,0:T(8,128)(2,1)S(1)} %get-tuple-element.57), channel_id=1, source_target_pairs={{0,8},{8,0},{16,24},{24,16},{1,9},{9,1},{17,25},{25,17},{2,10},{10... | collective-permute-start | bytes 190472 | tf_op jit(solution)/shard_map/ppermute | solution.py:375
  35.3 2.7 %input_gradient.1 = bf16[8,64,192]{2,1,0:T(8,128)(2,1)} custom-call(bf16[10,80,192]{2,1,0:T(8,128)(2,1)S(1)} %get-tuple-element.42.gp, f32[8,64,128]{2,1,0:T(8,128)S(1)} %get-tuple-element.39.live, bf16[192,5184]{1,0:T(8,128)(2,1)S(1)} %bitcast.6), custom_call_target="tpu_custom_call" | custom-call | flops 1358954496 | bytes 4194304 | tf_op jit(solution)/shard_map/input_gradient/pallas_call | solution.py:346
  38.0 0.0 collective-permute-done.10.one
  38.0 2.4 %collective-permute-done.11.two = bf16[8,3968]{1,0:T(8,128)(2,1)S(1)} collective-permute-done((bf16[8,3968]{1,0:T(8,128)(2,1)S(1)}, bf16[8,3968]{1,0:T(8,128)(2,1)S(1)}, u32[]{:S(2)}, u32[]{:S(2)}) %collective-permute-start.11) | collective-permute-done | bytes 63520 | tf_op jit(solution)/shard_map/ppermute | solution.py:375
  40.4 0.0 collective-permute-done.12.three
  40.4 1.2 %collective-permute-start.13 = (bf16[8,3968]{1,0:T(8,128)(2,1)S(1)}, bf16[8,3968]{1,0:T(8,128)(2,1)S(1)}, u32[]{:S(2)}, u32[]{:S(2)}) collective-permute-start(bf16[8,3968]{1,0:T(8,128)(2,1)S(1)} %plane_sum.1.mine), channel_id=1, source_target_pairs={{0,1},{1,0},{2,3},{3,2},{4,5},{5,4},{6,7},{7,6},{8,9},{9,8},{10,11... | collective-permute-start | bytes 190472 | tf_op jit(solution)/shard_map/ppermute | solution.py:375
  41.7 3.1 %collective-permute-done.13.other = bf16[8,3968]{1,0:T(8,128)(2,1)S(1)} collective-permute-done((bf16[8,3968]{1,0:T(8,128)(2,1)S(1)}, bf16[8,3968]{1,0:T(8,128)(2,1)S(1)}, u32[]{:S(2)}, u32[]{:S(2)}) %collective-permute-start.13) | collective-permute-done | bytes 63520 | tf_op jit(solution)/shard_map/ppermute | solution.py:375
  44.8 0.8 %join.1 = f32[12,5184]{1,0:T(8,128)} custom-call(bf16[8,3968]{1,0:T(8,128)(2,1)S(1)} %plane_sum.1.mine, bf16[8,3968]{1,0:T(8,128)(2,1)S(1)} %collective-permute-done.13.other), custom_call_target="tpu_custom_call" | custom-call | flops 41472 | bytes 580608 | tf_op jit(solution)/shard_map/join/pallas_call | solution.py:346
  (2 shorter events, 0.1 us)
Async XLA Ops:
  0.6 1.0 %copy-start.2 = (bf16[8,8,8,192]{3,2,1,0:T(8,128)(2,1)S(1)}, bf16[8,8,8,192]{3,2,1,0:T(8,128)(2,1)}, u32[]{:S(2)}) copy-start(bf16[8,8,8,192]{3,2,1,0:T(8,128)(2,1)} %param.7) | copy-start | bytes 589828
  0.6 0.9 %copy-start.3 = (s32[8,8,8]{2,1,0:T(8,128)S(1)}, s32[8,8,8]{2,1,0:T(8,128)}, u32[]{:S(2)}) copy-start(s32[8,8,8]{2,1,0:T(8,128)} %mask.1) | copy-start | bytes 6148
  0.7 1.0 %copy-start.1 = (bf16[8,8,8,192]{3,2,1,0:T(8,128)(2,1)S(1)}, bf16[8,8,8,192]{3,2,1,0:T(8,128)(2,1)}, u32[]{:S(2)}) copy-start(bf16[8,8,8,192]{3,2,1,0:T(8,128)(2,1)} %param.4) | copy-start | bytes 589828
  0.7 5.0 %copy-start = (bf16[5184,192]{0,1:T(8,128)(2,1)S(1)}, bf16[5184,192]{0,1:T(8,128)(2,1)}, u32[]{:S(2)}) copy-start(bf16[5184,192]{0,1:T(8,128)(2,1)} %param.5) | copy-start | bytes 5971972
  2.0 12.1 %collective-permute-start.2 = (bf16[14,64,128]{2,1,0:T(8,128)(2,1)S(1)}, bf16[14,64,128]{2,1,0:T(8,128)(2,1)S(1)}, u32[]{:S(2)}, u32[]{:S(2)}) collective-permute-start(bf16[14,64,128]{2,1,0:T(8,128)(2,1)S(1)} %across.1), channel_id=1, source_target_pairs={{0,1},{1,0},{2,3},{3,2},{4,5},{5,4},{6,7},{7,6},{8,9},{9,8},{10,11... | collective-permute-start | bytes 688136 | tf_op jit(solution)/shard_map/ppermute | solution.py:375
  5.0 5.0 %collective-permute-start = (bf16[3,64,192]{2,1,0:T(8,128)(2,1)S(1)}, bf16[3,64,192]{2,1,0:T(8,128)(2,1)S(1)}, u32[]{:S(2)}, u32[]{:S(2)}) collective-permute-start(bf16[3,64,192]{2,1,0:T(8,128)(2,1)S(1)} %get-tuple-element.35), channel_id=1, source_target_pairs={{0,2},{2,0},{4,6},{6,4},{8,10},{10,8},{12,14},{14,12},{16,18},{18,... | collective-permute-start | bytes 221192 | tf_op jit(solution)/shard_map/ppermute | solution.py:375
  5.0 5.0 %collective-permute-start.1 = (bf16[3,64,192]{2,1,0:T(8,128)(2,1)S(1)}, bf16[3,64,192]{2,1,0:T(8,128)(2,1)S(1)}, u32[]{:S(2)}, u32[]{:S(2)}) collective-permute-start(bf16[3,64,192]{2,1,0:T(8,128)(2,1)S(1)} %get-tuple-element.36), channel_id=1, source_target_pairs={{0,0},{2,4},{4,2},{6,8},{8,6},{10,12},{12,10},{14,16},{16,14},{18,... | collective-permute-start | bytes 221192 | tf_op jit(solution)/shard_map/ppermute | solution.py:400
  6.5 11.2 %collective-permute-start.4 = (bf16[12,64,128]{2,1,0:T(8,128)(2,1)S(1)}, bf16[12,64,128]{2,1,0:T(8,128)(2,1)S(1)}, u32[]{:S(2)}, u32[]{:S(2)}) collective-permute-start(bf16[12,64,128]{2,1,0:T(8,128)(2,1)S(1)} %pack.1.refs_4_), channel_id=1, source_target_pairs={{0,4},{1,5},{2,6},{3,7},{4,0},{5,1},{6,2},{7,3},{8,12},{9,13},{10,... | collective-permute-start | bytes 589832 | tf_op jit(solution)/shard_map/ppermute | solution.py:375
  10.0 4.1 %collective-permute-start.3 = (bf16[80,192]{1,0:T(8,128)(2,1)S(1)}, bf16[80,192]{1,0:T(8,128)(2,1)S(1)}, u32[]{:S(2)}, u32[]{:S(2)}) collective-permute-start(bf16[80,192]{1,0:T(8,128)(2,1)S(1)} %corner.1), channel_id=1, source_target_pairs={{0,1},{1,0},{2,3},{3,2},{4,5},{5,4},{6,7},{7,6},{8,9},{9,8},{10,11... | collective-permute-start | bytes 92168 | tf_op jit(solution)/shard_map/ppermute | solution.py:375
  10.2 11.4 %collective-permute-start.8 = (bf16[12,64,128]{2,1,0:T(8,128)(2,1)S(1)}, bf16[12,64,128]{2,1,0:T(8,128)(2,1)S(1)}, u32[]{:S(2)}, u32[]{:S(2)}) collective-permute-start(bf16[12,64,128]{2,1,0:T(8,128)(2,1)S(1)} %pack.1.refs_4_), channel_id=1, source_target_pairs={{0,5},{1,4},{2,7},{3,6},{4,1},{5,0},{6,3},{7,2},{8,13},{9,12},{10,... | collective-permute-start | bytes 589832 | tf_op jit(solution)/shard_map/ppermute | solution.py:375
  17.7 4.7 %collective-permute-start.5 = (bf16[48,640]{1,0:T(8,128)(2,1)S(1)}, bf16[48,640]{1,0:T(8,128)(2,1)S(1)}, u32[]{:S(2)}, u32[]{:S(2)}) collective-permute-start(bf16[48,640]{1,0:T(8,128)(2,1)S(1)} %get-tuple-element.48), channel_id=1, source_target_pairs={{0,1},{1,0},{2,3},{3,2},{4,5},{5,4},{6,7},{7,6},{8,9},{9,8},{10,11... | collective-permute-start | bytes 184328 | tf_op jit(solution)/shard_map/ppermute | solution.py:375
  18.1 5.1 %collective-permute-start.6 = (bf16[48,640]{1,0:T(8,128)(2,1)S(1)}, bf16[48,640]{1,0:T(8,128)(2,1)S(1)}, u32[]{:S(2)}, u32[]{:S(2)}) collective-permute-start(bf16[48,640]{1,0:T(8,128)(2,1)S(1)} %get-tuple-element.49), channel_id=1, source_target_pairs={{0,4},{1,5},{2,6},{3,7},{4,0},{5,1},{6,2},{7,3},{8,12},{9,13},{10,... | collective-permute-start | bytes 184328 | tf_op jit(solution)/shard_map/ppermute | solution.py:375
  20.7 5.1 %collective-permute-start.7 = (bf16[48,640]{1,0:T(8,128)(2,1)S(1)}, bf16[48,640]{1,0:T(8,128)(2,1)S(1)}, u32[]{:S(2)}, u32[]{:S(2)}) collective-permute-start(bf16[48,640]{1,0:T(8,128)(2,1)S(1)} %get-tuple-element.50), channel_id=1, source_target_pairs={{0,5},{1,4},{2,7},{3,6},{4,1},{5,0},{6,3},{7,2},{8,13},{9,12},{10,... | collective-permute-start | bytes 184328 | tf_op jit(solution)/shard_map/ppermute | solution.py:375
  28.4 1.6 %collective-permute-start.9 = (bf16[24,5184]{1,0:T(8,128)(2,1)S(1)}, bf16[24,5184]{1,0:T(8,128)(2,1)S(1)}, u32[]{:S(2)}, u32[]{:S(2)}) collective-permute-start(bf16[24,5184]{1,0:T(8,128)(2,1)S(1)} %get-tuple-element.54), channel_id=1, source_target_pairs={{0,2},{1,3},{2,0},{3,1},{4,6},{5,7},{6,4},{7,5},{8,10},{9,11},{10,... | collective-permute-start | bytes 746504 | tf_op jit(solution)/shard_map/ppermute | solution.py:375
  30.2 7.8 %collective-permute-start.10 = (bf16[8,3968]{1,0:T(8,128)(2,1)S(1)}, bf16[8,3968]{1,0:T(8,128)(2,1)S(1)}, u32[]{:S(2)}, u32[]{:S(2)}) collective-permute-start(bf16[8,3968]{1,0:T(8,128)(2,1)S(1)} %get-tuple-element.55), channel_id=1, source_target_pairs={{0,24},{8,16},{16,8},{24,0},{1,25},{9,17},{17,9},{25,1},{2,26},{10... | collective-permute-start | bytes 190472 | tf_op jit(solution)/shard_map/ppermute | solution.py:375
  34.7 5.7 %collective-permute-start.11 = (bf16[8,3968]{1,0:T(8,128)(2,1)S(1)}, bf16[8,3968]{1,0:T(8,128)(2,1)S(1)}, u32[]{:S(2)}, u32[]{:S(2)}) collective-permute-start(bf16[8,3968]{1,0:T(8,128)(2,1)S(1)} %get-tuple-element.56), channel_id=1, source_target_pairs={{0,16},{8,24},{16,0},{24,8},{1,17},{9,25},{17,1},{25,9},{2,18},{10... | collective-permute-start | bytes 190472 | tf_op jit(solution)/shard_map/ppermute | solution.py:375
  34.7 5.7 %collective-permute-start.12 = (bf16[8,3968]{1,0:T(8,128)(2,1)S(1)}, bf16[8,3968]{1,0:T(8,128)(2,1)S(1)}, u32[]{:S(2)}, u32[]{:S(2)}) collective-permute-start(bf16[8,3968]{1,0:T(8,128)(2,1)S(1)} %get-tuple-element.57), channel_id=1, source_target_pairs={{0,8},{8,0},{16,24},{24,16},{1,9},{9,1},{17,25},{25,17},{2,10},{10... | collective-permute-start | bytes 190472 | tf_op jit(solution)/shard_map/ppermute | solution.py:375
  40.4 4.3 %collective-permute-start.13 = (bf16[8,3968]{1,0:T(8,128)(2,1)S(1)}, bf16[8,3968]{1,0:T(8,128)(2,1)S(1)}, u32[]{:S(2)}, u32[]{:S(2)}) collective-permute-start(bf16[8,3968]{1,0:T(8,128)(2,1)S(1)} %plane_sum.1.mine), channel_id=1, source_target_pairs={{0,1},{1,0},{2,3},{3,2},{4,5},{5,4},{6,7},{7,6},{8,9},{9,8},{10,11... | collective-permute-start | bytes 190472 | tf_op jit(solution)/shard_map/ppermute | solution.py:375

commit v14 on v13

--- a/solution.py
+++ b/solution.py
@@ -71,6 +71,18 @@
     return jnp.concatenate([block, tail], axis=1)[:, :total]
 
 
+def rows_of_128(block):
+    half = block.shape[0] // 2
+    rest = jnp.concatenate([block[:half, 128:], block[half:, 128:]], axis=1)
+    return jnp.concatenate([block[:, :128], rest], axis=0)
+
+
+def rows_of_192(block):
+    count = block.shape[0] * 2 // 3
+    rest = jnp.concatenate([block[count:, :64], block[count:, 64:]], axis=0)
+    return jnp.concatenate([block[:count], rest], axis=1)
+
+
 def prepare_kernel(features, cot, mask, first, masked_ref, cot_ref, live_ref, near_ref, far_ref):
     width, rows, channels = features.shape
     f32 = jnp.float32
@@ -81,48 +93,46 @@
     cot_ref[...] = (cot[...].astype(f32) * live).astype(jnp.bfloat16)
     odd = lax.rem(position()[2], 2)
     for ref, upper in ((near_ref, 1 - odd), (far_ref, odd)):
-        ref[0:2] = masked_ref[pl.ds(upper * (width - 2), 2)]
-        ref[2:3] = cot_ref[pl.ds(upper * (width - 1), 1)]
-
-
-def rows_of_128(masked, out_ref):
-    width = masked.shape[0]
-    half = width // 2
-    rest = jnp.concatenate([masked[:half, :, 128:], masked[half:, :, 128:]], axis=2)
-    out_ref[:width] = masked[:, :, :128]
-    out_ref[width : width + half] = rest
+        slabs = [
+            masked_ref[pl.ds(upper * (width - 2), 2)],
+            cot_ref[pl.ds(upper * (width - 1), 1)],
+        ]
+        slabs = jnp.concatenate(slabs, axis=0).astype(f32).reshape(3 * rows, channels)
+        ref[...] = rows_of_128(slabs).astype(jnp.bfloat16)
 
 
 def pack_kernel(masked, after, packed_ref):
-    rows_of_128(masked, packed_ref)
+    count, channels = packed_ref.shape[0] * 128 // masked.shape[2], masked.shape[2]
+    block = masked[...].reshape(count, channels)
+    packed_ref[...] = rows_of_128(block)
 
 
 def across_kernel(masked, cot, across_ref):
     width, rows, channels = masked.shape
-    rows_of_128(masked, across_ref)
-    count = across_ref.shape[0] - 2
+    packed = rows_of_128(masked[...].reshape(width * rows, channels))
+    across_ref[: packed.shape[0]] = packed
     ahead = position()[3] == 0
     grown = cot[...].astype(jnp.float32)
     strip = jnp.where(ahead, grown[:, rows - DEPTH :], grown[:, :DEPTH])
-    strip = strip.reshape(width * DEPTH, channels)
-    rest = jnp.concatenate([strip[:, 128:], jnp.zeros_like(strip[:, 128:])], axis=1)
-    across_ref[count] = strip[:, :128].astype(jnp.bfloat16)
-    across_ref[count + 1] = rest.astype(jnp.bfloat16)
+    strip = rows_of_128(strip.reshape(width * DEPTH, channels))
+    across_ref[packed.shape[0] :] = strip.astype(jnp.bfloat16)
 
 
 def corner_kernel(near, far, out_ref, edge):
-    _, rows, channels = near.shape
+    _, slabs, rows, channels = edge.shape
     _, _, quad, side = position()
     odd = lax.rem(quad, 2)
-    edge[odd] = far[...]
-    edge[1 - odd] = near[...]
+    f32 = jnp.float32
+    edge[odd] = rows_of_192(far[...].astype(f32)).reshape(edge.shape[1:])
+    edge[1 - odd] = rows_of_192(near[...].astype(f32)).reshape(edge.shape[1:])
     halo = 2 * DEPTH
     ahead = side == 0
-    held = edge[...].astype(jnp.float32)
-    strip = jnp.where(ahead, held[:, :2, rows - halo :], held[:, :2, :halo])
-    cots = jnp.where(ahead, held[:, 2, rows - DEPTH :], held[:, 2, :DEPTH])
-    out_ref[: 4 * halo] = strip.reshape(4 * halo, channels).astype(jnp.bfloat16)
-    out_ref[4 * halo :] = cots.reshape(2 * DEPTH, channels).astype(jnp.bfloat16)
+    strip = jnp.where(ahead, edge[:, :2, rows - halo :], edge[:, :2, :halo])
+    cots = jnp.where(ahead, edge[:, 2, rows - DEPTH :], edge[:, 2, :DEPTH])
+    both = [strip.reshape(4 * halo, channels), cots.reshape(2 * DEPTH, channels)]
+    both = rows_of_128(jnp.concatenate(both, axis=0))
+    blank = jnp.zeros((out_ref.shape[0] - both.shape[0], 128), f32)
+    out_ref[...] = jnp.concatenate([both, blank], axis=0).astype(jnp.bfloat16)
 
 
 def turn_kernel(weight, out_ref):
@@ -152,19 +162,22 @@
     mid = rows + 2 * DEPTH
     span = width + 4
     odd = lax.rem(quad, 2)
-    edge[odd] = far[...]
-    edge[1 - odd] = near[...]
-    left, right = edge[0].astype(f32) * use_left, edge[1].astype(f32) * use_right
-    corners = corner[: 4 * halo].astype(f32).reshape(2, 2, halo, channels)
+    edge[odd] = rows_of_192(far[...].astype(f32)).reshape(edge.shape[1:])
+    edge[1 - odd] = rows_of_192(near[...].astype(f32)).reshape(edge.shape[1:])
+    left, right = edge[0] * use_left, edge[1] * use_right
+    count = 4 * halo + 2 * DEPTH
+    both = rows_of_192(corner[...].astype(f32)[: count * channels // 128])
+    corners = both[: 4 * halo].reshape(2, 2, halo, channels)
     lower, upper = corners[0] * use_left, corners[1] * use_right
-    ends = corner[4 * halo :].astype(f32).reshape(2, 1, DEPTH, channels)
+    ends = both[4 * halo :].reshape(2, 1, DEPTH, channels)
     ext[0:2, halo : halo + rows, :] = left[0:2]
     ext[2 : 2 + width, halo : halo + rows, :] = masked[...].astype(f32)
     ext[2 + width :, halo : halo + rows, :] = right[0:2]
     half = width // 2
     ahead = side == 0
-    held = across[...].astype(f32)
-    brick = jnp.where(ahead, held[: width + half, :halo], held[: width + half, rows - halo :])
+    count = width * rows * channels // 128
+    held = across[:count].astype(f32).reshape(width + half, rows, 128)
+    brick = jnp.where(ahead, held[:, :halo], held[:, rows - halo :])
     rest = jnp.concatenate([brick[width:, :, :64], brick[width:, :, 64:]], axis=0)
     beside = jnp.concatenate([brick[:width], rest], axis=2)
     for use, start in ((use_low, 0), (use_high, halo + rows)):
@@ -187,16 +200,14 @@
             weight[a * nine : (a + 1) * nine, :],
             preferred_element_type=f32,
         )
-    sig = jax.nn.sigmoid(pre)
+    sig = 0.5 * jnp.tanh(0.5 * pre) + 0.5
     act = (pre * sig).reshape(width + 2, mid, channels)[1 : 1 + width, DEPTH : DEPTH + rows]
     act_ref[...] = (act * live[:, :, 0:1]).astype(jnp.bfloat16)
     slope = (sig * (1.0 + pre * (1.0 - sig))).reshape(width + 2, mid, channels)
     beyond = jnp.concatenate(
         [
             ends[0] * use_left,
-            jnp.concatenate([held[width + half], held[width + half + 1, :, :64]], axis=1).reshape(
-                width, DEPTH, channels
-            ),
+            rows_of_192(across[count:].astype(f32)).reshape(width, DEPTH, channels),
             ends[1] * use_right,
         ],
         axis=0,
@@ -260,8 +271,8 @@
         at_rows = pl.ds(pl.multiple_of(sided * half, half), half)
         for x in range(per):
             shift = 64 * (x // (per // 2))
-            rest = bricks[i][per + x % (per // 2)]
-            masked[block, x, at_rows, :128] = bricks[i][x]
+            rest = bricks[i][pl.ds((per + x % (per // 2)) * half, half)]
+            masked[block, x, at_rows, :128] = bricks[i][pl.ds(x * half, half)]
             masked[block, x, at_rows, 128:] = rest[:, shift : shift + 64]
     at = lax.broadcasted_iota(jnp.int32, (group, lane), 1)
     y, z = at // DEPTH, at % DEPTH
@@ -378,7 +389,8 @@
         return swap(piece, ("quad", "narrow"), distance, MEMBERS)
 
     brick = array((width, rows, channels), bf16)
-    slab = array((3, rows, channels), bf16)
+    slab = array((3 * rows * channels // 128, 128), bf16)
+    slabs = (2, 3, rows, channels)
     pick = call(
         functools.partial(pick_kernel, planes), "pick", 4, 1 << 32, 1 << 16,
         array((MEMBERS * group, channels), bf16),
@@ -401,20 +413,21 @@
     weight_rows = call(
         turn_kernel, "turn", 8, 1 << 20, 4 << 20, array((total, channels), bf16)
     )(weight.T)
-    slabs = width * channels // 128
+    count_128 = width * rows * channels // 128
+    strip_128 = width * DEPTH * channels // 128
     across = call(
-        across_kernel, "across", 4, 1 << 16, 1 << 19, array((slabs + 2, rows, 128), bf16)
+        across_kernel, "across", 4, 1 << 16, 1 << 19, array((count_128 + strip_128, 128), bf16)
     )(masked, cot)
     across = in_plane(across, CHIPS[1])
     packed = call(
-        pack_kernel, "pack", 4, 1 << 16, 1 << 19, array((slabs, rows, 128), bf16), (),
+        pack_kernel, "pack", 4, 1 << 16, 1 << 19, array((count_128, 128), bf16), (),
         [vmem, pl.BlockSpec(memory_space=pl.ANY)],
     )(masked, weight_rows)
     near, far, weight_rows, late = lax.optimization_barrier((near, far, weight_rows, packed))
     corner = call(
         corner_kernel, "corner", 4, 1 << 16, 1 << 18,
-        array((4 * halo + 2 * DEPTH, channels), bf16),
-        (pltpu.VMEM((2,) + slab.shape, bf16),),
+        array((128, 128), bf16),
+        (pltpu.VMEM(slabs, f32),),
     )(near, far)
     corner = in_plane(corner, 1)
     bricks = [packed, across, in_plane(packed, CHIPS[2]), in_plane(late, CHIPS[3])]
@@ -426,7 +439,7 @@
         + (array((2 * group, span), bf16),) * len(CHIPS),
         (
             pltpu.VMEM((width + 4, rows + 2 * halo, channels), f32),
-            pltpu.VMEM((2,) + slab.shape, bf16),
+            pltpu.VMEM(slabs, f32),
             pltpu.VMEM((width + 4, mid, 9 * channels), bf16),
             pltpu.VMEM((MEMBERS, group, span), f32),
         ),

time: 45.7 us -> 45 us (0.985)
  starting transfers between devices: 21.4 us -> 20.2 us
    ppermute x13, starting transfers between devices: 20.7 us -> 19.6 us  [swap(): return lax.ppermute(piece, axes, [(i, i ^ distance) for i in range(size)])]
where the time goes in v14:
time: 45 us; the launch traced here: 44.8 us
  starting transfers between devices  20.2 us (45%)
  Pallas kernels  11.5 us (26%)
  waiting for transfers between devices  11.5 us (26%)
  local copies, waits for them, and re-layouts  0.86 us (2%)
  between operations  0.73 us (2%)
    ppermute x13, starting transfers between devices, swap(): return lax.ppermute(piece, axes, [(i, i ^ distance) for i in range(size)])  19.6 us
    ppermute x13, waiting for transfers between devices, swap(): return lax.ppermute(piece, axes, [(i, i ^ distance) for i in range(size)])  11.5 us
    pallas_call x12, Pallas kernels, run(): pl.pallas_call(body, out_shape=out_shape, in_specs=in_specs or [spec] * l...  11.5 us
  transfers between devices with their start and end apart: 14, of which 7 were waited for; matrix products, arithmetic and copies ran while one was open for 0% of the time, Pallas kernels for 16%

profile of v14, /device:TPU:0, one launch (start us, length us, event | category | flops | bytes accessed | tf_op | source)
XLA Modules:
  0.0 44.8 jit_solution(8010870737225455097)
XLA Ops:
  0.6 0.0 copy-start.2
  0.6 0.0 copy-start.3
  0.7 0.0 copy-start.1
  0.7 0.0 copy-start
  0.7 0.2 pick.1.first
  0.8 0.7 %copy-done.2 = bf16[8,8,8,192]{3,2,1,0:T(8,128)(2,1)S(1)} copy-done((bf16[8,8,8,192]{3,2,1,0:T(8,128)(2,1)S(1)}, bf16[8,8,8,192]{3,2,1,0:T(8,128)(2,1)}, u32[]{:S(2)}) %copy-start.2) | copy-done | bytes 196632
  1.6 0.0 copy-done.3
  1.6 0.1 copy-done.1
  1.7 0.2 prepare.1
  1.9 0.1 across.1
  2.0 3.0 %collective-permute-start.2 = (bf16[864,128]{1,0:T(8,128)(2,1)S(1)}, bf16[864,128]{1,0:T(8,128)(2,1)S(1)}, u32[]{:S(2)}, u32[]{:S(2)}) collective-permute-start(bf16[864,128]{1,0:T(8,128)(2,1)S(1)} %across.1), channel_id=1, source_target_pairs={{0,1},{1,0},{2,3},{3,2},{4,5},{5,4},{6,7},{7,6},{8,9},{9,8},{10,11... | collective-permute-start | bytes 663560 | tf_op jit(solution)/shard_map/ppermute | solution.py:386
  5.0 0.0 collective-permute-start
  5.0 0.7 %collective-permute-start.1 = (bf16[288,128]{1,0:T(8,128)(2,1)S(1)}, bf16[288,128]{1,0:T(8,128)(2,1)S(1)}, u32[]{:S(2)}, u32[]{:S(2)}) collective-permute-start(bf16[288,128]{1,0:T(8,128)(2,1)S(1)} %get-tuple-element.36), channel_id=1, source_target_pairs={{0,0},{2,4},{4,2},{6,8},{8,6},{10,12},{12,10},{14,16},{16,14},{18,... | collective-permute-start | bytes 221192 | tf_op jit(solution)/shard_map/ppermute | solution.py:412
  5.7 0.0 copy-done
  5.7 0.8 %turn.1.after.weight = bf16[5184,192]{1,0:T(8,128)(2,1)S(1)} custom-call(bf16[192,5184]{1,0:T(8,128)(2,1)S(1)} %bitcast.5), custom_call_target="tpu_custom_call" | custom-call | flops 1048576 | bytes 4194304 | tf_op jit(solution)/shard_map/turn/pallas_call | solution.py:357
  6.5 0.1 pack.1.refs_4_
  6.6 3.4 %collective-permute-start.4 = (bf16[768,128]{1,0:T(8,128)(2,1)S(1)}, bf16[768,128]{1,0:T(8,128)(2,1)S(1)}, u32[]{:S(2)}, u32[]{:S(2)}) collective-permute-start(bf16[768,128]{1,0:T(8,128)(2,1)S(1)} %pack.1.refs_4_), channel_id=1, source_target_pairs={{0,4},{1,5},{2,6},{3,7},{4,0},{5,1},{6,2},{7,3},{8,12},{9,13},{10,... | collective-permute-start | bytes 589832 | tf_op jit(solution)/shard_map/ppermute | solution.py:386
  10.0 0.0 collective-permute-done.near
  10.0 0.0 collective-permute-done.1.far
  10.0 0.2 corner.1
  10.2 0.1 collective-permute-start.3
  10.3 3.5 %collective-permute-start.8 = (bf16[768,128]{1,0:T(8,128)(2,1)S(1)}, bf16[768,128]{1,0:T(8,128)(2,1)S(1)}, u32[]{:S(2)}, u32[]{:S(2)}) collective-permute-start(bf16[768,128]{1,0:T(8,128)(2,1)S(1)} %pack.1.refs_4_), channel_id=1, source_target_pairs={{0,5},{1,4},{2,7},{3,6},{4,1},{5,0},{6,3},{7,2},{8,13},{9,12},{10,... | collective-permute-start | bytes 589832 | tf_op jit(solution)/shard_map/ppermute | solution.py:386
  13.9 0.5 %collective-permute-done.3.corner = bf16[128,128]{1,0:T(8,128)(2,1)S(1)} collective-permute-done((bf16[128,128]{1,0:T(8,128)(2,1)S(1)}, bf16[128,128]{1,0:T(8,128)(2,1)S(1)}, u32[]{:S(2)}, u32[]{:S(2)}) %collective-permute-start.3) | collective-permute-done | bytes 32800 | tf_op jit(solution)/shard_map/ppermute | solution.py:386
  14.3 0.0 collective-permute-done.2.across.refs_5_
  14.3 3.7 %forward.1 = (bf16[8,64,192]{2,1,0:T(8,128)(2,1)}, bf16[10,80,192]{2,1,0:T(8,128)(2,1)S(1)}, bf16[48,640]{1,0:T(8,128)(2,1)S(1)}, bf16[48,640]{1,0:T(8,128)(2,1)...) custom-call(bf16[8,64,192]{2,1,0:T(8,128)(2,1)S(1)} %get-tuple-element.33.masked, ...), custom_call_target="tpu_custom_call" | custom-call | flops 1610612736 | bytes 1048576 | tf_op jit(solution)/shard_map/forward/pallas_call | solution.py:357
  18.0 0.0 collective-permute-done.4.refs_6_
  18.0 0.1 collective-permute-start.5
  18.1 2.4 %collective-permute-start.6 = (bf16[48,640]{1,0:T(8,128)(2,1)S(1)}, bf16[48,640]{1,0:T(8,128)(2,1)S(1)}, u32[]{:S(2)}, u32[]{:S(2)}) collective-permute-start(bf16[48,640]{1,0:T(8,128)(2,1)S(1)} %get-tuple-element.49), channel_id=1, source_target_pairs={{0,4},{1,5},{2,6},{3,7},{4,0},{5,1},{6,2},{7,3},{8,12},{9,13},{10,... | collective-permute-start | bytes 184328 | tf_op jit(solution)/shard_map/ppermute | solution.py:386
  20.5 1.0 %collective-permute-start.7 = (bf16[48,640]{1,0:T(8,128)(2,1)S(1)}, bf16[48,640]{1,0:T(8,128)(2,1)S(1)}, u32[]{:S(2)}, u32[]{:S(2)}) collective-permute-start(bf16[48,640]{1,0:T(8,128)(2,1)S(1)} %get-tuple-element.50), channel_id=1, source_target_pairs={{0,5},{1,4},{2,7},{3,6},{4,1},{5,0},{6,3},{7,2},{8,13},{9,12},{10,... | collective-permute-start | bytes 184328 | tf_op jit(solution)/shard_map/ppermute | solution.py:386
  21.5 0.0 collective-permute-done.8.refs_7_
  21.5 0.8 %collective-permute-done.5.refs_1_ = bf16[48,640]{1,0:T(8,128)(2,1)S(1)} collective-permute-done((bf16[48,640]{1,0:T(8,128)(2,1)S(1)}, bf16[48,640]{1,0:T(8,128)(2,1)S(1)}, u32[]{:S(2)}, u32[]{:S(2)}) %collective-permute-start.5) | collective-permute-done | bytes 61472 | tf_op jit(solution)/shard_map/ppermute | solution.py:386
  22.4 0.7 %collective-permute-done.6.refs_2_ = bf16[48,640]{1,0:T(8,128)(2,1)S(1)} collective-permute-done((bf16[48,640]{1,0:T(8,128)(2,1)S(1)}, bf16[48,640]{1,0:T(8,128)(2,1)S(1)}, u32[]{:S(2)}, u32[]{:S(2)}) %collective-permute-start.6) | collective-permute-done | bytes 61472 | tf_op jit(solution)/shard_map/ppermute | solution.py:386
  23.0 2.6 %collective-permute-done.7.refs_3_ = bf16[48,640]{1,0:T(8,128)(2,1)S(1)} collective-permute-done((bf16[48,640]{1,0:T(8,128)(2,1)S(1)}, bf16[48,640]{1,0:T(8,128)(2,1)S(1)}, u32[]{:S(2)}, u32[]{:S(2)}) %collective-permute-start.7) | collective-permute-done | bytes 61472 | tf_op jit(solution)/shard_map/ppermute | solution.py:386
  25.6 2.6 %kernel_gradient.1 = (f32[24,5184]{1,0:T(8,128)S(1)}, bf16[24,5184]{1,0:T(8,128)(2,1)S(1)}) custom-call(bf16[48,640]{1,0:T(8,128)(2,1)S(1)} %get-tuple-element.47.refs_0_, bf16[48,640]{1,0:T(8,128)(2,1)S(1)} %collective-permute-done.5.refs_1_, bf16[48,640]{1,0:T(8,128)(2,1)S(1)} %collective-permute-done.6.refs_2_, ...), custom_call_target="tpu_custom_call" | custom-call | flops 1358954496 | bytes 4194304 | tf_op jit(solution)/shard_map/kernel_gradient/pallas_call | solution.py:357
  28.2 0.1 collective-permute-start.9
  28.3 1.5 %collective-permute-done.9.other = bf16[24,5184]{1,0:T(8,128)(2,1)S(1)} collective-permute-done((bf16[24,5184]{1,0:T(8,128)(2,1)S(1)}, bf16[24,5184]{1,0:T(8,128)(2,1)S(1)}, u32[]{:S(2)}, u32[]{:S(2)}) %collective-permute-start.9) | collective-permute-done | bytes 248864 | tf_op jit(solution)/shard_map/ppermute | solution.py:386
  29.8 0.2 fold.1
  30.0 3.9 %collective-permute-start.10 = (bf16[8,3968]{1,0:T(8,128)(2,1)S(1)}, bf16[8,3968]{1,0:T(8,128)(2,1)S(1)}, u32[]{:S(2)}, u32[]{:S(2)}) collective-permute-start(bf16[8,3968]{1,0:T(8,128)(2,1)S(1)} %get-tuple-element.55), channel_id=1, source_target_pairs={{0,24},{8,16},{16,8},{24,0},{1,25},{9,17},{17,9},{25,1},{2,26},{10... | collective-permute-start | bytes 190472 | tf_op jit(solution)/shard_map/ppermute | solution.py:386
  33.9 0.0 collective-permute-start.11
  33.9 0.6 %collective-permute-start.12 = (bf16[8,3968]{1,0:T(8,128)(2,1)S(1)}, bf16[8,3968]{1,0:T(8,128)(2,1)S(1)}, u32[]{:S(2)}, u32[]{:S(2)}) collective-permute-start(bf16[8,3968]{1,0:T(8,128)(2,1)S(1)} %get-tuple-element.57), channel_id=1, source_target_pairs={{0,8},{8,0},{16,24},{24,16},{1,9},{9,1},{17,25},{25,17},{2,10},{10... | collective-permute-start | bytes 190472 | tf_op jit(solution)/shard_map/ppermute | solution.py:386
  34.6 2.7 %input_gradient.1 = bf16[8,64,192]{2,1,0:T(8,128)(2,1)} custom-call(bf16[10,80,192]{2,1,0:T(8,128)(2,1)S(1)} %get-tuple-element.42.gp, f32[8,64,128]{2,1,0:T(8,128)S(1)} %get-tuple-element.39.live, bf16[192,5184]{1,0:T(8,128)(2,1)S(1)} %bitcast.6), custom_call_target="tpu_custom_call" | custom-call | flops 1358954496 | bytes 4194304 | tf_op jit(solution)/shard_map/input_gradient/pallas_call | solution.py:357
  37.2 0.0 collective-permute-done.10.one
  37.2 2.4 %collective-permute-done.11.two = bf16[8,3968]{1,0:T(8,128)(2,1)S(1)} collective-permute-done((bf16[8,3968]{1,0:T(8,128)(2,1)S(1)}, bf16[8,3968]{1,0:T(8,128)(2,1)S(1)}, u32[]{:S(2)}, u32[]{:S(2)}) %collective-permute-start.11) | collective-permute-done | bytes 63520 | tf_op jit(solution)/shard_map/ppermute | solution.py:386
  39.7 0.0 collective-permute-done.12.three
  39.7 1.3 %collective-permute-start.13 = (bf16[8,3968]{1,0:T(8,128)(2,1)S(1)}, bf16[8,3968]{1,0:T(8,128)(2,1)S(1)}, u32[]{:S(2)}, u32[]{:S(2)}) collective-permute-start(bf16[8,3968]{1,0:T(8,128)(2,1)S(1)} %plane_sum.1.mine), channel_id=1, source_target_pairs={{0,1},{1,0},{2,3},{3,2},{4,5},{5,4},{6,7},{7,6},{8,9},{9,8},{10,11... | collective-permute-start | bytes 190472 | tf_op jit(solution)/shard_map/ppermute | solution.py:386
  41.0 3.0 %collective-permute-done.13.other = bf16[8,3968]{1,0:T(8,128)(2,1)S(1)} collective-permute-done((bf16[8,3968]{1,0:T(8,128)(2,1)S(1)}, bf16[8,3968]{1,0:T(8,128)(2,1)S(1)}, u32[]{:S(2)}, u32[]{:S(2)}) %collective-permute-start.13) | collective-permute-done | bytes 63520 | tf_op jit(solution)/shard_map/ppermute | solution.py:386
  44.0 0.8 %join.1 = f32[12,5184]{1,0:T(8,128)} custom-call(bf16[8,3968]{1,0:T(8,128)(2,1)S(1)} %plane_sum.1.mine, bf16[8,3968]{1,0:T(8,128)(2,1)S(1)} %collective-permute-done.13.other), custom_call_target="tpu_custom_call" | custom-call | flops 41472 | bytes 580608 | tf_op jit(solution)/shard_map/join/pallas_call | solution.py:357
  (1 shorter events, 0.0 us)
Async XLA Ops:
  0.6 1.0 %copy-start.2 = (bf16[8,8,8,192]{3,2,1,0:T(8,128)(2,1)S(1)}, bf16[8,8,8,192]{3,2,1,0:T(8,128)(2,1)}, u32[]{:S(2)}) copy-start(bf16[8,8,8,192]{3,2,1,0:T(8,128)(2,1)} %param.7) | copy-start | bytes 589828
  0.6 0.9 %copy-start.3 = (s32[8,8,8]{2,1,0:T(8,128)S(1)}, s32[8,8,8]{2,1,0:T(8,128)}, u32[]{:S(2)}) copy-start(s32[8,8,8]{2,1,0:T(8,128)} %mask.1) | copy-start | bytes 6148
  0.7 1.0 %copy-start.1 = (bf16[8,8,8,192]{3,2,1,0:T(8,128)(2,1)S(1)}, bf16[8,8,8,192]{3,2,1,0:T(8,128)(2,1)}, u32[]{:S(2)}) copy-start(bf16[8,8,8,192]{3,2,1,0:T(8,128)(2,1)} %param.4) | copy-start | bytes 589828
  0.7 5.0 %copy-start = (bf16[5184,192]{0,1:T(8,128)(2,1)S(1)}, bf16[5184,192]{0,1:T(8,128)(2,1)}, u32[]{:S(2)}) copy-start(bf16[5184,192]{0,1:T(8,128)(2,1)} %param.5) | copy-start | bytes 5971972
  2.0 12.3 %collective-permute-start.2 = (bf16[864,128]{1,0:T(8,128)(2,1)S(1)}, bf16[864,128]{1,0:T(8,128)(2,1)S(1)}, u32[]{:S(2)}, u32[]{:S(2)}) collective-permute-start(bf16[864,128]{1,0:T(8,128)(2,1)S(1)} %across.1), channel_id=1, source_target_pairs={{0,1},{1,0},{2,3},{3,2},{4,5},{5,4},{6,7},{7,6},{8,9},{9,8},{10,11... | collective-permute-start | bytes 663560 | tf_op jit(solution)/shard_map/ppermute | solution.py:386
  5.0 5.0 %collective-permute-start = (bf16[288,128]{1,0:T(8,128)(2,1)S(1)}, bf16[288,128]{1,0:T(8,128)(2,1)S(1)}, u32[]{:S(2)}, u32[]{:S(2)}) collective-permute-start(bf16[288,128]{1,0:T(8,128)(2,1)S(1)} %get-tuple-element.35), channel_id=1, source_target_pairs={{0,2},{2,0},{4,6},{6,4},{8,10},{10,8},{12,14},{14,12},{16,18},{18,... | collective-permute-start | bytes 221192 | tf_op jit(solution)/shard_map/ppermute | solution.py:386
  5.0 5.0 %collective-permute-start.1 = (bf16[288,128]{1,0:T(8,128)(2,1)S(1)}, bf16[288,128]{1,0:T(8,128)(2,1)S(1)}, u32[]{:S(2)}, u32[]{:S(2)}) collective-permute-start(bf16[288,128]{1,0:T(8,128)(2,1)S(1)} %get-tuple-element.36), channel_id=1, source_target_pairs={{0,0},{2,4},{4,2},{6,8},{8,6},{10,12},{12,10},{14,16},{16,14},{18,... | collective-permute-start | bytes 221192 | tf_op jit(solution)/shard_map/ppermute | solution.py:412
  6.6 11.4 %collective-permute-start.4 = (bf16[768,128]{1,0:T(8,128)(2,1)S(1)}, bf16[768,128]{1,0:T(8,128)(2,1)S(1)}, u32[]{:S(2)}, u32[]{:S(2)}) collective-permute-start(bf16[768,128]{1,0:T(8,128)(2,1)S(1)} %pack.1.refs_4_), channel_id=1, source_target_pairs={{0,4},{1,5},{2,6},{3,7},{4,0},{5,1},{6,2},{7,3},{8,12},{9,13},{10,... | collective-permute-start | bytes 589832 | tf_op jit(solution)/shard_map/ppermute | solution.py:386
  10.2 4.1 %collective-permute-start.3 = (bf16[128,128]{1,0:T(8,128)(2,1)S(1)}, bf16[128,128]{1,0:T(8,128)(2,1)S(1)}, u32[]{:S(2)}, u32[]{:S(2)}) collective-permute-start(bf16[128,128]{1,0:T(8,128)(2,1)S(1)} %corner.1), channel_id=1, source_target_pairs={{0,1},{1,0},{2,3},{3,2},{4,5},{5,4},{6,7},{7,6},{8,9},{9,8},{10,11... | collective-permute-start | bytes 98312 | tf_op jit(solution)/shard_map/ppermute | solution.py:386
  10.3 11.2 %collective-permute-start.8 = (bf16[768,128]{1,0:T(8,128)(2,1)S(1)}, bf16[768,128]{1,0:T(8,128)(2,1)S(1)}, u32[]{:S(2)}, u32[]{:S(2)}) collective-permute-start(bf16[768,128]{1,0:T(8,128)(2,1)S(1)} %pack.1.refs_4_), channel_id=1, source_target_pairs={{0,5},{1,4},{2,7},{3,6},{4,1},{5,0},{6,3},{7,2},{8,13},{9,12},{10,... | collective-permute-start | bytes 589832 | tf_op jit(solution)/shard_map/ppermute | solution.py:386
  18.0 4.3 %collective-permute-start.5 = (bf16[48,640]{1,0:T(8,128)(2,1)S(1)}, bf16[48,640]{1,0:T(8,128)(2,1)S(1)}, u32[]{:S(2)}, u32[]{:S(2)}) collective-permute-start(bf16[48,640]{1,0:T(8,128)(2,1)S(1)} %get-tuple-element.48), channel_id=1, source_target_pairs={{0,1},{1,0},{2,3},{3,2},{4,5},{5,4},{6,7},{7,6},{8,9},{9,8},{10,11... | collective-permute-start | bytes 184328 | tf_op jit(solution)/shard_map/ppermute | solution.py:386
  18.1 5.0 %collective-permute-start.6 = (bf16[48,640]{1,0:T(8,128)(2,1)S(1)}, bf16[48,640]{1,0:T(8,128)(2,1)S(1)}, u32[]{:S(2)}, u32[]{:S(2)}) collective-permute-start(bf16[48,640]{1,0:T(8,128)(2,1)S(1)} %get-tuple-element.49), channel_id=1, source_target_pairs={{0,4},{1,5},{2,6},{3,7},{4,0},{5,1},{6,2},{7,3},{8,12},{9,13},{10,... | collective-permute-start | bytes 184328 | tf_op jit(solution)/shard_map/ppermute | solution.py:386
  20.5 5.1 %collective-permute-start.7 = (bf16[48,640]{1,0:T(8,128)(2,1)S(1)}, bf16[48,640]{1,0:T(8,128)(2,1)S(1)}, u32[]{:S(2)}, u32[]{:S(2)}) collective-permute-start(bf16[48,640]{1,0:T(8,128)(2,1)S(1)} %get-tuple-element.50), channel_id=1, source_target_pairs={{0,5},{1,4},{2,7},{3,6},{4,1},{5,0},{6,3},{7,2},{8,13},{9,12},{10,... | collective-permute-start | bytes 184328 | tf_op jit(solution)/shard_map/ppermute | solution.py:386
  28.2 1.6 %collective-permute-start.9 = (bf16[24,5184]{1,0:T(8,128)(2,1)S(1)}, bf16[24,5184]{1,0:T(8,128)(2,1)S(1)}, u32[]{:S(2)}, u32[]{:S(2)}) collective-permute-start(bf16[24,5184]{1,0:T(8,128)(2,1)S(1)} %get-tuple-element.54), channel_id=1, source_target_pairs={{0,2},{1,3},{2,0},{3,1},{4,6},{5,7},{6,4},{7,5},{8,10},{9,11},{10,... | collective-permute-start | bytes 746504 | tf_op jit(solution)/shard_map/ppermute | solution.py:386
  30.0 7.2 %collective-permute-start.10 = (bf16[8,3968]{1,0:T(8,128)(2,1)S(1)}, bf16[8,3968]{1,0:T(8,128)(2,1)S(1)}, u32[]{:S(2)}, u32[]{:S(2)}) collective-permute-start(bf16[8,3968]{1,0:T(8,128)(2,1)S(1)} %get-tuple-element.55), channel_id=1, source_target_pairs={{0,24},{8,16},{16,8},{24,0},{1,25},{9,17},{17,9},{25,1},{2,26},{10... | collective-permute-start | bytes 190472 | tf_op jit(solution)/shard_map/ppermute | solution.py:386
  33.9 5.8 %collective-permute-start.11 = (bf16[8,3968]{1,0:T(8,128)(2,1)S(1)}, bf16[8,3968]{1,0:T(8,128)(2,1)S(1)}, u32[]{:S(2)}, u32[]{:S(2)}) collective-permute-start(bf16[8,3968]{1,0:T(8,128)(2,1)S(1)} %get-tuple-element.56), channel_id=1, source_target_pairs={{0,16},{8,24},{16,0},{24,8},{1,17},{9,25},{17,1},{25,9},{2,18},{10... | collective-permute-start | bytes 190472 | tf_op jit(solution)/shard_map/ppermute | solution.py:386
  33.9 5.8 %collective-permute-start.12 = (bf16[8,3968]{1,0:T(8,128)(2,1)S(1)}, bf16[8,3968]{1,0:T(8,128)(2,1)S(1)}, u32[]{:S(2)}, u32[]{:S(2)}) collective-permute-start(bf16[8,3968]{1,0:T(8,128)(2,1)S(1)} %get-tuple-element.57), channel_id=1, source_target_pairs={{0,8},{8,0},{16,24},{24,16},{1,9},{9,1},{17,25},{25,17},{2,10},{10... | collective-permute-start | bytes 190472 | tf_op jit(solution)/shard_map/ppermute | solution.py:386
  39.7 4.3 %collective-permute-start.13 = (bf16[8,3968]{1,0:T(8,128)(2,1)S(1)}, bf16[8,3968]{1,0:T(8,128)(2,1)S(1)}, u32[]{:S(2)}, u32[]{:S(2)}) collective-permute-start(bf16[8,3968]{1,0:T(8,128)(2,1)S(1)} %plane_sum.1.mine), channel_id=1, source_target_pairs={{0,1},{1,0},{2,3},{3,2},{4,5},{5,4},{6,7},{7,6},{8,9},{9,8},{10,11... | collective-permute-start | bytes 190472 | tf_op jit(solution)/shard_map/ppermute | solution.py:386

commit v15 on v14

--- a/solution.py
+++ b/solution.py
@@ -143,15 +143,10 @@
         out_ref[start:stop, :] = weight[:, start:stop].T
 
 
-def forward_kernel(
-    masked, cot, near, far, across, corner, live, weight, pick, *refs
-):
-    act_ref, gp_ref = refs[:2]
-    slice_refs = refs[2 : 2 + len(CHIPS)]
-    ext, edge, cols, slices = refs[2 + len(CHIPS) :]
+def bulk_kernel(masked, near, far, across, weight, pre_ref, ext, edge, cols):
     width, rows, channels = masked.shape
     f32 = jnp.float32
-    plane, me, quad, side = position()
+    plane, _, quad, side = position()
     use_low = side.astype(f32)
     use_high = (1 - side).astype(f32)
     place = plane * QUAD + quad
@@ -164,27 +159,21 @@
     odd = lax.rem(quad, 2)
     edge[odd] = rows_of_192(far[...].astype(f32)).reshape(edge.shape[1:])
     edge[1 - odd] = rows_of_192(near[...].astype(f32)).reshape(edge.shape[1:])
-    left, right = edge[0] * use_left, edge[1] * use_right
-    count = 4 * halo + 2 * DEPTH
-    both = rows_of_192(corner[...].astype(f32)[: count * channels // 128])
-    corners = both[: 4 * halo].reshape(2, 2, halo, channels)
-    lower, upper = corners[0] * use_left, corners[1] * use_right
-    ends = both[4 * halo :].reshape(2, 1, DEPTH, channels)
-    ext[0:2, halo : halo + rows, :] = left[0:2]
+    ext[0:2, halo : halo + rows, :] = edge[0, 0:2] * use_left
     ext[2 : 2 + width, halo : halo + rows, :] = masked[...].astype(f32)
-    ext[2 + width :, halo : halo + rows, :] = right[0:2]
+    ext[2 + width :, halo : halo + rows, :] = edge[1, 0:2] * use_right
     half = width // 2
-    ahead = side == 0
     count = width * rows * channels // 128
     held = across[:count].astype(f32).reshape(width + half, rows, 128)
-    brick = jnp.where(ahead, held[:, :halo], held[:, rows - halo :])
+    brick = jnp.where(side == 0, held[:, :halo], held[:, rows - halo :])
     rest = jnp.concatenate([brick[width:, :, :64], brick[width:, :, 64:]], axis=0)
     beside = jnp.concatenate([brick[:width], rest], axis=2)
+    blank = jnp.zeros((2, halo, channels), f32)
     for use, start in ((use_low, 0), (use_high, halo + rows)):
         at = slice(start, start + halo)
-        ext[0:2, at, :] = lower * use
+        ext[0:2, at, :] = blank
         ext[2 : 2 + width, at, :] = beside * use
-        ext[2 + width :, at, :] = upper * use
+        ext[2 + width :, at, :] = blank
     field = ext[...].reshape(span * tall // DEPTH, DEPTH, channels)
     for c in OFFSETS:
         moved = shift_z(field, c).reshape(span, tall, channels)
@@ -200,19 +189,81 @@
             weight[a * nine : (a + 1) * nine, :],
             preferred_element_type=f32,
         )
+    pre_ref[...] = pre.reshape(pre_ref.shape)
+
+
+def forward_kernel(bulk, cot, near, far, across, corner, live, weight, pick, *refs):
+    act_ref, gp_ref = refs[:2]
+    slice_refs = refs[2 : 2 + len(CHIPS)]
+    edge, cols, total, slices = refs[2 + len(CHIPS) :]
+    width, rows, channels = cot.shape
+    f32 = jnp.float32
+    plane, me, quad, side = position()
+    use_low = side.astype(f32)
+    use_high = (1 - side).astype(f32)
+    place = plane * QUAD + quad
+    use_left = (place > 0).astype(f32)
+    use_right = (place < QUAD * lax.axis_size("depth") - 1).astype(f32)
+    halo = 2 * DEPTH
+    mid = rows + 2 * DEPTH
+    count = 4 * halo + 2 * DEPTH
+    both = rows_of_192(corner[...].astype(f32)[: count * channels // 128])
+    corners = both[: 4 * halo].reshape(2, 2, halo, channels)
+    corners = jnp.concatenate([corners[0] * use_left, corners[1] * use_right], axis=0)
+    sources = ((0, 1, None, None), (1, None, None, 2), (None, None, 2, 3))
+    blank = jnp.zeros((DEPTH, channels), f32)
+    for c in OFFSETS:
+        moved = shift_z(corners.reshape(8, DEPTH, channels), c)
+        for b in OFFSETS:
+            low = {-1: (0, 1), 0: (1, None), 1: (None, None)}[b]
+            high = {-1: (None, None), 0: (None, 0), 1: (0, 1)}[b]
+            at = ((b + 1) * 3 + c + 1) * channels
+            parts = []
+            for slab in range(4):
+                for below, above in zip(low, high):
+                    part = blank if below is None else moved[2 * slab + below] * use_low
+                    if above is not None:
+                        part = part + moved[2 * slab + above] * use_high
+                    parts.append(part)
+            for a in range(3):
+                rows_a = []
+                for source in sources[a]:
+                    pair = [blank] * 2 if source is None else parts[2 * source : 2 * source + 2]
+                    rows_a += pair
+                cols[a, :, at : at + channels] = jnp.concatenate(rows_a, axis=0).astype(
+                    jnp.bfloat16
+                )
+    nine = 9 * channels
+    share = jnp.zeros((4 * halo, channels), f32)
+    for a in range(3):
+        share += jnp.dot(
+            cols[a], weight[a * nine : (a + 1) * nine, :], preferred_element_type=f32
+        )
+    share = share.reshape(4, halo, channels)
+    total[...] = bulk[...]
+    at = pl.ds(pl.multiple_of((1 - side) * (mid - halo), DEPTH), halo)
+    total[0:2, at, :] += share[0:2]
+    total[width : width + 2, at, :] += share[2:4]
+    pre = total[...].reshape((width + 2) * mid, channels)
     sig = 0.5 * jnp.tanh(0.5 * pre) + 0.5
     act = (pre * sig).reshape(width + 2, mid, channels)[1 : 1 + width, DEPTH : DEPTH + rows]
     act_ref[...] = (act * live[:, :, 0:1]).astype(jnp.bfloat16)
     slope = (sig * (1.0 + pre * (1.0 - sig))).reshape(width + 2, mid, channels)
+    ends = both[4 * halo :].reshape(2, 1, DEPTH, channels)
+    strip = across[width * rows * channels // 128 :].astype(f32)
     beyond = jnp.concatenate(
         [
             ends[0] * use_left,
-            rows_of_192(across[count:].astype(f32)).reshape(width, DEPTH, channels),
+            rows_of_192(strip).reshape(width, DEPTH, channels),
             ends[1] * use_right,
         ],
         axis=0,
     )
-    centre = jnp.concatenate([left[2:3], cot[...].astype(f32), right[2:3]], axis=0)
+    odd = lax.rem(quad, 2)
+    edge[odd] = rows_of_192(far[...].astype(f32))[2 * rows :]
+    edge[1 - odd] = rows_of_192(near[...].astype(f32))[2 * rows :]
+    centre = [edge[0:1] * use_left, cot[...].astype(f32), edge[1:2] * use_right]
+    centre = jnp.concatenate(centre, axis=0)
     full = jnp.concatenate([beyond * use_low, centre, beyond * use_high], axis=1)
     grad = full * slope
     gp_ref[...] = grad.astype(jnp.bfloat16)
@@ -423,29 +474,39 @@
         pack_kernel, "pack", 4, 1 << 16, 1 << 19, array((count_128, 128), bf16), (),
         [vmem, pl.BlockSpec(memory_space=pl.ANY)],
     )(masked, weight_rows)
-    near, far, weight_rows, late = lax.optimization_barrier((near, far, weight_rows, packed))
+    near, far, weight_rows = lax.optimization_barrier((near, far, weight_rows))
     corner = call(
         corner_kernel, "corner", 4, 1 << 16, 1 << 18,
         array((128, 128), bf16),
         (pltpu.VMEM(slabs, f32),),
     )(near, far)
     corner = in_plane(corner, 1)
-    bricks = [packed, across, in_plane(packed, CHIPS[2]), in_plane(late, CHIPS[3])]
-
     mid = rows + 2 * DEPTH
-    act, gp, *slices = call(
-        forward_kernel, "forward", 28, 3 << 29, 1 << 20,
-        (brick, array((width + 2, mid, channels), bf16))
-        + (array((2 * group, span), bf16),) * len(CHIPS),
+    bulk = call(
+        bulk_kernel, "bulk", 24, 3 << 29, 1 << 20, array((width + 2, mid, channels), f32),
         (
             pltpu.VMEM((width + 4, rows + 2 * halo, channels), f32),
             pltpu.VMEM(slabs, f32),
             pltpu.VMEM((width + 4, mid, 9 * channels), bf16),
+        ),
+    )(masked, near, far, across, weight_rows)
+    late, bulk = lax.optimization_barrier((packed, bulk))
+    bricks = [packed, across, in_plane(packed, CHIPS[2]), in_plane(late, CHIPS[3])]
+
+    act, gp, *slices = call(
+        forward_kernel, "forward", 24, 3 << 29, 1 << 20,
+        (brick, array((width + 2, mid, channels), bf16))
+        + (array((2 * group, span), bf16),) * len(CHIPS),
+        (
+            pltpu.VMEM((2, rows, channels), f32),
+            pltpu.VMEM((3, 4 * halo, 9 * channels), bf16),
+            pltpu.VMEM((width + 2, mid, channels), f32),
             pltpu.VMEM((MEMBERS, group, span), f32),
         ),
-    )(masked, cot, near, far, across, corner, live, weight_rows, pick)
+    )(bulk, cot, near, far, across, corner, live, weight_rows, pick)
     bricks[2], *slices = lax.optimization_barrier((bricks[2], *slices))
-    slices = [slices[0]] + [in_plane(part, d) for part, d in zip(slices[1:], CHIPS[1:])]
+    for place in (3, 2, 1):
+        slices[place] = in_plane(slices[place], CHIPS[place])
 
     grad_input = call(
         input_kernel, "input_gradient", 20, 2 * 512 * 5184 * 256, 4 << 20, brick,

time: 45 us -> 44.8 us (level)
  waiting for transfers between devices: 11.5 us -> 10.5 us
  Pallas kernels: 11.5 us -> 12.4 us
    ppermute x13, waiting for transfers between devices: 11.5 us -> 10.5 us  [swap(): return lax.ppermute(piece, axes, [(i, i ^ distance) for i in range(size)])]
    pallas_call x12 -> x13, Pallas kernels: 11.5 us -> 12.4 us  [run(): pl.pallas_call(body, out_shape=out_shape, in_specs=in_specs or [spec] * l...]
  transfers between devices with their start and end apart: 14 -> 14, of which waited for: 7 -> 7; matrix products, arithmetic and copies ran while one was open for 0% -> 0% of each run, Pallas kernels for 16% -> 19%
where the time goes in v15:
time: 44.8 us; the launch traced here: 44.7 us
  starting transfers between devices  20.3 us (45%)
  Pallas kernels  12.4 us (28%)
  waiting for transfers between devices  10.5 us (23%)
  local copies, waits for them, and re-layouts  0.84 us (2%)
  between operations  0.74 us (2%)
    ppermute x13, starting transfers between devices, swap(): return lax.ppermute(piece, axes, [(i, i ^ distance) for i in range(size)])  19.6 us
    pallas_call x13, Pallas kernels, run(): pl.pallas_call(body, out_shape=out_shape, in_specs=in_specs or [spec] * l...  12.4 us
    ppermute x13, waiting for transfers between devices, swap(): return lax.ppermute(piece, axes, [(i, i ^ distance) for i in range(size)])  10.5 us
  transfers between devices with their start and end apart: 14, of which 7 were waited for; matrix products, arithmetic and copies ran while one was open for 0% of the time, Pallas kernels for 19%

profile of v15, /device:TPU:0, one launch (start us, length us, event | category | flops | bytes accessed | tf_op | source)
XLA Modules:
  0.0 44.7 jit_solution(16070378695156214255)
XLA Ops:
  0.6 0.0 copy-start.1
  0.6 0.0 copy-start.2
  0.7 0.0 copy-start.3
  0.7 0.0 copy-start
  0.7 0.2 pick.1.first
  0.8 0.7 %copy-done.1 = bf16[8,8,8,192]{3,2,1,0:T(8,128)(2,1)S(1)} copy-done((bf16[8,8,8,192]{3,2,1,0:T(8,128)(2,1)S(1)}, bf16[8,8,8,192]{3,2,1,0:T(8,128)(2,1)}, u32[]{:S(2)}) %copy-start.1) | copy-done | bytes 196632
  1.6 0.1 copy-done.2
  1.7 0.0 copy-done.3
  1.7 0.2 prepare.1
  1.9 0.1 across.1
  2.0 3.0 %collective-permute-start.2 = (bf16[864,128]{1,0:T(8,128)(2,1)S(1)}, bf16[864,128]{1,0:T(8,128)(2,1)S(1)}, u32[]{:S(2)}, u32[]{:S(2)}) collective-permute-start(bf16[864,128]{1,0:T(8,128)(2,1)S(1)} %across.1), channel_id=1, source_target_pairs={{0,1},{1,0},{2,3},{3,2},{4,5},{5,4},{6,7},{7,6},{8,9},{9,8},{10,11... | collective-permute-start | bytes 663560 | tf_op jit(solution)/shard_map/ppermute | solution.py:437
  5.0 0.0 collective-permute-start
  5.0 0.7 %collective-permute-start.1 = (bf16[288,128]{1,0:T(8,128)(2,1)S(1)}, bf16[288,128]{1,0:T(8,128)(2,1)S(1)}, u32[]{:S(2)}, u32[]{:S(2)}) collective-permute-start(bf16[288,128]{1,0:T(8,128)(2,1)S(1)} %get-tuple-element.36), channel_id=1, source_target_pairs={{0,0},{2,4},{4,2},{6,8},{8,6},{10,12},{12,10},{14,16},{16,14},{18,... | collective-permute-start | bytes 221192 | tf_op jit(solution)/shard_map/ppermute | solution.py:463
  5.7 0.0 copy-done
  5.7 0.8 %turn.1.after.weight = bf16[5184,192]{1,0:T(8,128)(2,1)S(1)} custom-call(bf16[192,5184]{1,0:T(8,128)(2,1)S(1)} %bitcast.5), custom_call_target="tpu_custom_call" | custom-call | flops 1048576 | bytes 4194304 | tf_op jit(solution)/shard_map/turn/pallas_call | solution.py:408
  6.5 0.1 pack.1.refs_4_
  6.6 3.4 %collective-permute-start.4 = (bf16[768,128]{1,0:T(8,128)(2,1)S(1)}, bf16[768,128]{1,0:T(8,128)(2,1)S(1)}, u32[]{:S(2)}, u32[]{:S(2)}) collective-permute-start(bf16[768,128]{1,0:T(8,128)(2,1)S(1)} %pack.1.refs_4_), channel_id=1, source_target_pairs={{0,4},{1,5},{2,6},{3,7},{4,0},{5,1},{6,2},{7,3},{8,12},{9,13},{10,... | collective-permute-start | bytes 589832 | tf_op jit(solution)/shard_map/ppermute | solution.py:437
  10.0 0.0 collective-permute-done.near
  10.0 0.0 collective-permute-done.1.far
  10.0 0.2 corner.1
  10.2 0.1 collective-permute-start.3
  10.3 0.1 collective-permute-done.2.across.refs_5_
  10.5 2.8 %bulk.1 = f32[10,80,192]{2,1,0:T(8,128)S(1)} custom-call(bf16[8,64,192]{2,1,0:T(8,128)(2,1)S(1)} %get-tuple-element.34.masked, bf16[288,128]{1,0:T(8,128)(2,1)S(1)} %collective-permute-done.near, bf16[288,128]{1,0:T(8,128)(2,1)S(1)} %collective-permute-done.1.far, bf16[864,128]{1,0:T(8,128)(2,1)S(1)} %collective-permute-done.2.across.refs_5_, ...), custom_call_target="tpu_custom_call" | custom-call | flops 1610612736 | bytes 1048576 | tf_op jit(solution)/shard_map/bulk/pallas_call | solution.py:408
  13.3 3.5 %collective-permute-start.8 = (bf16[768,128]{1,0:T(8,128)(2,1)S(1)}, bf16[768,128]{1,0:T(8,128)(2,1)S(1)}, u32[]{:S(2)}, u32[]{:S(2)}) collective-permute-start(bf16[768,128]{1,0:T(8,128)(2,1)S(1)} %pack.1.refs_4_), channel_id=1, source_target_pairs={{0,5},{1,4},{2,7},{3,6},{4,1},{5,0},{6,3},{7,2},{8,13},{9,12},{10,... | collective-permute-start | bytes 589832 | tf_op jit(solution)/shard_map/ppermute | solution.py:437
  16.7 0.0 collective-permute-done.3.corner
  16.7 1.8 %forward.1 = (bf16[8,64,192]{2,1,0:T(8,128)(2,1)}, bf16[10,80,192]{2,1,0:T(8,128)(2,1)S(1)}, bf16[48,640]{1,0:T(8,128)(2,1)S(1)}, bf16[48,640]{1,0:T(8,128)(2,1)...) custom-call(f32[10,80,192]{2,1,0:T(8,128)S(1)} %bulk.1, bf16[8,64,192]{2,1,0:T(8,128)(2,1)S(1)} %get-tuple-element.39.cot, ...), custom_call_target="tpu_custom_call" | custom-call | flops 1610612736 | bytes 1048576 | tf_op jit(solution)/shard_map/forward/pallas_call | solution.py:408
  18.5 0.0 collective-permute-done.4.refs_6_
  18.5 0.5 %collective-permute-start.5 = (bf16[48,640]{1,0:T(8,128)(2,1)S(1)}, bf16[48,640]{1,0:T(8,128)(2,1)S(1)}, u32[]{:S(2)}, u32[]{:S(2)}) collective-permute-start(bf16[48,640]{1,0:T(8,128)(2,1)S(1)} %get-tuple-element.50), channel_id=1, source_target_pairs={{0,1},{1,0},{2,3},{3,2},{4,5},{5,4},{6,7},{7,6},{8,9},{9,8},{10,11... | collective-permute-start | bytes 184328 | tf_op jit(solution)/shard_map/ppermute | solution.py:437
  19.0 0.1 collective-permute-start.6
  19.1 2.9 %collective-permute-start.7 = (bf16[48,640]{1,0:T(8,128)(2,1)S(1)}, bf16[48,640]{1,0:T(8,128)(2,1)S(1)}, u32[]{:S(2)}, u32[]{:S(2)}) collective-permute-start(bf16[48,640]{1,0:T(8,128)(2,1)S(1)} %get-tuple-element.52), channel_id=1, source_target_pairs={{0,5},{1,4},{2,7},{3,6},{4,1},{5,0},{6,3},{7,2},{8,13},{9,12},{10,... | collective-permute-start | bytes 184328 | tf_op jit(solution)/shard_map/ppermute | solution.py:437
  22.0 1.8 %collective-permute-done.5.refs_1_ = bf16[48,640]{1,0:T(8,128)(2,1)S(1)} collective-permute-done((bf16[48,640]{1,0:T(8,128)(2,1)S(1)}, bf16[48,640]{1,0:T(8,128)(2,1)S(1)}, u32[]{:S(2)}, u32[]{:S(2)}) %collective-permute-start.5) | collective-permute-done | bytes 61472 | tf_op jit(solution)/shard_map/ppermute | solution.py:437
  23.8 0.1 collective-permute-done.6.refs_2_
  23.9 1.9 %collective-permute-done.7.refs_3_ = bf16[48,640]{1,0:T(8,128)(2,1)S(1)} collective-permute-done((bf16[48,640]{1,0:T(8,128)(2,1)S(1)}, bf16[48,640]{1,0:T(8,128)(2,1)S(1)}, u32[]{:S(2)}, u32[]{:S(2)}) %collective-permute-start.7) | collective-permute-done | bytes 61472 | tf_op jit(solution)/shard_map/ppermute | solution.py:437
  25.8 0.0 collective-permute-done.8.refs_7_
  25.8 2.6 %kernel_gradient.1 = (f32[24,5184]{1,0:T(8,128)S(1)}, bf16[24,5184]{1,0:T(8,128)(2,1)S(1)}) custom-call(bf16[48,640]{1,0:T(8,128)(2,1)S(1)} %get-tuple-element.49.refs_0_, bf16[48,640]{1,0:T(8,128)(2,1)S(1)} %collective-permute-done.5.refs_1_, bf16[48,640]{1,0:T(8,128)(2,1)S(1)} %collective-permute-done.6.refs_2_, ...), custom_call_target="tpu_custom_call" | custom-call | flops 1358954496 | bytes 4194304 | tf_op jit(solution)/shard_map/kernel_gradient/pallas_call | solution.py:408
  28.4 0.1 collective-permute-start.9
  28.5 1.5 %collective-permute-done.9.other = bf16[24,5184]{1,0:T(8,128)(2,1)S(1)} collective-permute-done((bf16[24,5184]{1,0:T(8,128)(2,1)S(1)}, bf16[24,5184]{1,0:T(8,128)(2,1)S(1)}, u32[]{:S(2)}, u32[]{:S(2)}) %collective-permute-start.9) | collective-permute-done | bytes 248864 | tf_op jit(solution)/shard_map/ppermute | solution.py:437
  30.0 0.2 fold.1
  30.2 3.6 %collective-permute-start.10 = (bf16[8,3968]{1,0:T(8,128)(2,1)S(1)}, bf16[8,3968]{1,0:T(8,128)(2,1)S(1)}, u32[]{:S(2)}, u32[]{:S(2)}) collective-permute-start(bf16[8,3968]{1,0:T(8,128)(2,1)S(1)} %get-tuple-element.57), channel_id=1, source_target_pairs={{0,24},{8,16},{16,8},{24,0},{1,25},{9,17},{17,9},{25,1},{2,26},{10... | collective-permute-start | bytes 190472 | tf_op jit(solution)/shard_map/ppermute | solution.py:437
  33.7 0.0 collective-permute-start.11
  33.7 0.9 %collective-permute-start.12 = (bf16[8,3968]{1,0:T(8,128)(2,1)S(1)}, bf16[8,3968]{1,0:T(8,128)(2,1)S(1)}, u32[]{:S(2)}, u32[]{:S(2)}) collective-permute-start(bf16[8,3968]{1,0:T(8,128)(2,1)S(1)} %get-tuple-element.59), channel_id=1, source_target_pairs={{0,8},{8,0},{16,24},{24,16},{1,9},{9,1},{17,25},{25,17},{2,10},{10... | collective-permute-start | bytes 190472 | tf_op jit(solution)/shard_map/ppermute | solution.py:437
  34.6 2.7 %input_gradient.1 = bf16[8,64,192]{2,1,0:T(8,128)(2,1)} custom-call(bf16[10,80,192]{2,1,0:T(8,128)(2,1)S(1)} %get-tuple-element.44.gp, f32[8,64,128]{2,1,0:T(8,128)S(1)} %get-tuple-element.42.live, bf16[192,5184]{1,0:T(8,128)(2,1)S(1)} %bitcast.6), custom_call_target="tpu_custom_call" | custom-call | flops 1358954496 | bytes 4194304 | tf_op jit(solution)/shard_map/input_gradient/pallas_call | solution.py:408
  37.3 0.0 collective-permute-done.10.one
  37.3 2.2 %collective-permute-done.11.two = bf16[8,3968]{1,0:T(8,128)(2,1)S(1)} collective-permute-done((bf16[8,3968]{1,0:T(8,128)(2,1)S(1)}, bf16[8,3968]{1,0:T(8,128)(2,1)S(1)}, u32[]{:S(2)}, u32[]{:S(2)}) %collective-permute-start.11) | collective-permute-done | bytes 63520 | tf_op jit(solution)/shard_map/ppermute | solution.py:437
  39.5 0.0 collective-permute-done.12.three
  39.6 1.5 %collective-permute-start.13 = (bf16[8,3968]{1,0:T(8,128)(2,1)S(1)}, bf16[8,3968]{1,0:T(8,128)(2,1)S(1)}, u32[]{:S(2)}, u32[]{:S(2)}) collective-permute-start(bf16[8,3968]{1,0:T(8,128)(2,1)S(1)} %plane_sum.1.mine), channel_id=1, source_target_pairs={{0,1},{1,0},{2,3},{3,2},{4,5},{5,4},{6,7},{7,6},{8,9},{9,8},{10,11... | collective-permute-start | bytes 190472 | tf_op jit(solution)/shard_map/ppermute | solution.py:437
  41.1 2.8 %collective-permute-done.13.other = bf16[8,3968]{1,0:T(8,128)(2,1)S(1)} collective-permute-done((bf16[8,3968]{1,0:T(8,128)(2,1)S(1)}, bf16[8,3968]{1,0:T(8,128)(2,1)S(1)}, u32[]{:S(2)}, u32[]{:S(2)}) %collective-permute-start.13) | collective-permute-done | bytes 63520 | tf_op jit(solution)/shard_map/ppermute | solution.py:437
  43.9 0.8 %join.1 = f32[12,5184]{1,0:T(8,128)} custom-call(bf16[8,3968]{1,0:T(8,128)(2,1)S(1)} %plane_sum.1.mine, bf16[8,3968]{1,0:T(8,128)(2,1)S(1)} %collective-permute-done.13.other), custom_call_target="tpu_custom_call" | custom-call | flops 41472 | bytes 580608 | tf_op jit(solution)/shard_map/join/pallas_call | solution.py:408
  (1 shorter events, 0.0 us)
Async XLA Ops:
  0.6 1.0 %copy-start.1 = (bf16[8,8,8,192]{3,2,1,0:T(8,128)(2,1)S(1)}, bf16[8,8,8,192]{3,2,1,0:T(8,128)(2,1)}, u32[]{:S(2)}) copy-start(bf16[8,8,8,192]{3,2,1,0:T(8,128)(2,1)} %param.4) | copy-start | bytes 589828
  0.6 1.0 %copy-start.2 = (bf16[8,8,8,192]{3,2,1,0:T(8,128)(2,1)S(1)}, bf16[8,8,8,192]{3,2,1,0:T(8,128)(2,1)}, u32[]{:S(2)}) copy-start(bf16[8,8,8,192]{3,2,1,0:T(8,128)(2,1)} %param.7) | copy-start | bytes 589828
  0.7 1.0 %copy-start.3 = (s32[8,8,8]{2,1,0:T(8,128)S(1)}, s32[8,8,8]{2,1,0:T(8,128)}, u32[]{:S(2)}) copy-start(s32[8,8,8]{2,1,0:T(8,128)} %mask.1) | copy-start | bytes 6148
  0.7 5.0 %copy-start = (bf16[5184,192]{0,1:T(8,128)(2,1)S(1)}, bf16[5184,192]{0,1:T(8,128)(2,1)}, u32[]{:S(2)}) copy-start(bf16[5184,192]{0,1:T(8,128)(2,1)} %param.5) | copy-start | bytes 5971972
  2.0 8.5 %collective-permute-start.2 = (bf16[864,128]{1,0:T(8,128)(2,1)S(1)}, bf16[864,128]{1,0:T(8,128)(2,1)S(1)}, u32[]{:S(2)}, u32[]{:S(2)}) collective-permute-start(bf16[864,128]{1,0:T(8,128)(2,1)S(1)} %across.1), channel_id=1, source_target_pairs={{0,1},{1,0},{2,3},{3,2},{4,5},{5,4},{6,7},{7,6},{8,9},{9,8},{10,11... | collective-permute-start | bytes 663560 | tf_op jit(solution)/shard_map/ppermute | solution.py:437
  5.0 5.0 %collective-permute-start = (bf16[288,128]{1,0:T(8,128)(2,1)S(1)}, bf16[288,128]{1,0:T(8,128)(2,1)S(1)}, u32[]{:S(2)}, u32[]{:S(2)}) collective-permute-start(bf16[288,128]{1,0:T(8,128)(2,1)S(1)} %get-tuple-element.35), channel_id=1, source_target_pairs={{0,2},{2,0},{4,6},{6,4},{8,10},{10,8},{12,14},{14,12},{16,18},{18,... | collective-permute-start | bytes 221192 | tf_op jit(solution)/shard_map/ppermute | solution.py:437
  5.0 5.0 %collective-permute-start.1 = (bf16[288,128]{1,0:T(8,128)(2,1)S(1)}, bf16[288,128]{1,0:T(8,128)(2,1)S(1)}, u32[]{:S(2)}, u32[]{:S(2)}) collective-permute-start(bf16[288,128]{1,0:T(8,128)(2,1)S(1)} %get-tuple-element.36), channel_id=1, source_target_pairs={{0,0},{2,4},{4,2},{6,8},{8,6},{10,12},{12,10},{14,16},{16,14},{18,... | collective-permute-start | bytes 221192 | tf_op jit(solution)/shard_map/ppermute | solution.py:463
  6.6 11.9 %collective-permute-start.4 = (bf16[768,128]{1,0:T(8,128)(2,1)S(1)}, bf16[768,128]{1,0:T(8,128)(2,1)S(1)}, u32[]{:S(2)}, u32[]{:S(2)}) collective-permute-start(bf16[768,128]{1,0:T(8,128)(2,1)S(1)} %pack.1.refs_4_), channel_id=1, source_target_pairs={{0,4},{1,5},{2,6},{3,7},{4,0},{5,1},{6,2},{7,3},{8,12},{9,13},{10,... | collective-permute-start | bytes 589832 | tf_op jit(solution)/shard_map/ppermute | solution.py:437
  10.2 6.6 %collective-permute-start.3 = (bf16[128,128]{1,0:T(8,128)(2,1)S(1)}, bf16[128,128]{1,0:T(8,128)(2,1)S(1)}, u32[]{:S(2)}, u32[]{:S(2)}) collective-permute-start(bf16[128,128]{1,0:T(8,128)(2,1)S(1)} %corner.1), channel_id=1, source_target_pairs={{0,1},{1,0},{2,3},{3,2},{4,5},{5,4},{6,7},{7,6},{8,9},{9,8},{10,11... | collective-permute-start | bytes 98312 | tf_op jit(solution)/shard_map/ppermute | solution.py:437
  13.3 12.5 %collective-permute-start.8 = (bf16[768,128]{1,0:T(8,128)(2,1)S(1)}, bf16[768,128]{1,0:T(8,128)(2,1)S(1)}, u32[]{:S(2)}, u32[]{:S(2)}) collective-permute-start(bf16[768,128]{1,0:T(8,128)(2,1)S(1)} %pack.1.refs_4_), channel_id=1, source_target_pairs={{0,5},{1,4},{2,7},{3,6},{4,1},{5,0},{6,3},{7,2},{8,13},{9,12},{10,... | collective-permute-start | bytes 589832 | tf_op jit(solution)/shard_map/ppermute | solution.py:437
  18.5 5.3 %collective-permute-start.5 = (bf16[48,640]{1,0:T(8,128)(2,1)S(1)}, bf16[48,640]{1,0:T(8,128)(2,1)S(1)}, u32[]{:S(2)}, u32[]{:S(2)}) collective-permute-start(bf16[48,640]{1,0:T(8,128)(2,1)S(1)} %get-tuple-element.50), channel_id=1, source_target_pairs={{0,1},{1,0},{2,3},{3,2},{4,5},{5,4},{6,7},{7,6},{8,9},{9,8},{10,11... | collective-permute-start | bytes 184328 | tf_op jit(solution)/shard_map/ppermute | solution.py:437
  19.0 4.9 %collective-permute-start.6 = (bf16[48,640]{1,0:T(8,128)(2,1)S(1)}, bf16[48,640]{1,0:T(8,128)(2,1)S(1)}, u32[]{:S(2)}, u32[]{:S(2)}) collective-permute-start(bf16[48,640]{1,0:T(8,128)(2,1)S(1)} %get-tuple-element.51), channel_id=1, source_target_pairs={{0,4},{1,5},{2,6},{3,7},{4,0},{5,1},{6,2},{7,3},{8,12},{9,13},{10,... | collective-permute-start | bytes 184328 | tf_op jit(solution)/shard_map/ppermute | solution.py:437
  19.1 6.7 %collective-permute-start.7 = (bf16[48,640]{1,0:T(8,128)(2,1)S(1)}, bf16[48,640]{1,0:T(8,128)(2,1)S(1)}, u32[]{:S(2)}, u32[]{:S(2)}) collective-permute-start(bf16[48,640]{1,0:T(8,128)(2,1)S(1)} %get-tuple-element.52), channel_id=1, source_target_pairs={{0,5},{1,4},{2,7},{3,6},{4,1},{5,0},{6,3},{7,2},{8,13},{9,12},{10,... | collective-permute-start | bytes 184328 | tf_op jit(solution)/shard_map/ppermute | solution.py:437
  28.4 1.6 %collective-permute-start.9 = (bf16[24,5184]{1,0:T(8,128)(2,1)S(1)}, bf16[24,5184]{1,0:T(8,128)(2,1)S(1)}, u32[]{:S(2)}, u32[]{:S(2)}) collective-permute-start(bf16[24,5184]{1,0:T(8,128)(2,1)S(1)} %get-tuple-element.56), channel_id=1, source_target_pairs={{0,2},{1,3},{2,0},{3,1},{4,6},{5,7},{6,4},{7,5},{8,10},{9,11},{10,... | collective-permute-start | bytes 746504 | tf_op jit(solution)/shard_map/ppermute | solution.py:437
  30.2 7.1 %collective-permute-start.10 = (bf16[8,3968]{1,0:T(8,128)(2,1)S(1)}, bf16[8,3968]{1,0:T(8,128)(2,1)S(1)}, u32[]{:S(2)}, u32[]{:S(2)}) collective-permute-start(bf16[8,3968]{1,0:T(8,128)(2,1)S(1)} %get-tuple-element.57), channel_id=1, source_target_pairs={{0,24},{8,16},{16,8},{24,0},{1,25},{9,17},{17,9},{25,1},{2,26},{10... | collective-permute-start | bytes 190472 | tf_op jit(solution)/shard_map/ppermute | solution.py:437
  33.7 5.8 %collective-permute-start.11 = (bf16[8,3968]{1,0:T(8,128)(2,1)S(1)}, bf16[8,3968]{1,0:T(8,128)(2,1)S(1)}, u32[]{:S(2)}, u32[]{:S(2)}) collective-permute-start(bf16[8,3968]{1,0:T(8,128)(2,1)S(1)} %get-tuple-element.58), channel_id=1, source_target_pairs={{0,16},{8,24},{16,0},{24,8},{1,17},{9,25},{17,1},{25,9},{2,18},{10... | collective-permute-start | bytes 190472 | tf_op jit(solution)/shard_map/ppermute | solution.py:437
  33.7 5.8 %collective-permute-start.12 = (bf16[8,3968]{1,0:T(8,128)(2,1)S(1)}, bf16[8,3968]{1,0:T(8,128)(2,1)S(1)}, u32[]{:S(2)}, u32[]{:S(2)}) collective-permute-start(bf16[8,3968]{1,0:T(8,128)(2,1)S(1)} %get-tuple-element.59), channel_id=1, source_target_pairs={{0,8},{8,0},{16,24},{24,16},{1,9},{9,1},{17,25},{25,17},{2,10},{10... | collective-permute-start | bytes 190472 | tf_op jit(solution)/shard_map/ppermute | solution.py:437
  39.6 4.3 %collective-permute-start.13 = (bf16[8,3968]{1,0:T(8,128)(2,1)S(1)}, bf16[8,3968]{1,0:T(8,128)(2,1)S(1)}, u32[]{:S(2)}, u32[]{:S(2)}) collective-permute-start(bf16[8,3968]{1,0:T(8,128)(2,1)S(1)} %plane_sum.1.mine), channel_id=1, source_target_pairs={{0,1},{1,0},{2,3},{3,2},{4,5},{5,4},{6,7},{7,6},{8,9},{9,8},{10,11... | collective-permute-start | bytes 190472 | tf_op jit(solution)/shard_map/ppermute | solution.py:437

commit v16 on v15

--- a/solution.py
+++ b/solution.py
@@ -474,7 +474,7 @@
         pack_kernel, "pack", 4, 1 << 16, 1 << 19, array((count_128, 128), bf16), (),
         [vmem, pl.BlockSpec(memory_space=pl.ANY)],
     )(masked, weight_rows)
-    near, far, weight_rows = lax.optimization_barrier((near, far, weight_rows))
+    near, far, weight_rows, late = lax.optimization_barrier((near, far, weight_rows, packed))
     corner = call(
         corner_kernel, "corner", 4, 1 << 16, 1 << 18,
         array((128, 128), bf16),
@@ -490,7 +490,6 @@
             pltpu.VMEM((width + 4, mid, 9 * channels), bf16),
         ),
     )(masked, near, far, across, weight_rows)
-    late, bulk = lax.optimization_barrier((packed, bulk))
     bricks = [packed, across, in_plane(packed, CHIPS[2]), in_plane(late, CHIPS[3])]
 
     act, gp, *slices = call(

time: 44.8 us -> 44.8 us (level)
  transfers between devices with their start and end apart: 14 -> 14, of which waited for: 7 -> 6; matrix products, arithmetic and copies ran while one was open for 0% -> 0% of each run, Pallas kernels for 19% -> 19%
where the time goes in v16:
time: 44.8 us; the launch traced here: 44.6 us
  starting transfers between devices  20.3 us (45%)
  Pallas kernels  12.4 us (28%)
  waiting for transfers between devices  10.3 us (23%)
  local copies, waits for them, and re-layouts  0.84 us (2%)
  between operations  0.75 us (2%)
    ppermute x13, starting transfers between devices, swap(): return lax.ppermute(piece, axes, [(i, i ^ distance) for i in range(size)])  19.7 us
    pallas_call x13, Pallas kernels, run(): pl.pallas_call(body, out_shape=out_shape, in_specs=in_specs or [spec] * l...  12.4 us
    ppermute x13, waiting for transfers between devices, swap(): return lax.ppermute(piece, axes, [(i, i ^ distance) for i in range(size)])  10.3 us
  transfers between devices with their start and end apart: 14, of which 6 were waited for; matrix products, arithmetic and copies ran while one was open for 0% of the time, Pallas kernels for 19%

profile of v16, /device:TPU:0, one launch (start us, length us, event | category | flops | bytes accessed | tf_op | source)
XLA Modules:
  0.0 44.6 jit_solution(13871536490747083597)
XLA Ops:
  0.6 0.0 copy-start.1
  0.6 0.0 copy-start.2
  0.7 0.0 copy-start.3
  0.7 0.0 copy-start
  0.7 0.2 pick.1.first
  0.8 0.7 %copy-done.1 = bf16[8,8,8,192]{3,2,1,0:T(8,128)(2,1)S(1)} copy-done((bf16[8,8,8,192]{3,2,1,0:T(8,128)(2,1)S(1)}, bf16[8,8,8,192]{3,2,1,0:T(8,128)(2,1)}, u32[]{:S(2)}) %copy-start.1) | copy-done | bytes 196632
  1.6 0.1 copy-done.2
  1.7 0.0 copy-done.3
  1.7 0.2 prepare.1
  1.9 0.1 across.1
  2.0 3.0 %collective-permute-start.2 = (bf16[864,128]{1,0:T(8,128)(2,1)S(1)}, bf16[864,128]{1,0:T(8,128)(2,1)S(1)}, u32[]{:S(2)}, u32[]{:S(2)}) collective-permute-start(bf16[864,128]{1,0:T(8,128)(2,1)S(1)} %across.1), channel_id=1, source_target_pairs={{0,1},{1,0},{2,3},{3,2},{4,5},{5,4},{6,7},{7,6},{8,9},{9,8},{10,11... | collective-permute-start | bytes 663560 | tf_op jit(solution)/shard_map/ppermute | solution.py:437
  5.0 0.0 collective-permute-start
  5.0 0.7 %collective-permute-start.1 = (bf16[288,128]{1,0:T(8,128)(2,1)S(1)}, bf16[288,128]{1,0:T(8,128)(2,1)S(1)}, u32[]{:S(2)}, u32[]{:S(2)}) collective-permute-start(bf16[288,128]{1,0:T(8,128)(2,1)S(1)} %get-tuple-element.35), channel_id=1, source_target_pairs={{0,0},{2,4},{4,2},{6,8},{8,6},{10,12},{12,10},{14,16},{16,14},{18,... | collective-permute-start | bytes 221192 | tf_op jit(solution)/shard_map/ppermute | solution.py:463
  5.7 0.0 copy-done
  5.7 0.8 %turn.1.after.weight = bf16[5184,192]{1,0:T(8,128)(2,1)S(1)} custom-call(bf16[192,5184]{1,0:T(8,128)(2,1)S(1)} %bitcast.5), custom_call_target="tpu_custom_call" | custom-call | flops 1048576 | bytes 4194304 | tf_op jit(solution)/shard_map/turn/pallas_call | solution.py:408
  6.5 0.1 pack.1.refs_4_
  6.6 3.4 %collective-permute-start.4 = (bf16[768,128]{1,0:T(8,128)(2,1)S(1)}, bf16[768,128]{1,0:T(8,128)(2,1)S(1)}, u32[]{:S(2)}, u32[]{:S(2)}) collective-permute-start(bf16[768,128]{1,0:T(8,128)(2,1)S(1)} %pack.1.refs_4_), channel_id=1, source_target_pairs={{0,4},{1,5},{2,6},{3,7},{4,0},{5,1},{6,2},{7,3},{8,12},{9,13},{10,... | collective-permute-start | bytes 589832 | tf_op jit(solution)/shard_map/ppermute | solution.py:437
  10.0 0.0 collective-permute-done.near
  10.0 0.0 collective-permute-done.1.far
  10.0 0.2 corner.1
  10.2 0.1 collective-permute-start.3
  10.3 3.5 %collective-permute-start.8 = (bf16[768,128]{1,0:T(8,128)(2,1)S(1)}, bf16[768,128]{1,0:T(8,128)(2,1)S(1)}, u32[]{:S(2)}, u32[]{:S(2)}) collective-permute-start(bf16[768,128]{1,0:T(8,128)(2,1)S(1)} %pack.1.refs_4_), channel_id=1, source_target_pairs={{0,5},{1,4},{2,7},{3,6},{4,1},{5,0},{6,3},{7,2},{8,13},{9,12},{10,... | collective-permute-start | bytes 589832 | tf_op jit(solution)/shard_map/ppermute | solution.py:437
  13.9 0.0 collective-permute-done.2.across.refs_5_
  13.9 2.8 %bulk.1 = f32[10,80,192]{2,1,0:T(8,128)S(1)} custom-call(bf16[8,64,192]{2,1,0:T(8,128)(2,1)S(1)} %get-tuple-element.33.masked, bf16[288,128]{1,0:T(8,128)(2,1)S(1)} %collective-permute-done.near, bf16[288,128]{1,0:T(8,128)(2,1)S(1)} %collective-permute-done.1.far, bf16[864,128]{1,0:T(8,128)(2,1)S(1)} %collective-permute-done.2.across.refs_5_, ...), custom_call_target="tpu_custom_call" | custom-call | flops 1610612736 | bytes 1048576 | tf_op jit(solution)/shard_map/bulk/pallas_call | solution.py:408
  16.7 0.0 collective-permute-done.3.corner
  16.7 1.8 %forward.1 = (bf16[8,64,192]{2,1,0:T(8,128)(2,1)}, bf16[10,80,192]{2,1,0:T(8,128)(2,1)S(1)}, bf16[48,640]{1,0:T(8,128)(2,1)S(1)}, bf16[48,640]{1,0:T(8,128)(2,1)...) custom-call(f32[10,80,192]{2,1,0:T(8,128)S(1)} %bulk.1, bf16[8,64,192]{2,1,0:T(8,128)(2,1)S(1)} %get-tuple-element.38.cot, ...), custom_call_target="tpu_custom_call" | custom-call | flops 1610612736 | bytes 1048576 | tf_op jit(solution)/shard_map/forward/pallas_call | solution.py:408
  18.5 0.0 collective-permute-done.4.refs_6_
  18.5 0.5 %collective-permute-start.5 = (bf16[48,640]{1,0:T(8,128)(2,1)S(1)}, bf16[48,640]{1,0:T(8,128)(2,1)S(1)}, u32[]{:S(2)}, u32[]{:S(2)}) collective-permute-start(bf16[48,640]{1,0:T(8,128)(2,1)S(1)} %get-tuple-element.48), channel_id=1, source_target_pairs={{0,1},{1,0},{2,3},{3,2},{4,5},{5,4},{6,7},{7,6},{8,9},{9,8},{10,11... | collective-permute-start | bytes 184328 | tf_op jit(solution)/shard_map/ppermute | solution.py:437
  19.0 0.1 collective-permute-start.6
  19.0 2.9 %collective-permute-start.7 = (bf16[48,640]{1,0:T(8,128)(2,1)S(1)}, bf16[48,640]{1,0:T(8,128)(2,1)S(1)}, u32[]{:S(2)}, u32[]{:S(2)}) collective-permute-start(bf16[48,640]{1,0:T(8,128)(2,1)S(1)} %get-tuple-element.50), channel_id=1, source_target_pairs={{0,5},{1,4},{2,7},{3,6},{4,1},{5,0},{6,3},{7,2},{8,13},{9,12},{10,... | collective-permute-start | bytes 184328 | tf_op jit(solution)/shard_map/ppermute | solution.py:437
  22.0 0.0 collective-permute-done.8.refs_7_
  22.0 1.3 %collective-permute-done.5.refs_1_ = bf16[48,640]{1,0:T(8,128)(2,1)S(1)} collective-permute-done((bf16[48,640]{1,0:T(8,128)(2,1)S(1)}, bf16[48,640]{1,0:T(8,128)(2,1)S(1)}, u32[]{:S(2)}, u32[]{:S(2)}) %collective-permute-start.5) | collective-permute-done | bytes 61472 | tf_op jit(solution)/shard_map/ppermute | solution.py:437
  23.2 0.6 %collective-permute-done.6.refs_2_ = bf16[48,640]{1,0:T(8,128)(2,1)S(1)} collective-permute-done((bf16[48,640]{1,0:T(8,128)(2,1)S(1)}, bf16[48,640]{1,0:T(8,128)(2,1)S(1)}, u32[]{:S(2)}, u32[]{:S(2)}) %collective-permute-start.6) | collective-permute-done | bytes 61472 | tf_op jit(solution)/shard_map/ppermute | solution.py:437
  23.8 1.9 %collective-permute-done.7.refs_3_ = bf16[48,640]{1,0:T(8,128)(2,1)S(1)} collective-permute-done((bf16[48,640]{1,0:T(8,128)(2,1)S(1)}, bf16[48,640]{1,0:T(8,128)(2,1)S(1)}, u32[]{:S(2)}, u32[]{:S(2)}) %collective-permute-start.7) | collective-permute-done | bytes 61472 | tf_op jit(solution)/shard_map/ppermute | solution.py:437
  25.7 2.6 %kernel_gradient.1 = (f32[24,5184]{1,0:T(8,128)S(1)}, bf16[24,5184]{1,0:T(8,128)(2,1)S(1)}) custom-call(bf16[48,640]{1,0:T(8,128)(2,1)S(1)} %get-tuple-element.47.refs_0_, bf16[48,640]{1,0:T(8,128)(2,1)S(1)} %collective-permute-done.5.refs_1_, bf16[48,640]{1,0:T(8,128)(2,1)S(1)} %collective-permute-done.6.refs_2_, ...), custom_call_target="tpu_custom_call" | custom-call | flops 1358954496 | bytes 4194304 | tf_op jit(solution)/shard_map/kernel_gradient/pallas_call | solution.py:408
  28.3 0.1 collective-permute-start.9
  28.4 1.5 %collective-permute-done.9.other = bf16[24,5184]{1,0:T(8,128)(2,1)S(1)} collective-permute-done((bf16[24,5184]{1,0:T(8,128)(2,1)S(1)}, bf16[24,5184]{1,0:T(8,128)(2,1)S(1)}, u32[]{:S(2)}, u32[]{:S(2)}) %collective-permute-start.9) | collective-permute-done | bytes 248864 | tf_op jit(solution)/shard_map/ppermute | solution.py:437
  29.9 0.2 fold.1
  30.1 3.6 %collective-permute-start.10 = (bf16[8,3968]{1,0:T(8,128)(2,1)S(1)}, bf16[8,3968]{1,0:T(8,128)(2,1)S(1)}, u32[]{:S(2)}, u32[]{:S(2)}) collective-permute-start(bf16[8,3968]{1,0:T(8,128)(2,1)S(1)} %get-tuple-element.55), channel_id=1, source_target_pairs={{0,24},{8,16},{16,8},{24,0},{1,25},{9,17},{17,9},{25,1},{2,26},{10... | collective-permute-start | bytes 190472 | tf_op jit(solution)/shard_map/ppermute | solution.py:437
  33.7 0.0 collective-permute-start.11
  33.7 0.9 %collective-permute-start.12 = (bf16[8,3968]{1,0:T(8,128)(2,1)S(1)}, bf16[8,3968]{1,0:T(8,128)(2,1)S(1)}, u32[]{:S(2)}, u32[]{:S(2)}) collective-permute-start(bf16[8,3968]{1,0:T(8,128)(2,1)S(1)} %get-tuple-element.57), channel_id=1, source_target_pairs={{0,8},{8,0},{16,24},{24,16},{1,9},{9,1},{17,25},{25,17},{2,10},{10... | collective-permute-start | bytes 190472 | tf_op jit(solution)/shard_map/ppermute | solution.py:437
  34.6 2.7 %input_gradient.1 = bf16[8,64,192]{2,1,0:T(8,128)(2,1)} custom-call(bf16[10,80,192]{2,1,0:T(8,128)(2,1)S(1)} %get-tuple-element.42.gp, f32[8,64,128]{2,1,0:T(8,128)S(1)} %get-tuple-element.40.live, bf16[192,5184]{1,0:T(8,128)(2,1)S(1)} %bitcast.6), custom_call_target="tpu_custom_call" | custom-call | flops 1358954496 | bytes 4194304 | tf_op jit(solution)/shard_map/input_gradient/pallas_call | solution.py:408
  37.2 0.0 collective-permute-done.10.one
  37.2 2.2 %collective-permute-done.11.two = bf16[8,3968]{1,0:T(8,128)(2,1)S(1)} collective-permute-done((bf16[8,3968]{1,0:T(8,128)(2,1)S(1)}, bf16[8,3968]{1,0:T(8,128)(2,1)S(1)}, u32[]{:S(2)}, u32[]{:S(2)}) %collective-permute-start.11) | collective-permute-done | bytes 63520 | tf_op jit(solution)/shard_map/ppermute | solution.py:437
  39.5 0.0 collective-permute-done.12.three
  39.5 1.5 %collective-permute-start.13 = (bf16[8,3968]{1,0:T(8,128)(2,1)S(1)}, bf16[8,3968]{1,0:T(8,128)(2,1)S(1)}, u32[]{:S(2)}, u32[]{:S(2)}) collective-permute-start(bf16[8,3968]{1,0:T(8,128)(2,1)S(1)} %plane_sum.1.mine), channel_id=1, source_target_pairs={{0,1},{1,0},{2,3},{3,2},{4,5},{5,4},{6,7},{7,6},{8,9},{9,8},{10,11... | collective-permute-start | bytes 190472 | tf_op jit(solution)/shard_map/ppermute | solution.py:437
  41.0 2.8 %collective-permute-done.13.other = bf16[8,3968]{1,0:T(8,128)(2,1)S(1)} collective-permute-done((bf16[8,3968]{1,0:T(8,128)(2,1)S(1)}, bf16[8,3968]{1,0:T(8,128)(2,1)S(1)}, u32[]{:S(2)}, u32[]{:S(2)}) %collective-permute-start.13) | collective-permute-done | bytes 63520 | tf_op jit(solution)/shard_map/ppermute | solution.py:437
  43.8 0.8 %join.1 = f32[12,5184]{1,0:T(8,128)} custom-call(bf16[8,3968]{1,0:T(8,128)(2,1)S(1)} %plane_sum.1.mine, bf16[8,3968]{1,0:T(8,128)(2,1)S(1)} %collective-permute-done.13.other), custom_call_target="tpu_custom_call" | custom-call | flops 41472 | bytes 580608 | tf_op jit(solution)/shard_map/join/pallas_call | solution.py:408
  (1 shorter events, 0.0 us)
Async XLA Ops:
  0.6 1.0 %copy-start.1 = (bf16[8,8,8,192]{3,2,1,0:T(8,128)(2,1)S(1)}, bf16[8,8,8,192]{3,2,1,0:T(8,128)(2,1)}, u32[]{:S(2)}) copy-start(bf16[8,8,8,192]{3,2,1,0:T(8,128)(2,1)} %param.4) | copy-start | bytes 589828
  0.6 1.0 %copy-start.2 = (bf16[8,8,8,192]{3,2,1,0:T(8,128)(2,1)S(1)}, bf16[8,8,8,192]{3,2,1,0:T(8,128)(2,1)}, u32[]{:S(2)}) copy-start(bf16[8,8,8,192]{3,2,1,0:T(8,128)(2,1)} %param.7) | copy-start | bytes 589828
  0.7 1.0 %copy-start.3 = (s32[8,8,8]{2,1,0:T(8,128)S(1)}, s32[8,8,8]{2,1,0:T(8,128)}, u32[]{:S(2)}) copy-start(s32[8,8,8]{2,1,0:T(8,128)} %mask.1) | copy-start | bytes 6148
  0.7 5.0 %copy-start = (bf16[5184,192]{0,1:T(8,128)(2,1)S(1)}, bf16[5184,192]{0,1:T(8,128)(2,1)}, u32[]{:S(2)}) copy-start(bf16[5184,192]{0,1:T(8,128)(2,1)} %param.5) | copy-start | bytes 5971972
  2.0 11.9 %collective-permute-start.2 = (bf16[864,128]{1,0:T(8,128)(2,1)S(1)}, bf16[864,128]{1,0:T(8,128)(2,1)S(1)}, u32[]{:S(2)}, u32[]{:S(2)}) collective-permute-start(bf16[864,128]{1,0:T(8,128)(2,1)S(1)} %across.1), channel_id=1, source_target_pairs={{0,1},{1,0},{2,3},{3,2},{4,5},{5,4},{6,7},{7,6},{8,9},{9,8},{10,11... | collective-permute-start | bytes 663560 | tf_op jit(solution)/shard_map/ppermute | solution.py:437
  5.0 5.0 %collective-permute-start = (bf16[288,128]{1,0:T(8,128)(2,1)S(1)}, bf16[288,128]{1,0:T(8,128)(2,1)S(1)}, u32[]{:S(2)}, u32[]{:S(2)}) collective-permute-start(bf16[288,128]{1,0:T(8,128)(2,1)S(1)} %get-tuple-element.34), channel_id=1, source_target_pairs={{0,2},{2,0},{4,6},{6,4},{8,10},{10,8},{12,14},{14,12},{16,18},{18,... | collective-permute-start | bytes 221192 | tf_op jit(solution)/shard_map/ppermute | solution.py:437
  5.0 5.0 %collective-permute-start.1 = (bf16[288,128]{1,0:T(8,128)(2,1)S(1)}, bf16[288,128]{1,0:T(8,128)(2,1)S(1)}, u32[]{:S(2)}, u32[]{:S(2)}) collective-permute-start(bf16[288,128]{1,0:T(8,128)(2,1)S(1)} %get-tuple-element.35), channel_id=1, source_target_pairs={{0,0},{2,4},{4,2},{6,8},{8,6},{10,12},{12,10},{14,16},{16,14},{18,... | collective-permute-start | bytes 221192 | tf_op jit(solution)/shard_map/ppermute | solution.py:463
  6.6 11.9 %collective-permute-start.4 = (bf16[768,128]{1,0:T(8,128)(2,1)S(1)}, bf16[768,128]{1,0:T(8,128)(2,1)S(1)}, u32[]{:S(2)}, u32[]{:S(2)}) collective-permute-start(bf16[768,128]{1,0:T(8,128)(2,1)S(1)} %pack.1.refs_4_), channel_id=1, source_target_pairs={{0,4},{1,5},{2,6},{3,7},{4,0},{5,1},{6,2},{7,3},{8,12},{9,13},{10,... | collective-permute-start | bytes 589832 | tf_op jit(solution)/shard_map/ppermute | solution.py:437
  10.2 6.5 %collective-permute-start.3 = (bf16[128,128]{1,0:T(8,128)(2,1)S(1)}, bf16[128,128]{1,0:T(8,128)(2,1)S(1)}, u32[]{:S(2)}, u32[]{:S(2)}) collective-permute-start(bf16[128,128]{1,0:T(8,128)(2,1)S(1)} %corner.1), channel_id=1, source_target_pairs={{0,1},{1,0},{2,3},{3,2},{4,5},{5,4},{6,7},{7,6},{8,9},{9,8},{10,11... | collective-permute-start | bytes 98312 | tf_op jit(solution)/shard_map/ppermute | solution.py:437
  10.3 11.6 %collective-permute-start.8 = (bf16[768,128]{1,0:T(8,128)(2,1)S(1)}, bf16[768,128]{1,0:T(8,128)(2,1)S(1)}, u32[]{:S(2)}, u32[]{:S(2)}) collective-permute-start(bf16[768,128]{1,0:T(8,128)(2,1)S(1)} %pack.1.refs_4_), channel_id=1, source_target_pairs={{0,5},{1,4},{2,7},{3,6},{4,1},{5,0},{6,3},{7,2},{8,13},{9,12},{10,... | collective-permute-start | bytes 589832 | tf_op jit(solution)/shard_map/ppermute | solution.py:437
  18.5 4.8 %collective-permute-start.5 = (bf16[48,640]{1,0:T(8,128)(2,1)S(1)}, bf16[48,640]{1,0:T(8,128)(2,1)S(1)}, u32[]{:S(2)}, u32[]{:S(2)}) collective-permute-start(bf16[48,640]{1,0:T(8,128)(2,1)S(1)} %get-tuple-element.48), channel_id=1, source_target_pairs={{0,1},{1,0},{2,3},{3,2},{4,5},{5,4},{6,7},{7,6},{8,9},{9,8},{10,11... | collective-permute-start | bytes 184328 | tf_op jit(solution)/shard_map/ppermute | solution.py:437
  19.0 4.9 %collective-permute-start.6 = (bf16[48,640]{1,0:T(8,128)(2,1)S(1)}, bf16[48,640]{1,0:T(8,128)(2,1)S(1)}, u32[]{:S(2)}, u32[]{:S(2)}) collective-permute-start(bf16[48,640]{1,0:T(8,128)(2,1)S(1)} %get-tuple-element.49), channel_id=1, source_target_pairs={{0,4},{1,5},{2,6},{3,7},{4,0},{5,1},{6,2},{7,3},{8,12},{9,13},{10,... | collective-permute-start | bytes 184328 | tf_op jit(solution)/shard_map/ppermute | solution.py:437
  19.0 6.7 %collective-permute-start.7 = (bf16[48,640]{1,0:T(8,128)(2,1)S(1)}, bf16[48,640]{1,0:T(8,128)(2,1)S(1)}, u32[]{:S(2)}, u32[]{:S(2)}) collective-permute-start(bf16[48,640]{1,0:T(8,128)(2,1)S(1)} %get-tuple-element.50), channel_id=1, source_target_pairs={{0,5},{1,4},{2,7},{3,6},{4,1},{5,0},{6,3},{7,2},{8,13},{9,12},{10,... | collective-permute-start | bytes 184328 | tf_op jit(solution)/shard_map/ppermute | solution.py:437
  28.3 1.6 %collective-permute-start.9 = (bf16[24,5184]{1,0:T(8,128)(2,1)S(1)}, bf16[24,5184]{1,0:T(8,128)(2,1)S(1)}, u32[]{:S(2)}, u32[]{:S(2)}) collective-permute-start(bf16[24,5184]{1,0:T(8,128)(2,1)S(1)} %get-tuple-element.54), channel_id=1, source_target_pairs={{0,2},{1,3},{2,0},{3,1},{4,6},{5,7},{6,4},{7,5},{8,10},{9,11},{10,... | collective-permute-start | bytes 746504 | tf_op jit(solution)/shard_map/ppermute | solution.py:437
  30.1 7.1 %collective-permute-start.10 = (bf16[8,3968]{1,0:T(8,128)(2,1)S(1)}, bf16[8,3968]{1,0:T(8,128)(2,1)S(1)}, u32[]{:S(2)}, u32[]{:S(2)}) collective-permute-start(bf16[8,3968]{1,0:T(8,128)(2,1)S(1)} %get-tuple-element.55), channel_id=1, source_target_pairs={{0,24},{8,16},{16,8},{24,0},{1,25},{9,17},{17,9},{25,1},{2,26},{10... | collective-permute-start | bytes 190472 | tf_op jit(solution)/shard_map/ppermute | solution.py:437
  33.7 5.8 %collective-permute-start.11 = (bf16[8,3968]{1,0:T(8,128)(2,1)S(1)}, bf16[8,3968]{1,0:T(8,128)(2,1)S(1)}, u32[]{:S(2)}, u32[]{:S(2)}) collective-permute-start(bf16[8,3968]{1,0:T(8,128)(2,1)S(1)} %get-tuple-element.56), channel_id=1, source_target_pairs={{0,16},{8,24},{16,0},{24,8},{1,17},{9,25},{17,1},{25,9},{2,18},{10... | collective-permute-start | bytes 190472 | tf_op jit(solution)/shard_map/ppermute | solution.py:437
  33.7 5.8 %collective-permute-start.12 = (bf16[8,3968]{1,0:T(8,128)(2,1)S(1)}, bf16[8,3968]{1,0:T(8,128)(2,1)S(1)}, u32[]{:S(2)}, u32[]{:S(2)}) collective-permute-start(bf16[8,3968]{1,0:T(8,128)(2,1)S(1)} %get-tuple-element.57), channel_id=1, source_target_pairs={{0,8},{8,0},{16,24},{24,16},{1,9},{9,1},{17,25},{25,17},{2,10},{10... | collective-permute-start | bytes 190472 | tf_op jit(solution)/shard_map/ppermute | solution.py:437
  39.5 4.3 %collective-permute-start.13 = (bf16[8,3968]{1,0:T(8,128)(2,1)S(1)}, bf16[8,3968]{1,0:T(8,128)(2,1)S(1)}, u32[]{:S(2)}, u32[]{:S(2)}) collective-permute-start(bf16[8,3968]{1,0:T(8,128)(2,1)S(1)} %plane_sum.1.mine), channel_id=1, source_target_pairs={{0,1},{1,0},{2,3},{3,2},{4,5},{5,4},{6,7},{7,6},{8,9},{9,8},{10,11... | collective-permute-start | bytes 190472 | tf_op jit(solution)/shard_map/ppermute | solution.py:437

commit v17 on v16

--- a/solution.py
+++ b/solution.py
@@ -307,63 +307,64 @@
     out_ref[...] = (total.reshape(width, rows, channels) * live[:, :, 0:1]).astype(jnp.bfloat16)
 
 
-def kernel_grad_kernel(*refs):
-    chips = len(CHIPS)
-    received, bricks = refs[:chips], refs[chips : 2 * chips]
-    keep_ref, send_ref, slices, cols, part, masked = refs[2 * chips :]
+def pair_product(received, bricks, cols, masked):
     f32 = jnp.float32
     group, lanes = received[0].shape
-    blocks, per, lane, channels = masked.shape
+    per, lane, channels = masked.shape
     half = lane // 2
-    _, _, quad, side = position()
-    for i, distance in enumerate(CHIPS):
-        block, sided = distance // 4, side ^ (distance % 2)
-        slices[block, sided] = received[i][...]
-        at_rows = pl.ds(pl.multiple_of(sided * half, half), half)
+    side = position()[3]
+    for i, brick in enumerate(bricks):
+        at_rows = pl.ds(pl.multiple_of((side ^ i) * half, half), half)
         for x in range(per):
             shift = 64 * (x // (per // 2))
-            rest = bricks[i][pl.ds((per + x % (per // 2)) * half, half)]
-            masked[block, x, at_rows, :128] = bricks[i][pl.ds(x * half, half)]
-            masked[block, x, at_rows, 128:] = rest[:, shift : shift + 64]
+            rest = brick[pl.ds((per + x % (per // 2)) * half, half)]
+            masked[x, at_rows, :128] = brick[pl.ds(x * half, half)]
+            masked[x, at_rows, 128:] = rest[:, shift : shift + 64]
     at = lax.broadcasted_iota(jnp.int32, (group, lane), 1)
     y, z = at // DEPTH, at % DEPTH
     tall = lane // DEPTH
-    for block in range(blocks):
-        first = slices[block, 0].astype(f32)
-        second = slices[block, 1].astype(f32)
-        for k in range(per + 2):
-            one = first[:, k // 2 * lane : (k // 2 + 1) * lane]
-            two = second[:, k // 2 * lane : (k // 2 + 1) * lane]
-            if k % 2 == 0:
-                base = jnp.where(at < half, one, pltpu.roll(two, half, 1))
-            else:
-                base = jnp.where(at < half, pltpu.roll(one, half, 1), two)
-            pieces = []
-            for b in OFFSETS:
-                for c in OFFSETS:
-                    step = (DEPTH * b + c) % lane
-                    moved = base if step == 0 else pltpu.roll(base, step, 1)
-                    keep = (y - b >= 0) & (y - b < tall) & (z - c >= 0) & (z - c < DEPTH)
-                    pieces.append(jnp.where(keep, moved, 0.0))
-            slab = block * (per + 2) + k
-            cols[:, slab * lane : (slab + 1) * lane] = jnp.concatenate(pieces, axis=0).astype(
-                jnp.bfloat16
-            )
+    own, other = (ref[...].astype(f32) for ref in received)
+    first = jnp.where(side == 0, own, other)
+    second = jnp.where(side == 0, other, own)
+    for k in range(per + 2):
+        one = first[:, k // 2 * lane : (k // 2 + 1) * lane]
+        two = second[:, k // 2 * lane : (k // 2 + 1) * lane]
+        if k % 2 == 0:
+            base = jnp.where(at < half, one, pltpu.roll(two, half, 1))
+        else:
+            base = jnp.where(at < half, pltpu.roll(one, half, 1), two)
+        pieces = []
+        for b in OFFSETS:
+            for c in OFFSETS:
+                step = (DEPTH * b + c) % lane
+                moved = base if step == 0 else pltpu.roll(base, step, 1)
+                keep = (y - b >= 0) & (y - b < tall) & (z - c >= 0) & (z - c < DEPTH)
+                pieces.append(jnp.where(keep, moved, 0.0))
+        cols[:, k * lane : (k + 1) * lane] = jnp.concatenate(pieces, axis=0).astype(jnp.bfloat16)
+    field = masked[...].reshape(per * lane, channels)
     for a in range(3):
-        got = jnp.zeros((cols.shape[0], channels), f32)
-        for block in range(blocks):
-            start = (block * (per + 2) + 2 - a) * lane
-            got += jnp.dot(
-                cols[:, start : start + per * lane],
-                masked[block].reshape(per * lane, channels),
-                preferred_element_type=f32,
-            )
-        got = got.reshape(9, group, channels)
-        part[:, a * 9 * channels : (a + 1) * 9 * channels] = jnp.concatenate(
-            [got[tap] for tap in range(9)], axis=1
-        )
-    core = lax.rem(quad, 2)
-    half = group // 2
+        start = (2 - a) * lane
+        got = jnp.dot(
+            cols[:, start : start + per * lane], field, preferred_element_type=f32
+        ).reshape(9, group, channels)
+        yield a, jnp.concatenate([got[tap] for tap in range(9)], axis=1)
+
+
+def first_pair_kernel(own, other, brick, across, part_ref, cols, masked):
+    for a, rows in pair_product((own, other), (brick, across), cols, masked):
+        width = rows.shape[1]
+        part_ref[:, a * width : (a + 1) * width] = rows
+
+
+def second_pair_kernel(
+    before, own, other, brick, across, keep_ref, send_ref, part, cols, masked
+):
+    for a, rows in pair_product((own, other), (brick, across), cols, masked):
+        width = rows.shape[1]
+        at = slice(a * width, (a + 1) * width)
+        part[:, at] = before[:, at] + rows
+    core = lax.rem(position()[2], 2)
+    half = part.shape[0] // 2
     keep_ref[...] = part[pl.ds(pl.multiple_of(core * half, 8), half)]
     send_ref[...] = part[pl.ds(pl.multiple_of((1 - core) * half, 8), half)].astype(jnp.bfloat16)
 
@@ -515,19 +516,20 @@
         ),
     )(gp, live, weight.T)
 
-    blocks = QUAD // 2
-    chips = len(CHIPS)
     lanes = dense(total)[0]
+    scratch = (
+        pltpu.VMEM((9 * 2 * group, (width + 2) * SIDES * rows), bf16),
+        pltpu.VMEM((width, SIDES * rows, channels), bf16),
+    )
+    part = call(
+        first_pair_kernel, "first_pair", 16, 1 << 30, 2 << 20,
+        array((2 * group, total), f32), scratch,
+    )(*slices[:2], *bricks[:2])
     keep, fold = call(
-        kernel_grad_kernel, "kernel_gradient", 28, 2 * 432 * 3 * 2048 * 256, 4 << 20,
+        second_pair_kernel, "second_pair", 16, 1 << 30, 2 << 20,
         (array((group, total), f32), array((group, total), bf16)),
-        (
-            pltpu.VMEM((blocks, SIDES, 2 * group, span), bf16),
-            pltpu.VMEM((9 * 2 * group, blocks * (width + 2) * SIDES * rows), bf16),
-            pltpu.VMEM((2 * group, total), f32),
-            pltpu.VMEM((blocks, width, SIDES * rows, channels), bf16),
-        ),
-    )(*slices, *bricks)
+        (pltpu.VMEM((2 * group, total), f32),) + scratch,
+    )(part, *slices[2:], *bricks[2:])
     own, *sends = call(
         fold_kernel, "fold", 8, 8 * total * 4, 8 * total * 40,
         (array((8, lanes), f32),) + (array((8, lanes), bf16),) * (planes - 1),

time: 44.8 us -> 43.8 us (0.978)
  waiting for transfers between devices: 10.3 us -> 8.91 us
    ppermute x13, waiting for transfers between devices: 10.3 us -> 8.91 us  [swap(): return lax.ppermute(piece, axes, [(i, i ^ distance) for i in range(size)])]
    pallas_call x13 -> x14, Pallas kernels: 12.4 us -> 12.8 us  [run(): pl.pallas_call(body, out_shape=out_shape, in_specs=in_specs or [spec] * l...]
  transfers between devices with their start and end apart: 14 -> 14, of which waited for: 6 -> 5; matrix products, arithmetic and copies ran while one was open for 0% -> 0% of each run, Pallas kernels for 19% -> 22%
where the time goes in v17:
time: 43.8 us; the launch traced here: 43.6 us
  starting transfers between devices  20.3 us (46%)
  Pallas kernels  12.8 us (29%)
  waiting for transfers between devices  8.91 us (20%)
  local copies, waits for them, and re-layouts  0.84 us (2%)
  between operations  0.76 us (2%)
    ppermute x13, starting transfers between devices, swap(): return lax.ppermute(piece, axes, [(i, i ^ distance) for i in range(size)])  19.7 us
    pallas_call x14, Pallas kernels, run(): pl.pallas_call(body, out_shape=out_shape, in_specs=in_specs or [spec] * l...  12.8 us
    ppermute x13, waiting for transfers between devices, swap(): return lax.ppermute(piece, axes, [(i, i ^ distance) for i in range(size)])  8.91 us
  transfers between devices with their start and end apart: 14, of which 5 were waited for; matrix products, arithmetic and copies ran while one was open for 0% of the time, Pallas kernels for 22%

profile of v17, /device:TPU:0, one launch (start us, length us, event | category | flops | bytes accessed | tf_op | source)
XLA Modules:
  0.0 43.6 jit_solution(4092432730755956967)
XLA Ops:
  0.6 0.0 copy-start.1
  0.6 0.0 copy-start.2
  0.7 0.0 copy-start.3
  0.7 0.0 copy-start
  0.7 0.2 pick.1.first
  0.8 0.7 %copy-done.1 = bf16[8,8,8,192]{3,2,1,0:T(8,128)(2,1)S(1)} copy-done((bf16[8,8,8,192]{3,2,1,0:T(8,128)(2,1)S(1)}, bf16[8,8,8,192]{3,2,1,0:T(8,128)(2,1)}, u32[]{:S(2)}) %copy-start.1) | copy-done | bytes 196632
  1.6 0.1 copy-done.2
  1.7 0.0 copy-done.3
  1.7 0.2 prepare.1
  1.9 0.1 across.1
  2.0 3.0 %collective-permute-start.2 = (bf16[864,128]{1,0:T(8,128)(2,1)S(1)}, bf16[864,128]{1,0:T(8,128)(2,1)S(1)}, u32[]{:S(2)}, u32[]{:S(2)}) collective-permute-start(bf16[864,128]{1,0:T(8,128)(2,1)S(1)} %across.1), channel_id=1, source_target_pairs={{0,1},{1,0},{2,3},{3,2},{4,5},{5,4},{6,7},{7,6},{8,9},{9,8},{10,11... | collective-permute-start | bytes 663560 | tf_op jit(solution)/shard_map/ppermute | solution.py:438
  5.0 0.0 collective-permute-start
  5.0 0.7 %collective-permute-start.1 = (bf16[288,128]{1,0:T(8,128)(2,1)S(1)}, bf16[288,128]{1,0:T(8,128)(2,1)S(1)}, u32[]{:S(2)}, u32[]{:S(2)}) collective-permute-start(bf16[288,128]{1,0:T(8,128)(2,1)S(1)} %get-tuple-element.35), channel_id=1, source_target_pairs={{0,0},{2,4},{4,2},{6,8},{8,6},{10,12},{12,10},{14,16},{16,14},{18,... | collective-permute-start | bytes 221192 | tf_op jit(solution)/shard_map/ppermute | solution.py:464
  5.7 0.0 copy-done
  5.7 0.8 %turn.1.after.weight = bf16[5184,192]{1,0:T(8,128)(2,1)S(1)} custom-call(bf16[192,5184]{1,0:T(8,128)(2,1)S(1)} %bitcast.5), custom_call_target="tpu_custom_call" | custom-call | flops 1048576 | bytes 4194304 | tf_op jit(solution)/shard_map/turn/pallas_call | solution.py:409
  6.5 0.1 pack.1.brick
  6.6 3.4 %collective-permute-start.4 = (bf16[768,128]{1,0:T(8,128)(2,1)S(1)}, bf16[768,128]{1,0:T(8,128)(2,1)S(1)}, u32[]{:S(2)}, u32[]{:S(2)}) collective-permute-start(bf16[768,128]{1,0:T(8,128)(2,1)S(1)} %pack.1.brick), channel_id=1, source_target_pairs={{0,4},{1,5},{2,6},{3,7},{4,0},{5,1},{6,2},{7,3},{8,12},{9,13},{10,... | collective-permute-start | bytes 589832 | tf_op jit(solution)/shard_map/ppermute | solution.py:438
  10.0 0.0 collective-permute-done.near
  10.0 0.0 collective-permute-done.1.far
  10.0 0.2 corner.1
  10.2 0.1 collective-permute-start.3
  10.3 3.5 %collective-permute-start.8 = (bf16[768,128]{1,0:T(8,128)(2,1)S(1)}, bf16[768,128]{1,0:T(8,128)(2,1)S(1)}, u32[]{:S(2)}, u32[]{:S(2)}) collective-permute-start(bf16[768,128]{1,0:T(8,128)(2,1)S(1)} %pack.1.brick), channel_id=1, source_target_pairs={{0,5},{1,4},{2,7},{3,6},{4,1},{5,0},{6,3},{7,2},{8,13},{9,12},{10,... | collective-permute-start | bytes 589832 | tf_op jit(solution)/shard_map/ppermute | solution.py:438
  13.9 0.0 collective-permute-done.2.across
  13.9 2.8 %bulk.1 = f32[10,80,192]{2,1,0:T(8,128)S(1)} custom-call(bf16[8,64,192]{2,1,0:T(8,128)(2,1)S(1)} %get-tuple-element.33.masked, bf16[288,128]{1,0:T(8,128)(2,1)S(1)} %collective-permute-done.near, bf16[288,128]{1,0:T(8,128)(2,1)S(1)} %collective-permute-done.1.far, bf16[864,128]{1,0:T(8,128)(2,1)S(1)} %collective-permute-done.2.across, ...), custom_call_target="tpu_custom_call" | custom-call | flops 1610612736 | bytes 1048576 | tf_op jit(solution)/shard_map/bulk/pallas_call | solution.py:409
  16.7 0.0 collective-permute-done.3.corner
  16.7 1.8 %forward.1 = (bf16[8,64,192]{2,1,0:T(8,128)(2,1)}, bf16[10,80,192]{2,1,0:T(8,128)(2,1)S(1)}, bf16[48,640]{1,0:T(8,128)(2,1)S(1)}, bf16[48,640]{1,0:T(8,128)(2,1)...) custom-call(f32[10,80,192]{2,1,0:T(8,128)S(1)} %bulk.1, bf16[8,64,192]{2,1,0:T(8,128)(2,1)S(1)} %get-tuple-element.38.cot, ...), custom_call_target="tpu_custom_call" | custom-call | flops 1610612736 | bytes 1048576 | tf_op jit(solution)/shard_map/forward/pallas_call | solution.py:409
  18.5 0.0 collective-permute-done.4.brick
  18.5 0.5 %collective-permute-start.5 = (bf16[48,640]{1,0:T(8,128)(2,1)S(1)}, bf16[48,640]{1,0:T(8,128)(2,1)S(1)}, u32[]{:S(2)}, u32[]{:S(2)}) collective-permute-start(bf16[48,640]{1,0:T(8,128)(2,1)S(1)} %get-tuple-element.48), channel_id=1, source_target_pairs={{0,1},{1,0},{2,3},{3,2},{4,5},{5,4},{6,7},{7,6},{8,9},{9,8},{10,11... | collective-permute-start | bytes 184328 | tf_op jit(solution)/shard_map/ppermute | solution.py:438
  19.0 0.1 collective-permute-start.6
  19.0 2.9 %collective-permute-start.7 = (bf16[48,640]{1,0:T(8,128)(2,1)S(1)}, bf16[48,640]{1,0:T(8,128)(2,1)S(1)}, u32[]{:S(2)}, u32[]{:S(2)}) collective-permute-start(bf16[48,640]{1,0:T(8,128)(2,1)S(1)} %get-tuple-element.50), channel_id=1, source_target_pairs={{0,5},{1,4},{2,7},{3,6},{4,1},{5,0},{6,3},{7,2},{8,13},{9,12},{10,... | collective-permute-start | bytes 184328 | tf_op jit(solution)/shard_map/ppermute | solution.py:438
  22.0 1.3 %collective-permute-done.5.other = bf16[48,640]{1,0:T(8,128)(2,1)S(1)} collective-permute-done((bf16[48,640]{1,0:T(8,128)(2,1)S(1)}, bf16[48,640]{1,0:T(8,128)(2,1)S(1)}, u32[]{:S(2)}, u32[]{:S(2)}) %collective-permute-start.5) | collective-permute-done | bytes 61472 | tf_op jit(solution)/shard_map/ppermute | solution.py:438
  23.2 1.5 %first_pair.1.before = f32[48,5184]{1,0:T(8,128)S(1)} custom-call(bf16[48,640]{1,0:T(8,128)(2,1)S(1)} %get-tuple-element.47.own, bf16[48,640]{1,0:T(8,128)(2,1)S(1)} %collective-permute-done.5.other, bf16[768,128]{1,0:T(8,128)(2,1)S(1)} %pack.1.brick, bf16[864,128]{1,0:T(8,128)(2,1)S(1)} %collective-permute-done.2.across), custom_call_target="tpu_custom_call" | custom-call | flops 1073741824 | bytes 2097152 | tf_op jit(solution)/shard_map/first_pair/pallas_call | solution.py:409
  24.7 0.0 collective-permute-done.8.across
  24.7 0.0 collective-permute-done.6.own
  24.8 1.0 %collective-permute-done.7.other = bf16[48,640]{1,0:T(8,128)(2,1)S(1)} collective-permute-done((bf16[48,640]{1,0:T(8,128)(2,1)S(1)}, bf16[48,640]{1,0:T(8,128)(2,1)S(1)}, u32[]{:S(2)}, u32[]{:S(2)}) %collective-permute-start.7) | collective-permute-done | bytes 61472 | tf_op jit(solution)/shard_map/ppermute | solution.py:438
  25.7 1.6 %second_pair.1 = (f32[24,5184]{1,0:T(8,128)S(1)}, bf16[24,5184]{1,0:T(8,128)(2,1)S(1)}) custom-call(f32[48,5184]{1,0:T(8,128)S(1)} %first_pair.1.before, bf16[48,640]{1,0:T(8,128)(2,1)S(1)} %collective-permute-done.6.own, bf16[48,640]{1,0:T(8,128)(2,1)S(1)} %collective-permute-done.7.other, bf16[768,128]{1,0:T(8,128)(2,1)S(1)} %collective-permute-done.4.brick, ...), custom_call_target="tpu_custom_call" | custom-call | flops 1073741824 | bytes 2097152 | tf_op jit(solution)/shard_map/second_pair/pallas_call | solution.py:409
  27.3 0.1 collective-permute-start.9
  27.4 1.5 %collective-permute-done.9.other = bf16[24,5184]{1,0:T(8,128)(2,1)S(1)} collective-permute-done((bf16[24,5184]{1,0:T(8,128)(2,1)S(1)}, bf16[24,5184]{1,0:T(8,128)(2,1)S(1)}, u32[]{:S(2)}, u32[]{:S(2)}) %collective-permute-start.9) | collective-permute-done | bytes 248864 | tf_op jit(solution)/shard_map/ppermute | solution.py:438
  28.9 0.2 fold.1
  29.1 3.6 %collective-permute-start.10 = (bf16[8,3968]{1,0:T(8,128)(2,1)S(1)}, bf16[8,3968]{1,0:T(8,128)(2,1)S(1)}, u32[]{:S(2)}, u32[]{:S(2)}) collective-permute-start(bf16[8,3968]{1,0:T(8,128)(2,1)S(1)} %get-tuple-element.55), channel_id=1, source_target_pairs={{0,24},{8,16},{16,8},{24,0},{1,25},{9,17},{17,9},{25,1},{2,26},{10... | collective-permute-start | bytes 190472 | tf_op jit(solution)/shard_map/ppermute | solution.py:438
  32.7 0.0 collective-permute-start.11
  32.7 0.9 %collective-permute-start.12 = (bf16[8,3968]{1,0:T(8,128)(2,1)S(1)}, bf16[8,3968]{1,0:T(8,128)(2,1)S(1)}, u32[]{:S(2)}, u32[]{:S(2)}) collective-permute-start(bf16[8,3968]{1,0:T(8,128)(2,1)S(1)} %get-tuple-element.57), channel_id=1, source_target_pairs={{0,8},{8,0},{16,24},{24,16},{1,9},{9,1},{17,25},{25,17},{2,10},{10... | collective-permute-start | bytes 190472 | tf_op jit(solution)/shard_map/ppermute | solution.py:438
  33.6 2.6 %input_gradient.1 = bf16[8,64,192]{2,1,0:T(8,128)(2,1)} custom-call(bf16[10,80,192]{2,1,0:T(8,128)(2,1)S(1)} %get-tuple-element.42.gp, f32[8,64,128]{2,1,0:T(8,128)S(1)} %get-tuple-element.40.live, bf16[192,5184]{1,0:T(8,128)(2,1)S(1)} %bitcast.6), custom_call_target="tpu_custom_call" | custom-call | flops 1358954496 | bytes 4194304 | tf_op jit(solution)/shard_map/input_gradient/pallas_call | solution.py:409
  36.1 0.0 collective-permute-done.10.one
  36.1 2.3 %collective-permute-done.11.two = bf16[8,3968]{1,0:T(8,128)(2,1)S(1)} collective-permute-done((bf16[8,3968]{1,0:T(8,128)(2,1)S(1)}, bf16[8,3968]{1,0:T(8,128)(2,1)S(1)}, u32[]{:S(2)}, u32[]{:S(2)}) %collective-permute-start.11) | collective-permute-done | bytes 63520 | tf_op jit(solution)/shard_map/ppermute | solution.py:438
  38.5 0.0 collective-permute-done.12.three
  38.5 1.5 %collective-permute-start.13 = (bf16[8,3968]{1,0:T(8,128)(2,1)S(1)}, bf16[8,3968]{1,0:T(8,128)(2,1)S(1)}, u32[]{:S(2)}, u32[]{:S(2)}) collective-permute-start(bf16[8,3968]{1,0:T(8,128)(2,1)S(1)} %plane_sum.1.mine), channel_id=1, source_target_pairs={{0,1},{1,0},{2,3},{3,2},{4,5},{5,4},{6,7},{7,6},{8,9},{9,8},{10,11... | collective-permute-start | bytes 190472 | tf_op jit(solution)/shard_map/ppermute | solution.py:438
  40.0 2.8 %collective-permute-done.13.other = bf16[8,3968]{1,0:T(8,128)(2,1)S(1)} collective-permute-done((bf16[8,3968]{1,0:T(8,128)(2,1)S(1)}, bf16[8,3968]{1,0:T(8,128)(2,1)S(1)}, u32[]{:S(2)}, u32[]{:S(2)}) %collective-permute-start.13) | collective-permute-done | bytes 63520 | tf_op jit(solution)/shard_map/ppermute | solution.py:438
  42.8 0.8 %join.1 = f32[12,5184]{1,0:T(8,128)} custom-call(bf16[8,3968]{1,0:T(8,128)(2,1)S(1)} %plane_sum.1.mine, bf16[8,3968]{1,0:T(8,128)(2,1)S(1)} %collective-permute-done.13.other), custom_call_target="tpu_custom_call" | custom-call | flops 41472 | bytes 580608 | tf_op jit(solution)/shard_map/join/pallas_call | solution.py:409
  (1 shorter events, 0.0 us)
Async XLA Ops:
  0.6 1.0 %copy-start.1 = (bf16[8,8,8,192]{3,2,1,0:T(8,128)(2,1)S(1)}, bf16[8,8,8,192]{3,2,1,0:T(8,128)(2,1)}, u32[]{:S(2)}) copy-start(bf16[8,8,8,192]{3,2,1,0:T(8,128)(2,1)} %param.4) | copy-start | bytes 589828
  0.6 1.0 %copy-start.2 = (bf16[8,8,8,192]{3,2,1,0:T(8,128)(2,1)S(1)}, bf16[8,8,8,192]{3,2,1,0:T(8,128)(2,1)}, u32[]{:S(2)}) copy-start(bf16[8,8,8,192]{3,2,1,0:T(8,128)(2,1)} %param.7) | copy-start | bytes 589828
  0.7 1.0 %copy-start.3 = (s32[8,8,8]{2,1,0:T(8,128)S(1)}, s32[8,8,8]{2,1,0:T(8,128)}, u32[]{:S(2)}) copy-start(s32[8,8,8]{2,1,0:T(8,128)} %mask.1) | copy-start | bytes 6148
  0.7 5.0 %copy-start = (bf16[5184,192]{0,1:T(8,128)(2,1)S(1)}, bf16[5184,192]{0,1:T(8,128)(2,1)}, u32[]{:S(2)}) copy-start(bf16[5184,192]{0,1:T(8,128)(2,1)} %param.5) | copy-start | bytes 5971972
  2.0 11.9 %collective-permute-start.2 = (bf16[864,128]{1,0:T(8,128)(2,1)S(1)}, bf16[864,128]{1,0:T(8,128)(2,1)S(1)}, u32[]{:S(2)}, u32[]{:S(2)}) collective-permute-start(bf16[864,128]{1,0:T(8,128)(2,1)S(1)} %across.1), channel_id=1, source_target_pairs={{0,1},{1,0},{2,3},{3,2},{4,5},{5,4},{6,7},{7,6},{8,9},{9,8},{10,11... | collective-permute-start | bytes 663560 | tf_op jit(solution)/shard_map/ppermute | solution.py:438
  5.0 5.0 %collective-permute-start = (bf16[288,128]{1,0:T(8,128)(2,1)S(1)}, bf16[288,128]{1,0:T(8,128)(2,1)S(1)}, u32[]{:S(2)}, u32[]{:S(2)}) collective-permute-start(bf16[288,128]{1,0:T(8,128)(2,1)S(1)} %get-tuple-element.34), channel_id=1, source_target_pairs={{0,2},{2,0},{4,6},{6,4},{8,10},{10,8},{12,14},{14,12},{16,18},{18,... | collective-permute-start | bytes 221192 | tf_op jit(solution)/shard_map/ppermute | solution.py:438
  5.0 5.0 %collective-permute-start.1 = (bf16[288,128]{1,0:T(8,128)(2,1)S(1)}, bf16[288,128]{1,0:T(8,128)(2,1)S(1)}, u32[]{:S(2)}, u32[]{:S(2)}) collective-permute-start(bf16[288,128]{1,0:T(8,128)(2,1)S(1)} %get-tuple-element.35), channel_id=1, source_target_pairs={{0,0},{2,4},{4,2},{6,8},{8,6},{10,12},{12,10},{14,16},{16,14},{18,... | collective-permute-start | bytes 221192 | tf_op jit(solution)/shard_map/ppermute | solution.py:464
  6.6 11.9 %collective-permute-start.4 = (bf16[768,128]{1,0:T(8,128)(2,1)S(1)}, bf16[768,128]{1,0:T(8,128)(2,1)S(1)}, u32[]{:S(2)}, u32[]{:S(2)}) collective-permute-start(bf16[768,128]{1,0:T(8,128)(2,1)S(1)} %pack.1.brick), channel_id=1, source_target_pairs={{0,4},{1,5},{2,6},{3,7},{4,0},{5,1},{6,2},{7,3},{8,12},{9,13},{10,... | collective-permute-start | bytes 589832 | tf_op jit(solution)/shard_map/ppermute | solution.py:438
  10.2 6.5 %collective-permute-start.3 = (bf16[128,128]{1,0:T(8,128)(2,1)S(1)}, bf16[128,128]{1,0:T(8,128)(2,1)S(1)}, u32[]{:S(2)}, u32[]{:S(2)}) collective-permute-start(bf16[128,128]{1,0:T(8,128)(2,1)S(1)} %corner.1), channel_id=1, source_target_pairs={{0,1},{1,0},{2,3},{3,2},{4,5},{5,4},{6,7},{7,6},{8,9},{9,8},{10,11... | collective-permute-start | bytes 98312 | tf_op jit(solution)/shard_map/ppermute | solution.py:438
  10.3 14.4 %collective-permute-start.8 = (bf16[768,128]{1,0:T(8,128)(2,1)S(1)}, bf16[768,128]{1,0:T(8,128)(2,1)S(1)}, u32[]{:S(2)}, u32[]{:S(2)}) collective-permute-start(bf16[768,128]{1,0:T(8,128)(2,1)S(1)} %pack.1.brick), channel_id=1, source_target_pairs={{0,5},{1,4},{2,7},{3,6},{4,1},{5,0},{6,3},{7,2},{8,13},{9,12},{10,... | collective-permute-start | bytes 589832 | tf_op jit(solution)/shard_map/ppermute | solution.py:438
  18.5 4.8 %collective-permute-start.5 = (bf16[48,640]{1,0:T(8,128)(2,1)S(1)}, bf16[48,640]{1,0:T(8,128)(2,1)S(1)}, u32[]{:S(2)}, u32[]{:S(2)}) collective-permute-start(bf16[48,640]{1,0:T(8,128)(2,1)S(1)} %get-tuple-element.48), channel_id=1, source_target_pairs={{0,1},{1,0},{2,3},{3,2},{4,5},{5,4},{6,7},{7,6},{8,9},{9,8},{10,11... | collective-permute-start | bytes 184328 | tf_op jit(solution)/shard_map/ppermute | solution.py:438
  19.0 5.8 %collective-permute-start.6 = (bf16[48,640]{1,0:T(8,128)(2,1)S(1)}, bf16[48,640]{1,0:T(8,128)(2,1)S(1)}, u32[]{:S(2)}, u32[]{:S(2)}) collective-permute-start(bf16[48,640]{1,0:T(8,128)(2,1)S(1)} %get-tuple-element.49), channel_id=1, source_target_pairs={{0,4},{1,5},{2,6},{3,7},{4,0},{5,1},{6,2},{7,3},{8,12},{9,13},{10,... | collective-permute-start | bytes 184328 | tf_op jit(solution)/shard_map/ppermute | solution.py:438
  19.0 6.7 %collective-permute-start.7 = (bf16[48,640]{1,0:T(8,128)(2,1)S(1)}, bf16[48,640]{1,0:T(8,128)(2,1)S(1)}, u32[]{:S(2)}, u32[]{:S(2)}) collective-permute-start(bf16[48,640]{1,0:T(8,128)(2,1)S(1)} %get-tuple-element.50), channel_id=1, source_target_pairs={{0,5},{1,4},{2,7},{3,6},{4,1},{5,0},{6,3},{7,2},{8,13},{9,12},{10,... | collective-permute-start | bytes 184328 | tf_op jit(solution)/shard_map/ppermute | solution.py:438
  27.3 1.6 %collective-permute-start.9 = (bf16[24,5184]{1,0:T(8,128)(2,1)S(1)}, bf16[24,5184]{1,0:T(8,128)(2,1)S(1)}, u32[]{:S(2)}, u32[]{:S(2)}) collective-permute-start(bf16[24,5184]{1,0:T(8,128)(2,1)S(1)} %get-tuple-element.54), channel_id=1, source_target_pairs={{0,2},{1,3},{2,0},{3,1},{4,6},{5,7},{6,4},{7,5},{8,10},{9,11},{10,... | collective-permute-start | bytes 746504 | tf_op jit(solution)/shard_map/ppermute | solution.py:438
  29.1 7.0 %collective-permute-start.10 = (bf16[8,3968]{1,0:T(8,128)(2,1)S(1)}, bf16[8,3968]{1,0:T(8,128)(2,1)S(1)}, u32[]{:S(2)}, u32[]{:S(2)}) collective-permute-start(bf16[8,3968]{1,0:T(8,128)(2,1)S(1)} %get-tuple-element.55), channel_id=1, source_target_pairs={{0,24},{8,16},{16,8},{24,0},{1,25},{9,17},{17,9},{25,1},{2,26},{10... | collective-permute-start | bytes 190472 | tf_op jit(solution)/shard_map/ppermute | solution.py:438
  32.7 5.8 %collective-permute-start.11 = (bf16[8,3968]{1,0:T(8,128)(2,1)S(1)}, bf16[8,3968]{1,0:T(8,128)(2,1)S(1)}, u32[]{:S(2)}, u32[]{:S(2)}) collective-permute-start(bf16[8,3968]{1,0:T(8,128)(2,1)S(1)} %get-tuple-element.56), channel_id=1, source_target_pairs={{0,16},{8,24},{16,0},{24,8},{1,17},{9,25},{17,1},{25,9},{2,18},{10... | collective-permute-start | bytes 190472 | tf_op jit(solution)/shard_map/ppermute | solution.py:438
  32.7 5.8 %collective-permute-start.12 = (bf16[8,3968]{1,0:T(8,128)(2,1)S(1)}, bf16[8,3968]{1,0:T(8,128)(2,1)S(1)}, u32[]{:S(2)}, u32[]{:S(2)}) collective-permute-start(bf16[8,3968]{1,0:T(8,128)(2,1)S(1)} %get-tuple-element.57), channel_id=1, source_target_pairs={{0,8},{8,0},{16,24},{24,16},{1,9},{9,1},{17,25},{25,17},{2,10},{10... | collective-permute-start | bytes 190472 | tf_op jit(solution)/shard_map/ppermute | solution.py:438
  38.5 4.3 %collective-permute-start.13 = (bf16[8,3968]{1,0:T(8,128)(2,1)S(1)}, bf16[8,3968]{1,0:T(8,128)(2,1)S(1)}, u32[]{:S(2)}, u32[]{:S(2)}) collective-permute-start(bf16[8,3968]{1,0:T(8,128)(2,1)S(1)} %plane_sum.1.mine), channel_id=1, source_target_pairs={{0,1},{1,0},{2,3},{3,2},{4,5},{5,4},{6,7},{7,6},{8,9},{9,8},{10,11... | collective-permute-start | bytes 190472 | tf_op jit(solution)/shard_map/ppermute | solution.py:438

commit v18 on v17

--- a/solution.py
+++ b/solution.py
@@ -212,12 +212,11 @@
     corners = jnp.concatenate([corners[0] * use_left, corners[1] * use_right], axis=0)
     sources = ((0, 1, None, None), (1, None, None, 2), (None, None, 2, 3))
     blank = jnp.zeros((DEPTH, channels), f32)
+    six = 6 * channels
     for c in OFFSETS:
         moved = shift_z(corners.reshape(8, DEPTH, channels), c)
-        for b in OFFSETS:
-            low = {-1: (0, 1), 0: (1, None), 1: (None, None)}[b]
-            high = {-1: (None, None), 0: (None, 0), 1: (0, 1)}[b]
-            at = ((b + 1) * 3 + c + 1) * channels
+        for b, low, high in ((0, (0, 1), (None, 0)), (1, (1, None), (0, 1))):
+            at = (b * 3 + c + 1) * channels
             parts = []
             for slab in range(4):
                 for below, above in zip(low, high):
@@ -233,12 +232,10 @@
                 cols[a, :, at : at + channels] = jnp.concatenate(rows_a, axis=0).astype(
                     jnp.bfloat16
                 )
-    nine = 9 * channels
     share = jnp.zeros((4 * halo, channels), f32)
     for a in range(3):
-        share += jnp.dot(
-            cols[a], weight[a * nine : (a + 1) * nine, :], preferred_element_type=f32
-        )
+        taps = pl.ds(pl.multiple_of((3 * a + 1 - side) * 3 * channels, 16), six)
+        share += jnp.dot(cols[a], weight[taps], preferred_element_type=f32)
     share = share.reshape(4, halo, channels)
     total[...] = bulk[...]
     at = pl.ds(pl.multiple_of((1 - side) * (mid - halo), DEPTH), halo)
@@ -350,7 +347,7 @@
         yield a, jnp.concatenate([got[tap] for tap in range(9)], axis=1)
 
 
-def first_pair_kernel(own, other, brick, across, part_ref, cols, masked):
+def first_pair_kernel(other, own, across, brick, part_ref, cols, masked):
     for a, rows in pair_product((own, other), (brick, across), cols, masked):
         width = rows.shape[1]
         part_ref[:, a * width : (a + 1) * width] = rows
@@ -499,7 +496,7 @@
         + (array((2 * group, span), bf16),) * len(CHIPS),
         (
             pltpu.VMEM((2, rows, channels), f32),
-            pltpu.VMEM((3, 4 * halo, 9 * channels), bf16),
+            pltpu.VMEM((3, 4 * halo, 6 * channels), bf16),
             pltpu.VMEM((width + 2, mid, channels), f32),
             pltpu.VMEM((MEMBERS, group, span), f32),
         ),
@@ -524,12 +521,12 @@
     part = call(
         first_pair_kernel, "first_pair", 16, 1 << 30, 2 << 20,
         array((2 * group, total), f32), scratch,
-    )(*slices[:2], *bricks[:2])
+    )(*slices[3:1:-1], *bricks[3:1:-1])
     keep, fold = call(
         second_pair_kernel, "second_pair", 16, 1 << 30, 2 << 20,
         (array((group, total), f32), array((group, total), bf16)),
         (pltpu.VMEM((2 * group, total), f32),) + scratch,
-    )(part, *slices[2:], *bricks[2:])
+    )(part, *slices[:2], *bricks[:2])
     own, *sends = call(
         fold_kernel, "fold", 8, 8 * total * 4, 8 * total * 40,
         (array((8, lanes), f32),) + (array((8, lanes), bf16),) * (planes - 1),

time: 43.8 us -> 44 us (level)
  no operation moved by 1% of the time
where the time goes in v18:
time: 44 us; the launch traced here: 43.8 us
  starting transfers between devices  20.4 us (46%)
  Pallas kernels  12.7 us (29%)
  waiting for transfers between devices  9.13 us (21%)
  local copies, waits for them, and re-layouts  0.84 us (2%)
  between operations  0.75 us (2%)
    ppermute x13, starting transfers between devices, swap(): return lax.ppermute(piece, axes, [(i, i ^ distance) for i in range(size)])  19.8 us
    pallas_call x14, Pallas kernels, run(): pl.pallas_call(body, out_shape=out_shape, in_specs=in_specs or [spec] * l...  12.7 us
    ppermute x13, waiting for transfers between devices, swap(): return lax.ppermute(piece, axes, [(i, i ^ distance) for i in range(size)])  9.13 us
  transfers between devices with their start and end apart: 14, of which 5 were waited for; matrix products, arithmetic and copies ran while one was open for 0% of the time, Pallas kernels for 22%

profile of v18, /device:TPU:0, one launch (start us, length us, event | category | flops | bytes accessed | tf_op | source)
XLA Modules:
  0.0 43.8 jit_solution(3332384885400460650)
XLA Ops:
  0.6 0.0 copy-start.1
  0.6 0.0 copy-start.2
  0.7 0.0 copy-start.3
  0.7 0.0 copy-start
  0.7 0.2 pick.1.first
  0.8 0.7 %copy-done.1 = bf16[8,8,8,192]{3,2,1,0:T(8,128)(2,1)S(1)} copy-done((bf16[8,8,8,192]{3,2,1,0:T(8,128)(2,1)S(1)}, bf16[8,8,8,192]{3,2,1,0:T(8,128)(2,1)}, u32[]{:S(2)}) %copy-start.1) | copy-done | bytes 196632
  1.6 0.1 copy-done.2
  1.7 0.0 copy-done.3
  1.7 0.2 prepare.1
  1.9 0.1 across.1
  2.0 3.0 %collective-permute-start.2 = (bf16[864,128]{1,0:T(8,128)(2,1)S(1)}, bf16[864,128]{1,0:T(8,128)(2,1)S(1)}, u32[]{:S(2)}, u32[]{:S(2)}) collective-permute-start(bf16[864,128]{1,0:T(8,128)(2,1)S(1)} %across.1), channel_id=1, source_target_pairs={{0,1},{1,0},{2,3},{3,2},{4,5},{5,4},{6,7},{7,6},{8,9},{9,8},{10,11... | collective-permute-start | bytes 663560 | tf_op jit(solution)/shard_map/ppermute | solution.py:435
  5.0 0.0 collective-permute-start
  5.0 0.7 %collective-permute-start.1 = (bf16[288,128]{1,0:T(8,128)(2,1)S(1)}, bf16[288,128]{1,0:T(8,128)(2,1)S(1)}, u32[]{:S(2)}, u32[]{:S(2)}) collective-permute-start(bf16[288,128]{1,0:T(8,128)(2,1)S(1)} %get-tuple-element.35), channel_id=1, source_target_pairs={{0,0},{2,4},{4,2},{6,8},{8,6},{10,12},{12,10},{14,16},{16,14},{18,... | collective-permute-start | bytes 221192 | tf_op jit(solution)/shard_map/ppermute | solution.py:461
  5.7 0.0 copy-done
  5.7 0.8 %turn.1.after.weight = bf16[5184,192]{1,0:T(8,128)(2,1)S(1)} custom-call(bf16[192,5184]{1,0:T(8,128)(2,1)S(1)} %bitcast.5), custom_call_target="tpu_custom_call" | custom-call | flops 1048576 | bytes 4194304 | tf_op jit(solution)/shard_map/turn/pallas_call | solution.py:406
  6.5 0.1 pack.1.brick
  6.6 3.4 %collective-permute-start.4 = (bf16[768,128]{1,0:T(8,128)(2,1)S(1)}, bf16[768,128]{1,0:T(8,128)(2,1)S(1)}, u32[]{:S(2)}, u32[]{:S(2)}) collective-permute-start(bf16[768,128]{1,0:T(8,128)(2,1)S(1)} %pack.1.brick), channel_id=1, source_target_pairs={{0,4},{1,5},{2,6},{3,7},{4,0},{5,1},{6,2},{7,3},{8,12},{9,13},{10,... | collective-permute-start | bytes 589832 | tf_op jit(solution)/shard_map/ppermute | solution.py:435
  10.0 0.0 collective-permute-done.near
  10.0 0.0 collective-permute-done.1.far
  10.0 0.2 corner.1
  10.2 0.1 collective-permute-start.3
  10.3 3.5 %collective-permute-start.7 = (bf16[768,128]{1,0:T(8,128)(2,1)S(1)}, bf16[768,128]{1,0:T(8,128)(2,1)S(1)}, u32[]{:S(2)}, u32[]{:S(2)}) collective-permute-start(bf16[768,128]{1,0:T(8,128)(2,1)S(1)} %pack.1.brick), channel_id=1, source_target_pairs={{0,5},{1,4},{2,7},{3,6},{4,1},{5,0},{6,3},{7,2},{8,13},{9,12},{10,... | collective-permute-start | bytes 589832 | tf_op jit(solution)/shard_map/ppermute | solution.py:435
  13.9 0.0 collective-permute-done.2.across
  13.9 2.8 %bulk.1 = f32[10,80,192]{2,1,0:T(8,128)S(1)} custom-call(bf16[8,64,192]{2,1,0:T(8,128)(2,1)S(1)} %get-tuple-element.33.masked, bf16[288,128]{1,0:T(8,128)(2,1)S(1)} %collective-permute-done.near, bf16[288,128]{1,0:T(8,128)(2,1)S(1)} %collective-permute-done.1.far, bf16[864,128]{1,0:T(8,128)(2,1)S(1)} %collective-permute-done.2.across, ...), custom_call_target="tpu_custom_call" | custom-call | flops 1610612736 | bytes 1048576 | tf_op jit(solution)/shard_map/bulk/pallas_call | solution.py:406
  16.7 0.0 collective-permute-done.3.corner
  16.7 1.7 %forward.1 = (bf16[8,64,192]{2,1,0:T(8,128)(2,1)}, bf16[10,80,192]{2,1,0:T(8,128)(2,1)S(1)}, bf16[48,640]{1,0:T(8,128)(2,1)S(1)}, bf16[48,640]{1,0:T(8,128)(2,1)...) custom-call(f32[10,80,192]{2,1,0:T(8,128)S(1)} %bulk.1, bf16[8,64,192]{2,1,0:T(8,128)(2,1)S(1)} %get-tuple-element.38.cot, ...), custom_call_target="tpu_custom_call" | custom-call | flops 1610612736 | bytes 1048576 | tf_op jit(solution)/shard_map/forward/pallas_call | solution.py:406
  18.4 0.0 collective-permute-done.4.brick
  18.4 0.0 collective-permute-start.5
  18.4 2.0 %collective-permute-start.6 = (bf16[48,640]{1,0:T(8,128)(2,1)S(1)}, bf16[48,640]{1,0:T(8,128)(2,1)S(1)}, u32[]{:S(2)}, u32[]{:S(2)}) collective-permute-start(bf16[48,640]{1,0:T(8,128)(2,1)S(1)} %get-tuple-element.48), channel_id=1, source_target_pairs={{0,4},{1,5},{2,6},{3,7},{4,0},{5,1},{6,2},{7,3},{8,12},{9,13},{10,... | collective-permute-start | bytes 184328 | tf_op jit(solution)/shard_map/ppermute | solution.py:435
  20.3 1.5 %collective-permute-start.8 = (bf16[48,640]{1,0:T(8,128)(2,1)S(1)}, bf16[48,640]{1,0:T(8,128)(2,1)S(1)}, u32[]{:S(2)}, u32[]{:S(2)}) collective-permute-start(bf16[48,640]{1,0:T(8,128)(2,1)S(1)} %get-tuple-element.52), channel_id=1, source_target_pairs={{0,1},{1,0},{2,3},{3,2},{4,5},{5,4},{6,7},{7,6},{8,9},{9,8},{10,11... | collective-permute-start | bytes 184328 | tf_op jit(solution)/shard_map/ppermute | solution.py:435
  21.8 0.0 collective-permute-done.7.across
  21.9 2.3 %collective-permute-done.5.other = bf16[48,640]{1,0:T(8,128)(2,1)S(1)} collective-permute-done((bf16[48,640]{1,0:T(8,128)(2,1)S(1)}, bf16[48,640]{1,0:T(8,128)(2,1)S(1)}, u32[]{:S(2)}, u32[]{:S(2)}) %collective-permute-start.5) | collective-permute-done | bytes 61472 | tf_op jit(solution)/shard_map/ppermute | solution.py:435
  24.1 0.3 collective-permute-done.6.own
  24.4 1.5 %first_pair.1.before = f32[48,5184]{1,0:T(8,128)S(1)} custom-call(bf16[48,640]{1,0:T(8,128)(2,1)S(1)} %collective-permute-done.5.other, bf16[48,640]{1,0:T(8,128)(2,1)S(1)} %collective-permute-done.6.own, bf16[768,128]{1,0:T(8,128)(2,1)S(1)} %collective-permute-done.7.across, bf16[768,128]{1,0:T(8,128)(2,1)S(1)} %collective-permute-done.4.brick), custom_call_target="tpu_custom_call" | custom-call | flops 1073741824 | bytes 2097152 | tf_op jit(solution)/shard_map/first_pair/pallas_call | solution.py:406
  25.9 0.0 collective-permute-done.8.other
  25.9 1.6 %second_pair.1 = (f32[24,5184]{1,0:T(8,128)S(1)}, bf16[24,5184]{1,0:T(8,128)(2,1)S(1)}) custom-call(f32[48,5184]{1,0:T(8,128)S(1)} %first_pair.1.before, bf16[48,640]{1,0:T(8,128)(2,1)S(1)} %get-tuple-element.51.own, bf16[48,640]{1,0:T(8,128)(2,1)S(1)} %collective-permute-done.8.other, bf16[768,128]{1,0:T(8,128)(2,1)S(1)} %pack.1.brick, ...), custom_call_target="tpu_custom_call" | custom-call | flops 1073741824 | bytes 2097152 | tf_op jit(solution)/shard_map/second_pair/pallas_call | solution.py:406
  27.5 0.1 collective-permute-start.9
  27.7 1.4 %collective-permute-done.9.other = bf16[24,5184]{1,0:T(8,128)(2,1)S(1)} collective-permute-done((bf16[24,5184]{1,0:T(8,128)(2,1)S(1)}, bf16[24,5184]{1,0:T(8,128)(2,1)S(1)}, u32[]{:S(2)}, u32[]{:S(2)}) %collective-permute-start.9) | collective-permute-done | bytes 248864 | tf_op jit(solution)/shard_map/ppermute | solution.py:435
  29.1 0.2 fold.1
  29.3 3.3 %collective-permute-start.10 = (bf16[8,3968]{1,0:T(8,128)(2,1)S(1)}, bf16[8,3968]{1,0:T(8,128)(2,1)S(1)}, u32[]{:S(2)}, u32[]{:S(2)}) collective-permute-start(bf16[8,3968]{1,0:T(8,128)(2,1)S(1)} %get-tuple-element.55), channel_id=1, source_target_pairs={{0,24},{8,16},{16,8},{24,0},{1,25},{9,17},{17,9},{25,1},{2,26},{10... | collective-permute-start | bytes 190472 | tf_op jit(solution)/shard_map/ppermute | solution.py:435
  32.6 0.0 collective-permute-start.11
  32.6 1.1 %collective-permute-start.12 = (bf16[8,3968]{1,0:T(8,128)(2,1)S(1)}, bf16[8,3968]{1,0:T(8,128)(2,1)S(1)}, u32[]{:S(2)}, u32[]{:S(2)}) collective-permute-start(bf16[8,3968]{1,0:T(8,128)(2,1)S(1)} %get-tuple-element.57), channel_id=1, source_target_pairs={{0,8},{8,0},{16,24},{24,16},{1,9},{9,1},{17,25},{25,17},{2,10},{10... | collective-permute-start | bytes 190472 | tf_op jit(solution)/shard_map/ppermute | solution.py:435
  33.8 2.6 %input_gradient.1 = bf16[8,64,192]{2,1,0:T(8,128)(2,1)} custom-call(bf16[10,80,192]{2,1,0:T(8,128)(2,1)S(1)} %get-tuple-element.42.gp, f32[8,64,128]{2,1,0:T(8,128)S(1)} %get-tuple-element.40.live, bf16[192,5184]{1,0:T(8,128)(2,1)S(1)} %bitcast.6), custom_call_target="tpu_custom_call" | custom-call | flops 1358954496 | bytes 4194304 | tf_op jit(solution)/shard_map/input_gradient/pallas_call | solution.py:406
  36.3 0.0 collective-permute-done.10.one
  36.4 2.3 %collective-permute-done.11.two = bf16[8,3968]{1,0:T(8,128)(2,1)S(1)} collective-permute-done((bf16[8,3968]{1,0:T(8,128)(2,1)S(1)}, bf16[8,3968]{1,0:T(8,128)(2,1)S(1)}, u32[]{:S(2)}, u32[]{:S(2)}) %collective-permute-start.11) | collective-permute-done | bytes 63520 | tf_op jit(solution)/shard_map/ppermute | solution.py:435
  38.7 0.0 collective-permute-done.12.three
  38.7 1.5 %collective-permute-start.13 = (bf16[8,3968]{1,0:T(8,128)(2,1)S(1)}, bf16[8,3968]{1,0:T(8,128)(2,1)S(1)}, u32[]{:S(2)}, u32[]{:S(2)}) collective-permute-start(bf16[8,3968]{1,0:T(8,128)(2,1)S(1)} %plane_sum.1.mine), channel_id=1, source_target_pairs={{0,1},{1,0},{2,3},{3,2},{4,5},{5,4},{6,7},{7,6},{8,9},{9,8},{10,11... | collective-permute-start | bytes 190472 | tf_op jit(solution)/shard_map/ppermute | solution.py:435
  40.2 2.8 %collective-permute-done.13.other = bf16[8,3968]{1,0:T(8,128)(2,1)S(1)} collective-permute-done((bf16[8,3968]{1,0:T(8,128)(2,1)S(1)}, bf16[8,3968]{1,0:T(8,128)(2,1)S(1)}, u32[]{:S(2)}, u32[]{:S(2)}) %collective-permute-start.13) | collective-permute-done | bytes 63520 | tf_op jit(solution)/shard_map/ppermute | solution.py:435
  43.0 0.8 %join.1 = f32[12,5184]{1,0:T(8,128)} custom-call(bf16[8,3968]{1,0:T(8,128)(2,1)S(1)} %plane_sum.1.mine, bf16[8,3968]{1,0:T(8,128)(2,1)S(1)} %collective-permute-done.13.other), custom_call_target="tpu_custom_call" | custom-call | flops 41472 | bytes 580608 | tf_op jit(solution)/shard_map/join/pallas_call | solution.py:406
  (1 shorter events, 0.0 us)
Async XLA Ops:
  0.6 1.0 %copy-start.1 = (bf16[8,8,8,192]{3,2,1,0:T(8,128)(2,1)S(1)}, bf16[8,8,8,192]{3,2,1,0:T(8,128)(2,1)}, u32[]{:S(2)}) copy-start(bf16[8,8,8,192]{3,2,1,0:T(8,128)(2,1)} %param.4) | copy-start | bytes 589828
  0.6 1.0 %copy-start.2 = (bf16[8,8,8,192]{3,2,1,0:T(8,128)(2,1)S(1)}, bf16[8,8,8,192]{3,2,1,0:T(8,128)(2,1)}, u32[]{:S(2)}) copy-start(bf16[8,8,8,192]{3,2,1,0:T(8,128)(2,1)} %param.7) | copy-start | bytes 589828
  0.7 1.0 %copy-start.3 = (s32[8,8,8]{2,1,0:T(8,128)S(1)}, s32[8,8,8]{2,1,0:T(8,128)}, u32[]{:S(2)}) copy-start(s32[8,8,8]{2,1,0:T(8,128)} %mask.1) | copy-start | bytes 6148
  0.7 5.0 %copy-start = (bf16[5184,192]{0,1:T(8,128)(2,1)S(1)}, bf16[5184,192]{0,1:T(8,128)(2,1)}, u32[]{:S(2)}) copy-start(bf16[5184,192]{0,1:T(8,128)(2,1)} %param.5) | copy-start | bytes 5971972
  2.0 11.9 %collective-permute-start.2 = (bf16[864,128]{1,0:T(8,128)(2,1)S(1)}, bf16[864,128]{1,0:T(8,128)(2,1)S(1)}, u32[]{:S(2)}, u32[]{:S(2)}) collective-permute-start(bf16[864,128]{1,0:T(8,128)(2,1)S(1)} %across.1), channel_id=1, source_target_pairs={{0,1},{1,0},{2,3},{3,2},{4,5},{5,4},{6,7},{7,6},{8,9},{9,8},{10,11... | collective-permute-start | bytes 663560 | tf_op jit(solution)/shard_map/ppermute | solution.py:435
  5.0 5.0 %collective-permute-start = (bf16[288,128]{1,0:T(8,128)(2,1)S(1)}, bf16[288,128]{1,0:T(8,128)(2,1)S(1)}, u32[]{:S(2)}, u32[]{:S(2)}) collective-permute-start(bf16[288,128]{1,0:T(8,128)(2,1)S(1)} %get-tuple-element.34), channel_id=1, source_target_pairs={{0,2},{2,0},{4,6},{6,4},{8,10},{10,8},{12,14},{14,12},{16,18},{18,... | collective-permute-start | bytes 221192 | tf_op jit(solution)/shard_map/ppermute | solution.py:435
  5.0 5.0 %collective-permute-start.1 = (bf16[288,128]{1,0:T(8,128)(2,1)S(1)}, bf16[288,128]{1,0:T(8,128)(2,1)S(1)}, u32[]{:S(2)}, u32[]{:S(2)}) collective-permute-start(bf16[288,128]{1,0:T(8,128)(2,1)S(1)} %get-tuple-element.35), channel_id=1, source_target_pairs={{0,0},{2,4},{4,2},{6,8},{8,6},{10,12},{12,10},{14,16},{16,14},{18,... | collective-permute-start | bytes 221192 | tf_op jit(solution)/shard_map/ppermute | solution.py:461
  6.6 11.8 %collective-permute-start.4 = (bf16[768,128]{1,0:T(8,128)(2,1)S(1)}, bf16[768,128]{1,0:T(8,128)(2,1)S(1)}, u32[]{:S(2)}, u32[]{:S(2)}) collective-permute-start(bf16[768,128]{1,0:T(8,128)(2,1)S(1)} %pack.1.brick), channel_id=1, source_target_pairs={{0,4},{1,5},{2,6},{3,7},{4,0},{5,1},{6,2},{7,3},{8,12},{9,13},{10,... | collective-permute-start | bytes 589832 | tf_op jit(solution)/shard_map/ppermute | solution.py:435
  10.2 6.5 %collective-permute-start.3 = (bf16[128,128]{1,0:T(8,128)(2,1)S(1)}, bf16[128,128]{1,0:T(8,128)(2,1)S(1)}, u32[]{:S(2)}, u32[]{:S(2)}) collective-permute-start(bf16[128,128]{1,0:T(8,128)(2,1)S(1)} %corner.1), channel_id=1, source_target_pairs={{0,1},{1,0},{2,3},{3,2},{4,5},{5,4},{6,7},{7,6},{8,9},{9,8},{10,11... | collective-permute-start | bytes 98312 | tf_op jit(solution)/shard_map/ppermute | solution.py:435
  10.3 11.5 %collective-permute-start.7 = (bf16[768,128]{1,0:T(8,128)(2,1)S(1)}, bf16[768,128]{1,0:T(8,128)(2,1)S(1)}, u32[]{:S(2)}, u32[]{:S(2)}) collective-permute-start(bf16[768,128]{1,0:T(8,128)(2,1)S(1)} %pack.1.brick), channel_id=1, source_target_pairs={{0,5},{1,4},{2,7},{3,6},{4,1},{5,0},{6,3},{7,2},{8,13},{9,12},{10,... | collective-permute-start | bytes 589832 | tf_op jit(solution)/shard_map/ppermute | solution.py:435
  18.4 5.8 %collective-permute-start.5 = (bf16[48,640]{1,0:T(8,128)(2,1)S(1)}, bf16[48,640]{1,0:T(8,128)(2,1)S(1)}, u32[]{:S(2)}, u32[]{:S(2)}) collective-permute-start(bf16[48,640]{1,0:T(8,128)(2,1)S(1)} %get-tuple-element.47), channel_id=1, source_target_pairs={{0,5},{1,4},{2,7},{3,6},{4,1},{5,0},{6,3},{7,2},{8,13},{9,12},{10,... | collective-permute-start | bytes 184328 | tf_op jit(solution)/shard_map/ppermute | solution.py:435
  18.4 6.1 %collective-permute-start.6 = (bf16[48,640]{1,0:T(8,128)(2,1)S(1)}, bf16[48,640]{1,0:T(8,128)(2,1)S(1)}, u32[]{:S(2)}, u32[]{:S(2)}) collective-permute-start(bf16[48,640]{1,0:T(8,128)(2,1)S(1)} %get-tuple-element.48), channel_id=1, source_target_pairs={{0,4},{1,5},{2,6},{3,7},{4,0},{5,1},{6,2},{7,3},{8,12},{9,13},{10,... | collective-permute-start | bytes 184328 | tf_op jit(solution)/shard_map/ppermute | solution.py:435
  20.3 5.6 %collective-permute-start.8 = (bf16[48,640]{1,0:T(8,128)(2,1)S(1)}, bf16[48,640]{1,0:T(8,128)(2,1)S(1)}, u32[]{:S(2)}, u32[]{:S(2)}) collective-permute-start(bf16[48,640]{1,0:T(8,128)(2,1)S(1)} %get-tuple-element.52), channel_id=1, source_target_pairs={{0,1},{1,0},{2,3},{3,2},{4,5},{5,4},{6,7},{7,6},{8,9},{9,8},{10,11... | collective-permute-start | bytes 184328 | tf_op jit(solution)/shard_map/ppermute | solution.py:435
  27.5 1.6 %collective-permute-start.9 = (bf16[24,5184]{1,0:T(8,128)(2,1)S(1)}, bf16[24,5184]{1,0:T(8,128)(2,1)S(1)}, u32[]{:S(2)}, u32[]{:S(2)}) collective-permute-start(bf16[24,5184]{1,0:T(8,128)(2,1)S(1)} %get-tuple-element.54), channel_id=1, source_target_pairs={{0,2},{1,3},{2,0},{3,1},{4,6},{5,7},{6,4},{7,5},{8,10},{9,11},{10,... | collective-permute-start | bytes 746504 | tf_op jit(solution)/shard_map/ppermute | solution.py:435
  29.3 7.0 %collective-permute-start.10 = (bf16[8,3968]{1,0:T(8,128)(2,1)S(1)}, bf16[8,3968]{1,0:T(8,128)(2,1)S(1)}, u32[]{:S(2)}, u32[]{:S(2)}) collective-permute-start(bf16[8,3968]{1,0:T(8,128)(2,1)S(1)} %get-tuple-element.55), channel_id=1, source_target_pairs={{0,24},{8,16},{16,8},{24,0},{1,25},{9,17},{17,9},{25,1},{2,26},{10... | collective-permute-start | bytes 190472 | tf_op jit(solution)/shard_map/ppermute | solution.py:435
  32.6 6.0 %collective-permute-start.11 = (bf16[8,3968]{1,0:T(8,128)(2,1)S(1)}, bf16[8,3968]{1,0:T(8,128)(2,1)S(1)}, u32[]{:S(2)}, u32[]{:S(2)}) collective-permute-start(bf16[8,3968]{1,0:T(8,128)(2,1)S(1)} %get-tuple-element.56), channel_id=1, source_target_pairs={{0,16},{8,24},{16,0},{24,8},{1,17},{9,25},{17,1},{25,9},{2,18},{10... | collective-permute-start | bytes 190472 | tf_op jit(solution)/shard_map/ppermute | solution.py:435
  32.6 6.0 %collective-permute-start.12 = (bf16[8,3968]{1,0:T(8,128)(2,1)S(1)}, bf16[8,3968]{1,0:T(8,128)(2,1)S(1)}, u32[]{:S(2)}, u32[]{:S(2)}) collective-permute-start(bf16[8,3968]{1,0:T(8,128)(2,1)S(1)} %get-tuple-element.57), channel_id=1, source_target_pairs={{0,8},{8,0},{16,24},{24,16},{1,9},{9,1},{17,25},{25,17},{2,10},{10... | collective-permute-start | bytes 190472 | tf_op jit(solution)/shard_map/ppermute | solution.py:435
  38.7 4.3 %collective-permute-start.13 = (bf16[8,3968]{1,0:T(8,128)(2,1)S(1)}, bf16[8,3968]{1,0:T(8,128)(2,1)S(1)}, u32[]{:S(2)}, u32[]{:S(2)}) collective-permute-start(bf16[8,3968]{1,0:T(8,128)(2,1)S(1)} %plane_sum.1.mine), channel_id=1, source_target_pairs={{0,1},{1,0},{2,3},{3,2},{4,5},{5,4},{6,7},{7,6},{8,9},{9,8},{10,11... | collective-permute-start | bytes 190472 | tf_op jit(solution)/shard_map/ppermute | solution.py:435

commit v19 on v18

--- a/solution.py
+++ b/solution.py
@@ -347,14 +347,14 @@
         yield a, jnp.concatenate([got[tap] for tap in range(9)], axis=1)
 
 
-def first_pair_kernel(other, own, across, brick, part_ref, cols, masked):
+def first_pair_kernel(own, other, brick, across, part_ref, cols, masked):
     for a, rows in pair_product((own, other), (brick, across), cols, masked):
         width = rows.shape[1]
         part_ref[:, a * width : (a + 1) * width] = rows
 
 
 def second_pair_kernel(
-    before, own, other, brick, across, keep_ref, send_ref, part, cols, masked
+    before, other, own, across, brick, keep_ref, send_ref, part, cols, masked
 ):
     for a, rows in pair_product((own, other), (brick, across), cols, masked):
         width = rows.shape[1]
@@ -521,12 +521,12 @@
     part = call(
         first_pair_kernel, "first_pair", 16, 1 << 30, 2 << 20,
         array((2 * group, total), f32), scratch,
-    )(*slices[3:1:-1], *bricks[3:1:-1])
+    )(*slices[:2], *bricks[:2])
     keep, fold = call(
         second_pair_kernel, "second_pair", 16, 1 << 30, 2 << 20,
         (array((group, total), f32), array((group, total), bf16)),
         (pltpu.VMEM((2 * group, total), f32),) + scratch,
-    )(part, *slices[:2], *bricks[:2])
+    )(part, *slices[3:1:-1], *bricks[3:1:-1])
     own, *sends = call(
         fold_kernel, "fold", 8, 8 * total * 4, 8 * total * 40,
         (array((8, lanes), f32),) + (array((8, lanes), bf16),) * (planes - 1),

time: 44 us -> 43.7 us (level)
  starting transfers between devices: 20.4 us -> 19.4 us
  waiting for transfers between devices: 9.13 us -> 9.93 us
    ppermute x13, starting transfers between devices: 19.8 us -> 18.7 us  [swap(): return lax.ppermute(piece, axes, [(i, i ^ distance) for i in range(size)])]
    ppermute x13, waiting for transfers between devices: 9.13 us -> 9.93 us  [swap(): return lax.ppermute(piece, axes, [(i, i ^ distance) for i in range(size)])]
  transfers between devices with their start and end apart: 14 -> 14, of which waited for: 5 -> 4; matrix products, arithmetic and copies ran while one was open for 0% -> 0% of each run, Pallas kernels for 22% -> 22%
where the time goes in v19:
time: 43.7 us; the launch traced here: 43.6 us
  starting transfers between devices  19.4 us (44%)
  Pallas kernels  12.7 us (29%)
  waiting for transfers between devices  9.93 us (23%)
  local copies, waits for them, and re-layouts  0.84 us (2%)
  between operations  0.77 us (2%)
    ppermute x13, starting transfers between devices, swap(): return lax.ppermute(piece, axes, [(i, i ^ distance) for i in range(size)])  18.7 us
    pallas_call x14, Pallas kernels, run(): pl.pallas_call(body, out_shape=out_shape, in_specs=in_specs or [spec] * l...  12.7 us
    ppermute x13, waiting for transfers between devices, swap(): return lax.ppermute(piece, axes, [(i, i ^ distance) for i in range(size)])  9.93 us
  transfers between devices with their start and end apart: 14, of which 4 were waited for; matrix products, arithmetic and copies ran while one was open for 0% of the time, Pallas kernels for 22%

profile of v19, /device:TPU:0, one launch (start us, length us, event | category | flops | bytes accessed | tf_op | source)
XLA Modules:
  0.0 43.6 jit_solution(13585011822678028920)
XLA Ops:
  0.6 0.0 copy-start.1
  0.6 0.0 copy-start.2
  0.7 0.0 copy-start.3
  0.7 0.0 copy-start
  0.7 0.2 pick.1.first
  0.8 0.7 %copy-done.1 = bf16[8,8,8,192]{3,2,1,0:T(8,128)(2,1)S(1)} copy-done((bf16[8,8,8,192]{3,2,1,0:T(8,128)(2,1)S(1)}, bf16[8,8,8,192]{3,2,1,0:T(8,128)(2,1)}, u32[]{:S(2)}) %copy-start.1) | copy-done | bytes 196632
  1.6 0.1 copy-done.2
  1.7 0.0 copy-done.3
  1.7 0.2 prepare.1
  1.9 0.1 across.1
  2.0 3.0 %collective-permute-start.2 = (bf16[864,128]{1,0:T(8,128)(2,1)S(1)}, bf16[864,128]{1,0:T(8,128)(2,1)S(1)}, u32[]{:S(2)}, u32[]{:S(2)}) collective-permute-start(bf16[864,128]{1,0:T(8,128)(2,1)S(1)} %across.1), channel_id=1, source_target_pairs={{0,1},{1,0},{2,3},{3,2},{4,5},{5,4},{6,7},{7,6},{8,9},{9,8},{10,11... | collective-permute-start | bytes 663560 | tf_op jit(solution)/shard_map/ppermute | solution.py:435
  5.0 0.0 collective-permute-start
  5.0 0.7 %collective-permute-start.1 = (bf16[288,128]{1,0:T(8,128)(2,1)S(1)}, bf16[288,128]{1,0:T(8,128)(2,1)S(1)}, u32[]{:S(2)}, u32[]{:S(2)}) collective-permute-start(bf16[288,128]{1,0:T(8,128)(2,1)S(1)} %get-tuple-element.35), channel_id=1, source_target_pairs={{0,0},{2,4},{4,2},{6,8},{8,6},{10,12},{12,10},{14,16},{16,14},{18,... | collective-permute-start | bytes 221192 | tf_op jit(solution)/shard_map/ppermute | solution.py:461
  5.7 0.0 copy-done
  5.7 0.8 %turn.1.after.weight = bf16[5184,192]{1,0:T(8,128)(2,1)S(1)} custom-call(bf16[192,5184]{1,0:T(8,128)(2,1)S(1)} %bitcast.5), custom_call_target="tpu_custom_call" | custom-call | flops 1048576 | bytes 4194304 | tf_op jit(solution)/shard_map/turn/pallas_call | solution.py:406
  6.5 0.1 pack.1.brick
  6.6 3.4 %collective-permute-start.4 = (bf16[768,128]{1,0:T(8,128)(2,1)S(1)}, bf16[768,128]{1,0:T(8,128)(2,1)S(1)}, u32[]{:S(2)}, u32[]{:S(2)}) collective-permute-start(bf16[768,128]{1,0:T(8,128)(2,1)S(1)} %pack.1.brick), channel_id=1, source_target_pairs={{0,4},{1,5},{2,6},{3,7},{4,0},{5,1},{6,2},{7,3},{8,12},{9,13},{10,... | collective-permute-start | bytes 589832 | tf_op jit(solution)/shard_map/ppermute | solution.py:435
  10.0 0.0 collective-permute-done.near
  10.0 0.0 collective-permute-done.1.far
  10.0 0.2 corner.1
  10.2 0.1 collective-permute-start.3
  10.3 3.5 %collective-permute-start.8 = (bf16[768,128]{1,0:T(8,128)(2,1)S(1)}, bf16[768,128]{1,0:T(8,128)(2,1)S(1)}, u32[]{:S(2)}, u32[]{:S(2)}) collective-permute-start(bf16[768,128]{1,0:T(8,128)(2,1)S(1)} %pack.1.brick), channel_id=1, source_target_pairs={{0,5},{1,4},{2,7},{3,6},{4,1},{5,0},{6,3},{7,2},{8,13},{9,12},{10,... | collective-permute-start | bytes 589832 | tf_op jit(solution)/shard_map/ppermute | solution.py:435
  13.9 0.0 collective-permute-done.2.across
  13.9 2.8 %bulk.1 = f32[10,80,192]{2,1,0:T(8,128)S(1)} custom-call(bf16[8,64,192]{2,1,0:T(8,128)(2,1)S(1)} %get-tuple-element.33.masked, bf16[288,128]{1,0:T(8,128)(2,1)S(1)} %collective-permute-done.near, bf16[288,128]{1,0:T(8,128)(2,1)S(1)} %collective-permute-done.1.far, bf16[864,128]{1,0:T(8,128)(2,1)S(1)} %collective-permute-done.2.across, ...), custom_call_target="tpu_custom_call" | custom-call | flops 1610612736 | bytes 1048576 | tf_op jit(solution)/shard_map/bulk/pallas_call | solution.py:406
  16.7 0.0 collective-permute-done.3.corner
  16.7 1.7 %forward.1 = (bf16[8,64,192]{2,1,0:T(8,128)(2,1)}, bf16[10,80,192]{2,1,0:T(8,128)(2,1)S(1)}, bf16[48,640]{1,0:T(8,128)(2,1)S(1)}, bf16[48,640]{1,0:T(8,128)(2,1)...) custom-call(f32[10,80,192]{2,1,0:T(8,128)S(1)} %bulk.1, bf16[8,64,192]{2,1,0:T(8,128)(2,1)S(1)} %get-tuple-element.38.cot, ...), custom_call_target="tpu_custom_call" | custom-call | flops 1610612736 | bytes 1048576 | tf_op jit(solution)/shard_map/forward/pallas_call | solution.py:406
  18.4 0.0 collective-permute-done.4.brick
  18.4 0.5 %collective-permute-start.5 = (bf16[48,640]{1,0:T(8,128)(2,1)S(1)}, bf16[48,640]{1,0:T(8,128)(2,1)S(1)}, u32[]{:S(2)}, u32[]{:S(2)}) collective-permute-start(bf16[48,640]{1,0:T(8,128)(2,1)S(1)} %get-tuple-element.48), channel_id=1, source_target_pairs={{0,1},{1,0},{2,3},{3,2},{4,5},{5,4},{6,7},{7,6},{8,9},{9,8},{10,11... | collective-permute-start | bytes 184328 | tf_op jit(solution)/shard_map/ppermute | solution.py:435
  18.9 0.8 %collective-permute-start.6 = (bf16[48,640]{1,0:T(8,128)(2,1)S(1)}, bf16[48,640]{1,0:T(8,128)(2,1)S(1)}, u32[]{:S(2)}, u32[]{:S(2)}) collective-permute-start(bf16[48,640]{1,0:T(8,128)(2,1)S(1)} %get-tuple-element.49), channel_id=1, source_target_pairs={{0,5},{1,4},{2,7},{3,6},{4,1},{5,0},{6,3},{7,2},{8,13},{9,12},{10,... | collective-permute-start | bytes 184328 | tf_op jit(solution)/shard_map/ppermute | solution.py:435
  19.7 2.1 %collective-permute-start.7 = (bf16[48,640]{1,0:T(8,128)(2,1)S(1)}, bf16[48,640]{1,0:T(8,128)(2,1)S(1)}, u32[]{:S(2)}, u32[]{:S(2)}) collective-permute-start(bf16[48,640]{1,0:T(8,128)(2,1)S(1)} %get-tuple-element.50), channel_id=1, source_target_pairs={{0,4},{1,5},{2,6},{3,7},{4,0},{5,1},{6,2},{7,3},{8,12},{9,13},{10,... | collective-permute-start | bytes 184328 | tf_op jit(solution)/shard_map/ppermute | solution.py:435
  21.8 2.4 %collective-permute-done.5.other = bf16[48,640]{1,0:T(8,128)(2,1)S(1)} collective-permute-done((bf16[48,640]{1,0:T(8,128)(2,1)S(1)}, bf16[48,640]{1,0:T(8,128)(2,1)S(1)}, u32[]{:S(2)}, u32[]{:S(2)}) %collective-permute-start.5) | collective-permute-done | bytes 61472 | tf_op jit(solution)/shard_map/ppermute | solution.py:435
  24.2 1.5 %first_pair.1.before = f32[48,5184]{1,0:T(8,128)S(1)} custom-call(bf16[48,640]{1,0:T(8,128)(2,1)S(1)} %get-tuple-element.47.own, bf16[48,640]{1,0:T(8,128)(2,1)S(1)} %collective-permute-done.5.other, bf16[768,128]{1,0:T(8,128)(2,1)S(1)} %pack.1.brick, bf16[864,128]{1,0:T(8,128)(2,1)S(1)} %collective-permute-done.2.across), custom_call_target="tpu_custom_call" | custom-call | flops 1073741824 | bytes 2097152 | tf_op jit(solution)/shard_map/first_pair/pallas_call | solution.py:406
  25.7 0.0 collective-permute-done.8.across
  25.7 0.0 collective-permute-done.6.other
  25.7 0.0 collective-permute-done.7.own
  25.7 1.6 %second_pair.1 = (f32[24,5184]{1,0:T(8,128)S(1)}, bf16[24,5184]{1,0:T(8,128)(2,1)S(1)}) custom-call(f32[48,5184]{1,0:T(8,128)S(1)} %first_pair.1.before, bf16[48,640]{1,0:T(8,128)(2,1)S(1)} %collective-permute-done.6.other, bf16[48,640]{1,0:T(8,128)(2,1)S(1)} %collective-permute-done.7.own, bf16[768,128]{1,0:T(8,128)(2,1)S(1)} %collective-permute-done.8.across, ...), custom_call_target="tpu_custom_call" | custom-call | flops 1073741824 | bytes 2097152 | tf_op jit(solution)/shard_map/second_pair/pallas_call | solution.py:406
  27.3 0.1 collective-permute-start.9
  27.4 1.5 %collective-permute-done.9.other = bf16[24,5184]{1,0:T(8,128)(2,1)S(1)} collective-permute-done((bf16[24,5184]{1,0:T(8,128)(2,1)S(1)}, bf16[24,5184]{1,0:T(8,128)(2,1)S(1)}, u32[]{:S(2)}, u32[]{:S(2)}) %collective-permute-start.9) | collective-permute-done | bytes 248864 | tf_op jit(solution)/shard_map/ppermute | solution.py:435
  28.9 0.2 fold.1
  29.1 3.5 %collective-permute-start.10 = (bf16[8,3968]{1,0:T(8,128)(2,1)S(1)}, bf16[8,3968]{1,0:T(8,128)(2,1)S(1)}, u32[]{:S(2)}, u32[]{:S(2)}) collective-permute-start(bf16[8,3968]{1,0:T(8,128)(2,1)S(1)} %get-tuple-element.55), channel_id=1, source_target_pairs={{0,24},{8,16},{16,8},{24,0},{1,25},{9,17},{17,9},{25,1},{2,26},{10... | collective-permute-start | bytes 190472 | tf_op jit(solution)/shard_map/ppermute | solution.py:435
  32.6 0.0 collective-permute-start.11
  32.6 0.9 %collective-permute-start.12 = (bf16[8,3968]{1,0:T(8,128)(2,1)S(1)}, bf16[8,3968]{1,0:T(8,128)(2,1)S(1)}, u32[]{:S(2)}, u32[]{:S(2)}) collective-permute-start(bf16[8,3968]{1,0:T(8,128)(2,1)S(1)} %get-tuple-element.57), channel_id=1, source_target_pairs={{0,8},{8,0},{16,24},{24,16},{1,9},{9,1},{17,25},{25,17},{2,10},{10... | collective-permute-start | bytes 190472 | tf_op jit(solution)/shard_map/ppermute | solution.py:435
  33.5 2.6 %input_gradient.1 = bf16[8,64,192]{2,1,0:T(8,128)(2,1)} custom-call(bf16[10,80,192]{2,1,0:T(8,128)(2,1)S(1)} %get-tuple-element.42.gp, f32[8,64,128]{2,1,0:T(8,128)S(1)} %get-tuple-element.40.live, bf16[192,5184]{1,0:T(8,128)(2,1)S(1)} %bitcast.6), custom_call_target="tpu_custom_call" | custom-call | flops 1358954496 | bytes 4194304 | tf_op jit(solution)/shard_map/input_gradient/pallas_call | solution.py:406
  36.1 0.0 collective-permute-done.10.one
  36.1 2.3 %collective-permute-done.11.two = bf16[8,3968]{1,0:T(8,128)(2,1)S(1)} collective-permute-done((bf16[8,3968]{1,0:T(8,128)(2,1)S(1)}, bf16[8,3968]{1,0:T(8,128)(2,1)S(1)}, u32[]{:S(2)}, u32[]{:S(2)}) %collective-permute-start.11) | collective-permute-done | bytes 63520 | tf_op jit(solution)/shard_map/ppermute | solution.py:435
  38.4 0.0 collective-permute-done.12.three
  38.5 0.6 %collective-permute-start.13 = (bf16[8,3968]{1,0:T(8,128)(2,1)S(1)}, bf16[8,3968]{1,0:T(8,128)(2,1)S(1)}, u32[]{:S(2)}, u32[]{:S(2)}) collective-permute-start(bf16[8,3968]{1,0:T(8,128)(2,1)S(1)} %plane_sum.1.mine), channel_id=1, source_target_pairs={{0,1},{1,0},{2,3},{3,2},{4,5},{5,4},{6,7},{7,6},{8,9},{9,8},{10,11... | collective-permute-start | bytes 190472 | tf_op jit(solution)/shard_map/ppermute | solution.py:435
  39.1 3.7 %collective-permute-done.13.other = bf16[8,3968]{1,0:T(8,128)(2,1)S(1)} collective-permute-done((bf16[8,3968]{1,0:T(8,128)(2,1)S(1)}, bf16[8,3968]{1,0:T(8,128)(2,1)S(1)}, u32[]{:S(2)}, u32[]{:S(2)}) %collective-permute-start.13) | collective-permute-done | bytes 63520 | tf_op jit(solution)/shard_map/ppermute | solution.py:435
  42.8 0.8 %join.1 = f32[12,5184]{1,0:T(8,128)} custom-call(bf16[8,3968]{1,0:T(8,128)(2,1)S(1)} %plane_sum.1.mine, bf16[8,3968]{1,0:T(8,128)(2,1)S(1)} %collective-permute-done.13.other), custom_call_target="tpu_custom_call" | custom-call | flops 41472 | bytes 580608 | tf_op jit(solution)/shard_map/join/pallas_call | solution.py:406
  (1 shorter events, 0.0 us)
Async XLA Ops:
  0.6 1.0 %copy-start.1 = (bf16[8,8,8,192]{3,2,1,0:T(8,128)(2,1)S(1)}, bf16[8,8,8,192]{3,2,1,0:T(8,128)(2,1)}, u32[]{:S(2)}) copy-start(bf16[8,8,8,192]{3,2,1,0:T(8,128)(2,1)} %param.4) | copy-start | bytes 589828
  0.6 1.0 %copy-start.2 = (bf16[8,8,8,192]{3,2,1,0:T(8,128)(2,1)S(1)}, bf16[8,8,8,192]{3,2,1,0:T(8,128)(2,1)}, u32[]{:S(2)}) copy-start(bf16[8,8,8,192]{3,2,1,0:T(8,128)(2,1)} %param.7) | copy-start | bytes 589828
  0.7 1.0 %copy-start.3 = (s32[8,8,8]{2,1,0:T(8,128)S(1)}, s32[8,8,8]{2,1,0:T(8,128)}, u32[]{:S(2)}) copy-start(s32[8,8,8]{2,1,0:T(8,128)} %mask.1) | copy-start | bytes 6148
  0.7 5.0 %copy-start = (bf16[5184,192]{0,1:T(8,128)(2,1)S(1)}, bf16[5184,192]{0,1:T(8,128)(2,1)}, u32[]{:S(2)}) copy-start(bf16[5184,192]{0,1:T(8,128)(2,1)} %param.5) | copy-start | bytes 5971972
  2.0 11.9 %collective-permute-start.2 = (bf16[864,128]{1,0:T(8,128)(2,1)S(1)}, bf16[864,128]{1,0:T(8,128)(2,1)S(1)}, u32[]{:S(2)}, u32[]{:S(2)}) collective-permute-start(bf16[864,128]{1,0:T(8,128)(2,1)S(1)} %across.1), channel_id=1, source_target_pairs={{0,1},{1,0},{2,3},{3,2},{4,5},{5,4},{6,7},{7,6},{8,9},{9,8},{10,11... | collective-permute-start | bytes 663560 | tf_op jit(solution)/shard_map/ppermute | solution.py:435
  5.0 5.0 %collective-permute-start = (bf16[288,128]{1,0:T(8,128)(2,1)S(1)}, bf16[288,128]{1,0:T(8,128)(2,1)S(1)}, u32[]{:S(2)}, u32[]{:S(2)}) collective-permute-start(bf16[288,128]{1,0:T(8,128)(2,1)S(1)} %get-tuple-element.34), channel_id=1, source_target_pairs={{0,2},{2,0},{4,6},{6,4},{8,10},{10,8},{12,14},{14,12},{16,18},{18,... | collective-permute-start | bytes 221192 | tf_op jit(solution)/shard_map/ppermute | solution.py:435
  5.0 5.0 %collective-permute-start.1 = (bf16[288,128]{1,0:T(8,128)(2,1)S(1)}, bf16[288,128]{1,0:T(8,128)(2,1)S(1)}, u32[]{:S(2)}, u32[]{:S(2)}) collective-permute-start(bf16[288,128]{1,0:T(8,128)(2,1)S(1)} %get-tuple-element.35), channel_id=1, source_target_pairs={{0,0},{2,4},{4,2},{6,8},{8,6},{10,12},{12,10},{14,16},{16,14},{18,... | collective-permute-start | bytes 221192 | tf_op jit(solution)/shard_map/ppermute | solution.py:461
  6.6 11.8 %collective-permute-start.4 = (bf16[768,128]{1,0:T(8,128)(2,1)S(1)}, bf16[768,128]{1,0:T(8,128)(2,1)S(1)}, u32[]{:S(2)}, u32[]{:S(2)}) collective-permute-start(bf16[768,128]{1,0:T(8,128)(2,1)S(1)} %pack.1.brick), channel_id=1, source_target_pairs={{0,4},{1,5},{2,6},{3,7},{4,0},{5,1},{6,2},{7,3},{8,12},{9,13},{10,... | collective-permute-start | bytes 589832 | tf_op jit(solution)/shard_map/ppermute | solution.py:435
  10.2 6.5 %collective-permute-start.3 = (bf16[128,128]{1,0:T(8,128)(2,1)S(1)}, bf16[128,128]{1,0:T(8,128)(2,1)S(1)}, u32[]{:S(2)}, u32[]{:S(2)}) collective-permute-start(bf16[128,128]{1,0:T(8,128)(2,1)S(1)} %corner.1), channel_id=1, source_target_pairs={{0,1},{1,0},{2,3},{3,2},{4,5},{5,4},{6,7},{7,6},{8,9},{9,8},{10,11... | collective-permute-start | bytes 98312 | tf_op jit(solution)/shard_map/ppermute | solution.py:435
  10.3 15.4 %collective-permute-start.8 = (bf16[768,128]{1,0:T(8,128)(2,1)S(1)}, bf16[768,128]{1,0:T(8,128)(2,1)S(1)}, u32[]{:S(2)}, u32[]{:S(2)}) collective-permute-start(bf16[768,128]{1,0:T(8,128)(2,1)S(1)} %pack.1.brick), channel_id=1, source_target_pairs={{0,5},{1,4},{2,7},{3,6},{4,1},{5,0},{6,3},{7,2},{8,13},{9,12},{10,... | collective-permute-start | bytes 589832 | tf_op jit(solution)/shard_map/ppermute | solution.py:435
  18.4 5.8 %collective-permute-start.5 = (bf16[48,640]{1,0:T(8,128)(2,1)S(1)}, bf16[48,640]{1,0:T(8,128)(2,1)S(1)}, u32[]{:S(2)}, u32[]{:S(2)}) collective-permute-start(bf16[48,640]{1,0:T(8,128)(2,1)S(1)} %get-tuple-element.48), channel_id=1, source_target_pairs={{0,1},{1,0},{2,3},{3,2},{4,5},{5,4},{6,7},{7,6},{8,9},{9,8},{10,11... | collective-permute-start | bytes 184328 | tf_op jit(solution)/shard_map/ppermute | solution.py:435
  18.9 6.8 %collective-permute-start.6 = (bf16[48,640]{1,0:T(8,128)(2,1)S(1)}, bf16[48,640]{1,0:T(8,128)(2,1)S(1)}, u32[]{:S(2)}, u32[]{:S(2)}) collective-permute-start(bf16[48,640]{1,0:T(8,128)(2,1)S(1)} %get-tuple-element.49), channel_id=1, source_target_pairs={{0,5},{1,4},{2,7},{3,6},{4,1},{5,0},{6,3},{7,2},{8,13},{9,12},{10,... | collective-permute-start | bytes 184328 | tf_op jit(solution)/shard_map/ppermute | solution.py:435
  19.7 6.0 %collective-permute-start.7 = (bf16[48,640]{1,0:T(8,128)(2,1)S(1)}, bf16[48,640]{1,0:T(8,128)(2,1)S(1)}, u32[]{:S(2)}, u32[]{:S(2)}) collective-permute-start(bf16[48,640]{1,0:T(8,128)(2,1)S(1)} %get-tuple-element.50), channel_id=1, source_target_pairs={{0,4},{1,5},{2,6},{3,7},{4,0},{5,1},{6,2},{7,3},{8,12},{9,13},{10,... | collective-permute-start | bytes 184328 | tf_op jit(solution)/shard_map/ppermute | solution.py:435
  27.3 1.6 %collective-permute-start.9 = (bf16[24,5184]{1,0:T(8,128)(2,1)S(1)}, bf16[24,5184]{1,0:T(8,128)(2,1)S(1)}, u32[]{:S(2)}, u32[]{:S(2)}) collective-permute-start(bf16[24,5184]{1,0:T(8,128)(2,1)S(1)} %get-tuple-element.54), channel_id=1, source_target_pairs={{0,2},{1,3},{2,0},{3,1},{4,6},{5,7},{6,4},{7,5},{8,10},{9,11},{10,... | collective-permute-start | bytes 746504 | tf_op jit(solution)/shard_map/ppermute | solution.py:435
  29.1 7.0 %collective-permute-start.10 = (bf16[8,3968]{1,0:T(8,128)(2,1)S(1)}, bf16[8,3968]{1,0:T(8,128)(2,1)S(1)}, u32[]{:S(2)}, u32[]{:S(2)}) collective-permute-start(bf16[8,3968]{1,0:T(8,128)(2,1)S(1)} %get-tuple-element.55), channel_id=1, source_target_pairs={{0,24},{8,16},{16,8},{24,0},{1,25},{9,17},{17,9},{25,1},{2,26},{10... | collective-permute-start | bytes 190472 | tf_op jit(solution)/shard_map/ppermute | solution.py:435
  32.6 5.8 %collective-permute-start.11 = (bf16[8,3968]{1,0:T(8,128)(2,1)S(1)}, bf16[8,3968]{1,0:T(8,128)(2,1)S(1)}, u32[]{:S(2)}, u32[]{:S(2)}) collective-permute-start(bf16[8,3968]{1,0:T(8,128)(2,1)S(1)} %get-tuple-element.56), channel_id=1, source_target_pairs={{0,16},{8,24},{16,0},{24,8},{1,17},{9,25},{17,1},{25,9},{2,18},{10... | collective-permute-start | bytes 190472 | tf_op jit(solution)/shard_map/ppermute | solution.py:435
  32.6 5.8 %collective-permute-start.12 = (bf16[8,3968]{1,0:T(8,128)(2,1)S(1)}, bf16[8,3968]{1,0:T(8,128)(2,1)S(1)}, u32[]{:S(2)}, u32[]{:S(2)}) collective-permute-start(bf16[8,3968]{1,0:T(8,128)(2,1)S(1)} %get-tuple-element.57), channel_id=1, source_target_pairs={{0,8},{8,0},{16,24},{24,16},{1,9},{9,1},{17,25},{25,17},{2,10},{10... | collective-permute-start | bytes 190472 | tf_op jit(solution)/shard_map/ppermute | solution.py:435
  38.5 4.3 %collective-permute-start.13 = (bf16[8,3968]{1,0:T(8,128)(2,1)S(1)}, bf16[8,3968]{1,0:T(8,128)(2,1)S(1)}, u32[]{:S(2)}, u32[]{:S(2)}) collective-permute-start(bf16[8,3968]{1,0:T(8,128)(2,1)S(1)} %plane_sum.1.mine), channel_id=1, source_target_pairs={{0,1},{1,0},{2,3},{3,2},{4,5},{5,4},{6,7},{7,6},{8,9},{9,8},{10,11... | collective-permute-start | bytes 190472 | tf_op jit(solution)/shard_map/ppermute | solution.py:435

commit v20 on v19

--- a/solution.py
+++ b/solution.py
@@ -278,7 +278,8 @@
         ref[...] = jnp.concatenate(both, axis=0).astype(jnp.bfloat16)
 
 
-def input_kernel(gp, live, turned, out_ref, cols, weight):
+def input_kernel(gp, live, turned, act, out_ref, act_ref, cols, weight):
+    act_ref[...] = act[...]
     width, rows, channels = out_ref.shape
     f32 = jnp.float32
     tall = rows + 2 * DEPTH
@@ -304,10 +305,8 @@
     out_ref[...] = (total.reshape(width, rows, channels) * live[:, :, 0:1]).astype(jnp.bfloat16)
 
 
-def pair_product(received, bricks, cols, masked):
-    f32 = jnp.float32
-    group, lanes = received[0].shape
-    per, lane, channels = masked.shape
+def unpack_pair(bricks, masked):
+    per, lane, _ = masked.shape
     half = lane // 2
     side = position()[3]
     for i, brick in enumerate(bricks):
@@ -317,6 +316,14 @@
             rest = brick[pl.ds((per + x % (per // 2)) * half, half)]
             masked[x, at_rows, :128] = brick[pl.ds(x * half, half)]
             masked[x, at_rows, 128:] = rest[:, shift : shift + 64]
+
+
+def pair_product(received, masked, cols):
+    f32 = jnp.float32
+    group, lanes = received[0].shape
+    per, lane, channels = masked.shape
+    half = lane // 2
+    side = position()[3]
     at = lax.broadcasted_iota(jnp.int32, (group, lane), 1)
     y, z = at // DEPTH, at % DEPTH
     tall = lane // DEPTH
@@ -347,16 +354,16 @@
         yield a, jnp.concatenate([got[tap] for tap in range(9)], axis=1)
 
 
-def first_pair_kernel(own, other, brick, across, part_ref, cols, masked):
-    for a, rows in pair_product((own, other), (brick, across), cols, masked):
+def first_pair_kernel(own, other, brick, across, beside, beyond, part_ref, next_ref, cols, masked):
+    unpack_pair((beside, beyond), next_ref)
+    unpack_pair((brick, across), masked)
+    for a, rows in pair_product((own, other), masked, cols):
         width = rows.shape[1]
         part_ref[:, a * width : (a + 1) * width] = rows
 
 
-def second_pair_kernel(
-    before, other, own, across, brick, keep_ref, send_ref, part, cols, masked
-):
-    for a, rows in pair_product((own, other), (brick, across), cols, masked):
+def second_pair_kernel(before, other, own, masked, keep_ref, send_ref, part, cols):
+    for a, rows in pair_product((own, other), masked, cols):
         width = rows.shape[1]
         at = slice(a * width, (a + 1) * width)
         part[:, at] = before[:, at] + rows
@@ -505,28 +512,27 @@
     for place in (3, 2, 1):
         slices[place] = in_plane(slices[place], CHIPS[place])
 
-    grad_input = call(
-        input_kernel, "input_gradient", 20, 2 * 512 * 5184 * 256, 4 << 20, brick,
+    grad_input, act = call(
+        input_kernel, "input_gradient", 20, 2 * 512 * 5184 * 256, 4 << 20, (brick, brick),
         (
             pltpu.VMEM((width + 2, rows, 9 * channels), bf16),
             pltpu.VMEM((total, channels), bf16),
         ),
-    )(gp, live, weight.T)
+    )(gp, live, weight.T, act)
 
     lanes = dense(total)[0]
-    scratch = (
-        pltpu.VMEM((9 * 2 * group, (width + 2) * SIDES * rows), bf16),
-        pltpu.VMEM((width, SIDES * rows, channels), bf16),
-    )
-    part = call(
+    cols = pltpu.VMEM((9 * 2 * group, (width + 2) * SIDES * rows), bf16)
+    pair = (width, SIDES * rows, channels)
+    part, pair_masked = call(
         first_pair_kernel, "first_pair", 16, 1 << 30, 2 << 20,
-        array((2 * group, total), f32), scratch,
-    )(*slices[:2], *bricks[:2])
+        (array((2 * group, total), f32), array(pair, bf16)),
+        (cols, pltpu.VMEM(pair, bf16)),
+    )(*slices[:2], *bricks)
     keep, fold = call(
         second_pair_kernel, "second_pair", 16, 1 << 30, 2 << 20,
         (array((group, total), f32), array((group, total), bf16)),
-        (pltpu.VMEM((2 * group, total), f32),) + scratch,
-    )(part, *slices[3:1:-1], *bricks[3:1:-1])
+        (pltpu.VMEM((2 * group, total), f32), cols),
+    )(part, *slices[3:1:-1], pair_masked)
     own, *sends = call(
         fold_kernel, "fold", 8, 8 * total * 4, 8 * total * 40,
         (array((8, lanes), f32),) + (array((8, lanes), bf16),) * (planes - 1),

time: 43.7 us -> 43.3 us (level)
  Pallas kernels: 12.7 us -> 12.2 us
    pallas_call x14, Pallas kernels: 12.7 us -> 12.2 us  [run(): pl.pallas_call(body, out_shape=out_shape, in_specs=in_specs or [spec] * l...]
  transfers between devices with their start and end apart: 14 -> 14, of which waited for: 4 -> 4; matrix products, arithmetic and copies ran while one was open for 0% -> 0% of each run, Pallas kernels for 22% -> 21%
where the time goes in v20:
time: 43.3 us; the launch traced here: 43.2 us
  starting transfers between devices  19.4 us (45%)
  Pallas kernels  12.2 us (28%)
  waiting for transfers between devices  9.98 us (23%)
  local copies, waits for them, and re-layouts  0.84 us (2%)
  between operations  0.78 us (2%)
    ppermute x13, starting transfers between devices, swap(): return lax.ppermute(piece, axes, [(i, i ^ distance) for i in range(size)])  18.7 us
    pallas_call x14, Pallas kernels, run(): pl.pallas_call(body, out_shape=out_shape, in_specs=in_specs or [spec] * l...  12.2 us
    ppermute x13, waiting for transfers between devices, swap(): return lax.ppermute(piece, axes, [(i, i ^ distance) for i in range(size)])  9.98 us
  transfers between devices with their start and end apart: 14, of which 4 were waited for; matrix products, arithmetic and copies ran while one was open for 0% of the time, Pallas kernels for 21%

profile of v20, /device:TPU:0, one launch (start us, length us, event | category | flops | bytes accessed | tf_op | source)
XLA Modules:
  0.0 43.2 jit_solution(11911908170977635339)
XLA Ops:
  0.6 0.0 copy-start.1
  0.6 0.0 copy-start.2
  0.7 0.0 copy-start.3
  0.7 0.0 copy-start
  0.7 0.2 pick.1.first
  0.8 0.7 %copy-done.1 = bf16[8,8,8,192]{3,2,1,0:T(8,128)(2,1)S(1)} copy-done((bf16[8,8,8,192]{3,2,1,0:T(8,128)(2,1)S(1)}, bf16[8,8,8,192]{3,2,1,0:T(8,128)(2,1)}, u32[]{:S(2)}) %copy-start.1) | copy-done | bytes 196632
  1.6 0.1 copy-done.2
  1.7 0.0 copy-done.3
  1.7 0.2 prepare.1
  1.9 0.1 across.1
  2.0 3.0 %collective-permute-start.2 = (bf16[864,128]{1,0:T(8,128)(2,1)S(1)}, bf16[864,128]{1,0:T(8,128)(2,1)S(1)}, u32[]{:S(2)}, u32[]{:S(2)}) collective-permute-start(bf16[864,128]{1,0:T(8,128)(2,1)S(1)} %across.1), channel_id=1, source_target_pairs={{0,1},{1,0},{2,3},{3,2},{4,5},{5,4},{6,7},{7,6},{8,9},{9,8},{10,11... | collective-permute-start | bytes 663560 | tf_op jit(solution)/shard_map/ppermute | solution.py:442
  5.0 0.0 collective-permute-start
  5.0 0.7 %collective-permute-start.1 = (bf16[288,128]{1,0:T(8,128)(2,1)S(1)}, bf16[288,128]{1,0:T(8,128)(2,1)S(1)}, u32[]{:S(2)}, u32[]{:S(2)}) collective-permute-start(bf16[288,128]{1,0:T(8,128)(2,1)S(1)} %get-tuple-element.39), channel_id=1, source_target_pairs={{0,0},{2,4},{4,2},{6,8},{8,6},{10,12},{12,10},{14,16},{16,14},{18,... | collective-permute-start | bytes 221192 | tf_op jit(solution)/shard_map/ppermute | solution.py:468
  5.7 0.0 copy-done
  5.7 0.8 %turn.1.after.weight = bf16[5184,192]{1,0:T(8,128)(2,1)S(1)} custom-call(bf16[192,5184]{1,0:T(8,128)(2,1)S(1)} %bitcast.5), custom_call_target="tpu_custom_call" | custom-call | flops 1048576 | bytes 4194304 | tf_op jit(solution)/shard_map/turn/pallas_call | solution.py:413
  6.5 0.1 pack.1.brick
  6.6 3.4 %collective-permute-start.4 = (bf16[768,128]{1,0:T(8,128)(2,1)S(1)}, bf16[768,128]{1,0:T(8,128)(2,1)S(1)}, u32[]{:S(2)}, u32[]{:S(2)}) collective-permute-start(bf16[768,128]{1,0:T(8,128)(2,1)S(1)} %pack.1.brick), channel_id=1, source_target_pairs={{0,4},{1,5},{2,6},{3,7},{4,0},{5,1},{6,2},{7,3},{8,12},{9,13},{10,... | collective-permute-start | bytes 589832 | tf_op jit(solution)/shard_map/ppermute | solution.py:442
  10.0 0.0 collective-permute-done.near
  10.0 0.0 collective-permute-done.1.far
  10.0 0.2 corner.1
  10.2 0.1 collective-permute-start.3
  10.3 3.5 %collective-permute-start.6 = (bf16[768,128]{1,0:T(8,128)(2,1)S(1)}, bf16[768,128]{1,0:T(8,128)(2,1)S(1)}, u32[]{:S(2)}, u32[]{:S(2)}) collective-permute-start(bf16[768,128]{1,0:T(8,128)(2,1)S(1)} %pack.1.brick), channel_id=1, source_target_pairs={{0,5},{1,4},{2,7},{3,6},{4,1},{5,0},{6,3},{7,2},{8,13},{9,12},{10,... | collective-permute-start | bytes 589832 | tf_op jit(solution)/shard_map/ppermute | solution.py:442
  13.9 0.0 collective-permute-done.2.across
  13.9 2.8 %bulk.1 = f32[10,80,192]{2,1,0:T(8,128)S(1)} custom-call(bf16[8,64,192]{2,1,0:T(8,128)(2,1)S(1)} %get-tuple-element.37.masked, bf16[288,128]{1,0:T(8,128)(2,1)S(1)} %collective-permute-done.near, bf16[288,128]{1,0:T(8,128)(2,1)S(1)} %collective-permute-done.1.far, bf16[864,128]{1,0:T(8,128)(2,1)S(1)} %collective-permute-done.2.across, ...), custom_call_target="tpu_custom_call" | custom-call | flops 1610612736 | bytes 1048576 | tf_op jit(solution)/shard_map/bulk/pallas_call | solution.py:413
  16.7 0.0 collective-permute-done.3.corner
  16.7 1.1 %forward.1 = (bf16[8,64,192]{2,1,0:T(8,128)(2,1)S(1)}, bf16[10,80,192]{2,1,0:T(8,128)(2,1)S(1)}, bf16[48,640]{1,0:T(8,128)(2,1)S(1)}, bf16[48,640]{1,0:T(8,128)(...) custom-call(f32[10,80,192]{2,1,0:T(8,128)S(1)} %bulk.1, ...), custom_call_target="tpu_custom_call" | custom-call | flops 1610612736 | bytes 1048576 | tf_op jit(solution)/shard_map/forward/pallas_call | solution.py:413
  17.8 0.0 collective-permute-done.4.beside
  17.8 0.6 %collective-permute-start.5 = (bf16[48,640]{1,0:T(8,128)(2,1)S(1)}, bf16[48,640]{1,0:T(8,128)(2,1)S(1)}, u32[]{:S(2)}, u32[]{:S(2)}) collective-permute-start(bf16[48,640]{1,0:T(8,128)(2,1)S(1)} %get-tuple-element.54), channel_id=1, source_target_pairs={{0,1},{1,0},{2,3},{3,2},{4,5},{5,4},{6,7},{7,6},{8,9},{9,8},{10,11... | collective-permute-start | bytes 184328 | tf_op jit(solution)/shard_map/ppermute | solution.py:442
  18.4 1.1 %collective-permute-start.7 = (bf16[48,640]{1,0:T(8,128)(2,1)S(1)}, bf16[48,640]{1,0:T(8,128)(2,1)S(1)}, u32[]{:S(2)}, u32[]{:S(2)}) collective-permute-start(bf16[48,640]{1,0:T(8,128)(2,1)S(1)} %get-tuple-element.58), channel_id=1, source_target_pairs={{0,5},{1,4},{2,7},{3,6},{4,1},{5,0},{6,3},{7,2},{8,13},{9,12},{10,... | collective-permute-start | bytes 184328 | tf_op jit(solution)/shard_map/ppermute | solution.py:442
  19.5 1.9 %collective-permute-start.8 = (bf16[48,640]{1,0:T(8,128)(2,1)S(1)}, bf16[48,640]{1,0:T(8,128)(2,1)S(1)}, u32[]{:S(2)}, u32[]{:S(2)}) collective-permute-start(bf16[48,640]{1,0:T(8,128)(2,1)S(1)} %get-tuple-element.59), channel_id=1, source_target_pairs={{0,4},{1,5},{2,6},{3,7},{4,0},{5,1},{6,2},{7,3},{8,12},{9,13},{10,... | collective-permute-start | bytes 184328 | tf_op jit(solution)/shard_map/ppermute | solution.py:442
  21.4 0.0 collective-permute-done.6.beyond
  21.4 2.4 %collective-permute-done.5.other = bf16[48,640]{1,0:T(8,128)(2,1)S(1)} collective-permute-done((bf16[48,640]{1,0:T(8,128)(2,1)S(1)}, bf16[48,640]{1,0:T(8,128)(2,1)S(1)}, u32[]{:S(2)}, u32[]{:S(2)}) %collective-permute-start.5) | collective-permute-done | bytes 61472 | tf_op jit(solution)/shard_map/ppermute | solution.py:442
  23.7 1.6 %first_pair.1 = (f32[48,5184]{1,0:T(8,128)S(1)}, bf16[8,128,192]{2,1,0:T(8,128)(2,1)S(1)}) custom-call(bf16[48,640]{1,0:T(8,128)(2,1)S(1)} %get-tuple-element.53.own, bf16[48,640]{1,0:T(8,128)(2,1)S(1)} %collective-permute-done.5.other, bf16[768,128]{1,0:T(8,128)(2,1)S(1)} %pack.1.brick, bf16[864,128]{1,0:T(8,128)(2,1)S(1)} %collective-permute-done.2.across, ...), custom_call_target="tpu_custom_call" | custom-call | flops 1073741824 | bytes 2097152 | tf_op jit(solution)/shard_map/first_pair/pallas_call | solution.py:413
  25.3 0.0 collective-permute-done.7.other
  25.3 0.0 collective-permute-done.8.own
  25.3 1.5 %second_pair.1 = (f32[24,5184]{1,0:T(8,128)S(1)}, bf16[24,5184]{1,0:T(8,128)(2,1)S(1)}) custom-call(f32[48,5184]{1,0:T(8,128)S(1)} %get-tuple-element.57.before, bf16[48,640]{1,0:T(8,128)(2,1)S(1)} %collective-permute-done.7.other, bf16[48,640]{1,0:T(8,128)(2,1)S(1)} %collective-permute-done.8.own, bf16[8,128,192]{2,1,0:T(8,128)(2,1)S(1)} %get-tuple-element.60.masked), custom_call_target="tpu_custom_call" | custom-call | flops 1073741824 | bytes 2097152 | tf_op jit(solution)/shard_map/second_pair/pallas_call | solution.py:413
  26.9 0.1 collective-permute-start.9
  26.9 1.5 %collective-permute-done.9.other = bf16[24,5184]{1,0:T(8,128)(2,1)S(1)} collective-permute-done((bf16[24,5184]{1,0:T(8,128)(2,1)S(1)}, bf16[24,5184]{1,0:T(8,128)(2,1)S(1)}, u32[]{:S(2)}, u32[]{:S(2)}) %collective-permute-start.9) | collective-permute-done | bytes 248864 | tf_op jit(solution)/shard_map/ppermute | solution.py:442
  28.5 0.2 fold.1
  28.7 3.4 %collective-permute-start.10 = (bf16[8,3968]{1,0:T(8,128)(2,1)S(1)}, bf16[8,3968]{1,0:T(8,128)(2,1)S(1)}, u32[]{:S(2)}, u32[]{:S(2)}) collective-permute-start(bf16[8,3968]{1,0:T(8,128)(2,1)S(1)} %get-tuple-element.63), channel_id=1, source_target_pairs={{0,24},{8,16},{16,8},{24,0},{1,25},{9,17},{17,9},{25,1},{2,26},{10... | collective-permute-start | bytes 190472 | tf_op jit(solution)/shard_map/ppermute | solution.py:442
  32.1 0.0 collective-permute-start.11
  32.1 1.0 %collective-permute-start.12 = (bf16[8,3968]{1,0:T(8,128)(2,1)S(1)}, bf16[8,3968]{1,0:T(8,128)(2,1)S(1)}, u32[]{:S(2)}, u32[]{:S(2)}) collective-permute-start(bf16[8,3968]{1,0:T(8,128)(2,1)S(1)} %get-tuple-element.65), channel_id=1, source_target_pairs={{0,8},{8,0},{16,24},{24,16},{1,9},{9,1},{17,25},{25,17},{2,10},{10... | collective-permute-start | bytes 190472 | tf_op jit(solution)/shard_map/ppermute | solution.py:442
  33.1 2.6 %input_gradient.1 = (bf16[8,64,192]{2,1,0:T(8,128)(2,1)}, bf16[8,64,192]{2,1,0:T(8,128)(2,1)}) custom-call(bf16[10,80,192]{2,1,0:T(8,128)(2,1)S(1)} %get-tuple-element.45.gp, f32[8,64,128]{2,1,0:T(8,128)S(1)} %get-tuple-element.44.live, bf16[192,5184]{1,0:T(8,128)(2,1)S(1)} %bitcast.6, bf16[8,64,192]{2,1,0:T(8,128)(2,1)S(1)} %get-tuple-element.46.act), custom_call_target="tpu_custom_call" | custom-call | flops 1358954496 | bytes 4194304 | tf_op jit(solution)/shard_map/input_gradient/pallas_call | solution.py:413
  35.7 0.0 collective-permute-done.10.one
  35.7 2.3 %collective-permute-done.11.two = bf16[8,3968]{1,0:T(8,128)(2,1)S(1)} collective-permute-done((bf16[8,3968]{1,0:T(8,128)(2,1)S(1)}, bf16[8,3968]{1,0:T(8,128)(2,1)S(1)}, u32[]{:S(2)}, u32[]{:S(2)}) %collective-permute-start.11) | collective-permute-done | bytes 63520 | tf_op jit(solution)/shard_map/ppermute | solution.py:442
  38.0 0.0 collective-permute-done.12.three
  38.1 0.5 %collective-permute-start.13 = (bf16[8,3968]{1,0:T(8,128)(2,1)S(1)}, bf16[8,3968]{1,0:T(8,128)(2,1)S(1)}, u32[]{:S(2)}, u32[]{:S(2)}) collective-permute-start(bf16[8,3968]{1,0:T(8,128)(2,1)S(1)} %plane_sum.1.mine), channel_id=1, source_target_pairs={{0,1},{1,0},{2,3},{3,2},{4,5},{5,4},{6,7},{7,6},{8,9},{9,8},{10,11... | collective-permute-start | bytes 190472 | tf_op jit(solution)/shard_map/ppermute | solution.py:442
  38.5 3.8 %collective-permute-done.13.other = bf16[8,3968]{1,0:T(8,128)(2,1)S(1)} collective-permute-done((bf16[8,3968]{1,0:T(8,128)(2,1)S(1)}, bf16[8,3968]{1,0:T(8,128)(2,1)S(1)}, u32[]{:S(2)}, u32[]{:S(2)}) %collective-permute-start.13) | collective-permute-done | bytes 63520 | tf_op jit(solution)/shard_map/ppermute | solution.py:442
  42.4 0.8 %join.1 = f32[12,5184]{1,0:T(8,128)} custom-call(bf16[8,3968]{1,0:T(8,128)(2,1)S(1)} %plane_sum.1.mine, bf16[8,3968]{1,0:T(8,128)(2,1)S(1)} %collective-permute-done.13.other), custom_call_target="tpu_custom_call" | custom-call | flops 41472 | bytes 580608 | tf_op jit(solution)/shard_map/join/pallas_call | solution.py:413
  (1 shorter events, 0.0 us)
Async XLA Ops:
  0.6 1.0 %copy-start.1 = (bf16[8,8,8,192]{3,2,1,0:T(8,128)(2,1)S(1)}, bf16[8,8,8,192]{3,2,1,0:T(8,128)(2,1)}, u32[]{:S(2)}) copy-start(bf16[8,8,8,192]{3,2,1,0:T(8,128)(2,1)} %param.4) | copy-start | bytes 589828
  0.6 1.0 %copy-start.2 = (bf16[8,8,8,192]{3,2,1,0:T(8,128)(2,1)S(1)}, bf16[8,8,8,192]{3,2,1,0:T(8,128)(2,1)}, u32[]{:S(2)}) copy-start(bf16[8,8,8,192]{3,2,1,0:T(8,128)(2,1)} %param.7) | copy-start | bytes 589828
  0.7 1.0 %copy-start.3 = (s32[8,8,8]{2,1,0:T(8,128)S(1)}, s32[8,8,8]{2,1,0:T(8,128)}, u32[]{:S(2)}) copy-start(s32[8,8,8]{2,1,0:T(8,128)} %mask.1) | copy-start | bytes 6148
  0.7 5.0 %copy-start = (bf16[5184,192]{0,1:T(8,128)(2,1)S(1)}, bf16[5184,192]{0,1:T(8,128)(2,1)}, u32[]{:S(2)}) copy-start(bf16[5184,192]{0,1:T(8,128)(2,1)} %param.5) | copy-start | bytes 5971972
  2.0 11.9 %collective-permute-start.2 = (bf16[864,128]{1,0:T(8,128)(2,1)S(1)}, bf16[864,128]{1,0:T(8,128)(2,1)S(1)}, u32[]{:S(2)}, u32[]{:S(2)}) collective-permute-start(bf16[864,128]{1,0:T(8,128)(2,1)S(1)} %across.1), channel_id=1, source_target_pairs={{0,1},{1,0},{2,3},{3,2},{4,5},{5,4},{6,7},{7,6},{8,9},{9,8},{10,11... | collective-permute-start | bytes 663560 | tf_op jit(solution)/shard_map/ppermute | solution.py:442
  5.0 5.0 %collective-permute-start = (bf16[288,128]{1,0:T(8,128)(2,1)S(1)}, bf16[288,128]{1,0:T(8,128)(2,1)S(1)}, u32[]{:S(2)}, u32[]{:S(2)}) collective-permute-start(bf16[288,128]{1,0:T(8,128)(2,1)S(1)} %get-tuple-element.38), channel_id=1, source_target_pairs={{0,2},{2,0},{4,6},{6,4},{8,10},{10,8},{12,14},{14,12},{16,18},{18,... | collective-permute-start | bytes 221192 | tf_op jit(solution)/shard_map/ppermute | solution.py:442
  5.0 5.0 %collective-permute-start.1 = (bf16[288,128]{1,0:T(8,128)(2,1)S(1)}, bf16[288,128]{1,0:T(8,128)(2,1)S(1)}, u32[]{:S(2)}, u32[]{:S(2)}) collective-permute-start(bf16[288,128]{1,0:T(8,128)(2,1)S(1)} %get-tuple-element.39), channel_id=1, source_target_pairs={{0,0},{2,4},{4,2},{6,8},{8,6},{10,12},{12,10},{14,16},{16,14},{18,... | collective-permute-start | bytes 221192 | tf_op jit(solution)/shard_map/ppermute | solution.py:468
  6.6 11.2 %collective-permute-start.4 = (bf16[768,128]{1,0:T(8,128)(2,1)S(1)}, bf16[768,128]{1,0:T(8,128)(2,1)S(1)}, u32[]{:S(2)}, u32[]{:S(2)}) collective-permute-start(bf16[768,128]{1,0:T(8,128)(2,1)S(1)} %pack.1.brick), channel_id=1, source_target_pairs={{0,4},{1,5},{2,6},{3,7},{4,0},{5,1},{6,2},{7,3},{8,12},{9,13},{10,... | collective-permute-start | bytes 589832 | tf_op jit(solution)/shard_map/ppermute | solution.py:442
  10.2 6.5 %collective-permute-start.3 = (bf16[128,128]{1,0:T(8,128)(2,1)S(1)}, bf16[128,128]{1,0:T(8,128)(2,1)S(1)}, u32[]{:S(2)}, u32[]{:S(2)}) collective-permute-start(bf16[128,128]{1,0:T(8,128)(2,1)S(1)} %corner.1), channel_id=1, source_target_pairs={{0,1},{1,0},{2,3},{3,2},{4,5},{5,4},{6,7},{7,6},{8,9},{9,8},{10,11... | collective-permute-start | bytes 98312 | tf_op jit(solution)/shard_map/ppermute | solution.py:442
  10.3 11.0 %collective-permute-start.6 = (bf16[768,128]{1,0:T(8,128)(2,1)S(1)}, bf16[768,128]{1,0:T(8,128)(2,1)S(1)}, u32[]{:S(2)}, u32[]{:S(2)}) collective-permute-start(bf16[768,128]{1,0:T(8,128)(2,1)S(1)} %pack.1.brick), channel_id=1, source_target_pairs={{0,5},{1,4},{2,7},{3,6},{4,1},{5,0},{6,3},{7,2},{8,13},{9,12},{10,... | collective-permute-start | bytes 589832 | tf_op jit(solution)/shard_map/ppermute | solution.py:442
  17.8 5.9 %collective-permute-start.5 = (bf16[48,640]{1,0:T(8,128)(2,1)S(1)}, bf16[48,640]{1,0:T(8,128)(2,1)S(1)}, u32[]{:S(2)}, u32[]{:S(2)}) collective-permute-start(bf16[48,640]{1,0:T(8,128)(2,1)S(1)} %get-tuple-element.54), channel_id=1, source_target_pairs={{0,1},{1,0},{2,3},{3,2},{4,5},{5,4},{6,7},{7,6},{8,9},{9,8},{10,11... | collective-permute-start | bytes 184328 | tf_op jit(solution)/shard_map/ppermute | solution.py:442
  18.4 6.9 %collective-permute-start.7 = (bf16[48,640]{1,0:T(8,128)(2,1)S(1)}, bf16[48,640]{1,0:T(8,128)(2,1)S(1)}, u32[]{:S(2)}, u32[]{:S(2)}) collective-permute-start(bf16[48,640]{1,0:T(8,128)(2,1)S(1)} %get-tuple-element.58), channel_id=1, source_target_pairs={{0,5},{1,4},{2,7},{3,6},{4,1},{5,0},{6,3},{7,2},{8,13},{9,12},{10,... | collective-permute-start | bytes 184328 | tf_op jit(solution)/shard_map/ppermute | solution.py:442
  19.5 5.9 %collective-permute-start.8 = (bf16[48,640]{1,0:T(8,128)(2,1)S(1)}, bf16[48,640]{1,0:T(8,128)(2,1)S(1)}, u32[]{:S(2)}, u32[]{:S(2)}) collective-permute-start(bf16[48,640]{1,0:T(8,128)(2,1)S(1)} %get-tuple-element.59), channel_id=1, source_target_pairs={{0,4},{1,5},{2,6},{3,7},{4,0},{5,1},{6,2},{7,3},{8,12},{9,13},{10,... | collective-permute-start | bytes 184328 | tf_op jit(solution)/shard_map/ppermute | solution.py:442
  26.9 1.6 %collective-permute-start.9 = (bf16[24,5184]{1,0:T(8,128)(2,1)S(1)}, bf16[24,5184]{1,0:T(8,128)(2,1)S(1)}, u32[]{:S(2)}, u32[]{:S(2)}) collective-permute-start(bf16[24,5184]{1,0:T(8,128)(2,1)S(1)} %get-tuple-element.62), channel_id=1, source_target_pairs={{0,2},{1,3},{2,0},{3,1},{4,6},{5,7},{6,4},{7,5},{8,10},{9,11},{10,... | collective-permute-start | bytes 746504 | tf_op jit(solution)/shard_map/ppermute | solution.py:442
  28.7 7.1 %collective-permute-start.10 = (bf16[8,3968]{1,0:T(8,128)(2,1)S(1)}, bf16[8,3968]{1,0:T(8,128)(2,1)S(1)}, u32[]{:S(2)}, u32[]{:S(2)}) collective-permute-start(bf16[8,3968]{1,0:T(8,128)(2,1)S(1)} %get-tuple-element.63), channel_id=1, source_target_pairs={{0,24},{8,16},{16,8},{24,0},{1,25},{9,17},{17,9},{25,1},{2,26},{10... | collective-permute-start | bytes 190472 | tf_op jit(solution)/shard_map/ppermute | solution.py:442
  32.1 5.9 %collective-permute-start.11 = (bf16[8,3968]{1,0:T(8,128)(2,1)S(1)}, bf16[8,3968]{1,0:T(8,128)(2,1)S(1)}, u32[]{:S(2)}, u32[]{:S(2)}) collective-permute-start(bf16[8,3968]{1,0:T(8,128)(2,1)S(1)} %get-tuple-element.64), channel_id=1, source_target_pairs={{0,16},{8,24},{16,0},{24,8},{1,17},{9,25},{17,1},{25,9},{2,18},{10... | collective-permute-start | bytes 190472 | tf_op jit(solution)/shard_map/ppermute | solution.py:442
  32.1 5.9 %collective-permute-start.12 = (bf16[8,3968]{1,0:T(8,128)(2,1)S(1)}, bf16[8,3968]{1,0:T(8,128)(2,1)S(1)}, u32[]{:S(2)}, u32[]{:S(2)}) collective-permute-start(bf16[8,3968]{1,0:T(8,128)(2,1)S(1)} %get-tuple-element.65), channel_id=1, source_target_pairs={{0,8},{8,0},{16,24},{24,16},{1,9},{9,1},{17,25},{25,17},{2,10},{10... | collective-permute-start | bytes 190472 | tf_op jit(solution)/shard_map/ppermute | solution.py:442
  38.1 4.3 %collective-permute-start.13 = (bf16[8,3968]{1,0:T(8,128)(2,1)S(1)}, bf16[8,3968]{1,0:T(8,128)(2,1)S(1)}, u32[]{:S(2)}, u32[]{:S(2)}) collective-permute-start(bf16[8,3968]{1,0:T(8,128)(2,1)S(1)} %plane_sum.1.mine), channel_id=1, source_target_pairs={{0,1},{1,0},{2,3},{3,2},{4,5},{5,4},{6,7},{7,6},{8,9},{9,8},{10,11... | collective-permute-start | bytes 190472 | tf_op jit(solution)/shard_map/ppermute | solution.py:442

commit v21 on v20

--- a/solution.py
+++ b/solution.py
@@ -541,7 +541,7 @@
             pltpu.VMEM((planes, 8, lanes), f32),
         ),
     )(keep, in_plane(fold, 2))
-    got = [swap(sent, "depth", d, planes) for d, sent in list(enumerate(sends, 1))[::-1]]
+    got = [swap(sends[d - 1], "depth", d, planes) for d in (2, 3, 1)]
     grad_input, *got = lax.optimization_barrier((grad_input, *got))
     voxels = count * SIDES * width * rows
     mine = call(

time: 43.3 us -> 43.2 us (level)
  transfers between devices with their start and end apart: 14 -> 14, of which waited for: 4 -> 6; matrix products, arithmetic and copies ran while one was open for 0% -> 0% of each run, Pallas kernels for 21% -> 21%
where the time goes in v21:
time: 43.2 us; the launch traced here: 43 us
  starting transfers between devices  19 us (44%)
  Pallas kernels  12.2 us (28%)
  waiting for transfers between devices  10.2 us (24%)
  local copies, waits for them, and re-layouts  0.84 us (2%)
  between operations  0.77 us (2%)
    ppermute x13, starting transfers between devices, swap(): return lax.ppermute(piece, axes, [(i, i ^ distance) for i in range(size)])  18.4 us
    pallas_call x14, Pallas kernels, run(): pl.pallas_call(body, out_shape=out_shape, in_specs=in_specs or [spec] * l...  12.2 us
    ppermute x13, waiting for transfers between devices, swap(): return lax.ppermute(piece, axes, [(i, i ^ distance) for i in range(size)])  10.2 us
  transfers between devices with their start and end apart: 14, of which 6 were waited for; matrix products, arithmetic and copies ran while one was open for 0% of the time, Pallas kernels for 21%

profile of v21, /device:TPU:0, one launch (start us, length us, event | category | flops | bytes accessed | tf_op | source)
XLA Modules:
  0.0 43.0 jit_solution(13315892568732341573)
XLA Ops:
  0.6 0.0 copy-start.1
  0.6 0.0 copy-start.2
  0.7 0.0 copy-start.3
  0.7 0.0 copy-start
  0.7 0.2 pick.1.first
  0.8 0.7 %copy-done.1 = bf16[8,8,8,192]{3,2,1,0:T(8,128)(2,1)S(1)} copy-done((bf16[8,8,8,192]{3,2,1,0:T(8,128)(2,1)S(1)}, bf16[8,8,8,192]{3,2,1,0:T(8,128)(2,1)}, u32[]{:S(2)}) %copy-start.1) | copy-done | bytes 196632
  1.6 0.1 copy-done.2
  1.7 0.0 copy-done.3
  1.7 0.2 prepare.1
  1.9 0.1 across.1
  2.0 3.0 %collective-permute-start.2 = (bf16[864,128]{1,0:T(8,128)(2,1)S(1)}, bf16[864,128]{1,0:T(8,128)(2,1)S(1)}, u32[]{:S(2)}, u32[]{:S(2)}) collective-permute-start(bf16[864,128]{1,0:T(8,128)(2,1)S(1)} %across.1), channel_id=1, source_target_pairs={{0,1},{1,0},{2,3},{3,2},{4,5},{5,4},{6,7},{7,6},{8,9},{9,8},{10,11... | collective-permute-start | bytes 663560 | tf_op jit(solution)/shard_map/ppermute | solution.py:442
  5.0 0.0 collective-permute-start
  5.0 0.7 %collective-permute-start.1 = (bf16[288,128]{1,0:T(8,128)(2,1)S(1)}, bf16[288,128]{1,0:T(8,128)(2,1)S(1)}, u32[]{:S(2)}, u32[]{:S(2)}) collective-permute-start(bf16[288,128]{1,0:T(8,128)(2,1)S(1)} %get-tuple-element.39), channel_id=1, source_target_pairs={{0,0},{2,4},{4,2},{6,8},{8,6},{10,12},{12,10},{14,16},{16,14},{18,... | collective-permute-start | bytes 221192 | tf_op jit(solution)/shard_map/ppermute | solution.py:468
  5.7 0.0 copy-done
  5.7 0.8 %turn.1.after.weight = bf16[5184,192]{1,0:T(8,128)(2,1)S(1)} custom-call(bf16[192,5184]{1,0:T(8,128)(2,1)S(1)} %bitcast.5), custom_call_target="tpu_custom_call" | custom-call | flops 1048576 | bytes 4194304 | tf_op jit(solution)/shard_map/turn/pallas_call | solution.py:413
  6.5 0.1 pack.1.brick
  6.6 3.4 %collective-permute-start.4 = (bf16[768,128]{1,0:T(8,128)(2,1)S(1)}, bf16[768,128]{1,0:T(8,128)(2,1)S(1)}, u32[]{:S(2)}, u32[]{:S(2)}) collective-permute-start(bf16[768,128]{1,0:T(8,128)(2,1)S(1)} %pack.1.brick), channel_id=1, source_target_pairs={{0,4},{1,5},{2,6},{3,7},{4,0},{5,1},{6,2},{7,3},{8,12},{9,13},{10,... | collective-permute-start | bytes 589832 | tf_op jit(solution)/shard_map/ppermute | solution.py:442
  10.0 0.0 collective-permute-done.near
  10.0 0.0 collective-permute-done.1.far
  10.0 0.2 corner.1
  10.2 0.1 collective-permute-start.3
  10.3 3.5 %collective-permute-start.6 = (bf16[768,128]{1,0:T(8,128)(2,1)S(1)}, bf16[768,128]{1,0:T(8,128)(2,1)S(1)}, u32[]{:S(2)}, u32[]{:S(2)}) collective-permute-start(bf16[768,128]{1,0:T(8,128)(2,1)S(1)} %pack.1.brick), channel_id=1, source_target_pairs={{0,5},{1,4},{2,7},{3,6},{4,1},{5,0},{6,3},{7,2},{8,13},{9,12},{10,... | collective-permute-start | bytes 589832 | tf_op jit(solution)/shard_map/ppermute | solution.py:442
  13.9 0.0 collective-permute-done.2.across
  13.9 2.8 %bulk.1 = f32[10,80,192]{2,1,0:T(8,128)S(1)} custom-call(bf16[8,64,192]{2,1,0:T(8,128)(2,1)S(1)} %get-tuple-element.37.masked, bf16[288,128]{1,0:T(8,128)(2,1)S(1)} %collective-permute-done.near, bf16[288,128]{1,0:T(8,128)(2,1)S(1)} %collective-permute-done.1.far, bf16[864,128]{1,0:T(8,128)(2,1)S(1)} %collective-permute-done.2.across, ...), custom_call_target="tpu_custom_call" | custom-call | flops 1610612736 | bytes 1048576 | tf_op jit(solution)/shard_map/bulk/pallas_call | solution.py:413
  16.7 0.0 collective-permute-done.3.corner
  16.7 1.1 %forward.1 = (bf16[8,64,192]{2,1,0:T(8,128)(2,1)S(1)}, bf16[10,80,192]{2,1,0:T(8,128)(2,1)S(1)}, bf16[48,640]{1,0:T(8,128)(2,1)S(1)}, bf16[48,640]{1,0:T(8,128)(...) custom-call(f32[10,80,192]{2,1,0:T(8,128)S(1)} %bulk.1, ...), custom_call_target="tpu_custom_call" | custom-call | flops 1610612736 | bytes 1048576 | tf_op jit(solution)/shard_map/forward/pallas_call | solution.py:413
  17.8 0.0 collective-permute-done.4.beside
  17.8 0.6 %collective-permute-start.5 = (bf16[48,640]{1,0:T(8,128)(2,1)S(1)}, bf16[48,640]{1,0:T(8,128)(2,1)S(1)}, u32[]{:S(2)}, u32[]{:S(2)}) collective-permute-start(bf16[48,640]{1,0:T(8,128)(2,1)S(1)} %get-tuple-element.54), channel_id=1, source_target_pairs={{0,1},{1,0},{2,3},{3,2},{4,5},{5,4},{6,7},{7,6},{8,9},{9,8},{10,11... | collective-permute-start | bytes 184328 | tf_op jit(solution)/shard_map/ppermute | solution.py:442
  18.4 1.1 %collective-permute-start.7 = (bf16[48,640]{1,0:T(8,128)(2,1)S(1)}, bf16[48,640]{1,0:T(8,128)(2,1)S(1)}, u32[]{:S(2)}, u32[]{:S(2)}) collective-permute-start(bf16[48,640]{1,0:T(8,128)(2,1)S(1)} %get-tuple-element.58), channel_id=1, source_target_pairs={{0,5},{1,4},{2,7},{3,6},{4,1},{5,0},{6,3},{7,2},{8,13},{9,12},{10,... | collective-permute-start | bytes 184328 | tf_op jit(solution)/shard_map/ppermute | solution.py:442
  19.5 1.9 %collective-permute-start.8 = (bf16[48,640]{1,0:T(8,128)(2,1)S(1)}, bf16[48,640]{1,0:T(8,128)(2,1)S(1)}, u32[]{:S(2)}, u32[]{:S(2)}) collective-permute-start(bf16[48,640]{1,0:T(8,128)(2,1)S(1)} %get-tuple-element.59), channel_id=1, source_target_pairs={{0,4},{1,5},{2,6},{3,7},{4,0},{5,1},{6,2},{7,3},{8,12},{9,13},{10,... | collective-permute-start | bytes 184328 | tf_op jit(solution)/shard_map/ppermute | solution.py:442
  21.4 0.0 collective-permute-done.6.beyond
  21.4 2.4 %collective-permute-done.5.other = bf16[48,640]{1,0:T(8,128)(2,1)S(1)} collective-permute-done((bf16[48,640]{1,0:T(8,128)(2,1)S(1)}, bf16[48,640]{1,0:T(8,128)(2,1)S(1)}, u32[]{:S(2)}, u32[]{:S(2)}) %collective-permute-start.5) | collective-permute-done | bytes 61472 | tf_op jit(solution)/shard_map/ppermute | solution.py:442
  23.7 1.6 %first_pair.1 = (f32[48,5184]{1,0:T(8,128)S(1)}, bf16[8,128,192]{2,1,0:T(8,128)(2,1)S(1)}) custom-call(bf16[48,640]{1,0:T(8,128)(2,1)S(1)} %get-tuple-element.53.own, bf16[48,640]{1,0:T(8,128)(2,1)S(1)} %collective-permute-done.5.other, bf16[768,128]{1,0:T(8,128)(2,1)S(1)} %pack.1.brick, bf16[864,128]{1,0:T(8,128)(2,1)S(1)} %collective-permute-done.2.across, ...), custom_call_target="tpu_custom_call" | custom-call | flops 1073741824 | bytes 2097152 | tf_op jit(solution)/shard_map/first_pair/pallas_call | solution.py:413
  25.3 0.0 collective-permute-done.7.other
  25.3 0.0 collective-permute-done.8.own
  25.3 1.5 %second_pair.1 = (f32[24,5184]{1,0:T(8,128)S(1)}, bf16[24,5184]{1,0:T(8,128)(2,1)S(1)}) custom-call(f32[48,5184]{1,0:T(8,128)S(1)} %get-tuple-element.57.before, bf16[48,640]{1,0:T(8,128)(2,1)S(1)} %collective-permute-done.7.other, bf16[48,640]{1,0:T(8,128)(2,1)S(1)} %collective-permute-done.8.own, bf16[8,128,192]{2,1,0:T(8,128)(2,1)S(1)} %get-tuple-element.60.masked), custom_call_target="tpu_custom_call" | custom-call | flops 1073741824 | bytes 2097152 | tf_op jit(solution)/shard_map/second_pair/pallas_call | solution.py:413
  26.9 0.1 collective-permute-start.9
  26.9 1.5 %collective-permute-done.9.other = bf16[24,5184]{1,0:T(8,128)(2,1)S(1)} collective-permute-done((bf16[24,5184]{1,0:T(8,128)(2,1)S(1)}, bf16[24,5184]{1,0:T(8,128)(2,1)S(1)}, u32[]{:S(2)}, u32[]{:S(2)}) %collective-permute-start.9) | collective-permute-done | bytes 248864 | tf_op jit(solution)/shard_map/ppermute | solution.py:442
  28.5 0.2 fold.1
  28.7 2.7 %collective-permute-start.10 = (bf16[8,3968]{1,0:T(8,128)(2,1)S(1)}, bf16[8,3968]{1,0:T(8,128)(2,1)S(1)}, u32[]{:S(2)}, u32[]{:S(2)}) collective-permute-start(bf16[8,3968]{1,0:T(8,128)(2,1)S(1)} %get-tuple-element.63), channel_id=1, source_target_pairs={{0,16},{8,24},{16,0},{24,8},{1,17},{9,25},{17,1},{25,9},{2,18},{10... | collective-permute-start | bytes 190472 | tf_op jit(solution)/shard_map/ppermute | solution.py:442
  31.4 1.4 %collective-permute-start.11 = (bf16[8,3968]{1,0:T(8,128)(2,1)S(1)}, bf16[8,3968]{1,0:T(8,128)(2,1)S(1)}, u32[]{:S(2)}, u32[]{:S(2)}) collective-permute-start(bf16[8,3968]{1,0:T(8,128)(2,1)S(1)} %get-tuple-element.64), channel_id=1, source_target_pairs={{0,24},{8,16},{16,8},{24,0},{1,25},{9,17},{17,9},{25,1},{2,26},{10... | collective-permute-start | bytes 190472 | tf_op jit(solution)/shard_map/ppermute | solution.py:442
  32.7 0.0 collective-permute-start.12
  32.7 2.6 %input_gradient.1 = (bf16[8,64,192]{2,1,0:T(8,128)(2,1)}, bf16[8,64,192]{2,1,0:T(8,128)(2,1)}) custom-call(bf16[10,80,192]{2,1,0:T(8,128)(2,1)S(1)} %get-tuple-element.45.gp, f32[8,64,128]{2,1,0:T(8,128)S(1)} %get-tuple-element.44.live, bf16[192,5184]{1,0:T(8,128)(2,1)S(1)} %bitcast.6, bf16[8,64,192]{2,1,0:T(8,128)(2,1)S(1)} %get-tuple-element.46.act), custom_call_target="tpu_custom_call" | custom-call | flops 1358954496 | bytes 4194304 | tf_op jit(solution)/shard_map/input_gradient/pallas_call | solution.py:413
  35.4 0.1 collective-permute-done.10.one
  35.4 2.3 %collective-permute-done.11.two = bf16[8,3968]{1,0:T(8,128)(2,1)S(1)} collective-permute-done((bf16[8,3968]{1,0:T(8,128)(2,1)S(1)}, bf16[8,3968]{1,0:T(8,128)(2,1)S(1)}, u32[]{:S(2)}, u32[]{:S(2)}) %collective-permute-start.11) | collective-permute-done | bytes 63520 | tf_op jit(solution)/shard_map/ppermute | solution.py:442
  37.7 0.2 collective-permute-done.12.three
  37.9 0.5 %collective-permute-start.13 = (bf16[8,3968]{1,0:T(8,128)(2,1)S(1)}, bf16[8,3968]{1,0:T(8,128)(2,1)S(1)}, u32[]{:S(2)}, u32[]{:S(2)}) collective-permute-start(bf16[8,3968]{1,0:T(8,128)(2,1)S(1)} %plane_sum.1.mine), channel_id=1, source_target_pairs={{0,1},{1,0},{2,3},{3,2},{4,5},{5,4},{6,7},{7,6},{8,9},{9,8},{10,11... | collective-permute-start | bytes 190472 | tf_op jit(solution)/shard_map/ppermute | solution.py:442
  38.4 3.8 %collective-permute-done.13.other = bf16[8,3968]{1,0:T(8,128)(2,1)S(1)} collective-permute-done((bf16[8,3968]{1,0:T(8,128)(2,1)S(1)}, bf16[8,3968]{1,0:T(8,128)(2,1)S(1)}, u32[]{:S(2)}, u32[]{:S(2)}) %collective-permute-start.13) | collective-permute-done | bytes 63520 | tf_op jit(solution)/shard_map/ppermute | solution.py:442
  42.2 0.8 %join.1 = f32[12,5184]{1,0:T(8,128)} custom-call(bf16[8,3968]{1,0:T(8,128)(2,1)S(1)} %plane_sum.1.mine, bf16[8,3968]{1,0:T(8,128)(2,1)S(1)} %collective-permute-done.13.other), custom_call_target="tpu_custom_call" | custom-call | flops 41472 | bytes 580608 | tf_op jit(solution)/shard_map/join/pallas_call | solution.py:413
  (1 shorter events, 0.0 us)
Async XLA Ops:
  0.6 1.0 %copy-start.1 = (bf16[8,8,8,192]{3,2,1,0:T(8,128)(2,1)S(1)}, bf16[8,8,8,192]{3,2,1,0:T(8,128)(2,1)}, u32[]{:S(2)}) copy-start(bf16[8,8,8,192]{3,2,1,0:T(8,128)(2,1)} %param.4) | copy-start | bytes 589828
  0.6 1.0 %copy-start.2 = (bf16[8,8,8,192]{3,2,1,0:T(8,128)(2,1)S(1)}, bf16[8,8,8,192]{3,2,1,0:T(8,128)(2,1)}, u32[]{:S(2)}) copy-start(bf16[8,8,8,192]{3,2,1,0:T(8,128)(2,1)} %param.7) | copy-start | bytes 589828
  0.7 1.0 %copy-start.3 = (s32[8,8,8]{2,1,0:T(8,128)S(1)}, s32[8,8,8]{2,1,0:T(8,128)}, u32[]{:S(2)}) copy-start(s32[8,8,8]{2,1,0:T(8,128)} %mask.1) | copy-start | bytes 6148
  0.7 5.0 %copy-start = (bf16[5184,192]{0,1:T(8,128)(2,1)S(1)}, bf16[5184,192]{0,1:T(8,128)(2,1)}, u32[]{:S(2)}) copy-start(bf16[5184,192]{0,1:T(8,128)(2,1)} %param.5) | copy-start | bytes 5971972
  2.0 11.9 %collective-permute-start.2 = (bf16[864,128]{1,0:T(8,128)(2,1)S(1)}, bf16[864,128]{1,0:T(8,128)(2,1)S(1)}, u32[]{:S(2)}, u32[]{:S(2)}) collective-permute-start(bf16[864,128]{1,0:T(8,128)(2,1)S(1)} %across.1), channel_id=1, source_target_pairs={{0,1},{1,0},{2,3},{3,2},{4,5},{5,4},{6,7},{7,6},{8,9},{9,8},{10,11... | collective-permute-start | bytes 663560 | tf_op jit(solution)/shard_map/ppermute | solution.py:442
  5.0 5.0 %collective-permute-start = (bf16[288,128]{1,0:T(8,128)(2,1)S(1)}, bf16[288,128]{1,0:T(8,128)(2,1)S(1)}, u32[]{:S(2)}, u32[]{:S(2)}) collective-permute-start(bf16[288,128]{1,0:T(8,128)(2,1)S(1)} %get-tuple-element.38), channel_id=1, source_target_pairs={{0,2},{2,0},{4,6},{6,4},{8,10},{10,8},{12,14},{14,12},{16,18},{18,... | collective-permute-start | bytes 221192 | tf_op jit(solution)/shard_map/ppermute | solution.py:442
  5.0 5.0 %collective-permute-start.1 = (bf16[288,128]{1,0:T(8,128)(2,1)S(1)}, bf16[288,128]{1,0:T(8,128)(2,1)S(1)}, u32[]{:S(2)}, u32[]{:S(2)}) collective-permute-start(bf16[288,128]{1,0:T(8,128)(2,1)S(1)} %get-tuple-element.39), channel_id=1, source_target_pairs={{0,0},{2,4},{4,2},{6,8},{8,6},{10,12},{12,10},{14,16},{16,14},{18,... | collective-permute-start | bytes 221192 | tf_op jit(solution)/shard_map/ppermute | solution.py:468
  6.6 11.2 %collective-permute-start.4 = (bf16[768,128]{1,0:T(8,128)(2,1)S(1)}, bf16[768,128]{1,0:T(8,128)(2,1)S(1)}, u32[]{:S(2)}, u32[]{:S(2)}) collective-permute-start(bf16[768,128]{1,0:T(8,128)(2,1)S(1)} %pack.1.brick), channel_id=1, source_target_pairs={{0,4},{1,5},{2,6},{3,7},{4,0},{5,1},{6,2},{7,3},{8,12},{9,13},{10,... | collective-permute-start | bytes 589832 | tf_op jit(solution)/shard_map/ppermute | solution.py:442
  10.2 6.5 %collective-permute-start.3 = (bf16[128,128]{1,0:T(8,128)(2,1)S(1)}, bf16[128,128]{1,0:T(8,128)(2,1)S(1)}, u32[]{:S(2)}, u32[]{:S(2)}) collective-permute-start(bf16[128,128]{1,0:T(8,128)(2,1)S(1)} %corner.1), channel_id=1, source_target_pairs={{0,1},{1,0},{2,3},{3,2},{4,5},{5,4},{6,7},{7,6},{8,9},{9,8},{10,11... | collective-permute-start | bytes 98312 | tf_op jit(solution)/shard_map/ppermute | solution.py:442
  10.3 11.0 %collective-permute-start.6 = (bf16[768,128]{1,0:T(8,128)(2,1)S(1)}, bf16[768,128]{1,0:T(8,128)(2,1)S(1)}, u32[]{:S(2)}, u32[]{:S(2)}) collective-permute-start(bf16[768,128]{1,0:T(8,128)(2,1)S(1)} %pack.1.brick), channel_id=1, source_target_pairs={{0,5},{1,4},{2,7},{3,6},{4,1},{5,0},{6,3},{7,2},{8,13},{9,12},{10,... | collective-permute-start | bytes 589832 | tf_op jit(solution)/shard_map/ppermute | solution.py:442
  17.8 5.9 %collective-permute-start.5 = (bf16[48,640]{1,0:T(8,128)(2,1)S(1)}, bf16[48,640]{1,0:T(8,128)(2,1)S(1)}, u32[]{:S(2)}, u32[]{:S(2)}) collective-permute-start(bf16[48,640]{1,0:T(8,128)(2,1)S(1)} %get-tuple-element.54), channel_id=1, source_target_pairs={{0,1},{1,0},{2,3},{3,2},{4,5},{5,4},{6,7},{7,6},{8,9},{9,8},{10,11... | collective-permute-start | bytes 184328 | tf_op jit(solution)/shard_map/ppermute | solution.py:442
  18.4 6.9 %collective-permute-start.7 = (bf16[48,640]{1,0:T(8,128)(2,1)S(1)}, bf16[48,640]{1,0:T(8,128)(2,1)S(1)}, u32[]{:S(2)}, u32[]{:S(2)}) collective-permute-start(bf16[48,640]{1,0:T(8,128)(2,1)S(1)} %get-tuple-element.58), channel_id=1, source_target_pairs={{0,5},{1,4},{2,7},{3,6},{4,1},{5,0},{6,3},{7,2},{8,13},{9,12},{10,... | collective-permute-start | bytes 184328 | tf_op jit(solution)/shard_map/ppermute | solution.py:442
  19.5 5.9 %collective-permute-start.8 = (bf16[48,640]{1,0:T(8,128)(2,1)S(1)}, bf16[48,640]{1,0:T(8,128)(2,1)S(1)}, u32[]{:S(2)}, u32[]{:S(2)}) collective-permute-start(bf16[48,640]{1,0:T(8,128)(2,1)S(1)} %get-tuple-element.59), channel_id=1, source_target_pairs={{0,4},{1,5},{2,6},{3,7},{4,0},{5,1},{6,2},{7,3},{8,12},{9,13},{10,... | collective-permute-start | bytes 184328 | tf_op jit(solution)/shard_map/ppermute | solution.py:442
  26.9 1.6 %collective-permute-start.9 = (bf16[24,5184]{1,0:T(8,128)(2,1)S(1)}, bf16[24,5184]{1,0:T(8,128)(2,1)S(1)}, u32[]{:S(2)}, u32[]{:S(2)}) collective-permute-start(bf16[24,5184]{1,0:T(8,128)(2,1)S(1)} %get-tuple-element.62), channel_id=1, source_target_pairs={{0,2},{1,3},{2,0},{3,1},{4,6},{5,7},{6,4},{7,5},{8,10},{9,11},{10,... | collective-permute-start | bytes 746504 | tf_op jit(solution)/shard_map/ppermute | solution.py:442
  28.7 6.8 %collective-permute-start.10 = (bf16[8,3968]{1,0:T(8,128)(2,1)S(1)}, bf16[8,3968]{1,0:T(8,128)(2,1)S(1)}, u32[]{:S(2)}, u32[]{:S(2)}) collective-permute-start(bf16[8,3968]{1,0:T(8,128)(2,1)S(1)} %get-tuple-element.63), channel_id=1, source_target_pairs={{0,16},{8,24},{16,0},{24,8},{1,17},{9,25},{17,1},{25,9},{2,18},{10... | collective-permute-start | bytes 190472 | tf_op jit(solution)/shard_map/ppermute | solution.py:442
  31.4 6.3 %collective-permute-start.11 = (bf16[8,3968]{1,0:T(8,128)(2,1)S(1)}, bf16[8,3968]{1,0:T(8,128)(2,1)S(1)}, u32[]{:S(2)}, u32[]{:S(2)}) collective-permute-start(bf16[8,3968]{1,0:T(8,128)(2,1)S(1)} %get-tuple-element.64), channel_id=1, source_target_pairs={{0,24},{8,16},{16,8},{24,0},{1,25},{9,17},{17,9},{25,1},{2,26},{10... | collective-permute-start | bytes 190472 | tf_op jit(solution)/shard_map/ppermute | solution.py:442
  32.7 5.1 %collective-permute-start.12 = (bf16[8,3968]{1,0:T(8,128)(2,1)S(1)}, bf16[8,3968]{1,0:T(8,128)(2,1)S(1)}, u32[]{:S(2)}, u32[]{:S(2)}) collective-permute-start(bf16[8,3968]{1,0:T(8,128)(2,1)S(1)} %get-tuple-element.65), channel_id=1, source_target_pairs={{0,8},{8,0},{16,24},{24,16},{1,9},{9,1},{17,25},{25,17},{2,10},{10... | collective-permute-start | bytes 190472 | tf_op jit(solution)/shard_map/ppermute | solution.py:442
  37.9 4.3 %collective-permute-start.13 = (bf16[8,3968]{1,0:T(8,128)(2,1)S(1)}, bf16[8,3968]{1,0:T(8,128)(2,1)S(1)}, u32[]{:S(2)}, u32[]{:S(2)}) collective-permute-start(bf16[8,3968]{1,0:T(8,128)(2,1)S(1)} %plane_sum.1.mine), channel_id=1, source_target_pairs={{0,1},{1,0},{2,3},{3,2},{4,5},{5,4},{6,7},{7,6},{8,9},{9,8},{10,11... | collective-permute-start | bytes 190472 | tf_op jit(solution)/shard_map/ppermute | solution.py:442

commit v22 on v21

--- a/solution.py
+++ b/solution.py
@@ -101,7 +101,7 @@
         ref[...] = rows_of_128(slabs).astype(jnp.bfloat16)
 
 
-def pack_kernel(masked, after, packed_ref):
+def pack_kernel(masked, packed_ref):
     count, channels = packed_ref.shape[0] * 128 // masked.shape[2], masked.shape[2]
     block = masked[...].reshape(count, channels)
     packed_ref[...] = rows_of_128(block)
@@ -476,10 +476,12 @@
     )(masked, cot)
     across = in_plane(across, CHIPS[1])
     packed = call(
-        pack_kernel, "pack", 4, 1 << 16, 1 << 19, array((count_128, 128), bf16), (),
-        [vmem, pl.BlockSpec(memory_space=pl.ANY)],
-    )(masked, weight_rows)
-    near, far, weight_rows, late = lax.optimization_barrier((near, far, weight_rows, packed))
+        pack_kernel, "pack", 4, 1 << 16, 1 << 19, array((count_128, 128), bf16)
+    )(masked)
+    beside = in_plane(packed, CHIPS[2])
+    near, far, weight_rows, late, beside = lax.optimization_barrier(
+        (near, far, weight_rows, packed, beside)
+    )
     corner = call(
         corner_kernel, "corner", 4, 1 << 16, 1 << 18,
         array((128, 128), bf16),
@@ -495,7 +497,7 @@
             pltpu.VMEM((width + 4, mid, 9 * channels), bf16),
         ),
     )(masked, near, far, across, weight_rows)
-    bricks = [packed, across, in_plane(packed, CHIPS[2]), in_plane(late, CHIPS[3])]
+    bricks = [packed, across, beside, in_plane(late, CHIPS[3])]
 
     act, gp, *slices = call(
         forward_kernel, "forward", 24, 3 << 29, 1 << 20,
@@ -508,7 +510,6 @@
             pltpu.VMEM((MEMBERS, group, span), f32),
         ),
     )(bulk, cot, near, far, across, corner, live, weight_rows, pick)
-    bricks[2], *slices = lax.optimization_barrier((bricks[2], *slices))
     for place in (3, 2, 1):
         slices[place] = in_plane(slices[place], CHIPS[place])
 

time: 43.2 us -> 47.8 us (1.11)
  waiting for transfers between devices: 10.2 us -> 14.5 us
    ppermute x13, waiting for transfers between devices: 10.2 us -> 14.5 us  [swap(): return lax.ppermute(piece, axes, [(i, i ^ distance) for i in range(size)])]
  transfers between devices with their start and end apart: 14 -> 14, of which waited for: 6 -> 8; matrix products, arithmetic and copies ran while one was open for 0% -> 0% of each run, Pallas kernels for 21% -> 19%
where the time goes in v22:
time: 47.8 us; the launch traced here: 47.6 us
  starting transfers between devices  19.3 us (40%)
  waiting for transfers between devices  14.5 us (30%)
  Pallas kernels  12.2 us (26%)
  local copies, waits for them, and re-layouts  0.84 us (2%)
  between operations  0.77 us (2%)
    ppermute x13, starting transfers between devices, swap(): return lax.ppermute(piece, axes, [(i, i ^ distance) for i in range(size)])  18.7 us
    ppermute x13, waiting for transfers between devices, swap(): return lax.ppermute(piece, axes, [(i, i ^ distance) for i in range(size)])  14.5 us
    pallas_call x14, Pallas kernels, run(): pl.pallas_call(body, out_shape=out_shape, in_specs=in_specs or [spec] * l...  12.2 us
  transfers between devices with their start and end apart: 14, of which 8 were waited for; matrix products, arithmetic and copies ran while one was open for 0% of the time, Pallas kernels for 19%

profile of v22, /device:TPU:0, one launch (start us, length us, event | category | flops | bytes accessed | tf_op | source)
XLA Modules:
  0.0 47.6 jit_solution(4995099283777811753)
XLA Ops:
  0.6 0.0 copy-start.1
  0.6 0.0 copy-start.2
  0.7 0.0 copy-start.3
  0.7 0.0 copy-start
  0.7 0.2 pick.1.first
  0.8 0.7 %copy-done.1 = bf16[8,8,8,192]{3,2,1,0:T(8,128)(2,1)S(1)} copy-done((bf16[8,8,8,192]{3,2,1,0:T(8,128)(2,1)S(1)}, bf16[8,8,8,192]{3,2,1,0:T(8,128)(2,1)}, u32[]{:S(2)}) %copy-start.1) | copy-done | bytes 196632
  1.6 0.1 copy-done.2
  1.7 0.0 copy-done.3
  1.7 0.2 prepare.1
  1.9 0.1 across.1
  2.0 3.0 %collective-permute-start.3 = (bf16[864,128]{1,0:T(8,128)(2,1)S(1)}, bf16[864,128]{1,0:T(8,128)(2,1)S(1)}, u32[]{:S(2)}, u32[]{:S(2)}) collective-permute-start(bf16[864,128]{1,0:T(8,128)(2,1)S(1)} %across.1), channel_id=1, source_target_pairs={{0,1},{1,0},{2,3},{3,2},{4,5},{5,4},{6,7},{7,6},{8,9},{9,8},{10,11... | collective-permute-start | bytes 663560 | tf_op jit(solution)/shard_map/ppermute | solution.py:442
  5.0 0.1 pack.1.brick
  5.1 1.6 %collective-permute-start.2 = (bf16[768,128]{1,0:T(8,128)(2,1)S(1)}, bf16[768,128]{1,0:T(8,128)(2,1)S(1)}, u32[]{:S(2)}, u32[]{:S(2)}) collective-permute-start(bf16[768,128]{1,0:T(8,128)(2,1)S(1)} %pack.1.brick), channel_id=1, source_target_pairs={{0,4},{1,5},{2,6},{3,7},{4,0},{5,1},{6,2},{7,3},{8,12},{9,13},{10,... | collective-permute-start | bytes 589832 | tf_op jit(solution)/shard_map/ppermute | solution.py:442
  6.7 0.0 collective-permute-start
  6.7 0.7 %collective-permute-start.1 = (bf16[288,128]{1,0:T(8,128)(2,1)S(1)}, bf16[288,128]{1,0:T(8,128)(2,1)S(1)}, u32[]{:S(2)}, u32[]{:S(2)}) collective-permute-start(bf16[288,128]{1,0:T(8,128)(2,1)S(1)} %get-tuple-element.35), channel_id=1, source_target_pairs={{0,0},{2,4},{4,2},{6,8},{8,6},{10,12},{12,10},{14,16},{16,14},{18,... | collective-permute-start | bytes 221192 | tf_op jit(solution)/shard_map/ppermute | solution.py:468
  7.3 0.0 copy-done
  7.3 0.8 %turn.1.weight = bf16[5184,192]{1,0:T(8,128)(2,1)S(1)} custom-call(bf16[192,5184]{1,0:T(8,128)(2,1)S(1)} %bitcast.5), custom_call_target="tpu_custom_call" | custom-call | flops 1048576 | bytes 4194304 | tf_op jit(solution)/shard_map/turn/pallas_call | solution.py:413
  8.1 0.0 collective-permute-done.near
  8.1 0.0 collective-permute-done.1.far
  8.2 3.4 %collective-permute-done.2.beside = bf16[768,128]{1,0:T(8,128)(2,1)S(1)} collective-permute-done((bf16[768,128]{1,0:T(8,128)(2,1)S(1)}, bf16[768,128]{1,0:T(8,128)(2,1)S(1)}, u32[]{:S(2)}, u32[]{:S(2)}) %collective-permute-start.2) | collective-permute-done | bytes 196640 | tf_op jit(solution)/shard_map/ppermute | solution.py:442
  11.5 0.2 corner.1
  11.7 1.2 %collective-permute-start.4 = (bf16[128,128]{1,0:T(8,128)(2,1)S(1)}, bf16[128,128]{1,0:T(8,128)(2,1)S(1)}, u32[]{:S(2)}, u32[]{:S(2)}) collective-permute-start(bf16[128,128]{1,0:T(8,128)(2,1)S(1)} %corner.1), channel_id=1, source_target_pairs={{0,1},{1,0},{2,3},{3,2},{4,5},{5,4},{6,7},{7,6},{8,9},{9,8},{10,11... | collective-permute-start | bytes 98312 | tf_op jit(solution)/shard_map/ppermute | solution.py:442
  12.9 3.4 %collective-permute-start.6 = (bf16[768,128]{1,0:T(8,128)(2,1)S(1)}, bf16[768,128]{1,0:T(8,128)(2,1)S(1)}, u32[]{:S(2)}, u32[]{:S(2)}) collective-permute-start(bf16[768,128]{1,0:T(8,128)(2,1)S(1)} %pack.1.brick), channel_id=1, source_target_pairs={{0,5},{1,4},{2,7},{3,6},{4,1},{5,0},{6,3},{7,2},{8,13},{9,12},{10,... | collective-permute-start | bytes 589832 | tf_op jit(solution)/shard_map/ppermute | solution.py:442
  16.3 0.0 collective-permute-done.3.across
  16.3 2.8 %bulk.1 = f32[10,80,192]{2,1,0:T(8,128)S(1)} custom-call(bf16[8,64,192]{2,1,0:T(8,128)(2,1)S(1)} %get-tuple-element.33.masked, bf16[288,128]{1,0:T(8,128)(2,1)S(1)} %collective-permute-done.near, bf16[288,128]{1,0:T(8,128)(2,1)S(1)} %collective-permute-done.1.far, bf16[864,128]{1,0:T(8,128)(2,1)S(1)} %collective-permute-done.3.across, ...), custom_call_target="tpu_custom_call" | custom-call | flops 1610612736 | bytes 1048576 | tf_op jit(solution)/shard_map/bulk/pallas_call | solution.py:413
  19.1 0.0 collective-permute-done.4.corner
  19.1 1.1 %forward.1 = (bf16[8,64,192]{2,1,0:T(8,128)(2,1)S(1)}, bf16[10,80,192]{2,1,0:T(8,128)(2,1)S(1)}, bf16[48,640]{1,0:T(8,128)(2,1)S(1)}, bf16[48,640]{1,0:T(8,128)(...) custom-call(f32[10,80,192]{2,1,0:T(8,128)S(1)} %bulk.1, ...), custom_call_target="tpu_custom_call" | custom-call | flops 1610612736 | bytes 1048576 | tf_op jit(solution)/shard_map/forward/pallas_call | solution.py:413
  20.2 0.6 %collective-permute-start.5 = (bf16[48,640]{1,0:T(8,128)(2,1)S(1)}, bf16[48,640]{1,0:T(8,128)(2,1)S(1)}, u32[]{:S(2)}, u32[]{:S(2)}) collective-permute-start(bf16[48,640]{1,0:T(8,128)(2,1)S(1)} %get-tuple-element.46), channel_id=1, source_target_pairs={{0,1},{1,0},{2,3},{3,2},{4,5},{5,4},{6,7},{7,6},{8,9},{9,8},{10,11... | collective-permute-start | bytes 184328 | tf_op jit(solution)/shard_map/ppermute | solution.py:442
  20.8 4.7 %collective-permute-start.7 = (bf16[48,640]{1,0:T(8,128)(2,1)S(1)}, bf16[48,640]{1,0:T(8,128)(2,1)S(1)}, u32[]{:S(2)}, u32[]{:S(2)}) collective-permute-start(bf16[48,640]{1,0:T(8,128)(2,1)S(1)} %get-tuple-element.50), channel_id=1, source_target_pairs={{0,5},{1,4},{2,7},{3,6},{4,1},{5,0},{6,3},{7,2},{8,13},{9,12},{10,... | collective-permute-start | bytes 184328 | tf_op jit(solution)/shard_map/ppermute | solution.py:442
  25.5 0.0 collective-permute-start.8
  25.5 0.0 collective-permute-done.5.other
  25.5 0.0 collective-permute-done.6.beyond
  25.5 1.6 %first_pair.1 = (f32[48,5184]{1,0:T(8,128)S(1)}, bf16[8,128,192]{2,1,0:T(8,128)(2,1)S(1)}) custom-call(bf16[48,640]{1,0:T(8,128)(2,1)S(1)} %get-tuple-element.45.own, bf16[48,640]{1,0:T(8,128)(2,1)S(1)} %collective-permute-done.5.other, bf16[768,128]{1,0:T(8,128)(2,1)S(1)} %pack.1.brick, bf16[864,128]{1,0:T(8,128)(2,1)S(1)} %collective-permute-done.3.across, ...), custom_call_target="tpu_custom_call" | custom-call | flops 1073741824 | bytes 2097152 | tf_op jit(solution)/shard_map/first_pair/pallas_call | solution.py:413
  27.1 0.6 %collective-permute-done.7.other = bf16[48,640]{1,0:T(8,128)(2,1)S(1)} collective-permute-done((bf16[48,640]{1,0:T(8,128)(2,1)S(1)}, bf16[48,640]{1,0:T(8,128)(2,1)S(1)}, u32[]{:S(2)}, u32[]{:S(2)}) %collective-permute-start.7) | collective-permute-done | bytes 61472 | tf_op jit(solution)/shard_map/ppermute | solution.py:442
  27.7 2.0 %collective-permute-done.8.own = bf16[48,640]{1,0:T(8,128)(2,1)S(1)} collective-permute-done((bf16[48,640]{1,0:T(8,128)(2,1)S(1)}, bf16[48,640]{1,0:T(8,128)(2,1)S(1)}, u32[]{:S(2)}, u32[]{:S(2)}) %collective-permute-start.8) | collective-permute-done | bytes 61472 | tf_op jit(solution)/shard_map/ppermute | solution.py:442
  29.7 1.5 %second_pair.1 = (f32[24,5184]{1,0:T(8,128)S(1)}, bf16[24,5184]{1,0:T(8,128)(2,1)S(1)}) custom-call(f32[48,5184]{1,0:T(8,128)S(1)} %get-tuple-element.49.before, bf16[48,640]{1,0:T(8,128)(2,1)S(1)} %collective-permute-done.7.other, bf16[48,640]{1,0:T(8,128)(2,1)S(1)} %collective-permute-done.8.own, bf16[8,128,192]{2,1,0:T(8,128)(2,1)S(1)} %get-tuple-element.52.masked), custom_call_target="tpu_custom_call" | custom-call | flops 1073741824 | bytes 2097152 | tf_op jit(solution)/shard_map/second_pair/pallas_call | solution.py:413
  31.3 0.1 collective-permute-start.9
  31.4 1.5 %collective-permute-done.9.other = bf16[24,5184]{1,0:T(8,128)(2,1)S(1)} collective-permute-done((bf16[24,5184]{1,0:T(8,128)(2,1)S(1)}, bf16[24,5184]{1,0:T(8,128)(2,1)S(1)}, u32[]{:S(2)}, u32[]{:S(2)}) %collective-permute-start.9) | collective-permute-done | bytes 248864 | tf_op jit(solution)/shard_map/ppermute | solution.py:442
  32.9 0.2 fold.1
  33.1 2.7 %collective-permute-start.10 = (bf16[8,3968]{1,0:T(8,128)(2,1)S(1)}, bf16[8,3968]{1,0:T(8,128)(2,1)S(1)}, u32[]{:S(2)}, u32[]{:S(2)}) collective-permute-start(bf16[8,3968]{1,0:T(8,128)(2,1)S(1)} %get-tuple-element.55), channel_id=1, source_target_pairs={{0,16},{8,24},{16,0},{24,8},{1,17},{9,25},{17,1},{25,9},{2,18},{10... | collective-permute-start | bytes 190472 | tf_op jit(solution)/shard_map/ppermute | solution.py:442
  35.7 1.3 %collective-permute-start.11 = (bf16[8,3968]{1,0:T(8,128)(2,1)S(1)}, bf16[8,3968]{1,0:T(8,128)(2,1)S(1)}, u32[]{:S(2)}, u32[]{:S(2)}) collective-permute-start(bf16[8,3968]{1,0:T(8,128)(2,1)S(1)} %get-tuple-element.56), channel_id=1, source_target_pairs={{0,24},{8,16},{16,8},{24,0},{1,25},{9,17},{17,9},{25,1},{2,26},{10... | collective-permute-start | bytes 190472 | tf_op jit(solution)/shard_map/ppermute | solution.py:442
  37.1 0.0 collective-permute-start.12
  37.1 2.6 %input_gradient.1 = (bf16[8,64,192]{2,1,0:T(8,128)(2,1)}, bf16[8,64,192]{2,1,0:T(8,128)(2,1)}) custom-call(bf16[10,80,192]{2,1,0:T(8,128)(2,1)S(1)} %get-tuple-element.41.gp, f32[8,64,128]{2,1,0:T(8,128)S(1)} %get-tuple-element.40.live, bf16[192,5184]{1,0:T(8,128)(2,1)S(1)} %bitcast.6, bf16[8,64,192]{2,1,0:T(8,128)(2,1)S(1)} %get-tuple-element.42.act), custom_call_target="tpu_custom_call" | custom-call | flops 1358954496 | bytes 4194304 | tf_op jit(solution)/shard_map/input_gradient/pallas_call | solution.py:413
  39.7 1.2 %collective-permute-done.10.one = bf16[8,3968]{1,0:T(8,128)(2,1)S(1)} collective-permute-done((bf16[8,3968]{1,0:T(8,128)(2,1)S(1)}, bf16[8,3968]{1,0:T(8,128)(2,1)S(1)}, u32[]{:S(2)}, u32[]{:S(2)}) %collective-permute-start.10) | collective-permute-done | bytes 63520 | tf_op jit(solution)/shard_map/ppermute | solution.py:442
  40.9 1.2 %collective-permute-done.11.two = bf16[8,3968]{1,0:T(8,128)(2,1)S(1)} collective-permute-done((bf16[8,3968]{1,0:T(8,128)(2,1)S(1)}, bf16[8,3968]{1,0:T(8,128)(2,1)S(1)}, u32[]{:S(2)}, u32[]{:S(2)}) %collective-permute-start.11) | collective-permute-done | bytes 63520 | tf_op jit(solution)/shard_map/ppermute | solution.py:442
  42.1 0.4 collective-permute-done.12.three
  42.5 0.1 collective-permute-start.13
  42.7 4.2 %collective-permute-done.13.other = bf16[8,3968]{1,0:T(8,128)(2,1)S(1)} collective-permute-done((bf16[8,3968]{1,0:T(8,128)(2,1)S(1)}, bf16[8,3968]{1,0:T(8,128)(2,1)S(1)}, u32[]{:S(2)}, u32[]{:S(2)}) %collective-permute-start.13) | collective-permute-done | bytes 63520 | tf_op jit(solution)/shard_map/ppermute | solution.py:442
  46.8 0.8 %join.1 = f32[12,5184]{1,0:T(8,128)} custom-call(bf16[8,3968]{1,0:T(8,128)(2,1)S(1)} %plane_sum.1.mine, bf16[8,3968]{1,0:T(8,128)(2,1)S(1)} %collective-permute-done.13.other), custom_call_target="tpu_custom_call" | custom-call | flops 41472 | bytes 580608 | tf_op jit(solution)/shard_map/join/pallas_call | solution.py:413
  (1 shorter events, 0.0 us)
Async XLA Ops:
  0.6 1.0 %copy-start.1 = (bf16[8,8,8,192]{3,2,1,0:T(8,128)(2,1)S(1)}, bf16[8,8,8,192]{3,2,1,0:T(8,128)(2,1)}, u32[]{:S(2)}) copy-start(bf16[8,8,8,192]{3,2,1,0:T(8,128)(2,1)} %param.4) | copy-start | bytes 589828
  0.6 1.0 %copy-start.2 = (bf16[8,8,8,192]{3,2,1,0:T(8,128)(2,1)S(1)}, bf16[8,8,8,192]{3,2,1,0:T(8,128)(2,1)}, u32[]{:S(2)}) copy-start(bf16[8,8,8,192]{3,2,1,0:T(8,128)(2,1)} %param.7) | copy-start | bytes 589828
  0.7 1.0 %copy-start.3 = (s32[8,8,8]{2,1,0:T(8,128)S(1)}, s32[8,8,8]{2,1,0:T(8,128)}, u32[]{:S(2)}) copy-start(s32[8,8,8]{2,1,0:T(8,128)} %mask.1) | copy-start | bytes 6148
  0.7 6.7 %copy-start = (bf16[5184,192]{0,1:T(8,128)(2,1)S(1)}, bf16[5184,192]{0,1:T(8,128)(2,1)}, u32[]{:S(2)}) copy-start(bf16[5184,192]{0,1:T(8,128)(2,1)} %param.5) | copy-start | bytes 5971972
  2.0 14.3 %collective-permute-start.3 = (bf16[864,128]{1,0:T(8,128)(2,1)S(1)}, bf16[864,128]{1,0:T(8,128)(2,1)S(1)}, u32[]{:S(2)}, u32[]{:S(2)}) collective-permute-start(bf16[864,128]{1,0:T(8,128)(2,1)S(1)} %across.1), channel_id=1, source_target_pairs={{0,1},{1,0},{2,3},{3,2},{4,5},{5,4},{6,7},{7,6},{8,9},{9,8},{10,11... | collective-permute-start | bytes 663560 | tf_op jit(solution)/shard_map/ppermute | solution.py:442
  5.1 6.4 %collective-permute-start.2 = (bf16[768,128]{1,0:T(8,128)(2,1)S(1)}, bf16[768,128]{1,0:T(8,128)(2,1)S(1)}, u32[]{:S(2)}, u32[]{:S(2)}) collective-permute-start(bf16[768,128]{1,0:T(8,128)(2,1)S(1)} %pack.1.brick), channel_id=1, source_target_pairs={{0,4},{1,5},{2,6},{3,7},{4,0},{5,1},{6,2},{7,3},{8,12},{9,13},{10,... | collective-permute-start | bytes 589832 | tf_op jit(solution)/shard_map/ppermute | solution.py:442
  6.7 1.5 %collective-permute-start = (bf16[288,128]{1,0:T(8,128)(2,1)S(1)}, bf16[288,128]{1,0:T(8,128)(2,1)S(1)}, u32[]{:S(2)}, u32[]{:S(2)}) collective-permute-start(bf16[288,128]{1,0:T(8,128)(2,1)S(1)} %get-tuple-element.34), channel_id=1, source_target_pairs={{0,2},{2,0},{4,6},{6,4},{8,10},{10,8},{12,14},{14,12},{16,18},{18,... | collective-permute-start | bytes 221192 | tf_op jit(solution)/shard_map/ppermute | solution.py:442
  6.7 1.5 %collective-permute-start.1 = (bf16[288,128]{1,0:T(8,128)(2,1)S(1)}, bf16[288,128]{1,0:T(8,128)(2,1)S(1)}, u32[]{:S(2)}, u32[]{:S(2)}) collective-permute-start(bf16[288,128]{1,0:T(8,128)(2,1)S(1)} %get-tuple-element.35), channel_id=1, source_target_pairs={{0,0},{2,4},{4,2},{6,8},{8,6},{10,12},{12,10},{14,16},{16,14},{18,... | collective-permute-start | bytes 221192 | tf_op jit(solution)/shard_map/ppermute | solution.py:468
  11.7 7.4 %collective-permute-start.4 = (bf16[128,128]{1,0:T(8,128)(2,1)S(1)}, bf16[128,128]{1,0:T(8,128)(2,1)S(1)}, u32[]{:S(2)}, u32[]{:S(2)}) collective-permute-start(bf16[128,128]{1,0:T(8,128)(2,1)S(1)} %corner.1), channel_id=1, source_target_pairs={{0,1},{1,0},{2,3},{3,2},{4,5},{5,4},{6,7},{7,6},{8,9},{9,8},{10,11... | collective-permute-start | bytes 98312 | tf_op jit(solution)/shard_map/ppermute | solution.py:442
  12.9 12.6 %collective-permute-start.6 = (bf16[768,128]{1,0:T(8,128)(2,1)S(1)}, bf16[768,128]{1,0:T(8,128)(2,1)S(1)}, u32[]{:S(2)}, u32[]{:S(2)}) collective-permute-start(bf16[768,128]{1,0:T(8,128)(2,1)S(1)} %pack.1.brick), channel_id=1, source_target_pairs={{0,5},{1,4},{2,7},{3,6},{4,1},{5,0},{6,3},{7,2},{8,13},{9,12},{10,... | collective-permute-start | bytes 589832 | tf_op jit(solution)/shard_map/ppermute | solution.py:442
  20.2 5.3 %collective-permute-start.5 = (bf16[48,640]{1,0:T(8,128)(2,1)S(1)}, bf16[48,640]{1,0:T(8,128)(2,1)S(1)}, u32[]{:S(2)}, u32[]{:S(2)}) collective-permute-start(bf16[48,640]{1,0:T(8,128)(2,1)S(1)} %get-tuple-element.46), channel_id=1, source_target_pairs={{0,1},{1,0},{2,3},{3,2},{4,5},{5,4},{6,7},{7,6},{8,9},{9,8},{10,11... | collective-permute-start | bytes 184328 | tf_op jit(solution)/shard_map/ppermute | solution.py:442
  20.8 6.9 %collective-permute-start.7 = (bf16[48,640]{1,0:T(8,128)(2,1)S(1)}, bf16[48,640]{1,0:T(8,128)(2,1)S(1)}, u32[]{:S(2)}, u32[]{:S(2)}) collective-permute-start(bf16[48,640]{1,0:T(8,128)(2,1)S(1)} %get-tuple-element.50), channel_id=1, source_target_pairs={{0,5},{1,4},{2,7},{3,6},{4,1},{5,0},{6,3},{7,2},{8,13},{9,12},{10,... | collective-permute-start | bytes 184328 | tf_op jit(solution)/shard_map/ppermute | solution.py:442
  25.5 4.2 %collective-permute-start.8 = (bf16[48,640]{1,0:T(8,128)(2,1)S(1)}, bf16[48,640]{1,0:T(8,128)(2,1)S(1)}, u32[]{:S(2)}, u32[]{:S(2)}) collective-permute-start(bf16[48,640]{1,0:T(8,128)(2,1)S(1)} %get-tuple-element.51), channel_id=1, source_target_pairs={{0,4},{1,5},{2,6},{3,7},{4,0},{5,1},{6,2},{7,3},{8,12},{9,13},{10,... | collective-permute-start | bytes 184328 | tf_op jit(solution)/shard_map/ppermute | solution.py:442
  31.3 1.6 %collective-permute-start.9 = (bf16[24,5184]{1,0:T(8,128)(2,1)S(1)}, bf16[24,5184]{1,0:T(8,128)(2,1)S(1)}, u32[]{:S(2)}, u32[]{:S(2)}) collective-permute-start(bf16[24,5184]{1,0:T(8,128)(2,1)S(1)} %get-tuple-element.54), channel_id=1, source_target_pairs={{0,2},{1,3},{2,0},{3,1},{4,6},{5,7},{6,4},{7,5},{8,10},{9,11},{10,... | collective-permute-start | bytes 746504 | tf_op jit(solution)/shard_map/ppermute | solution.py:442
  33.1 7.9 %collective-permute-start.10 = (bf16[8,3968]{1,0:T(8,128)(2,1)S(1)}, bf16[8,3968]{1,0:T(8,128)(2,1)S(1)}, u32[]{:S(2)}, u32[]{:S(2)}) collective-permute-start(bf16[8,3968]{1,0:T(8,128)(2,1)S(1)} %get-tuple-element.55), channel_id=1, source_target_pairs={{0,16},{8,24},{16,0},{24,8},{1,17},{9,25},{17,1},{25,9},{2,18},{10... | collective-permute-start | bytes 190472 | tf_op jit(solution)/shard_map/ppermute | solution.py:442
  35.7 6.3 %collective-permute-start.11 = (bf16[8,3968]{1,0:T(8,128)(2,1)S(1)}, bf16[8,3968]{1,0:T(8,128)(2,1)S(1)}, u32[]{:S(2)}, u32[]{:S(2)}) collective-permute-start(bf16[8,3968]{1,0:T(8,128)(2,1)S(1)} %get-tuple-element.56), channel_id=1, source_target_pairs={{0,24},{8,16},{16,8},{24,0},{1,25},{9,17},{17,9},{25,1},{2,26},{10... | collective-permute-start | bytes 190472 | tf_op jit(solution)/shard_map/ppermute | solution.py:442
  37.1 5.4 %collective-permute-start.12 = (bf16[8,3968]{1,0:T(8,128)(2,1)S(1)}, bf16[8,3968]{1,0:T(8,128)(2,1)S(1)}, u32[]{:S(2)}, u32[]{:S(2)}) collective-permute-start(bf16[8,3968]{1,0:T(8,128)(2,1)S(1)} %get-tuple-element.57), channel_id=1, source_target_pairs={{0,8},{8,0},{16,24},{24,16},{1,9},{9,1},{17,25},{25,17},{2,10},{10... | collective-permute-start | bytes 190472 | tf_op jit(solution)/shard_map/ppermute | solution.py:442
  42.5 4.3 %collective-permute-start.13 = (bf16[8,3968]{1,0:T(8,128)(2,1)S(1)}, bf16[8,3968]{1,0:T(8,128)(2,1)S(1)}, u32[]{:S(2)}, u32[]{:S(2)}) collective-permute-start(bf16[8,3968]{1,0:T(8,128)(2,1)S(1)} %plane_sum.1.mine), channel_id=1, source_target_pairs={{0,1},{1,0},{2,3},{3,2},{4,5},{5,4},{6,7},{7,6},{8,9},{9,8},{10,11... | collective-permute-start | bytes 190472 | tf_op jit(solution)/shard_map/ppermute | solution.py:442

commit v23 on v21

--- a/solution.py
+++ b/solution.py
@@ -320,14 +320,14 @@
 
 def pair_product(received, masked, cols):
     f32 = jnp.float32
-    group, lanes = received[0].shape
+    group = received[0].shape[0]
     per, lane, channels = masked.shape
     half = lane // 2
     side = position()[3]
     at = lax.broadcasted_iota(jnp.int32, (group, lane), 1)
     y, z = at // DEPTH, at % DEPTH
     tall = lane // DEPTH
-    own, other = (ref[...].astype(f32) for ref in received)
+    own, other = received
     first = jnp.where(side == 0, own, other)
     second = jnp.where(side == 0, other, own)
     for k in range(per + 2):
@@ -357,20 +357,23 @@
 def first_pair_kernel(own, other, brick, across, beside, beyond, part_ref, next_ref, cols, masked):
     unpack_pair((beside, beyond), next_ref)
     unpack_pair((brick, across), masked)
-    for a, rows in pair_product((own, other), masked, cols):
+    received = own[...].astype(jnp.float32), other[...].astype(jnp.float32)
+    for a, rows in pair_product(received, masked, cols):
         width = rows.shape[1]
         part_ref[:, a * width : (a + 1) * width] = rows
 
 
-def second_pair_kernel(before, other, own, masked, keep_ref, send_ref, part, cols):
-    for a, rows in pair_product((own, other), masked, cols):
+def second_pair_kernel(own_rows, before, other, own, masked, out_ref, cols):
+    core = lax.rem(position()[2], 2)
+    half = before.shape[0] // 2
+    upper = core if own_rows else 1 - core
+    received = [ref[...].astype(jnp.float32) for ref in (own, other)]
+    received = [jnp.where(upper == 1, block[half:], block[:half]) for block in received]
+    held = pl.ds(pl.multiple_of(upper * half, 8), half)
+    for a, rows in pair_product(received, masked, cols):
         width = rows.shape[1]
         at = slice(a * width, (a + 1) * width)
-        part[:, at] = before[:, at] + rows
-    core = lax.rem(position()[2], 2)
-    half = part.shape[0] // 2
-    keep_ref[...] = part[pl.ds(pl.multiple_of(core * half, 8), half)]
-    send_ref[...] = part[pl.ds(pl.multiple_of((1 - core) * half, 8), half)].astype(jnp.bfloat16)
+        out_ref[:, at] = (before[held, at] + rows).astype(out_ref.dtype)
 
 
 def fold_kernel(keep, other, own_ref, *refs):
@@ -528,11 +531,16 @@
         (array((2 * group, total), f32), array(pair, bf16)),
         (cols, pltpu.VMEM(pair, bf16)),
     )(*slices[:2], *bricks)
-    keep, fold = call(
-        second_pair_kernel, "second_pair", 16, 1 << 30, 2 << 20,
-        (array((group, total), f32), array((group, total), bf16)),
-        (pltpu.VMEM((2 * group, total), f32), cols),
-    )(part, *slices[3:1:-1], pair_masked)
+    half_cols = pltpu.VMEM((9 * group, (width + 2) * SIDES * rows), bf16)
+    second = part, *slices[3:1:-1], pair_masked
+    fold = call(
+        functools.partial(second_pair_kernel, False), "second_pair_other", 16, 1 << 29, 1 << 20,
+        array((group, total), bf16), (half_cols,),
+    )(*second)
+    keep = call(
+        functools.partial(second_pair_kernel, True), "second_pair_own", 16, 1 << 29, 1 << 20,
+        array((group, total), f32), (half_cols,),
+    )(*second)
     own, *sends = call(
         fold_kernel, "fold", 8, 8 * total * 4, 8 * total * 40,
         (array((8, lanes), f32),) + (array((8, lanes), bf16),) * (planes - 1),

time: 43.2 us -> 42.6 us (0.986)
  waiting for transfers between devices: 10.2 us -> 9.23 us
    ppermute x13, waiting for transfers between devices: 10.2 us -> 9.23 us  [swap(): return lax.ppermute(piece, axes, [(i, i ^ distance) for i in range(size)])]
    pallas_call x14 -> x15, Pallas kernels: 12.2 us -> 12.6 us  [run(): pl.pallas_call(body, out_shape=out_shape, in_specs=in_specs or [spec] * l...]
  transfers between devices with their start and end apart: 14 -> 14, of which waited for: 6 -> 6; matrix products, arithmetic and copies ran while one was open for 0% -> 0% of each run, Pallas kernels for 21% -> 24%
where the time goes in v23:
time: 42.6 us; the launch traced here: 42.5 us
  starting transfers between devices  19 us (45%)
  Pallas kernels  12.6 us (30%)
  waiting for transfers between devices  9.23 us (22%)
  local copies, waits for them, and re-layouts  0.84 us (2%)
  between operations  0.78 us (2%)
    ppermute x13, starting transfers between devices, swap(): return lax.ppermute(piece, axes, [(i, i ^ distance) for i in range(size)])  18.4 us
    pallas_call x15, Pallas kernels, run(): pl.pallas_call(body, out_shape=out_shape, in_specs=in_specs or [spec] * l...  12.6 us
    ppermute x13, waiting for transfers between devices, swap(): return lax.ppermute(piece, axes, [(i, i ^ distance) for i in range(size)])  9.23 us
  transfers between devices with their start and end apart: 14, of which 6 were waited for; matrix products, arithmetic and copies ran while one was open for 0% of the time, Pallas kernels for 24%

profile of v23, /device:TPU:0, one launch (start us, length us, event | category | flops | bytes accessed | tf_op | source)
XLA Modules:
  0.0 42.5 jit_solution(11226534744434037249)
XLA Ops:
  0.6 0.0 copy-start.1
  0.6 0.0 copy-start.2
  0.7 0.0 copy-start.3
  0.7 0.0 copy-start
  0.7 0.2 pick.1.first
  0.8 0.7 %copy-done.1 = bf16[8,8,8,192]{3,2,1,0:T(8,128)(2,1)S(1)} copy-done((bf16[8,8,8,192]{3,2,1,0:T(8,128)(2,1)S(1)}, bf16[8,8,8,192]{3,2,1,0:T(8,128)(2,1)}, u32[]{:S(2)}) %copy-start.1) | copy-done | bytes 196632
  1.6 0.1 copy-done.2
  1.7 0.0 copy-done.3
  1.7 0.2 prepare.1
  1.9 0.1 across.1
  2.0 3.0 %collective-permute-start.2 = (bf16[864,128]{1,0:T(8,128)(2,1)S(1)}, bf16[864,128]{1,0:T(8,128)(2,1)S(1)}, u32[]{:S(2)}, u32[]{:S(2)}) collective-permute-start(bf16[864,128]{1,0:T(8,128)(2,1)S(1)} %across.1), channel_id=1, source_target_pairs={{0,1},{1,0},{2,3},{3,2},{4,5},{5,4},{6,7},{7,6},{8,9},{9,8},{10,11... | collective-permute-start | bytes 663560 | tf_op jit(solution)/shard_map/ppermute | solution.py:445
  5.0 0.0 collective-permute-start
  5.0 0.7 %collective-permute-start.1 = (bf16[288,128]{1,0:T(8,128)(2,1)S(1)}, bf16[288,128]{1,0:T(8,128)(2,1)S(1)}, u32[]{:S(2)}, u32[]{:S(2)}) collective-permute-start(bf16[288,128]{1,0:T(8,128)(2,1)S(1)} %get-tuple-element.37), channel_id=1, source_target_pairs={{0,0},{2,4},{4,2},{6,8},{8,6},{10,12},{12,10},{14,16},{16,14},{18,... | collective-permute-start | bytes 221192 | tf_op jit(solution)/shard_map/ppermute | solution.py:471
  5.7 0.0 copy-done
  5.7 0.8 %turn.1.after.weight = bf16[5184,192]{1,0:T(8,128)(2,1)S(1)} custom-call(bf16[192,5184]{1,0:T(8,128)(2,1)S(1)} %bitcast.5), custom_call_target="tpu_custom_call" | custom-call | flops 1048576 | bytes 4194304 | tf_op jit(solution)/shard_map/turn/pallas_call | solution.py:416
  6.5 0.1 pack.1.brick
  6.6 3.4 %collective-permute-start.4 = (bf16[768,128]{1,0:T(8,128)(2,1)S(1)}, bf16[768,128]{1,0:T(8,128)(2,1)S(1)}, u32[]{:S(2)}, u32[]{:S(2)}) collective-permute-start(bf16[768,128]{1,0:T(8,128)(2,1)S(1)} %pack.1.brick), channel_id=1, source_target_pairs={{0,4},{1,5},{2,6},{3,7},{4,0},{5,1},{6,2},{7,3},{8,12},{9,13},{10,... | collective-permute-start | bytes 589832 | tf_op jit(solution)/shard_map/ppermute | solution.py:445
  10.0 0.0 collective-permute-done.near
  10.0 0.0 collective-permute-done.1.far
  10.0 0.2 corner.1
  10.2 0.1 collective-permute-start.3
  10.3 3.5 %collective-permute-start.6 = (bf16[768,128]{1,0:T(8,128)(2,1)S(1)}, bf16[768,128]{1,0:T(8,128)(2,1)S(1)}, u32[]{:S(2)}, u32[]{:S(2)}) collective-permute-start(bf16[768,128]{1,0:T(8,128)(2,1)S(1)} %pack.1.brick), channel_id=1, source_target_pairs={{0,5},{1,4},{2,7},{3,6},{4,1},{5,0},{6,3},{7,2},{8,13},{9,12},{10,... | collective-permute-start | bytes 589832 | tf_op jit(solution)/shard_map/ppermute | solution.py:445
  13.9 0.0 collective-permute-done.2.across
  13.9 2.8 %bulk.1 = f32[10,80,192]{2,1,0:T(8,128)S(1)} custom-call(bf16[8,64,192]{2,1,0:T(8,128)(2,1)S(1)} %get-tuple-element.35.masked, bf16[288,128]{1,0:T(8,128)(2,1)S(1)} %collective-permute-done.near, bf16[288,128]{1,0:T(8,128)(2,1)S(1)} %collective-permute-done.1.far, bf16[864,128]{1,0:T(8,128)(2,1)S(1)} %collective-permute-done.2.across, ...), custom_call_target="tpu_custom_call" | custom-call | flops 1610612736 | bytes 1048576 | tf_op jit(solution)/shard_map/bulk/pallas_call | solution.py:416
  16.7 0.0 collective-permute-done.3.corner
  16.7 1.1 %forward.1 = (bf16[8,64,192]{2,1,0:T(8,128)(2,1)S(1)}, bf16[10,80,192]{2,1,0:T(8,128)(2,1)S(1)}, bf16[48,640]{1,0:T(8,128)(2,1)S(1)}, bf16[48,640]{1,0:T(8,128)(...) custom-call(f32[10,80,192]{2,1,0:T(8,128)S(1)} %bulk.1, ...), custom_call_target="tpu_custom_call" | custom-call | flops 1610612736 | bytes 1048576 | tf_op jit(solution)/shard_map/forward/pallas_call | solution.py:416
  17.8 0.0 collective-permute-done.4.beside
  17.8 0.6 %collective-permute-start.5 = (bf16[48,640]{1,0:T(8,128)(2,1)S(1)}, bf16[48,640]{1,0:T(8,128)(2,1)S(1)}, u32[]{:S(2)}, u32[]{:S(2)}) collective-permute-start(bf16[48,640]{1,0:T(8,128)(2,1)S(1)} %get-tuple-element.52), channel_id=1, source_target_pairs={{0,1},{1,0},{2,3},{3,2},{4,5},{5,4},{6,7},{7,6},{8,9},{9,8},{10,11... | collective-permute-start | bytes 184328 | tf_op jit(solution)/shard_map/ppermute | solution.py:445
  18.4 1.1 %collective-permute-start.7 = (bf16[48,640]{1,0:T(8,128)(2,1)S(1)}, bf16[48,640]{1,0:T(8,128)(2,1)S(1)}, u32[]{:S(2)}, u32[]{:S(2)}) collective-permute-start(bf16[48,640]{1,0:T(8,128)(2,1)S(1)} %get-tuple-element.56), channel_id=1, source_target_pairs={{0,5},{1,4},{2,7},{3,6},{4,1},{5,0},{6,3},{7,2},{8,13},{9,12},{10,... | collective-permute-start | bytes 184328 | tf_op jit(solution)/shard_map/ppermute | solution.py:445
  19.5 1.9 %collective-permute-start.8 = (bf16[48,640]{1,0:T(8,128)(2,1)S(1)}, bf16[48,640]{1,0:T(8,128)(2,1)S(1)}, u32[]{:S(2)}, u32[]{:S(2)}) collective-permute-start(bf16[48,640]{1,0:T(8,128)(2,1)S(1)} %get-tuple-element.57), channel_id=1, source_target_pairs={{0,4},{1,5},{2,6},{3,7},{4,0},{5,1},{6,2},{7,3},{8,12},{9,13},{10,... | collective-permute-start | bytes 184328 | tf_op jit(solution)/shard_map/ppermute | solution.py:445
  21.4 0.0 collective-permute-done.6.beyond
  21.4 2.4 %collective-permute-done.5.other = bf16[48,640]{1,0:T(8,128)(2,1)S(1)} collective-permute-done((bf16[48,640]{1,0:T(8,128)(2,1)S(1)}, bf16[48,640]{1,0:T(8,128)(2,1)S(1)}, u32[]{:S(2)}, u32[]{:S(2)}) %collective-permute-start.5) | collective-permute-done | bytes 61472 | tf_op jit(solution)/shard_map/ppermute | solution.py:445
  23.7 1.6 %first_pair.1 = (f32[48,5184]{1,0:T(8,128)S(1)}, bf16[8,128,192]{2,1,0:T(8,128)(2,1)S(1)}) custom-call(bf16[48,640]{1,0:T(8,128)(2,1)S(1)} %get-tuple-element.51.own, bf16[48,640]{1,0:T(8,128)(2,1)S(1)} %collective-permute-done.5.other, bf16[768,128]{1,0:T(8,128)(2,1)S(1)} %pack.1.brick, bf16[864,128]{1,0:T(8,128)(2,1)S(1)} %collective-permute-done.2.across, ...), custom_call_target="tpu_custom_call" | custom-call | flops 1073741824 | bytes 2097152 | tf_op jit(solution)/shard_map/first_pair/pallas_call | solution.py:416
  25.3 0.0 collective-permute-done.7.other
  25.3 0.0 collective-permute-done.8.own
  25.3 1.0 %second_pair_other.1 = bf16[24,5184]{1,0:T(8,128)(2,1)S(1)} custom-call(f32[48,5184]{1,0:T(8,128)S(1)} %get-tuple-element.55.before, bf16[48,640]{1,0:T(8,128)(2,1)S(1)} %collective-permute-done.7.other, bf16[48,640]{1,0:T(8,128)(2,1)S(1)} %collective-permute-done.8.own, bf16[8,128,192]{2,1,0:T(8,128)(2,1)S(1)} %get-tuple-element.58.masked), custom_call_target="tpu_custom_call" | custom-call | flops 536870912 | bytes 1048576 | tf_op jit(solution)/shard_map/second_pair_other/pallas_call | solution.py:416
  26.3 0.1 collective-permute-start.9
  26.4 1.0 %second_pair_own.1.keep = f32[24,5184]{1,0:T(8,128)S(1)} custom-call(f32[48,5184]{1,0:T(8,128)S(1)} %get-tuple-element.55.before, bf16[48,640]{1,0:T(8,128)(2,1)S(1)} %collective-permute-done.7.other, bf16[48,640]{1,0:T(8,128)(2,1)S(1)} %collective-permute-done.8.own, bf16[8,128,192]{2,1,0:T(8,128)(2,1)S(1)} %get-tuple-element.58.masked), custom_call_target="tpu_custom_call" | custom-call | flops 536870912 | bytes 1048576 | tf_op jit(solution)/shard_map/second_pair_own/pallas_call | solution.py:416
  27.4 0.5 %collective-permute-done.9.other = bf16[24,5184]{1,0:T(8,128)(2,1)S(1)} collective-permute-done((bf16[24,5184]{1,0:T(8,128)(2,1)S(1)}, bf16[24,5184]{1,0:T(8,128)(2,1)S(1)}, u32[]{:S(2)}, u32[]{:S(2)}) %collective-permute-start.9) | collective-permute-done | bytes 248864 | tf_op jit(solution)/shard_map/ppermute | solution.py:445
  27.9 0.2 fold.1
  28.1 2.7 %collective-permute-start.10 = (bf16[8,3968]{1,0:T(8,128)(2,1)S(1)}, bf16[8,3968]{1,0:T(8,128)(2,1)S(1)}, u32[]{:S(2)}, u32[]{:S(2)}) collective-permute-start(bf16[8,3968]{1,0:T(8,128)(2,1)S(1)} %get-tuple-element.59), channel_id=1, source_target_pairs={{0,16},{8,24},{16,0},{24,8},{1,17},{9,25},{17,1},{25,9},{2,18},{10... | collective-permute-start | bytes 190472 | tf_op jit(solution)/shard_map/ppermute | solution.py:445
  30.8 1.4 %collective-permute-start.11 = (bf16[8,3968]{1,0:T(8,128)(2,1)S(1)}, bf16[8,3968]{1,0:T(8,128)(2,1)S(1)}, u32[]{:S(2)}, u32[]{:S(2)}) collective-permute-start(bf16[8,3968]{1,0:T(8,128)(2,1)S(1)} %get-tuple-element.60), channel_id=1, source_target_pairs={{0,24},{8,16},{16,8},{24,0},{1,25},{9,17},{17,9},{25,1},{2,26},{10... | collective-permute-start | bytes 190472 | tf_op jit(solution)/shard_map/ppermute | solution.py:445
  32.2 0.0 collective-permute-start.12
  32.2 2.6 %input_gradient.1 = (bf16[8,64,192]{2,1,0:T(8,128)(2,1)}, bf16[8,64,192]{2,1,0:T(8,128)(2,1)}) custom-call(bf16[10,80,192]{2,1,0:T(8,128)(2,1)S(1)} %get-tuple-element.43.gp, f32[8,64,128]{2,1,0:T(8,128)S(1)} %get-tuple-element.42.live, bf16[192,5184]{1,0:T(8,128)(2,1)S(1)} %bitcast.6, bf16[8,64,192]{2,1,0:T(8,128)(2,1)S(1)} %get-tuple-element.44.act), custom_call_target="tpu_custom_call" | custom-call | flops 1358954496 | bytes 4194304 | tf_op jit(solution)/shard_map/input_gradient/pallas_call | solution.py:416
  34.8 0.1 collective-permute-done.10.one
  34.9 2.3 %collective-permute-done.11.two = bf16[8,3968]{1,0:T(8,128)(2,1)S(1)} collective-permute-done((bf16[8,3968]{1,0:T(8,128)(2,1)S(1)}, bf16[8,3968]{1,0:T(8,128)(2,1)S(1)}, u32[]{:S(2)}, u32[]{:S(2)}) %collective-permute-start.11) | collective-permute-done | bytes 63520 | tf_op jit(solution)/shard_map/ppermute | solution.py:445
  37.2 0.2 collective-permute-done.12.three
  37.4 0.5 %collective-permute-start.13 = (bf16[8,3968]{1,0:T(8,128)(2,1)S(1)}, bf16[8,3968]{1,0:T(8,128)(2,1)S(1)}, u32[]{:S(2)}, u32[]{:S(2)}) collective-permute-start(bf16[8,3968]{1,0:T(8,128)(2,1)S(1)} %plane_sum.1.mine), channel_id=1, source_target_pairs={{0,1},{1,0},{2,3},{3,2},{4,5},{5,4},{6,7},{7,6},{8,9},{9,8},{10,11... | collective-permute-start | bytes 190472 | tf_op jit(solution)/shard_map/ppermute | solution.py:445
  37.9 3.8 %collective-permute-done.13.other = bf16[8,3968]{1,0:T(8,128)(2,1)S(1)} collective-permute-done((bf16[8,3968]{1,0:T(8,128)(2,1)S(1)}, bf16[8,3968]{1,0:T(8,128)(2,1)S(1)}, u32[]{:S(2)}, u32[]{:S(2)}) %collective-permute-start.13) | collective-permute-done | bytes 63520 | tf_op jit(solution)/shard_map/ppermute | solution.py:445
  41.7 0.8 %join.1 = f32[12,5184]{1,0:T(8,128)} custom-call(bf16[8,3968]{1,0:T(8,128)(2,1)S(1)} %plane_sum.1.mine, bf16[8,3968]{1,0:T(8,128)(2,1)S(1)} %collective-permute-done.13.other), custom_call_target="tpu_custom_call" | custom-call | flops 41472 | bytes 580608 | tf_op jit(solution)/shard_map/join/pallas_call | solution.py:416
  (1 shorter events, 0.0 us)
Async XLA Ops:
  0.6 1.0 %copy-start.1 = (bf16[8,8,8,192]{3,2,1,0:T(8,128)(2,1)S(1)}, bf16[8,8,8,192]{3,2,1,0:T(8,128)(2,1)}, u32[]{:S(2)}) copy-start(bf16[8,8,8,192]{3,2,1,0:T(8,128)(2,1)} %param.4) | copy-start | bytes 589828
  0.6 1.0 %copy-start.2 = (bf16[8,8,8,192]{3,2,1,0:T(8,128)(2,1)S(1)}, bf16[8,8,8,192]{3,2,1,0:T(8,128)(2,1)}, u32[]{:S(2)}) copy-start(bf16[8,8,8,192]{3,2,1,0:T(8,128)(2,1)} %param.7) | copy-start | bytes 589828
  0.7 1.0 %copy-start.3 = (s32[8,8,8]{2,1,0:T(8,128)S(1)}, s32[8,8,8]{2,1,0:T(8,128)}, u32[]{:S(2)}) copy-start(s32[8,8,8]{2,1,0:T(8,128)} %mask.1) | copy-start | bytes 6148
  0.7 5.0 %copy-start = (bf16[5184,192]{0,1:T(8,128)(2,1)S(1)}, bf16[5184,192]{0,1:T(8,128)(2,1)}, u32[]{:S(2)}) copy-start(bf16[5184,192]{0,1:T(8,128)(2,1)} %param.5) | copy-start | bytes 5971972
  2.0 11.9 %collective-permute-start.2 = (bf16[864,128]{1,0:T(8,128)(2,1)S(1)}, bf16[864,128]{1,0:T(8,128)(2,1)S(1)}, u32[]{:S(2)}, u32[]{:S(2)}) collective-permute-start(bf16[864,128]{1,0:T(8,128)(2,1)S(1)} %across.1), channel_id=1, source_target_pairs={{0,1},{1,0},{2,3},{3,2},{4,5},{5,4},{6,7},{7,6},{8,9},{9,8},{10,11... | collective-permute-start | bytes 663560 | tf_op jit(solution)/shard_map/ppermute | solution.py:445
  5.0 5.0 %collective-permute-start = (bf16[288,128]{1,0:T(8,128)(2,1)S(1)}, bf16[288,128]{1,0:T(8,128)(2,1)S(1)}, u32[]{:S(2)}, u32[]{:S(2)}) collective-permute-start(bf16[288,128]{1,0:T(8,128)(2,1)S(1)} %get-tuple-element.36), channel_id=1, source_target_pairs={{0,2},{2,0},{4,6},{6,4},{8,10},{10,8},{12,14},{14,12},{16,18},{18,... | collective-permute-start | bytes 221192 | tf_op jit(solution)/shard_map/ppermute | solution.py:445
  5.0 5.0 %collective-permute-start.1 = (bf16[288,128]{1,0:T(8,128)(2,1)S(1)}, bf16[288,128]{1,0:T(8,128)(2,1)S(1)}, u32[]{:S(2)}, u32[]{:S(2)}) collective-permute-start(bf16[288,128]{1,0:T(8,128)(2,1)S(1)} %get-tuple-element.37), channel_id=1, source_target_pairs={{0,0},{2,4},{4,2},{6,8},{8,6},{10,12},{12,10},{14,16},{16,14},{18,... | collective-permute-start | bytes 221192 | tf_op jit(solution)/shard_map/ppermute | solution.py:471
  6.6 11.2 %collective-permute-start.4 = (bf16[768,128]{1,0:T(8,128)(2,1)S(1)}, bf16[768,128]{1,0:T(8,128)(2,1)S(1)}, u32[]{:S(2)}, u32[]{:S(2)}) collective-permute-start(bf16[768,128]{1,0:T(8,128)(2,1)S(1)} %pack.1.brick), channel_id=1, source_target_pairs={{0,4},{1,5},{2,6},{3,7},{4,0},{5,1},{6,2},{7,3},{8,12},{9,13},{10,... | collective-permute-start | bytes 589832 | tf_op jit(solution)/shard_map/ppermute | solution.py:445
  10.2 6.5 %collective-permute-start.3 = (bf16[128,128]{1,0:T(8,128)(2,1)S(1)}, bf16[128,128]{1,0:T(8,128)(2,1)S(1)}, u32[]{:S(2)}, u32[]{:S(2)}) collective-permute-start(bf16[128,128]{1,0:T(8,128)(2,1)S(1)} %corner.1), channel_id=1, source_target_pairs={{0,1},{1,0},{2,3},{3,2},{4,5},{5,4},{6,7},{7,6},{8,9},{9,8},{10,11... | collective-permute-start | bytes 98312 | tf_op jit(solution)/shard_map/ppermute | solution.py:445
  10.3 11.0 %collective-permute-start.6 = (bf16[768,128]{1,0:T(8,128)(2,1)S(1)}, bf16[768,128]{1,0:T(8,128)(2,1)S(1)}, u32[]{:S(2)}, u32[]{:S(2)}) collective-permute-start(bf16[768,128]{1,0:T(8,128)(2,1)S(1)} %pack.1.brick), channel_id=1, source_target_pairs={{0,5},{1,4},{2,7},{3,6},{4,1},{5,0},{6,3},{7,2},{8,13},{9,12},{10,... | collective-permute-start | bytes 589832 | tf_op jit(solution)/shard_map/ppermute | solution.py:445
  17.8 5.9 %collective-permute-start.5 = (bf16[48,640]{1,0:T(8,128)(2,1)S(1)}, bf16[48,640]{1,0:T(8,128)(2,1)S(1)}, u32[]{:S(2)}, u32[]{:S(2)}) collective-permute-start(bf16[48,640]{1,0:T(8,128)(2,1)S(1)} %get-tuple-element.52), channel_id=1, source_target_pairs={{0,1},{1,0},{2,3},{3,2},{4,5},{5,4},{6,7},{7,6},{8,9},{9,8},{10,11... | collective-permute-start | bytes 184328 | tf_op jit(solution)/shard_map/ppermute | solution.py:445
  18.4 6.9 %collective-permute-start.7 = (bf16[48,640]{1,0:T(8,128)(2,1)S(1)}, bf16[48,640]{1,0:T(8,128)(2,1)S(1)}, u32[]{:S(2)}, u32[]{:S(2)}) collective-permute-start(bf16[48,640]{1,0:T(8,128)(2,1)S(1)} %get-tuple-element.56), channel_id=1, source_target_pairs={{0,5},{1,4},{2,7},{3,6},{4,1},{5,0},{6,3},{7,2},{8,13},{9,12},{10,... | collective-permute-start | bytes 184328 | tf_op jit(solution)/shard_map/ppermute | solution.py:445
  19.5 5.8 %collective-permute-start.8 = (bf16[48,640]{1,0:T(8,128)(2,1)S(1)}, bf16[48,640]{1,0:T(8,128)(2,1)S(1)}, u32[]{:S(2)}, u32[]{:S(2)}) collective-permute-start(bf16[48,640]{1,0:T(8,128)(2,1)S(1)} %get-tuple-element.57), channel_id=1, source_target_pairs={{0,4},{1,5},{2,6},{3,7},{4,0},{5,1},{6,2},{7,3},{8,12},{9,13},{10,... | collective-permute-start | bytes 184328 | tf_op jit(solution)/shard_map/ppermute | solution.py:445
  26.3 1.6 %collective-permute-start.9 = (bf16[24,5184]{1,0:T(8,128)(2,1)S(1)}, bf16[24,5184]{1,0:T(8,128)(2,1)S(1)}, u32[]{:S(2)}, u32[]{:S(2)}) collective-permute-start(bf16[24,5184]{1,0:T(8,128)(2,1)S(1)} %second_pair_other.1), channel_id=1, source_target_pairs={{0,2},{1,3},{2,0},{3,1},{4,6},{5,7},{6,4},{7,5},{8,10},{9,11},{10,... | collective-permute-start | bytes 746504 | tf_op jit(solution)/shard_map/ppermute | solution.py:445
  28.1 6.8 %collective-permute-start.10 = (bf16[8,3968]{1,0:T(8,128)(2,1)S(1)}, bf16[8,3968]{1,0:T(8,128)(2,1)S(1)}, u32[]{:S(2)}, u32[]{:S(2)}) collective-permute-start(bf16[8,3968]{1,0:T(8,128)(2,1)S(1)} %get-tuple-element.59), channel_id=1, source_target_pairs={{0,16},{8,24},{16,0},{24,8},{1,17},{9,25},{17,1},{25,9},{2,18},{10... | collective-permute-start | bytes 190472 | tf_op jit(solution)/shard_map/ppermute | solution.py:445
  30.8 6.3 %collective-permute-start.11 = (bf16[8,3968]{1,0:T(8,128)(2,1)S(1)}, bf16[8,3968]{1,0:T(8,128)(2,1)S(1)}, u32[]{:S(2)}, u32[]{:S(2)}) collective-permute-start(bf16[8,3968]{1,0:T(8,128)(2,1)S(1)} %get-tuple-element.60), channel_id=1, source_target_pairs={{0,24},{8,16},{16,8},{24,0},{1,25},{9,17},{17,9},{25,1},{2,26},{10... | collective-permute-start | bytes 190472 | tf_op jit(solution)/shard_map/ppermute | solution.py:445
  32.2 5.1 %collective-permute-start.12 = (bf16[8,3968]{1,0:T(8,128)(2,1)S(1)}, bf16[8,3968]{1,0:T(8,128)(2,1)S(1)}, u32[]{:S(2)}, u32[]{:S(2)}) collective-permute-start(bf16[8,3968]{1,0:T(8,128)(2,1)S(1)} %get-tuple-element.61), channel_id=1, source_target_pairs={{0,8},{8,0},{16,24},{24,16},{1,9},{9,1},{17,25},{25,17},{2,10},{10... | collective-permute-start | bytes 190472 | tf_op jit(solution)/shard_map/ppermute | solution.py:445
  37.4 4.3 %collective-permute-start.13 = (bf16[8,3968]{1,0:T(8,128)(2,1)S(1)}, bf16[8,3968]{1,0:T(8,128)(2,1)S(1)}, u32[]{:S(2)}, u32[]{:S(2)}) collective-permute-start(bf16[8,3968]{1,0:T(8,128)(2,1)S(1)} %plane_sum.1.mine), channel_id=1, source_target_pairs={{0,1},{1,0},{2,3},{3,2},{4,5},{5,4},{6,7},{7,6},{8,9},{9,8},{10,11... | collective-permute-start | bytes 190472 | tf_op jit(solution)/shard_map/ppermute | solution.py:445

commit v24 on v23

--- a/solution.py
+++ b/solution.py
@@ -354,9 +354,12 @@
         yield a, jnp.concatenate([got[tap] for tap in range(9)], axis=1)
 
 
-def first_pair_kernel(own, other, brick, across, beside, beyond, part_ref, next_ref, cols, masked):
+def unpack_kernel(brick, across, beside, beyond, here_ref, next_ref):
+    unpack_pair((brick, across), here_ref)
     unpack_pair((beside, beyond), next_ref)
-    unpack_pair((brick, across), masked)
+
+
+def first_pair_kernel(own, other, masked, part_ref, cols):
     received = own[...].astype(jnp.float32), other[...].astype(jnp.float32)
     for a, rows in pair_product(received, masked, cols):
         width = rows.shape[1]
@@ -526,13 +529,15 @@
     lanes = dense(total)[0]
     cols = pltpu.VMEM((9 * 2 * group, (width + 2) * SIDES * rows), bf16)
     pair = (width, SIDES * rows, channels)
-    part, pair_masked = call(
+    here_masked, next_masked = call(
+        unpack_kernel, "unpack", 4, 1 << 20, 1 << 20, (array(pair, bf16),) * 2
+    )(*bricks)
+    part = call(
         first_pair_kernel, "first_pair", 16, 1 << 30, 2 << 20,
-        (array((2 * group, total), f32), array(pair, bf16)),
-        (cols, pltpu.VMEM(pair, bf16)),
-    )(*slices[:2], *bricks)
+        array((2 * group, total), f32), (cols,),
+    )(*slices[:2], here_masked)
     half_cols = pltpu.VMEM((9 * group, (width + 2) * SIDES * rows), bf16)
-    second = part, *slices[3:1:-1], pair_masked
+    second = part, *slices[3:1:-1], next_masked
     fold = call(
         functools.partial(second_pair_kernel, False), "second_pair_other", 16, 1 << 29, 1 << 20,
         array((group, total), bf16), (half_cols,),

time: 42.6 us -> 42.5 us (level)
  waiting for transfers between devices: 9.23 us -> 8.75 us
    ppermute x13, waiting for transfers between devices: 9.23 us -> 8.75 us  [swap(): return lax.ppermute(piece, axes, [(i, i ^ distance) for i in range(size)])]
    pallas_call x15 -> x16, Pallas kernels: 12.6 us -> 12.7 us  [run(): pl.pallas_call(body, out_shape=out_shape, in_specs=in_specs or [spec] * l...]
  transfers between devices with their start and end apart: 14 -> 14, of which waited for: 6 -> 5; matrix products, arithmetic and copies ran while one was open for 0% -> 0% of each run, Pallas kernels for 24% -> 24%
where the time goes in v24:
time: 42.5 us; the launch traced here: 42.3 us
  starting transfers between devices  19.2 us (45%)
  Pallas kernels  12.7 us (30%)
  waiting for transfers between devices  8.75 us (21%)
  local copies, waits for them, and re-layouts  0.84 us (2%)
  between operations  0.79 us (2%)
    ppermute x13, starting transfers between devices, swap(): return lax.ppermute(piece, axes, [(i, i ^ distance) for i in range(size)])  18.6 us
    pallas_call x16, Pallas kernels, run(): pl.pallas_call(body, out_shape=out_shape, in_specs=in_specs or [spec] * l...  12.7 us
    ppermute x13, waiting for transfers between devices, swap(): return lax.ppermute(piece, axes, [(i, i ^ distance) for i in range(size)])  8.75 us
  transfers between devices with their start and end apart: 14, of which 5 were waited for; matrix products, arithmetic and copies ran while one was open for 0% of the time, Pallas kernels for 24%

profile of v24, /device:TPU:0, one launch (start us, length us, event | category | flops | bytes accessed | tf_op | source)
XLA Modules:
  0.0 42.3 jit_solution(15928395217555802183)
XLA Ops:
  0.6 0.0 copy-start.1
  0.6 0.0 copy-start.2
  0.7 0.0 copy-start.3
  0.7 0.0 copy-start
  0.7 0.2 pick.1.first
  0.8 0.7 %copy-done.1 = bf16[8,8,8,192]{3,2,1,0:T(8,128)(2,1)S(1)} copy-done((bf16[8,8,8,192]{3,2,1,0:T(8,128)(2,1)S(1)}, bf16[8,8,8,192]{3,2,1,0:T(8,128)(2,1)}, u32[]{:S(2)}) %copy-start.1) | copy-done | bytes 196632
  1.6 0.1 copy-done.2
  1.7 0.0 copy-done.3
  1.7 0.2 prepare.1
  1.9 0.1 across.1
  2.0 3.0 %collective-permute-start.2 = (bf16[864,128]{1,0:T(8,128)(2,1)S(1)}, bf16[864,128]{1,0:T(8,128)(2,1)S(1)}, u32[]{:S(2)}, u32[]{:S(2)}) collective-permute-start(bf16[864,128]{1,0:T(8,128)(2,1)S(1)} %across.1), channel_id=1, source_target_pairs={{0,1},{1,0},{2,3},{3,2},{4,5},{5,4},{6,7},{7,6},{8,9},{9,8},{10,11... | collective-permute-start | bytes 663560 | tf_op jit(solution)/shard_map/ppermute | solution.py:448
  5.0 0.0 collective-permute-start
  5.0 0.7 %collective-permute-start.1 = (bf16[288,128]{1,0:T(8,128)(2,1)S(1)}, bf16[288,128]{1,0:T(8,128)(2,1)S(1)}, u32[]{:S(2)}, u32[]{:S(2)}) collective-permute-start(bf16[288,128]{1,0:T(8,128)(2,1)S(1)} %get-tuple-element.37), channel_id=1, source_target_pairs={{0,0},{2,4},{4,2},{6,8},{8,6},{10,12},{12,10},{14,16},{16,14},{18,... | collective-permute-start | bytes 221192 | tf_op jit(solution)/shard_map/ppermute | solution.py:474
  5.7 0.0 copy-done
  5.7 0.8 %turn.1.after.weight = bf16[5184,192]{1,0:T(8,128)(2,1)S(1)} custom-call(bf16[192,5184]{1,0:T(8,128)(2,1)S(1)} %bitcast.5), custom_call_target="tpu_custom_call" | custom-call | flops 1048576 | bytes 4194304 | tf_op jit(solution)/shard_map/turn/pallas_call | solution.py:419
  6.5 0.1 pack.1.brick
  6.6 3.4 %collective-permute-start.4 = (bf16[768,128]{1,0:T(8,128)(2,1)S(1)}, bf16[768,128]{1,0:T(8,128)(2,1)S(1)}, u32[]{:S(2)}, u32[]{:S(2)}) collective-permute-start(bf16[768,128]{1,0:T(8,128)(2,1)S(1)} %pack.1.brick), channel_id=1, source_target_pairs={{0,4},{1,5},{2,6},{3,7},{4,0},{5,1},{6,2},{7,3},{8,12},{9,13},{10,... | collective-permute-start | bytes 589832 | tf_op jit(solution)/shard_map/ppermute | solution.py:448
  10.0 0.0 collective-permute-done.near
  10.0 0.0 collective-permute-done.1.far
  10.0 0.2 corner.1
  10.2 0.1 collective-permute-start.3
  10.3 3.5 %collective-permute-start.6 = (bf16[768,128]{1,0:T(8,128)(2,1)S(1)}, bf16[768,128]{1,0:T(8,128)(2,1)S(1)}, u32[]{:S(2)}, u32[]{:S(2)}) collective-permute-start(bf16[768,128]{1,0:T(8,128)(2,1)S(1)} %pack.1.brick), channel_id=1, source_target_pairs={{0,5},{1,4},{2,7},{3,6},{4,1},{5,0},{6,3},{7,2},{8,13},{9,12},{10,... | collective-permute-start | bytes 589832 | tf_op jit(solution)/shard_map/ppermute | solution.py:448
  13.9 0.0 collective-permute-done.2.across
  13.9 2.8 %bulk.1 = f32[10,80,192]{2,1,0:T(8,128)S(1)} custom-call(bf16[8,64,192]{2,1,0:T(8,128)(2,1)S(1)} %get-tuple-element.35.masked, bf16[288,128]{1,0:T(8,128)(2,1)S(1)} %collective-permute-done.near, bf16[288,128]{1,0:T(8,128)(2,1)S(1)} %collective-permute-done.1.far, bf16[864,128]{1,0:T(8,128)(2,1)S(1)} %collective-permute-done.2.across, ...), custom_call_target="tpu_custom_call" | custom-call | flops 1610612736 | bytes 1048576 | tf_op jit(solution)/shard_map/bulk/pallas_call | solution.py:419
  16.7 0.0 collective-permute-done.3.corner
  16.7 1.1 %forward.1 = (bf16[8,64,192]{2,1,0:T(8,128)(2,1)S(1)}, bf16[10,80,192]{2,1,0:T(8,128)(2,1)S(1)}, bf16[48,640]{1,0:T(8,128)(2,1)S(1)}, bf16[48,640]{1,0:T(8,128)(...) custom-call(f32[10,80,192]{2,1,0:T(8,128)S(1)} %bulk.1, ...), custom_call_target="tpu_custom_call" | custom-call | flops 1610612736 | bytes 1048576 | tf_op jit(solution)/shard_map/forward/pallas_call | solution.py:419
  17.8 0.0 collective-permute-done.4.beside
  17.8 0.6 %collective-permute-start.5 = (bf16[48,640]{1,0:T(8,128)(2,1)S(1)}, bf16[48,640]{1,0:T(8,128)(2,1)S(1)}, u32[]{:S(2)}, u32[]{:S(2)}) collective-permute-start(bf16[48,640]{1,0:T(8,128)(2,1)S(1)} %get-tuple-element.52), channel_id=1, source_target_pairs={{0,1},{1,0},{2,3},{3,2},{4,5},{5,4},{6,7},{7,6},{8,9},{9,8},{10,11... | collective-permute-start | bytes 184328 | tf_op jit(solution)/shard_map/ppermute | solution.py:448
  18.4 1.1 %collective-permute-start.7 = (bf16[48,640]{1,0:T(8,128)(2,1)S(1)}, bf16[48,640]{1,0:T(8,128)(2,1)S(1)}, u32[]{:S(2)}, u32[]{:S(2)}) collective-permute-start(bf16[48,640]{1,0:T(8,128)(2,1)S(1)} %get-tuple-element.56), channel_id=1, source_target_pairs={{0,5},{1,4},{2,7},{3,6},{4,1},{5,0},{6,3},{7,2},{8,13},{9,12},{10,... | collective-permute-start | bytes 184328 | tf_op jit(solution)/shard_map/ppermute | solution.py:448
  19.5 1.9 %collective-permute-start.8 = (bf16[48,640]{1,0:T(8,128)(2,1)S(1)}, bf16[48,640]{1,0:T(8,128)(2,1)S(1)}, u32[]{:S(2)}, u32[]{:S(2)}) collective-permute-start(bf16[48,640]{1,0:T(8,128)(2,1)S(1)} %get-tuple-element.57), channel_id=1, source_target_pairs={{0,4},{1,5},{2,6},{3,7},{4,0},{5,1},{6,2},{7,3},{8,12},{9,13},{10,... | collective-permute-start | bytes 184328 | tf_op jit(solution)/shard_map/ppermute | solution.py:448
  21.4 0.0 collective-permute-done.6.beyond
  21.4 0.2 unpack.1
  21.6 2.1 %collective-permute-done.5.other = bf16[48,640]{1,0:T(8,128)(2,1)S(1)} collective-permute-done((bf16[48,640]{1,0:T(8,128)(2,1)S(1)}, bf16[48,640]{1,0:T(8,128)(2,1)S(1)}, u32[]{:S(2)}, u32[]{:S(2)}) %collective-permute-start.5) | collective-permute-done | bytes 61472 | tf_op jit(solution)/shard_map/ppermute | solution.py:448
  23.7 1.4 %first_pair.1.before = f32[48,5184]{1,0:T(8,128)S(1)} custom-call(bf16[48,640]{1,0:T(8,128)(2,1)S(1)} %get-tuple-element.51.own, bf16[48,640]{1,0:T(8,128)(2,1)S(1)} %collective-permute-done.5.other, bf16[8,128,192]{2,1,0:T(8,128)(2,1)S(1)} %get-tuple-element.55.masked), custom_call_target="tpu_custom_call" | custom-call | flops 1073741824 | bytes 2097152 | tf_op jit(solution)/shard_map/first_pair/pallas_call | solution.py:419
  25.1 0.0 collective-permute-done.7.other
  25.2 0.0 collective-permute-done.8.own
  25.2 1.0 %second_pair_other.1 = bf16[24,5184]{1,0:T(8,128)(2,1)S(1)} custom-call(f32[48,5184]{1,0:T(8,128)S(1)} %first_pair.1.before, bf16[48,640]{1,0:T(8,128)(2,1)S(1)} %collective-permute-done.7.other, bf16[48,640]{1,0:T(8,128)(2,1)S(1)} %collective-permute-done.8.own, bf16[8,128,192]{2,1,0:T(8,128)(2,1)S(1)} %get-tuple-element.58.masked), custom_call_target="tpu_custom_call" | custom-call | flops 536870912 | bytes 1048576 | tf_op jit(solution)/shard_map/second_pair_other/pallas_call | solution.py:419
  26.2 0.1 collective-permute-start.9
  26.2 1.0 %second_pair_own.1.keep = f32[24,5184]{1,0:T(8,128)S(1)} custom-call(f32[48,5184]{1,0:T(8,128)S(1)} %first_pair.1.before, bf16[48,640]{1,0:T(8,128)(2,1)S(1)} %collective-permute-done.7.other, bf16[48,640]{1,0:T(8,128)(2,1)S(1)} %collective-permute-done.8.own, bf16[8,128,192]{2,1,0:T(8,128)(2,1)S(1)} %get-tuple-element.58.masked), custom_call_target="tpu_custom_call" | custom-call | flops 536870912 | bytes 1048576 | tf_op jit(solution)/shard_map/second_pair_own/pallas_call | solution.py:419
  27.2 0.5 %collective-permute-done.9.other = bf16[24,5184]{1,0:T(8,128)(2,1)S(1)} collective-permute-done((bf16[24,5184]{1,0:T(8,128)(2,1)S(1)}, bf16[24,5184]{1,0:T(8,128)(2,1)S(1)}, u32[]{:S(2)}, u32[]{:S(2)}) %collective-permute-start.9) | collective-permute-done | bytes 248864 | tf_op jit(solution)/shard_map/ppermute | solution.py:448
  27.7 0.2 fold.1
  27.9 2.7 %collective-permute-start.10 = (bf16[8,3968]{1,0:T(8,128)(2,1)S(1)}, bf16[8,3968]{1,0:T(8,128)(2,1)S(1)}, u32[]{:S(2)}, u32[]{:S(2)}) collective-permute-start(bf16[8,3968]{1,0:T(8,128)(2,1)S(1)} %get-tuple-element.59), channel_id=1, source_target_pairs={{0,16},{8,24},{16,0},{24,8},{1,17},{9,25},{17,1},{25,9},{2,18},{10... | collective-permute-start | bytes 190472 | tf_op jit(solution)/shard_map/ppermute | solution.py:448
  30.7 1.4 %collective-permute-start.11 = (bf16[8,3968]{1,0:T(8,128)(2,1)S(1)}, bf16[8,3968]{1,0:T(8,128)(2,1)S(1)}, u32[]{:S(2)}, u32[]{:S(2)}) collective-permute-start(bf16[8,3968]{1,0:T(8,128)(2,1)S(1)} %get-tuple-element.60), channel_id=1, source_target_pairs={{0,24},{8,16},{16,8},{24,0},{1,25},{9,17},{17,9},{25,1},{2,26},{10... | collective-permute-start | bytes 190472 | tf_op jit(solution)/shard_map/ppermute | solution.py:448
  32.0 0.1 collective-permute-start.12
  32.1 2.6 %input_gradient.1 = (bf16[8,64,192]{2,1,0:T(8,128)(2,1)}, bf16[8,64,192]{2,1,0:T(8,128)(2,1)}) custom-call(bf16[10,80,192]{2,1,0:T(8,128)(2,1)S(1)} %get-tuple-element.43.gp, f32[8,64,128]{2,1,0:T(8,128)S(1)} %get-tuple-element.42.live, bf16[192,5184]{1,0:T(8,128)(2,1)S(1)} %bitcast.6, bf16[8,64,192]{2,1,0:T(8,128)(2,1)S(1)} %get-tuple-element.44.act), custom_call_target="tpu_custom_call" | custom-call | flops 1358954496 | bytes 4194304 | tf_op jit(solution)/shard_map/input_gradient/pallas_call | solution.py:419
  34.7 0.0 collective-permute-done.10.one
  34.7 2.3 %collective-permute-done.11.two = bf16[8,3968]{1,0:T(8,128)(2,1)S(1)} collective-permute-done((bf16[8,3968]{1,0:T(8,128)(2,1)S(1)}, bf16[8,3968]{1,0:T(8,128)(2,1)S(1)}, u32[]{:S(2)}, u32[]{:S(2)}) %collective-permute-start.11) | collective-permute-done | bytes 63520 | tf_op jit(solution)/shard_map/ppermute | solution.py:448
  37.0 0.1 collective-permute-done.12.three
  37.2 0.6 %collective-permute-start.13 = (bf16[8,3968]{1,0:T(8,128)(2,1)S(1)}, bf16[8,3968]{1,0:T(8,128)(2,1)S(1)}, u32[]{:S(2)}, u32[]{:S(2)}) collective-permute-start(bf16[8,3968]{1,0:T(8,128)(2,1)S(1)} %plane_sum.1.mine), channel_id=1, source_target_pairs={{0,1},{1,0},{2,3},{3,2},{4,5},{5,4},{6,7},{7,6},{8,9},{9,8},{10,11... | collective-permute-start | bytes 190472 | tf_op jit(solution)/shard_map/ppermute | solution.py:448
  37.9 3.7 %collective-permute-done.13.other = bf16[8,3968]{1,0:T(8,128)(2,1)S(1)} collective-permute-done((bf16[8,3968]{1,0:T(8,128)(2,1)S(1)}, bf16[8,3968]{1,0:T(8,128)(2,1)S(1)}, u32[]{:S(2)}, u32[]{:S(2)}) %collective-permute-start.13) | collective-permute-done | bytes 63520 | tf_op jit(solution)/shard_map/ppermute | solution.py:448
  41.5 0.8 %join.1 = f32[12,5184]{1,0:T(8,128)} custom-call(bf16[8,3968]{1,0:T(8,128)(2,1)S(1)} %plane_sum.1.mine, bf16[8,3968]{1,0:T(8,128)(2,1)S(1)} %collective-permute-done.13.other), custom_call_target="tpu_custom_call" | custom-call | flops 41472 | bytes 580608 | tf_op jit(solution)/shard_map/join/pallas_call | solution.py:419
  (1 shorter events, 0.0 us)
Async XLA Ops:
  0.6 1.0 %copy-start.1 = (bf16[8,8,8,192]{3,2,1,0:T(8,128)(2,1)S(1)}, bf16[8,8,8,192]{3,2,1,0:T(8,128)(2,1)}, u32[]{:S(2)}) copy-start(bf16[8,8,8,192]{3,2,1,0:T(8,128)(2,1)} %param.4) | copy-start | bytes 589828
  0.6 1.0 %copy-start.2 = (bf16[8,8,8,192]{3,2,1,0:T(8,128)(2,1)S(1)}, bf16[8,8,8,192]{3,2,1,0:T(8,128)(2,1)}, u32[]{:S(2)}) copy-start(bf16[8,8,8,192]{3,2,1,0:T(8,128)(2,1)} %param.7) | copy-start | bytes 589828
  0.7 1.0 %copy-start.3 = (s32[8,8,8]{2,1,0:T(8,128)S(1)}, s32[8,8,8]{2,1,0:T(8,128)}, u32[]{:S(2)}) copy-start(s32[8,8,8]{2,1,0:T(8,128)} %mask.1) | copy-start | bytes 6148
  0.7 5.0 %copy-start = (bf16[5184,192]{0,1:T(8,128)(2,1)S(1)}, bf16[5184,192]{0,1:T(8,128)(2,1)}, u32[]{:S(2)}) copy-start(bf16[5184,192]{0,1:T(8,128)(2,1)} %param.5) | copy-start | bytes 5971972
  2.0 11.9 %collective-permute-start.2 = (bf16[864,128]{1,0:T(8,128)(2,1)S(1)}, bf16[864,128]{1,0:T(8,128)(2,1)S(1)}, u32[]{:S(2)}, u32[]{:S(2)}) collective-permute-start(bf16[864,128]{1,0:T(8,128)(2,1)S(1)} %across.1), channel_id=1, source_target_pairs={{0,1},{1,0},{2,3},{3,2},{4,5},{5,4},{6,7},{7,6},{8,9},{9,8},{10,11... | collective-permute-start | bytes 663560 | tf_op jit(solution)/shard_map/ppermute | solution.py:448
  5.0 5.0 %collective-permute-start = (bf16[288,128]{1,0:T(8,128)(2,1)S(1)}, bf16[288,128]{1,0:T(8,128)(2,1)S(1)}, u32[]{:S(2)}, u32[]{:S(2)}) collective-permute-start(bf16[288,128]{1,0:T(8,128)(2,1)S(1)} %get-tuple-element.36), channel_id=1, source_target_pairs={{0,2},{2,0},{4,6},{6,4},{8,10},{10,8},{12,14},{14,12},{16,18},{18,... | collective-permute-start | bytes 221192 | tf_op jit(solution)/shard_map/ppermute | solution.py:448
  5.0 5.0 %collective-permute-start.1 = (bf16[288,128]{1,0:T(8,128)(2,1)S(1)}, bf16[288,128]{1,0:T(8,128)(2,1)S(1)}, u32[]{:S(2)}, u32[]{:S(2)}) collective-permute-start(bf16[288,128]{1,0:T(8,128)(2,1)S(1)} %get-tuple-element.37), channel_id=1, source_target_pairs={{0,0},{2,4},{4,2},{6,8},{8,6},{10,12},{12,10},{14,16},{16,14},{18,... | collective-permute-start | bytes 221192 | tf_op jit(solution)/shard_map/ppermute | solution.py:474
  6.6 11.2 %collective-permute-start.4 = (bf16[768,128]{1,0:T(8,128)(2,1)S(1)}, bf16[768,128]{1,0:T(8,128)(2,1)S(1)}, u32[]{:S(2)}, u32[]{:S(2)}) collective-permute-start(bf16[768,128]{1,0:T(8,128)(2,1)S(1)} %pack.1.brick), channel_id=1, source_target_pairs={{0,4},{1,5},{2,6},{3,7},{4,0},{5,1},{6,2},{7,3},{8,12},{9,13},{10,... | collective-permute-start | bytes 589832 | tf_op jit(solution)/shard_map/ppermute | solution.py:448
  10.2 6.5 %collective-permute-start.3 = (bf16[128,128]{1,0:T(8,128)(2,1)S(1)}, bf16[128,128]{1,0:T(8,128)(2,1)S(1)}, u32[]{:S(2)}, u32[]{:S(2)}) collective-permute-start(bf16[128,128]{1,0:T(8,128)(2,1)S(1)} %corner.1), channel_id=1, source_target_pairs={{0,1},{1,0},{2,3},{3,2},{4,5},{5,4},{6,7},{7,6},{8,9},{9,8},{10,11... | collective-permute-start | bytes 98312 | tf_op jit(solution)/shard_map/ppermute | solution.py:448
  10.3 11.1 %collective-permute-start.6 = (bf16[768,128]{1,0:T(8,128)(2,1)S(1)}, bf16[768,128]{1,0:T(8,128)(2,1)S(1)}, u32[]{:S(2)}, u32[]{:S(2)}) collective-permute-start(bf16[768,128]{1,0:T(8,128)(2,1)S(1)} %pack.1.brick), channel_id=1, source_target_pairs={{0,5},{1,4},{2,7},{3,6},{4,1},{5,0},{6,3},{7,2},{8,13},{9,12},{10,... | collective-permute-start | bytes 589832 | tf_op jit(solution)/shard_map/ppermute | solution.py:448
  17.8 5.9 %collective-permute-start.5 = (bf16[48,640]{1,0:T(8,128)(2,1)S(1)}, bf16[48,640]{1,0:T(8,128)(2,1)S(1)}, u32[]{:S(2)}, u32[]{:S(2)}) collective-permute-start(bf16[48,640]{1,0:T(8,128)(2,1)S(1)} %get-tuple-element.52), channel_id=1, source_target_pairs={{0,1},{1,0},{2,3},{3,2},{4,5},{5,4},{6,7},{7,6},{8,9},{9,8},{10,11... | collective-permute-start | bytes 184328 | tf_op jit(solution)/shard_map/ppermute | solution.py:448
  18.4 6.8 %collective-permute-start.7 = (bf16[48,640]{1,0:T(8,128)(2,1)S(1)}, bf16[48,640]{1,0:T(8,128)(2,1)S(1)}, u32[]{:S(2)}, u32[]{:S(2)}) collective-permute-start(bf16[48,640]{1,0:T(8,128)(2,1)S(1)} %get-tuple-element.56), channel_id=1, source_target_pairs={{0,5},{1,4},{2,7},{3,6},{4,1},{5,0},{6,3},{7,2},{8,13},{9,12},{10,... | collective-permute-start | bytes 184328 | tf_op jit(solution)/shard_map/ppermute | solution.py:448
  19.5 5.7 %collective-permute-start.8 = (bf16[48,640]{1,0:T(8,128)(2,1)S(1)}, bf16[48,640]{1,0:T(8,128)(2,1)S(1)}, u32[]{:S(2)}, u32[]{:S(2)}) collective-permute-start(bf16[48,640]{1,0:T(8,128)(2,1)S(1)} %get-tuple-element.57), channel_id=1, source_target_pairs={{0,4},{1,5},{2,6},{3,7},{4,0},{5,1},{6,2},{7,3},{8,12},{9,13},{10,... | collective-permute-start | bytes 184328 | tf_op jit(solution)/shard_map/ppermute | solution.py:448
  26.2 1.6 %collective-permute-start.9 = (bf16[24,5184]{1,0:T(8,128)(2,1)S(1)}, bf16[24,5184]{1,0:T(8,128)(2,1)S(1)}, u32[]{:S(2)}, u32[]{:S(2)}) collective-permute-start(bf16[24,5184]{1,0:T(8,128)(2,1)S(1)} %second_pair_other.1), channel_id=1, source_target_pairs={{0,2},{1,3},{2,0},{3,1},{4,6},{5,7},{6,4},{7,5},{8,10},{9,11},{10,... | collective-permute-start | bytes 746504 | tf_op jit(solution)/shard_map/ppermute | solution.py:448
  27.9 6.8 %collective-permute-start.10 = (bf16[8,3968]{1,0:T(8,128)(2,1)S(1)}, bf16[8,3968]{1,0:T(8,128)(2,1)S(1)}, u32[]{:S(2)}, u32[]{:S(2)}) collective-permute-start(bf16[8,3968]{1,0:T(8,128)(2,1)S(1)} %get-tuple-element.59), channel_id=1, source_target_pairs={{0,16},{8,24},{16,0},{24,8},{1,17},{9,25},{17,1},{25,9},{2,18},{10... | collective-permute-start | bytes 190472 | tf_op jit(solution)/shard_map/ppermute | solution.py:448
  30.7 6.3 %collective-permute-start.11 = (bf16[8,3968]{1,0:T(8,128)(2,1)S(1)}, bf16[8,3968]{1,0:T(8,128)(2,1)S(1)}, u32[]{:S(2)}, u32[]{:S(2)}) collective-permute-start(bf16[8,3968]{1,0:T(8,128)(2,1)S(1)} %get-tuple-element.60), channel_id=1, source_target_pairs={{0,24},{8,16},{16,8},{24,0},{1,25},{9,17},{17,9},{25,1},{2,26},{10... | collective-permute-start | bytes 190472 | tf_op jit(solution)/shard_map/ppermute | solution.py:448
  32.0 5.1 %collective-permute-start.12 = (bf16[8,3968]{1,0:T(8,128)(2,1)S(1)}, bf16[8,3968]{1,0:T(8,128)(2,1)S(1)}, u32[]{:S(2)}, u32[]{:S(2)}) collective-permute-start(bf16[8,3968]{1,0:T(8,128)(2,1)S(1)} %get-tuple-element.61), channel_id=1, source_target_pairs={{0,8},{8,0},{16,24},{24,16},{1,9},{9,1},{17,25},{25,17},{2,10},{10... | collective-permute-start | bytes 190472 | tf_op jit(solution)/shard_map/ppermute | solution.py:448
  37.2 4.3 %collective-permute-start.13 = (bf16[8,3968]{1,0:T(8,128)(2,1)S(1)}, bf16[8,3968]{1,0:T(8,128)(2,1)S(1)}, u32[]{:S(2)}, u32[]{:S(2)}) collective-permute-start(bf16[8,3968]{1,0:T(8,128)(2,1)S(1)} %plane_sum.1.mine), channel_id=1, source_target_pairs={{0,1},{1,0},{2,3},{3,2},{4,5},{5,4},{6,7},{7,6},{8,9},{9,8},{10,11... | collective-permute-start | bytes 190472 | tf_op jit(solution)/shard_map/ppermute | solution.py:448

commit v25 on v24

--- a/solution.py
+++ b/solution.py
@@ -400,16 +400,16 @@
     out_ref[...] = (total * scale).astype(out_ref.dtype)
 
 
-def join_kernel(mine, other, out_ref):
+def unfold_kernel(mine, out_ref):
+    out_ref[...] = unfold_rows(mine[...].astype(jnp.float32), out_ref.shape[1])
+
+
+def join_kernel(here, other, out_ref):
     share = out_ref.shape[0] // SIDES
+    there = unfold_rows(other[...].astype(jnp.float32), out_ref.shape[1])
     ahead = position()[3] == 0
-    total = out_ref.shape[1]
-    here = unfold_rows(mine[...].astype(jnp.float32), total)
-    there = unfold_rows(other[...].astype(jnp.float32), total)
-    first = jnp.where(ahead, here, there)
-    second = jnp.where(ahead, there, here)
-    out_ref[0:share] = first[:share]
-    out_ref[share:] = second[:share]
+    out_ref[0:share] = jnp.where(ahead, here[...], there)[:share]
+    out_ref[share:] = jnp.where(ahead, there, here[...])[:share]
 
 
 def call(body, name, mebibytes, flops, moved, out_shape, scratch=(), in_specs=None):
@@ -561,9 +561,12 @@
         functools.partial(sum_kernel, float(1.0 / voxels**0.5)),
         "plane_sum", 4, 8 * total * 4, 8 * total * 14, array((8, lanes), bf16),
     )(own, *got)
+    here = call(
+        unfold_kernel, "unfold", 4, 8 * total, 8 * total * 6, array((8, total), f32)
+    )(mine)
     grad_weight = call(
         join_kernel, "join", 4, 8 * total, 8 * total * 14, array((channels // count, total), f32)
-    )(mine, in_plane(mine, 1))
+    )(here, in_plane(mine, 1))
     shape = features.shape
     return act.reshape(shape), grad_input.reshape(shape), grad_weight
 

time: 42.5 us -> 42.5 us (level)
    pallas_call x16 -> x17, Pallas kernels: 12.7 us -> 12.7 us  [run(): pl.pallas_call(body, out_shape=out_shape, in_specs=in_specs or [spec] * l...]
where the time goes in v25:
time: 42.5 us; the launch traced here: 42.3 us
  starting transfers between devices  19.2 us (45%)
  Pallas kernels  12.7 us (30%)
  waiting for transfers between devices  8.72 us (21%)
  local copies, waits for them, and re-layouts  0.84 us (2%)
  between operations  0.79 us (2%)
    ppermute x13, starting transfers between devices, swap(): return lax.ppermute(piece, axes, [(i, i ^ distance) for i in range(size)])  18.6 us
    pallas_call x17, Pallas kernels, run(): pl.pallas_call(body, out_shape=out_shape, in_specs=in_specs or [spec] * l...  12.7 us
    ppermute x13, waiting for transfers between devices, swap(): return lax.ppermute(piece, axes, [(i, i ^ distance) for i in range(size)])  8.72 us
  transfers between devices with their start and end apart: 14, of which 5 were waited for; matrix products, arithmetic and copies ran while one was open for 0% of the time, Pallas kernels for 24%

profile of v25, /device:TPU:0, one launch (start us, length us, event | category | flops | bytes accessed | tf_op | source)
XLA Modules:
  0.0 42.3 jit_solution(12053343786250507495)
XLA Ops:
  0.6 0.0 copy-start.1
  0.6 0.0 copy-start.2
  0.7 0.0 copy-start.3
  0.7 0.0 copy-start
  0.7 0.2 pick.1.first
  0.8 0.7 %copy-done.1 = bf16[8,8,8,192]{3,2,1,0:T(8,128)(2,1)S(1)} copy-done((bf16[8,8,8,192]{3,2,1,0:T(8,128)(2,1)S(1)}, bf16[8,8,8,192]{3,2,1,0:T(8,128)(2,1)}, u32[]{:S(2)}) %copy-start.1) | copy-done | bytes 196632
  1.6 0.1 copy-done.2
  1.7 0.0 copy-done.3
  1.7 0.2 prepare.1
  1.9 0.1 across.1
  2.0 3.0 %collective-permute-start.2 = (bf16[864,128]{1,0:T(8,128)(2,1)S(1)}, bf16[864,128]{1,0:T(8,128)(2,1)S(1)}, u32[]{:S(2)}, u32[]{:S(2)}) collective-permute-start(bf16[864,128]{1,0:T(8,128)(2,1)S(1)} %across.1), channel_id=1, source_target_pairs={{0,1},{1,0},{2,3},{3,2},{4,5},{5,4},{6,7},{7,6},{8,9},{9,8},{10,11... | collective-permute-start | bytes 663560 | tf_op jit(solution)/shard_map/ppermute | solution.py:448
  5.0 0.0 collective-permute-start
  5.0 0.7 %collective-permute-start.1 = (bf16[288,128]{1,0:T(8,128)(2,1)S(1)}, bf16[288,128]{1,0:T(8,128)(2,1)S(1)}, u32[]{:S(2)}, u32[]{:S(2)}) collective-permute-start(bf16[288,128]{1,0:T(8,128)(2,1)S(1)} %get-tuple-element.37), channel_id=1, source_target_pairs={{0,0},{2,4},{4,2},{6,8},{8,6},{10,12},{12,10},{14,16},{16,14},{18,... | collective-permute-start | bytes 221192 | tf_op jit(solution)/shard_map/ppermute | solution.py:474
  5.7 0.0 copy-done
  5.7 0.8 %turn.1.after.weight = bf16[5184,192]{1,0:T(8,128)(2,1)S(1)} custom-call(bf16[192,5184]{1,0:T(8,128)(2,1)S(1)} %bitcast.5), custom_call_target="tpu_custom_call" | custom-call | flops 1048576 | bytes 4194304 | tf_op jit(solution)/shard_map/turn/pallas_call | solution.py:419
  6.5 0.1 pack.1.brick
  6.6 3.4 %collective-permute-start.4 = (bf16[768,128]{1,0:T(8,128)(2,1)S(1)}, bf16[768,128]{1,0:T(8,128)(2,1)S(1)}, u32[]{:S(2)}, u32[]{:S(2)}) collective-permute-start(bf16[768,128]{1,0:T(8,128)(2,1)S(1)} %pack.1.brick), channel_id=1, source_target_pairs={{0,4},{1,5},{2,6},{3,7},{4,0},{5,1},{6,2},{7,3},{8,12},{9,13},{10,... | collective-permute-start | bytes 589832 | tf_op jit(solution)/shard_map/ppermute | solution.py:448
  10.0 0.0 collective-permute-done.near
  10.0 0.0 collective-permute-done.1.far
  10.0 0.2 corner.1
  10.2 0.1 collective-permute-start.3
  10.3 3.5 %collective-permute-start.6 = (bf16[768,128]{1,0:T(8,128)(2,1)S(1)}, bf16[768,128]{1,0:T(8,128)(2,1)S(1)}, u32[]{:S(2)}, u32[]{:S(2)}) collective-permute-start(bf16[768,128]{1,0:T(8,128)(2,1)S(1)} %pack.1.brick), channel_id=1, source_target_pairs={{0,5},{1,4},{2,7},{3,6},{4,1},{5,0},{6,3},{7,2},{8,13},{9,12},{10,... | collective-permute-start | bytes 589832 | tf_op jit(solution)/shard_map/ppermute | solution.py:448
  13.9 0.0 collective-permute-done.2.across
  13.9 2.8 %bulk.1 = f32[10,80,192]{2,1,0:T(8,128)S(1)} custom-call(bf16[8,64,192]{2,1,0:T(8,128)(2,1)S(1)} %get-tuple-element.35.masked, bf16[288,128]{1,0:T(8,128)(2,1)S(1)} %collective-permute-done.near, bf16[288,128]{1,0:T(8,128)(2,1)S(1)} %collective-permute-done.1.far, bf16[864,128]{1,0:T(8,128)(2,1)S(1)} %collective-permute-done.2.across, ...), custom_call_target="tpu_custom_call" | custom-call | flops 1610612736 | bytes 1048576 | tf_op jit(solution)/shard_map/bulk/pallas_call | solution.py:419
  16.7 0.0 collective-permute-done.3.corner
  16.7 1.1 %forward.1 = (bf16[8,64,192]{2,1,0:T(8,128)(2,1)S(1)}, bf16[10,80,192]{2,1,0:T(8,128)(2,1)S(1)}, bf16[48,640]{1,0:T(8,128)(2,1)S(1)}, bf16[48,640]{1,0:T(8,128)(...) custom-call(f32[10,80,192]{2,1,0:T(8,128)S(1)} %bulk.1, ...), custom_call_target="tpu_custom_call" | custom-call | flops 1610612736 | bytes 1048576 | tf_op jit(solution)/shard_map/forward/pallas_call | solution.py:419
  17.8 0.0 collective-permute-done.4.beside
  17.8 0.6 %collective-permute-start.5 = (bf16[48,640]{1,0:T(8,128)(2,1)S(1)}, bf16[48,640]{1,0:T(8,128)(2,1)S(1)}, u32[]{:S(2)}, u32[]{:S(2)}) collective-permute-start(bf16[48,640]{1,0:T(8,128)(2,1)S(1)} %get-tuple-element.52), channel_id=1, source_target_pairs={{0,1},{1,0},{2,3},{3,2},{4,5},{5,4},{6,7},{7,6},{8,9},{9,8},{10,11... | collective-permute-start | bytes 184328 | tf_op jit(solution)/shard_map/ppermute | solution.py:448
  18.4 1.1 %collective-permute-start.7 = (bf16[48,640]{1,0:T(8,128)(2,1)S(1)}, bf16[48,640]{1,0:T(8,128)(2,1)S(1)}, u32[]{:S(2)}, u32[]{:S(2)}) collective-permute-start(bf16[48,640]{1,0:T(8,128)(2,1)S(1)} %get-tuple-element.56), channel_id=1, source_target_pairs={{0,5},{1,4},{2,7},{3,6},{4,1},{5,0},{6,3},{7,2},{8,13},{9,12},{10,... | collective-permute-start | bytes 184328 | tf_op jit(solution)/shard_map/ppermute | solution.py:448
  19.5 1.9 %collective-permute-start.8 = (bf16[48,640]{1,0:T(8,128)(2,1)S(1)}, bf16[48,640]{1,0:T(8,128)(2,1)S(1)}, u32[]{:S(2)}, u32[]{:S(2)}) collective-permute-start(bf16[48,640]{1,0:T(8,128)(2,1)S(1)} %get-tuple-element.57), channel_id=1, source_target_pairs={{0,4},{1,5},{2,6},{3,7},{4,0},{5,1},{6,2},{7,3},{8,12},{9,13},{10,... | collective-permute-start | bytes 184328 | tf_op jit(solution)/shard_map/ppermute | solution.py:448
  21.4 0.0 collective-permute-done.6.beyond
  21.4 0.2 unpack.1
  21.6 2.1 %collective-permute-done.5.other = bf16[48,640]{1,0:T(8,128)(2,1)S(1)} collective-permute-done((bf16[48,640]{1,0:T(8,128)(2,1)S(1)}, bf16[48,640]{1,0:T(8,128)(2,1)S(1)}, u32[]{:S(2)}, u32[]{:S(2)}) %collective-permute-start.5) | collective-permute-done | bytes 61472 | tf_op jit(solution)/shard_map/ppermute | solution.py:448
  23.7 1.4 %first_pair.1.before = f32[48,5184]{1,0:T(8,128)S(1)} custom-call(bf16[48,640]{1,0:T(8,128)(2,1)S(1)} %get-tuple-element.51.own, bf16[48,640]{1,0:T(8,128)(2,1)S(1)} %collective-permute-done.5.other, bf16[8,128,192]{2,1,0:T(8,128)(2,1)S(1)} %get-tuple-element.55.masked), custom_call_target="tpu_custom_call" | custom-call | flops 1073741824 | bytes 2097152 | tf_op jit(solution)/shard_map/first_pair/pallas_call | solution.py:419
  25.1 0.0 collective-permute-done.7.other
  25.2 0.0 collective-permute-done.8.own
  25.2 1.0 %second_pair_other.1 = bf16[24,5184]{1,0:T(8,128)(2,1)S(1)} custom-call(f32[48,5184]{1,0:T(8,128)S(1)} %first_pair.1.before, bf16[48,640]{1,0:T(8,128)(2,1)S(1)} %collective-permute-done.7.other, bf16[48,640]{1,0:T(8,128)(2,1)S(1)} %collective-permute-done.8.own, bf16[8,128,192]{2,1,0:T(8,128)(2,1)S(1)} %get-tuple-element.58.masked), custom_call_target="tpu_custom_call" | custom-call | flops 536870912 | bytes 1048576 | tf_op jit(solution)/shard_map/second_pair_other/pallas_call | solution.py:419
  26.2 0.1 collective-permute-start.9
  26.2 1.0 %second_pair_own.1.keep = f32[24,5184]{1,0:T(8,128)S(1)} custom-call(f32[48,5184]{1,0:T(8,128)S(1)} %first_pair.1.before, bf16[48,640]{1,0:T(8,128)(2,1)S(1)} %collective-permute-done.7.other, bf16[48,640]{1,0:T(8,128)(2,1)S(1)} %collective-permute-done.8.own, bf16[8,128,192]{2,1,0:T(8,128)(2,1)S(1)} %get-tuple-element.58.masked), custom_call_target="tpu_custom_call" | custom-call | flops 536870912 | bytes 1048576 | tf_op jit(solution)/shard_map/second_pair_own/pallas_call | solution.py:419
  27.2 0.5 %collective-permute-done.9.other = bf16[24,5184]{1,0:T(8,128)(2,1)S(1)} collective-permute-done((bf16[24,5184]{1,0:T(8,128)(2,1)S(1)}, bf16[24,5184]{1,0:T(8,128)(2,1)S(1)}, u32[]{:S(2)}, u32[]{:S(2)}) %collective-permute-start.9) | collective-permute-done | bytes 248864 | tf_op jit(solution)/shard_map/ppermute | solution.py:448
  27.7 0.2 fold.1
  27.9 2.7 %collective-permute-start.10 = (bf16[8,3968]{1,0:T(8,128)(2,1)S(1)}, bf16[8,3968]{1,0:T(8,128)(2,1)S(1)}, u32[]{:S(2)}, u32[]{:S(2)}) collective-permute-start(bf16[8,3968]{1,0:T(8,128)(2,1)S(1)} %get-tuple-element.59), channel_id=1, source_target_pairs={{0,16},{8,24},{16,0},{24,8},{1,17},{9,25},{17,1},{25,9},{2,18},{10... | collective-permute-start | bytes 190472 | tf_op jit(solution)/shard_map/ppermute | solution.py:448
  30.7 1.4 %collective-permute-start.11 = (bf16[8,3968]{1,0:T(8,128)(2,1)S(1)}, bf16[8,3968]{1,0:T(8,128)(2,1)S(1)}, u32[]{:S(2)}, u32[]{:S(2)}) collective-permute-start(bf16[8,3968]{1,0:T(8,128)(2,1)S(1)} %get-tuple-element.60), channel_id=1, source_target_pairs={{0,24},{8,16},{16,8},{24,0},{1,25},{9,17},{17,9},{25,1},{2,26},{10... | collective-permute-start | bytes 190472 | tf_op jit(solution)/shard_map/ppermute | solution.py:448
  32.0 0.1 collective-permute-start.12
  32.1 2.6 %input_gradient.1 = (bf16[8,64,192]{2,1,0:T(8,128)(2,1)}, bf16[8,64,192]{2,1,0:T(8,128)(2,1)}) custom-call(bf16[10,80,192]{2,1,0:T(8,128)(2,1)S(1)} %get-tuple-element.43.gp, f32[8,64,128]{2,1,0:T(8,128)S(1)} %get-tuple-element.42.live, bf16[192,5184]{1,0:T(8,128)(2,1)S(1)} %bitcast.6, bf16[8,64,192]{2,1,0:T(8,128)(2,1)S(1)} %get-tuple-element.44.act), custom_call_target="tpu_custom_call" | custom-call | flops 1358954496 | bytes 4194304 | tf_op jit(solution)/shard_map/input_gradient/pallas_call | solution.py:419
  34.7 0.0 collective-permute-done.10.one
  34.7 2.3 %collective-permute-done.11.two = bf16[8,3968]{1,0:T(8,128)(2,1)S(1)} collective-permute-done((bf16[8,3968]{1,0:T(8,128)(2,1)S(1)}, bf16[8,3968]{1,0:T(8,128)(2,1)S(1)}, u32[]{:S(2)}, u32[]{:S(2)}) %collective-permute-start.11) | collective-permute-done | bytes 63520 | tf_op jit(solution)/shard_map/ppermute | solution.py:448
  37.0 0.1 collective-permute-done.12.three
  37.2 0.6 %collective-permute-start.13 = (bf16[8,3968]{1,0:T(8,128)(2,1)S(1)}, bf16[8,3968]{1,0:T(8,128)(2,1)S(1)}, u32[]{:S(2)}, u32[]{:S(2)}) collective-permute-start(bf16[8,3968]{1,0:T(8,128)(2,1)S(1)} %plane_sum.1.mine), channel_id=1, source_target_pairs={{0,1},{1,0},{2,3},{3,2},{4,5},{5,4},{6,7},{7,6},{8,9},{9,8},{10,11... | collective-permute-start | bytes 190472 | tf_op jit(solution)/shard_map/ppermute | solution.py:448
  37.9 3.6 %collective-permute-done.13.other = bf16[8,3968]{1,0:T(8,128)(2,1)S(1)} collective-permute-done((bf16[8,3968]{1,0:T(8,128)(2,1)S(1)}, bf16[8,3968]{1,0:T(8,128)(2,1)S(1)}, u32[]{:S(2)}, u32[]{:S(2)}) %collective-permute-start.13) | collective-permute-done | bytes 63520 | tf_op jit(solution)/shard_map/ppermute | solution.py:448
  41.5 0.8 %join.1 = f32[12,5184]{1,0:T(8,128)} custom-call(f32[8,5184]{1,0:T(8,128)S(1)} %unfold.1.here, bf16[8,3968]{1,0:T(8,128)(2,1)S(1)} %collective-permute-done.13.other), custom_call_target="tpu_custom_call" | custom-call | flops 41472 | bytes 580608 | tf_op jit(solution)/shard_map/join/pallas_call | solution.py:419
  (2 shorter events, 0.1 us)
Async XLA Ops:
  0.6 1.0 %copy-start.1 = (bf16[8,8,8,192]{3,2,1,0:T(8,128)(2,1)S(1)}, bf16[8,8,8,192]{3,2,1,0:T(8,128)(2,1)}, u32[]{:S(2)}) copy-start(bf16[8,8,8,192]{3,2,1,0:T(8,128)(2,1)} %param.4) | copy-start | bytes 589828
  0.6 1.0 %copy-start.2 = (bf16[8,8,8,192]{3,2,1,0:T(8,128)(2,1)S(1)}, bf16[8,8,8,192]{3,2,1,0:T(8,128)(2,1)}, u32[]{:S(2)}) copy-start(bf16[8,8,8,192]{3,2,1,0:T(8,128)(2,1)} %param.7) | copy-start | bytes 589828
  0.7 1.0 %copy-start.3 = (s32[8,8,8]{2,1,0:T(8,128)S(1)}, s32[8,8,8]{2,1,0:T(8,128)}, u32[]{:S(2)}) copy-start(s32[8,8,8]{2,1,0:T(8,128)} %mask.1) | copy-start | bytes 6148
  0.7 5.0 %copy-start = (bf16[5184,192]{0,1:T(8,128)(2,1)S(1)}, bf16[5184,192]{0,1:T(8,128)(2,1)}, u32[]{:S(2)}) copy-start(bf16[5184,192]{0,1:T(8,128)(2,1)} %param.5) | copy-start | bytes 5971972
  2.0 11.9 %collective-permute-start.2 = (bf16[864,128]{1,0:T(8,128)(2,1)S(1)}, bf16[864,128]{1,0:T(8,128)(2,1)S(1)}, u32[]{:S(2)}, u32[]{:S(2)}) collective-permute-start(bf16[864,128]{1,0:T(8,128)(2,1)S(1)} %across.1), channel_id=1, source_target_pairs={{0,1},{1,0},{2,3},{3,2},{4,5},{5,4},{6,7},{7,6},{8,9},{9,8},{10,11... | collective-permute-start | bytes 663560 | tf_op jit(solution)/shard_map/ppermute | solution.py:448
  5.0 5.0 %collective-permute-start = (bf16[288,128]{1,0:T(8,128)(2,1)S(1)}, bf16[288,128]{1,0:T(8,128)(2,1)S(1)}, u32[]{:S(2)}, u32[]{:S(2)}) collective-permute-start(bf16[288,128]{1,0:T(8,128)(2,1)S(1)} %get-tuple-element.36), channel_id=1, source_target_pairs={{0,2},{2,0},{4,6},{6,4},{8,10},{10,8},{12,14},{14,12},{16,18},{18,... | collective-permute-start | bytes 221192 | tf_op jit(solution)/shard_map/ppermute | solution.py:448
  5.0 5.0 %collective-permute-start.1 = (bf16[288,128]{1,0:T(8,128)(2,1)S(1)}, bf16[288,128]{1,0:T(8,128)(2,1)S(1)}, u32[]{:S(2)}, u32[]{:S(2)}) collective-permute-start(bf16[288,128]{1,0:T(8,128)(2,1)S(1)} %get-tuple-element.37), channel_id=1, source_target_pairs={{0,0},{2,4},{4,2},{6,8},{8,6},{10,12},{12,10},{14,16},{16,14},{18,... | collective-permute-start | bytes 221192 | tf_op jit(solution)/shard_map/ppermute | solution.py:474
  6.6 11.2 %collective-permute-start.4 = (bf16[768,128]{1,0:T(8,128)(2,1)S(1)}, bf16[768,128]{1,0:T(8,128)(2,1)S(1)}, u32[]{:S(2)}, u32[]{:S(2)}) collective-permute-start(bf16[768,128]{1,0:T(8,128)(2,1)S(1)} %pack.1.brick), channel_id=1, source_target_pairs={{0,4},{1,5},{2,6},{3,7},{4,0},{5,1},{6,2},{7,3},{8,12},{9,13},{10,... | collective-permute-start | bytes 589832 | tf_op jit(solution)/shard_map/ppermute | solution.py:448
  10.2 6.5 %collective-permute-start.3 = (bf16[128,128]{1,0:T(8,128)(2,1)S(1)}, bf16[128,128]{1,0:T(8,128)(2,1)S(1)}, u32[]{:S(2)}, u32[]{:S(2)}) collective-permute-start(bf16[128,128]{1,0:T(8,128)(2,1)S(1)} %corner.1), channel_id=1, source_target_pairs={{0,1},{1,0},{2,3},{3,2},{4,5},{5,4},{6,7},{7,6},{8,9},{9,8},{10,11... | collective-permute-start | bytes 98312 | tf_op jit(solution)/shard_map/ppermute | solution.py:448
  10.3 11.1 %collective-permute-start.6 = (bf16[768,128]{1,0:T(8,128)(2,1)S(1)}, bf16[768,128]{1,0:T(8,128)(2,1)S(1)}, u32[]{:S(2)}, u32[]{:S(2)}) collective-permute-start(bf16[768,128]{1,0:T(8,128)(2,1)S(1)} %pack.1.brick), channel_id=1, source_target_pairs={{0,5},{1,4},{2,7},{3,6},{4,1},{5,0},{6,3},{7,2},{8,13},{9,12},{10,... | collective-permute-start | bytes 589832 | tf_op jit(solution)/shard_map/ppermute | solution.py:448
  17.8 5.9 %collective-permute-start.5 = (bf16[48,640]{1,0:T(8,128)(2,1)S(1)}, bf16[48,640]{1,0:T(8,128)(2,1)S(1)}, u32[]{:S(2)}, u32[]{:S(2)}) collective-permute-start(bf16[48,640]{1,0:T(8,128)(2,1)S(1)} %get-tuple-element.52), channel_id=1, source_target_pairs={{0,1},{1,0},{2,3},{3,2},{4,5},{5,4},{6,7},{7,6},{8,9},{9,8},{10,11... | collective-permute-start | bytes 184328 | tf_op jit(solution)/shard_map/ppermute | solution.py:448
  18.4 6.8 %collective-permute-start.7 = (bf16[48,640]{1,0:T(8,128)(2,1)S(1)}, bf16[48,640]{1,0:T(8,128)(2,1)S(1)}, u32[]{:S(2)}, u32[]{:S(2)}) collective-permute-start(bf16[48,640]{1,0:T(8,128)(2,1)S(1)} %get-tuple-element.56), channel_id=1, source_target_pairs={{0,5},{1,4},{2,7},{3,6},{4,1},{5,0},{6,3},{7,2},{8,13},{9,12},{10,... | collective-permute-start | bytes 184328 | tf_op jit(solution)/shard_map/ppermute | solution.py:448
  19.5 5.7 %collective-permute-start.8 = (bf16[48,640]{1,0:T(8,128)(2,1)S(1)}, bf16[48,640]{1,0:T(8,128)(2,1)S(1)}, u32[]{:S(2)}, u32[]{:S(2)}) collective-permute-start(bf16[48,640]{1,0:T(8,128)(2,1)S(1)} %get-tuple-element.57), channel_id=1, source_target_pairs={{0,4},{1,5},{2,6},{3,7},{4,0},{5,1},{6,2},{7,3},{8,12},{9,13},{10,... | collective-permute-start | bytes 184328 | tf_op jit(solution)/shard_map/ppermute | solution.py:448
  26.2 1.6 %collective-permute-start.9 = (bf16[24,5184]{1,0:T(8,128)(2,1)S(1)}, bf16[24,5184]{1,0:T(8,128)(2,1)S(1)}, u32[]{:S(2)}, u32[]{:S(2)}) collective-permute-start(bf16[24,5184]{1,0:T(8,128)(2,1)S(1)} %second_pair_other.1), channel_id=1, source_target_pairs={{0,2},{1,3},{2,0},{3,1},{4,6},{5,7},{6,4},{7,5},{8,10},{9,11},{10,... | collective-permute-start | bytes 746504 | tf_op jit(solution)/shard_map/ppermute | solution.py:448
  27.9 6.8 %collective-permute-start.10 = (bf16[8,3968]{1,0:T(8,128)(2,1)S(1)}, bf16[8,3968]{1,0:T(8,128)(2,1)S(1)}, u32[]{:S(2)}, u32[]{:S(2)}) collective-permute-start(bf16[8,3968]{1,0:T(8,128)(2,1)S(1)} %get-tuple-element.59), channel_id=1, source_target_pairs={{0,16},{8,24},{16,0},{24,8},{1,17},{9,25},{17,1},{25,9},{2,18},{10... | collective-permute-start | bytes 190472 | tf_op jit(solution)/shard_map/ppermute | solution.py:448
  30.7 6.3 %collective-permute-start.11 = (bf16[8,3968]{1,0:T(8,128)(2,1)S(1)}, bf16[8,3968]{1,0:T(8,128)(2,1)S(1)}, u32[]{:S(2)}, u32[]{:S(2)}) collective-permute-start(bf16[8,3968]{1,0:T(8,128)(2,1)S(1)} %get-tuple-element.60), channel_id=1, source_target_pairs={{0,24},{8,16},{16,8},{24,0},{1,25},{9,17},{17,9},{25,1},{2,26},{10... | collective-permute-start | bytes 190472 | tf_op jit(solution)/shard_map/ppermute | solution.py:448
  32.0 5.1 %collective-permute-start.12 = (bf16[8,3968]{1,0:T(8,128)(2,1)S(1)}, bf16[8,3968]{1,0:T(8,128)(2,1)S(1)}, u32[]{:S(2)}, u32[]{:S(2)}) collective-permute-start(bf16[8,3968]{1,0:T(8,128)(2,1)S(1)} %get-tuple-element.61), channel_id=1, source_target_pairs={{0,8},{8,0},{16,24},{24,16},{1,9},{9,1},{17,25},{25,17},{2,10},{10... | collective-permute-start | bytes 190472 | tf_op jit(solution)/shard_map/ppermute | solution.py:448
  37.2 4.3 %collective-permute-start.13 = (bf16[8,3968]{1,0:T(8,128)(2,1)S(1)}, bf16[8,3968]{1,0:T(8,128)(2,1)S(1)}, u32[]{:S(2)}, u32[]{:S(2)}) collective-permute-start(bf16[8,3968]{1,0:T(8,128)(2,1)S(1)} %plane_sum.1.mine), channel_id=1, source_target_pairs={{0,1},{1,0},{2,3},{3,2},{4,5},{5,4},{6,7},{7,6},{8,9},{9,8},{10,11... | collective-permute-start | bytes 190472 | tf_op jit(solution)/shard_map/ppermute | solution.py:448

commit v26 on v24

--- a/solution.py
+++ b/solution.py
@@ -484,7 +484,7 @@
     packed = call(
         pack_kernel, "pack", 4, 1 << 16, 1 << 19, array((count_128, 128), bf16), (),
         [vmem, pl.BlockSpec(memory_space=pl.ANY)],
-    )(masked, weight_rows)
+    )(masked, near)
     near, far, weight_rows, late = lax.optimization_barrier((near, far, weight_rows, packed))
     corner = call(
         corner_kernel, "corner", 4, 1 << 16, 1 << 18,

time: 42.5 us -> 42.5 us (level)
  no operation moved by 1% of the time
where the time goes in v26:
time: 42.5 us; the launch traced here: 42.3 us
  starting transfers between devices  19.2 us (45%)
  Pallas kernels  12.7 us (30%)
  waiting for transfers between devices  8.79 us (21%)
  local copies, waits for them, and re-layouts  0.84 us (2%)
  between operations  0.8 us (2%)
    ppermute x13, starting transfers between devices, swap(): return lax.ppermute(piece, axes, [(i, i ^ distance) for i in range(size)])  18.5 us
    pallas_call x16, Pallas kernels, run(): pl.pallas_call(body, out_shape=out_shape, in_specs=in_specs or [spec] * l...  12.7 us
    ppermute x13, waiting for transfers between devices, swap(): return lax.ppermute(piece, axes, [(i, i ^ distance) for i in range(size)])  8.79 us
  transfers between devices with their start and end apart: 14, of which 5 were waited for; matrix products, arithmetic and copies ran while one was open for 0% of the time, Pallas kernels for 24%

profile of v26, /device:TPU:0, one launch (start us, length us, event | category | flops | bytes accessed | tf_op | source)
XLA Modules:
  0.0 42.3 jit_solution(13575934584762152013)
XLA Ops:
  0.6 0.0 copy-start.1
  0.6 0.0 copy-start.2
  0.7 0.0 copy-start.3
  0.7 0.0 copy-start
  0.7 0.2 pick.1.first
  0.8 0.7 %copy-done.1 = bf16[8,8,8,192]{3,2,1,0:T(8,128)(2,1)S(1)} copy-done((bf16[8,8,8,192]{3,2,1,0:T(8,128)(2,1)S(1)}, bf16[8,8,8,192]{3,2,1,0:T(8,128)(2,1)}, u32[]{:S(2)}) %copy-start.1) | copy-done | bytes 196632
  1.6 0.1 copy-done.2
  1.7 0.0 copy-done.3
  1.7 0.2 prepare.1
  1.9 0.1 across.1
  2.0 3.0 %collective-permute-start.2 = (bf16[864,128]{1,0:T(8,128)(2,1)S(1)}, bf16[864,128]{1,0:T(8,128)(2,1)S(1)}, u32[]{:S(2)}, u32[]{:S(2)}) collective-permute-start(bf16[864,128]{1,0:T(8,128)(2,1)S(1)} %across.1), channel_id=1, source_target_pairs={{0,1},{1,0},{2,3},{3,2},{4,5},{5,4},{6,7},{7,6},{8,9},{9,8},{10,11... | collective-permute-start | bytes 663560 | tf_op jit(solution)/shard_map/ppermute | solution.py:448
  5.0 0.0 collective-permute-start
  5.0 0.7 %collective-permute-start.1 = (bf16[288,128]{1,0:T(8,128)(2,1)S(1)}, bf16[288,128]{1,0:T(8,128)(2,1)S(1)}, u32[]{:S(2)}, u32[]{:S(2)}) collective-permute-start(bf16[288,128]{1,0:T(8,128)(2,1)S(1)} %get-tuple-element.37), channel_id=1, source_target_pairs={{0,0},{2,4},{4,2},{6,8},{8,6},{10,12},{12,10},{14,16},{16,14},{18,... | collective-permute-start | bytes 221192 | tf_op jit(solution)/shard_map/ppermute | solution.py:474
  5.7 0.0 copy-done
  5.7 0.8 %turn.1.weight = bf16[5184,192]{1,0:T(8,128)(2,1)S(1)} custom-call(bf16[192,5184]{1,0:T(8,128)(2,1)S(1)} %bitcast.5), custom_call_target="tpu_custom_call" | custom-call | flops 1048576 | bytes 4194304 | tf_op jit(solution)/shard_map/turn/pallas_call | solution.py:419
  6.5 0.0 collective-permute-done.after.near
  6.5 0.1 pack.1.brick
  6.6 3.4 %collective-permute-start.4 = (bf16[768,128]{1,0:T(8,128)(2,1)S(1)}, bf16[768,128]{1,0:T(8,128)(2,1)S(1)}, u32[]{:S(2)}, u32[]{:S(2)}) collective-permute-start(bf16[768,128]{1,0:T(8,128)(2,1)S(1)} %pack.1.brick), channel_id=1, source_target_pairs={{0,4},{1,5},{2,6},{3,7},{4,0},{5,1},{6,2},{7,3},{8,12},{9,13},{10,... | collective-permute-start | bytes 589832 | tf_op jit(solution)/shard_map/ppermute | solution.py:448
  10.0 0.0 collective-permute-done.1.far
  10.0 0.2 corner.1
  10.2 0.1 collective-permute-start.3
  10.3 3.5 %collective-permute-start.6 = (bf16[768,128]{1,0:T(8,128)(2,1)S(1)}, bf16[768,128]{1,0:T(8,128)(2,1)S(1)}, u32[]{:S(2)}, u32[]{:S(2)}) collective-permute-start(bf16[768,128]{1,0:T(8,128)(2,1)S(1)} %pack.1.brick), channel_id=1, source_target_pairs={{0,5},{1,4},{2,7},{3,6},{4,1},{5,0},{6,3},{7,2},{8,13},{9,12},{10,... | collective-permute-start | bytes 589832 | tf_op jit(solution)/shard_map/ppermute | solution.py:448
  13.9 0.0 collective-permute-done.2.across
  13.9 2.8 %bulk.1 = f32[10,80,192]{2,1,0:T(8,128)S(1)} custom-call(bf16[8,64,192]{2,1,0:T(8,128)(2,1)S(1)} %get-tuple-element.35.masked, bf16[288,128]{1,0:T(8,128)(2,1)S(1)} %collective-permute-done.after.near, bf16[288,128]{1,0:T(8,128)(2,1)S(1)} %collective-permute-done.1.far, bf16[864,128]{1,0:T(8,128)(2,1)S(1)} %collective-permute-done.2.across, ...), custom_call_target="tpu_custom_call" | custom-call | flops 1610612736 | bytes 1048576 | tf_op jit(solution)/shard_map/bulk/pallas_call | solution.py:419
  16.7 0.0 collective-permute-done.3.corner
  16.7 1.1 %forward.1 = (bf16[8,64,192]{2,1,0:T(8,128)(2,1)S(1)}, bf16[10,80,192]{2,1,0:T(8,128)(2,1)S(1)}, bf16[48,640]{1,0:T(8,128)(2,1)S(1)}, bf16[48,640]{1,0:T(8,128)(...) custom-call(f32[10,80,192]{2,1,0:T(8,128)S(1)} %bulk.1, ...), custom_call_target="tpu_custom_call" | custom-call | flops 1610612736 | bytes 1048576 | tf_op jit(solution)/shard_map/forward/pallas_call | solution.py:419
  17.8 0.0 collective-permute-done.4.beside
  17.8 0.6 %collective-permute-start.5 = (bf16[48,640]{1,0:T(8,128)(2,1)S(1)}, bf16[48,640]{1,0:T(8,128)(2,1)S(1)}, u32[]{:S(2)}, u32[]{:S(2)}) collective-permute-start(bf16[48,640]{1,0:T(8,128)(2,1)S(1)} %get-tuple-element.52), channel_id=1, source_target_pairs={{0,1},{1,0},{2,3},{3,2},{4,5},{5,4},{6,7},{7,6},{8,9},{9,8},{10,11... | collective-permute-start | bytes 184328 | tf_op jit(solution)/shard_map/ppermute | solution.py:448
  18.4 1.1 %collective-permute-start.7 = (bf16[48,640]{1,0:T(8,128)(2,1)S(1)}, bf16[48,640]{1,0:T(8,128)(2,1)S(1)}, u32[]{:S(2)}, u32[]{:S(2)}) collective-permute-start(bf16[48,640]{1,0:T(8,128)(2,1)S(1)} %get-tuple-element.56), channel_id=1, source_target_pairs={{0,5},{1,4},{2,7},{3,6},{4,1},{5,0},{6,3},{7,2},{8,13},{9,12},{10,... | collective-permute-start | bytes 184328 | tf_op jit(solution)/shard_map/ppermute | solution.py:448
  19.4 1.9 %collective-permute-start.8 = (bf16[48,640]{1,0:T(8,128)(2,1)S(1)}, bf16[48,640]{1,0:T(8,128)(2,1)S(1)}, u32[]{:S(2)}, u32[]{:S(2)}) collective-permute-start(bf16[48,640]{1,0:T(8,128)(2,1)S(1)} %get-tuple-element.57), channel_id=1, source_target_pairs={{0,4},{1,5},{2,6},{3,7},{4,0},{5,1},{6,2},{7,3},{8,12},{9,13},{10,... | collective-permute-start | bytes 184328 | tf_op jit(solution)/shard_map/ppermute | solution.py:448
  21.4 0.0 collective-permute-done.6.beyond
  21.4 0.2 unpack.1
  21.6 2.1 %collective-permute-done.5.other = bf16[48,640]{1,0:T(8,128)(2,1)S(1)} collective-permute-done((bf16[48,640]{1,0:T(8,128)(2,1)S(1)}, bf16[48,640]{1,0:T(8,128)(2,1)S(1)}, u32[]{:S(2)}, u32[]{:S(2)}) %collective-permute-start.5) | collective-permute-done | bytes 61472 | tf_op jit(solution)/shard_map/ppermute | solution.py:448
  23.7 1.4 %first_pair.1.before = f32[48,5184]{1,0:T(8,128)S(1)} custom-call(bf16[48,640]{1,0:T(8,128)(2,1)S(1)} %get-tuple-element.51.own, bf16[48,640]{1,0:T(8,128)(2,1)S(1)} %collective-permute-done.5.other, bf16[8,128,192]{2,1,0:T(8,128)(2,1)S(1)} %get-tuple-element.55.masked), custom_call_target="tpu_custom_call" | custom-call | flops 1073741824 | bytes 2097152 | tf_op jit(solution)/shard_map/first_pair/pallas_call | solution.py:419
  25.1 0.0 collective-permute-done.7.other
  25.2 0.0 collective-permute-done.8.own
  25.2 1.0 %second_pair_other.1 = bf16[24,5184]{1,0:T(8,128)(2,1)S(1)} custom-call(f32[48,5184]{1,0:T(8,128)S(1)} %first_pair.1.before, bf16[48,640]{1,0:T(8,128)(2,1)S(1)} %collective-permute-done.7.other, bf16[48,640]{1,0:T(8,128)(2,1)S(1)} %collective-permute-done.8.own, bf16[8,128,192]{2,1,0:T(8,128)(2,1)S(1)} %get-tuple-element.58.masked), custom_call_target="tpu_custom_call" | custom-call | flops 536870912 | bytes 1048576 | tf_op jit(solution)/shard_map/second_pair_other/pallas_call | solution.py:419
  26.2 0.1 collective-permute-start.9
  26.2 1.0 %second_pair_own.1.keep = f32[24,5184]{1,0:T(8,128)S(1)} custom-call(f32[48,5184]{1,0:T(8,128)S(1)} %first_pair.1.before, bf16[48,640]{1,0:T(8,128)(2,1)S(1)} %collective-permute-done.7.other, bf16[48,640]{1,0:T(8,128)(2,1)S(1)} %collective-permute-done.8.own, bf16[8,128,192]{2,1,0:T(8,128)(2,1)S(1)} %get-tuple-element.58.masked), custom_call_target="tpu_custom_call" | custom-call | flops 536870912 | bytes 1048576 | tf_op jit(solution)/shard_map/second_pair_own/pallas_call | solution.py:419
  27.2 0.5 %collective-permute-done.9.other = bf16[24,5184]{1,0:T(8,128)(2,1)S(1)} collective-permute-done((bf16[24,5184]{1,0:T(8,128)(2,1)S(1)}, bf16[24,5184]{1,0:T(8,128)(2,1)S(1)}, u32[]{:S(2)}, u32[]{:S(2)}) %collective-permute-start.9) | collective-permute-done | bytes 248864 | tf_op jit(solution)/shard_map/ppermute | solution.py:448
  27.7 0.2 fold.1
  27.9 2.7 %collective-permute-start.10 = (bf16[8,3968]{1,0:T(8,128)(2,1)S(1)}, bf16[8,3968]{1,0:T(8,128)(2,1)S(1)}, u32[]{:S(2)}, u32[]{:S(2)}) collective-permute-start(bf16[8,3968]{1,0:T(8,128)(2,1)S(1)} %get-tuple-element.59), channel_id=1, source_target_pairs={{0,16},{8,24},{16,0},{24,8},{1,17},{9,25},{17,1},{25,9},{2,18},{10... | collective-permute-start | bytes 190472 | tf_op jit(solution)/shard_map/ppermute | solution.py:448
  30.7 1.4 %collective-permute-start.11 = (bf16[8,3968]{1,0:T(8,128)(2,1)S(1)}, bf16[8,3968]{1,0:T(8,128)(2,1)S(1)}, u32[]{:S(2)}, u32[]{:S(2)}) collective-permute-start(bf16[8,3968]{1,0:T(8,128)(2,1)S(1)} %get-tuple-element.60), channel_id=1, source_target_pairs={{0,24},{8,16},{16,8},{24,0},{1,25},{9,17},{17,9},{25,1},{2,26},{10... | collective-permute-start | bytes 190472 | tf_op jit(solution)/shard_map/ppermute | solution.py:448
  32.0 0.1 collective-permute-start.12
  32.1 2.6 %input_gradient.1 = (bf16[8,64,192]{2,1,0:T(8,128)(2,1)}, bf16[8,64,192]{2,1,0:T(8,128)(2,1)}) custom-call(bf16[10,80,192]{2,1,0:T(8,128)(2,1)S(1)} %get-tuple-element.43.gp, f32[8,64,128]{2,1,0:T(8,128)S(1)} %get-tuple-element.42.live, bf16[192,5184]{1,0:T(8,128)(2,1)S(1)} %bitcast.6, bf16[8,64,192]{2,1,0:T(8,128)(2,1)S(1)} %get-tuple-element.44.act), custom_call_target="tpu_custom_call" | custom-call | flops 1358954496 | bytes 4194304 | tf_op jit(solution)/shard_map/input_gradient/pallas_call | solution.py:419
  34.7 0.0 collective-permute-done.10.one
  34.7 2.3 %collective-permute-done.11.two = bf16[8,3968]{1,0:T(8,128)(2,1)S(1)} collective-permute-done((bf16[8,3968]{1,0:T(8,128)(2,1)S(1)}, bf16[8,3968]{1,0:T(8,128)(2,1)S(1)}, u32[]{:S(2)}, u32[]{:S(2)}) %collective-permute-start.11) | collective-permute-done | bytes 63520 | tf_op jit(solution)/shard_map/ppermute | solution.py:448
  37.0 0.2 collective-permute-done.12.three
  37.2 0.6 %collective-permute-start.13 = (bf16[8,3968]{1,0:T(8,128)(2,1)S(1)}, bf16[8,3968]{1,0:T(8,128)(2,1)S(1)}, u32[]{:S(2)}, u32[]{:S(2)}) collective-permute-start(bf16[8,3968]{1,0:T(8,128)(2,1)S(1)} %plane_sum.1.mine), channel_id=1, source_target_pairs={{0,1},{1,0},{2,3},{3,2},{4,5},{5,4},{6,7},{7,6},{8,9},{9,8},{10,11... | collective-permute-start | bytes 190472 | tf_op jit(solution)/shard_map/ppermute | solution.py:448
  37.9 3.7 %collective-permute-done.13.other = bf16[8,3968]{1,0:T(8,128)(2,1)S(1)} collective-permute-done((bf16[8,3968]{1,0:T(8,128)(2,1)S(1)}, bf16[8,3968]{1,0:T(8,128)(2,1)S(1)}, u32[]{:S(2)}, u32[]{:S(2)}) %collective-permute-start.13) | collective-permute-done | bytes 63520 | tf_op jit(solution)/shard_map/ppermute | solution.py:448
  41.5 0.8 %join.1 = f32[12,5184]{1,0:T(8,128)} custom-call(bf16[8,3968]{1,0:T(8,128)(2,1)S(1)} %plane_sum.1.mine, bf16[8,3968]{1,0:T(8,128)(2,1)S(1)} %collective-permute-done.13.other), custom_call_target="tpu_custom_call" | custom-call | flops 41472 | bytes 580608 | tf_op jit(solution)/shard_map/join/pallas_call | solution.py:419
  (1 shorter events, 0.0 us)
Async XLA Ops:
  0.6 1.0 %copy-start.1 = (bf16[8,8,8,192]{3,2,1,0:T(8,128)(2,1)S(1)}, bf16[8,8,8,192]{3,2,1,0:T(8,128)(2,1)}, u32[]{:S(2)}) copy-start(bf16[8,8,8,192]{3,2,1,0:T(8,128)(2,1)} %param.4) | copy-start | bytes 589828
  0.6 1.0 %copy-start.2 = (bf16[8,8,8,192]{3,2,1,0:T(8,128)(2,1)S(1)}, bf16[8,8,8,192]{3,2,1,0:T(8,128)(2,1)}, u32[]{:S(2)}) copy-start(bf16[8,8,8,192]{3,2,1,0:T(8,128)(2,1)} %param.7) | copy-start | bytes 589828
  0.7 1.0 %copy-start.3 = (s32[8,8,8]{2,1,0:T(8,128)S(1)}, s32[8,8,8]{2,1,0:T(8,128)}, u32[]{:S(2)}) copy-start(s32[8,8,8]{2,1,0:T(8,128)} %mask.1) | copy-start | bytes 6148
  0.7 5.0 %copy-start = (bf16[5184,192]{0,1:T(8,128)(2,1)S(1)}, bf16[5184,192]{0,1:T(8,128)(2,1)}, u32[]{:S(2)}) copy-start(bf16[5184,192]{0,1:T(8,128)(2,1)} %param.5) | copy-start | bytes 5971972
  2.0 11.9 %collective-permute-start.2 = (bf16[864,128]{1,0:T(8,128)(2,1)S(1)}, bf16[864,128]{1,0:T(8,128)(2,1)S(1)}, u32[]{:S(2)}, u32[]{:S(2)}) collective-permute-start(bf16[864,128]{1,0:T(8,128)(2,1)S(1)} %across.1), channel_id=1, source_target_pairs={{0,1},{1,0},{2,3},{3,2},{4,5},{5,4},{6,7},{7,6},{8,9},{9,8},{10,11... | collective-permute-start | bytes 663560 | tf_op jit(solution)/shard_map/ppermute | solution.py:448
  5.0 1.5 %collective-permute-start = (bf16[288,128]{1,0:T(8,128)(2,1)S(1)}, bf16[288,128]{1,0:T(8,128)(2,1)S(1)}, u32[]{:S(2)}, u32[]{:S(2)}) collective-permute-start(bf16[288,128]{1,0:T(8,128)(2,1)S(1)} %get-tuple-element.36), channel_id=1, source_target_pairs={{0,2},{2,0},{4,6},{6,4},{8,10},{10,8},{12,14},{14,12},{16,18},{18,... | collective-permute-start | bytes 221192 | tf_op jit(solution)/shard_map/ppermute | solution.py:448
  5.0 5.0 %collective-permute-start.1 = (bf16[288,128]{1,0:T(8,128)(2,1)S(1)}, bf16[288,128]{1,0:T(8,128)(2,1)S(1)}, u32[]{:S(2)}, u32[]{:S(2)}) collective-permute-start(bf16[288,128]{1,0:T(8,128)(2,1)S(1)} %get-tuple-element.37), channel_id=1, source_target_pairs={{0,0},{2,4},{4,2},{6,8},{8,6},{10,12},{12,10},{14,16},{16,14},{18,... | collective-permute-start | bytes 221192 | tf_op jit(solution)/shard_map/ppermute | solution.py:474
  6.6 11.2 %collective-permute-start.4 = (bf16[768,128]{1,0:T(8,128)(2,1)S(1)}, bf16[768,128]{1,0:T(8,128)(2,1)S(1)}, u32[]{:S(2)}, u32[]{:S(2)}) collective-permute-start(bf16[768,128]{1,0:T(8,128)(2,1)S(1)} %pack.1.brick), channel_id=1, source_target_pairs={{0,4},{1,5},{2,6},{3,7},{4,0},{5,1},{6,2},{7,3},{8,12},{9,13},{10,... | collective-permute-start | bytes 589832 | tf_op jit(solution)/shard_map/ppermute | solution.py:448
  10.2 6.5 %collective-permute-start.3 = (bf16[128,128]{1,0:T(8,128)(2,1)S(1)}, bf16[128,128]{1,0:T(8,128)(2,1)S(1)}, u32[]{:S(2)}, u32[]{:S(2)}) collective-permute-start(bf16[128,128]{1,0:T(8,128)(2,1)S(1)} %corner.1), channel_id=1, source_target_pairs={{0,1},{1,0},{2,3},{3,2},{4,5},{5,4},{6,7},{7,6},{8,9},{9,8},{10,11... | collective-permute-start | bytes 98312 | tf_op jit(solution)/shard_map/ppermute | solution.py:448
  10.3 11.0 %collective-permute-start.6 = (bf16[768,128]{1,0:T(8,128)(2,1)S(1)}, bf16[768,128]{1,0:T(8,128)(2,1)S(1)}, u32[]{:S(2)}, u32[]{:S(2)}) collective-permute-start(bf16[768,128]{1,0:T(8,128)(2,1)S(1)} %pack.1.brick), channel_id=1, source_target_pairs={{0,5},{1,4},{2,7},{3,6},{4,1},{5,0},{6,3},{7,2},{8,13},{9,12},{10,... | collective-permute-start | bytes 589832 | tf_op jit(solution)/shard_map/ppermute | solution.py:448
  17.8 5.9 %collective-permute-start.5 = (bf16[48,640]{1,0:T(8,128)(2,1)S(1)}, bf16[48,640]{1,0:T(8,128)(2,1)S(1)}, u32[]{:S(2)}, u32[]{:S(2)}) collective-permute-start(bf16[48,640]{1,0:T(8,128)(2,1)S(1)} %get-tuple-element.52), channel_id=1, source_target_pairs={{0,1},{1,0},{2,3},{3,2},{4,5},{5,4},{6,7},{7,6},{8,9},{9,8},{10,11... | collective-permute-start | bytes 184328 | tf_op jit(solution)/shard_map/ppermute | solution.py:448
  18.4 6.8 %collective-permute-start.7 = (bf16[48,640]{1,0:T(8,128)(2,1)S(1)}, bf16[48,640]{1,0:T(8,128)(2,1)S(1)}, u32[]{:S(2)}, u32[]{:S(2)}) collective-permute-start(bf16[48,640]{1,0:T(8,128)(2,1)S(1)} %get-tuple-element.56), channel_id=1, source_target_pairs={{0,5},{1,4},{2,7},{3,6},{4,1},{5,0},{6,3},{7,2},{8,13},{9,12},{10,... | collective-permute-start | bytes 184328 | tf_op jit(solution)/shard_map/ppermute | solution.py:448
  19.4 5.7 %collective-permute-start.8 = (bf16[48,640]{1,0:T(8,128)(2,1)S(1)}, bf16[48,640]{1,0:T(8,128)(2,1)S(1)}, u32[]{:S(2)}, u32[]{:S(2)}) collective-permute-start(bf16[48,640]{1,0:T(8,128)(2,1)S(1)} %get-tuple-element.57), channel_id=1, source_target_pairs={{0,4},{1,5},{2,6},{3,7},{4,0},{5,1},{6,2},{7,3},{8,12},{9,13},{10,... | collective-permute-start | bytes 184328 | tf_op jit(solution)/shard_map/ppermute | solution.py:448
  26.2 1.6 %collective-permute-start.9 = (bf16[24,5184]{1,0:T(8,128)(2,1)S(1)}, bf16[24,5184]{1,0:T(8,128)(2,1)S(1)}, u32[]{:S(2)}, u32[]{:S(2)}) collective-permute-start(bf16[24,5184]{1,0:T(8,128)(2,1)S(1)} %second_pair_other.1), channel_id=1, source_target_pairs={{0,2},{1,3},{2,0},{3,1},{4,6},{5,7},{6,4},{7,5},{8,10},{9,11},{10,... | collective-permute-start | bytes 746504 | tf_op jit(solution)/shard_map/ppermute | solution.py:448
  27.9 6.8 %collective-permute-start.10 = (bf16[8,3968]{1,0:T(8,128)(2,1)S(1)}, bf16[8,3968]{1,0:T(8,128)(2,1)S(1)}, u32[]{:S(2)}, u32[]{:S(2)}) collective-permute-start(bf16[8,3968]{1,0:T(8,128)(2,1)S(1)} %get-tuple-element.59), channel_id=1, source_target_pairs={{0,16},{8,24},{16,0},{24,8},{1,17},{9,25},{17,1},{25,9},{2,18},{10... | collective-permute-start | bytes 190472 | tf_op jit(solution)/shard_map/ppermute | solution.py:448
  30.7 6.3 %collective-permute-start.11 = (bf16[8,3968]{1,0:T(8,128)(2,1)S(1)}, bf16[8,3968]{1,0:T(8,128)(2,1)S(1)}, u32[]{:S(2)}, u32[]{:S(2)}) collective-permute-start(bf16[8,3968]{1,0:T(8,128)(2,1)S(1)} %get-tuple-element.60), channel_id=1, source_target_pairs={{0,24},{8,16},{16,8},{24,0},{1,25},{9,17},{17,9},{25,1},{2,26},{10... | collective-permute-start | bytes 190472 | tf_op jit(solution)/shard_map/ppermute | solution.py:448
  32.0 5.2 %collective-permute-start.12 = (bf16[8,3968]{1,0:T(8,128)(2,1)S(1)}, bf16[8,3968]{1,0:T(8,128)(2,1)S(1)}, u32[]{:S(2)}, u32[]{:S(2)}) collective-permute-start(bf16[8,3968]{1,0:T(8,128)(2,1)S(1)} %get-tuple-element.61), channel_id=1, source_target_pairs={{0,8},{8,0},{16,24},{24,16},{1,9},{9,1},{17,25},{25,17},{2,10},{10... | collective-permute-start | bytes 190472 | tf_op jit(solution)/shard_map/ppermute | solution.py:448
  37.2 4.3 %collective-permute-start.13 = (bf16[8,3968]{1,0:T(8,128)(2,1)S(1)}, bf16[8,3968]{1,0:T(8,128)(2,1)S(1)}, u32[]{:S(2)}, u32[]{:S(2)}) collective-permute-start(bf16[8,3968]{1,0:T(8,128)(2,1)S(1)} %plane_sum.1.mine), channel_id=1, source_target_pairs={{0,1},{1,0},{2,3},{3,2},{4,5},{5,4},{6,7},{7,6},{8,9},{9,8},{10,11... | collective-permute-start | bytes 190472 | tf_op jit(solution)/shard_map/ppermute | solution.py:448
